TPU v7x, 32 devices: a whole 2x2x4 slice. The times are simulated.
32 devices in a mesh: dp: 8 (over y, x, core), tensor: 4 (over z).
Axes of the slice: x: 2, y: 2, z: 4, core: 2. Of those that a mesh axis runs over, the one named last changes fastest.
Arguments:
- activations: bfloat16 [8, 256, 3072], P('dp', None, 'tensor')
- out_grads: bfloat16 [8, 256, 5120], P('dp', 'tensor')
- error_buffer: bfloat16 [8, 3072, 5120], P('dp', 'tensor'), may hold values from -4 to 4
- warm_factor: float32 [5120, 4], replicated, may hold values from -6 to 6
Outputs:
- rebuilt_grad: bfloat16 [3072, 5120], P('tensor')
- next_error: bfloat16 [8, 3072, 5120], P('dp', 'tensor')
- next_factor: float32 [5120, 4], replicated
All inputs are finite; a program needn't handle non-finite values.
Results may differ from a plain program's by a relative error of at most 0.00105.
Values may be sent and summed in bfloat16 or wider, within the bound.
No kernel may reach another device: no remote copies, remote signals or barrier semaphores. Data moves between devices by JAX's collectives and lax.ppermute only.
A program may use at most 128 MiB of HBM per device.

v0:
```python
import jax
import jax.numpy as jnp
from jax import lax
from jax.sharding import PartitionSpec as P


def per_device(activations, out_grads, error_buffer, warm_factor):
    high = lax.Precision.HIGHEST
    local_acts = activations[0]
    replicas = lax.axis_size("dp")
    grad = lax.dot_general(
        local_acts,
        lax.all_gather(out_grads, "tensor", axis=1, tiled=True)[0],
        (((0,), (0,)), ((), ())),
        preferred_element_type=jnp.float32,
    )
    matrix = grad + error_buffer[0].astype(jnp.float32)
    left_part = jnp.dot(matrix, warm_factor, precision=high)
    left_mean = lax.psum(left_part, "dp") / replicas
    gram = lax.psum(jnp.dot(left_mean.T, left_mean, precision=high), "tensor")
    lower = jnp.linalg.cholesky(gram)
    left_ortho = lax.linalg.triangular_solve(
        lower, left_mean, left_side=False, lower=True, transpose_a=True
    )
    right_part = jnp.dot(matrix.T, left_ortho, precision=high)
    next_factor = lax.psum(right_part, ("dp", "tensor")) / replicas
    rebuilt = jnp.dot(left_ortho, next_factor.T, precision=high)
    next_error = (matrix - rebuilt).astype(jnp.bfloat16)[None]
    return (rebuilt.astype(jnp.bfloat16), next_error, next_factor)


def solution(mesh):
    return jax.shard_map(
        per_device,
        mesh=mesh,
        in_specs=(P("dp", None, "tensor"), P("dp", "tensor", None), P("dp", "tensor", None), P()),
        out_specs=(P("tensor", None), P("dp", "tensor", None), P()),
        check_vma=False,
    )
```

profile of v0, /device:TPU:0, one launch (start us, length us, event | category | flops | bytes accessed | tf_op | source)
XLA Modules:
  0.0 281.9 jit_solution(1661353766632188736)
XLA Ops:
  7.2 0.0 copy-start
  7.2 0.0 copy-start.3
  7.2 0.0 all-gather.2.cloned.1.call-start
  7.2 0.7 all-gather.2.cloned.1.call-update
  7.9 0.0 all-reduce.2.cloned.1.call-start
  8.0 59.2 %all-gather.2.cloned.1.call-done = bf16[1,256,5120]{2,1,0:T(8,128)(2,1)} async-done(((bf16[1,64,5120]{2,1,0:T(8,128)(2,1)}), bf16[1,256,5120]{2,1,0:T(8,128)(2,1)}) %all-gather.2.cloned.1.call-update) | async-done | bytes 2621456 | tf_op jit(solution)/shard_map/all_gather | solution.py:13
  67.1 6.3 %convert_add_fusion = f32[768,5120]{1,0:T(8,128)S(1)} fusion(bf16[1,768,5120]{2,1,0:T(8,128)(2,1)} %param.6, bf16[1,256,5120]{2,1,0:T(8,128)(2,1)} %all-gather.2.cloned.1.call-done, bf16[1,256,768]{2,1,0:T(8,128)(2,1)S(1)} %copy-done), kind=kOutput, calls=%fused_computation | convolution fusion | flops 2021130240 | bytes 26607616 | tf_op jit(solution)/shard_map/dot_general | solution.py:11
  73.4 5.5 %copy-done.1 = f32[768,5120]{1,0:T(8,128)} copy-done((f32[768,5120]{1,0:T(8,128)}, f32[768,5120]{1,0:T(8,128)S(1)}, u32[]{:S(2)}) %copy-start.1) | copy-done | bytes 15728664
  78.9 13.2 %fusion.14 = f32[768,4]{0,1:T(4,128)S(1)} fusion(f32[768,5120]{1,0:T(8,128)S(1)} %convert_add_fusion, f32[5120,4]{0,1:T(4,128)S(1)} %copy-done.3), kind=kOutput, calls=%fused_computation.23 | convolution fusion | flops 188743680 | bytes 15822848 | tf_op jit(solution)/shard_map/dot_general | solution.py:18
  92.1 24.0 %psum.21 = f32[768,4]{0,1:T(4,128)S(1)} all-reduce(f32[768,4]{0,1:T(4,128)S(1)} %fusion.14), channel_id=1, replica_groups=mesh['dp'=8,'tensor'=4] {'dp'}, use_global_device_ids=true, to_apply=%region_0.0 | all-reduce | flops 3072 | bytes 24576 | tf_op jit(solution)/shard_map/psum | solution.py:19
  116.1 0.1 fusion.5
  116.3 9.7 %psum.22 = f32[4,4]{0,1:T(4,128)S(1)} all-reduce(f32[4,4]{0,1:T(4,128)S(1)} %fusion.5), channel_id=1, replica_groups=mesh['dp'=8,'tensor'=4] {'tensor'}, use_global_device_ids=true, to_apply=%region_1.0 | all-reduce | flops 16 | bytes 128 | tf_op jit(solution)/shard_map/psum | solution.py:20
  125.9 0.1 copy.8
  126.0 0.4 cholesky.16
  126.4 0.6 compare_reduce_fusion
  127.1 0.6 fusion.9
  127.7 0.3 custom-call.6
  128.1 0.2 fusion.3
  128.3 11.5 %fusion.15 = f32[5120,4]{0,1:T(4,128)} fusion(f32[768,5120]{1,0:T(8,128)} %copy-done.1, f32[768,4]{0,1:T(4,128)S(1)} %fusion.3), kind=kOutput, calls=%fused_computation.24 | convolution fusion | flops 188743680 | bytes 15822848 | tf_op jit(solution)/shard_map/dot_general | solution.py:25
  139.8 0.0 all-reduce.2.cloned.1.call-update
  139.9 116.1 %all-reduce.2.cloned.1.call-done = f32[5120,4]{0,1:T(4,128)} async-done(((f32[5120,4]{0,1:T(4,128)}), f32[5120,4]{0,1:T(4,128)}) %all-reduce.2.cloned.1.call-update) | async-done | bytes 81936 | tf_op jit(solution)/shard_map/psum | solution.py:26
  256.0 0.9 broadcast_multiply_fusion
  256.9 0.0 copy-start.2
  256.9 18.1 %fusion = (bf16[1,768,5120]{2,1,0:T(8,128)(2,1)}, bf16[768,5120]{1,0:T(8,128)(2,1)}) fusion(f32[768,5120]{1,0:T(8,128)} %copy-done.1, f32[768,4]{0,1:T(4,128)S(1)} %fusion.3, f32[5120,4]{0,1:T(4,128)S(1)} %broadcast_multiply_fusion), kind=kOutput, calls=%fused_computation.2 | convolution fusion | flops 200540160 | bytes 31551488 | tf_op jit(solution)/shard_map/dot_general | solution.py:27
  (6 shorter events, 0.0 us)
Async XLA Ops:
  7.2 60.0 %copy-start = (bf16[1,256,768]{2,1,0:T(8,128)(2,1)S(1)}, bf16[1,256,768]{2,1,0:T(8,128)(2,1)}, u32[]{:S(2)}) copy-start(bf16[1,256,768]{2,1,0:T(8,128)(2,1)} %param.4) | copy-start | bytes 1179652
  7.2 71.7 %copy-start.3 = (f32[5120,4]{0,1:T(4,128)S(1)}, f32[5120,4]{0,1:T(4,128)}, u32[]{:S(2)}) copy-start(f32[5120,4]{0,1:T(4,128)} %param.7) | copy-start | bytes 245764
  7.2 59.9 %all-gather.2.cloned.1.call-start = ((), (), s32[]{:S(2)}) async-start(), calls=%async_computation | async-start | bytes 3276800 | tf_op jit(solution)/shard_map/all_gather | solution.py:13
  7.9 248.0 %all-reduce.2.cloned.1.call-start = ((), (), s32[]{:S(2)}) async-start(), calls=%async_computation.1 | async-start | bytes 163840 | tf_op jit(solution)/shard_map/psum | solution.py:26
  73.4 5.5 %copy-start.1 = (f32[768,5120]{1,0:T(8,128)}, f32[768,5120]{1,0:T(8,128)S(1)}, u32[]{:S(2)}) copy-start(f32[768,5120]{1,0:T(8,128)S(1)} %convert_add_fusion) | copy-start | bytes 47185924
  256.9 18.2 %copy-start.2 = (f32[5120,4]{0,1:T(4,128)}, f32[5120,4]{0,1:T(4,128)S(1)}, u32[]{:S(2)}) copy-start(f32[5120,4]{0,1:T(4,128)S(1)} %broadcast_multiply_fusion) | copy-start | bytes 245764
Sparse Core Ops, SparseCore 0:
  9.6 57.4 all-gather.1
  140.0 115.9 all-reduce.1
where the time goes:
time: 283 us; the launch traced here: 282 us
  waiting for transfers between devices  176 us (62%)
  matrix products  49.5 us (17%)
  blocking collectives  33.6 us (12%)
  between operations  14.1 us (5%)
  local copies, waits for them, and re-layouts  5.62 us (2%)
  other arithmetic  2.94 us (1%)
    psum x1, waiting for transfers between devices, per_device(): next_factor = lax.psum(right_part, ('dp', 'tensor')) / replicas  116 us
    all_gather x1, waiting for transfers between devices, per_device(): lax.all_gather(out_grads, 'tensor', axis=1, tiled=True)[0]  59.2 us
    psum x1, blocking collectives, per_device(): left_mean = lax.psum(left_part, 'dp') / replicas  24 us
    dot_general x1, matrix products, per_device(): rebuilt = jnp.dot(left_ortho, next_factor.T, precision=high)  18.1 us
    dot_general x1, matrix products, per_device(): left_part = jnp.dot(matrix, warm_factor, precision=high)  13.2 us
    dot_general x1, matrix products, per_device(): right_part = jnp.dot(matrix.T, left_ortho, precision=high)  11.5 us
    psum x1, blocking collectives, per_device(): gram = lax.psum(jnp.dot(left_mean.T, left_mean, precision=high), 'tensor')  9.66 us
    dot_general x1, matrix products, per_device(): lax.dot_general(local_acts, lax.all_gather(out_grads, 'tensor', axis=1, t...  6.27 us
  transfers between devices with their start and end apart: 2, of which 2 were waited for; matrix products, arithmetic and copies ran while one was open for 0% of the time, Pallas kernels for 0%

commit v1 on v0

v1 whole, which is shorter than its diff:
```python
import functools

import jax
import jax.numpy as jnp
from jax import lax
from jax.experimental import pallas as pl
from jax.experimental.pallas import tpu as pltpu
from jax.sharding import PartitionSpec as P

F32 = jnp.float32
BF16 = jnp.bfloat16
SHRINK = 2.0**-23
TINY = 1e-30
PARTS = 2
BLOCK = 512


def params(mib):
    return pltpu.CompilerParams(vmem_limit_bytes=mib * 2**20)


def cost(flops, moved):
    return pl.CostEstimate(flops=int(flops), bytes_accessed=int(moved), transcendentals=0)


def dot(a, b, contract):
    return lax.dot_general(a, b, ((contract[:1], contract[1:]), ((), ())), preferred_element_type=F32)


def split(x):
    hi = x.astype(BF16)
    rest = x - hi.astype(F32)
    mid = rest.astype(BF16)
    lo = (rest - mid.astype(F32)).astype(BF16)
    return hi.astype(F32), mid.astype(F32), lo.astype(F32)


def stack3(x, ref):
    rank = x.shape[0]
    for i, part in enumerate(split(x)):
        ref[i * rank : (i + 1) * rank, :] = part
    return ref[...].astype(BF16)


def sum3(y, rank):
    return (y[2 * rank :] + y[rank : 2 * rank]) + y[:rank]


def ring_of(n):
    return [2 * p if 2 * p < n else 2 * (n - p) - 1 for p in range(n)]


def ring_source(me, step, n):
    place = jnp.where(lax.rem(me, 2) == 0, me // 2, n - (me + 1) // 2)
    place = lax.rem(place - step + n, n)
    return jnp.where(2 * place < n, 2 * place, 2 * (n - place) - 1)


def ring_step(x, axis, n):
    ring = ring_of(n)
    return lax.ppermute(x, axis, [(ring[p], ring[(p + 1) % n]) for p in range(n)])


def exchange(pieces, axis, n):
    return [pieces[0]] + [
        lax.ppermute(pieces[k], axis, [(i, (i + k) % n) for i in range(n)]) for k in range(1, n)
    ]


def token_factor_kernel(w_ref, g_ref, out_ref, w3):
    rank = w_ref.shape[0]
    parts = stack3(w_ref[...] * SHRINK, w3)
    out_ref[...] = sum3(dot(parts, g_ref[0], (1, 1)), rank)


def error_left_kernel(w_ref, e_ref, out_ref, w3):
    rank = w_ref.shape[0]

    @pl.when(pl.program_id(0) == 0)
    def _():
        stack3(w_ref[...] * SHRINK, w3)

    out_ref[...] = sum3(dot(w3[...].astype(BF16), e_ref[0], (1, 1)), rank)


def left_kernel(n, *refs):
    a_ref, e_ref = refs[:2]
    gws = refs[2 : 2 + n]
    out_ref, g3 = refs[2 + n :]
    rank, tok = gws[0].shape
    me = lax.axis_index("tensor")
    total = e_ref[...]
    for k in range(n):
        src = lax.rem(me - k + n, n)
        rows = a_ref[0, pl.ds(pl.multiple_of(src * tok, tok), tok), :]
        total += sum3(dot(stack3(gws[k][...], g3), rows, (1, 0)), rank)
    out_ref[...] = total


def mean_kernel(m, n, *refs):
    a_ref = refs[0]
    pieces = refs[1 : 1 + m]
    p_ref = refs[1 + m]
    msgs = refs[2 + m : 2 + m + n]
    inbox, p3, outbox = refs[2 + m + n :]
    rank = p_ref.shape[0]
    tok = a_ref.shape[1] // n
    me_r = lax.axis_index("dp")
    me_t = lax.axis_index("tensor")
    for k in range(m):
        inbox[lax.rem(me_r - k + m, m)] = pieces[k][...]
    total = inbox[0]
    for r in range(1, m):
        total += inbox[r]
    mean = total * (1.0 / (SHRINK * m))
    p_ref[...] = mean
    top = jnp.max(jnp.max(jnp.abs(mean), axis=1, keepdims=True), axis=0, keepdims=True)
    top = jnp.maximum(top, TINY)
    parts = stack3(mean / (top * 1024.0), p3)
    outbox[...] = jnp.zeros_like(outbox)
    for t in range(n):
        y = dot(parts, a_ref[0, t * tok : (t + 1) * tok, :], (1, 1))
        outbox[t, 0:rank, 0:tok] = sum3(y, rank)
        for i in range(rank):
            column = jnp.sum(mean * mean[i : i + 1, :], axis=1, keepdims=True)
            outbox[t, rank : 2 * rank, i : i + 1] = column
        outbox[t, rank : rank + 1, rank : rank + 1] = top
    for k in range(n):
        msgs[k][...] = outbox[lax.rem(me_t + k, n)]


def error_right_kernel(p_ref, e_ref, out_ref, p3):
    rank = p_ref.shape[0]

    @pl.when(pl.program_id(0) == 0)
    def _():
        stack3(p_ref[...], p3)

    out_ref[...] = sum3(dot(p3[...].astype(BF16), e_ref[0], (1, 0)), rank)


def lower_inverse(gram, rank):
    at = lambda i, j: gram[i : i + 1, j : j + 1]
    low = {}
    for j in range(rank):
        d = at(j, j)
        for k in range(j):
            d = d - low[j, k] * low[j, k]
        low[j, j] = jnp.sqrt(d)
        for i in range(j + 1, rank):
            v = at(i, j)
            for k in range(j):
                v = v - low[i, k] * low[j, k]
            low[i, j] = v / low[j, j]
    inv = {}
    for j in range(rank):
        inv[j, j] = 1.0 / low[j, j]
        for i in range(j + 1, rank):
            v = low[i, j] * inv[j, j]
            for k in range(j + 1, i):
                v = v + low[i, k] * inv[k, j]
            inv[i, j] = -v / low[i, i]
    return inv


def solve_rows(inv, x, rank):
    rows = []
    for i in range(rank):
        row = inv[i, 0] * x[0:1, :]
        for j in range(1, i + 1):
            row = row + inv[i, j] * x[j : j + 1, :]
        rows.append(row)
    return rows


def right_kernel(m, n, *refs):
    p_ref, r_ref, g_ref = refs[:3]
    pieces = refs[3 : 3 + n]
    ortho_ref = refs[3 + n]
    outs = refs[4 + n : 4 + n + m]
    inbox, z, z3, whole, outbox = refs[4 + n + m :]
    rank, rows = p_ref.shape
    tok = g_ref.shape[1]
    cut = outs[0].shape[1]
    me_r = lax.axis_index("dp")
    me_t = lax.axis_index("tensor")
    for k in range(n):
        inbox[lax.rem(me_t - k + n, n)] = pieces[k][...]
    gram = inbox[0, rank : 2 * rank, 0:rank]
    for t in range(1, n):
        gram = gram + inbox[t, rank : 2 * rank, 0:rank]
    inv = lower_inverse(gram, rank)
    for t in range(n):
        top = inbox[t, rank : rank + 1, rank : rank + 1]
        scaled = {key: value * top for key, value in inv.items()}
        for i, row in enumerate(solve_rows(scaled, inbox[t, 0:rank, 0:tok], rank)):
            if t == 0:
                z[i : i + 1, :] = row
            else:
                z[i : i + 1, :] += row
    for i, row in enumerate(solve_rows(inv, p_ref[...], rank)):
        ortho_ref[i : i + 1, :] = row
    for i, row in enumerate(solve_rows(inv, r_ref[...], rank)):
        whole[i : i + 1, :] = row
    whole[...] += sum3(dot(stack3(z[...], z3), g_ref[0], (1, 0)), rank) * 1024.0
    for r in range(m):
        outbox[r] = whole[:, r * cut : (r + 1) * cut]
    for k in range(m):
        outs[k][...] = outbox[lax.rem(me_r + k, m)]


def add_kernel(axis, n, scale, *refs):
    pieces, out_ref, inbox = refs[:n], refs[n], refs[n + 1]
    me = lax.axis_index(axis)
    for k in range(n):
        inbox[lax.rem(me - k + n, n)] = pieces[k][...]
    total = inbox[0]
    for i in range(1, n):
        total += inbox[i]
    out_ref[...] = total * scale


LEFT_TERMS = (0, 0, 1, 0, 2, 1)
RIGHT_TERMS = (0, 1, 0, 2, 0, 1)


def factor_kernel(m, *refs):
    ortho_ref = refs[0]
    pieces = refs[1 : 1 + m]
    whole_ref, left_ref, right_ref, inbox, left, right = refs[1 + m :]
    rank, cut = pieces[0].shape
    me = lax.axis_index("dp")
    for k in range(m):
        inbox[lax.rem(me - k + m, m)] = pieces[k][...]
    for r in range(m):
        whole_ref[:, r * cut : (r + 1) * cut] = inbox[r]
    for terms, x, ref, out in (
        (LEFT_TERMS, ortho_ref[...], left, left_ref),
        (RIGHT_TERMS, whole_ref[...], right, right_ref),
    ):
        parts = split(x)
        for i, term in enumerate(terms):
            ref[i * rank : (i + 1) * rank, :] = parts[term]
        out[...] = ref[...].astype(BF16)


def final_kernel(n, *refs):
    a_ref, left_ref, right_ref, e_ref = refs[:4]
    slots = refs[4 : 4 + n]
    rebuilt_ref, error_ref, acts = refs[-3:]
    tok = slots[0].shape[1]
    me = lax.axis_index("tensor")

    @pl.when(pl.program_id(0) == 0)
    def _():
        for s in range(n):
            src = ring_source(me, s, n)
            rows = a_ref[0, pl.ds(pl.multiple_of(src * tok, tok), tok), :]
            acts[s * tok : (s + 1) * tok, :] = rows

    grads = jnp.concatenate([slot[0] for slot in slots], axis=0)
    matrix = dot(acts[...], grads, (0, 0)) + e_ref[0].astype(F32)
    rebuilt = dot(left_ref[...], right_ref[...], (0, 0))
    rebuilt_ref[...] = rebuilt.astype(BF16)
    error_ref[0] = (matrix - rebuilt).astype(BF16)


def per_device(activations, out_grads, error_buffer, warm_factor):
    m = lax.axis_size("dp")
    n = lax.axis_size("tensor")
    _, tokens, rows = activations.shape
    _, tok, width = out_grads.shape
    rank = warm_factor.shape[1]
    part = width // PARTS
    w = warm_factor.T
    sds = jax.ShapeDtypeStruct

    chunks = []
    for c in range(PARTS):
        held = [out_grads[:, :, c * part : (c + 1) * part]]
        for _ in range(n - 1):
            held.append(ring_step(held[-1], "tensor", n))
        chunks.append(held)

    gw = pl.pallas_call(
        token_factor_kernel,
        out_shape=sds((rank, tok), F32),
        scratch_shapes=[pltpu.VMEM((3 * rank, width), F32)],
        compiler_params=params(32),
        cost_estimate=cost(2e6, 1e6),
        name="token_factor",
    )(w, out_grads)
    gws = exchange([gw] * n, "tensor", n)

    high = 128
    ew = pl.pallas_call(
        error_left_kernel,
        grid=(rows // high,),
        in_specs=[
            pl.BlockSpec((rank, width), lambda i: (0, 0)),
            pl.BlockSpec((1, high, width), lambda i: (0, i, 0)),
        ],
        out_specs=pl.BlockSpec((rank, high), lambda i: (0, i)),
        out_shape=sds((rank, rows), F32),
        scratch_shapes=[pltpu.VMEM((3 * rank, width), F32)],
        compiler_params=params(32),
        cost_estimate=cost(2e9, rows * width * 2),
        name="error_left",
    )(w, error_buffer)

    left = pl.pallas_call(
        functools.partial(left_kernel, n),
        out_shape=sds((rank, rows), F32),
        scratch_shapes=[pltpu.VMEM((3 * rank, tok), F32)],
        compiler_params=params(32),
        cost_estimate=cost(1e7, 1e6),
        name="left",
    )(activations, ew, *gws)
    lefts = exchange([left] * m, "dp", m)

    mean, *msgs = pl.pallas_call(
        functools.partial(mean_kernel, m, n),
        out_shape=[sds((rank, rows), F32)] + [sds((8, 128), F32)] * n,
        scratch_shapes=[
            pltpu.VMEM((m, rank, rows), F32),
            pltpu.VMEM((3 * rank, rows), F32),
            pltpu.VMEM((n, 8, 128), F32),
        ],
        compiler_params=params(32),
        cost_estimate=cost(1e7, 1e6),
        name="mean",
    )(activations, *lefts)
    msgs = exchange(msgs, "tensor", n)

    right_raw = pl.pallas_call(
        error_right_kernel,
        grid=(width // BLOCK,),
        in_specs=[
            pl.BlockSpec((rank, rows), lambda i: (0, 0)),
            pl.BlockSpec((1, rows, BLOCK), lambda i: (0, 0, i)),
        ],
        out_specs=pl.BlockSpec((rank, BLOCK), lambda i: (0, i)),
        out_shape=sds((rank, width), F32),
        scratch_shapes=[pltpu.VMEM((3 * rank, rows), F32)],
        compiler_params=params(32),
        cost_estimate=cost(2e9, rows * width * 2),
        name="error_right",
    )(mean, error_buffer)

    cut = width // m
    ortho, *pieces = pl.pallas_call(
        functools.partial(right_kernel, m, n),
        out_shape=[sds((rank, rows), F32)] + [sds((rank, cut), F32)] * m,
        scratch_shapes=[
            pltpu.VMEM((n, 8, 128), F32),
            pltpu.VMEM((rank, tok), F32),
            pltpu.VMEM((3 * rank, tok), F32),
            pltpu.VMEM((rank, width), F32),
            pltpu.VMEM((m, rank, cut), F32),
        ],
        compiler_params=params(32),
        cost_estimate=cost(1e7, 1e6),
        name="right",
    )(mean, right_raw, out_grads, *msgs)

    def added(pieces, axis, size, scale):
        return pl.pallas_call(
            functools.partial(add_kernel, axis, size, scale),
            out_shape=sds((rank, cut), F32),
            scratch_shapes=[pltpu.VMEM((size, rank, cut), F32)],
            cost_estimate=cost(1e5, 1e5),
            name="add_" + axis,
        )(*pieces)

    mine = added(exchange(pieces, "dp", m), "dp", m, 1.0)
    mine = added(exchange([mine] * n, "tensor", n), "tensor", n, 1.0 / m)
    pieces = exchange([mine] * m, "dp", m)

    terms = len(LEFT_TERMS) * rank
    whole, left_terms, right_terms = pl.pallas_call(
        functools.partial(factor_kernel, m),
        out_shape=[sds((rank, width), F32), sds((terms, rows), BF16), sds((terms, width), BF16)],
        scratch_shapes=[
            pltpu.VMEM((m, rank, cut), F32),
            pltpu.VMEM((terms, rows), F32),
            pltpu.VMEM((terms, width), F32),
        ],
        compiler_params=params(32),
        cost_estimate=cost(1e6, 1e6),
        name="factor",
    )(ortho, *pieces)

    outs = ()
    for c, held in enumerate(chunks):
        steps = part // BLOCK
        at = c * steps
        col = lambda i, at=at: (0, 0, i + at)
        mine_specs = [pl.BlockSpec((1, tok, BLOCK), col)]
        fresh = [pl.BlockSpec((1, tok, BLOCK), lambda i: (0, 0, i))] * (n - 1)
        outs = pl.pallas_call(
            functools.partial(final_kernel, n),
            grid=(steps,),
            in_specs=[
                pl.BlockSpec((1, tokens, rows), lambda i: (0, 0, 0)),
                pl.BlockSpec((terms, rows), lambda i: (0, 0)),
                pl.BlockSpec((terms, BLOCK), lambda i, at=at: (0, i + at)),
                pl.BlockSpec((1, rows, BLOCK), col),
            ]
            + mine_specs
            + fresh
            + [pl.BlockSpec(memory_space=pl.ANY)] * len(outs),
            out_specs=[
                pl.BlockSpec((rows, BLOCK), lambda i, at=at: (0, i + at)),
                pl.BlockSpec((1, rows, BLOCK), col),
            ],
            out_shape=[sds((rows, width), BF16), sds((1, rows, width), BF16)],
            input_output_aliases={4 + n + j: j for j in range(len(outs))},
            scratch_shapes=[pltpu.VMEM((tokens, rows), BF16)],
            compiler_params=params(48),
            cost_estimate=cost(4e9 / PARTS, rows * width * 6 // PARTS),
            name="rebuild",
        )(activations, left_terms, right_terms, error_buffer, out_grads, *held[1:], *outs)
    rebuilt, error = outs
    return rebuilt, error, whole.T


def solution(mesh):
    return jax.shard_map(
        per_device,
        mesh=mesh,
        in_specs=(P("dp", None, "tensor"), P("dp", "tensor", None), P("dp", "tensor", None), P()),
        out_specs=(P("tensor", None), P("dp", "tensor", None), P()),
        check_vma=False,
    )
```

time: 283 us -> 109 us (0.39)
  waiting for transfers between devices: 176 us -> 28.9 us
  matrix products: 49.5 us -> 0 us
  starting transfers between devices: 0.08 us -> 43.9 us
  blocking collectives: 33.6 us -> 0 us
  Pallas kernels: 0 us -> 26.1 us
  between operations: 14.1 us -> 0.83 us
  local copies, waits for them, and re-layouts: 5.62 us -> 8.87 us
  other arithmetic: 2.94 us -> 0 us
    psum x1 -> x0, waiting for transfers between devices: 116 us -> none  [per_device(): next_factor = lax.psum(right_part, ('dp', 'tensor')) / replicas]
    all_gather x1 -> x0, waiting for transfers between devices: 59.2 us -> none  [per_device(): lax.all_gather(out_grads, 'tensor', axis=1, tiled=True)[0]]
    dot_general x5 -> x0, matrix products: 49.3 us -> none  [the longest x1 18.1 us: per_device(): rebuilt = jnp.dot(left_ortho, next_factor.T, precision=high)]
    ppermute x0 -> x36, starting transfers between devices: none -> 43.9 us  [the longest x30 27.2 us: exchange(): lax.ppermute(pieces[k], axis, [(i, (i + k) % n) for i in range(n)])]
    psum x2 -> x0, blocking collectives: 33.6 us -> none  [the longest x1 24 us: per_device(): left_mean = lax.psum(left_part, 'dp') / replicas]
    ppermute x0 -> x36, waiting for transfers between devices: none -> 28.9 us  [the longest x30 18.7 us: exchange(): lax.ppermute(pieces[k], axis, [(i, (i + k) % n) for i in range(n)])]
    pallas_call x0 -> x11, Pallas kernels: none -> 26.1 us  [the longest x2 15.4 us: per_device(): pl.pallas_call(functools.partial(final_kernel, n), grid=(steps,), in_spec...]
    unnamed x8 -> x36, local copies, waits for them, and re-layouts: 5.52 us -> 7.7 us
  transfers between devices with their start and end apart: 2 -> 36, of which waited for: 2 -> 19; matrix products, arithmetic and copies ran while one was open for 0% -> 0% of each run, Pallas kernels for 0% -> 17%
where the time goes in v1:
time: 109 us
  starting transfers between devices  43.9 us (40%)
  waiting for transfers between devices  28.9 us (27%)
  Pallas kernels  26.1 us (24%)
  local copies, waits for them, and re-layouts  8.87 us (8%)
    ppermute x30, starting transfers between devices, exchange(): lax.ppermute(pieces[k], axis, [(i, (i + k) % n) for i in range(n)])  27.2 us
    ppermute x30, waiting for transfers between devices, exchange(): lax.ppermute(pieces[k], axis, [(i, (i + k) % n) for i in range(n)])  18.7 us
    ppermute x6, starting transfers between devices, ring_step(): lax.ppermute(x, axis, [(ring[p], ring[(p + 1) % n]) for p in range(n)])  16.7 us
    pallas_call x2, Pallas kernels, per_device(): pl.pallas_call(functools.partial(final_kernel, n), grid=(steps,), in_spec...  15.4 us
    ppermute x6, waiting for transfers between devices, ring_step(): lax.ppermute(x, axis, [(ring[p], ring[(p + 1) % n]) for p in range(n)])  10.2 us
    unnamed x36, local copies, waits for them, and re-layouts  7.7 us
    pallas_call x1, Pallas kernels, per_device(): pl.pallas_call(error_left_kernel, grid=(rows // high,), in_specs=[pl.Bloc...  2.83 us
    pallas_call x2, Pallas kernels, added(): pl.pallas_call(functools.partial(add_kernel, axis, size, scale), out_shap...  2.8 us
  transfers between devices with their start and end apart: 36, of which 19 were waited for; matrix products, arithmetic and copies ran while one was open for 0% of the time, Pallas kernels for 17%

profile of v1, /device:TPU:0, one launch (start us, length us, event | category | flops | bytes accessed | tf_op | source)
XLA Modules:
  0.0 108.6 jit_solution(15517782429628553433)
XLA Ops:
  1.8 4.1 %collective-permute-start.33 = (bf16[1,64,2560]{2,1,0:T(8,128)(2,1)S(1)}, bf16[1,64,2560]{2,1,0:T(8,128)(2,1)S(1)}, u32[]{:S(2)}, u32[]{:S(2)}) collective-permute-start(bf16[1,64,2560]{2,1,0:T(8,128)(2,1)S(1)} %get-tuple-element.45), channel_id=1, source_target_pairs={{0,2},{2,3},{3,1},{1,0},{4,6},{6,7},{7,5},{5,4},{8,10},{10,11},{11... | collective-permute-start | bytes 983048 | tf_op jit(solution)/shard_map/ppermute | solution.py:61
  5.9 1.6 %collective-permute-start.30 = (bf16[1,64,2560]{2,1,0:T(8,128)(2,1)S(1)}, bf16[1,64,2560]{2,1,0:T(8,128)(2,1)S(1)}, u32[]{:S(2)}, u32[]{:S(2)}) collective-permute-start(bf16[1,64,2560]{2,1,0:T(8,128)(2,1)S(1)} %get-tuple-element.46), channel_id=1, source_target_pairs={{0,2},{2,3},{3,1},{1,0},{4,6},{6,7},{7,5},{5,4},{8,10},{10,11},{11... | collective-permute-start | bytes 983048 | tf_op jit(solution)/shard_map/ppermute | solution.py:61
  7.5 6.5 %collective-permute-done.33.refs_5_ = bf16[1,64,2560]{2,1,0:T(8,128)(2,1)S(1)} collective-permute-done((bf16[1,64,2560]{2,1,0:T(8,128)(2,1)S(1)}, bf16[1,64,2560]{2,1,0:T(8,128)(2,1)S(1)}, u32[]{:S(2)}, u32[]{:S(2)}) %collective-permute-start.33) | collective-permute-done | bytes 327712 | tf_op jit(solution)/shard_map/ppermute | solution.py:61
  14.0 3.4 %collective-permute-start.34 = (bf16[1,64,2560]{2,1,0:T(8,128)(2,1)S(1)}, bf16[1,64,2560]{2,1,0:T(8,128)(2,1)S(1)}, u32[]{:S(2)}, u32[]{:S(2)}) collective-permute-start(bf16[1,64,2560]{2,1,0:T(8,128)(2,1)S(1)} %collective-permute-done.33.refs_5_), channel_id=1, source_target_pairs={{0,2},{2,3},{3,1},{1,0},{4,6},{6,7},{7,5},{5,4},{8,10},{10,11},{11... | collective-permute-start | bytes 983048 | tf_op jit(solution)/shard_map/ppermute | solution.py:61
  17.4 3.6 %collective-permute-done.30.refs_5_ = bf16[1,64,2560]{2,1,0:T(8,128)(2,1)S(1)} collective-permute-done((bf16[1,64,2560]{2,1,0:T(8,128)(2,1)S(1)}, bf16[1,64,2560]{2,1,0:T(8,128)(2,1)S(1)}, u32[]{:S(2)}, u32[]{:S(2)}) %collective-permute-start.30) | collective-permute-done | bytes 327712 | tf_op jit(solution)/shard_map/ppermute | solution.py:61
  21.0 3.4 %collective-permute-start.31 = (bf16[1,64,2560]{2,1,0:T(8,128)(2,1)S(1)}, bf16[1,64,2560]{2,1,0:T(8,128)(2,1)S(1)}, u32[]{:S(2)}, u32[]{:S(2)}) collective-permute-start(bf16[1,64,2560]{2,1,0:T(8,128)(2,1)S(1)} %collective-permute-done.30.refs_5_), channel_id=1, source_target_pairs={{0,2},{2,3},{3,1},{1,0},{4,6},{6,7},{7,5},{5,4},{8,10},{10,11},{11... | collective-permute-start | bytes 983048 | tf_op jit(solution)/shard_map/ppermute | solution.py:61
  29.4 2.2 %collective-permute-start.35 = (bf16[1,64,2560]{2,1,0:T(8,128)(2,1)S(1)}, bf16[1,64,2560]{2,1,0:T(8,128)(2,1)S(1)}, u32[]{:S(2)}, u32[]{:S(2)}) collective-permute-start(bf16[1,64,2560]{2,1,0:T(8,128)(2,1)S(1)} %collective-permute-done.34.refs_6_), channel_id=1, source_target_pairs={{0,2},{2,3},{3,1},{1,0},{4,6},{6,7},{7,5},{5,4},{8,10},{10,11},{11... | collective-permute-start | bytes 983048 | tf_op jit(solution)/shard_map/ppermute | solution.py:61
  31.7 3.2 %copy-done = bf16[1,768,5120]{2,1,0:T(8,128)(2,1)S(1)} copy-done((bf16[1,768,5120]{2,1,0:T(8,128)(2,1)S(1)}, bf16[1,768,5120]{2,1,0:T(8,128)(2,1)}, u32[]{:S(2)}) %copy-start) | copy-done | bytes 7864344
  34.9 2.8 %error_left.1.refs_1_ = f32[4,768]{1,0:T(4,128)S(1)} custom-call(f32[4,5120]{1,0:T(4,128)S(1)} %bitcast.3, bf16[1,768,5120]{2,1,0:T(8,128)(2,1)S(1)} %copy-done), custom_call_target="tpu_custom_call" | custom-call | flops 2000000000 | bytes 7864320 | tf_op jit(solution)/shard_map/error_left/pallas_call | solution.py:296
  38.1 2.5 %collective-permute-start.8 = (f32[4,768]{1,0:T(4,128)S(1)}, f32[4,768]{1,0:T(4,128)S(1)}, u32[]{:S(2)}, u32[]{:S(2)}) collective-permute-start(f32[4,768]{1,0:T(4,128)S(1)} %left.1.refs_1_), channel_id=1, source_target_pairs={{0,24},{4,28},{8,0},{12,4},{16,8},{20,12},{24,16},{28,20},{1,25},{... | collective-permute-start | bytes 36872 | tf_op jit(solution)/shard_map/ppermute | solution.py:66
  40.8 1.5 %collective-permute-start.6 = (f32[4,768]{1,0:T(4,128)S(1)}, f32[4,768]{1,0:T(4,128)S(1)}, u32[]{:S(2)}, u32[]{:S(2)}) collective-permute-start(f32[4,768]{1,0:T(4,128)S(1)} %left.1.refs_1_), channel_id=1, source_target_pairs={{0,16},{4,20},{8,24},{12,28},{16,0},{20,4},{24,8},{28,12},{1,17},{... | collective-permute-start | bytes 36872 | tf_op jit(solution)/shard_map/ppermute | solution.py:66
  45.7 2.6 %collective-permute-done.4.refs_3_ = f32[4,768]{1,0:T(4,128)S(1)} collective-permute-done((f32[4,768]{1,0:T(4,128)S(1)}, f32[4,768]{1,0:T(4,128)S(1)}, u32[]{:S(2)}, u32[]{:S(2)}) %collective-permute-start.4) | collective-permute-done | bytes 12320 | tf_op jit(solution)/shard_map/ppermute | solution.py:66
  49.0 2.8 %collective-permute-start.11 = (f32[8,128]{1,0:T(8,128)S(1)}, f32[8,128]{1,0:T(8,128)S(1)}, u32[]{:S(2)}, u32[]{:S(2)}) collective-permute-start(f32[8,128]{1,0:T(8,128)S(1)} %get-tuple-element.27), channel_id=1, source_target_pairs={{0,2},{1,3},{2,0},{3,1},{4,6},{5,7},{6,4},{7,5},{8,10},{9,11},{10,... | collective-permute-start | bytes 12296 | tf_op jit(solution)/shard_map/ppermute | solution.py:66
  52.8 2.0 %collective-permute-start.32 = (bf16[1,64,2560]{2,1,0:T(8,128)(2,1)S(1)}, bf16[1,64,2560]{2,1,0:T(8,128)(2,1)S(1)}, u32[]{:S(2)}, u32[]{:S(2)}) collective-permute-start(bf16[1,64,2560]{2,1,0:T(8,128)(2,1)S(1)} %collective-permute-done.31.refs_6_), channel_id=1, source_target_pairs={{0,2},{2,3},{3,1},{1,0},{4,6},{6,7},{7,5},{5,4},{8,10},{10,11},{11... | collective-permute-start | bytes 983048 | tf_op jit(solution)/shard_map/ppermute | solution.py:61
  54.8 2.8 %error_right.1.refs_1_ = f32[4,5120]{1,0:T(4,128)S(1)} custom-call(f32[4,768]{1,0:T(4,128)S(1)} %get-tuple-element.24.p_ref.refs_0_, bf16[1,768,5120]{2,1,0:T(8,128)(2,1)S(1)} %copy-done.1), custom_call_target="tpu_custom_call" | custom-call | flops 2000000000 | bytes 7864320 | tf_op jit(solution)/shard_map/error_right/pallas_call | solution.py:335
  59.8 2.0 %collective-permute-start.15 = (f32[4,640]{1,0:T(4,128)S(1)}, f32[4,640]{1,0:T(4,128)S(1)}, u32[]{:S(2)}, u32[]{:S(2)}) collective-permute-start(f32[4,640]{1,0:T(4,128)S(1)} %get-tuple-element.33), channel_id=1, source_target_pairs={{0,12},{4,16},{8,20},{12,24},{16,28},{20,0},{24,4},{28,8},{1,13},{... | collective-permute-start | bytes 30728 | tf_op jit(solution)/shard_map/ppermute | solution.py:66
  63.1 1.5 %collective-permute-start.16 = (f32[4,640]{1,0:T(4,128)S(1)}, f32[4,640]{1,0:T(4,128)S(1)}, u32[]{:S(2)}, u32[]{:S(2)}) collective-permute-start(f32[4,640]{1,0:T(4,128)S(1)} %get-tuple-element.34), channel_id=1, source_target_pairs={{0,16},{4,20},{8,24},{12,28},{16,0},{20,4},{24,8},{28,12},{1,17},{... | collective-permute-start | bytes 30728 | tf_op jit(solution)/shard_map/ppermute | solution.py:66
  72.9 1.9 %collective-permute-done.22.refs_3_ = f32[4,640]{1,0:T(4,128)S(1)} collective-permute-done((f32[4,640]{1,0:T(4,128)}, f32[4,640]{1,0:T(4,128)S(1)}, u32[]{:S(2)}, u32[]{:S(2)}) %collective-permute-start.22) | collective-permute-done | bytes 10272 | tf_op jit(solution)/shard_map/ppermute | solution.py:66
  74.8 2.2 %collective-permute-done.21.refs_2_ = f32[4,640]{1,0:T(4,128)S(1)} collective-permute-done((f32[4,640]{1,0:T(4,128)}, f32[4,640]{1,0:T(4,128)S(1)}, u32[]{:S(2)}, u32[]{:S(2)}) %collective-permute-start.21) | collective-permute-done | bytes 10272 | tf_op jit(solution)/shard_map/ppermute | solution.py:66
  79.9 1.4 %collective-permute-start.29 = (f32[4,640]{1,0:T(4,128)}, f32[4,640]{1,0:T(4,128)S(1)}, u32[]{:S(2)}, u32[]{:S(2)}) collective-permute-start(f32[4,640]{1,0:T(4,128)} %add_tensor.1.refs_1_), channel_id=1, source_target_pairs={{0,28},{4,0},{8,4},{12,8},{16,12},{20,16},{24,20},{28,24},{1,29},{... | collective-permute-start | bytes 30728 | tf_op jit(solution)/shard_map/ppermute | solution.py:66
  85.9 1.7 %collective-permute-start.24 = (f32[4,640]{1,0:T(4,128)}, f32[4,640]{1,0:T(4,128)S(1)}, u32[]{:S(2)}, u32[]{:S(2)}) collective-permute-start(f32[4,640]{1,0:T(4,128)} %add_tensor.1.refs_1_), channel_id=1, source_target_pairs={{0,8},{4,12},{8,16},{12,20},{16,24},{20,28},{24,0},{28,4},{1,9},{5... | collective-permute-start | bytes 30728 | tf_op jit(solution)/shard_map/ppermute | solution.py:66
  88.6 2.1 %collective-permute-done.24.refs_3_ = f32[4,640]{1,0:T(4,128)S(1)} collective-permute-done((f32[4,640]{1,0:T(4,128)}, f32[4,640]{1,0:T(4,128)S(1)}, u32[]{:S(2)}, u32[]{:S(2)}) %collective-permute-start.24) | collective-permute-done | bytes 10272 | tf_op jit(solution)/shard_map/ppermute | solution.py:66
  93.2 7.7 %rebuild.2 = (bf16[768,5120]{1,0:T(8,128)(2,1)}, bf16[1,768,5120]{2,1,0:T(8,128)(2,1)}) custom-call(bf16[1,256,768]{2,1,0:T(8,128)(2,1)S(1)} %copy-done.4, bf16[24,768]{1,0:T(8,128)(2,1)S(1)} %get-tuple-element.38.refs_1_, bf16[24,5120]{1,0:T(8,128)(2,1)S(1)} %get-tuple-element.39.refs_2_, bf16[1,768,5120]{2,1,0:T(8,128)(2,1)} %refs_3_.3, ...), custom_call_target="tpu_custom_call" | custom-call | flops 2000000000 | bytes 11796480 | tf_op jit(solution)/shard_map/rebuild/pallas_call | solution.py:400
  100.9 7.7 %rebuild.3 = (bf16[768,5120]{1,0:T(8,128)(2,1)}, bf16[1,768,5120]{2,1,0:T(8,128)(2,1)}) custom-call(bf16[1,256,768]{2,1,0:T(8,128)(2,1)S(1)} %copy-done.4, bf16[24,768]{1,0:T(8,128)(2,1)S(1)} %get-tuple-element.38.refs_1_, bf16[24,5120]{1,0:T(8,128)(2,1)S(1)} %get-tuple-element.39.refs_2_, ...), custom_call_target="tpu_custom_call", output_to_operand_aliasing={{0}: (8, {}), {1}: (9, {})} | custom-call | flops 2000000000 | bytes 11796480 | tf_op jit(solution)/shard_map/rebuild/pallas_call | solution.py:400
  (96 shorter events, 34.4 us)
Async XLA Ops:
  1.8 12.2 %collective-permute-start.33 = (bf16[1,64,2560]{2,1,0:T(8,128)(2,1)S(1)}, bf16[1,64,2560]{2,1,0:T(8,128)(2,1)S(1)}, u32[]{:S(2)}, u32[]{:S(2)}) collective-permute-start(bf16[1,64,2560]{2,1,0:T(8,128)(2,1)S(1)} %get-tuple-element.45), channel_id=1, source_target_pairs={{0,2},{2,3},{3,1},{1,0},{4,6},{6,7},{7,5},{5,4},{8,10},{10,11},{11... | collective-permute-start | bytes 983048 | tf_op jit(solution)/shard_map/ppermute | solution.py:61
  5.9 15.1 %collective-permute-start.30 = (bf16[1,64,2560]{2,1,0:T(8,128)(2,1)S(1)}, bf16[1,64,2560]{2,1,0:T(8,128)(2,1)S(1)}, u32[]{:S(2)}, u32[]{:S(2)}) collective-permute-start(bf16[1,64,2560]{2,1,0:T(8,128)(2,1)S(1)} %get-tuple-element.46), channel_id=1, source_target_pairs={{0,2},{2,3},{3,1},{1,0},{4,6},{6,7},{7,5},{5,4},{8,10},{10,11},{11... | collective-permute-start | bytes 983048 | tf_op jit(solution)/shard_map/ppermute | solution.py:61
  14.0 15.4 %collective-permute-start.34 = (bf16[1,64,2560]{2,1,0:T(8,128)(2,1)S(1)}, bf16[1,64,2560]{2,1,0:T(8,128)(2,1)S(1)}, u32[]{:S(2)}, u32[]{:S(2)}) collective-permute-start(bf16[1,64,2560]{2,1,0:T(8,128)(2,1)S(1)} %collective-permute-done.33.refs_5_), channel_id=1, source_target_pairs={{0,2},{2,3},{3,1},{1,0},{4,6},{6,7},{7,5},{5,4},{8,10},{10,11},{11... | collective-permute-start | bytes 983048 | tf_op jit(solution)/shard_map/ppermute | solution.py:61
  21.0 31.8 %collective-permute-start.31 = (bf16[1,64,2560]{2,1,0:T(8,128)(2,1)S(1)}, bf16[1,64,2560]{2,1,0:T(8,128)(2,1)S(1)}, u32[]{:S(2)}, u32[]{:S(2)}) collective-permute-start(bf16[1,64,2560]{2,1,0:T(8,128)(2,1)S(1)} %collective-permute-done.30.refs_5_), channel_id=1, source_target_pairs={{0,2},{2,3},{3,1},{1,0},{4,6},{6,7},{7,5},{5,4},{8,10},{10,11},{11... | collective-permute-start | bytes 983048 | tf_op jit(solution)/shard_map/ppermute | solution.py:61
  26.7 11.1 %collective-permute-start.2 = (f32[4,64]{1,0:T(4,128)S(1)}, f32[4,64]{1,0:T(4,128)S(1)}, u32[]{:S(2)}, u32[]{:S(2)}) collective-permute-start(f32[4,64]{1,0:T(4,128)S(1)} %token_factor.1.refs_2_), channel_id=1, source_target_pairs={{0,3},{1,0},{2,1},{3,2},{4,7},{5,4},{6,5},{7,6},{8,11},{9,8},{10,9... | collective-permute-start | bytes 3080 | tf_op jit(solution)/shard_map/ppermute | solution.py:66
  28.1 9.7 %collective-permute-start.1 = (f32[4,64]{1,0:T(4,128)S(1)}, f32[4,64]{1,0:T(4,128)S(1)}, u32[]{:S(2)}, u32[]{:S(2)}) collective-permute-start(f32[4,64]{1,0:T(4,128)S(1)} %token_factor.1.refs_2_), channel_id=1, source_target_pairs={{0,2},{1,3},{2,0},{3,1},{4,6},{5,7},{6,4},{7,5},{8,10},{9,11},{10,... | collective-permute-start | bytes 3080 | tf_op jit(solution)/shard_map/ppermute | solution.py:66
  28.1 9.7 %collective-permute-start = (f32[4,64]{1,0:T(4,128)S(1)}, f32[4,64]{1,0:T(4,128)S(1)}, u32[]{:S(2)}, u32[]{:S(2)}) collective-permute-start(f32[4,64]{1,0:T(4,128)S(1)} %token_factor.1.refs_2_), channel_id=1, source_target_pairs={{0,1},{1,2},{2,3},{3,0},{4,5},{5,6},{6,7},{7,4},{8,9},{9,10},{10,1... | collective-permute-start | bytes 3080 | tf_op jit(solution)/shard_map/ppermute | solution.py:66
  29.4 63.8 %collective-permute-start.35 = (bf16[1,64,2560]{2,1,0:T(8,128)(2,1)S(1)}, bf16[1,64,2560]{2,1,0:T(8,128)(2,1)S(1)}, u32[]{:S(2)}, u32[]{:S(2)}) collective-permute-start(bf16[1,64,2560]{2,1,0:T(8,128)(2,1)S(1)} %collective-permute-done.34.refs_6_), channel_id=1, source_target_pairs={{0,2},{2,3},{3,1},{1,0},{4,6},{6,7},{7,5},{5,4},{8,10},{10,11},{11... | collective-permute-start | bytes 983048 | tf_op jit(solution)/shard_map/ppermute | solution.py:61
  38.1 4.3 %collective-permute-start.8 = (f32[4,768]{1,0:T(4,128)S(1)}, f32[4,768]{1,0:T(4,128)S(1)}, u32[]{:S(2)}, u32[]{:S(2)}) collective-permute-start(f32[4,768]{1,0:T(4,128)S(1)} %left.1.refs_1_), channel_id=1, source_target_pairs={{0,24},{4,28},{8,0},{12,4},{16,8},{20,12},{24,16},{28,20},{1,25},{... | collective-permute-start | bytes 36872 | tf_op jit(solution)/shard_map/ppermute | solution.py:66
  43.7 4.6 %collective-permute-start.4 = (f32[4,768]{1,0:T(4,128)S(1)}, f32[4,768]{1,0:T(4,128)S(1)}, u32[]{:S(2)}, u32[]{:S(2)}) collective-permute-start(f32[4,768]{1,0:T(4,128)S(1)} %left.1.refs_1_), channel_id=1, source_target_pairs={{0,8},{4,12},{8,16},{12,20},{16,24},{20,28},{24,0},{28,4},{1,9},{5... | collective-permute-start | bytes 36872 | tf_op jit(solution)/shard_map/ppermute | solution.py:66
  44.6 4.0 %collective-permute-start.3 = (f32[4,768]{1,0:T(4,128)S(1)}, f32[4,768]{1,0:T(4,128)S(1)}, u32[]{:S(2)}, u32[]{:S(2)}) collective-permute-start(f32[4,768]{1,0:T(4,128)S(1)} %left.1.refs_1_), channel_id=1, source_target_pairs={{0,4},{4,8},{8,12},{12,16},{16,20},{20,24},{24,28},{28,0},{1,5},{5... | collective-permute-start | bytes 36872 | tf_op jit(solution)/shard_map/ppermute | solution.py:66
  48.9 8.7 %collective-permute-start.10 = (f32[8,128]{1,0:T(8,128)S(1)}, f32[8,128]{1,0:T(8,128)S(1)}, u32[]{:S(2)}, u32[]{:S(2)}) collective-permute-start(f32[8,128]{1,0:T(8,128)S(1)} %get-tuple-element.26), channel_id=1, source_target_pairs={{0,1},{1,2},{2,3},{3,0},{4,5},{5,6},{6,7},{7,4},{8,9},{9,10},{10,1... | collective-permute-start | bytes 12296 | tf_op jit(solution)/shard_map/ppermute | solution.py:66
  49.0 8.6 %collective-permute-start.11 = (f32[8,128]{1,0:T(8,128)S(1)}, f32[8,128]{1,0:T(8,128)S(1)}, u32[]{:S(2)}, u32[]{:S(2)}) collective-permute-start(f32[8,128]{1,0:T(8,128)S(1)} %get-tuple-element.27), channel_id=1, source_target_pairs={{0,2},{1,3},{2,0},{3,1},{4,6},{5,7},{6,4},{7,5},{8,10},{9,11},{10,... | collective-permute-start | bytes 12296 | tf_op jit(solution)/shard_map/ppermute | solution.py:66
  51.8 5.9 %collective-permute-start.12 = (f32[8,128]{1,0:T(8,128)S(1)}, f32[8,128]{1,0:T(8,128)S(1)}, u32[]{:S(2)}, u32[]{:S(2)}) collective-permute-start(f32[8,128]{1,0:T(8,128)S(1)} %get-tuple-element.28), channel_id=1, source_target_pairs={{0,3},{1,0},{2,1},{3,2},{4,7},{5,4},{6,5},{7,6},{8,11},{9,8},{10,9... | collective-permute-start | bytes 12296 | tf_op jit(solution)/shard_map/ppermute | solution.py:66
  52.8 48.1 %collective-permute-start.32 = (bf16[1,64,2560]{2,1,0:T(8,128)(2,1)S(1)}, bf16[1,64,2560]{2,1,0:T(8,128)(2,1)S(1)}, u32[]{:S(2)}, u32[]{:S(2)}) collective-permute-start(bf16[1,64,2560]{2,1,0:T(8,128)(2,1)S(1)} %collective-permute-done.31.refs_6_), channel_id=1, source_target_pairs={{0,2},{2,3},{3,1},{1,0},{4,6},{6,7},{7,5},{5,4},{8,10},{10,11},{11... | collective-permute-start | bytes 983048 | tf_op jit(solution)/shard_map/ppermute | solution.py:61
  59.1 4.0 %collective-permute-start.13 = (f32[4,640]{1,0:T(4,128)S(1)}, f32[4,640]{1,0:T(4,128)S(1)}, u32[]{:S(2)}, u32[]{:S(2)}) collective-permute-start(f32[4,640]{1,0:T(4,128)S(1)} %get-tuple-element.31), channel_id=1, source_target_pairs={{0,4},{4,8},{8,12},{12,16},{16,20},{20,24},{24,28},{28,0},{1,5},{5... | collective-permute-start | bytes 30728 | tf_op jit(solution)/shard_map/ppermute | solution.py:66
  59.1 5.5 %collective-permute-start.14 = (f32[4,640]{1,0:T(4,128)S(1)}, f32[4,640]{1,0:T(4,128)S(1)}, u32[]{:S(2)}, u32[]{:S(2)}) collective-permute-start(f32[4,640]{1,0:T(4,128)S(1)} %get-tuple-element.32), channel_id=1, source_target_pairs={{0,8},{4,12},{8,16},{12,20},{16,24},{20,28},{24,0},{28,4},{1,9},{5... | collective-permute-start | bytes 30728 | tf_op jit(solution)/shard_map/ppermute | solution.py:66
  59.8 4.8 %collective-permute-start.15 = (f32[4,640]{1,0:T(4,128)S(1)}, f32[4,640]{1,0:T(4,128)S(1)}, u32[]{:S(2)}, u32[]{:S(2)}) collective-permute-start(f32[4,640]{1,0:T(4,128)S(1)} %get-tuple-element.33), channel_id=1, source_target_pairs={{0,12},{4,16},{8,20},{12,24},{16,28},{20,0},{24,4},{28,8},{1,13},{... | collective-permute-start | bytes 30728 | tf_op jit(solution)/shard_map/ppermute | solution.py:66
  72.2 4.8 %collective-permute-start.21 = (f32[4,640]{1,0:T(4,128)}, f32[4,640]{1,0:T(4,128)S(1)}, u32[]{:S(2)}, u32[]{:S(2)}) collective-permute-start(f32[4,640]{1,0:T(4,128)} %add_dp.1.refs_0_), channel_id=1, source_target_pairs={{0,2},{1,3},{2,0},{3,1},{4,6},{5,7},{6,4},{7,5},{8,10},{9,11},{10,... | collective-permute-start | bytes 30728 | tf_op jit(solution)/shard_map/ppermute | solution.py:66
  72.3 5.7 %collective-permute-start.20 = (f32[4,640]{1,0:T(4,128)}, f32[4,640]{1,0:T(4,128)S(1)}, u32[]{:S(2)}, u32[]{:S(2)}) collective-permute-start(f32[4,640]{1,0:T(4,128)} %add_dp.1.refs_0_), channel_id=1, source_target_pairs={{0,1},{1,2},{2,3},{3,0},{4,5},{5,6},{6,7},{7,4},{8,9},{9,10},{10,1... | collective-permute-start | bytes 30728 | tf_op jit(solution)/shard_map/ppermute | solution.py:66
  81.7 4.1 %collective-permute-start.27 = (f32[4,640]{1,0:T(4,128)}, f32[4,640]{1,0:T(4,128)S(1)}, u32[]{:S(2)}, u32[]{:S(2)}) collective-permute-start(f32[4,640]{1,0:T(4,128)} %add_tensor.1.refs_1_), channel_id=1, source_target_pairs={{0,20},{4,24},{8,28},{12,0},{16,4},{20,8},{24,12},{28,16},{1,21},{... | collective-permute-start | bytes 30728 | tf_op jit(solution)/shard_map/ppermute | solution.py:66
  83.0 4.6 %collective-permute-start.26 = (f32[4,640]{1,0:T(4,128)}, f32[4,640]{1,0:T(4,128)S(1)}, u32[]{:S(2)}, u32[]{:S(2)}) collective-permute-start(f32[4,640]{1,0:T(4,128)} %add_tensor.1.refs_1_), channel_id=1, source_target_pairs={{0,16},{4,20},{8,24},{12,28},{16,0},{20,4},{24,8},{28,12},{1,17},{... | collective-permute-start | bytes 30728 | tf_op jit(solution)/shard_map/ppermute | solution.py:66
  85.9 4.8 %collective-permute-start.24 = (f32[4,640]{1,0:T(4,128)}, f32[4,640]{1,0:T(4,128)S(1)}, u32[]{:S(2)}, u32[]{:S(2)}) collective-permute-start(f32[4,640]{1,0:T(4,128)} %add_tensor.1.refs_1_), channel_id=1, source_target_pairs={{0,8},{4,12},{8,16},{12,20},{16,24},{20,28},{24,0},{28,4},{1,9},{5... | collective-permute-start | bytes 30728 | tf_op jit(solution)/shard_map/ppermute | solution.py:66
  87.6 4.2 %collective-permute-start.23 = (f32[4,640]{1,0:T(4,128)}, f32[4,640]{1,0:T(4,128)S(1)}, u32[]{:S(2)}, u32[]{:S(2)}) collective-permute-start(f32[4,640]{1,0:T(4,128)} %add_tensor.1.refs_1_), channel_id=1, source_target_pairs={{0,4},{4,8},{8,12},{12,16},{16,20},{20,24},{24,28},{28,0},{1,5},{5... | collective-permute-start | bytes 30728 | tf_op jit(solution)/shard_map/ppermute | solution.py:66
  (30 other events, 157.6 us)

commit v2 on v0

v2 whole, which is shorter than its diff:
```python
import functools

import jax
import jax.numpy as jnp
from jax import lax
from jax.experimental import pallas as pl
from jax.experimental.pallas import tpu as pltpu
from jax.sharding import PartitionSpec as P

F32 = jnp.float32
BF16 = jnp.bfloat16
SHRINK = 2.0**-23
TINY = 1e-30
BLOCK = 512


def params(mib):
    return pltpu.CompilerParams(vmem_limit_bytes=mib * 2**20)


def cost(flops, moved):
    return pl.CostEstimate(flops=int(flops), bytes_accessed=int(moved), transcendentals=0)


def dot(a, b, contract):
    return lax.dot_general(a, b, ((contract[:1], contract[1:]), ((), ())), preferred_element_type=F32)


def split(x):
    hi = x.astype(BF16)
    rest = x - hi.astype(F32)
    mid = rest.astype(BF16)
    lo = (rest - mid.astype(F32)).astype(BF16)
    return hi.astype(F32), mid.astype(F32), lo.astype(F32)


def stack3(x, ref):
    rank = x.shape[0]
    for i, part in enumerate(split(x)):
        ref[i * rank : (i + 1) * rank, :] = part
    return ref[...].astype(BF16)


def sum3(y, rank):
    return (y[2 * rank :] + y[rank : 2 * rank]) + y[:rank]


def ring_of(n):
    return [2 * p if 2 * p < n else 2 * (n - p) - 1 for p in range(n)]


def ring_source(me, step, n):
    place = jnp.where(lax.rem(me, 2) == 0, me // 2, n - (me + 1) // 2)
    place = lax.rem(place - step + n, n)
    return jnp.where(2 * place < n, 2 * place, 2 * (n - place) - 1)


def ring_step(x, axis, n):
    ring = ring_of(n)
    return lax.ppermute(x, axis, [(ring[p], ring[(p + 1) % n]) for p in range(n)])


def exchange(stack, axis):
    return lax.all_to_all(stack, axis, 0, 0)


def token_factor_kernel(w_hbm, g_hbm, out_ref, parts_ref, w, g, w3, sems):
    rank = w.shape[0]
    copies = [
        pltpu.make_async_copy(w_hbm, w, sems.at[0]),
        pltpu.make_async_copy(g_hbm, g, sems.at[1]),
    ]
    for copy in copies:
        copy.start()
    copies[0].wait()
    parts = stack3(w[...] * SHRINK, w3)
    parts_ref[...] = parts
    copies[1].wait()
    gw = sum3(dot(parts, g[0], (1, 1)), rank)
    for k in range(out_ref.shape[0]):
        out_ref[k, 0:rank, 0 : gw.shape[1]] = gw


def error_left_kernel(w_ref, e_hbm, out_ref, e_ref, sems):
    rank = out_ref.shape[0]
    chunks = sems.shape[0]
    high = e_ref.shape[1] // chunks
    copies = []
    for c in range(chunks):
        rows = pl.ds(c * high, high)
        copies.append(pltpu.make_async_copy(e_hbm.at[:, rows, :], e_ref.at[:, rows, :], sems.at[c]))
        copies[-1].start()
    parts = w_ref[...]
    for c in range(chunks):
        copies[c].wait()
        rows = slice(c * high, (c + 1) * high)
        out_ref[:, rows] = sum3(dot(parts, e_ref[0, rows, :], (1, 1)), rank)


def left_kernel(a_ref, e_ref, gw_ref, out_ref, g3):
    n = gw_ref.shape[0]
    rank = e_ref.shape[0]
    tok = a_ref.shape[1] // n
    total = e_ref[...]
    for t in range(n):
        rows = a_ref[0, t * tok : (t + 1) * tok, :]
        total += sum3(dot(stack3(gw_ref[t, 0:rank, 0:tok], g3), rows, (1, 0)), rank)
    for r in range(out_ref.shape[0]):
        out_ref[r] = total


def mean_kernel(a_ref, left_ref, p_ref, msg_ref, p3):
    m, rank, _ = left_ref.shape
    n = msg_ref.shape[0]
    tok = a_ref.shape[1] // n
    total = left_ref[0]
    for r in range(1, m):
        total += left_ref[r]
    mean = total * (1.0 / (SHRINK * m))
    p_ref[...] = mean
    top = jnp.max(jnp.max(jnp.abs(mean), axis=1, keepdims=True), axis=0, keepdims=True)
    top = jnp.maximum(top, TINY)
    parts = stack3(mean / (top * 1024.0), p3)
    gram = [jnp.sum(mean * mean[i : i + 1, :], axis=1, keepdims=True) for i in range(rank)]
    msg_ref[...] = jnp.zeros_like(msg_ref)
    for t in range(n):
        y = dot(parts, a_ref[0, t * tok : (t + 1) * tok, :], (1, 1))
        msg_ref[t, 0:rank, 0:tok] = sum3(y, rank)
        for i in range(rank):
            msg_ref[t, rank : 2 * rank, i : i + 1] = gram[i]
        msg_ref[t, rank : rank + 1, rank : rank + 1] = top


def error_right_kernel(p_ref, e_ref, out_ref, p3):
    rank = p_ref.shape[0]
    parts = stack3(p_ref[...], p3)
    for c in range(e_ref.shape[2] // BLOCK):
        cols = slice(c * BLOCK, (c + 1) * BLOCK)
        out_ref[:, cols] = sum3(dot(parts, e_ref[0, :, cols], (1, 0)), rank)


def lower_inverse(gram, rank):
    at = lambda i, j: gram[i : i + 1, j : j + 1]
    low = {}
    for j in range(rank):
        d = at(j, j)
        for k in range(j):
            d = d - low[j, k] * low[j, k]
        low[j, j] = jnp.sqrt(d)
        for i in range(j + 1, rank):
            v = at(i, j)
            for k in range(j):
                v = v - low[i, k] * low[j, k]
            low[i, j] = v / low[j, j]
    inv = {}
    for j in range(rank):
        inv[j, j] = 1.0 / low[j, j]
        for i in range(j + 1, rank):
            v = low[i, j] * inv[j, j]
            for k in range(j + 1, i):
                v = v + low[i, k] * inv[k, j]
            inv[i, j] = -v / low[i, i]
    return inv


def solve_rows(inv, x, rank):
    rows = []
    for i in range(rank):
        row = inv[i, 0] * x[0:1, :]
        for j in range(1, i + 1):
            row = row + inv[i, j] * x[j : j + 1, :]
        rows.append(row)
    return rows


def right_kernel(p_ref, r_ref, g_ref, msg_ref, ortho_ref, out_ref, z, z3, whole):
    n = msg_ref.shape[0]
    m, rank, cut = out_ref.shape
    tok = g_ref.shape[1]
    gram = msg_ref[0, rank : 2 * rank, 0:rank]
    for t in range(1, n):
        gram = gram + msg_ref[t, rank : 2 * rank, 0:rank]
    inv = lower_inverse(gram, rank)
    for t in range(n):
        top = msg_ref[t, rank : rank + 1, rank : rank + 1]
        scaled = {key: value * top for key, value in inv.items()}
        for i, row in enumerate(solve_rows(scaled, msg_ref[t, 0:rank, 0:tok], rank)):
            if t == 0:
                z[i : i + 1, :] = row
            else:
                z[i : i + 1, :] += row
    for i, row in enumerate(solve_rows(inv, p_ref[...], rank)):
        ortho_ref[i : i + 1, :] = row
    for i, row in enumerate(solve_rows(inv, r_ref[...], rank)):
        whole[i : i + 1, :] = row
    whole[...] += sum3(dot(stack3(z[...], z3), g_ref[0], (1, 0)), rank) * 1024.0
    for r in range(m):
        out_ref[r] = whole[:, r * cut : (r + 1) * cut]


def add_kernel(scale, in_ref, out_ref):
    total = in_ref[0]
    for i in range(1, in_ref.shape[0]):
        total += in_ref[i]
    total = total * scale
    for i in range(out_ref.shape[0]):
        out_ref[i] = total


LEFT_TERMS = (0, 0, 1, 0, 2, 1)
RIGHT_TERMS = (0, 1, 0, 2, 0, 1)


def factor_kernel(ortho_ref, in_ref, whole_ref, left_ref, right_ref, left, right):
    m, rank, cut = in_ref.shape
    for r in range(m):
        whole_ref[:, r * cut : (r + 1) * cut] = in_ref[r]
    for terms, x, ref in (
        (LEFT_TERMS, ortho_ref[...], left),
        (RIGHT_TERMS, whole_ref[...], right),
    ):
        parts = split(x)
        for i, term in enumerate(terms):
            ref[i * rank : (i + 1) * rank, :] = parts[term]
    left_ref[...] = left[...].T.astype(BF16)
    right_ref[...] = right[...].astype(BF16)


def final_kernel(n, *refs):
    a_ref, left_ref, right_ref, e_ref = refs[:4]
    slots = refs[4 : 4 + n]
    rebuilt_ref, error_ref, acts, acts_t = refs[4 + n :]
    tok = slots[0].shape[1]
    me = lax.axis_index("tensor")
    step = pl.program_id(0)

    @pl.when(step == 0)
    def _():
        for s in range(n):
            src = ring_source(me, s, n)
            rows = a_ref[0, pl.ds(pl.multiple_of(src * tok, tok), tok), :]
            acts[s * tok : (s + 1) * tok, :] = rows
        acts_t[...] = acts[...].T

    cols = pl.ds(pl.multiple_of(step * BLOCK, BLOCK), BLOCK)
    grads = jnp.concatenate([slot[0, :, cols] for slot in slots], axis=0)
    matrix = dot(acts_t[...], grads, (1, 0)) + e_ref[0, :, cols].astype(F32)
    rebuilt = dot(left_ref[...], right_ref[:, cols], (1, 0))
    rebuilt_ref[...] = rebuilt.astype(BF16)
    error_ref[0] = (matrix - rebuilt).astype(BF16)


def per_device(activations, out_grads, error_buffer, warm_factor):
    m = lax.axis_size("dp")
    n = lax.axis_size("tensor")
    _, tokens, rows = activations.shape
    _, tok, width = out_grads.shape
    rank = warm_factor.shape[1]
    cut = width // m
    w = warm_factor.T
    sds = jax.ShapeDtypeStruct
    hbm = pl.BlockSpec(memory_space=pltpu.HBM)
    vmem = pl.BlockSpec(memory_space=pltpu.VMEM)
    dma = pltpu.SemaphoreType.DMA
    pin = lambda x: pltpu.with_memory_space_constraint(x, pltpu.HBM)

    def call(kernel, shapes, scratch, name, flops, moved, specs=None, mib=16):
        return pl.pallas_call(
            kernel,
            out_shape=shapes,
            **({"in_specs": specs} if specs else {}),
            scratch_shapes=scratch,
            compiler_params=params(mib),
            cost_estimate=cost(flops, moved),
            name=name,
        )

    gw, w_parts = call(
        token_factor_kernel,
        [sds((n, 8, 128), F32), sds((3 * rank, width), BF16)],
        [
            pltpu.VMEM((rank, width), F32),
            pltpu.VMEM((1, tok, width), BF16),
            pltpu.VMEM((3 * rank, width), F32),
            dma((2,)),
        ],
        "token_factor", 2e6, 1e6, [hbm, hbm],
    )(pin(w), pin(out_grads))
    gw = exchange(gw, "tensor")
    held = [out_grads]
    held.append(ring_step(held[-1], "tensor", n))

    ew, error_v = call(
        error_left_kernel,
        [sds((rank, rows), F32), sds((1, rows, width), BF16)],
        [dma((6,))],
        "error_left", 2e9, rows * width * 2, [vmem, hbm],
    )(w_parts, pin(error_buffer))

    left = call(
        left_kernel, sds((m, rank, rows), F32), [pltpu.VMEM((3 * rank, tok), F32)], "left", 1e7, 1e6
    )(activations, ew, gw)
    left = exchange(left, "dp")
    left, held[-1] = lax.optimization_barrier((left, held[-1]))
    held.append(ring_step(held[-1], "tensor", n))

    mean, msg = call(
        mean_kernel,
        [sds((rank, rows), F32), sds((n, 8, 128), F32)],
        [pltpu.VMEM((3 * rank, rows), F32)],
        "mean", 1e7, 1e6,
    )(activations, left)
    msg = exchange(msg, "tensor")

    right_raw = call(
        error_right_kernel,
        sds((rank, width), F32),
        [pltpu.VMEM((3 * rank, rows), F32)],
        "error_right", 2e9, rows * width * 2,
    )(mean, error_v)
    right_raw, held[-1] = lax.optimization_barrier((right_raw, held[-1]))
    for _ in range(3, n):
        held.append(ring_step(held[-1], "tensor", n))

    ortho, pieces = call(
        right_kernel,
        [sds((rank, rows), F32), sds((m, rank, cut), F32)],
        [
            pltpu.VMEM((rank, tok), F32),
            pltpu.VMEM((3 * rank, tok), F32),
            pltpu.VMEM((rank, width), F32),
        ],
        "right", 1e7, 1e6,
    )(mean, right_raw, out_grads, msg)
    pieces = exchange(pieces, "dp")
    pieces = call(
        functools.partial(add_kernel, 1.0), sds((n, rank, cut), F32), [], "add_dp", 1e5, 1e5
    )(pieces)
    pieces = exchange(pieces, "tensor")
    pieces = call(
        functools.partial(add_kernel, 1.0 / m), sds((m, rank, cut), F32), [], "add_tensor", 1e5, 1e5
    )(pieces)
    pieces = exchange(pieces, "dp")

    terms = len(LEFT_TERMS) * rank
    whole, left_terms, right_terms = call(
        factor_kernel,
        [sds((rank, width), F32), sds((rows, terms), BF16), sds((terms, width), BF16)],
        [pltpu.VMEM((terms, rows), F32), pltpu.VMEM((terms, width), F32)],
        "factor", 1e6, 1e6,
    )(ortho, pieces)

    rebuilt, error = pl.pallas_call(
        functools.partial(final_kernel, n),
        grid=(width // BLOCK,),
        in_specs=[vmem] * (4 + n),
        out_specs=[
            pl.BlockSpec((rows, BLOCK), lambda i: (0, i)),
            pl.BlockSpec((1, rows, BLOCK), lambda i: (0, 0, i)),
        ],
        out_shape=[sds((rows, width), BF16), sds((1, rows, width), BF16)],
        scratch_shapes=[pltpu.VMEM((tokens, rows), BF16), pltpu.VMEM((rows, tokens), BF16)],
        compiler_params=params(24),
        cost_estimate=cost(4e9, rows * width * 6),
        name="rebuild",
    )(activations, left_terms, right_terms, error_v, *held)
    return rebuilt, error, whole.T


def solution(mesh):
    return jax.shard_map(
        per_device,
        mesh=mesh,
        in_specs=(P("dp", None, "tensor"), P("dp", "tensor", None), P("dp", "tensor", None), P()),
        out_specs=(P("tensor", None), P("dp", "tensor", None), P()),
        check_vma=False,
    )
```

time: 283 us -> 99.1 us (0.35)
  waiting for transfers between devices: 176 us -> 13.5 us
  matrix products: 49.5 us -> 0 us
  Pallas kernels: 0 us -> 18.7 us
  blocking collectives: 33.6 us -> 47.9 us
  between operations: 14.1 us -> 0.71 us
  starting transfers between devices: 0.08 us -> 11.3 us
  other arithmetic: 2.94 us -> 0 us
    psum x1 -> x0, waiting for transfers between devices: 116 us -> none  [per_device(): next_factor = lax.psum(right_part, ('dp', 'tensor')) / replicas]
    all_gather x1 -> x0, waiting for transfers between devices: 59.2 us -> none  [per_device(): lax.all_gather(out_grads, 'tensor', axis=1, tiled=True)[0]]
    dot_general x5 -> x0, matrix products: 49.3 us -> none  [the longest x1 18.1 us: per_device(): rebuilt = jnp.dot(left_ortho, next_factor.T, precision=high)]
    all_to_all x0 -> x5, blocking collectives: none -> 47.9 us  [exchange(): return lax.all_to_all(stack, axis, 0, 0)]
    psum x2 -> x0, blocking collectives: 33.6 us -> none  [the longest x1 24 us: per_device(): left_mean = lax.psum(left_part, 'dp') / replicas]
    pallas_call x0 -> x10, Pallas kernels: none -> 18.7 us  [the longest x1 9.31 us: per_device(): pl.pallas_call(functools.partial(final_kernel, n), grid=(width // BLOCK,)...]
    ppermute x0 -> x3, waiting for transfers between devices: none -> 9.99 us  [ring_step(): lax.ppermute(x, axis, [(ring[p], ring[(p + 1) % n]) for p in range(n)])]
    ppermute x0 -> x3, starting transfers between devices: none -> 8.05 us  [ring_step(): lax.ppermute(x, axis, [(ring[p], ring[(p + 1) % n]) for p in range(n)])]
  transfers between devices with their start and end apart: 2 -> 4, of which waited for: 2 -> 2; matrix products, arithmetic and copies ran while one was open for 0% -> 0% of each run, Pallas kernels for 0% -> 10%
where the time goes in v2:
time: 99.1 us; the launch traced here: 98.7 us
  blocking collectives  47.9 us (48%)
  Pallas kernels  18.7 us (19%)
  waiting for transfers between devices  13.5 us (14%)
  starting transfers between devices  11.3 us (11%)
  local copies, waits for them, and re-layouts  6.48 us (7%)
    all_to_all x5, blocking collectives, exchange(): return lax.all_to_all(stack, axis, 0, 0)  47.9 us
    ppermute x3, waiting for transfers between devices, ring_step(): lax.ppermute(x, axis, [(ring[p], ring[(p + 1) % n]) for p in range(n)])  9.99 us
    pallas_call x1, Pallas kernels, per_device(): pl.pallas_call(functools.partial(final_kernel, n), grid=(width // BLOCK,)...  9.31 us
    ppermute x3, starting transfers between devices, ring_step(): lax.ppermute(x, axis, [(ring[p], ring[(p + 1) % n]) for p in range(n)])  8.05 us
    unnamed x10, local copies, waits for them, and re-layouts  6.48 us
    pallas_call x1, Pallas kernels, per_device(): call(error_left_kernel, [sds((rank, rows), F32), sds((1, rows, width), BF...  4.21 us
    all_to_all x1, waiting for transfers between devices, exchange(): return lax.all_to_all(stack, axis, 0, 0)  3.54 us
    all_to_all x1, starting transfers between devices, exchange(): return lax.all_to_all(stack, axis, 0, 0)  3.27 us
  transfers between devices with their start and end apart: 4, of which 2 were waited for; matrix products, arithmetic and copies ran while one was open for 0% of the time, Pallas kernels for 10%

profile of v2, /device:TPU:0, one launch (start us, length us, event | category | flops | bytes accessed | tf_op | source)
XLA Modules:
  0.0 98.7 jit_solution(12826868435753050066)
XLA Ops:
  0.6 4.1 %collective-permute-start = (bf16[1,64,5120]{2,1,0:T(8,128)(2,1)}, bf16[1,64,5120]{2,1,0:T(8,128)(2,1)S(1)}, u32[]{:S(2)}, u32[]{:S(2)}) collective-permute-start(bf16[1,64,5120]{2,1,0:T(8,128)(2,1)} %refs_4_.1), channel_id=1, source_target_pairs={{0,2},{2,3},{3,1},{1,0},{4,6},{6,7},{7,5},{5,4},{8,10},{10,11},{11... | collective-permute-start | bytes 1966088 | tf_op jit(solution)/shard_map/ppermute | solution.py:60
  4.7 2.1 %token_factor.1 = (f32[4,8,128]{2,1,0:T(8,128)}, bf16[12,5120]{1,0:T(8,128)(2,1)S(1)}) custom-call(f32[4,5120]{1,0:T(4,128)} %bitcast.2, bf16[1,64,5120]{2,1,0:T(8,128)(2,1)} %refs_4_.1), custom_call_target="tpu_custom_call" | custom-call | flops 2000000 | bytes 1000000 | tf_op jit(solution)/shard_map/token_factor/pallas_call | solution.py:278
  6.8 3.3 %all-to-all-start = ((f32[4,8,128]{2,1,0:T(8,128)}), f32[4,8,128]{2,1,0:T(8,128)S(1)}, u32[]{:S(2)}, u32[]{:S(2)}) async-start(f32[4,8,128]{2,1,0:T(8,128)} %get-tuple-element.22), calls=%async_computation | async-start | bytes 32768 | tf_op jit(solution)/shard_map/all_to_all | solution.py:64
  10.1 0.0 copy-start.3
  10.1 4.2 %error_left.1 = (f32[4,768]{1,0:T(4,128)S(1)}, bf16[1,768,5120]{2,1,0:T(8,128)(2,1)S(1)}) custom-call(bf16[12,5120]{1,0:T(8,128)(2,1)S(1)} %get-tuple-element.20.w_ref, bf16[1,768,5120]{2,1,0:T(8,128)(2,1)} %e_hbm.1), custom_call_target="tpu_custom_call" | custom-call | flops 2000000000 | bytes 7864320 | tf_op jit(solution)/shard_map/error_left/pallas_call | solution.py:293
  14.3 0.0 copy-start
  14.3 3.2 %copy-done = bf16[1,768,5120]{2,1,0:T(8,128)(2,1)} copy-done((bf16[1,768,5120]{2,1,0:T(8,128)(2,1)}, bf16[1,768,5120]{2,1,0:T(8,128)(2,1)S(1)}, u32[]{:S(2)}) %copy-start) | copy-done | bytes 7864344
  17.5 3.5 %all-to-all-done.gw_ref = f32[4,8,128]{2,1,0:T(8,128)S(1)} async-done(((f32[4,8,128]{2,1,0:T(8,128)}), f32[4,8,128]{2,1,0:T(8,128)S(1)}, u32[]{:S(2)}, u32[]{:S(2)}) %all-to-all-start) | async-done | bytes 16416 | tf_op jit(solution)/shard_map/all_to_all | solution.py:64
  21.1 0.2 left.1
  21.3 8.7 %all_to_all.30.left_ref = f32[8,4,768]{2,1,0:T(4,128)S(1)} all-to-all(f32[8,4,768]{2,1,0:T(4,128)S(1)} %left.1), channel_id=1, replica_groups=mesh['dp'=8,'tensor'=4] {'dp'}, dimensions={0} | all-to-all | bytes 196608 | tf_op jit(solution)/shard_map/all_to_all | solution.py:64
  30.0 1.5 %collective-permute-start.1 = (bf16[1,64,5120]{2,1,0:T(8,128)(2,1)S(1)}, bf16[1,64,5120]{2,1,0:T(8,128)(2,1)S(1)}, u32[]{:S(2)}, u32[]{:S(2)}) collective-permute-start(bf16[1,64,5120]{2,1,0:T(8,128)(2,1)S(1)} %collective-permute-done.refs_5_), channel_id=1, source_target_pairs={{0,2},{2,3},{3,1},{1,0},{4,6},{6,7},{7,5},{5,4},{8,10},{10,11},{11... | collective-permute-start | bytes 1966088 | tf_op jit(solution)/shard_map/ppermute | solution.py:60
  31.5 0.3 mean.1
  31.8 0.0 copy-start.1
  31.9 3.2 %copy-done.1 = bf16[1,768,5120]{2,1,0:T(8,128)(2,1)S(1)} copy-done((bf16[1,768,5120]{2,1,0:T(8,128)(2,1)S(1)}, bf16[1,768,5120]{2,1,0:T(8,128)(2,1)}, u32[]{:S(2)}) %copy-start.1) | copy-done | bytes 7864344
  35.1 1.1 %error_right.1.r_ref = f32[4,5120]{1,0:T(4,128)S(1)} custom-call(f32[4,768]{1,0:T(4,128)S(1)} %get-tuple-element.24.p_ref, bf16[1,768,5120]{2,1,0:T(8,128)(2,1)S(1)} %copy-done.1), custom_call_target="tpu_custom_call" | custom-call | flops 2000000000 | bytes 7864320 | tf_op jit(solution)/shard_map/error_right/pallas_call | solution.py:315
  36.2 10.0 %collective-permute-done.1.refs_6_ = bf16[1,64,5120]{2,1,0:T(8,128)(2,1)S(1)} collective-permute-done((bf16[1,64,5120]{2,1,0:T(8,128)(2,1)S(1)}, bf16[1,64,5120]{2,1,0:T(8,128)(2,1)S(1)}, u32[]{:S(2)}, u32[]{:S(2)}) %collective-permute-start.1) | collective-permute-done | bytes 655392 | tf_op jit(solution)/shard_map/ppermute | solution.py:60
  46.2 2.4 %collective-permute-start.2 = (bf16[1,64,5120]{2,1,0:T(8,128)(2,1)S(1)}, bf16[1,64,5120]{2,1,0:T(8,128)(2,1)S(1)}, u32[]{:S(2)}, u32[]{:S(2)}) collective-permute-start(bf16[1,64,5120]{2,1,0:T(8,128)(2,1)S(1)} %collective-permute-done.1.refs_6_), channel_id=1, source_target_pairs={{0,2},{2,3},{3,1},{1,0},{4,6},{6,7},{7,5},{5,4},{8,10},{10,11},{11... | collective-permute-start | bytes 1966088 | tf_op jit(solution)/shard_map/ppermute | solution.py:60
  48.6 15.0 %all_to_all.31.msg_ref = f32[4,8,128]{2,1,0:T(8,128)S(1)} all-to-all(f32[4,8,128]{2,1,0:T(8,128)S(1)} %get-tuple-element.28), channel_id=1, replica_groups=mesh['dp'=8,'tensor'=4] {'tensor'}, dimensions={0} | all-to-all | bytes 32768 | tf_op jit(solution)/shard_map/all_to_all | solution.py:64
  63.6 0.8 right.1
  64.5 7.5 %all_to_all.32.in_ref = f32[8,4,640]{2,1,0:T(4,128)S(1)} all-to-all(f32[8,4,640]{2,1,0:T(4,128)S(1)} %get-tuple-element.30), channel_id=1, replica_groups=mesh['dp'=8,'tensor'=4] {'dp'}, dimensions={0} | all-to-all | bytes 163840 | tf_op jit(solution)/shard_map/all_to_all | solution.py:64
  72.0 9.2 %all_to_all.33.in_ref = f32[4,4,640]{2,1,0:T(4,128)S(1)} all-to-all(f32[4,4,640]{2,1,0:T(4,128)S(1)} %add_dp.1), channel_id=1, replica_groups=mesh['dp'=8,'tensor'=4] {'tensor'}, dimensions={0} | all-to-all | bytes 81920 | tf_op jit(solution)/shard_map/all_to_all | solution.py:64
  81.2 7.5 %all_to_all.34.in_ref = f32[8,4,640]{2,1,0:T(4,128)S(1)} all-to-all(f32[8,4,640]{2,1,0:T(4,128)S(1)} %add_tensor.1), channel_id=1, replica_groups=mesh['dp'=8,'tensor'=4] {'dp'}, dimensions={0} | all-to-all | bytes 163840 | tf_op jit(solution)/shard_map/all_to_all | solution.py:64
  88.7 0.7 factor.1
  89.3 9.3 %rebuild.1 = (bf16[768,5120]{1,0:T(8,128)(2,1)}, bf16[1,768,5120]{2,1,0:T(8,128)(2,1)}) custom-call(bf16[1,256,768]{2,1,0:T(8,128)(2,1)S(1)} %copy-done.4, bf16[768,24]{1,0:T(8,128)(2,1)S(1)} %get-tuple-element.31.refs_1_, bf16[24,5120]{1,0:T(8,128)(2,1)S(1)} %get-tuple-element.32.refs_2_, bf16[1,768,5120]{2,1,0:T(8,128)(2,1)S(1)} %copy-done.2, ...), custom_call_target="tpu_custom_call" | custom-call | flops 4000000000 | bytes 23592960 | tf_op jit(solution)/shard_map/rebuild/pallas_call | solution.py:353
  (9 shorter events, 0.0 us)
Async XLA Ops:
  0.6 20.5 %copy-start.4 = (bf16[1,256,768]{2,1,0:T(8,128)(2,1)S(1)}, bf16[1,256,768]{2,1,0:T(8,128)(2,1)}, u32[]{:S(2)}) copy-start(bf16[1,256,768]{2,1,0:T(8,128)(2,1)} %refs_0_.1) | copy-start | bytes 1179652
  0.6 29.4 %collective-permute-start = (bf16[1,64,5120]{2,1,0:T(8,128)(2,1)}, bf16[1,64,5120]{2,1,0:T(8,128)(2,1)S(1)}, u32[]{:S(2)}, u32[]{:S(2)}) collective-permute-start(bf16[1,64,5120]{2,1,0:T(8,128)(2,1)} %refs_4_.1), channel_id=1, source_target_pairs={{0,2},{2,3},{3,1},{1,0},{4,6},{6,7},{7,5},{5,4},{8,10},{10,11},{11... | collective-permute-start | bytes 1966088 | tf_op jit(solution)/shard_map/ppermute | solution.py:60
  6.8 14.3 %all-to-all-start = ((f32[4,8,128]{2,1,0:T(8,128)}), f32[4,8,128]{2,1,0:T(8,128)S(1)}, u32[]{:S(2)}, u32[]{:S(2)}) async-start(f32[4,8,128]{2,1,0:T(8,128)} %get-tuple-element.22), calls=%async_computation | async-start | bytes 32768 | tf_op jit(solution)/shard_map/all_to_all | solution.py:64
  10.1 53.6 %copy-start.3 = (bf16[1,64,5120]{2,1,0:T(8,128)(2,1)S(1)}, bf16[1,64,5120]{2,1,0:T(8,128)(2,1)}, u32[]{:S(2)}) copy-start(bf16[1,64,5120]{2,1,0:T(8,128)(2,1)} %refs_4_.1) | copy-start | bytes 1966084
  14.3 3.2 %copy-start = (bf16[1,768,5120]{2,1,0:T(8,128)(2,1)}, bf16[1,768,5120]{2,1,0:T(8,128)(2,1)S(1)}, u32[]{:S(2)}) copy-start(bf16[1,768,5120]{2,1,0:T(8,128)(2,1)S(1)} %get-tuple-element.25.e_ref.refs_3_) | copy-start | bytes 23592964
  30.0 16.2 %collective-permute-start.1 = (bf16[1,64,5120]{2,1,0:T(8,128)(2,1)S(1)}, bf16[1,64,5120]{2,1,0:T(8,128)(2,1)S(1)}, u32[]{:S(2)}, u32[]{:S(2)}) collective-permute-start(bf16[1,64,5120]{2,1,0:T(8,128)(2,1)S(1)} %collective-permute-done.refs_5_), channel_id=1, source_target_pairs={{0,2},{2,3},{3,1},{1,0},{4,6},{6,7},{7,5},{5,4},{8,10},{10,11},{11... | collective-permute-start | bytes 1966088 | tf_op jit(solution)/shard_map/ppermute | solution.py:60
  31.8 3.3 %copy-start.1 = (bf16[1,768,5120]{2,1,0:T(8,128)(2,1)S(1)}, bf16[1,768,5120]{2,1,0:T(8,128)(2,1)}, u32[]{:S(2)}) copy-start(bf16[1,768,5120]{2,1,0:T(8,128)(2,1)} %copy-done) | copy-start | bytes 23592964
  35.1 54.2 %copy-start.2 = (bf16[1,768,5120]{2,1,0:T(8,128)(2,1)S(1)}, bf16[1,768,5120]{2,1,0:T(8,128)(2,1)}, u32[]{:S(2)}) copy-start(bf16[1,768,5120]{2,1,0:T(8,128)(2,1)} %copy-done) | copy-start | bytes 23592964
  46.2 43.1 %collective-permute-start.2 = (bf16[1,64,5120]{2,1,0:T(8,128)(2,1)S(1)}, bf16[1,64,5120]{2,1,0:T(8,128)(2,1)S(1)}, u32[]{:S(2)}, u32[]{:S(2)}) collective-permute-start(bf16[1,64,5120]{2,1,0:T(8,128)(2,1)S(1)} %collective-permute-done.1.refs_6_), channel_id=1, source_target_pairs={{0,2},{2,3},{3,1},{1,0},{4,6},{6,7},{7,5},{5,4},{8,10},{10,11},{11... | collective-permute-start | bytes 1966088 | tf_op jit(solution)/shard_map/ppermute | solution.py:60

commit v3 on v2

v3 whole, which is shorter than its diff:
```python
import functools

import jax
import jax.numpy as jnp
from jax import lax
from jax.experimental import pallas as pl
from jax.experimental.pallas import tpu as pltpu
from jax.sharding import PartitionSpec as P

F32 = jnp.float32
BF16 = jnp.bfloat16
SHRINK = 2.0**-23
TINY = 1e-30
BLOCK = 512
PARTS = 2


def params(mib):
    return pltpu.CompilerParams(vmem_limit_bytes=mib * 2**20)


def cost(flops, moved):
    return pl.CostEstimate(flops=int(flops), bytes_accessed=int(moved), transcendentals=0)


def dot(a, b, contract):
    return lax.dot_general(a, b, ((contract[:1], contract[1:]), ((), ())), preferred_element_type=F32)


def split(x):
    hi = x.astype(BF16)
    rest = x - hi.astype(F32)
    mid = rest.astype(BF16)
    lo = (rest - mid.astype(F32)).astype(BF16)
    return hi.astype(F32), mid.astype(F32), lo.astype(F32)


def stack3(x, ref):
    rank = x.shape[0]
    for i, part in enumerate(split(x)):
        ref[i * rank : (i + 1) * rank, :] = part
    return ref[...].astype(BF16)


def sum3(y, rank):
    return (y[2 * rank :] + y[rank : 2 * rank]) + y[:rank]


def ring_of(n):
    return [2 * p if 2 * p < n else 2 * (n - p) - 1 for p in range(n)]


def ring_source(me, step, n):
    place = jnp.where(lax.rem(me, 2) == 0, me // 2, n - (me + 1) // 2)
    place = lax.rem(place - step + n, n)
    return jnp.where(2 * place < n, 2 * place, 2 * (n - place) - 1)


def ring_step(x, axis, n):
    ring = ring_of(n)
    return lax.ppermute(x, axis, [(ring[p], ring[(p + 1) % n]) for p in range(n)])


def exchange(pieces, axis, n):
    return [pieces[0]] + [
        lax.ppermute(pieces[k], axis, [(i, (i + k) % n) for i in range(n)]) for k in range(1, n)
    ]


def swap(x, axis, n, bit):
    return lax.ppermute(x, axis, [(i, i ^ bit) for i in range(n)])


def bits(n):
    assert n & (n - 1) == 0
    return [1 << i for i in range(n.bit_length() - 1)]


def token_factor_kernel(w_hbm, g_hbm, *refs):
    out_ref, terms_ref = refs[:2]
    chunks = refs[2:-3]
    w, w3, sems = refs[-3:]
    rank = w.shape[0]
    part = chunks[0].shape[2]
    copies = [pltpu.make_async_copy(w_hbm, w, sems.at[0])]
    for c, chunk in enumerate(chunks):
        part_of = g_hbm.at[:, :, pl.ds(c * part, part)]
        copies.append(pltpu.make_async_copy(part_of, chunk, sems.at[c + 1]))
    for copy in copies:
        copy.start()
    copies[0].wait()
    stack3(w[...] * SHRINK, w3)
    terms_ref[...] = w3[...].T.astype(BF16)
    total = 0.0
    for c, chunk in enumerate(chunks):
        copies[c + 1].wait()
        total += dot(chunk[0], terms_ref[c * part : (c + 1) * part, :], (1, 0))
    out_ref[...] = jnp.zeros_like(out_ref)
    out_ref[0:rank, 0 : total.shape[0]] = sum3(total.T, rank)


def error_left_kernel(terms_ref, e_hbm, out_ref, e_ref, sems):
    rank = out_ref.shape[0]
    chunks = sems.shape[0]
    high = e_ref.shape[1] // chunks
    copies = []
    for c in range(chunks):
        rows = pl.ds(c * high, high)
        copies.append(pltpu.make_async_copy(e_hbm.at[:, rows, :], e_ref.at[:, rows, :], sems.at[c]))
        copies[-1].start()
    for c in range(chunks):
        copies[c].wait()
        rows = slice(c * high, (c + 1) * high)
        out_ref[:, rows] = sum3(dot(e_ref[0, rows, :], terms_ref[...], (1, 0)).T, rank)


def left_kernel(a_ref, e_ref, *refs):
    gws, out_ref, g3 = refs[:-2], refs[-2], refs[-1]
    n = len(gws)
    rank = e_ref.shape[0]
    tok = a_ref.shape[1] // n
    me = lax.axis_index("tensor")
    total = e_ref[...]
    for k in range(n):
        src = lax.rem(me - k + n, n)
        rows = a_ref[0, pl.ds(pl.multiple_of(src * tok, tok), tok), :]
        total += sum3(dot(stack3(gws[k][0:rank, 0:tok], g3), rows, (1, 0)), rank)
    out_ref[...] = total


def mean_kernel(n, scale, a_ref, x_ref, y_ref, p_ref, *refs):
    msgs, p3, outbox = refs[:n], refs[n], refs[n + 1]
    rank = x_ref.shape[0]
    tok = a_ref.shape[1] // n
    me = lax.axis_index("tensor")
    mean = (x_ref[...] + y_ref[...]) * scale
    p_ref[...] = mean
    top = jnp.max(jnp.max(jnp.abs(mean), axis=1, keepdims=True), axis=0, keepdims=True)
    top = jnp.maximum(top, TINY)
    parts = stack3(mean / (top * 1024.0), p3)
    gram = [jnp.sum(mean * mean[i : i + 1, :], axis=1, keepdims=True) for i in range(rank)]
    outbox[...] = jnp.zeros_like(outbox)
    for t in range(n):
        y = dot(parts, a_ref[0, t * tok : (t + 1) * tok, :], (1, 1))
        outbox[t, 0:rank, 0:tok] = sum3(y, rank)
        for i in range(rank):
            outbox[t, rank : 2 * rank, i : i + 1] = gram[i]
        outbox[t, rank : rank + 1, rank : rank + 1] = top
    for k in range(n):
        msgs[k][...] = outbox[lax.rem(me + k, n)]


def error_right_kernel(p_ref, e_ref, out_ref, p3):
    rank = p_ref.shape[0]
    parts = stack3(p_ref[...], p3)
    for c in range(e_ref.shape[2] // BLOCK):
        cols = slice(c * BLOCK, (c + 1) * BLOCK)
        out_ref[:, cols] = sum3(dot(parts, e_ref[0, :, cols], (1, 0)), rank)


def lower_inverse(gram, rank):
    at = lambda i, j: gram[i : i + 1, j : j + 1]
    low = {}
    for j in range(rank):
        d = at(j, j)
        for k in range(j):
            d = d - low[j, k] * low[j, k]
        low[j, j] = jnp.sqrt(d)
        for i in range(j + 1, rank):
            v = at(i, j)
            for k in range(j):
                v = v - low[i, k] * low[j, k]
            low[i, j] = v / low[j, j]
    inv = {}
    for j in range(rank):
        inv[j, j] = 1.0 / low[j, j]
        for i in range(j + 1, rank):
            v = low[i, j] * inv[j, j]
            for k in range(j + 1, i):
                v = v + low[i, k] * inv[k, j]
            inv[i, j] = -v / low[i, i]
    return inv


def solve_rows(inv, x, rank):
    rows = []
    for i in range(rank):
        row = inv[i, 0] * x[0:1, :]
        for j in range(1, i + 1):
            row = row + inv[i, j] * x[j : j + 1, :]
        rows.append(row)
    return rows


def right_kernel(n, parts, p_ref, r_ref, *refs):
    chunks = refs[:parts]
    pieces = refs[parts : parts + n]
    ortho_ref, keep_ref, send_ref, inbox, z, z3, outbox = refs[parts + n :]
    rank = p_ref.shape[0]
    tok = chunks[0].shape[1]
    part = chunks[0].shape[2]
    half = keep_ref.shape[1]
    me_t = lax.axis_index("tensor")
    core = lax.rem(lax.axis_index("dp"), 2)
    for k in range(n):
        inbox[lax.rem(me_t - k + n, n)] = pieces[k][...]
    gram = inbox[0, rank : 2 * rank, 0:rank]
    for t in range(1, n):
        gram = gram + inbox[t, rank : 2 * rank, 0:rank]
    inv = lower_inverse(gram, rank)
    for t in range(n):
        top = inbox[t, rank : rank + 1, rank : rank + 1]
        scaled = {key: value * top for key, value in inv.items()}
        for i, row in enumerate(solve_rows(scaled, inbox[t, 0:rank, 0:tok], rank)):
            if t == 0:
                z[i : i + 1, :] = row
            else:
                z[i : i + 1, :] += row
    for i, row in enumerate(solve_rows(inv, p_ref[...], rank)):
        ortho_ref[i : i + 1, :] = row
    terms = stack3(z[...], z3)
    for c in range(parts):
        fresh = sum3(dot(terms, chunks[c][0], (1, 0)), rank) * 1024.0
        old = solve_rows(inv, r_ref[:, c * part : (c + 1) * part], rank)
        for i, row in enumerate(old):
            row = row + fresh[i : i + 1, :]
            for h in range(2):
                lo, hi = max(h * half, c * part), min((h + 1) * half, (c + 1) * part)
                if lo < hi:
                    outbox[h, i : i + 1, lo - h * half : hi - h * half] = row[
                        :, lo - c * part : hi - c * part
                    ]
    keep_ref[...] = outbox[core]
    send_ref[...] = outbox[1 - core]


def add_kernel(x_ref, y_ref, out_ref):
    out_ref[...] = x_ref[...] + y_ref[...]


LEFT_TERMS = (0, 0, 1, 0, 2, 1)
RIGHT_TERMS = (0, 1, 0, 2, 0, 1)


def factor_kernel(scale, ortho_ref, mine_ref, other_ref, whole_ref, left_ref, right_ref, inbox, left, right):
    rank, half = mine_ref.shape
    core = lax.rem(lax.axis_index("dp"), 2)
    inbox[core] = mine_ref[...]
    inbox[1 - core] = other_ref[...]
    for h in range(2):
        whole_ref[:, h * half : (h + 1) * half] = inbox[h] * scale
    for terms, x, ref in (
        (LEFT_TERMS, ortho_ref[...], left),
        (RIGHT_TERMS, whole_ref[...], right),
    ):
        parts = split(x)
        for i, term in enumerate(terms):
            ref[i * rank : (i + 1) * rank, :] = parts[term]
    left_ref[...] = left[...].T.astype(BF16)
    right_ref[...] = right[...].astype(BF16)


def final_kernel(n, at, a_ref, left_ref, right_ref, e_ref, *refs):
    slots = refs[:n]
    rebuilt_ref, error_ref, acts, acts_t = refs[-4:]
    tok = slots[0].shape[1]
    rows = e_ref.shape[1]
    me = lax.axis_index("tensor")
    step = pl.program_id(0)

    @pl.when(step == 0)
    def _():
        for s in range(n):
            src = ring_source(me, s, n)
            here = a_ref[0, pl.ds(pl.multiple_of(src * tok, tok), tok), :]
            acts[s * tok : (s + 1) * tok, :] = here
        acts_t[...] = acts[...].T

    high = 256 if rows % 256 == 0 else 128
    for c in range(BLOCK // 256):
        cols = pl.ds(pl.multiple_of(step * BLOCK + c * 256, 256), 256)
        wide = pl.ds(pl.multiple_of(at + step * BLOCK + c * 256, 256), 256)
        grads = jnp.concatenate([slot[0, :, cols] for slot in slots], axis=0)
        right = right_ref[:, wide]
        for r in range(rows // high):
            here = slice(r * high, (r + 1) * high)
            there = slice(c * 256, (c + 1) * 256)
            matrix = dot(acts_t[here, :], grads, (1, 0)) + e_ref[0, here, wide].astype(F32)
            rebuilt = dot(left_ref[here, :], right, (1, 0))
            rebuilt_ref[here, there] = rebuilt.astype(BF16)
            error_ref[0, here, there] = (matrix - rebuilt).astype(BF16)


def per_device(activations, out_grads, error_buffer, warm_factor):
    m = lax.axis_size("dp")
    n = lax.axis_size("tensor")
    _, tokens, rows = activations.shape
    _, tok, width = out_grads.shape
    rank = warm_factor.shape[1]
    part = width // PARTS
    half = width // 2
    w = warm_factor.T
    sds = jax.ShapeDtypeStruct
    hbm = pl.BlockSpec(memory_space=pltpu.HBM)
    vmem = pl.BlockSpec(memory_space=pltpu.VMEM)
    dma = pltpu.SemaphoreType.DMA
    pin = lambda x: pltpu.with_memory_space_constraint(x, pltpu.HBM)

    def call(kernel, shapes, scratch, name, flops, moved, specs=None, mib=16):
        return pl.pallas_call(
            kernel,
            out_shape=shapes,
            **({"in_specs": specs} if specs else {}),
            scratch_shapes=scratch,
            compiler_params=params(mib),
            cost_estimate=cost(flops, moved),
            name=name,
        )

    def add(x, y):
        return call(add_kernel, sds(x.shape, F32), [], "add", 1e5, 1e5)(x, y)

    gw, w_terms, *chunks = call(
        token_factor_kernel,
        [sds((8, 128), F32), sds((width, 3 * rank), BF16)] + [sds((1, tok, part), BF16)] * PARTS,
        [pltpu.VMEM((rank, width), F32), pltpu.VMEM((3 * rank, width), F32), dma((PARTS + 1,))],
        "token_factor", 2e6, 1e6, [hbm, hbm],
    )(pin(w), pin(out_grads))
    gws = exchange([gw] * n, "tensor", n)
    rings = [[chunk] for chunk in chunks]

    def turn(c, after):
        after, last = lax.optimization_barrier((after, rings[c][-1]))
        if len(rings[c]) < n:
            rings[c].append(ring_step(last, "tensor", n))
        return after

    ew, error_v = call(
        error_left_kernel,
        [sds((rank, rows), F32), sds((1, rows, width), BF16)],
        [dma((6,))],
        "error_left", 2e9, rows * width * 2, [vmem, hbm],
    )(w_terms, pin(error_buffer))

    for c in range(PARTS):
        gws = turn(c, gws)
    left = call(
        left_kernel, sds((rank, rows), F32), [pltpu.VMEM((3 * rank, tok), F32)], "left", 1e7, 1e6
    )(activations, ew, *gws)
    for bit in bits(m)[:-1]:
        left = add(left, swap(left, "dp", m, bit))

    mean, *msgs = call(
        functools.partial(mean_kernel, n, 1.0 / (SHRINK * m)),
        [sds((rank, rows), F32)] + [sds((8, 128), F32)] * n,
        [pltpu.VMEM((3 * rank, rows), F32), pltpu.VMEM((n, 8, 128), F32)],
        "mean", 1e7, 1e6,
    )(activations, left, swap(left, "dp", m, bits(m)[-1]))
    msgs = exchange(msgs, "tensor", n)

    right_raw = call(
        error_right_kernel,
        sds((rank, width), F32),
        [pltpu.VMEM((3 * rank, rows), F32)],
        "error_right", 2e9, rows * width * 2,
    )(mean, error_v)
    for c in range(PARTS):
        msgs = turn(c, msgs)

    ortho, keep, send = call(
        functools.partial(right_kernel, n, PARTS),
        [sds((rank, rows), F32), sds((rank, half), F32), sds((rank, half), F32)],
        [
            pltpu.VMEM((n, 8, 128), F32),
            pltpu.VMEM((rank, tok), F32),
            pltpu.VMEM((3 * rank, tok), F32),
            pltpu.VMEM((2, rank, half), F32),
        ],
        "right", 1e7, 1e6,
    )(mean, right_raw, *chunks, *msgs)
    total = add(keep, swap(send, "dp", m, 1))
    for bit in bits(m)[1:]:
        total = add(total, swap(total, "dp", m, bit))
    for bit in bits(n):
        total = add(total, swap(total, "tensor", n, bit))
    for _ in range(2, n - 1):
        for c in range(PARTS):
            total = turn(c, total)
    for c in range(PARTS):
        total = turn(c, total)

    terms = len(LEFT_TERMS) * rank
    whole, left_terms, right_terms = call(
        functools.partial(factor_kernel, 1.0 / m),
        [sds((rank, width), F32), sds((rows, terms), BF16), sds((terms, width), BF16)],
        [
            pltpu.VMEM((2, rank, half), F32),
            pltpu.VMEM((terms, rows), F32),
            pltpu.VMEM((terms, width), F32),
        ],
        "factor", 1e6, 1e6,
    )(ortho, total, swap(total, "dp", m, 1))

    outs = ()
    for c, ring in enumerate(rings):
        first = c * part // BLOCK
        outs = pl.pallas_call(
            functools.partial(final_kernel, n, c * part),
            grid=(part // BLOCK,),
            in_specs=[vmem] * (4 + n) + [pl.BlockSpec(memory_space=pl.ANY)] * len(outs),
            out_specs=[
                pl.BlockSpec((rows, BLOCK), lambda i, first=first: (0, first + i)),
                pl.BlockSpec((1, rows, BLOCK), lambda i, first=first: (0, 0, first + i)),
            ],
            out_shape=[sds((rows, width), BF16), sds((1, rows, width), BF16)],
            input_output_aliases={4 + n + j: j for j in range(len(outs))},
            scratch_shapes=[pltpu.VMEM((tokens, rows), BF16), pltpu.VMEM((rows, tokens), BF16)],
            compiler_params=params(24),
            cost_estimate=cost(4e9 / PARTS, rows * width * 6 // PARTS),
            name="rebuild",
        )(activations, left_terms, right_terms, error_v, *ring, *outs)
    rebuilt, error = outs
    return rebuilt, error, whole.T


def solution(mesh):
    return jax.shard_map(
        per_device,
        mesh=mesh,
        in_specs=(P("dp", None, "tensor"), P("dp", "tensor", None), P("dp", "tensor", None), P()),
        out_specs=(P("tensor", None), P("dp", "tensor", None), P()),
        check_vma=False,
    )
```

time: 99.1 us -> 89 us (0.90)
  blocking collectives: 47.9 us -> 0 us
  waiting for transfers between devices: 13.5 us -> 43.9 us
  starting transfers between devices: 11.3 us -> 23.9 us
  local copies, waits for them, and re-layouts: 6.48 us -> 0.01 us
  Pallas kernels: 18.7 us -> 20.3 us
    all_to_all x5 -> x0, blocking collectives: 47.9 us -> none  [exchange(): return lax.all_to_all(stack, axis, 0, 0)]
    ppermute x0 -> x15, waiting for transfers between devices: none -> 35.7 us  [the longest x9 28.3 us: swap(): return lax.ppermute(x, axis, [(i, i ^ bit) for i in range(n)])]
    ppermute x0 -> x15, starting transfers between devices: none -> 17.4 us  [the longest x6 10.6 us: exchange(): lax.ppermute(pieces[k], axis, [(i, (i + k) % n) for i in range(n)])]
    unnamed x10 -> x2, local copies, waits for them, and re-layouts: 6.48 us -> 0.01 us
    all_to_all x1 -> x0, waiting for transfers between devices: 3.54 us -> none  [exchange(): return lax.all_to_all(stack, axis, 0, 0)]
    all_to_all x1 -> x0, starting transfers between devices: 3.27 us -> none  [exchange(): return lax.all_to_all(stack, axis, 0, 0)]
    ppermute x3 -> x6, waiting for transfers between devices: 9.99 us -> 8.24 us  [ring_step(): lax.ppermute(x, axis, [(ring[p], ring[(p + 1) % n]) for p in range(n)])]
    ppermute x3 -> x6, starting transfers between devices: 8.05 us -> 6.57 us  [ring_step(): lax.ppermute(x, axis, [(ring[p], ring[(p + 1) % n]) for p in range(n)])]
  transfers between devices with their start and end apart: 4 -> 21, of which waited for: 2 -> 17; matrix products, arithmetic and copies ran while one was open for 0% -> 0% of each run, Pallas kernels for 10% -> 8%
where the time goes in v3:
time: 89 us; the launch traced here: 88.9 us
  waiting for transfers between devices  43.9 us (49%)
  starting transfers between devices  23.9 us (27%)
  Pallas kernels  20.3 us (23%)
    ppermute x9, waiting for transfers between devices, swap(): return lax.ppermute(x, axis, [(i, i ^ bit) for i in range(n)])  28.3 us
    ppermute x6, starting transfers between devices, exchange(): lax.ppermute(pieces[k], axis, [(i, (i + k) % n) for i in range(n)])  10.6 us
    pallas_call x2, Pallas kernels, per_device(): pl.pallas_call(functools.partial(final_kernel, n, c * part), grid=(part /...  10.5 us
    ppermute x6, waiting for transfers between devices, ring_step(): lax.ppermute(x, axis, [(ring[p], ring[(p + 1) % n]) for p in range(n)])  8.24 us
    ppermute x6, waiting for transfers between devices, exchange(): lax.ppermute(pieces[k], axis, [(i, (i + k) % n) for i in range(n)])  7.38 us
    ppermute x9, starting transfers between devices, swap(): return lax.ppermute(x, axis, [(i, i ^ bit) for i in range(n)])  6.78 us
    ppermute x6, starting transfers between devices, ring_step(): lax.ppermute(x, axis, [(ring[p], ring[(p + 1) % n]) for p in range(n)])  6.57 us
    pallas_call x1, Pallas kernels, per_device(): call(error_left_kernel, [sds((rank, rows), F32), sds((1, rows, width), BF...  4.69 us
  transfers between devices with their start and end apart: 21, of which 17 were waited for; matrix products, arithmetic and copies ran while one was open for 0% of the time, Pallas kernels for 8%

profile of v3, /device:TPU:0, one launch (start us, length us, event | category | flops | bytes accessed | tf_op | source)
XLA Modules:
  0.0 88.9 jit_solution(8498193641862149736)
XLA Ops:
  0.6 1.9 %token_factor.1 = (f32[8,128]{1,0:T(8,128)S(1)}, bf16[5120,12]{1,0:T(8,128)(2,1)S(1)}, bf16[1,64,2560]{2,1,0:T(8,128)(2,1)S(1)}, bf16[1,64,2560]{2,1,0:T(8,128)(2,1)S(1)}) custom-call(f32[4,5120]{1,0:T(4,128)} %bitcast.2, bf16[1,64,5120]{2,1,0:T(8,128)(2,1)} %g_hbm.1), custom_call_target="tpu_custom_call" | custom-call | flops 2000000 | bytes 1000000 | tf_op jit(solution)/shard_map/token_factor/pallas_call | solution.py:323
  2.6 5.1 %collective-permute-start.2 = (f32[8,128]{1,0:T(8,128)S(1)}, f32[8,128]{1,0:T(8,128)S(1)}, u32[]{:S(2)}, u32[]{:S(2)}) collective-permute-start(f32[8,128]{1,0:T(8,128)S(1)} %get-tuple-element.59.refs_0_), channel_id=1, source_target_pairs={{0,3},{1,0},{2,1},{3,2},{4,7},{5,4},{6,5},{7,6},{8,11},{9,8},{10,9... | collective-permute-start | bytes 12296 | tf_op jit(solution)/shard_map/ppermute | solution.py:66
  9.0 3.2 %collective-permute-done.1.refs_2_ = f32[8,128]{1,0:T(8,128)S(1)} collective-permute-done((f32[8,128]{1,0:T(8,128)S(1)}, f32[8,128]{1,0:T(8,128)S(1)}, u32[]{:S(2)}, u32[]{:S(2)}) %collective-permute-start.1) | collective-permute-done | bytes 4128 | tf_op jit(solution)/shard_map/ppermute | solution.py:66
  14.2 4.7 %error_left.1 = (f32[4,768]{1,0:T(4,128)S(1)}, bf16[1,768,5120]{2,1,0:T(8,128)(2,1)S(1)}) custom-call(bf16[5120,12]{1,0:T(8,128)(2,1)S(1)} %get-tuple-element.50.terms_ref, bf16[1,768,5120]{2,1,0:T(8,128)(2,1)} %e_hbm.1), custom_call_target="tpu_custom_call" | custom-call | flops 2000000000 | bytes 7864320 | tf_op jit(solution)/shard_map/error_left/pallas_call | solution.py:338
  20.4 1.5 %collective-permute-start.4 = (f32[4,768]{1,0:T(4,128)S(1)}, f32[4,768]{1,0:T(4,128)S(1)}, u32[]{:S(2)}, u32[]{:S(2)}) collective-permute-start(f32[4,768]{1,0:T(4,128)S(1)} %add.7.x_ref), channel_id=1, source_target_pairs={{0,8},{4,12},{8,0},{12,4},{16,24},{20,28},{24,16},{28,20},{1,9},{5... | collective-permute-start | bytes 36872 | tf_op jit(solution)/shard_map/ppermute | solution.py:71
  21.9 2.2 %collective-permute-done.4.y_ref = f32[4,768]{1,0:T(4,128)S(1)} collective-permute-done((f32[4,768]{1,0:T(4,128)S(1)}, f32[4,768]{1,0:T(4,128)S(1)}, u32[]{:S(2)}, u32[]{:S(2)}) %collective-permute-start.4) | collective-permute-done | bytes 12320 | tf_op jit(solution)/shard_map/ppermute | solution.py:71
  24.1 1.5 %collective-permute-start.5 = (f32[4,768]{1,0:T(4,128)S(1)}, f32[4,768]{1,0:T(4,128)S(1)}, u32[]{:S(2)}, u32[]{:S(2)}) collective-permute-start(f32[4,768]{1,0:T(4,128)S(1)} %add.8.x_ref), channel_id=1, source_target_pairs={{0,16},{4,20},{8,24},{12,28},{16,0},{20,4},{24,8},{28,12},{1,17},{... | collective-permute-start | bytes 36872 | tf_op jit(solution)/shard_map/ppermute | solution.py:71
  25.6 2.2 %collective-permute-done.5.y_ref = f32[4,768]{1,0:T(4,128)S(1)} collective-permute-done((f32[4,768]{1,0:T(4,128)S(1)}, f32[4,768]{1,0:T(4,128)S(1)}, u32[]{:S(2)}, u32[]{:S(2)}) %collective-permute-start.5) | collective-permute-done | bytes 12320 | tf_op jit(solution)/shard_map/ppermute | solution.py:71
  28.1 2.0 %collective-permute-start.6 = (f32[8,128]{1,0:T(8,128)S(1)}, f32[8,128]{1,0:T(8,128)S(1)}, u32[]{:S(2)}, u32[]{:S(2)}) collective-permute-start(f32[8,128]{1,0:T(8,128)S(1)} %get-tuple-element.66), channel_id=1, source_target_pairs={{0,1},{1,2},{2,3},{3,0},{4,5},{5,6},{6,7},{7,4},{8,9},{9,10},{10,1... | collective-permute-start | bytes 12296 | tf_op jit(solution)/shard_map/ppermute | solution.py:66
  30.1 1.8 %collective-permute-start.7 = (f32[8,128]{1,0:T(8,128)S(1)}, f32[8,128]{1,0:T(8,128)S(1)}, u32[]{:S(2)}, u32[]{:S(2)}) collective-permute-start(f32[8,128]{1,0:T(8,128)S(1)} %get-tuple-element.67), channel_id=1, source_target_pairs={{0,2},{1,3},{2,0},{3,1},{4,6},{5,7},{6,4},{7,5},{8,10},{9,11},{10,... | collective-permute-start | bytes 12296 | tf_op jit(solution)/shard_map/ppermute | solution.py:66
  36.7 1.9 %collective-permute-start.16 = (bf16[1,64,2560]{2,1,0:T(8,128)(2,1)S(1)}, bf16[1,64,2560]{2,1,0:T(8,128)(2,1)S(1)}, u32[]{:S(2)}, u32[]{:S(2)}) collective-permute-start(bf16[1,64,2560]{2,1,0:T(8,128)(2,1)S(1)} %collective-permute-done.9.refs_1_), channel_id=1, source_target_pairs={{0,2},{2,3},{3,1},{1,0},{4,6},{6,7},{7,5},{5,4},{8,10},{10,11},{11... | collective-permute-start | bytes 983048 | tf_op jit(solution)/shard_map/ppermute | solution.py:61
  40.6 1.2 %collective-permute-done.11.y_ref = f32[4,2560]{1,0:T(4,128)S(1)} collective-permute-done((f32[4,2560]{1,0:T(4,128)S(1)}, f32[4,2560]{1,0:T(4,128)S(1)}, u32[]{:S(2)}, u32[]{:S(2)}) %collective-permute-start.11) | collective-permute-done | bytes 40992 | tf_op jit(solution)/shard_map/ppermute | solution.py:71
  41.9 1.5 %collective-permute-start.12 = (f32[4,2560]{1,0:T(4,128)S(1)}, f32[4,2560]{1,0:T(4,128)S(1)}, u32[]{:S(2)}, u32[]{:S(2)}) collective-permute-start(f32[4,2560]{1,0:T(4,128)S(1)} %add.9.x_ref), channel_id=1, source_target_pairs={{0,8},{4,12},{8,0},{12,4},{16,24},{20,28},{24,16},{28,20},{1,9},{5... | collective-permute-start | bytes 122888 | tf_op jit(solution)/shard_map/ppermute | solution.py:71
  43.3 2.5 %collective-permute-done.12.y_ref = f32[4,2560]{1,0:T(4,128)S(1)} collective-permute-done((f32[4,2560]{1,0:T(4,128)S(1)}, f32[4,2560]{1,0:T(4,128)S(1)}, u32[]{:S(2)}, u32[]{:S(2)}) %collective-permute-start.12) | collective-permute-done | bytes 40992 | tf_op jit(solution)/shard_map/ppermute | solution.py:71
  45.9 1.5 %collective-permute-start.13 = (f32[4,2560]{1,0:T(4,128)S(1)}, f32[4,2560]{1,0:T(4,128)S(1)}, u32[]{:S(2)}, u32[]{:S(2)}) collective-permute-start(f32[4,2560]{1,0:T(4,128)S(1)} %add.10.x_ref), channel_id=1, source_target_pairs={{0,16},{4,20},{8,24},{12,28},{16,0},{20,4},{24,8},{28,12},{1,17},{... | collective-permute-start | bytes 122888 | tf_op jit(solution)/shard_map/ppermute | solution.py:71
  47.4 2.5 %collective-permute-done.13.y_ref = f32[4,2560]{1,0:T(4,128)S(1)} collective-permute-done((f32[4,2560]{1,0:T(4,128)S(1)}, f32[4,2560]{1,0:T(4,128)S(1)}, u32[]{:S(2)}, u32[]{:S(2)}) %collective-permute-start.13) | collective-permute-done | bytes 40992 | tf_op jit(solution)/shard_map/ppermute | solution.py:71
  50.0 3.9 %collective-permute-done.14.y_ref = f32[4,2560]{1,0:T(4,128)S(1)} collective-permute-done((f32[4,2560]{1,0:T(4,128)S(1)}, f32[4,2560]{1,0:T(4,128)S(1)}, u32[]{:S(2)}, u32[]{:S(2)}) %collective-permute-start.14) | collective-permute-done | bytes 40992 | tf_op jit(solution)/shard_map/ppermute | solution.py:71
  54.4 11.5 %collective-permute-done.15.y_ref = f32[4,2560]{1,0:T(4,128)S(1)} collective-permute-done((f32[4,2560]{1,0:T(4,128)S(1)}, f32[4,2560]{1,0:T(4,128)S(1)}, u32[]{:S(2)}, u32[]{:S(2)}) %collective-permute-start.15) | collective-permute-done | bytes 40992 | tf_op jit(solution)/shard_map/ppermute | solution.py:71
  65.9 2.3 %collective-permute-start.19 = (bf16[1,64,2560]{2,1,0:T(8,128)(2,1)S(1)}, bf16[1,64,2560]{2,1,0:T(8,128)(2,1)S(1)}, u32[]{:S(2)}, u32[]{:S(2)}) collective-permute-start(bf16[1,64,2560]{2,1,0:T(8,128)(2,1)S(1)} %collective-permute-done.17.refs_2_), channel_id=1, source_target_pairs={{0,2},{2,3},{3,1},{1,0},{4,6},{6,7},{7,5},{5,4},{8,10},{10,11},{11... | collective-permute-start | bytes 983048 | tf_op jit(solution)/shard_map/ppermute | solution.py:61
  68.2 4.7 %collective-permute-done.18.refs_3_ = bf16[1,64,2560]{2,1,0:T(8,128)(2,1)S(1)} collective-permute-done((bf16[1,64,2560]{2,1,0:T(8,128)(2,1)S(1)}, bf16[1,64,2560]{2,1,0:T(8,128)(2,1)S(1)}, u32[]{:S(2)}, u32[]{:S(2)}) %collective-permute-start.18) | collective-permute-done | bytes 327712 | tf_op jit(solution)/shard_map/ppermute | solution.py:61
  73.0 3.5 %collective-permute-done.19.refs_3_ = bf16[1,64,2560]{2,1,0:T(8,128)(2,1)S(1)} collective-permute-done((bf16[1,64,2560]{2,1,0:T(8,128)(2,1)S(1)}, bf16[1,64,2560]{2,1,0:T(8,128)(2,1)S(1)}, u32[]{:S(2)}, u32[]{:S(2)}) %collective-permute-start.19) | collective-permute-done | bytes 327712 | tf_op jit(solution)/shard_map/ppermute | solution.py:61
  76.5 1.2 %collective-permute-done.20.other_ref = f32[4,2560]{1,0:T(4,128)S(1)} collective-permute-done((f32[4,2560]{1,0:T(4,128)S(1)}, f32[4,2560]{1,0:T(4,128)S(1)}, u32[]{:S(2)}, u32[]{:S(2)}) %collective-permute-start.20) | collective-permute-done | bytes 40992 | tf_op jit(solution)/shard_map/ppermute | solution.py:71
  78.4 5.2 %rebuild.2 = (bf16[768,5120]{1,0:T(8,128)(2,1)}, bf16[1,768,5120]{2,1,0:T(8,128)(2,1)}) custom-call(bf16[1,256,768]{2,1,0:T(8,128)(2,1)S(1)} %copy-done, bf16[768,24]{1,0:T(8,128)(2,1)S(1)} %get-tuple-element.90.left_ref, bf16[24,5120]{1,0:T(8,128)(2,1)S(1)} %get-tuple-element.91.right_ref, bf16[1,768,5120]{2,1,0:T(8,128)(2,1)S(1)} %get-tuple-element.64.e_ref, ...), custom_call_target="tpu_custom_call" | custom-call | flops 2000000000 | bytes 11796480 | tf_op jit(solution)/shard_map/rebuild/pallas_call | solution.py:407
  83.6 5.3 %rebuild.3 = (bf16[768,5120]{1,0:T(8,128)(2,1)}, bf16[1,768,5120]{2,1,0:T(8,128)(2,1)}) custom-call(bf16[1,256,768]{2,1,0:T(8,128)(2,1)S(1)} %copy-done, bf16[768,24]{1,0:T(8,128)(2,1)S(1)} %get-tuple-element.90.left_ref, bf16[24,5120]{1,0:T(8,128)(2,1)S(1)} %get-tuple-element.91.right_ref, ...), custom_call_target="tpu_custom_call", output_to_operand_aliasing={{0}: (8, {}), {1}: (9, {})} | custom-call | flops 2000000000 | bytes 11796480 | tf_op jit(solution)/shard_map/rebuild/pallas_call | solution.py:407
  (36 shorter events, 13.4 us)
Async XLA Ops:
  0.6 18.3 %copy-start = (bf16[1,256,768]{2,1,0:T(8,128)(2,1)S(1)}, bf16[1,256,768]{2,1,0:T(8,128)(2,1)}, u32[]{:S(2)}) copy-start(bf16[1,256,768]{2,1,0:T(8,128)(2,1)} %a_ref.7) | copy-start | bytes 1179652
  2.6 6.4 %collective-permute-start.2 = (f32[8,128]{1,0:T(8,128)S(1)}, f32[8,128]{1,0:T(8,128)S(1)}, u32[]{:S(2)}, u32[]{:S(2)}) collective-permute-start(f32[8,128]{1,0:T(8,128)S(1)} %get-tuple-element.59.refs_0_), channel_id=1, source_target_pairs={{0,3},{1,0},{2,1},{3,2},{4,7},{5,4},{6,5},{7,6},{8,11},{9,8},{10,9... | collective-permute-start | bytes 12296 | tf_op jit(solution)/shard_map/ppermute | solution.py:66
  7.7 4.5 %collective-permute-start.1 = (f32[8,128]{1,0:T(8,128)S(1)}, f32[8,128]{1,0:T(8,128)S(1)}, u32[]{:S(2)}, u32[]{:S(2)}) collective-permute-start(f32[8,128]{1,0:T(8,128)S(1)} %get-tuple-element.59.refs_0_), channel_id=1, source_target_pairs={{0,2},{1,3},{2,0},{3,1},{4,6},{5,7},{6,4},{7,5},{8,10},{9,11},{10,... | collective-permute-start | bytes 12296 | tf_op jit(solution)/shard_map/ppermute | solution.py:66
  7.7 5.4 %collective-permute-start = (f32[8,128]{1,0:T(8,128)S(1)}, f32[8,128]{1,0:T(8,128)S(1)}, u32[]{:S(2)}, u32[]{:S(2)}) collective-permute-start(f32[8,128]{1,0:T(8,128)S(1)} %get-tuple-element.59.refs_0_), channel_id=1, source_target_pairs={{0,1},{1,2},{2,3},{3,0},{4,5},{5,6},{6,7},{7,4},{8,9},{9,10},{10,1... | collective-permute-start | bytes 12296 | tf_op jit(solution)/shard_map/ppermute | solution.py:66
  13.1 22.5 %collective-permute-start.9 = (bf16[1,64,2560]{2,1,0:T(8,128)(2,1)S(1)}, bf16[1,64,2560]{2,1,0:T(8,128)(2,1)S(1)}, u32[]{:S(2)}, u32[]{:S(2)}) collective-permute-start(bf16[1,64,2560]{2,1,0:T(8,128)(2,1)S(1)} %get-tuple-element.69.refs_0_), channel_id=1, source_target_pairs={{0,2},{2,3},{3,1},{1,0},{4,6},{6,7},{7,5},{5,4},{8,10},{10,11},{11... | collective-permute-start | bytes 983048 | tf_op jit(solution)/shard_map/ppermute | solution.py:61
  14.2 21.4 %collective-permute-start.10 = (bf16[1,64,2560]{2,1,0:T(8,128)(2,1)S(1)}, bf16[1,64,2560]{2,1,0:T(8,128)(2,1)S(1)}, u32[]{:S(2)}, u32[]{:S(2)}) collective-permute-start(bf16[1,64,2560]{2,1,0:T(8,128)(2,1)S(1)} %get-tuple-element.74.refs_1_.refs_0_), channel_id=1, source_target_pairs={{0,2},{2,3},{3,1},{1,0},{4,6},{6,7},{7,5},{5,4},{8,10},{10,11},{11... | collective-permute-start | bytes 983048 | tf_op jit(solution)/shard_map/ppermute | solution.py:61
  19.1 1.2 %collective-permute-start.3 = (f32[4,768]{1,0:T(4,128)S(1)}, f32[4,768]{1,0:T(4,128)S(1)}, u32[]{:S(2)}, u32[]{:S(2)}) collective-permute-start(f32[4,768]{1,0:T(4,128)S(1)} %left.1.x_ref), channel_id=1, source_target_pairs={{0,4},{4,0},{8,12},{12,8},{16,20},{20,16},{24,28},{28,24},{1,5},{5... | collective-permute-start | bytes 36872 | tf_op jit(solution)/shard_map/ppermute | solution.py:71
  20.4 3.7 %collective-permute-start.4 = (f32[4,768]{1,0:T(4,128)S(1)}, f32[4,768]{1,0:T(4,128)S(1)}, u32[]{:S(2)}, u32[]{:S(2)}) collective-permute-start(f32[4,768]{1,0:T(4,128)S(1)} %add.7.x_ref), channel_id=1, source_target_pairs={{0,8},{4,12},{8,0},{12,4},{16,24},{20,28},{24,16},{28,20},{1,9},{5... | collective-permute-start | bytes 36872 | tf_op jit(solution)/shard_map/ppermute | solution.py:71
  24.1 3.7 %collective-permute-start.5 = (f32[4,768]{1,0:T(4,128)S(1)}, f32[4,768]{1,0:T(4,128)S(1)}, u32[]{:S(2)}, u32[]{:S(2)}) collective-permute-start(f32[4,768]{1,0:T(4,128)S(1)} %add.8.x_ref), channel_id=1, source_target_pairs={{0,16},{4,20},{8,24},{12,28},{16,0},{20,4},{24,8},{28,12},{1,17},{... | collective-permute-start | bytes 36872 | tf_op jit(solution)/shard_map/ppermute | solution.py:71
  28.1 5.5 %collective-permute-start.6 = (f32[8,128]{1,0:T(8,128)S(1)}, f32[8,128]{1,0:T(8,128)S(1)}, u32[]{:S(2)}, u32[]{:S(2)}) collective-permute-start(f32[8,128]{1,0:T(8,128)S(1)} %get-tuple-element.66), channel_id=1, source_target_pairs={{0,1},{1,2},{2,3},{3,0},{4,5},{5,6},{6,7},{7,4},{8,9},{9,10},{10,1... | collective-permute-start | bytes 12296 | tf_op jit(solution)/shard_map/ppermute | solution.py:66
  30.1 4.5 %collective-permute-start.7 = (f32[8,128]{1,0:T(8,128)S(1)}, f32[8,128]{1,0:T(8,128)S(1)}, u32[]{:S(2)}, u32[]{:S(2)}) collective-permute-start(f32[8,128]{1,0:T(8,128)S(1)} %get-tuple-element.67), channel_id=1, source_target_pairs={{0,2},{1,3},{2,0},{3,1},{4,6},{5,7},{6,4},{7,5},{8,10},{9,11},{10,... | collective-permute-start | bytes 12296 | tf_op jit(solution)/shard_map/ppermute | solution.py:66
  31.9 3.6 %collective-permute-start.8 = (f32[8,128]{1,0:T(8,128)S(1)}, f32[8,128]{1,0:T(8,128)S(1)}, u32[]{:S(2)}, u32[]{:S(2)}) collective-permute-start(f32[8,128]{1,0:T(8,128)S(1)} %get-tuple-element.68), channel_id=1, source_target_pairs={{0,3},{1,0},{2,1},{3,2},{4,7},{5,4},{6,5},{7,6},{8,11},{9,8},{10,9... | collective-permute-start | bytes 12296 | tf_op jit(solution)/shard_map/ppermute | solution.py:66
  35.6 30.3 %collective-permute-start.17 = (bf16[1,64,2560]{2,1,0:T(8,128)(2,1)S(1)}, bf16[1,64,2560]{2,1,0:T(8,128)(2,1)S(1)}, u32[]{:S(2)}, u32[]{:S(2)}) collective-permute-start(bf16[1,64,2560]{2,1,0:T(8,128)(2,1)S(1)} %collective-permute-done.10.refs_1_), channel_id=1, source_target_pairs={{0,2},{2,3},{3,1},{1,0},{4,6},{6,7},{7,5},{5,4},{8,10},{10,11},{11... | collective-permute-start | bytes 983048 | tf_op jit(solution)/shard_map/ppermute | solution.py:61
  36.7 29.1 %collective-permute-start.16 = (bf16[1,64,2560]{2,1,0:T(8,128)(2,1)S(1)}, bf16[1,64,2560]{2,1,0:T(8,128)(2,1)S(1)}, u32[]{:S(2)}, u32[]{:S(2)}) collective-permute-start(bf16[1,64,2560]{2,1,0:T(8,128)(2,1)S(1)} %collective-permute-done.9.refs_1_), channel_id=1, source_target_pairs={{0,2},{2,3},{3,1},{1,0},{4,6},{6,7},{7,5},{5,4},{8,10},{10,11},{11... | collective-permute-start | bytes 983048 | tf_op jit(solution)/shard_map/ppermute | solution.py:61
  40.6 1.3 %collective-permute-start.11 = (f32[4,2560]{1,0:T(4,128)S(1)}, f32[4,2560]{1,0:T(4,128)S(1)}, u32[]{:S(2)}, u32[]{:S(2)}) collective-permute-start(f32[4,2560]{1,0:T(4,128)S(1)} %get-tuple-element.81), channel_id=1, source_target_pairs={{0,4},{4,0},{8,12},{12,8},{16,20},{20,16},{24,28},{28,24},{1,5},{5... | collective-permute-start | bytes 122888 | tf_op jit(solution)/shard_map/ppermute | solution.py:71
  41.9 4.0 %collective-permute-start.12 = (f32[4,2560]{1,0:T(4,128)S(1)}, f32[4,2560]{1,0:T(4,128)S(1)}, u32[]{:S(2)}, u32[]{:S(2)}) collective-permute-start(f32[4,2560]{1,0:T(4,128)S(1)} %add.9.x_ref), channel_id=1, source_target_pairs={{0,8},{4,12},{8,0},{12,4},{16,24},{20,28},{24,16},{28,20},{1,9},{5... | collective-permute-start | bytes 122888 | tf_op jit(solution)/shard_map/ppermute | solution.py:71
  45.9 4.0 %collective-permute-start.13 = (f32[4,2560]{1,0:T(4,128)S(1)}, f32[4,2560]{1,0:T(4,128)S(1)}, u32[]{:S(2)}, u32[]{:S(2)}) collective-permute-start(f32[4,2560]{1,0:T(4,128)S(1)} %add.10.x_ref), channel_id=1, source_target_pairs={{0,16},{4,20},{8,24},{12,28},{16,0},{20,4},{24,8},{28,12},{1,17},{... | collective-permute-start | bytes 122888 | tf_op jit(solution)/shard_map/ppermute | solution.py:71
  49.9 4.0 %collective-permute-start.14 = (f32[4,2560]{1,0:T(4,128)S(1)}, f32[4,2560]{1,0:T(4,128)S(1)}, u32[]{:S(2)}, u32[]{:S(2)}) collective-permute-start(f32[4,2560]{1,0:T(4,128)S(1)} %add.11.x_ref), channel_id=1, source_target_pairs={{0,1},{1,0},{2,3},{3,2},{4,5},{5,4},{6,7},{7,6},{8,9},{9,8},{10,11... | collective-permute-start | bytes 122888 | tf_op jit(solution)/shard_map/ppermute | solution.py:71
  53.9 11.9 %collective-permute-start.15 = (f32[4,2560]{1,0:T(4,128)S(1)}, f32[4,2560]{1,0:T(4,128)S(1)}, u32[]{:S(2)}, u32[]{:S(2)}) collective-permute-start(f32[4,2560]{1,0:T(4,128)S(1)} %add.12.x_ref), channel_id=1, source_target_pairs={{0,2},{1,3},{2,0},{3,1},{4,6},{5,7},{6,4},{7,5},{8,10},{9,11},{10,... | collective-permute-start | bytes 122888 | tf_op jit(solution)/shard_map/ppermute | solution.py:71
  65.8 7.1 %collective-permute-start.18 = (bf16[1,64,2560]{2,1,0:T(8,128)(2,1)S(1)}, bf16[1,64,2560]{2,1,0:T(8,128)(2,1)S(1)}, u32[]{:S(2)}, u32[]{:S(2)}) collective-permute-start(bf16[1,64,2560]{2,1,0:T(8,128)(2,1)S(1)} %collective-permute-done.16.refs_2_), channel_id=1, source_target_pairs={{0,2},{2,3},{3,1},{1,0},{4,6},{6,7},{7,5},{5,4},{8,10},{10,11},{11... | collective-permute-start | bytes 983048 | tf_op jit(solution)/shard_map/ppermute | solution.py:61
  65.9 10.6 %collective-permute-start.19 = (bf16[1,64,2560]{2,1,0:T(8,128)(2,1)S(1)}, bf16[1,64,2560]{2,1,0:T(8,128)(2,1)S(1)}, u32[]{:S(2)}, u32[]{:S(2)}) collective-permute-start(bf16[1,64,2560]{2,1,0:T(8,128)(2,1)S(1)} %collective-permute-done.17.refs_2_), channel_id=1, source_target_pairs={{0,2},{2,3},{3,1},{1,0},{4,6},{6,7},{7,5},{5,4},{8,10},{10,11},{11... | collective-permute-start | bytes 983048 | tf_op jit(solution)/shard_map/ppermute | solution.py:61
  76.5 1.2 %collective-permute-start.20 = (f32[4,2560]{1,0:T(4,128)S(1)}, f32[4,2560]{1,0:T(4,128)S(1)}, u32[]{:S(2)}, u32[]{:S(2)}) collective-permute-start(f32[4,2560]{1,0:T(4,128)S(1)} %add.13.mine_ref), channel_id=1, source_target_pairs={{0,4},{4,0},{8,12},{12,8},{16,20},{20,16},{24,28},{28,24},{1,5},{5... | collective-permute-start | bytes 122888 | tf_op jit(solution)/shard_map/ppermute | solution.py:71

commit v4 on v3

--- a/solution.py
+++ b/solution.py
@@ -12,7 +12,7 @@
 SHRINK = 2.0**-23
 TINY = 1e-30
 BLOCK = 512
-PARTS = 2
+SHARES = (4, 2, 4)
 
 
 def params(mib):
@@ -20,7 +20,7 @@
 
 
 def cost(flops, moved):
-    return pl.CostEstimate(flops=int(flops), bytes_accessed=int(moved), transcendentals=0)
+    return pl.CostEstimate(flops=1, bytes_accessed=1, transcendentals=0)
 
 
 def dot(a, b, contract):
@@ -76,42 +76,49 @@
     return [1 << i for i in range(n.bit_length() - 1)]
 
 
-def token_factor_kernel(w_hbm, g_hbm, *refs):
-    out_ref, terms_ref = refs[:2]
-    chunks = refs[2:-3]
-    w, w3, sems = refs[-3:]
+def cut_kernel(g_hbm, *refs):
+    chunks, sems = refs[:-1], refs[-1]
+    copies = []
+    at = 0
+    for c, chunk in enumerate(chunks):
+        part = chunk.shape[2]
+        copies.append(pltpu.make_async_copy(g_hbm.at[:, :, pl.ds(at, part)], chunk, sems.at[c]))
+        copies[-1].start()
+        at += part
+    for copy in copies:
+        copy.wait()
+
+
+def products_kernel(parts, w_hbm, e_hbm, *refs):
+    chunks = refs[:parts]
+    gw_ref, ew_ref, e_ref, w, w3, terms, w_sem, sems = refs[parts:]
     rank = w.shape[0]
-    part = chunks[0].shape[2]
-    copies = [pltpu.make_async_copy(w_hbm, w, sems.at[0])]
-    for c, chunk in enumerate(chunks):
-        part_of = g_hbm.at[:, :, pl.ds(c * part, part)]
-        copies.append(pltpu.make_async_copy(part_of, chunk, sems.at[c + 1]))
-    for copy in copies:
-        copy.start()
-    copies[0].wait()
-    stack3(w[...] * SHRINK, w3)
-    terms_ref[...] = w3[...].T.astype(BF16)
-    total = 0.0
-    for c, chunk in enumerate(chunks):
-        copies[c + 1].wait()
-        total += dot(chunk[0], terms_ref[c * part : (c + 1) * part, :], (1, 0))
-    out_ref[...] = jnp.zeros_like(out_ref)
-    out_ref[0:rank, 0 : total.shape[0]] = sum3(total.T, rank)
-
-
-def error_left_kernel(terms_ref, e_hbm, out_ref, e_ref, sems):
-    rank = out_ref.shape[0]
-    chunks = sems.shape[0]
-    high = e_ref.shape[1] // chunks
+    count = sems.shape[0]
+    high = e_ref.shape[1] // count
+    w_copy = pltpu.make_async_copy(w_hbm, w, w_sem)
+    w_copy.start()
     copies = []
-    for c in range(chunks):
+    for c in range(count):
         rows = pl.ds(c * high, high)
         copies.append(pltpu.make_async_copy(e_hbm.at[:, rows, :], e_ref.at[:, rows, :], sems.at[c]))
         copies[-1].start()
-    for c in range(chunks):
-        copies[c].wait()
-        rows = slice(c * high, (c + 1) * high)
-        out_ref[:, rows] = sum3(dot(e_ref[0, rows, :], terms_ref[...], (1, 0)).T, rank)
+    w_copy.wait()
+    stack3(w[...] * SHRINK, w3)
+    terms[...] = w3[...].T.astype(BF16)
+    total = 0.0
+    at = 0
+    for chunk in chunks:
+        part = chunk.shape[2]
+        total += dot(chunk[0], terms[at : at + part, :], (1, 0))
+        at += part
+    gw_ref[...] = jnp.zeros_like(gw_ref)
+    gw_ref[0:rank, 0 : total.shape[0]] = sum3(total.T, rank)
+    group = 2 if count % 2 == 0 and (2 * high) % 128 == 0 else count
+    for c in range(0, count, group):
+        for copy in copies[c : c + group]:
+            copy.wait()
+        rows = slice(c * high, (c + group) * high)
+        ew_ref[:, rows] = sum3(dot(e_ref[0, rows, :], terms[...], (1, 0)).T, rank)
 
 
 def left_kernel(a_ref, e_ref, *refs):
@@ -198,7 +205,6 @@
     ortho_ref, keep_ref, send_ref, inbox, z, z3, outbox = refs[parts + n :]
     rank = p_ref.shape[0]
     tok = chunks[0].shape[1]
-    part = chunks[0].shape[2]
     half = keep_ref.shape[1]
     me_t = lax.axis_index("tensor")
     core = lax.rem(lax.axis_index("dp"), 2)
@@ -219,17 +225,19 @@
     for i, row in enumerate(solve_rows(inv, p_ref[...], rank)):
         ortho_ref[i : i + 1, :] = row
     terms = stack3(z[...], z3)
-    for c in range(parts):
-        fresh = sum3(dot(terms, chunks[c][0], (1, 0)), rank) * 1024.0
-        old = solve_rows(inv, r_ref[:, c * part : (c + 1) * part], rank)
+    at = 0
+    for chunk in chunks:
+        end = at + chunk.shape[2]
+        fresh = sum3(dot(terms, chunk[0], (1, 0)), rank) * 1024.0
+        old = solve_rows(inv, r_ref[:, at:end], rank)
         for i, row in enumerate(old):
             row = row + fresh[i : i + 1, :]
             for h in range(2):
-                lo, hi = max(h * half, c * part), min((h + 1) * half, (c + 1) * part)
+                lo, hi = max(h * half, at), min((h + 1) * half, end)
                 if lo < hi:
-                    outbox[h, i : i + 1, lo - h * half : hi - h * half] = row[
-                        :, lo - c * part : hi - c * part
-                    ]
+                    here = slice(lo - h * half, hi - h * half)
+                    outbox[h, i : i + 1, here] = row[:, lo - at : hi - at]
+        at = end
     keep_ref[...] = outbox[core]
     send_ref[...] = outbox[1 - core]
 
@@ -262,33 +270,45 @@
 
 def final_kernel(n, at, a_ref, left_ref, right_ref, e_ref, *refs):
     slots = refs[:n]
-    rebuilt_ref, error_ref, acts, acts_t = refs[-4:]
-    tok = slots[0].shape[1]
+    rebuilt_hbm, error_hbm, acts, acts_t, rebuilt_v, error_v, sems = refs[-7:]
+    tok, part = slots[0].shape[1:]
     rows = e_ref.shape[1]
     me = lax.axis_index("tensor")
-    step = pl.program_id(0)
-
-    @pl.when(step == 0)
-    def _():
-        for s in range(n):
-            src = ring_source(me, s, n)
-            here = a_ref[0, pl.ds(pl.multiple_of(src * tok, tok), tok), :]
-            acts[s * tok : (s + 1) * tok, :] = here
-        acts_t[...] = acts[...].T
-
-    high = 256 if rows % 256 == 0 else 128
-    for c in range(BLOCK // 256):
-        cols = pl.ds(pl.multiple_of(step * BLOCK + c * 256, 256), 256)
-        wide = pl.ds(pl.multiple_of(at + step * BLOCK + c * 256, 256), 256)
-        grads = jnp.concatenate([slot[0, :, cols] for slot in slots], axis=0)
-        right = right_ref[:, wide]
-        for r in range(rows // high):
-            here = slice(r * high, (r + 1) * high)
-            there = slice(c * 256, (c + 1) * 256)
-            matrix = dot(acts_t[here, :], grads, (1, 0)) + e_ref[0, here, wide].astype(F32)
-            rebuilt = dot(left_ref[here, :], right, (1, 0))
-            rebuilt_ref[here, there] = rebuilt.astype(BF16)
-            error_ref[0, here, there] = (matrix - rebuilt).astype(BF16)
+    for s in range(n):
+        src = ring_source(me, s, n)
+        here = a_ref[0, pl.ds(pl.multiple_of(src * tok, tok), tok), :]
+        acts[s * tok : (s + 1) * tok, :] = here
+    acts_t[...] = acts[...].T
+
+    wide = 256
+    high = rows // sems.shape[0]
+    copies = []
+    for r in range(sems.shape[0]):
+        here = slice(r * high, (r + 1) * high)
+        for c in range(part // wide):
+            cols = slice(c * wide, (c + 1) * wide)
+            there = slice(at + c * wide, at + (c + 1) * wide)
+            grads = jnp.concatenate([slot[0, :, cols] for slot in slots], axis=0)
+            matrix = dot(acts_t[here, :], grads, (1, 0)) + e_ref[0, here, there].astype(F32)
+            rebuilt = dot(left_ref[here, :], right_ref[:, there], (1, 0))
+            rebuilt_v[here, cols] = rebuilt.astype(BF16)
+            error_v[here, cols] = (matrix - rebuilt).astype(BF16)
+        strip = pl.ds(r * high, high)
+        span = pl.ds(at, part)
+        copies.append(
+            pltpu.make_async_copy(
+                rebuilt_v.at[strip, :], rebuilt_hbm.at[strip, span], sems.at[r, 0]
+            )
+        )
+        copies.append(
+            pltpu.make_async_copy(
+                error_v.at[strip, :], error_hbm.at[0, strip, span], sems.at[r, 1]
+            )
+        )
+        copies[-2].start()
+        copies[-1].start()
+    for copy in copies:
+        copy.wait()
 
 
 def per_device(activations, out_grads, error_buffer, warm_factor):
@@ -297,7 +317,8 @@
     _, tokens, rows = activations.shape
     _, tok, width = out_grads.shape
     rank = warm_factor.shape[1]
-    part = width // PARTS
+    widths = [width // share for share in SHARES]
+    parts = len(widths)
     half = width // 2
     w = warm_factor.T
     sds = jax.ShapeDtypeStruct
@@ -320,42 +341,58 @@
     def add(x, y):
         return call(add_kernel, sds(x.shape, F32), [], "add", 1e5, 1e5)(x, y)
 
-    gw, w_terms, *chunks = call(
-        token_factor_kernel,
-        [sds((8, 128), F32), sds((width, 3 * rank), BF16)] + [sds((1, tok, part), BF16)] * PARTS,
-        [pltpu.VMEM((rank, width), F32), pltpu.VMEM((3 * rank, width), F32), dma((PARTS + 1,))],
-        "token_factor", 2e6, 1e6, [hbm, hbm],
-    )(pin(w), pin(out_grads))
-    gws = exchange([gw] * n, "tensor", n)
+    chunks = call(
+        cut_kernel,
+        [sds((1, tok, part), BF16) for part in widths],
+        [dma((parts,))],
+        "cut", 1e3, 1e6, [hbm],
+    )(pin(out_grads))
     rings = [[chunk] for chunk in chunks]
 
-    def turn(c, after):
-        after, last = lax.optimization_barrier((after, rings[c][-1]))
-        if len(rings[c]) < n:
+    def turn(which, after):
+        for c in which:
+            after, last = lax.optimization_barrier((after, rings[c][-1]))
             rings[c].append(ring_step(last, "tensor", n))
         return after
 
-    ew, error_v = call(
-        error_left_kernel,
-        [sds((rank, rows), F32), sds((1, rows, width), BF16)],
-        [dma((6,))],
-        "error_left", 2e9, rows * width * 2, [vmem, hbm],
-    )(w_terms, pin(error_buffer))
-
-    for c in range(PARTS):
-        gws = turn(c, gws)
+    def settle(which, before):
+        last = [rings[c][-1] for c in which]
+        before, last = lax.optimization_barrier((before, last))
+        for c, x in zip(which, last):
+            rings[c][-1] = x
+        return before
+
+    small, others = [0], [1, 2]
+    turn(small, w)
+
+    gw, ew, error_v = call(
+        functools.partial(products_kernel, parts),
+        [sds((8, 128), F32), sds((rank, rows), F32), sds((1, rows, width), BF16)],
+        [
+            pltpu.VMEM((rank, width), F32),
+            pltpu.VMEM((3 * rank, width), F32),
+            pltpu.VMEM((width, 3 * rank), BF16),
+            dma(()),
+            dma((12,)),
+        ],
+        "products", 2e9, rows * width * 2, [hbm, hbm] + [vmem] * parts, 20,
+    )(pin(w), pin(error_buffer), *chunks)
+    gws = exchange([gw] * n, "tensor", n)
+    gws = settle(small, gws)
+    gws = turn(others, gws)
     left = call(
         left_kernel, sds((rank, rows), F32), [pltpu.VMEM((3 * rank, tok), F32)], "left", 1e7, 1e6
     )(activations, ew, *gws)
     for bit in bits(m)[:-1]:
         left = add(left, swap(left, "dp", m, bit))
+    last = settle(others, swap(left, "dp", m, bits(m)[-1]))
 
     mean, *msgs = call(
         functools.partial(mean_kernel, n, 1.0 / (SHRINK * m)),
         [sds((rank, rows), F32)] + [sds((8, 128), F32)] * n,
         [pltpu.VMEM((3 * rank, rows), F32), pltpu.VMEM((n, 8, 128), F32)],
         "mean", 1e7, 1e6,
-    )(activations, left, swap(left, "dp", m, bits(m)[-1]))
+    )(activations, left, last)
     msgs = exchange(msgs, "tensor", n)
 
     right_raw = call(
@@ -364,11 +401,10 @@
         [pltpu.VMEM((3 * rank, rows), F32)],
         "error_right", 2e9, rows * width * 2,
     )(mean, error_v)
-    for c in range(PARTS):
-        msgs = turn(c, msgs)
+    msgs = turn(others, msgs)
 
     ortho, keep, send = call(
-        functools.partial(right_kernel, n, PARTS),
+        functools.partial(right_kernel, n, parts),
         [sds((rank, rows), F32), sds((rank, half), F32), sds((rank, half), F32)],
         [
             pltpu.VMEM((n, 8, 128), F32),
@@ -381,13 +417,10 @@
     total = add(keep, swap(send, "dp", m, 1))
     for bit in bits(m)[1:]:
         total = add(total, swap(total, "dp", m, bit))
+    total = settle(others, total)
     for bit in bits(n):
         total = add(total, swap(total, "tensor", n, bit))
-    for _ in range(2, n - 1):
-        for c in range(PARTS):
-            total = turn(c, total)
-    for c in range(PARTS):
-        total = turn(c, total)
+    total = turn(small, total)
 
     terms = len(LEFT_TERMS) * rank
     whole, left_terms, right_terms = call(
@@ -401,22 +434,26 @@
         "factor", 1e6, 1e6,
     )(ortho, total, swap(total, "dp", m, 1))
 
+    for _ in range(3, n):
+        right_terms = turn([1, 0, 2], right_terms)
     outs = ()
-    for c, ring in enumerate(rings):
-        first = c * part // BLOCK
+    for c in [1, 0, 2]:
+        ring, part, at = rings[c], widths[c], sum(widths[:c])
         outs = pl.pallas_call(
-            functools.partial(final_kernel, n, c * part),
-            grid=(part // BLOCK,),
+            functools.partial(final_kernel, n, at),
             in_specs=[vmem] * (4 + n) + [pl.BlockSpec(memory_space=pl.ANY)] * len(outs),
-            out_specs=[
-                pl.BlockSpec((rows, BLOCK), lambda i, first=first: (0, first + i)),
-                pl.BlockSpec((1, rows, BLOCK), lambda i, first=first: (0, 0, first + i)),
-            ],
+            out_specs=[pl.BlockSpec(memory_space=pl.ANY)] * 2,
             out_shape=[sds((rows, width), BF16), sds((1, rows, width), BF16)],
             input_output_aliases={4 + n + j: j for j in range(len(outs))},
-            scratch_shapes=[pltpu.VMEM((tokens, rows), BF16), pltpu.VMEM((rows, tokens), BF16)],
-            compiler_params=params(24),
-            cost_estimate=cost(4e9 / PARTS, rows * width * 6 // PARTS),
+            scratch_shapes=[
+                pltpu.VMEM((tokens, rows), BF16),
+                pltpu.VMEM((rows, tokens), BF16),
+                pltpu.VMEM((rows, part), BF16),
+                pltpu.VMEM((rows, part), BF16),
+                dma((3, 2)),
+            ],
+            compiler_params=params(16),
+            cost_estimate=cost(4e9, rows * part * 4),
             name="rebuild",
         )(activations, left_terms, right_terms, error_v, *ring, *outs)
     rebuilt, error = outs

time: 89 us -> 86.1 us (0.967)
  waiting for transfers between devices: 43.9 us -> 27.9 us
  starting transfers between devices: 23.9 us -> 36.3 us
    ppermute x9, waiting for transfers between devices: 28.3 us -> 16.3 us  [swap(): return lax.ppermute(x, axis, [(i, i ^ bit) for i in range(n)])]
    ppermute x6 -> x9, starting transfers between devices: 6.57 us -> 18.2 us  [ring_step(): lax.ppermute(x, axis, [(ring[p], ring[(p + 1) % n]) for p in range(n)])]
    ppermute x9, starting transfers between devices: 6.78 us -> 10.6 us  [swap(): return lax.ppermute(x, axis, [(i, i ^ bit) for i in range(n)])]
    ppermute x6 -> x9, waiting for transfers between devices: 8.24 us -> 4.62 us  [ring_step(): lax.ppermute(x, axis, [(ring[p], ring[(p + 1) % n]) for p in range(n)])]
    ppermute x6, starting transfers between devices: 10.6 us -> 7.48 us  [exchange(): lax.ppermute(pieces[k], axis, [(i, (i + k) % n) for i in range(n)])]
    pallas_call x5 -> x6, Pallas kernels: 17.9 us -> 18.4 us  [the longest x3 9.24 us: per_device(): pl.pallas_call(functools.partial(final_kernel, n, at), in_specs=[vmem] *...]
  transfers between devices with their start and end apart: 21 -> 24, of which waited for: 17 -> 14; matrix products, arithmetic and copies ran while one was open for 0% -> 0% of each run, Pallas kernels for 8% -> 19%
where the time goes in v4:
time: 86.1 us; the launch traced here: 85.9 us
  starting transfers between devices  36.3 us (42%)
  waiting for transfers between devices  27.9 us (32%)
  Pallas kernels  20.8 us (24%)
  between operations  0.93 us (1%)
    ppermute x9, starting transfers between devices, ring_step(): lax.ppermute(x, axis, [(ring[p], ring[(p + 1) % n]) for p in range(n)])  18.2 us
    ppermute x9, waiting for transfers between devices, swap(): return lax.ppermute(x, axis, [(i, i ^ bit) for i in range(n)])  16.3 us
    ppermute x9, starting transfers between devices, swap(): return lax.ppermute(x, axis, [(i, i ^ bit) for i in range(n)])  10.6 us
    pallas_call x3, Pallas kernels, per_device(): pl.pallas_call(functools.partial(final_kernel, n, at), in_specs=[vmem] *...  9.24 us
    ppermute x6, starting transfers between devices, exchange(): lax.ppermute(pieces[k], axis, [(i, (i + k) % n) for i in range(n)])  7.48 us
    pallas_call x1, Pallas kernels, per_device(): call(functools.partial(products_kernel, parts), [sds((8, 128), F32), sds(...  7.18 us
    ppermute x6, waiting for transfers between devices, exchange(): lax.ppermute(pieces[k], axis, [(i, (i + k) % n) for i in range(n)])  6.98 us
    ppermute x9, waiting for transfers between devices, ring_step(): lax.ppermute(x, axis, [(ring[p], ring[(p + 1) % n]) for p in range(n)])  4.62 us
  transfers between devices with their start and end apart: 24, of which 14 were waited for; matrix products, arithmetic and copies ran while one was open for 0% of the time, Pallas kernels for 19%

profile of v4, /device:TPU:0, one launch (start us, length us, event | category | flops | bytes accessed | tf_op | source)
XLA Modules:
  0.0 85.9 jit_solution(15928139898474259897)
XLA Ops:
  1.8 4.1 %collective-permute-start.3 = (bf16[1,64,1280]{2,1,0:T(8,128)(2,1)S(1)}, bf16[1,64,1280]{2,1,0:T(8,128)(2,1)S(1)}, u32[]{:S(2)}, u32[]{:S(2)}) collective-permute-start(bf16[1,64,1280]{2,1,0:T(8,128)(2,1)S(1)} %get-tuple-element.71.refs_0_), channel_id=1, source_target_pairs={{0,2},{2,3},{3,1},{1,0},{4,6},{6,7},{7,5},{5,4},{8,10},{10,11},{11... | collective-permute-start | bytes 491528 | tf_op jit(solution)/shard_map/ppermute | solution.py:61
  5.9 7.2 %products.1 = (f32[8,128]{1,0:T(8,128)S(1)}, f32[4,768]{1,0:T(4,128)S(1)}, bf16[1,768,5120]{2,1,0:T(8,128)(2,1)S(1)}) custom-call(f32[4,5120]{1,0:T(4,128)} %bitcast.2, bf16[1,768,5120]{2,1,0:T(8,128)(2,1)} %e_hbm.1, bf16[1,64,1280]{2,1,0:T(8,128)(2,1)S(1)} %get-tuple-element.71.refs_0_, bf16[1,64,2560]{2,1,0:T(8,128)(2,1)S(1)} %get-tuple-element.84.refs_1_.refs_0_, ...), custom_call_target="tpu_custom_call" | custom-call | flops 1 | bytes 1 | tf_op jit(solution)/shard_map/products/pallas_call | solution.py:368
  13.2 1.9 %collective-permute-start.1 = (f32[8,128]{1,0:T(8,128)S(1)}, f32[8,128]{1,0:T(8,128)S(1)}, u32[]{:S(2)}, u32[]{:S(2)}) collective-permute-start(f32[8,128]{1,0:T(8,128)S(1)} %get-tuple-element.80.refs_0_), channel_id=1, source_target_pairs={{0,2},{1,3},{2,0},{3,1},{4,6},{5,7},{6,4},{7,5},{8,10},{9,11},{10,... | collective-permute-start | bytes 12296 | tf_op jit(solution)/shard_map/ppermute | solution.py:66
  15.1 2.6 %collective-permute-start.2 = (f32[8,128]{1,0:T(8,128)S(1)}, f32[8,128]{1,0:T(8,128)S(1)}, u32[]{:S(2)}, u32[]{:S(2)}) collective-permute-start(f32[8,128]{1,0:T(8,128)S(1)} %get-tuple-element.80.refs_0_), channel_id=1, source_target_pairs={{0,3},{1,0},{2,1},{3,2},{4,7},{5,4},{6,5},{7,6},{8,11},{9,8},{10,9... | collective-permute-start | bytes 12296 | tf_op jit(solution)/shard_map/ppermute | solution.py:66
  20.3 3.3 %collective-permute-start.8 = (bf16[1,64,1280]{2,1,0:T(8,128)(2,1)S(1)}, bf16[1,64,1280]{2,1,0:T(8,128)(2,1)S(1)}, u32[]{:S(2)}, u32[]{:S(2)}) collective-permute-start(bf16[1,64,1280]{2,1,0:T(8,128)(2,1)S(1)} %get-tuple-element.85.refs_2_.refs_0_), channel_id=1, source_target_pairs={{0,2},{2,3},{3,1},{1,0},{4,6},{6,7},{7,5},{5,4},{8,10},{10,11},{11... | collective-permute-start | bytes 491528 | tf_op jit(solution)/shard_map/ppermute | solution.py:61
  26.6 2.2 %collective-permute-done.5.y_ref = f32[4,768]{1,0:T(4,128)S(1)} collective-permute-done((f32[4,768]{1,0:T(4,128)S(1)}, f32[4,768]{1,0:T(4,128)S(1)}, u32[]{:S(2)}, u32[]{:S(2)}) %collective-permute-start.5) | collective-permute-done | bytes 12320 | tf_op jit(solution)/shard_map/ppermute | solution.py:71
  30.3 2.2 %collective-permute-done.6.y_ref = f32[4,768]{1,0:T(4,128)S(1)} collective-permute-done((f32[4,768]{1,0:T(4,128)S(1)}, f32[4,768]{1,0:T(4,128)S(1)}, u32[]{:S(2)}, u32[]{:S(2)}) %collective-permute-start.6) | collective-permute-done | bytes 12320 | tf_op jit(solution)/shard_map/ppermute | solution.py:71
  33.3 2.5 %collective-permute-start.11 = (f32[8,128]{1,0:T(8,128)S(1)}, f32[8,128]{1,0:T(8,128)S(1)}, u32[]{:S(2)}, u32[]{:S(2)}) collective-permute-start(f32[8,128]{1,0:T(8,128)S(1)} %get-tuple-element.92), channel_id=1, source_target_pairs={{0,3},{1,0},{2,1},{3,2},{4,7},{5,4},{6,5},{7,6},{8,11},{9,8},{10,9... | collective-permute-start | bytes 12296 | tf_op jit(solution)/shard_map/ppermute | solution.py:66
  35.8 1.6 %collective-permute-done.10.refs_5_ = f32[8,128]{1,0:T(8,128)S(1)} collective-permute-done((f32[8,128]{1,0:T(8,128)S(1)}, f32[8,128]{1,0:T(8,128)S(1)}, u32[]{:S(2)}, u32[]{:S(2)}) %collective-permute-start.10) | collective-permute-done | bytes 4128 | tf_op jit(solution)/shard_map/ppermute | solution.py:66
  37.4 3.9 %collective-permute-done.9.refs_4_ = f32[8,128]{1,0:T(8,128)S(1)} collective-permute-done((f32[8,128]{1,0:T(8,128)S(1)}, f32[8,128]{1,0:T(8,128)S(1)}, u32[]{:S(2)}, u32[]{:S(2)}) %collective-permute-start.9) | collective-permute-done | bytes 4128 | tf_op jit(solution)/shard_map/ppermute | solution.py:66
  46.5 2.5 %collective-permute-done.13.y_ref = f32[4,2560]{1,0:T(4,128)S(1)} collective-permute-done((f32[4,2560]{1,0:T(4,128)S(1)}, f32[4,2560]{1,0:T(4,128)S(1)}, u32[]{:S(2)}, u32[]{:S(2)}) %collective-permute-start.13) | collective-permute-done | bytes 40992 | tf_op jit(solution)/shard_map/ppermute | solution.py:71
  50.6 2.5 %collective-permute-done.14.y_ref = f32[4,2560]{1,0:T(4,128)S(1)} collective-permute-done((f32[4,2560]{1,0:T(4,128)S(1)}, f32[4,2560]{1,0:T(4,128)S(1)}, u32[]{:S(2)}, u32[]{:S(2)}) %collective-permute-start.14) | collective-permute-done | bytes 40992 | tf_op jit(solution)/shard_map/ppermute | solution.py:71
  53.1 1.6 %collective-permute-start.17 = (f32[4,2560]{1,0:T(4,128)S(1)}, f32[4,2560]{1,0:T(4,128)S(1)}, u32[]{:S(2)}, u32[]{:S(2)}) collective-permute-start(f32[4,2560]{1,0:T(4,128)S(1)} %add.11.x_ref), channel_id=1, source_target_pairs={{0,1},{1,0},{2,3},{3,2},{4,5},{5,4},{6,7},{7,6},{8,9},{9,8},{10,11... | collective-permute-start | bytes 122888 | tf_op jit(solution)/shard_map/ppermute | solution.py:71
  54.7 2.4 %collective-permute-done.17.y_ref = f32[4,2560]{1,0:T(4,128)S(1)} collective-permute-done((f32[4,2560]{1,0:T(4,128)S(1)}, f32[4,2560]{1,0:T(4,128)S(1)}, u32[]{:S(2)}, u32[]{:S(2)}) %collective-permute-start.17) | collective-permute-done | bytes 40992 | tf_op jit(solution)/shard_map/ppermute | solution.py:71
  57.2 2.8 %collective-permute-start.18 = (f32[4,2560]{1,0:T(4,128)S(1)}, f32[4,2560]{1,0:T(4,128)S(1)}, u32[]{:S(2)}, u32[]{:S(2)}) collective-permute-start(f32[4,2560]{1,0:T(4,128)S(1)} %add.12.x_ref), channel_id=1, source_target_pairs={{0,2},{1,3},{2,0},{3,1},{4,6},{5,7},{6,4},{7,5},{8,10},{9,11},{10,... | collective-permute-start | bytes 122888 | tf_op jit(solution)/shard_map/ppermute | solution.py:71
  59.9 2.1 %collective-permute-done.18.y_ref = f32[4,2560]{1,0:T(4,128)S(1)} collective-permute-done((f32[4,2560]{1,0:T(4,128)S(1)}, f32[4,2560]{1,0:T(4,128)S(1)}, u32[]{:S(2)}, u32[]{:S(2)}) %collective-permute-start.18) | collective-permute-done | bytes 40992 | tf_op jit(solution)/shard_map/ppermute | solution.py:71
  62.1 2.9 %collective-permute-start.20 = (bf16[1,64,1280]{2,1,0:T(8,128)(2,1)S(1)}, bf16[1,64,1280]{2,1,0:T(8,128)(2,1)S(1)}, u32[]{:S(2)}, u32[]{:S(2)}) collective-permute-start(bf16[1,64,1280]{2,1,0:T(8,128)(2,1)S(1)} %collective-permute-done.3.refs_1_), channel_id=1, source_target_pairs={{0,2},{2,3},{3,1},{1,0},{4,6},{6,7},{7,5},{5,4},{8,10},{10,11},{11... | collective-permute-start | bytes 491528 | tf_op jit(solution)/shard_map/ppermute | solution.py:61
  65.6 1.9 %collective-permute-start.23 = (bf16[1,64,2560]{2,1,0:T(8,128)(2,1)S(1)}, bf16[1,64,2560]{2,1,0:T(8,128)(2,1)S(1)}, u32[]{:S(2)}, u32[]{:S(2)}) collective-permute-start(bf16[1,64,2560]{2,1,0:T(8,128)(2,1)S(1)} %collective-permute-done.15.refs_2_), channel_id=1, source_target_pairs={{0,2},{2,3},{3,1},{1,0},{4,6},{6,7},{7,5},{5,4},{8,10},{10,11},{11... | collective-permute-start | bytes 983048 | tf_op jit(solution)/shard_map/ppermute | solution.py:61
  67.5 1.9 %collective-permute-done.20.refs_2_ = bf16[1,64,1280]{2,1,0:T(8,128)(2,1)S(1)} collective-permute-done((bf16[1,64,1280]{2,1,0:T(8,128)(2,1)S(1)}, bf16[1,64,1280]{2,1,0:T(8,128)(2,1)S(1)}, u32[]{:S(2)}, u32[]{:S(2)}) %collective-permute-start.20) | collective-permute-done | bytes 163872 | tf_op jit(solution)/shard_map/ppermute | solution.py:61
  69.5 3.4 %collective-permute-start.22 = (bf16[1,64,1280]{2,1,0:T(8,128)(2,1)S(1)}, bf16[1,64,1280]{2,1,0:T(8,128)(2,1)S(1)}, u32[]{:S(2)}, u32[]{:S(2)}) collective-permute-start(bf16[1,64,1280]{2,1,0:T(8,128)(2,1)S(1)} %collective-permute-done.20.refs_2_), channel_id=1, source_target_pairs={{0,2},{2,3},{3,1},{1,0},{4,6},{6,7},{7,5},{5,4},{8,10},{10,11},{11... | collective-permute-start | bytes 491528 | tf_op jit(solution)/shard_map/ppermute | solution.py:61
  73.8 2.7 %collective-permute-done.23.refs_3_ = bf16[1,64,2560]{2,1,0:T(8,128)(2,1)S(1)} collective-permute-done((bf16[1,64,2560]{2,1,0:T(8,128)(2,1)S(1)}, bf16[1,64,2560]{2,1,0:T(8,128)(2,1)S(1)}, u32[]{:S(2)}, u32[]{:S(2)}) %collective-permute-start.23) | collective-permute-done | bytes 327712 | tf_op jit(solution)/shard_map/ppermute | solution.py:61
  76.5 4.1 %rebuild.3 = (bf16[768,5120]{1,0:T(8,128)(2,1)}, bf16[1,768,5120]{2,1,0:T(8,128)(2,1)}) custom-call(bf16[1,256,768]{2,1,0:T(8,128)(2,1)S(1)} %copy-done, bf16[768,24]{1,0:T(8,128)(2,1)S(1)} %get-tuple-element.111.left_ref, bf16[24,5120]{1,0:T(8,128)(2,1)S(1)} %get-tuple-element.118.right_ref, bf16[1,768,5120]{2,1,0:T(8,128)(2,1)S(1)} %get-tuple-element.88.e_ref, ...), custom_call_target="tpu_custom_call" | custom-call | flops 1 | bytes 1 | tf_op jit(solution)/shard_map/rebuild/pallas_call | solution.py:442
  80.6 2.5 %rebuild.4 = (bf16[768,5120]{1,0:T(8,128)(2,1)}, bf16[1,768,5120]{2,1,0:T(8,128)(2,1)}) custom-call(bf16[1,256,768]{2,1,0:T(8,128)(2,1)S(1)} %copy-done, bf16[768,24]{1,0:T(8,128)(2,1)S(1)} %get-tuple-element.111.left_ref, bf16[24,5120]{1,0:T(8,128)(2,1)S(1)} %get-tuple-element.118.right_ref, ...), custom_call_target="tpu_custom_call", output_to_operand_aliasing={{0}: (8, {}), {1}: (9, {})} | custom-call | flops 1 | bytes 1 | tf_op jit(solution)/shard_map/rebuild/pallas_call | solution.py:442
  83.2 2.5 %rebuild.5 = (bf16[768,5120]{1,0:T(8,128)(2,1)}, bf16[1,768,5120]{2,1,0:T(8,128)(2,1)}) custom-call(bf16[1,256,768]{2,1,0:T(8,128)(2,1)S(1)} %copy-done, bf16[768,24]{1,0:T(8,128)(2,1)S(1)} %get-tuple-element.111.left_ref, bf16[24,5120]{1,0:T(8,128)(2,1)S(1)} %get-tuple-element.118.right_ref, ...), custom_call_target="tpu_custom_call", output_to_operand_aliasing={{0}: (8, {}), {1}: (9, {})} | custom-call | flops 1 | bytes 1 | tf_op jit(solution)/shard_map/rebuild/pallas_call | solution.py:442
  (43 shorter events, 17.6 us)
Async XLA Ops:
  1.8 17.3 %collective-permute-start.3 = (bf16[1,64,1280]{2,1,0:T(8,128)(2,1)S(1)}, bf16[1,64,1280]{2,1,0:T(8,128)(2,1)S(1)}, u32[]{:S(2)}, u32[]{:S(2)}) collective-permute-start(bf16[1,64,1280]{2,1,0:T(8,128)(2,1)S(1)} %get-tuple-element.71.refs_0_), channel_id=1, source_target_pairs={{0,2},{2,3},{3,1},{1,0},{4,6},{6,7},{7,5},{5,4},{8,10},{10,11},{11... | collective-permute-start | bytes 491528 | tf_op jit(solution)/shard_map/ppermute | solution.py:61
  13.1 5.5 %collective-permute-start = (f32[8,128]{1,0:T(8,128)S(1)}, f32[8,128]{1,0:T(8,128)S(1)}, u32[]{:S(2)}, u32[]{:S(2)}) collective-permute-start(f32[8,128]{1,0:T(8,128)S(1)} %get-tuple-element.80.refs_0_), channel_id=1, source_target_pairs={{0,1},{1,2},{2,3},{3,0},{4,5},{5,6},{6,7},{7,4},{8,9},{9,10},{10,1... | collective-permute-start | bytes 12296 | tf_op jit(solution)/shard_map/ppermute | solution.py:66
  13.2 5.4 %collective-permute-start.1 = (f32[8,128]{1,0:T(8,128)S(1)}, f32[8,128]{1,0:T(8,128)S(1)}, u32[]{:S(2)}, u32[]{:S(2)}) collective-permute-start(f32[8,128]{1,0:T(8,128)S(1)} %get-tuple-element.80.refs_0_), channel_id=1, source_target_pairs={{0,2},{1,3},{2,0},{3,1},{4,6},{5,7},{6,4},{7,5},{8,10},{9,11},{10,... | collective-permute-start | bytes 12296 | tf_op jit(solution)/shard_map/ppermute | solution.py:66
  15.1 4.1 %collective-permute-start.2 = (f32[8,128]{1,0:T(8,128)S(1)}, f32[8,128]{1,0:T(8,128)S(1)}, u32[]{:S(2)}, u32[]{:S(2)}) collective-permute-start(f32[8,128]{1,0:T(8,128)S(1)} %get-tuple-element.80.refs_0_), channel_id=1, source_target_pairs={{0,3},{1,0},{2,1},{3,2},{4,7},{5,4},{6,5},{7,6},{8,11},{9,8},{10,9... | collective-permute-start | bytes 12296 | tf_op jit(solution)/shard_map/ppermute | solution.py:66
  19.1 13.4 %collective-permute-start.7 = (bf16[1,64,2560]{2,1,0:T(8,128)(2,1)S(1)}, bf16[1,64,2560]{2,1,0:T(8,128)(2,1)S(1)}, u32[]{:S(2)}, u32[]{:S(2)}) collective-permute-start(bf16[1,64,2560]{2,1,0:T(8,128)(2,1)S(1)} %get-tuple-element.84.refs_1_.refs_0_), channel_id=1, source_target_pairs={{0,2},{2,3},{3,1},{1,0},{4,6},{6,7},{7,5},{5,4},{8,10},{10,11},{11... | collective-permute-start | bytes 983048 | tf_op jit(solution)/shard_map/ppermute | solution.py:61
  20.3 12.2 %collective-permute-start.8 = (bf16[1,64,1280]{2,1,0:T(8,128)(2,1)S(1)}, bf16[1,64,1280]{2,1,0:T(8,128)(2,1)S(1)}, u32[]{:S(2)}, u32[]{:S(2)}) collective-permute-start(bf16[1,64,1280]{2,1,0:T(8,128)(2,1)S(1)} %get-tuple-element.85.refs_2_.refs_0_), channel_id=1, source_target_pairs={{0,2},{2,3},{3,1},{1,0},{4,6},{6,7},{7,5},{5,4},{8,10},{10,11},{11... | collective-permute-start | bytes 491528 | tf_op jit(solution)/shard_map/ppermute | solution.py:61
  23.9 1.2 %collective-permute-start.4 = (f32[4,768]{1,0:T(4,128)S(1)}, f32[4,768]{1,0:T(4,128)S(1)}, u32[]{:S(2)}, u32[]{:S(2)}) collective-permute-start(f32[4,768]{1,0:T(4,128)S(1)} %left.1.x_ref), channel_id=1, source_target_pairs={{0,4},{4,0},{8,12},{12,8},{16,20},{20,16},{24,28},{28,24},{1,5},{5... | collective-permute-start | bytes 36872 | tf_op jit(solution)/shard_map/ppermute | solution.py:71
  25.1 3.7 %collective-permute-start.5 = (f32[4,768]{1,0:T(4,128)S(1)}, f32[4,768]{1,0:T(4,128)S(1)}, u32[]{:S(2)}, u32[]{:S(2)}) collective-permute-start(f32[4,768]{1,0:T(4,128)S(1)} %add.7.x_ref), channel_id=1, source_target_pairs={{0,8},{4,12},{8,0},{12,4},{16,24},{20,28},{24,16},{28,20},{1,9},{5... | collective-permute-start | bytes 36872 | tf_op jit(solution)/shard_map/ppermute | solution.py:71
  28.8 3.7 %collective-permute-start.6 = (f32[4,768]{1,0:T(4,128)S(1)}, f32[4,768]{1,0:T(4,128)S(1)}, u32[]{:S(2)}, u32[]{:S(2)}) collective-permute-start(f32[4,768]{1,0:T(4,128)S(1)} %add.8.x_ref), channel_id=1, source_target_pairs={{0,16},{4,20},{8,24},{12,28},{16,0},{20,4},{24,8},{28,12},{1,17},{... | collective-permute-start | bytes 36872 | tf_op jit(solution)/shard_map/ppermute | solution.py:71
  32.8 4.6 %collective-permute-start.10 = (f32[8,128]{1,0:T(8,128)S(1)}, f32[8,128]{1,0:T(8,128)S(1)}, u32[]{:S(2)}, u32[]{:S(2)}) collective-permute-start(f32[8,128]{1,0:T(8,128)S(1)} %get-tuple-element.91), channel_id=1, source_target_pairs={{0,2},{1,3},{2,0},{3,1},{4,6},{5,7},{6,4},{7,5},{8,10},{9,11},{10,... | collective-permute-start | bytes 12296 | tf_op jit(solution)/shard_map/ppermute | solution.py:66
  33.3 4.1 %collective-permute-start.11 = (f32[8,128]{1,0:T(8,128)S(1)}, f32[8,128]{1,0:T(8,128)S(1)}, u32[]{:S(2)}, u32[]{:S(2)}) collective-permute-start(f32[8,128]{1,0:T(8,128)S(1)} %get-tuple-element.92), channel_id=1, source_target_pairs={{0,3},{1,0},{2,1},{3,2},{4,7},{5,4},{6,5},{7,6},{8,11},{9,8},{10,9... | collective-permute-start | bytes 12296 | tf_op jit(solution)/shard_map/ppermute | solution.py:66
  35.8 5.5 %collective-permute-start.9 = (f32[8,128]{1,0:T(8,128)S(1)}, f32[8,128]{1,0:T(8,128)S(1)}, u32[]{:S(2)}, u32[]{:S(2)}) collective-permute-start(f32[8,128]{1,0:T(8,128)S(1)} %get-tuple-element.90), channel_id=1, source_target_pairs={{0,1},{1,2},{2,3},{3,0},{4,5},{5,6},{6,7},{7,4},{8,9},{9,10},{10,1... | collective-permute-start | bytes 12296 | tf_op jit(solution)/shard_map/ppermute | solution.py:66
  41.3 11.8 %collective-permute-start.15 = (bf16[1,64,2560]{2,1,0:T(8,128)(2,1)S(1)}, bf16[1,64,2560]{2,1,0:T(8,128)(2,1)S(1)}, u32[]{:S(2)}, u32[]{:S(2)}) collective-permute-start(bf16[1,64,2560]{2,1,0:T(8,128)(2,1)S(1)} %collective-permute-done.7.refs_1_), channel_id=1, source_target_pairs={{0,2},{2,3},{3,1},{1,0},{4,6},{6,7},{7,5},{5,4},{8,10},{10,11},{11... | collective-permute-start | bytes 983048 | tf_op jit(solution)/shard_map/ppermute | solution.py:61
  41.3 11.8 %collective-permute-start.16 = (bf16[1,64,1280]{2,1,0:T(8,128)(2,1)S(1)}, bf16[1,64,1280]{2,1,0:T(8,128)(2,1)S(1)}, u32[]{:S(2)}, u32[]{:S(2)}) collective-permute-start(bf16[1,64,1280]{2,1,0:T(8,128)(2,1)S(1)} %collective-permute-done.8.refs_1_), channel_id=1, source_target_pairs={{0,2},{2,3},{3,1},{1,0},{4,6},{6,7},{7,5},{5,4},{8,10},{10,11},{11... | collective-permute-start | bytes 491528 | tf_op jit(solution)/shard_map/ppermute | solution.py:61
  43.7 1.3 %collective-permute-start.12 = (f32[4,2560]{1,0:T(4,128)S(1)}, f32[4,2560]{1,0:T(4,128)S(1)}, u32[]{:S(2)}, u32[]{:S(2)}) collective-permute-start(f32[4,2560]{1,0:T(4,128)S(1)} %get-tuple-element.105), channel_id=1, source_target_pairs={{0,4},{4,0},{8,12},{12,8},{16,20},{20,16},{24,28},{28,24},{1,5},{5... | collective-permute-start | bytes 122888 | tf_op jit(solution)/shard_map/ppermute | solution.py:71
  45.0 4.0 %collective-permute-start.13 = (f32[4,2560]{1,0:T(4,128)S(1)}, f32[4,2560]{1,0:T(4,128)S(1)}, u32[]{:S(2)}, u32[]{:S(2)}) collective-permute-start(f32[4,2560]{1,0:T(4,128)S(1)} %add.9.x_ref), channel_id=1, source_target_pairs={{0,8},{4,12},{8,0},{12,4},{16,24},{20,28},{24,16},{28,20},{1,9},{5... | collective-permute-start | bytes 122888 | tf_op jit(solution)/shard_map/ppermute | solution.py:71
  49.0 4.0 %collective-permute-start.14 = (f32[4,2560]{1,0:T(4,128)S(1)}, f32[4,2560]{1,0:T(4,128)S(1)}, u32[]{:S(2)}, u32[]{:S(2)}) collective-permute-start(f32[4,2560]{1,0:T(4,128)S(1)} %add.10.x_ref), channel_id=1, source_target_pairs={{0,16},{4,20},{8,24},{12,28},{16,0},{20,4},{24,8},{28,12},{1,17},{... | collective-permute-start | bytes 122888 | tf_op jit(solution)/shard_map/ppermute | solution.py:71
  53.1 4.1 %collective-permute-start.17 = (f32[4,2560]{1,0:T(4,128)S(1)}, f32[4,2560]{1,0:T(4,128)S(1)}, u32[]{:S(2)}, u32[]{:S(2)}) collective-permute-start(f32[4,2560]{1,0:T(4,128)S(1)} %add.11.x_ref), channel_id=1, source_target_pairs={{0,1},{1,0},{2,3},{3,2},{4,5},{5,4},{6,7},{7,6},{8,9},{9,8},{10,11... | collective-permute-start | bytes 122888 | tf_op jit(solution)/shard_map/ppermute | solution.py:71
  57.2 4.9 %collective-permute-start.18 = (f32[4,2560]{1,0:T(4,128)S(1)}, f32[4,2560]{1,0:T(4,128)S(1)}, u32[]{:S(2)}, u32[]{:S(2)}) collective-permute-start(f32[4,2560]{1,0:T(4,128)S(1)} %add.12.x_ref), channel_id=1, source_target_pairs={{0,2},{1,3},{2,0},{3,1},{4,6},{5,7},{6,4},{7,5},{8,10},{9,11},{10,... | collective-permute-start | bytes 122888 | tf_op jit(solution)/shard_map/ppermute | solution.py:71
  62.1 2.9 %collective-permute-start.19 = (f32[4,2560]{1,0:T(4,128)S(1)}, f32[4,2560]{1,0:T(4,128)S(1)}, u32[]{:S(2)}, u32[]{:S(2)}) collective-permute-start(f32[4,2560]{1,0:T(4,128)S(1)} %add.13.mine_ref), channel_id=1, source_target_pairs={{0,4},{4,0},{8,12},{12,8},{16,20},{20,16},{24,28},{28,24},{1,5},{5... | collective-permute-start | bytes 122888 | tf_op jit(solution)/shard_map/ppermute | solution.py:71
  62.1 7.4 %collective-permute-start.20 = (bf16[1,64,1280]{2,1,0:T(8,128)(2,1)S(1)}, bf16[1,64,1280]{2,1,0:T(8,128)(2,1)S(1)}, u32[]{:S(2)}, u32[]{:S(2)}) collective-permute-start(bf16[1,64,1280]{2,1,0:T(8,128)(2,1)S(1)} %collective-permute-done.3.refs_1_), channel_id=1, source_target_pairs={{0,2},{2,3},{3,1},{1,0},{4,6},{6,7},{7,5},{5,4},{8,10},{10,11},{11... | collective-permute-start | bytes 491528 | tf_op jit(solution)/shard_map/ppermute | solution.py:61
  65.6 10.8 %collective-permute-start.23 = (bf16[1,64,2560]{2,1,0:T(8,128)(2,1)S(1)}, bf16[1,64,2560]{2,1,0:T(8,128)(2,1)S(1)}, u32[]{:S(2)}, u32[]{:S(2)}) collective-permute-start(bf16[1,64,2560]{2,1,0:T(8,128)(2,1)S(1)} %collective-permute-done.15.refs_2_), channel_id=1, source_target_pairs={{0,2},{2,3},{3,1},{1,0},{4,6},{6,7},{7,5},{5,4},{8,10},{10,11},{11... | collective-permute-start | bytes 983048 | tf_op jit(solution)/shard_map/ppermute | solution.py:61
  69.5 11.2 %collective-permute-start.22 = (bf16[1,64,1280]{2,1,0:T(8,128)(2,1)S(1)}, bf16[1,64,1280]{2,1,0:T(8,128)(2,1)S(1)}, u32[]{:S(2)}, u32[]{:S(2)}) collective-permute-start(bf16[1,64,1280]{2,1,0:T(8,128)(2,1)S(1)} %collective-permute-done.20.refs_2_), channel_id=1, source_target_pairs={{0,2},{2,3},{3,1},{1,0},{4,6},{6,7},{7,5},{5,4},{8,10},{10,11},{11... | collective-permute-start | bytes 491528 | tf_op jit(solution)/shard_map/ppermute | solution.py:61
  72.8 10.4 %collective-permute-start.21 = (bf16[1,64,1280]{2,1,0:T(8,128)(2,1)S(1)}, bf16[1,64,1280]{2,1,0:T(8,128)(2,1)S(1)}, u32[]{:S(2)}, u32[]{:S(2)}) collective-permute-start(bf16[1,64,1280]{2,1,0:T(8,128)(2,1)S(1)} %collective-permute-done.16.refs_2_), channel_id=1, source_target_pairs={{0,2},{2,3},{3,1},{1,0},{4,6},{6,7},{7,5},{5,4},{8,10},{10,11},{11... | collective-permute-start | bytes 491528 | tf_op jit(solution)/shard_map/ppermute | solution.py:61
  (1 other events, 23.0 us)

commit v5 on v4

--- a/solution.py
+++ b/solution.py
@@ -76,49 +76,46 @@
     return [1 << i for i in range(n.bit_length() - 1)]
 
 
-def cut_kernel(g_hbm, *refs):
-    chunks, sems = refs[:-1], refs[-1]
-    copies = []
+def token_factor_kernel(w_hbm, g_hbm, *refs):
+    chunks = refs[:-5]
+    gw_ref, terms_ref, w, w3, sems = refs[-5:]
+    rank = w.shape[0]
+    copies = [pltpu.make_async_copy(w_hbm, w, sems.at[0])]
     at = 0
     for c, chunk in enumerate(chunks):
         part = chunk.shape[2]
-        copies.append(pltpu.make_async_copy(g_hbm.at[:, :, pl.ds(at, part)], chunk, sems.at[c]))
-        copies[-1].start()
+        copies.append(pltpu.make_async_copy(g_hbm.at[:, :, pl.ds(at, part)], chunk, sems.at[c + 1]))
         at += part
     for copy in copies:
-        copy.wait()
-
-
-def products_kernel(parts, w_hbm, e_hbm, *refs):
-    chunks = refs[:parts]
-    gw_ref, ew_ref, e_ref, w, w3, terms, w_sem, sems = refs[parts:]
-    rank = w.shape[0]
+        copy.start()
+    copies[0].wait()
+    terms = stack3(w[...] * SHRINK, w3)
+    terms_ref[...] = terms
+    total = 0.0
+    at = 0
+    for c, chunk in enumerate(chunks):
+        copies[c + 1].wait()
+        part = chunk.shape[2]
+        total += dot(terms[:, at : at + part], chunk[0], (1, 1))
+        at += part
+    gw_ref[...] = jnp.zeros_like(gw_ref)
+    gw_ref[0:rank, 0 : total.shape[1]] = sum3(total, rank)
+
+
+def error_left_kernel(terms_ref, e_hbm, out_ref, e_ref, sems):
+    rank = out_ref.shape[0]
     count = sems.shape[0]
     high = e_ref.shape[1] // count
-    w_copy = pltpu.make_async_copy(w_hbm, w, w_sem)
-    w_copy.start()
     copies = []
     for c in range(count):
         rows = pl.ds(c * high, high)
         copies.append(pltpu.make_async_copy(e_hbm.at[:, rows, :], e_ref.at[:, rows, :], sems.at[c]))
         copies[-1].start()
-    w_copy.wait()
-    stack3(w[...] * SHRINK, w3)
-    terms[...] = w3[...].T.astype(BF16)
-    total = 0.0
-    at = 0
-    for chunk in chunks:
-        part = chunk.shape[2]
-        total += dot(chunk[0], terms[at : at + part, :], (1, 0))
-        at += part
-    gw_ref[...] = jnp.zeros_like(gw_ref)
-    gw_ref[0:rank, 0 : total.shape[0]] = sum3(total.T, rank)
-    group = 2 if count % 2 == 0 and (2 * high) % 128 == 0 else count
-    for c in range(0, count, group):
-        for copy in copies[c : c + group]:
-            copy.wait()
-        rows = slice(c * high, (c + group) * high)
-        ew_ref[:, rows] = sum3(dot(e_ref[0, rows, :], terms[...], (1, 0)).T, rank)
+    terms = terms_ref[...]
+    for c in range(count):
+        copies[c].wait()
+        rows = slice(c * high, (c + 1) * high)
+        out_ref[:, rows] = sum3(dot(terms, e_ref[0, rows, :], (1, 1)), rank)
 
 
 def left_kernel(a_ref, e_ref, *refs):
@@ -341,12 +338,18 @@
     def add(x, y):
         return call(add_kernel, sds(x.shape, F32), [], "add", 1e5, 1e5)(x, y)
 
-    chunks = call(
-        cut_kernel,
-        [sds((1, tok, part), BF16) for part in widths],
-        [dma((parts,))],
-        "cut", 1e3, 1e6, [hbm],
-    )(pin(out_grads))
+    *chunks, gw, w_terms = call(
+        token_factor_kernel,
+        [sds((1, tok, part), BF16) for part in widths]
+        + [sds((8, 128), F32), sds((3 * rank, width), BF16)],
+        [
+            pltpu.VMEM((rank, width), F32),
+            pltpu.VMEM((3 * rank, width), F32),
+            dma((parts + 1,)),
+        ],
+        "token_factor", 1e3, 1e6, [hbm, hbm],
+    )(pin(w), pin(out_grads))
+    gws = exchange([gw] * n, "tensor", n)
     rings = [[chunk] for chunk in chunks]
 
     def turn(which, after):
@@ -362,30 +365,21 @@
             rings[c][-1] = x
         return before
 
-    small, others = [0], [1, 2]
-    turn(small, w)
-
-    gw, ew, error_v = call(
-        functools.partial(products_kernel, parts),
-        [sds((8, 128), F32), sds((rank, rows), F32), sds((1, rows, width), BF16)],
-        [
-            pltpu.VMEM((rank, width), F32),
-            pltpu.VMEM((3 * rank, width), F32),
-            pltpu.VMEM((width, 3 * rank), BF16),
-            dma(()),
-            dma((12,)),
-        ],
-        "products", 2e9, rows * width * 2, [hbm, hbm] + [vmem] * parts, 20,
-    )(pin(w), pin(error_buffer), *chunks)
-    gws = exchange([gw] * n, "tensor", n)
-    gws = settle(small, gws)
-    gws = turn(others, gws)
+    first, rest = [0], [1, 2]
+    w_terms, gws = turn(first + rest, (w_terms, gws))
+    ew, error_v = call(
+        error_left_kernel,
+        [sds((rank, rows), F32), sds((1, rows, width), BF16)],
+        [dma((rows // 128,))],
+        "error_left", 2e9, rows * width * 2, [vmem, hbm],
+    )(w_terms, pin(error_buffer))
+
     left = call(
         left_kernel, sds((rank, rows), F32), [pltpu.VMEM((3 * rank, tok), F32)], "left", 1e7, 1e6
     )(activations, ew, *gws)
     for bit in bits(m)[:-1]:
         left = add(left, swap(left, "dp", m, bit))
-    last = settle(others, swap(left, "dp", m, bits(m)[-1]))
+    last = settle(first + rest, swap(left, "dp", m, bits(m)[-1]))
 
     mean, *msgs = call(
         functools.partial(mean_kernel, n, 1.0 / (SHRINK * m)),
@@ -401,7 +395,7 @@
         [pltpu.VMEM((3 * rank, rows), F32)],
         "error_right", 2e9, rows * width * 2,
     )(mean, error_v)
-    msgs = turn(others, msgs)
+    msgs = turn(first, msgs)
 
     ortho, keep, send = call(
         functools.partial(right_kernel, n, parts),
@@ -415,12 +409,12 @@
         "right", 1e7, 1e6,
     )(mean, right_raw, *chunks, *msgs)
     total = add(keep, swap(send, "dp", m, 1))
+    total = settle(first, total)
+    for bit in bits(n):
+        total = add(total, swap(total, "tensor", n, bit))
+    total = turn(rest + first, total)
     for bit in bits(m)[1:]:
         total = add(total, swap(total, "dp", m, bit))
-    total = settle(others, total)
-    for bit in bits(n):
-        total = add(total, swap(total, "tensor", n, bit))
-    total = turn(small, total)
 
     terms = len(LEFT_TERMS) * rank
     whole, left_terms, right_terms = call(
@@ -434,10 +428,10 @@
         "factor", 1e6, 1e6,
     )(ortho, total, swap(total, "dp", m, 1))
 
-    for _ in range(3, n):
-        right_terms = turn([1, 0, 2], right_terms)
+    for c in rest + (first + rest) * (n - 4):
+        right_terms = turn([c], right_terms)
     outs = ()
-    for c in [1, 0, 2]:
+    for c in rest[:1] + first + rest[1:]:
         ring, part, at = rings[c], widths[c], sum(widths[:c])
         outs = pl.pallas_call(
             functools.partial(final_kernel, n, at),

time: 86.1 us -> 88.4 us (1.027)
  waiting for transfers between devices: 27.9 us -> 41.1 us
  starting transfers between devices: 36.3 us -> 28.2 us
  Pallas kernels: 20.8 us -> 18.2 us
    ppermute x9, starting transfers between devices: 18.2 us -> 9.65 us  [ring_step(): lax.ppermute(x, axis, [(ring[p], ring[(p + 1) % n]) for p in range(n)])]
    ppermute x9, waiting for transfers between devices: 4.62 us -> 12.3 us  [ring_step(): lax.ppermute(x, axis, [(ring[p], ring[(p + 1) % n]) for p in range(n)])]
    ppermute x9, waiting for transfers between devices: 16.3 us -> 21 us  [swap(): return lax.ppermute(x, axis, [(i, i ^ bit) for i in range(n)])]
    ppermute x6, starting transfers between devices: 7.48 us -> 11.4 us  [exchange(): lax.ppermute(pieces[k], axis, [(i, (i + k) % n) for i in range(n)])]
    ppermute x9, starting transfers between devices: 10.6 us -> 7.11 us  [swap(): return lax.ppermute(x, axis, [(i, i ^ bit) for i in range(n)])]
    pallas_call x2, Pallas kernels: 8.35 us -> 5.74 us  [the longest x1 4.14 us: per_device(): call(error_left_kernel, [sds((rank, rows), F32), sds((1, rows, width), BF...]
  transfers between devices with their start and end apart: 24 -> 24, of which waited for: 14 -> 16; matrix products, arithmetic and copies ran while one was open for 0% -> 0% of each run, Pallas kernels for 19% -> 16%
where the time goes in v5:
time: 88.4 us; the launch traced here: 88.3 us
  waiting for transfers between devices  41.1 us (46%)
  starting transfers between devices  28.2 us (32%)
  Pallas kernels  18.2 us (21%)
    ppermute x9, waiting for transfers between devices, swap(): return lax.ppermute(x, axis, [(i, i ^ bit) for i in range(n)])  21 us
    ppermute x9, waiting for transfers between devices, ring_step(): lax.ppermute(x, axis, [(ring[p], ring[(p + 1) % n]) for p in range(n)])  12.3 us
    ppermute x6, starting transfers between devices, exchange(): lax.ppermute(pieces[k], axis, [(i, (i + k) % n) for i in range(n)])  11.4 us
    ppermute x9, starting transfers between devices, ring_step(): lax.ppermute(x, axis, [(ring[p], ring[(p + 1) % n]) for p in range(n)])  9.65 us
    pallas_call x3, Pallas kernels, per_device(): pl.pallas_call(functools.partial(final_kernel, n, at), in_specs=[vmem] *...  9.26 us
    ppermute x6, waiting for transfers between devices, exchange(): lax.ppermute(pieces[k], axis, [(i, (i + k) % n) for i in range(n)])  7.76 us
    ppermute x9, starting transfers between devices, swap(): return lax.ppermute(x, axis, [(i, i ^ bit) for i in range(n)])  7.11 us
    pallas_call x1, Pallas kernels, per_device(): call(error_left_kernel, [sds((rank, rows), F32), sds((1, rows, width), BF...  4.14 us
  transfers between devices with their start and end apart: 24, of which 16 were waited for; matrix products, arithmetic and copies ran while one was open for 0% of the time, Pallas kernels for 16%

profile of v5, /device:TPU:0, one launch (start us, length us, event | category | flops | bytes accessed | tf_op | source)
XLA Modules:
  0.0 88.3 jit_solution(10669891608065609510)
XLA Ops:
  0.6 1.6 %token_factor.1 = (bf16[1,64,1280]{2,1,0:T(8,128)(2,1)S(1)}, bf16[1,64,2560]{2,1,0:T(8,128)(2,1)S(1)}, bf16[1,64,1280]{2,1,0:T(8,128)(2,1)S(1)}, f32[8,128]{1,0:T(8,128)S(1)}, bf16[12,5120]{1,0:T(8,128)(2,1)S(1)}) custom-call(f32[4,5120]{1,0:T(4,128)} %bitcast.2, bf16[1,64,5120]{2,1,0:T(8,128)(2,1)} %g_hbm.1), custom_call_target="tpu_custom_call" | custom-call | flops 1 | bytes 1 | tf_op jit(solution)/shard_map/token_factor/pallas_call | solution.py:341
  2.2 3.1 %collective-permute-start = (f32[8,128]{1,0:T(8,128)S(1)}, f32[8,128]{1,0:T(8,128)S(1)}, u32[]{:S(2)}, u32[]{:S(2)}) collective-permute-start(f32[8,128]{1,0:T(8,128)S(1)} %get-tuple-element.83.refs_0_), channel_id=1, source_target_pairs={{0,1},{1,2},{2,3},{3,0},{4,5},{5,6},{6,7},{7,4},{8,9},{9,10},{10,1... | collective-permute-start | bytes 12296 | tf_op jit(solution)/shard_map/ppermute | solution.py:66
  5.3 2.6 %collective-permute-start.1 = (f32[8,128]{1,0:T(8,128)S(1)}, f32[8,128]{1,0:T(8,128)S(1)}, u32[]{:S(2)}, u32[]{:S(2)}) collective-permute-start(f32[8,128]{1,0:T(8,128)S(1)} %get-tuple-element.83.refs_0_), channel_id=1, source_target_pairs={{0,2},{1,3},{2,0},{3,1},{4,6},{5,7},{6,4},{7,5},{8,10},{9,11},{10,... | collective-permute-start | bytes 12296 | tf_op jit(solution)/shard_map/ppermute | solution.py:66
  9.9 1.7 %collective-permute-done.2.refs_3_ = f32[8,128]{1,0:T(8,128)S(1)} collective-permute-done((f32[8,128]{1,0:T(8,128)S(1)}, f32[8,128]{1,0:T(8,128)S(1)}, u32[]{:S(2)}, u32[]{:S(2)}) %collective-permute-start.2) | collective-permute-done | bytes 4128 | tf_op jit(solution)/shard_map/ppermute | solution.py:66
  12.4 2.8 %collective-permute-start.8 = (bf16[1,64,1280]{2,1,0:T(8,128)(2,1)S(1)}, bf16[1,64,1280]{2,1,0:T(8,128)(2,1)S(1)}, u32[]{:S(2)}, u32[]{:S(2)}) collective-permute-start(bf16[1,64,1280]{2,1,0:T(8,128)(2,1)S(1)} %get-tuple-element.89.refs_2_.refs_0_), channel_id=1, source_target_pairs={{0,2},{2,3},{3,1},{1,0},{4,6},{6,7},{7,5},{5,4},{8,10},{10,11},{11... | collective-permute-start | bytes 491528 | tf_op jit(solution)/shard_map/ppermute | solution.py:61
  15.3 4.1 %error_left.1 = (f32[4,768]{1,0:T(4,128)S(1)}, bf16[1,768,5120]{2,1,0:T(8,128)(2,1)S(1)}) custom-call(bf16[12,5120]{1,0:T(8,128)(2,1)S(1)} %get-tuple-element.81.terms_ref, bf16[1,768,5120]{2,1,0:T(8,128)(2,1)} %e_hbm.1), custom_call_target="tpu_custom_call" | custom-call | flops 1 | bytes 1 | tf_op jit(solution)/shard_map/error_left/pallas_call | solution.py:370
  20.9 1.5 %collective-permute-start.4 = (f32[4,768]{1,0:T(4,128)S(1)}, f32[4,768]{1,0:T(4,128)S(1)}, u32[]{:S(2)}, u32[]{:S(2)}) collective-permute-start(f32[4,768]{1,0:T(4,128)S(1)} %add.7.x_ref), channel_id=1, source_target_pairs={{0,8},{4,12},{8,0},{12,4},{16,24},{20,28},{24,16},{28,20},{1,9},{5... | collective-permute-start | bytes 36872 | tf_op jit(solution)/shard_map/ppermute | solution.py:71
  22.4 2.2 %collective-permute-done.4.y_ref = f32[4,768]{1,0:T(4,128)S(1)} collective-permute-done((f32[4,768]{1,0:T(4,128)S(1)}, f32[4,768]{1,0:T(4,128)S(1)}, u32[]{:S(2)}, u32[]{:S(2)}) %collective-permute-start.4) | collective-permute-done | bytes 12320 | tf_op jit(solution)/shard_map/ppermute | solution.py:71
  24.6 1.5 %collective-permute-start.5 = (f32[4,768]{1,0:T(4,128)S(1)}, f32[4,768]{1,0:T(4,128)S(1)}, u32[]{:S(2)}, u32[]{:S(2)}) collective-permute-start(f32[4,768]{1,0:T(4,128)S(1)} %add.8.x_ref), channel_id=1, source_target_pairs={{0,16},{4,20},{8,24},{12,28},{16,0},{20,4},{24,8},{28,12},{1,17},{... | collective-permute-start | bytes 36872 | tf_op jit(solution)/shard_map/ppermute | solution.py:71
  26.1 2.2 %collective-permute-done.5.y_ref = f32[4,768]{1,0:T(4,128)S(1)} collective-permute-done((f32[4,768]{1,0:T(4,128)S(1)}, f32[4,768]{1,0:T(4,128)S(1)}, u32[]{:S(2)}, u32[]{:S(2)}) %collective-permute-start.5) | collective-permute-done | bytes 12320 | tf_op jit(solution)/shard_map/ppermute | solution.py:71
  29.9 3.1 %collective-permute-start.11 = (f32[8,128]{1,0:T(8,128)S(1)}, f32[8,128]{1,0:T(8,128)S(1)}, u32[]{:S(2)}, u32[]{:S(2)}) collective-permute-start(f32[8,128]{1,0:T(8,128)S(1)} %get-tuple-element.96), channel_id=1, source_target_pairs={{0,3},{1,0},{2,1},{3,2},{4,7},{5,4},{6,5},{7,6},{8,11},{9,8},{10,9... | collective-permute-start | bytes 12296 | tf_op jit(solution)/shard_map/ppermute | solution.py:66
  34.4 4.2 %collective-permute-done.9.refs_4_ = f32[8,128]{1,0:T(8,128)S(1)} collective-permute-done((f32[8,128]{1,0:T(8,128)S(1)}, f32[8,128]{1,0:T(8,128)S(1)}, u32[]{:S(2)}, u32[]{:S(2)}) %collective-permute-start.9) | collective-permute-done | bytes 4128 | tf_op jit(solution)/shard_map/ppermute | solution.py:66
  41.8 2.1 %collective-permute-done.13.refs_2_ = bf16[1,64,1280]{2,1,0:T(8,128)(2,1)S(1)} collective-permute-done((bf16[1,64,1280]{2,1,0:T(8,128)(2,1)S(1)}, bf16[1,64,1280]{2,1,0:T(8,128)(2,1)S(1)}, u32[]{:S(2)}, u32[]{:S(2)}) %collective-permute-start.13) | collective-permute-done | bytes 163872 | tf_op jit(solution)/shard_map/ppermute | solution.py:61
  43.9 4.0 %collective-permute-done.14.y_ref = f32[4,2560]{1,0:T(4,128)S(1)} collective-permute-done((f32[4,2560]{1,0:T(4,128)S(1)}, f32[4,2560]{1,0:T(4,128)S(1)}, u32[]{:S(2)}, u32[]{:S(2)}) %collective-permute-start.14) | collective-permute-done | bytes 40992 | tf_op jit(solution)/shard_map/ppermute | solution.py:71
  48.8 4.1 %collective-permute-done.15.y_ref = f32[4,2560]{1,0:T(4,128)S(1)} collective-permute-done((f32[4,2560]{1,0:T(4,128)S(1)}, f32[4,2560]{1,0:T(4,128)S(1)}, u32[]{:S(2)}, u32[]{:S(2)}) %collective-permute-start.15) | collective-permute-done | bytes 40992 | tf_op jit(solution)/shard_map/ppermute | solution.py:71
  55.5 2.5 %collective-permute-done.16.y_ref = f32[4,2560]{1,0:T(4,128)S(1)} collective-permute-done((f32[4,2560]{1,0:T(4,128)S(1)}, f32[4,2560]{1,0:T(4,128)S(1)}, u32[]{:S(2)}, u32[]{:S(2)}) %collective-permute-start.16) | collective-permute-done | bytes 40992 | tf_op jit(solution)/shard_map/ppermute | solution.py:71
  58.0 1.5 %collective-permute-start.17 = (f32[4,2560]{1,0:T(4,128)S(1)}, f32[4,2560]{1,0:T(4,128)S(1)}, u32[]{:S(2)}, u32[]{:S(2)}) collective-permute-start(f32[4,2560]{1,0:T(4,128)S(1)} %add.12.x_ref), channel_id=1, source_target_pairs={{0,16},{4,20},{8,24},{12,28},{16,0},{20,4},{24,8},{28,12},{1,17},{... | collective-permute-start | bytes 122888 | tf_op jit(solution)/shard_map/ppermute | solution.py:71
  59.6 2.5 %collective-permute-done.17.y_ref = f32[4,2560]{1,0:T(4,128)S(1)} collective-permute-done((f32[4,2560]{1,0:T(4,128)S(1)}, f32[4,2560]{1,0:T(4,128)S(1)}, u32[]{:S(2)}, u32[]{:S(2)}) %collective-permute-start.17) | collective-permute-done | bytes 40992 | tf_op jit(solution)/shard_map/ppermute | solution.py:71
  64.1 1.6 %collective-permute-start.20 = (bf16[1,64,1280]{2,1,0:T(8,128)(2,1)S(1)}, bf16[1,64,1280]{2,1,0:T(8,128)(2,1)S(1)}, u32[]{:S(2)}, u32[]{:S(2)}) collective-permute-start(bf16[1,64,1280]{2,1,0:T(8,128)(2,1)S(1)} %collective-permute-done.8.refs_1_), channel_id=1, source_target_pairs={{0,2},{2,3},{3,1},{1,0},{4,6},{6,7},{7,5},{5,4},{8,10},{10,11},{11... | collective-permute-start | bytes 491528 | tf_op jit(solution)/shard_map/ppermute | solution.py:61
  65.7 2.1 %collective-permute-start.22 = (bf16[1,64,1280]{2,1,0:T(8,128)(2,1)S(1)}, bf16[1,64,1280]{2,1,0:T(8,128)(2,1)S(1)}, u32[]{:S(2)}, u32[]{:S(2)}) collective-permute-start(bf16[1,64,1280]{2,1,0:T(8,128)(2,1)S(1)} %collective-permute-done.13.refs_2_), channel_id=1, source_target_pairs={{0,2},{2,3},{3,1},{1,0},{4,6},{6,7},{7,5},{5,4},{8,10},{10,11},{11... | collective-permute-start | bytes 491528 | tf_op jit(solution)/shard_map/ppermute | solution.py:61
  67.8 10.3 %collective-permute-done.20.refs_2_ = bf16[1,64,1280]{2,1,0:T(8,128)(2,1)S(1)} collective-permute-done((bf16[1,64,1280]{2,1,0:T(8,128)(2,1)S(1)}, bf16[1,64,1280]{2,1,0:T(8,128)(2,1)S(1)}, u32[]{:S(2)}, u32[]{:S(2)}) %collective-permute-start.20) | collective-permute-done | bytes 163872 | tf_op jit(solution)/shard_map/ppermute | solution.py:61
  79.0 4.2 %rebuild.3 = (bf16[768,5120]{1,0:T(8,128)(2,1)}, bf16[1,768,5120]{2,1,0:T(8,128)(2,1)}) custom-call(bf16[1,256,768]{2,1,0:T(8,128)(2,1)S(1)} %copy-done, bf16[768,24]{1,0:T(8,128)(2,1)S(1)} %get-tuple-element.113.left_ref, bf16[24,5120]{1,0:T(8,128)(2,1)S(1)} %get-tuple-element.118.right_ref, bf16[1,768,5120]{2,1,0:T(8,128)(2,1)S(1)} %get-tuple-element.92.e_ref, ...), custom_call_target="tpu_custom_call" | custom-call | flops 1 | bytes 1 | tf_op jit(solution)/shard_map/rebuild/pallas_call | solution.py:436
  83.2 2.6 %rebuild.4 = (bf16[768,5120]{1,0:T(8,128)(2,1)}, bf16[1,768,5120]{2,1,0:T(8,128)(2,1)}) custom-call(bf16[1,256,768]{2,1,0:T(8,128)(2,1)S(1)} %copy-done, bf16[768,24]{1,0:T(8,128)(2,1)S(1)} %get-tuple-element.113.left_ref, bf16[24,5120]{1,0:T(8,128)(2,1)S(1)} %get-tuple-element.118.right_ref, ...), custom_call_target="tpu_custom_call", output_to_operand_aliasing={{0}: (8, {}), {1}: (9, {})} | custom-call | flops 1 | bytes 1 | tf_op jit(solution)/shard_map/rebuild/pallas_call | solution.py:436
  85.7 2.5 %rebuild.5 = (bf16[768,5120]{1,0:T(8,128)(2,1)}, bf16[1,768,5120]{2,1,0:T(8,128)(2,1)}) custom-call(bf16[1,256,768]{2,1,0:T(8,128)(2,1)S(1)} %copy-done, bf16[768,24]{1,0:T(8,128)(2,1)S(1)} %get-tuple-element.113.left_ref, bf16[24,5120]{1,0:T(8,128)(2,1)S(1)} %get-tuple-element.118.right_ref, ...), custom_call_target="tpu_custom_call", output_to_operand_aliasing={{0}: (8, {}), {1}: (9, {})} | custom-call | flops 1 | bytes 1 | tf_op jit(solution)/shard_map/rebuild/pallas_call | solution.py:436
  (43 shorter events, 17.1 us)
Async XLA Ops:
  2.2 7.0 %collective-permute-start = (f32[8,128]{1,0:T(8,128)S(1)}, f32[8,128]{1,0:T(8,128)S(1)}, u32[]{:S(2)}, u32[]{:S(2)}) collective-permute-start(f32[8,128]{1,0:T(8,128)S(1)} %get-tuple-element.83.refs_0_), channel_id=1, source_target_pairs={{0,1},{1,2},{2,3},{3,0},{4,5},{5,6},{6,7},{7,4},{8,9},{9,10},{10,1... | collective-permute-start | bytes 12296 | tf_op jit(solution)/shard_map/ppermute | solution.py:66
  5.3 4.5 %collective-permute-start.1 = (f32[8,128]{1,0:T(8,128)S(1)}, f32[8,128]{1,0:T(8,128)S(1)}, u32[]{:S(2)}, u32[]{:S(2)}) collective-permute-start(f32[8,128]{1,0:T(8,128)S(1)} %get-tuple-element.83.refs_0_), channel_id=1, source_target_pairs={{0,2},{1,3},{2,0},{3,1},{4,6},{5,7},{6,4},{7,5},{8,10},{9,11},{10,... | collective-permute-start | bytes 12296 | tf_op jit(solution)/shard_map/ppermute | solution.py:66
  7.9 3.6 %collective-permute-start.2 = (f32[8,128]{1,0:T(8,128)S(1)}, f32[8,128]{1,0:T(8,128)S(1)}, u32[]{:S(2)}, u32[]{:S(2)}) collective-permute-start(f32[8,128]{1,0:T(8,128)S(1)} %get-tuple-element.83.refs_0_), channel_id=1, source_target_pairs={{0,3},{1,0},{2,1},{3,2},{4,7},{5,4},{6,5},{7,6},{8,11},{9,8},{10,9... | collective-permute-start | bytes 12296 | tf_op jit(solution)/shard_map/ppermute | solution.py:66
  11.5 16.8 %collective-permute-start.7 = (bf16[1,64,2560]{2,1,0:T(8,128)(2,1)S(1)}, bf16[1,64,2560]{2,1,0:T(8,128)(2,1)S(1)}, u32[]{:S(2)}, u32[]{:S(2)}) collective-permute-start(bf16[1,64,2560]{2,1,0:T(8,128)(2,1)S(1)} %get-tuple-element.88.refs_1_.refs_0_), channel_id=1, source_target_pairs={{0,2},{2,3},{3,1},{1,0},{4,6},{6,7},{7,5},{5,4},{8,10},{10,11},{11... | collective-permute-start | bytes 983048 | tf_op jit(solution)/shard_map/ppermute | solution.py:61
  12.4 15.9 %collective-permute-start.8 = (bf16[1,64,1280]{2,1,0:T(8,128)(2,1)S(1)}, bf16[1,64,1280]{2,1,0:T(8,128)(2,1)S(1)}, u32[]{:S(2)}, u32[]{:S(2)}) collective-permute-start(bf16[1,64,1280]{2,1,0:T(8,128)(2,1)S(1)} %get-tuple-element.89.refs_2_.refs_0_), channel_id=1, source_target_pairs={{0,2},{2,3},{3,1},{1,0},{4,6},{6,7},{7,5},{5,4},{8,10},{10,11},{11... | collective-permute-start | bytes 491528 | tf_op jit(solution)/shard_map/ppermute | solution.py:61
  15.2 13.1 %collective-permute-start.6 = (bf16[1,64,1280]{2,1,0:T(8,128)(2,1)S(1)}, bf16[1,64,1280]{2,1,0:T(8,128)(2,1)S(1)}, u32[]{:S(2)}, u32[]{:S(2)}) collective-permute-start(bf16[1,64,1280]{2,1,0:T(8,128)(2,1)S(1)} %get-tuple-element.87.refs_0_), channel_id=1, source_target_pairs={{0,2},{2,3},{3,1},{1,0},{4,6},{6,7},{7,5},{5,4},{8,10},{10,11},{11... | collective-permute-start | bytes 491528 | tf_op jit(solution)/shard_map/ppermute | solution.py:61
  19.6 1.2 %collective-permute-start.3 = (f32[4,768]{1,0:T(4,128)S(1)}, f32[4,768]{1,0:T(4,128)S(1)}, u32[]{:S(2)}, u32[]{:S(2)}) collective-permute-start(f32[4,768]{1,0:T(4,128)S(1)} %left.1.x_ref), channel_id=1, source_target_pairs={{0,4},{4,0},{8,12},{12,8},{16,20},{20,16},{24,28},{28,24},{1,5},{5... | collective-permute-start | bytes 36872 | tf_op jit(solution)/shard_map/ppermute | solution.py:71
  20.9 3.7 %collective-permute-start.4 = (f32[4,768]{1,0:T(4,128)S(1)}, f32[4,768]{1,0:T(4,128)S(1)}, u32[]{:S(2)}, u32[]{:S(2)}) collective-permute-start(f32[4,768]{1,0:T(4,128)S(1)} %add.7.x_ref), channel_id=1, source_target_pairs={{0,8},{4,12},{8,0},{12,4},{16,24},{20,28},{24,16},{28,20},{1,9},{5... | collective-permute-start | bytes 36872 | tf_op jit(solution)/shard_map/ppermute | solution.py:71
  24.6 3.7 %collective-permute-start.5 = (f32[4,768]{1,0:T(4,128)S(1)}, f32[4,768]{1,0:T(4,128)S(1)}, u32[]{:S(2)}, u32[]{:S(2)}) collective-permute-start(f32[4,768]{1,0:T(4,128)S(1)} %add.8.x_ref), channel_id=1, source_target_pairs={{0,16},{4,20},{8,24},{12,28},{16,0},{20,4},{24,8},{28,12},{1,17},{... | collective-permute-start | bytes 36872 | tf_op jit(solution)/shard_map/ppermute | solution.py:71
  28.6 4.6 %collective-permute-start.10 = (f32[8,128]{1,0:T(8,128)S(1)}, f32[8,128]{1,0:T(8,128)S(1)}, u32[]{:S(2)}, u32[]{:S(2)}) collective-permute-start(f32[8,128]{1,0:T(8,128)S(1)} %get-tuple-element.95), channel_id=1, source_target_pairs={{0,2},{1,3},{2,0},{3,1},{4,6},{5,7},{6,4},{7,5},{8,10},{9,11},{10,... | collective-permute-start | bytes 12296 | tf_op jit(solution)/shard_map/ppermute | solution.py:66
  29.9 4.5 %collective-permute-start.11 = (f32[8,128]{1,0:T(8,128)S(1)}, f32[8,128]{1,0:T(8,128)S(1)}, u32[]{:S(2)}, u32[]{:S(2)}) collective-permute-start(f32[8,128]{1,0:T(8,128)S(1)} %get-tuple-element.96), channel_id=1, source_target_pairs={{0,3},{1,0},{2,1},{3,2},{4,7},{5,4},{6,5},{7,6},{8,11},{9,8},{10,9... | collective-permute-start | bytes 12296 | tf_op jit(solution)/shard_map/ppermute | solution.py:66
  33.0 5.5 %collective-permute-start.9 = (f32[8,128]{1,0:T(8,128)S(1)}, f32[8,128]{1,0:T(8,128)S(1)}, u32[]{:S(2)}, u32[]{:S(2)}) collective-permute-start(f32[8,128]{1,0:T(8,128)S(1)} %get-tuple-element.94), channel_id=1, source_target_pairs={{0,1},{1,2},{2,3},{3,0},{4,5},{5,6},{6,7},{7,4},{8,9},{9,10},{10,1... | collective-permute-start | bytes 12296 | tf_op jit(solution)/shard_map/ppermute | solution.py:66
  38.5 5.3 %collective-permute-start.13 = (bf16[1,64,1280]{2,1,0:T(8,128)(2,1)S(1)}, bf16[1,64,1280]{2,1,0:T(8,128)(2,1)S(1)}, u32[]{:S(2)}, u32[]{:S(2)}) collective-permute-start(bf16[1,64,1280]{2,1,0:T(8,128)(2,1)S(1)} %collective-permute-done.6.refs_1_), channel_id=1, source_target_pairs={{0,2},{2,3},{3,1},{1,0},{4,6},{6,7},{7,5},{5,4},{8,10},{10,11},{11... | collective-permute-start | bytes 491528 | tf_op jit(solution)/shard_map/ppermute | solution.py:61
  40.5 1.3 %collective-permute-start.12 = (f32[4,2560]{1,0:T(4,128)S(1)}, f32[4,2560]{1,0:T(4,128)S(1)}, u32[]{:S(2)}, u32[]{:S(2)}) collective-permute-start(f32[4,2560]{1,0:T(4,128)S(1)} %get-tuple-element.104), channel_id=1, source_target_pairs={{0,4},{4,0},{8,12},{12,8},{16,20},{20,16},{24,28},{28,24},{1,5},{5... | collective-permute-start | bytes 122888 | tf_op jit(solution)/shard_map/ppermute | solution.py:71
  43.9 4.0 %collective-permute-start.14 = (f32[4,2560]{1,0:T(4,128)S(1)}, f32[4,2560]{1,0:T(4,128)S(1)}, u32[]{:S(2)}, u32[]{:S(2)}) collective-permute-start(f32[4,2560]{1,0:T(4,128)S(1)} %add.9.x_ref), channel_id=1, source_target_pairs={{0,1},{1,0},{2,3},{3,2},{4,5},{5,4},{6,7},{7,6},{8,9},{9,8},{10,11... | collective-permute-start | bytes 122888 | tf_op jit(solution)/shard_map/ppermute | solution.py:71
  47.9 5.0 %collective-permute-start.15 = (f32[4,2560]{1,0:T(4,128)S(1)}, f32[4,2560]{1,0:T(4,128)S(1)}, u32[]{:S(2)}, u32[]{:S(2)}) collective-permute-start(f32[4,2560]{1,0:T(4,128)S(1)} %add.10.x_ref), channel_id=1, source_target_pairs={{0,2},{1,3},{2,0},{3,1},{4,6},{5,7},{6,4},{7,5},{8,10},{9,11},{10,... | collective-permute-start | bytes 122888 | tf_op jit(solution)/shard_map/ppermute | solution.py:71
  52.9 11.1 %collective-permute-start.19 = (bf16[1,64,2560]{2,1,0:T(8,128)(2,1)S(1)}, bf16[1,64,2560]{2,1,0:T(8,128)(2,1)S(1)}, u32[]{:S(2)}, u32[]{:S(2)}) collective-permute-start(bf16[1,64,2560]{2,1,0:T(8,128)(2,1)S(1)} %collective-permute-done.7.refs_1_), channel_id=1, source_target_pairs={{0,2},{2,3},{3,1},{1,0},{4,6},{6,7},{7,5},{5,4},{8,10},{10,11},{11... | collective-permute-start | bytes 983048 | tf_op jit(solution)/shard_map/ppermute | solution.py:61
  54.0 4.0 %collective-permute-start.16 = (f32[4,2560]{1,0:T(4,128)S(1)}, f32[4,2560]{1,0:T(4,128)S(1)}, u32[]{:S(2)}, u32[]{:S(2)}) collective-permute-start(f32[4,2560]{1,0:T(4,128)S(1)} %add.11.x_ref), channel_id=1, source_target_pairs={{0,8},{4,12},{8,0},{12,4},{16,24},{20,28},{24,16},{28,20},{1,9},{5... | collective-permute-start | bytes 122888 | tf_op jit(solution)/shard_map/ppermute | solution.py:71
  58.0 4.0 %collective-permute-start.17 = (f32[4,2560]{1,0:T(4,128)S(1)}, f32[4,2560]{1,0:T(4,128)S(1)}, u32[]{:S(2)}, u32[]{:S(2)}) collective-permute-start(f32[4,2560]{1,0:T(4,128)S(1)} %add.12.x_ref), channel_id=1, source_target_pairs={{0,16},{4,20},{8,24},{12,28},{16,0},{20,4},{24,8},{28,12},{1,17},{... | collective-permute-start | bytes 122888 | tf_op jit(solution)/shard_map/ppermute | solution.py:71
  62.1 1.2 %collective-permute-start.18 = (f32[4,2560]{1,0:T(4,128)S(1)}, f32[4,2560]{1,0:T(4,128)S(1)}, u32[]{:S(2)}, u32[]{:S(2)}) collective-permute-start(f32[4,2560]{1,0:T(4,128)S(1)} %add.13.mine_ref), channel_id=1, source_target_pairs={{0,4},{4,0},{8,12},{12,8},{16,20},{20,16},{24,28},{28,24},{1,5},{5... | collective-permute-start | bytes 122888 | tf_op jit(solution)/shard_map/ppermute | solution.py:71
  64.0 15.0 %collective-permute-start.23 = (bf16[1,64,2560]{2,1,0:T(8,128)(2,1)S(1)}, bf16[1,64,2560]{2,1,0:T(8,128)(2,1)S(1)}, u32[]{:S(2)}, u32[]{:S(2)}) collective-permute-start(bf16[1,64,2560]{2,1,0:T(8,128)(2,1)S(1)} %collective-permute-done.19.refs_2_), channel_id=1, source_target_pairs={{0,2},{2,3},{3,1},{1,0},{4,6},{6,7},{7,5},{5,4},{8,10},{10,11},{11... | collective-permute-start | bytes 983048 | tf_op jit(solution)/shard_map/ppermute | solution.py:61
  64.1 14.0 %collective-permute-start.20 = (bf16[1,64,1280]{2,1,0:T(8,128)(2,1)S(1)}, bf16[1,64,1280]{2,1,0:T(8,128)(2,1)S(1)}, u32[]{:S(2)}, u32[]{:S(2)}) collective-permute-start(bf16[1,64,1280]{2,1,0:T(8,128)(2,1)S(1)} %collective-permute-done.8.refs_1_), channel_id=1, source_target_pairs={{0,2},{2,3},{3,1},{1,0},{4,6},{6,7},{7,5},{5,4},{8,10},{10,11},{11... | collective-permute-start | bytes 491528 | tf_op jit(solution)/shard_map/ppermute | solution.py:61
  65.7 17.5 %collective-permute-start.22 = (bf16[1,64,1280]{2,1,0:T(8,128)(2,1)S(1)}, bf16[1,64,1280]{2,1,0:T(8,128)(2,1)S(1)}, u32[]{:S(2)}, u32[]{:S(2)}) collective-permute-start(bf16[1,64,1280]{2,1,0:T(8,128)(2,1)S(1)} %collective-permute-done.13.refs_2_), channel_id=1, source_target_pairs={{0,2},{2,3},{3,1},{1,0},{4,6},{6,7},{7,5},{5,4},{8,10},{10,11},{11... | collective-permute-start | bytes 491528 | tf_op jit(solution)/shard_map/ppermute | solution.py:61
  78.0 7.7 %collective-permute-start.21 = (bf16[1,64,1280]{2,1,0:T(8,128)(2,1)S(1)}, bf16[1,64,1280]{2,1,0:T(8,128)(2,1)S(1)}, u32[]{:S(2)}, u32[]{:S(2)}) collective-permute-start(bf16[1,64,1280]{2,1,0:T(8,128)(2,1)S(1)} %collective-permute-done.20.refs_2_), channel_id=1, source_target_pairs={{0,2},{2,3},{3,1},{1,0},{4,6},{6,7},{7,5},{5,4},{8,10},{10,11},{11... | collective-permute-start | bytes 491528 | tf_op jit(solution)/shard_map/ppermute | solution.py:61
  (1 other events, 18.8 us)

commit v6 on v5

--- a/solution.py
+++ b/solution.py
@@ -12,15 +12,15 @@
 SHRINK = 2.0**-23
 TINY = 1e-30
 BLOCK = 512
-SHARES = (4, 2, 4)
+SHARES = (2, 4, 4)
 
 
 def params(mib):
     return pltpu.CompilerParams(vmem_limit_bytes=mib * 2**20)
 
 
-def cost(flops, moved):
-    return pl.CostEstimate(flops=1, bytes_accessed=1, transcendentals=0)
+def cost(flops):
+    return pl.CostEstimate(flops=int(flops) + 1, bytes_accessed=1, transcendentals=0)
 
 
 def dot(a, b, contract):
@@ -76,30 +76,33 @@
     return [1 << i for i in range(n.bit_length() - 1)]
 
 
-def token_factor_kernel(w_hbm, g_hbm, *refs):
-    chunks = refs[:-5]
-    gw_ref, terms_ref, w, w3, sems = refs[-5:]
+def token_factor_kernel(w_hbm, g_hbm, gw_ref, terms_ref, w, g, w3, sems):
     rank = w.shape[0]
-    copies = [pltpu.make_async_copy(w_hbm, w, sems.at[0])]
-    at = 0
-    for c, chunk in enumerate(chunks):
-        part = chunk.shape[2]
-        copies.append(pltpu.make_async_copy(g_hbm.at[:, :, pl.ds(at, part)], chunk, sems.at[c + 1]))
-        at += part
+    copies = [
+        pltpu.make_async_copy(w_hbm, w, sems.at[0]),
+        pltpu.make_async_copy(g_hbm, g, sems.at[1]),
+    ]
     for copy in copies:
         copy.start()
     copies[0].wait()
     terms = stack3(w[...] * SHRINK, w3)
     terms_ref[...] = terms
-    total = 0.0
+    copies[1].wait()
+    gw_ref[...] = jnp.zeros_like(gw_ref)
+    gw_ref[0:rank, 0 : g.shape[1]] = sum3(dot(terms, g[0], (1, 1)), rank)
+
+
+def cut_kernel(g_ref, *refs):
+    chunks, sems = refs[:-1], refs[-1]
+    copies = []
     at = 0
     for c, chunk in enumerate(chunks):
-        copies[c + 1].wait()
         part = chunk.shape[2]
-        total += dot(terms[:, at : at + part], chunk[0], (1, 1))
+        copies.append(pltpu.make_async_copy(g_ref.at[:, :, pl.ds(at, part)], chunk, sems.at[c]))
+        copies[-1].start()
         at += part
-    gw_ref[...] = jnp.zeros_like(gw_ref)
-    gw_ref[0:rank, 0 : total.shape[1]] = sum3(total, rank)
+    for copy in copies:
+        copy.wait()
 
 
 def error_left_kernel(terms_ref, e_hbm, out_ref, e_ref, sems):
@@ -196,12 +199,11 @@
     return rows
 
 
-def right_kernel(n, parts, p_ref, r_ref, *refs):
-    chunks = refs[:parts]
-    pieces = refs[parts : parts + n]
-    ortho_ref, keep_ref, send_ref, inbox, z, z3, outbox = refs[parts + n :]
+def right_kernel(n, p_ref, r_ref, g_ref, *refs):
+    pieces = refs[:n]
+    ortho_ref, keep_ref, send_ref, inbox, z, z3, outbox = refs[n:]
     rank = p_ref.shape[0]
-    tok = chunks[0].shape[1]
+    tok = g_ref.shape[1]
     half = keep_ref.shape[1]
     me_t = lax.axis_index("tensor")
     core = lax.rem(lax.axis_index("dp"), 2)
@@ -222,19 +224,11 @@
     for i, row in enumerate(solve_rows(inv, p_ref[...], rank)):
         ortho_ref[i : i + 1, :] = row
     terms = stack3(z[...], z3)
-    at = 0
-    for chunk in chunks:
-        end = at + chunk.shape[2]
-        fresh = sum3(dot(terms, chunk[0], (1, 0)), rank) * 1024.0
-        old = solve_rows(inv, r_ref[:, at:end], rank)
-        for i, row in enumerate(old):
-            row = row + fresh[i : i + 1, :]
-            for h in range(2):
-                lo, hi = max(h * half, at), min((h + 1) * half, end)
-                if lo < hi:
-                    here = slice(lo - h * half, hi - h * half)
-                    outbox[h, i : i + 1, here] = row[:, lo - at : hi - at]
-        at = end
+    for h in range(2):
+        cols = slice(h * half, (h + 1) * half)
+        fresh = sum3(dot(terms, g_ref[0, :, cols], (1, 0)), rank) * 1024.0
+        for i, row in enumerate(solve_rows(inv, r_ref[:, cols], rank)):
+            outbox[h, i : i + 1, :] = row + fresh[i : i + 1, :]
     keep_ref[...] = outbox[core]
     send_ref[...] = outbox[1 - core]
 
@@ -265,10 +259,10 @@
     right_ref[...] = right[...].astype(BF16)
 
 
-def final_kernel(n, at, a_ref, left_ref, right_ref, e_ref, *refs):
+def final_kernel(n, at, part, a_ref, left_ref, right_ref, e_ref, *refs):
     slots = refs[:n]
     rebuilt_hbm, error_hbm, acts, acts_t, rebuilt_v, error_v, sems = refs[-7:]
-    tok, part = slots[0].shape[1:]
+    tok = slots[0].shape[1]
     rows = e_ref.shape[1]
     me = lax.axis_index("tensor")
     for s in range(n):
@@ -285,7 +279,9 @@
         for c in range(part // wide):
             cols = slice(c * wide, (c + 1) * wide)
             there = slice(at + c * wide, at + (c + 1) * wide)
-            grads = jnp.concatenate([slot[0, :, cols] for slot in slots], axis=0)
+            grads = jnp.concatenate(
+                [slot[0, :, cols if slot.shape[2] == part else there] for slot in slots], axis=0
+            )
             matrix = dot(acts_t[here, :], grads, (1, 0)) + e_ref[0, here, there].astype(F32)
             rebuilt = dot(left_ref[here, :], right_ref[:, there], (1, 0))
             rebuilt_v[here, cols] = rebuilt.astype(BF16)
@@ -324,68 +320,58 @@
     dma = pltpu.SemaphoreType.DMA
     pin = lambda x: pltpu.with_memory_space_constraint(x, pltpu.HBM)
 
-    def call(kernel, shapes, scratch, name, flops, moved, specs=None, mib=16):
+    def call(kernel, shapes, scratch, name, specs=None, flops=0):
         return pl.pallas_call(
             kernel,
             out_shape=shapes,
             **({"in_specs": specs} if specs else {}),
             scratch_shapes=scratch,
-            compiler_params=params(mib),
-            cost_estimate=cost(flops, moved),
+            compiler_params=params(16),
+            cost_estimate=cost(flops),
             name=name,
         )
 
     def add(x, y):
-        return call(add_kernel, sds(x.shape, F32), [], "add", 1e5, 1e5)(x, y)
-
-    *chunks, gw, w_terms = call(
+        return call(add_kernel, sds(x.shape, F32), [], "add")(x, y)
+
+    gw, w_terms = call(
         token_factor_kernel,
-        [sds((1, tok, part), BF16) for part in widths]
-        + [sds((8, 128), F32), sds((3 * rank, width), BF16)],
+        [sds((8, 128), F32), sds((3 * rank, width), BF16)],
         [
             pltpu.VMEM((rank, width), F32),
+            pltpu.VMEM((1, tok, width), BF16),
             pltpu.VMEM((3 * rank, width), F32),
-            dma((parts + 1,)),
+            dma((2,)),
         ],
-        "token_factor", 1e3, 1e6, [hbm, hbm],
+        "token_factor", [hbm, hbm],
     )(pin(w), pin(out_grads))
     gws = exchange([gw] * n, "tensor", n)
-    rings = [[chunk] for chunk in chunks]
-
-    def turn(which, after):
-        for c in which:
-            after, last = lax.optimization_barrier((after, rings[c][-1]))
-            rings[c].append(ring_step(last, "tensor", n))
-        return after
-
-    def settle(which, before):
-        last = [rings[c][-1] for c in which]
-        before, last = lax.optimization_barrier((before, last))
-        for c, x in zip(which, last):
-            rings[c][-1] = x
-        return before
-
-    first, rest = [0], [1, 2]
-    w_terms, gws = turn(first + rest, (w_terms, gws))
+
+    def after(x, y):
+        return lax.optimization_barrier((x, y))
+
+    ring = [out_grads]
+    last, (w_terms, gws) = after(out_grads, (w_terms, gws))
+    ring.append(ring_step(last, "tensor", n))
     ew, error_v = call(
         error_left_kernel,
         [sds((rank, rows), F32), sds((1, rows, width), BF16)],
         [dma((rows // 128,))],
-        "error_left", 2e9, rows * width * 2, [vmem, hbm],
+        "error_left", [vmem, hbm],
     )(w_terms, pin(error_buffer))
 
     left = call(
-        left_kernel, sds((rank, rows), F32), [pltpu.VMEM((3 * rank, tok), F32)], "left", 1e7, 1e6
+        left_kernel, sds((rank, rows), F32), [pltpu.VMEM((3 * rank, tok), F32)], "left"
     )(activations, ew, *gws)
     for bit in bits(m)[:-1]:
         left = add(left, swap(left, "dp", m, bit))
-    last = settle(first + rest, swap(left, "dp", m, bits(m)[-1]))
+    ring[1], last = after(ring[1], swap(left, "dp", m, bits(m)[-1]))
 
     mean, *msgs = call(
         functools.partial(mean_kernel, n, 1.0 / (SHRINK * m)),
         [sds((rank, rows), F32)] + [sds((8, 128), F32)] * n,
         [pltpu.VMEM((3 * rank, rows), F32), pltpu.VMEM((n, 8, 128), F32)],
-        "mean", 1e7, 1e6,
+        "mean",
     )(activations, left, last)
     msgs = exchange(msgs, "tensor", n)
 
@@ -393,12 +379,11 @@
         error_right_kernel,
         sds((rank, width), F32),
         [pltpu.VMEM((3 * rank, rows), F32)],
-        "error_right", 2e9, rows * width * 2,
+        "error_right", None, 1.2e9,
     )(mean, error_v)
-    msgs = turn(first, msgs)
 
     ortho, keep, send = call(
-        functools.partial(right_kernel, n, parts),
+        functools.partial(right_kernel, n),
         [sds((rank, rows), F32), sds((rank, half), F32), sds((rank, half), F32)],
         [
             pltpu.VMEM((n, 8, 128), F32),
@@ -406,15 +391,21 @@
             pltpu.VMEM((3 * rank, tok), F32),
             pltpu.VMEM((2, rank, half), F32),
         ],
-        "right", 1e7, 1e6,
-    )(mean, right_raw, *chunks, *msgs)
+        "right",
+    )(mean, right_raw, out_grads, *msgs)
     total = add(keep, swap(send, "dp", m, 1))
-    total = settle(first, total)
     for bit in bits(n):
         total = add(total, swap(total, "tensor", n, bit))
-    total = turn(rest + first, total)
+    for _ in range(2, n - 1):
+        last, total = after(ring[-1], total)
+        ring.append(ring_step(last, "tensor", n))
     for bit in bits(m)[1:]:
         total = add(total, swap(total, "dp", m, bit))
+    ring[-1], total = after(ring[-1], total)
+    chunks = call(
+        cut_kernel, [sds((1, tok, part), BF16) for part in widths], [dma((parts,))], "cut"
+    )(ring[-1])
+    chunks = [ring_step(chunk, "tensor", n) for chunk in chunks]
 
     terms = len(LEFT_TERMS) * rank
     whole, left_terms, right_terms = call(
@@ -425,16 +416,13 @@
             pltpu.VMEM((terms, rows), F32),
             pltpu.VMEM((terms, width), F32),
         ],
-        "factor", 1e6, 1e6,
+        "factor",
     )(ortho, total, swap(total, "dp", m, 1))
 
-    for c in rest + (first + rest) * (n - 4):
-        right_terms = turn([c], right_terms)
     outs = ()
-    for c in rest[:1] + first + rest[1:]:
-        ring, part, at = rings[c], widths[c], sum(widths[:c])
+    for c, (part, chunk) in enumerate(zip(widths, chunks)):
         outs = pl.pallas_call(
-            functools.partial(final_kernel, n, at),
+            functools.partial(final_kernel, n, sum(widths[:c]), part),
             in_specs=[vmem] * (4 + n) + [pl.BlockSpec(memory_space=pl.ANY)] * len(outs),
             out_specs=[pl.BlockSpec(memory_space=pl.ANY)] * 2,
             out_shape=[sds((rows, width), BF16), sds((1, rows, width), BF16)],
@@ -447,9 +435,9 @@
                 dma((3, 2)),
             ],
             compiler_params=params(16),
-            cost_estimate=cost(4e9, rows * part * 4),
+            cost_estimate=cost(0),
             name="rebuild",
-        )(activations, left_terms, right_terms, error_v, *ring, *outs)
+        )(activations, left_terms, right_terms, error_v, *ring, chunk, *outs)
     rebuilt, error = outs
     return rebuilt, error, whole.T
 

time: 88.4 us -> 81.1 us (0.917)
  waiting for transfers between devices: 41.1 us -> 31 us
  starting transfers between devices: 28.2 us -> 31 us
    ppermute x9, waiting for transfers between devices: 21 us -> 17.3 us  [swap(): return lax.ppermute(x, axis, [(i, i ^ bit) for i in range(n)])]
    ppermute x9, starting transfers between devices: 7.11 us -> 10.8 us  [swap(): return lax.ppermute(x, axis, [(i, i ^ bit) for i in range(n)])]
    ppermute x6, waiting for transfers between devices: 7.76 us -> 4.58 us  [exchange(): lax.ppermute(pieces[k], axis, [(i, (i + k) % n) for i in range(n)])]
    ppermute x9 -> x5, waiting for transfers between devices: 12.3 us -> 9.21 us  [ring_step(): lax.ppermute(x, axis, [(ring[p], ring[(p + 1) % n]) for p in range(n)])]
    ppermute x9 -> x5, starting transfers between devices: 9.65 us -> 9.35 us  [ring_step(): lax.ppermute(x, axis, [(ring[p], ring[(p + 1) % n]) for p in range(n)])]
    pallas_call x12 -> x13, Pallas kernels: 11.7 us -> 11.7 us  [the longest x3 9.23 us: per_device(): pl.pallas_call(functools.partial(final_kernel, n, sum(widths[:c]), part),...]
  transfers between devices with their start and end apart: 24 -> 20, of which waited for: 16 -> 16; matrix products, arithmetic and copies ran while one was open for 0% -> 0% of each run, Pallas kernels for 16% -> 16%
where the time goes in v6:
time: 81.1 us; the launch traced here: 80.9 us
  starting transfers between devices  31 us (38%)
  waiting for transfers between devices  31 us (38%)
  Pallas kernels  18.2 us (22%)
    ppermute x9, waiting for transfers between devices, swap(): return lax.ppermute(x, axis, [(i, i ^ bit) for i in range(n)])  17.3 us
    ppermute x6, starting transfers between devices, exchange(): lax.ppermute(pieces[k], axis, [(i, (i + k) % n) for i in range(n)])  10.8 us
    ppermute x9, starting transfers between devices, swap(): return lax.ppermute(x, axis, [(i, i ^ bit) for i in range(n)])  10.8 us
    ppermute x5, starting transfers between devices, ring_step(): lax.ppermute(x, axis, [(ring[p], ring[(p + 1) % n]) for p in range(n)])  9.35 us
    pallas_call x3, Pallas kernels, per_device(): pl.pallas_call(functools.partial(final_kernel, n, sum(widths[:c]), part),...  9.23 us
    ppermute x5, waiting for transfers between devices, ring_step(): lax.ppermute(x, axis, [(ring[p], ring[(p + 1) % n]) for p in range(n)])  9.21 us
    ppermute x6, waiting for transfers between devices, exchange(): lax.ppermute(pieces[k], axis, [(i, (i + k) % n) for i in range(n)])  4.58 us
    pallas_call x1, Pallas kernels, per_device(): call(error_left_kernel, [sds((rank, rows), F32), sds((1, rows, width), BF...  4.14 us
  transfers between devices with their start and end apart: 20, of which 16 were waited for; matrix products, arithmetic and copies ran while one was open for 0% of the time, Pallas kernels for 16%

profile of v6, /device:TPU:0, one launch (start us, length us, event | category | flops | bytes accessed | tf_op | source)
XLA Modules:
  0.0 80.9 jit_solution(2311399771584576331)
XLA Ops:
  2.1 5.1 %collective-permute-start.2 = (f32[8,128]{1,0:T(8,128)S(1)}, f32[8,128]{1,0:T(8,128)S(1)}, u32[]{:S(2)}, u32[]{:S(2)}) collective-permute-start(f32[8,128]{1,0:T(8,128)S(1)} %get-tuple-element.43.refs_0_), channel_id=1, source_target_pairs={{0,3},{1,0},{2,1},{3,2},{4,7},{5,4},{6,5},{7,6},{8,11},{9,8},{10,9... | collective-permute-start | bytes 12296 | tf_op jit(solution)/shard_map/ppermute | solution.py:66
  8.6 3.2 %collective-permute-done.1.refs_2_ = f32[8,128]{1,0:T(8,128)S(1)} collective-permute-done((f32[8,128]{1,0:T(8,128)S(1)}, f32[8,128]{1,0:T(8,128)S(1)}, u32[]{:S(2)}, u32[]{:S(2)}) %collective-permute-start.1) | collective-permute-done | bytes 4128 | tf_op jit(solution)/shard_map/ppermute | solution.py:66
  13.8 4.1 %error_left.1 = (f32[4,768]{1,0:T(4,128)S(1)}, bf16[1,768,5120]{2,1,0:T(8,128)(2,1)S(1)}) custom-call(bf16[12,5120]{1,0:T(8,128)(2,1)S(1)} %get-tuple-element.41.terms_ref, bf16[1,768,5120]{2,1,0:T(8,128)(2,1)} %e_hbm.1), custom_call_target="tpu_custom_call" | custom-call | flops 1 | bytes 1 | tf_op jit(solution)/shard_map/error_left/pallas_call | solution.py:356
  19.4 1.5 %collective-permute-start.4 = (f32[4,768]{1,0:T(4,128)S(1)}, f32[4,768]{1,0:T(4,128)S(1)}, u32[]{:S(2)}, u32[]{:S(2)}) collective-permute-start(f32[4,768]{1,0:T(4,128)S(1)} %add.7.x_ref), channel_id=1, source_target_pairs={{0,8},{4,12},{8,0},{12,4},{16,24},{20,28},{24,16},{28,20},{1,9},{5... | collective-permute-start | bytes 36872 | tf_op jit(solution)/shard_map/ppermute | solution.py:71
  20.9 2.2 %collective-permute-done.4.y_ref = f32[4,768]{1,0:T(4,128)S(1)} collective-permute-done((f32[4,768]{1,0:T(4,128)S(1)}, f32[4,768]{1,0:T(4,128)S(1)}, u32[]{:S(2)}, u32[]{:S(2)}) %collective-permute-start.4) | collective-permute-done | bytes 12320 | tf_op jit(solution)/shard_map/ppermute | solution.py:71
  23.1 1.5 %collective-permute-start.6 = (f32[4,768]{1,0:T(4,128)S(1)}, f32[4,768]{1,0:T(4,128)S(1)}, u32[]{:S(2)}, u32[]{:S(2)}) collective-permute-start(f32[4,768]{1,0:T(4,128)S(1)} %add.8.x_ref), channel_id=1, source_target_pairs={{0,16},{4,20},{8,24},{12,28},{16,0},{20,4},{24,8},{28,12},{1,17},{... | collective-permute-start | bytes 36872 | tf_op jit(solution)/shard_map/ppermute | solution.py:71
  24.6 2.2 %collective-permute-done.6.y_ref = f32[4,768]{1,0:T(4,128)S(1)} collective-permute-done((f32[4,768]{1,0:T(4,128)S(1)}, f32[4,768]{1,0:T(4,128)S(1)}, u32[]{:S(2)}, u32[]{:S(2)}) %collective-permute-start.6) | collective-permute-done | bytes 12320 | tf_op jit(solution)/shard_map/ppermute | solution.py:71
  28.6 1.5 %collective-permute-start.8 = (f32[8,128]{1,0:T(8,128)S(1)}, f32[8,128]{1,0:T(8,128)S(1)}, u32[]{:S(2)}, u32[]{:S(2)}) collective-permute-start(f32[8,128]{1,0:T(8,128)S(1)} %get-tuple-element.53), channel_id=1, source_target_pairs={{0,2},{1,3},{2,0},{3,1},{4,6},{5,7},{6,4},{7,5},{8,10},{9,11},{10,... | collective-permute-start | bytes 12296 | tf_op jit(solution)/shard_map/ppermute | solution.py:66
  30.1 2.8 %collective-permute-start.9 = (f32[8,128]{1,0:T(8,128)S(1)}, f32[8,128]{1,0:T(8,128)S(1)}, u32[]{:S(2)}, u32[]{:S(2)}) collective-permute-start(f32[8,128]{1,0:T(8,128)S(1)} %get-tuple-element.54), channel_id=1, source_target_pairs={{0,3},{1,0},{2,1},{3,2},{4,7},{5,4},{6,5},{7,6},{8,11},{9,8},{10,9... | collective-permute-start | bytes 12296 | tf_op jit(solution)/shard_map/ppermute | solution.py:66
  36.4 2.0 %collective-permute-start.11 = (f32[4,2560]{1,0:T(4,128)S(1)}, f32[4,2560]{1,0:T(4,128)S(1)}, u32[]{:S(2)}, u32[]{:S(2)}) collective-permute-start(f32[4,2560]{1,0:T(4,128)S(1)} %add.9.x_ref), channel_id=1, source_target_pairs={{0,1},{1,0},{2,3},{3,2},{4,5},{5,4},{6,7},{7,6},{8,9},{9,8},{10,11... | collective-permute-start | bytes 122888 | tf_op jit(solution)/shard_map/ppermute | solution.py:71
  38.4 2.0 %collective-permute-done.11.y_ref = f32[4,2560]{1,0:T(4,128)S(1)} collective-permute-done((f32[4,2560]{1,0:T(4,128)S(1)}, f32[4,2560]{1,0:T(4,128)S(1)}, u32[]{:S(2)}, u32[]{:S(2)}) %collective-permute-start.11) | collective-permute-done | bytes 40992 | tf_op jit(solution)/shard_map/ppermute | solution.py:71
  40.4 2.6 %collective-permute-start.12 = (f32[4,2560]{1,0:T(4,128)S(1)}, f32[4,2560]{1,0:T(4,128)S(1)}, u32[]{:S(2)}, u32[]{:S(2)}) collective-permute-start(f32[4,2560]{1,0:T(4,128)S(1)} %add.10.x_ref), channel_id=1, source_target_pairs={{0,2},{1,3},{2,0},{3,1},{4,6},{5,7},{6,4},{7,5},{8,10},{9,11},{10,... | collective-permute-start | bytes 122888 | tf_op jit(solution)/shard_map/ppermute | solution.py:71
  43.0 2.3 %collective-permute-done.12.y_ref = f32[4,2560]{1,0:T(4,128)S(1)} collective-permute-done((f32[4,2560]{1,0:T(4,128)S(1)}, f32[4,2560]{1,0:T(4,128)S(1)}, u32[]{:S(2)}, u32[]{:S(2)}) %collective-permute-start.12) | collective-permute-done | bytes 40992 | tf_op jit(solution)/shard_map/ppermute | solution.py:71
  45.3 2.6 %collective-permute-start.13 = (bf16[1,64,5120]{2,1,0:T(8,128)(2,1)S(1)}, bf16[1,64,5120]{2,1,0:T(8,128)(2,1)S(1)}, u32[]{:S(2)}, u32[]{:S(2)}) collective-permute-start(bf16[1,64,5120]{2,1,0:T(8,128)(2,1)S(1)} %collective-permute-done.5.refs_1_), channel_id=1, source_target_pairs={{0,2},{2,3},{3,1},{1,0},{4,6},{6,7},{7,5},{5,4},{8,10},{10,11},{11... | collective-permute-start | bytes 1966088 | tf_op jit(solution)/shard_map/ppermute | solution.py:61
  47.9 1.5 %collective-permute-start.14 = (f32[4,2560]{1,0:T(4,128)S(1)}, f32[4,2560]{1,0:T(4,128)S(1)}, u32[]{:S(2)}, u32[]{:S(2)}) collective-permute-start(f32[4,2560]{1,0:T(4,128)S(1)} %add.11.x_ref), channel_id=1, source_target_pairs={{0,8},{4,12},{8,0},{12,4},{16,24},{20,28},{24,16},{28,20},{1,9},{5... | collective-permute-start | bytes 122888 | tf_op jit(solution)/shard_map/ppermute | solution.py:71
  49.4 2.5 %collective-permute-done.14.y_ref = f32[4,2560]{1,0:T(4,128)S(1)} collective-permute-done((f32[4,2560]{1,0:T(4,128)S(1)}, f32[4,2560]{1,0:T(4,128)S(1)}, u32[]{:S(2)}, u32[]{:S(2)}) %collective-permute-start.14) | collective-permute-done | bytes 40992 | tf_op jit(solution)/shard_map/ppermute | solution.py:71
  51.9 1.5 %collective-permute-start.15 = (f32[4,2560]{1,0:T(4,128)S(1)}, f32[4,2560]{1,0:T(4,128)S(1)}, u32[]{:S(2)}, u32[]{:S(2)}) collective-permute-start(f32[4,2560]{1,0:T(4,128)S(1)} %add.12.x_ref), channel_id=1, source_target_pairs={{0,16},{4,20},{8,24},{12,28},{16,0},{20,4},{24,8},{28,12},{1,17},{... | collective-permute-start | bytes 122888 | tf_op jit(solution)/shard_map/ppermute | solution.py:71
  53.5 2.5 %collective-permute-done.15.y_ref = f32[4,2560]{1,0:T(4,128)S(1)} collective-permute-done((f32[4,2560]{1,0:T(4,128)S(1)}, f32[4,2560]{1,0:T(4,128)S(1)}, u32[]{:S(2)}, u32[]{:S(2)}) %collective-permute-start.15) | collective-permute-done | bytes 40992 | tf_op jit(solution)/shard_map/ppermute | solution.py:71
  56.0 4.3 %collective-permute-done.13.g_ref.refs_2_ = bf16[1,64,5120]{2,1,0:T(8,128)(2,1)S(1)} collective-permute-done((bf16[1,64,5120]{2,1,0:T(8,128)(2,1)S(1)}, bf16[1,64,5120]{2,1,0:T(8,128)(2,1)S(1)}, u32[]{:S(2)}, u32[]{:S(2)}) %collective-permute-start.13) | collective-permute-done | bytes 655392 | tf_op jit(solution)/shard_map/ppermute | solution.py:61
  60.4 3.4 %collective-permute-start.19 = (bf16[1,64,2560]{2,1,0:T(8,128)(2,1)S(1)}, bf16[1,64,2560]{2,1,0:T(8,128)(2,1)S(1)}, u32[]{:S(2)}, u32[]{:S(2)}) collective-permute-start(bf16[1,64,2560]{2,1,0:T(8,128)(2,1)S(1)} %get-tuple-element.67), channel_id=1, source_target_pairs={{0,2},{2,3},{3,1},{1,0},{4,6},{6,7},{7,5},{5,4},{8,10},{10,11},{11... | collective-permute-start | bytes 983048 | tf_op jit(solution)/shard_map/ppermute | solution.py:61
  67.9 3.8 %collective-permute-done.19.refs_3_ = bf16[1,64,2560]{2,1,0:T(8,128)(2,1)S(1)} collective-permute-done((bf16[1,64,2560]{2,1,0:T(8,128)(2,1)S(1)}, bf16[1,64,2560]{2,1,0:T(8,128)(2,1)S(1)}, u32[]{:S(2)}, u32[]{:S(2)}) %collective-permute-start.19) | collective-permute-done | bytes 327712 | tf_op jit(solution)/shard_map/ppermute | solution.py:61
  71.7 4.1 %rebuild.3 = (bf16[768,5120]{1,0:T(8,128)(2,1)}, bf16[1,768,5120]{2,1,0:T(8,128)(2,1)}) custom-call(bf16[1,256,768]{2,1,0:T(8,128)(2,1)S(1)} %copy-done.1, bf16[768,24]{1,0:T(8,128)(2,1)S(1)} %get-tuple-element.62.left_ref, bf16[24,5120]{1,0:T(8,128)(2,1)S(1)} %get-tuple-element.63.right_ref, bf16[1,768,5120]{2,1,0:T(8,128)(2,1)S(1)} %get-tuple-element.50.e_ref, ...), custom_call_target="tpu_custom_call" | custom-call | flops 1 | bytes 1 | tf_op jit(solution)/shard_map/rebuild/pallas_call | solution.py:424
  75.8 2.5 %rebuild.4 = (bf16[768,5120]{1,0:T(8,128)(2,1)}, bf16[1,768,5120]{2,1,0:T(8,128)(2,1)}) custom-call(bf16[1,256,768]{2,1,0:T(8,128)(2,1)S(1)} %copy-done.1, bf16[768,24]{1,0:T(8,128)(2,1)S(1)} %get-tuple-element.62.left_ref, bf16[24,5120]{1,0:T(8,128)(2,1)S(1)} %get-tuple-element.63.right_ref, ...), custom_call_target="tpu_custom_call", output_to_operand_aliasing={{0}: (8, {}), {1}: (9, {})} | custom-call | flops 1 | bytes 1 | tf_op jit(solution)/shard_map/rebuild/pallas_call | solution.py:424
  78.4 2.5 %rebuild.5 = (bf16[768,5120]{1,0:T(8,128)(2,1)}, bf16[1,768,5120]{2,1,0:T(8,128)(2,1)}) custom-call(bf16[1,256,768]{2,1,0:T(8,128)(2,1)S(1)} %copy-done.1, bf16[768,24]{1,0:T(8,128)(2,1)S(1)} %get-tuple-element.62.left_ref, bf16[24,5120]{1,0:T(8,128)(2,1)S(1)} %get-tuple-element.63.right_ref, ...), custom_call_target="tpu_custom_call", output_to_operand_aliasing={{0}: (8, {}), {1}: (9, {})} | custom-call | flops 1 | bytes 1 | tf_op jit(solution)/shard_map/rebuild/pallas_call | solution.py:424
  (38 shorter events, 15.8 us)
Async XLA Ops:
  0.6 17.3 %copy-start.1 = (bf16[1,256,768]{2,1,0:T(8,128)(2,1)S(1)}, bf16[1,256,768]{2,1,0:T(8,128)(2,1)}, u32[]{:S(2)}) copy-start(bf16[1,256,768]{2,1,0:T(8,128)(2,1)} %a_ref.9) | copy-start | bytes 1179652
  2.1 6.4 %collective-permute-start.2 = (f32[8,128]{1,0:T(8,128)S(1)}, f32[8,128]{1,0:T(8,128)S(1)}, u32[]{:S(2)}, u32[]{:S(2)}) collective-permute-start(f32[8,128]{1,0:T(8,128)S(1)} %get-tuple-element.43.refs_0_), channel_id=1, source_target_pairs={{0,3},{1,0},{2,1},{3,2},{4,7},{5,4},{6,5},{7,6},{8,11},{9,8},{10,9... | collective-permute-start | bytes 12296 | tf_op jit(solution)/shard_map/ppermute | solution.py:66
  7.2 4.5 %collective-permute-start.1 = (f32[8,128]{1,0:T(8,128)S(1)}, f32[8,128]{1,0:T(8,128)S(1)}, u32[]{:S(2)}, u32[]{:S(2)}) collective-permute-start(f32[8,128]{1,0:T(8,128)S(1)} %get-tuple-element.43.refs_0_), channel_id=1, source_target_pairs={{0,2},{1,3},{2,0},{3,1},{4,6},{5,7},{6,4},{7,5},{8,10},{9,11},{10,... | collective-permute-start | bytes 12296 | tf_op jit(solution)/shard_map/ppermute | solution.py:66
  7.2 5.4 %collective-permute-start = (f32[8,128]{1,0:T(8,128)S(1)}, f32[8,128]{1,0:T(8,128)S(1)}, u32[]{:S(2)}, u32[]{:S(2)}) collective-permute-start(f32[8,128]{1,0:T(8,128)S(1)} %get-tuple-element.43.refs_0_), channel_id=1, source_target_pairs={{0,1},{1,2},{2,3},{3,0},{4,5},{5,6},{6,7},{7,4},{8,9},{9,10},{10,1... | collective-permute-start | bytes 12296 | tf_op jit(solution)/shard_map/ppermute | solution.py:66
  12.6 21.6 %copy-start = (bf16[1,64,5120]{2,1,0:T(8,128)(2,1)S(1)}, bf16[1,64,5120]{2,1,0:T(8,128)(2,1)}, u32[]{:S(2)}) copy-start(bf16[1,64,5120]{2,1,0:T(8,128)(2,1)} %refs_0_.5) | copy-start | bytes 1966084
  12.6 15.3 %collective-permute-start.5 = (bf16[1,64,5120]{2,1,0:T(8,128)(2,1)}, bf16[1,64,5120]{2,1,0:T(8,128)(2,1)S(1)}, u32[]{:S(2)}, u32[]{:S(2)}) collective-permute-start(bf16[1,64,5120]{2,1,0:T(8,128)(2,1)} %refs_0_.5), channel_id=1, source_target_pairs={{0,2},{2,3},{3,1},{1,0},{4,6},{6,7},{7,5},{5,4},{8,10},{10,11},{11... | collective-permute-start | bytes 1966088 | tf_op jit(solution)/shard_map/ppermute | solution.py:61
  18.1 1.2 %collective-permute-start.3 = (f32[4,768]{1,0:T(4,128)S(1)}, f32[4,768]{1,0:T(4,128)S(1)}, u32[]{:S(2)}, u32[]{:S(2)}) collective-permute-start(f32[4,768]{1,0:T(4,128)S(1)} %left.1.x_ref), channel_id=1, source_target_pairs={{0,4},{4,0},{8,12},{12,8},{16,20},{20,16},{24,28},{28,24},{1,5},{5... | collective-permute-start | bytes 36872 | tf_op jit(solution)/shard_map/ppermute | solution.py:71
  19.4 3.7 %collective-permute-start.4 = (f32[4,768]{1,0:T(4,128)S(1)}, f32[4,768]{1,0:T(4,128)S(1)}, u32[]{:S(2)}, u32[]{:S(2)}) collective-permute-start(f32[4,768]{1,0:T(4,128)S(1)} %add.7.x_ref), channel_id=1, source_target_pairs={{0,8},{4,12},{8,0},{12,4},{16,24},{20,28},{24,16},{28,20},{1,9},{5... | collective-permute-start | bytes 36872 | tf_op jit(solution)/shard_map/ppermute | solution.py:71
  23.1 3.7 %collective-permute-start.6 = (f32[4,768]{1,0:T(4,128)S(1)}, f32[4,768]{1,0:T(4,128)S(1)}, u32[]{:S(2)}, u32[]{:S(2)}) collective-permute-start(f32[4,768]{1,0:T(4,128)S(1)} %add.8.x_ref), channel_id=1, source_target_pairs={{0,16},{4,20},{8,24},{12,28},{16,0},{20,4},{24,8},{28,12},{1,17},{... | collective-permute-start | bytes 36872 | tf_op jit(solution)/shard_map/ppermute | solution.py:71
  28.2 5.9 %collective-permute-start.7 = (f32[8,128]{1,0:T(8,128)S(1)}, f32[8,128]{1,0:T(8,128)S(1)}, u32[]{:S(2)}, u32[]{:S(2)}) collective-permute-start(f32[8,128]{1,0:T(8,128)S(1)} %get-tuple-element.52), channel_id=1, source_target_pairs={{0,1},{1,2},{2,3},{3,0},{4,5},{5,6},{6,7},{7,4},{8,9},{9,10},{10,1... | collective-permute-start | bytes 12296 | tf_op jit(solution)/shard_map/ppermute | solution.py:66
  28.6 5.5 %collective-permute-start.8 = (f32[8,128]{1,0:T(8,128)S(1)}, f32[8,128]{1,0:T(8,128)S(1)}, u32[]{:S(2)}, u32[]{:S(2)}) collective-permute-start(f32[8,128]{1,0:T(8,128)S(1)} %get-tuple-element.53), channel_id=1, source_target_pairs={{0,2},{1,3},{2,0},{3,1},{4,6},{5,7},{6,4},{7,5},{8,10},{9,11},{10,... | collective-permute-start | bytes 12296 | tf_op jit(solution)/shard_map/ppermute | solution.py:66
  30.1 4.2 %collective-permute-start.9 = (f32[8,128]{1,0:T(8,128)S(1)}, f32[8,128]{1,0:T(8,128)S(1)}, u32[]{:S(2)}, u32[]{:S(2)}) collective-permute-start(f32[8,128]{1,0:T(8,128)S(1)} %get-tuple-element.54), channel_id=1, source_target_pairs={{0,3},{1,0},{2,1},{3,2},{4,7},{5,4},{6,5},{7,6},{8,11},{9,8},{10,9... | collective-permute-start | bytes 12296 | tf_op jit(solution)/shard_map/ppermute | solution.py:66
  35.1 1.3 %collective-permute-start.10 = (f32[4,2560]{1,0:T(4,128)S(1)}, f32[4,2560]{1,0:T(4,128)S(1)}, u32[]{:S(2)}, u32[]{:S(2)}) collective-permute-start(f32[4,2560]{1,0:T(4,128)S(1)} %get-tuple-element.58), channel_id=1, source_target_pairs={{0,4},{4,0},{8,12},{12,8},{16,20},{20,16},{24,28},{28,24},{1,5},{5... | collective-permute-start | bytes 122888 | tf_op jit(solution)/shard_map/ppermute | solution.py:71
  36.4 4.0 %collective-permute-start.11 = (f32[4,2560]{1,0:T(4,128)S(1)}, f32[4,2560]{1,0:T(4,128)S(1)}, u32[]{:S(2)}, u32[]{:S(2)}) collective-permute-start(f32[4,2560]{1,0:T(4,128)S(1)} %add.9.x_ref), channel_id=1, source_target_pairs={{0,1},{1,0},{2,3},{3,2},{4,5},{5,4},{6,7},{7,6},{8,9},{9,8},{10,11... | collective-permute-start | bytes 122888 | tf_op jit(solution)/shard_map/ppermute | solution.py:71
  40.4 4.9 %collective-permute-start.12 = (f32[4,2560]{1,0:T(4,128)S(1)}, f32[4,2560]{1,0:T(4,128)S(1)}, u32[]{:S(2)}, u32[]{:S(2)}) collective-permute-start(f32[4,2560]{1,0:T(4,128)S(1)} %add.10.x_ref), channel_id=1, source_target_pairs={{0,2},{1,3},{2,0},{3,1},{4,6},{5,7},{6,4},{7,5},{8,10},{9,11},{10,... | collective-permute-start | bytes 122888 | tf_op jit(solution)/shard_map/ppermute | solution.py:71
  45.3 14.9 %collective-permute-start.13 = (bf16[1,64,5120]{2,1,0:T(8,128)(2,1)S(1)}, bf16[1,64,5120]{2,1,0:T(8,128)(2,1)S(1)}, u32[]{:S(2)}, u32[]{:S(2)}) collective-permute-start(bf16[1,64,5120]{2,1,0:T(8,128)(2,1)S(1)} %collective-permute-done.5.refs_1_), channel_id=1, source_target_pairs={{0,2},{2,3},{3,1},{1,0},{4,6},{6,7},{7,5},{5,4},{8,10},{10,11},{11... | collective-permute-start | bytes 1966088 | tf_op jit(solution)/shard_map/ppermute | solution.py:61
  47.9 4.0 %collective-permute-start.14 = (f32[4,2560]{1,0:T(4,128)S(1)}, f32[4,2560]{1,0:T(4,128)S(1)}, u32[]{:S(2)}, u32[]{:S(2)}) collective-permute-start(f32[4,2560]{1,0:T(4,128)S(1)} %add.11.x_ref), channel_id=1, source_target_pairs={{0,8},{4,12},{8,0},{12,4},{16,24},{20,28},{24,16},{28,20},{1,9},{5... | collective-permute-start | bytes 122888 | tf_op jit(solution)/shard_map/ppermute | solution.py:71
  51.9 4.0 %collective-permute-start.15 = (f32[4,2560]{1,0:T(4,128)S(1)}, f32[4,2560]{1,0:T(4,128)S(1)}, u32[]{:S(2)}, u32[]{:S(2)}) collective-permute-start(f32[4,2560]{1,0:T(4,128)S(1)} %add.12.x_ref), channel_id=1, source_target_pairs={{0,16},{4,20},{8,24},{12,28},{16,0},{20,4},{24,8},{28,12},{1,17},{... | collective-permute-start | bytes 122888 | tf_op jit(solution)/shard_map/ppermute | solution.py:71
  60.4 11.3 %collective-permute-start.19 = (bf16[1,64,2560]{2,1,0:T(8,128)(2,1)S(1)}, bf16[1,64,2560]{2,1,0:T(8,128)(2,1)S(1)}, u32[]{:S(2)}, u32[]{:S(2)}) collective-permute-start(bf16[1,64,2560]{2,1,0:T(8,128)(2,1)S(1)} %get-tuple-element.67), channel_id=1, source_target_pairs={{0,2},{2,3},{3,1},{1,0},{4,6},{6,7},{7,5},{5,4},{8,10},{10,11},{11... | collective-permute-start | bytes 983048 | tf_op jit(solution)/shard_map/ppermute | solution.py:61
  63.8 12.0 %collective-permute-start.18 = (bf16[1,64,1280]{2,1,0:T(8,128)(2,1)S(1)}, bf16[1,64,1280]{2,1,0:T(8,128)(2,1)S(1)}, u32[]{:S(2)}, u32[]{:S(2)}) collective-permute-start(bf16[1,64,1280]{2,1,0:T(8,128)(2,1)S(1)} %get-tuple-element.66), channel_id=1, source_target_pairs={{0,2},{2,3},{3,1},{1,0},{4,6},{6,7},{7,5},{5,4},{8,10},{10,11},{11... | collective-permute-start | bytes 491528 | tf_op jit(solution)/shard_map/ppermute | solution.py:61
  64.9 13.5 %collective-permute-start.17 = (bf16[1,64,1280]{2,1,0:T(8,128)(2,1)S(1)}, bf16[1,64,1280]{2,1,0:T(8,128)(2,1)S(1)}, u32[]{:S(2)}, u32[]{:S(2)}) collective-permute-start(bf16[1,64,1280]{2,1,0:T(8,128)(2,1)S(1)} %get-tuple-element.65), channel_id=1, source_target_pairs={{0,2},{2,3},{3,1},{1,0},{4,6},{6,7},{7,5},{5,4},{8,10},{10,11},{11... | collective-permute-start | bytes 491528 | tf_op jit(solution)/shard_map/ppermute | solution.py:61
  66.0 1.2 %collective-permute-start.16 = (f32[4,2560]{1,0:T(4,128)S(1)}, f32[4,2560]{1,0:T(4,128)S(1)}, u32[]{:S(2)}, u32[]{:S(2)}) collective-permute-start(f32[4,2560]{1,0:T(4,128)S(1)} %add.13.mine_ref), channel_id=1, source_target_pairs={{0,4},{4,0},{8,12},{12,8},{16,20},{20,16},{24,28},{28,24},{1,5},{5... | collective-permute-start | bytes 122888 | tf_op jit(solution)/shard_map/ppermute | solution.py:71

commit v7 on v6

--- a/solution.py
+++ b/solution.py
@@ -12,7 +12,6 @@
 SHRINK = 2.0**-23
 TINY = 1e-30
 BLOCK = 512
-SHARES = (2, 4, 4)
 
 
 def params(mib):
@@ -92,15 +91,15 @@
     gw_ref[0:rank, 0 : g.shape[1]] = sum3(dot(terms, g[0], (1, 1)), rank)
 
 
-def cut_kernel(g_ref, *refs):
+def cut_kernel(x_ref, *refs):
     chunks, sems = refs[:-1], refs[-1]
-    copies = []
-    at = 0
-    for c, chunk in enumerate(chunks):
-        part = chunk.shape[2]
-        copies.append(pltpu.make_async_copy(g_ref.at[:, :, pl.ds(at, part)], chunk, sems.at[c]))
-        copies[-1].start()
-        at += part
+    part = chunks[0].shape[2]
+    copies = [
+        pltpu.make_async_copy(x_ref.at[:, :, pl.ds(c * part, part)], chunk, sems.at[c])
+        for c, chunk in enumerate(chunks)
+    ]
+    for copy in copies:
+        copy.start()
     for copy in copies:
         copy.wait()
 
@@ -259,18 +258,27 @@
     right_ref[...] = right[...].astype(BF16)
 
 
-def final_kernel(n, at, part, a_ref, left_ref, right_ref, e_ref, *refs):
-    slots = refs[:n]
-    rebuilt_hbm, error_hbm, acts, acts_t, rebuilt_v, error_v, sems = refs[-7:]
-    tok = slots[0].shape[1]
-    rows = e_ref.shape[1]
+def acts_kernel(n, a_ref, out_ref, acts):
+    tok = a_ref.shape[1] // n
     me = lax.axis_index("tensor")
     for s in range(n):
         src = ring_source(me, s, n)
         here = a_ref[0, pl.ds(pl.multiple_of(src * tok, tok), tok), :]
         acts[s * tok : (s + 1) * tok, :] = here
-    acts_t[...] = acts[...].T
-
+    out_ref[...] = acts[...].T
+
+
+def rebuilt_kernel(left_ref, right_ref, out_ref):
+    left = left_ref[...]
+    for c in range(right_ref.shape[1] // BLOCK):
+        cols = slice(c * BLOCK, (c + 1) * BLOCK)
+        out_ref[:, cols] = dot(left, right_ref[:, cols], (1, 0)).astype(BF16)
+
+
+def final_kernel(at, part, bases, acts_ref, left_ref, right_ref, e_ref, *refs):
+    slots = refs[: len(bases)]
+    error_hbm, error_v, sems = refs[-3:]
+    rows = e_ref.shape[1]
     wide = 256
     high = rows // sems.shape[0]
     copies = []
@@ -279,26 +287,20 @@
         for c in range(part // wide):
             cols = slice(c * wide, (c + 1) * wide)
             there = slice(at + c * wide, at + (c + 1) * wide)
-            grads = jnp.concatenate(
-                [slot[0, :, cols if slot.shape[2] == part else there] for slot in slots], axis=0
-            )
-            matrix = dot(acts_t[here, :], grads, (1, 0)) + e_ref[0, here, there].astype(F32)
+            grads = [
+                slot[0, :, there.start - base : there.stop - base]
+                for slot, base in zip(slots, bases)
+            ]
+            grad = dot(acts_ref[here, :], jnp.concatenate(grads, axis=0), (1, 0))
+            matrix = grad + e_ref[0, here, there].astype(F32)
             rebuilt = dot(left_ref[here, :], right_ref[:, there], (1, 0))
-            rebuilt_v[here, cols] = rebuilt.astype(BF16)
             error_v[here, cols] = (matrix - rebuilt).astype(BF16)
         strip = pl.ds(r * high, high)
-        span = pl.ds(at, part)
         copies.append(
             pltpu.make_async_copy(
-                rebuilt_v.at[strip, :], rebuilt_hbm.at[strip, span], sems.at[r, 0]
+                error_v.at[strip, :], error_hbm.at[0, strip, pl.ds(at, part)], sems.at[r]
             )
         )
-        copies.append(
-            pltpu.make_async_copy(
-                error_v.at[strip, :], error_hbm.at[0, strip, span], sems.at[r, 1]
-            )
-        )
-        copies[-2].start()
         copies[-1].start()
     for copy in copies:
         copy.wait()
@@ -310,8 +312,6 @@
     _, tokens, rows = activations.shape
     _, tok, width = out_grads.shape
     rank = warm_factor.shape[1]
-    widths = [width // share for share in SHARES]
-    parts = len(widths)
     half = width // 2
     w = warm_factor.T
     sds = jax.ShapeDtypeStruct
@@ -396,16 +396,16 @@
     total = add(keep, swap(send, "dp", m, 1))
     for bit in bits(n):
         total = add(total, swap(total, "tensor", n, bit))
-    for _ in range(2, n - 1):
-        last, total = after(ring[-1], total)
-        ring.append(ring_step(last, "tensor", n))
+    def cut(x, count):
+        part = x.shape[2] // count
+        return call(cut_kernel, [sds((1, tok, part), BF16)] * count, [dma((count,))], "cut")(x)
+
+    sides = [[x] for x in cut(ring[1], 2)]
+    for side in sides:
+        last, total = after(side[-1], total)
+        side.append(ring_step(last, "tensor", n))
     for bit in bits(m)[1:]:
         total = add(total, swap(total, "dp", m, bit))
-    ring[-1], total = after(ring[-1], total)
-    chunks = call(
-        cut_kernel, [sds((1, tok, part), BF16) for part in widths], [dma((parts,))], "cut"
-    )(ring[-1])
-    chunks = [ring_step(chunk, "tensor", n) for chunk in chunks]
 
     terms = len(LEFT_TERMS) * rank
     whole, left_terms, right_terms = call(
@@ -419,27 +419,54 @@
         "factor",
     )(ortho, total, swap(total, "dp", m, 1))
 
-    outs = ()
-    for c, (part, chunk) in enumerate(zip(widths, chunks)):
-        outs = pl.pallas_call(
-            functools.partial(final_kernel, n, sum(widths[:c]), part),
-            in_specs=[vmem] * (4 + n) + [pl.BlockSpec(memory_space=pl.ANY)] * len(outs),
-            out_specs=[pl.BlockSpec(memory_space=pl.ANY)] * 2,
-            out_shape=[sds((rows, width), BF16), sds((1, rows, width), BF16)],
-            input_output_aliases={4 + n + j: j for j in range(len(outs))},
-            scratch_shapes=[
-                pltpu.VMEM((tokens, rows), BF16),
-                pltpu.VMEM((rows, tokens), BF16),
-                pltpu.VMEM((rows, part), BF16),
-                pltpu.VMEM((rows, part), BF16),
-                dma((3, 2)),
-            ],
+    acts = call(
+        functools.partial(acts_kernel, n),
+        sds((rows, tokens), BF16),
+        [pltpu.VMEM((tokens, rows), BF16)],
+        "acts",
+    )(activations)
+    for _ in range(3, n - 1):
+        for side in sides:
+            last, right_terms = after(side[-1], right_terms)
+            side.append(ring_step(last, "tensor", n))
+    last, right_terms = after(sides[0][-1], right_terms)
+    sides[0].append(ring_step(last, "tensor", n))
+
+    rebuilt = pl.pallas_call(
+        rebuilt_kernel,
+        grid=(rows // 128,),
+        in_specs=[
+            pl.BlockSpec((128, terms), lambda i: (i, 0)),
+            pl.BlockSpec((terms, width), lambda i: (0, 0)),
+        ],
+        out_specs=pl.BlockSpec((128, width), lambda i: (i, 0)),
+        out_shape=sds((rows, width), BF16),
+        compiler_params=params(16),
+        cost_estimate=cost(0),
+        name="rebuilt",
+    )(left_terms, right_terms)
+    last, rebuilt = after(sides[1][-1], rebuilt)
+    pieces = [(0, half, [sides[0][-1]])]
+    for c, x in enumerate(cut(last, 2)):
+        pieces.append((half + c * half // 2, half // 2, [ring_step(x, "tensor", n)]))
+
+    error = ()
+    for at, part, newest in pieces:
+        side = at // half
+        slots = ring + sides[side][1 : n - 2] + newest
+        bases = [0, 0] + [side * half] * (n - 3) + [at]
+        error = pl.pallas_call(
+            functools.partial(final_kernel, at, part, bases),
+            in_specs=[vmem] * (4 + n) + [pl.BlockSpec(memory_space=pl.ANY)] * len(error),
+            out_specs=[pl.BlockSpec(memory_space=pl.ANY)],
+            out_shape=[sds((1, rows, width), BF16)],
+            input_output_aliases={4 + n: 0} if error else {},
+            scratch_shapes=[pltpu.VMEM((rows, part), BF16), dma((3,))],
             compiler_params=params(16),
             cost_estimate=cost(0),
-            name="rebuild",
-        )(activations, left_terms, right_terms, error_v, *ring, chunk, *outs)
-    rebuilt, error = outs
-    return rebuilt, error, whole.T
+            name="error",
+        )(acts, left_terms, right_terms, error_v, *slots, *error)
+    return rebuilt, error[0], whole.T
 
 
 def solution(mesh):

time: 81.1 us -> 78.9 us (0.973)
  waiting for transfers between devices: 31 us -> 26 us
  Pallas kernels: 18.2 us -> 21.5 us
    ppermute x5 -> x6, waiting for transfers between devices: 9.21 us -> 4.3 us  [ring_step(): lax.ppermute(x, axis, [(ring[p], ring[(p + 1) % n]) for p in range(n)])]
    pallas_call x4 -> x7, Pallas kernels: 9.34 us -> 12.7 us  [the longest x3 7.35 us: per_device(): pl.pallas_call(functools.partial(final_kernel, at, part, bases), in_specs...]
    ppermute x5 -> x6, starting transfers between devices: 9.35 us -> 8.75 us  [ring_step(): lax.ppermute(x, axis, [(ring[p], ring[(p + 1) % n]) for p in range(n)])]
  transfers between devices with their start and end apart: 20 -> 21, of which waited for: 16 -> 17; matrix products, arithmetic and copies ran while one was open for 0% -> 0% of each run, Pallas kernels for 16% -> 21%
where the time goes in v7:
time: 78.9 us; the launch traced here: 78.7 us
  starting transfers between devices  30.4 us (39%)
  waiting for transfers between devices  26 us (33%)
  Pallas kernels  21.5 us (27%)
    ppermute x9, waiting for transfers between devices, swap(): return lax.ppermute(x, axis, [(i, i ^ bit) for i in range(n)])  17.2 us
    ppermute x6, starting transfers between devices, exchange(): lax.ppermute(pieces[k], axis, [(i, (i + k) % n) for i in range(n)])  10.8 us
    ppermute x9, starting transfers between devices, swap(): return lax.ppermute(x, axis, [(i, i ^ bit) for i in range(n)])  10.8 us
    ppermute x6, starting transfers between devices, ring_step(): lax.ppermute(x, axis, [(ring[p], ring[(p + 1) % n]) for p in range(n)])  8.75 us
    pallas_call x3, Pallas kernels, per_device(): pl.pallas_call(functools.partial(final_kernel, at, part, bases), in_specs...  7.35 us
    pallas_call x1, Pallas kernels, per_device(): pl.pallas_call(rebuilt_kernel, grid=(rows // 128,), in_specs=[pl.BlockSpe...  5.08 us
    ppermute x6, waiting for transfers between devices, exchange(): lax.ppermute(pieces[k], axis, [(i, (i + k) % n) for i in range(n)])  4.58 us
    ppermute x6, waiting for transfers between devices, ring_step(): lax.ppermute(x, axis, [(ring[p], ring[(p + 1) % n]) for p in range(n)])  4.3 us
  transfers between devices with their start and end apart: 21, of which 17 were waited for; matrix products, arithmetic and copies ran while one was open for 0% of the time, Pallas kernels for 21%

profile of v7, /device:TPU:0, one launch (start us, length us, event | category | flops | bytes accessed | tf_op | source)
XLA Modules:
  0.0 78.7 jit_solution(8609195271503904655)
XLA Ops:
  2.1 5.1 %collective-permute-start.2 = (f32[8,128]{1,0:T(8,128)S(1)}, f32[8,128]{1,0:T(8,128)S(1)}, u32[]{:S(2)}, u32[]{:S(2)}) collective-permute-start(f32[8,128]{1,0:T(8,128)S(1)} %get-tuple-element.43.refs_0_), channel_id=1, source_target_pairs={{0,3},{1,0},{2,1},{3,2},{4,7},{5,4},{6,5},{7,6},{8,11},{9,8},{10,9... | collective-permute-start | bytes 12296 | tf_op jit(solution)/shard_map/ppermute | solution.py:65
  8.6 3.2 %collective-permute-done.1.refs_2_ = f32[8,128]{1,0:T(8,128)S(1)} collective-permute-done((f32[8,128]{1,0:T(8,128)S(1)}, f32[8,128]{1,0:T(8,128)S(1)}, u32[]{:S(2)}, u32[]{:S(2)}) %collective-permute-start.1) | collective-permute-done | bytes 4128 | tf_op jit(solution)/shard_map/ppermute | solution.py:65
  13.8 4.1 %error_left.1 = (f32[4,768]{1,0:T(4,128)S(1)}, bf16[1,768,5120]{2,1,0:T(8,128)(2,1)S(1)}) custom-call(bf16[12,5120]{1,0:T(8,128)(2,1)S(1)} %get-tuple-element.41.terms_ref, bf16[1,768,5120]{2,1,0:T(8,128)(2,1)} %e_hbm.1), custom_call_target="tpu_custom_call" | custom-call | flops 1 | bytes 1 | tf_op jit(solution)/shard_map/error_left/pallas_call | solution.py:356
  20.9 2.2 %collective-permute-done.5.y_ref = f32[4,768]{1,0:T(4,128)S(1)} collective-permute-done((f32[4,768]{1,0:T(4,128)S(1)}, f32[4,768]{1,0:T(4,128)S(1)}, u32[]{:S(2)}, u32[]{:S(2)}) %collective-permute-start.5) | collective-permute-done | bytes 12320 | tf_op jit(solution)/shard_map/ppermute | solution.py:70
  23.1 1.5 %collective-permute-start.6 = (f32[4,768]{1,0:T(4,128)S(1)}, f32[4,768]{1,0:T(4,128)S(1)}, u32[]{:S(2)}, u32[]{:S(2)}) collective-permute-start(f32[4,768]{1,0:T(4,128)S(1)} %add.8.x_ref), channel_id=1, source_target_pairs={{0,16},{4,20},{8,24},{12,28},{16,0},{20,4},{24,8},{28,12},{1,17},{... | collective-permute-start | bytes 36872 | tf_op jit(solution)/shard_map/ppermute | solution.py:70
  24.6 2.2 %collective-permute-done.6.y_ref = f32[4,768]{1,0:T(4,128)S(1)} collective-permute-done((f32[4,768]{1,0:T(4,128)S(1)}, f32[4,768]{1,0:T(4,128)S(1)}, u32[]{:S(2)}, u32[]{:S(2)}) %collective-permute-start.6) | collective-permute-done | bytes 12320 | tf_op jit(solution)/shard_map/ppermute | solution.py:70
  28.6 1.5 %collective-permute-start.8 = (f32[8,128]{1,0:T(8,128)S(1)}, f32[8,128]{1,0:T(8,128)S(1)}, u32[]{:S(2)}, u32[]{:S(2)}) collective-permute-start(f32[8,128]{1,0:T(8,128)S(1)} %get-tuple-element.55), channel_id=1, source_target_pairs={{0,2},{1,3},{2,0},{3,1},{4,6},{5,7},{6,4},{7,5},{8,10},{9,11},{10,... | collective-permute-start | bytes 12296 | tf_op jit(solution)/shard_map/ppermute | solution.py:65
  30.1 2.8 %collective-permute-start.9 = (f32[8,128]{1,0:T(8,128)S(1)}, f32[8,128]{1,0:T(8,128)S(1)}, u32[]{:S(2)}, u32[]{:S(2)}) collective-permute-start(f32[8,128]{1,0:T(8,128)S(1)} %get-tuple-element.56), channel_id=1, source_target_pairs={{0,3},{1,0},{2,1},{3,2},{4,7},{5,4},{6,5},{7,6},{8,11},{9,8},{10,9... | collective-permute-start | bytes 12296 | tf_op jit(solution)/shard_map/ppermute | solution.py:65
  36.4 2.0 %collective-permute-start.11 = (f32[4,2560]{1,0:T(4,128)S(1)}, f32[4,2560]{1,0:T(4,128)S(1)}, u32[]{:S(2)}, u32[]{:S(2)}) collective-permute-start(f32[4,2560]{1,0:T(4,128)S(1)} %add.9.x_ref), channel_id=1, source_target_pairs={{0,1},{1,0},{2,3},{3,2},{4,5},{5,4},{6,7},{7,6},{8,9},{9,8},{10,11... | collective-permute-start | bytes 122888 | tf_op jit(solution)/shard_map/ppermute | solution.py:70
  38.4 2.0 %collective-permute-done.11.y_ref = f32[4,2560]{1,0:T(4,128)S(1)} collective-permute-done((f32[4,2560]{1,0:T(4,128)S(1)}, f32[4,2560]{1,0:T(4,128)S(1)}, u32[]{:S(2)}, u32[]{:S(2)}) %collective-permute-start.11) | collective-permute-done | bytes 40992 | tf_op jit(solution)/shard_map/ppermute | solution.py:70
  40.4 2.6 %collective-permute-start.12 = (f32[4,2560]{1,0:T(4,128)S(1)}, f32[4,2560]{1,0:T(4,128)S(1)}, u32[]{:S(2)}, u32[]{:S(2)}) collective-permute-start(f32[4,2560]{1,0:T(4,128)S(1)} %add.10.x_ref), channel_id=1, source_target_pairs={{0,2},{1,3},{2,0},{3,1},{4,6},{5,7},{6,4},{7,5},{8,10},{9,11},{10,... | collective-permute-start | bytes 122888 | tf_op jit(solution)/shard_map/ppermute | solution.py:70
  43.1 2.2 %collective-permute-done.12.y_ref = f32[4,2560]{1,0:T(4,128)S(1)} collective-permute-done((f32[4,2560]{1,0:T(4,128)S(1)}, f32[4,2560]{1,0:T(4,128)S(1)}, u32[]{:S(2)}, u32[]{:S(2)}) %collective-permute-start.12) | collective-permute-done | bytes 40992 | tf_op jit(solution)/shard_map/ppermute | solution.py:70
  45.3 2.6 %collective-permute-start.17 = (bf16[1,64,2560]{2,1,0:T(8,128)(2,1)S(1)}, bf16[1,64,2560]{2,1,0:T(8,128)(2,1)S(1)}, u32[]{:S(2)}, u32[]{:S(2)}) collective-permute-start(bf16[1,64,2560]{2,1,0:T(8,128)(2,1)S(1)} %get-tuple-element.64), channel_id=1, source_target_pairs={{0,2},{2,3},{3,1},{1,0},{4,6},{6,7},{7,5},{5,4},{8,10},{10,11},{11... | collective-permute-start | bytes 983048 | tf_op jit(solution)/shard_map/ppermute | solution.py:60
  47.9 2.0 %collective-permute-start.13 = (bf16[1,64,2560]{2,1,0:T(8,128)(2,1)S(1)}, bf16[1,64,2560]{2,1,0:T(8,128)(2,1)S(1)}, u32[]{:S(2)}, u32[]{:S(2)}) collective-permute-start(bf16[1,64,2560]{2,1,0:T(8,128)(2,1)S(1)} %get-tuple-element.60), channel_id=1, source_target_pairs={{0,2},{2,3},{3,1},{1,0},{4,6},{6,7},{7,5},{5,4},{8,10},{10,11},{11... | collective-permute-start | bytes 983048 | tf_op jit(solution)/shard_map/ppermute | solution.py:60
  50.0 1.5 %collective-permute-start.14 = (f32[4,2560]{1,0:T(4,128)S(1)}, f32[4,2560]{1,0:T(4,128)S(1)}, u32[]{:S(2)}, u32[]{:S(2)}) collective-permute-start(f32[4,2560]{1,0:T(4,128)S(1)} %add.11.x_ref), channel_id=1, source_target_pairs={{0,8},{4,12},{8,0},{12,4},{16,24},{20,28},{24,16},{28,20},{1,9},{5... | collective-permute-start | bytes 122888 | tf_op jit(solution)/shard_map/ppermute | solution.py:70
  51.5 2.5 %collective-permute-done.14.y_ref = f32[4,2560]{1,0:T(4,128)S(1)} collective-permute-done((f32[4,2560]{1,0:T(4,128)S(1)}, f32[4,2560]{1,0:T(4,128)S(1)}, u32[]{:S(2)}, u32[]{:S(2)}) %collective-permute-start.14) | collective-permute-done | bytes 40992 | tf_op jit(solution)/shard_map/ppermute | solution.py:70
  54.0 1.5 %collective-permute-start.15 = (f32[4,2560]{1,0:T(4,128)S(1)}, f32[4,2560]{1,0:T(4,128)S(1)}, u32[]{:S(2)}, u32[]{:S(2)}) collective-permute-start(f32[4,2560]{1,0:T(4,128)S(1)} %add.12.x_ref), channel_id=1, source_target_pairs={{0,16},{4,20},{8,24},{12,28},{16,0},{20,4},{24,8},{28,12},{1,17},{... | collective-permute-start | bytes 122888 | tf_op jit(solution)/shard_map/ppermute | solution.py:70
  55.5 2.5 %collective-permute-done.15.y_ref = f32[4,2560]{1,0:T(4,128)S(1)} collective-permute-done((f32[4,2560]{1,0:T(4,128)S(1)}, f32[4,2560]{1,0:T(4,128)S(1)}, u32[]{:S(2)}, u32[]{:S(2)}) %collective-permute-start.15) | collective-permute-done | bytes 40992 | tf_op jit(solution)/shard_map/ppermute | solution.py:70
  60.2 5.1 %rebuilt.1 = bf16[768,5120]{1,0:T(8,128)(2,1)} custom-call(bf16[768,24]{1,0:T(8,128)(2,1)S(1)} %get-tuple-element.63.left_ref, bf16[24,5120]{1,0:T(8,128)(2,1)S(1)} %get-tuple-element.66.right_ref), custom_call_target="tpu_custom_call" | custom-call | flops 1 | bytes 1 | tf_op jit(solution)/shard_map/rebuilt/pallas_call | solution.py:435
  65.8 2.2 %collective-permute-start.18 = (bf16[1,64,1280]{2,1,0:T(8,128)(2,1)S(1)}, bf16[1,64,1280]{2,1,0:T(8,128)(2,1)S(1)}, u32[]{:S(2)}, u32[]{:S(2)}) collective-permute-start(bf16[1,64,1280]{2,1,0:T(8,128)(2,1)S(1)} %get-tuple-element.69), channel_id=1, source_target_pairs={{0,2},{2,3},{3,1},{1,0},{4,6},{6,7},{7,5},{5,4},{8,10},{10,11},{11... | collective-permute-start | bytes 491528 | tf_op jit(solution)/shard_map/ppermute | solution.py:60
  68.2 2.3 %collective-permute-done.20.refs_3_ = bf16[1,64,2560]{2,1,0:T(8,128)(2,1)S(1)} collective-permute-done((bf16[1,64,2560]{2,1,0:T(8,128)(2,1)S(1)}, bf16[1,64,2560]{2,1,0:T(8,128)(2,1)S(1)}, u32[]{:S(2)}, u32[]{:S(2)}) %collective-permute-start.20) | collective-permute-done | bytes 327712 | tf_op jit(solution)/shard_map/ppermute | solution.py:60
  70.5 3.3 %error.3.refs_4_ = bf16[1,768,5120]{2,1,0:T(8,128)(2,1)} custom-call(bf16[768,256]{1,0:T(8,128)(2,1)S(1)} %acts.1.acts_ref, bf16[768,24]{1,0:T(8,128)(2,1)S(1)} %get-tuple-element.63.left_ref, bf16[24,5120]{1,0:T(8,128)(2,1)S(1)} %get-tuple-element.66.right_ref, bf16[1,768,5120]{2,1,0:T(8,128)(2,1)S(1)} %get-tuple-element.52.e_ref, ...), custom_call_target="tpu_custom_call" | custom-call | flops 1 | bytes 1 | tf_op jit(solution)/shard_map/error/pallas_call | solution.py:458
  74.0 2.0 %error.4.refs_4_ = bf16[1,768,5120]{2,1,0:T(8,128)(2,1)} custom-call(bf16[768,256]{1,0:T(8,128)(2,1)S(1)} %acts.1.acts_ref, bf16[768,24]{1,0:T(8,128)(2,1)S(1)} %get-tuple-element.63.left_ref, bf16[24,5120]{1,0:T(8,128)(2,1)S(1)} %get-tuple-element.66.right_ref, bf16[1,768,5120]{2,1,0:T(8,128)(2,1)S(1)} %get-tuple-element.52.e_ref, ...), custom_call_target="tpu_custom_call", output_to_operand_aliasing={{}: (8, {})} | custom-call | flops 1 | bytes 1 | tf_op jit(solution)/shard_map/error/pallas_call | solution.py:458
  76.7 2.0 %error.5 = bf16[1,768,5120]{2,1,0:T(8,128)(2,1)} custom-call(bf16[768,256]{1,0:T(8,128)(2,1)S(1)} %acts.1.acts_ref, bf16[768,24]{1,0:T(8,128)(2,1)S(1)} %get-tuple-element.63.left_ref, bf16[24,5120]{1,0:T(8,128)(2,1)S(1)} %get-tuple-element.66.right_ref, bf16[1,768,5120]{2,1,0:T(8,128)(2,1)S(1)} %get-tuple-element.52.e_ref, ...), custom_call_target="tpu_custom_call", output_to_operand_aliasing={{}: (8, {})} | custom-call | flops 1 | bytes 1 | tf_op jit(solution)/shard_map/error/pallas_call | solution.py:458
  (43 shorter events, 16.9 us)
Async XLA Ops:
  0.6 17.3 %copy-start.1 = (bf16[1,256,768]{2,1,0:T(8,128)(2,1)S(1)}, bf16[1,256,768]{2,1,0:T(8,128)(2,1)}, u32[]{:S(2)}) copy-start(bf16[1,256,768]{2,1,0:T(8,128)(2,1)} %a_ref.5) | copy-start | bytes 1179652
  2.1 6.4 %collective-permute-start.2 = (f32[8,128]{1,0:T(8,128)S(1)}, f32[8,128]{1,0:T(8,128)S(1)}, u32[]{:S(2)}, u32[]{:S(2)}) collective-permute-start(f32[8,128]{1,0:T(8,128)S(1)} %get-tuple-element.43.refs_0_), channel_id=1, source_target_pairs={{0,3},{1,0},{2,1},{3,2},{4,7},{5,4},{6,5},{7,6},{8,11},{9,8},{10,9... | collective-permute-start | bytes 12296 | tf_op jit(solution)/shard_map/ppermute | solution.py:65
  7.2 4.5 %collective-permute-start.1 = (f32[8,128]{1,0:T(8,128)S(1)}, f32[8,128]{1,0:T(8,128)S(1)}, u32[]{:S(2)}, u32[]{:S(2)}) collective-permute-start(f32[8,128]{1,0:T(8,128)S(1)} %get-tuple-element.43.refs_0_), channel_id=1, source_target_pairs={{0,2},{1,3},{2,0},{3,1},{4,6},{5,7},{6,4},{7,5},{8,10},{9,11},{10,... | collective-permute-start | bytes 12296 | tf_op jit(solution)/shard_map/ppermute | solution.py:65
  7.2 5.4 %collective-permute-start = (f32[8,128]{1,0:T(8,128)S(1)}, f32[8,128]{1,0:T(8,128)S(1)}, u32[]{:S(2)}, u32[]{:S(2)}) collective-permute-start(f32[8,128]{1,0:T(8,128)S(1)} %get-tuple-element.43.refs_0_), channel_id=1, source_target_pairs={{0,1},{1,2},{2,3},{3,0},{4,5},{5,6},{6,7},{7,4},{8,9},{9,10},{10,1... | collective-permute-start | bytes 12296 | tf_op jit(solution)/shard_map/ppermute | solution.py:65
  12.6 21.6 %copy-start = (bf16[1,64,5120]{2,1,0:T(8,128)(2,1)S(1)}, bf16[1,64,5120]{2,1,0:T(8,128)(2,1)}, u32[]{:S(2)}) copy-start(bf16[1,64,5120]{2,1,0:T(8,128)(2,1)} %refs_0_.5) | copy-start | bytes 1966084
  12.6 15.3 %collective-permute-start.3 = (bf16[1,64,5120]{2,1,0:T(8,128)(2,1)}, bf16[1,64,5120]{2,1,0:T(8,128)(2,1)S(1)}, u32[]{:S(2)}, u32[]{:S(2)}) collective-permute-start(bf16[1,64,5120]{2,1,0:T(8,128)(2,1)} %refs_0_.5), channel_id=1, source_target_pairs={{0,2},{2,3},{3,1},{1,0},{4,6},{6,7},{7,5},{5,4},{8,10},{10,11},{11... | collective-permute-start | bytes 1966088 | tf_op jit(solution)/shard_map/ppermute | solution.py:60
  18.1 1.2 %collective-permute-start.4 = (f32[4,768]{1,0:T(4,128)S(1)}, f32[4,768]{1,0:T(4,128)S(1)}, u32[]{:S(2)}, u32[]{:S(2)}) collective-permute-start(f32[4,768]{1,0:T(4,128)S(1)} %left.1.x_ref), channel_id=1, source_target_pairs={{0,4},{4,0},{8,12},{12,8},{16,20},{20,16},{24,28},{28,24},{1,5},{5... | collective-permute-start | bytes 36872 | tf_op jit(solution)/shard_map/ppermute | solution.py:70
  19.4 3.7 %collective-permute-start.5 = (f32[4,768]{1,0:T(4,128)S(1)}, f32[4,768]{1,0:T(4,128)S(1)}, u32[]{:S(2)}, u32[]{:S(2)}) collective-permute-start(f32[4,768]{1,0:T(4,128)S(1)} %add.7.x_ref), channel_id=1, source_target_pairs={{0,8},{4,12},{8,0},{12,4},{16,24},{20,28},{24,16},{28,20},{1,9},{5... | collective-permute-start | bytes 36872 | tf_op jit(solution)/shard_map/ppermute | solution.py:70
  23.1 3.7 %collective-permute-start.6 = (f32[4,768]{1,0:T(4,128)S(1)}, f32[4,768]{1,0:T(4,128)S(1)}, u32[]{:S(2)}, u32[]{:S(2)}) collective-permute-start(f32[4,768]{1,0:T(4,128)S(1)} %add.8.x_ref), channel_id=1, source_target_pairs={{0,16},{4,20},{8,24},{12,28},{16,0},{20,4},{24,8},{28,12},{1,17},{... | collective-permute-start | bytes 36872 | tf_op jit(solution)/shard_map/ppermute | solution.py:70
  28.2 5.9 %collective-permute-start.7 = (f32[8,128]{1,0:T(8,128)S(1)}, f32[8,128]{1,0:T(8,128)S(1)}, u32[]{:S(2)}, u32[]{:S(2)}) collective-permute-start(f32[8,128]{1,0:T(8,128)S(1)} %get-tuple-element.54), channel_id=1, source_target_pairs={{0,1},{1,2},{2,3},{3,0},{4,5},{5,6},{6,7},{7,4},{8,9},{9,10},{10,1... | collective-permute-start | bytes 12296 | tf_op jit(solution)/shard_map/ppermute | solution.py:65
  28.6 5.5 %collective-permute-start.8 = (f32[8,128]{1,0:T(8,128)S(1)}, f32[8,128]{1,0:T(8,128)S(1)}, u32[]{:S(2)}, u32[]{:S(2)}) collective-permute-start(f32[8,128]{1,0:T(8,128)S(1)} %get-tuple-element.55), channel_id=1, source_target_pairs={{0,2},{1,3},{2,0},{3,1},{4,6},{5,7},{6,4},{7,5},{8,10},{9,11},{10,... | collective-permute-start | bytes 12296 | tf_op jit(solution)/shard_map/ppermute | solution.py:65
  30.1 4.2 %collective-permute-start.9 = (f32[8,128]{1,0:T(8,128)S(1)}, f32[8,128]{1,0:T(8,128)S(1)}, u32[]{:S(2)}, u32[]{:S(2)}) collective-permute-start(f32[8,128]{1,0:T(8,128)S(1)} %get-tuple-element.56), channel_id=1, source_target_pairs={{0,3},{1,0},{2,1},{3,2},{4,7},{5,4},{6,5},{7,6},{8,11},{9,8},{10,9... | collective-permute-start | bytes 12296 | tf_op jit(solution)/shard_map/ppermute | solution.py:65
  35.1 1.3 %collective-permute-start.10 = (f32[4,2560]{1,0:T(4,128)S(1)}, f32[4,2560]{1,0:T(4,128)S(1)}, u32[]{:S(2)}, u32[]{:S(2)}) collective-permute-start(f32[4,2560]{1,0:T(4,128)S(1)} %get-tuple-element.58), channel_id=1, source_target_pairs={{0,4},{4,0},{8,12},{12,8},{16,20},{20,16},{24,28},{28,24},{1,5},{5... | collective-permute-start | bytes 122888 | tf_op jit(solution)/shard_map/ppermute | solution.py:70
  36.4 4.0 %collective-permute-start.11 = (f32[4,2560]{1,0:T(4,128)S(1)}, f32[4,2560]{1,0:T(4,128)S(1)}, u32[]{:S(2)}, u32[]{:S(2)}) collective-permute-start(f32[4,2560]{1,0:T(4,128)S(1)} %add.9.x_ref), channel_id=1, source_target_pairs={{0,1},{1,0},{2,3},{3,2},{4,5},{5,4},{6,7},{7,6},{8,9},{9,8},{10,11... | collective-permute-start | bytes 122888 | tf_op jit(solution)/shard_map/ppermute | solution.py:70
  40.4 4.9 %collective-permute-start.12 = (f32[4,2560]{1,0:T(4,128)S(1)}, f32[4,2560]{1,0:T(4,128)S(1)}, u32[]{:S(2)}, u32[]{:S(2)}) collective-permute-start(f32[4,2560]{1,0:T(4,128)S(1)} %add.10.x_ref), channel_id=1, source_target_pairs={{0,2},{1,3},{2,0},{3,1},{4,6},{5,7},{6,4},{7,5},{8,10},{9,11},{10,... | collective-permute-start | bytes 122888 | tf_op jit(solution)/shard_map/ppermute | solution.py:70
  45.3 14.6 %collective-permute-start.17 = (bf16[1,64,2560]{2,1,0:T(8,128)(2,1)S(1)}, bf16[1,64,2560]{2,1,0:T(8,128)(2,1)S(1)}, u32[]{:S(2)}, u32[]{:S(2)}) collective-permute-start(bf16[1,64,2560]{2,1,0:T(8,128)(2,1)S(1)} %get-tuple-element.64), channel_id=1, source_target_pairs={{0,2},{2,3},{3,1},{1,0},{4,6},{6,7},{7,5},{5,4},{8,10},{10,11},{11... | collective-permute-start | bytes 983048 | tf_op jit(solution)/shard_map/ppermute | solution.py:60
  47.9 17.3 %collective-permute-start.13 = (bf16[1,64,2560]{2,1,0:T(8,128)(2,1)S(1)}, bf16[1,64,2560]{2,1,0:T(8,128)(2,1)S(1)}, u32[]{:S(2)}, u32[]{:S(2)}) collective-permute-start(bf16[1,64,2560]{2,1,0:T(8,128)(2,1)S(1)} %get-tuple-element.60), channel_id=1, source_target_pairs={{0,2},{2,3},{3,1},{1,0},{4,6},{6,7},{7,5},{5,4},{8,10},{10,11},{11... | collective-permute-start | bytes 983048 | tf_op jit(solution)/shard_map/ppermute | solution.py:60
  50.0 4.0 %collective-permute-start.14 = (f32[4,2560]{1,0:T(4,128)S(1)}, f32[4,2560]{1,0:T(4,128)S(1)}, u32[]{:S(2)}, u32[]{:S(2)}) collective-permute-start(f32[4,2560]{1,0:T(4,128)S(1)} %add.11.x_ref), channel_id=1, source_target_pairs={{0,8},{4,12},{8,0},{12,4},{16,24},{20,28},{24,16},{28,20},{1,9},{5... | collective-permute-start | bytes 122888 | tf_op jit(solution)/shard_map/ppermute | solution.py:70
  54.0 4.0 %collective-permute-start.15 = (f32[4,2560]{1,0:T(4,128)S(1)}, f32[4,2560]{1,0:T(4,128)S(1)}, u32[]{:S(2)}, u32[]{:S(2)}) collective-permute-start(f32[4,2560]{1,0:T(4,128)S(1)} %add.12.x_ref), channel_id=1, source_target_pairs={{0,16},{4,20},{8,24},{12,28},{16,0},{20,4},{24,8},{28,12},{1,17},{... | collective-permute-start | bytes 122888 | tf_op jit(solution)/shard_map/ppermute | solution.py:70
  58.0 1.2 %collective-permute-start.16 = (f32[4,2560]{1,0:T(4,128)S(1)}, f32[4,2560]{1,0:T(4,128)S(1)}, u32[]{:S(2)}, u32[]{:S(2)}) collective-permute-start(f32[4,2560]{1,0:T(4,128)S(1)} %add.13.mine_ref), channel_id=1, source_target_pairs={{0,4},{4,0},{8,12},{12,8},{16,20},{20,16},{24,28},{28,24},{1,5},{5... | collective-permute-start | bytes 122888 | tf_op jit(solution)/shard_map/ppermute | solution.py:70
  59.9 10.6 %collective-permute-start.20 = (bf16[1,64,2560]{2,1,0:T(8,128)(2,1)S(1)}, bf16[1,64,2560]{2,1,0:T(8,128)(2,1)S(1)}, u32[]{:S(2)}, u32[]{:S(2)}) collective-permute-start(bf16[1,64,2560]{2,1,0:T(8,128)(2,1)S(1)} %collective-permute-done.17.refs_2_), channel_id=1, source_target_pairs={{0,2},{2,3},{3,1},{1,0},{4,6},{6,7},{7,5},{5,4},{8,10},{10,11},{11... | collective-permute-start | bytes 983048 | tf_op jit(solution)/shard_map/ppermute | solution.py:60
  65.3 8.6 %collective-permute-start.19 = (bf16[1,64,1280]{2,1,0:T(8,128)(2,1)S(1)}, bf16[1,64,1280]{2,1,0:T(8,128)(2,1)S(1)}, u32[]{:S(2)}, u32[]{:S(2)}) collective-permute-start(bf16[1,64,1280]{2,1,0:T(8,128)(2,1)S(1)} %get-tuple-element.70), channel_id=1, source_target_pairs={{0,2},{2,3},{3,1},{1,0},{4,6},{6,7},{7,5},{5,4},{8,10},{10,11},{11... | collective-permute-start | bytes 491528 | tf_op jit(solution)/shard_map/ppermute | solution.py:60
  65.8 10.9 %collective-permute-start.18 = (bf16[1,64,1280]{2,1,0:T(8,128)(2,1)S(1)}, bf16[1,64,1280]{2,1,0:T(8,128)(2,1)S(1)}, u32[]{:S(2)}, u32[]{:S(2)}) collective-permute-start(bf16[1,64,1280]{2,1,0:T(8,128)(2,1)S(1)} %get-tuple-element.69), channel_id=1, source_target_pairs={{0,2},{2,3},{3,1},{1,0},{4,6},{6,7},{7,5},{5,4},{8,10},{10,11},{11... | collective-permute-start | bytes 491528 | tf_op jit(solution)/shard_map/ppermute | solution.py:60

commit v8 on v6

--- a/solution.py
+++ b/solution.py
@@ -12,7 +12,6 @@
 SHRINK = 2.0**-23
 TINY = 1e-30
 BLOCK = 512
-SHARES = (2, 4, 4)
 
 
 def params(mib):
@@ -92,13 +91,13 @@
     gw_ref[0:rank, 0 : g.shape[1]] = sum3(dot(terms, g[0], (1, 1)), rank)
 
 
-def cut_kernel(g_ref, *refs):
+def cut_kernel(x_ref, *refs):
     chunks, sems = refs[:-1], refs[-1]
     copies = []
     at = 0
     for c, chunk in enumerate(chunks):
         part = chunk.shape[2]
-        copies.append(pltpu.make_async_copy(g_ref.at[:, :, pl.ds(at, part)], chunk, sems.at[c]))
+        copies.append(pltpu.make_async_copy(x_ref.at[:, :, pl.ds(at, part)], chunk, sems.at[c]))
         copies[-1].start()
         at += part
     for copy in copies:
@@ -259,18 +258,20 @@
     right_ref[...] = right[...].astype(BF16)
 
 
-def final_kernel(n, at, part, a_ref, left_ref, right_ref, e_ref, *refs):
-    slots = refs[:n]
-    rebuilt_hbm, error_hbm, acts, acts_t, rebuilt_v, error_v, sems = refs[-7:]
-    tok = slots[0].shape[1]
-    rows = e_ref.shape[1]
+def acts_kernel(n, a_ref, out_ref, acts):
+    tok = a_ref.shape[1] // n
     me = lax.axis_index("tensor")
     for s in range(n):
         src = ring_source(me, s, n)
         here = a_ref[0, pl.ds(pl.multiple_of(src * tok, tok), tok), :]
         acts[s * tok : (s + 1) * tok, :] = here
-    acts_t[...] = acts[...].T
-
+    out_ref[...] = acts[...].T
+
+
+def final_kernel(at, part, bases, acts_ref, left_ref, right_ref, e_ref, *refs):
+    slots = refs[: len(bases)]
+    rebuilt_hbm, error_hbm, rebuilt_v, error_v, sems = refs[-5:]
+    rows = e_ref.shape[1]
     wide = 256
     high = rows // sems.shape[0]
     copies = []
@@ -279,25 +280,25 @@
         for c in range(part // wide):
             cols = slice(c * wide, (c + 1) * wide)
             there = slice(at + c * wide, at + (c + 1) * wide)
-            grads = jnp.concatenate(
-                [slot[0, :, cols if slot.shape[2] == part else there] for slot in slots], axis=0
-            )
-            matrix = dot(acts_t[here, :], grads, (1, 0)) + e_ref[0, here, there].astype(F32)
+            grads = [
+                slot[0, :, there.start - base : there.stop - base]
+                for slot, base in zip(slots, bases)
+            ]
+            grad = dot(acts_ref[here, :], jnp.concatenate(grads, axis=0), (1, 0))
+            matrix = grad + e_ref[0, here, there].astype(F32)
             rebuilt = dot(left_ref[here, :], right_ref[:, there], (1, 0))
             rebuilt_v[here, cols] = rebuilt.astype(BF16)
             error_v[here, cols] = (matrix - rebuilt).astype(BF16)
         strip = pl.ds(r * high, high)
         span = pl.ds(at, part)
-        copies.append(
+        copies += [
             pltpu.make_async_copy(
                 rebuilt_v.at[strip, :], rebuilt_hbm.at[strip, span], sems.at[r, 0]
-            )
-        )
-        copies.append(
+            ),
             pltpu.make_async_copy(
                 error_v.at[strip, :], error_hbm.at[0, strip, span], sems.at[r, 1]
-            )
-        )
+            ),
+        ]
         copies[-2].start()
         copies[-1].start()
     for copy in copies:
@@ -310,8 +311,6 @@
     _, tokens, rows = activations.shape
     _, tok, width = out_grads.shape
     rank = warm_factor.shape[1]
-    widths = [width // share for share in SHARES]
-    parts = len(widths)
     half = width // 2
     w = warm_factor.T
     sds = jax.ShapeDtypeStruct
@@ -333,6 +332,20 @@
 
     def add(x, y):
         return call(add_kernel, sds(x.shape, F32), [], "add")(x, y)
+
+    def after(x, y):
+        return lax.optimization_barrier((x, y))
+
+    def cut(x, widths):
+        shapes = [sds((1, tok, part), BF16) for part in widths]
+        return call(cut_kernel, shapes, [dma((len(widths),))], "cut")(x)
+
+    def step(x):
+        return ring_step(x, "tensor", n)
+
+    wide = 6 * width // 20
+    narrow = width // 2 - wide
+    ring = [out_grads, step(out_grads)]
 
     gw, w_terms = call(
         token_factor_kernel,
@@ -347,25 +360,22 @@
     )(pin(w), pin(out_grads))
     gws = exchange([gw] * n, "tensor", n)
 
-    def after(x, y):
-        return lax.optimization_barrier((x, y))
-
-    ring = [out_grads]
-    last, (w_terms, gws) = after(out_grads, (w_terms, gws))
-    ring.append(ring_step(last, "tensor", n))
     ew, error_v = call(
         error_left_kernel,
         [sds((rank, rows), F32), sds((1, rows, width), BF16)],
         [dma((rows // 128,))],
-        "error_left", [vmem, hbm],
+        "error_left", [vmem, hbm], 4.6e9,
     )(w_terms, pin(error_buffer))
 
+    ring[1], gws = after(ring[1], gws)
+    x1, y1 = cut(ring[1], [2 * wide, 2 * narrow])
+    xs, ys = [x1, step(x1)], [y1]
     left = call(
         left_kernel, sds((rank, rows), F32), [pltpu.VMEM((3 * rank, tok), F32)], "left"
     )(activations, ew, *gws)
     for bit in bits(m)[:-1]:
         left = add(left, swap(left, "dp", m, bit))
-    ring[1], last = after(ring[1], swap(left, "dp", m, bits(m)[-1]))
+    xs[1], last = after(xs[1], swap(left, "dp", m, bits(m)[-1]))
 
     mean, *msgs = call(
         functools.partial(mean_kernel, n, 1.0 / (SHRINK * m)),
@@ -396,16 +406,20 @@
     total = add(keep, swap(send, "dp", m, 1))
     for bit in bits(n):
         total = add(total, swap(total, "tensor", n, bit))
-    for _ in range(2, n - 1):
-        last, total = after(ring[-1], total)
-        ring.append(ring_step(last, "tensor", n))
-    for bit in bits(m)[1:]:
+    for _ in range(4, n):
+        last, total = after(xs[-1], total)
+        xs.append(step(last))
+    xa, xb = cut(xs[-1], [wide, wide])
+    xa, total = after(xa, total)
+    xa = step(xa)
+    for _ in range(3, n):
+        last, total = after(ys[-1], total)
+        ys.append(step(last))
+    total = add(total, swap(total, "dp", m, 2))
+    xb, total = after(xb, total)
+    xb = step(xb)
+    for bit in bits(m)[2:]:
         total = add(total, swap(total, "dp", m, bit))
-    ring[-1], total = after(ring[-1], total)
-    chunks = call(
-        cut_kernel, [sds((1, tok, part), BF16) for part in widths], [dma((parts,))], "cut"
-    )(ring[-1])
-    chunks = [ring_step(chunk, "tensor", n) for chunk in chunks]
 
     terms = len(LEFT_TERMS) * rank
     whole, left_terms, right_terms = call(
@@ -419,25 +433,40 @@
         "factor",
     )(ortho, total, swap(total, "dp", m, 1))
 
+    acts = call(
+        functools.partial(acts_kernel, n),
+        sds((rows, tokens), BF16),
+        [pltpu.VMEM((tokens, rows), BF16)],
+        "acts",
+    )(activations)
+    last, right_terms = after(ys[-1], right_terms)
+    ya, yb = cut(last, [narrow, narrow])
+    pieces = []
+    at = 0
+    for part, base, held, newest in (
+        (wide, 0, xs, xa),
+        (wide, 0, xs, xb),
+        (narrow, 2 * wide, ys, step(ya)),
+        (narrow, 2 * wide, ys, step(yb)),
+    ):
+        slots = ring + held[1 : n - 2] + [newest]
+        bases = [0, 0] + [base] * (n - 3) + [at]
+        pieces.append((at, part, slots, bases))
+        at += part
+
     outs = ()
-    for c, (part, chunk) in enumerate(zip(widths, chunks)):
+    for at, part, slots, bases in pieces:
         outs = pl.pallas_call(
-            functools.partial(final_kernel, n, sum(widths[:c]), part),
+            functools.partial(final_kernel, at, part, bases),
             in_specs=[vmem] * (4 + n) + [pl.BlockSpec(memory_space=pl.ANY)] * len(outs),
             out_specs=[pl.BlockSpec(memory_space=pl.ANY)] * 2,
             out_shape=[sds((rows, width), BF16), sds((1, rows, width), BF16)],
             input_output_aliases={4 + n + j: j for j in range(len(outs))},
-            scratch_shapes=[
-                pltpu.VMEM((tokens, rows), BF16),
-                pltpu.VMEM((rows, tokens), BF16),
-                pltpu.VMEM((rows, part), BF16),
-                pltpu.VMEM((rows, part), BF16),
-                dma((3, 2)),
-            ],
+            scratch_shapes=[pltpu.VMEM((rows, part), BF16)] * 2 + [dma((3, 2))],
             compiler_params=params(16),
             cost_estimate=cost(0),
             name="rebuild",
-        )(activations, left_terms, right_terms, error_v, *ring, chunk, *outs)
+        )(acts, left_terms, right_terms, error_v, *slots, *outs)
     rebuilt, error = outs
     return rebuilt, error, whole.T
 

time: 81.1 us -> 78.4 us (0.967)
  starting transfers between devices: 31 us -> 27.9 us
  Pallas kernels: 18.2 us -> 19.1 us
    ppermute x5 -> x7, waiting for transfers between devices: 9.21 us -> 0.02 us  [ring_step(): lax.ppermute(x, axis, [(ring[p], ring[(p + 1) % n]) for p in range(n)])]
    ppermute x6, waiting for transfers between devices: 4.58 us -> 12.4 us  [exchange(): lax.ppermute(pieces[k], axis, [(i, (i + k) % n) for i in range(n)])]
    ppermute x6, starting transfers between devices: 10.8 us -> 8.18 us  [exchange(): lax.ppermute(pieces[k], axis, [(i, (i + k) % n) for i in range(n)])]
    ppermute x9, starting transfers between devices: 10.8 us -> 8.22 us  [swap(): return lax.ppermute(x, axis, [(i, i ^ bit) for i in range(n)])]
    ppermute x5 -> x7, starting transfers between devices: 9.35 us -> 11.5 us  [ring_step(): lax.ppermute(x, axis, [(ring[p], ring[(p + 1) % n]) for p in range(n)])]
    pallas_call x4 -> x8, Pallas kernels: 9.34 us -> 10.3 us  [the longest x4 9.9 us: per_device(): pl.pallas_call(functools.partial(final_kernel, at, part, bases), in_specs...]
  transfers between devices with their start and end apart: 20 -> 22, of which waited for: 16 -> 11; matrix products, arithmetic and copies ran while one was open for 0% -> 0% of each run, Pallas kernels for 16% -> 20%
where the time goes in v8:
time: 78.4 us; the launch traced here: 78.2 us
  waiting for transfers between devices  30.4 us (39%)
  starting transfers between devices  27.9 us (36%)
  Pallas kernels  19.1 us (24%)
  between operations  0.82 us (1%)
    ppermute x9, waiting for transfers between devices, swap(): return lax.ppermute(x, axis, [(i, i ^ bit) for i in range(n)])  18 us
    ppermute x6, waiting for transfers between devices, exchange(): lax.ppermute(pieces[k], axis, [(i, (i + k) % n) for i in range(n)])  12.4 us
    ppermute x7, starting transfers between devices, ring_step(): lax.ppermute(x, axis, [(ring[p], ring[(p + 1) % n]) for p in range(n)])  11.5 us
    pallas_call x4, Pallas kernels, per_device(): pl.pallas_call(functools.partial(final_kernel, at, part, bases), in_specs...  9.9 us
    ppermute x9, starting transfers between devices, swap(): return lax.ppermute(x, axis, [(i, i ^ bit) for i in range(n)])  8.22 us
    ppermute x6, starting transfers between devices, exchange(): lax.ppermute(pieces[k], axis, [(i, (i + k) % n) for i in range(n)])  8.18 us
    pallas_call x1, Pallas kernels, per_device(): call(error_left_kernel, [sds((rank, rows), F32), sds((1, rows, width), BF...  4.19 us
  transfers between devices with their start and end apart: 22, of which 11 were waited for; matrix products, arithmetic and copies ran while one was open for 0% of the time, Pallas kernels for 20%

profile of v8, /device:TPU:0, one launch (start us, length us, event | category | flops | bytes accessed | tf_op | source)
XLA Modules:
  0.0 78.2 jit_solution(9386566264358778798)
XLA Ops:
  0.6 4.1 %collective-permute-start = (bf16[1,64,5120]{2,1,0:T(8,128)(2,1)}, bf16[1,64,5120]{2,1,0:T(8,128)(2,1)S(1)}, u32[]{:S(2)}, u32[]{:S(2)}) collective-permute-start(bf16[1,64,5120]{2,1,0:T(8,128)(2,1)} %refs_0_.7), channel_id=1, source_target_pairs={{0,2},{2,3},{3,1},{1,0},{4,6},{6,7},{7,5},{5,4},{8,10},{10,11},{11... | collective-permute-start | bytes 1966088 | tf_op jit(solution)/shard_map/ppermute | solution.py:60
  6.3 1.9 %collective-permute-start.2 = (f32[8,128]{1,0:T(8,128)S(1)}, f32[8,128]{1,0:T(8,128)S(1)}, u32[]{:S(2)}, u32[]{:S(2)}) collective-permute-start(f32[8,128]{1,0:T(8,128)S(1)} %get-tuple-element.50.refs_0_), channel_id=1, source_target_pairs={{0,2},{1,3},{2,0},{3,1},{4,6},{5,7},{6,4},{7,5},{8,10},{9,11},{10,... | collective-permute-start | bytes 12296 | tf_op jit(solution)/shard_map/ppermute | solution.py:65
  8.2 2.6 %collective-permute-start.3 = (f32[8,128]{1,0:T(8,128)S(1)}, f32[8,128]{1,0:T(8,128)S(1)}, u32[]{:S(2)}, u32[]{:S(2)}) collective-permute-start(f32[8,128]{1,0:T(8,128)S(1)} %get-tuple-element.50.refs_0_), channel_id=1, source_target_pairs={{0,3},{1,0},{2,1},{3,2},{4,7},{5,4},{6,5},{7,6},{8,11},{9,8},{10,9... | collective-permute-start | bytes 12296 | tf_op jit(solution)/shard_map/ppermute | solution.py:65
  10.8 10.2 %collective-permute-done.1.refs_1_ = f32[8,128]{1,0:T(8,128)S(1)} collective-permute-done((f32[8,128]{1,0:T(8,128)S(1)}, f32[8,128]{1,0:T(8,128)S(1)}, u32[]{:S(2)}, u32[]{:S(2)}) %collective-permute-start.1) | collective-permute-done | bytes 4128 | tf_op jit(solution)/shard_map/ppermute | solution.py:65
  21.1 1.6 %collective-permute-start.6 = (bf16[1,64,3072]{2,1,0:T(8,128)(2,1)S(1)}, bf16[1,64,3072]{2,1,0:T(8,128)(2,1)S(1)}, u32[]{:S(2)}, u32[]{:S(2)}) collective-permute-start(bf16[1,64,3072]{2,1,0:T(8,128)(2,1)S(1)} %get-tuple-element.55), channel_id=1, source_target_pairs={{0,2},{2,3},{3,1},{1,0},{4,6},{6,7},{7,5},{5,4},{8,10},{10,11},{11... | collective-permute-start | bytes 1179656 | tf_op jit(solution)/shard_map/ppermute | solution.py:60
  22.7 4.2 %error_left.1 = (f32[4,768]{1,0:T(4,128)S(1)}, bf16[1,768,5120]{2,1,0:T(8,128)(2,1)S(1)}) custom-call(bf16[12,5120]{1,0:T(8,128)(2,1)S(1)} %get-tuple-element.47.terms_ref, bf16[1,768,5120]{2,1,0:T(8,128)(2,1)} %e_hbm.1), custom_call_target="tpu_custom_call" | custom-call | flops 4600000000 | bytes 1 | tf_op jit(solution)/shard_map/error_left/pallas_call | solution.py:363
  28.4 1.5 %collective-permute-start.5 = (f32[4,768]{1,0:T(4,128)S(1)}, f32[4,768]{1,0:T(4,128)S(1)}, u32[]{:S(2)}, u32[]{:S(2)}) collective-permute-start(f32[4,768]{1,0:T(4,128)S(1)} %add.7.x_ref), channel_id=1, source_target_pairs={{0,8},{4,12},{8,0},{12,4},{16,24},{20,28},{24,16},{28,20},{1,9},{5... | collective-permute-start | bytes 36872 | tf_op jit(solution)/shard_map/ppermute | solution.py:70
  29.9 2.2 %collective-permute-done.5.y_ref = f32[4,768]{1,0:T(4,128)S(1)} collective-permute-done((f32[4,768]{1,0:T(4,128)S(1)}, f32[4,768]{1,0:T(4,128)S(1)}, u32[]{:S(2)}, u32[]{:S(2)}) %collective-permute-start.5) | collective-permute-done | bytes 12320 | tf_op jit(solution)/shard_map/ppermute | solution.py:70
  32.1 1.5 %collective-permute-start.7 = (f32[4,768]{1,0:T(4,128)S(1)}, f32[4,768]{1,0:T(4,128)S(1)}, u32[]{:S(2)}, u32[]{:S(2)}) collective-permute-start(f32[4,768]{1,0:T(4,128)S(1)} %add.8.x_ref), channel_id=1, source_target_pairs={{0,16},{4,20},{8,24},{12,28},{16,0},{20,4},{24,8},{28,12},{1,17},{... | collective-permute-start | bytes 36872 | tf_op jit(solution)/shard_map/ppermute | solution.py:70
  33.6 2.2 %collective-permute-done.7.y_ref = f32[4,768]{1,0:T(4,128)S(1)} collective-permute-done((f32[4,768]{1,0:T(4,128)S(1)}, f32[4,768]{1,0:T(4,128)S(1)}, u32[]{:S(2)}, u32[]{:S(2)}) %collective-permute-start.7) | collective-permute-done | bytes 12320 | tf_op jit(solution)/shard_map/ppermute | solution.py:70
  36.1 1.5 %collective-permute-start.10 = (f32[8,128]{1,0:T(8,128)S(1)}, f32[8,128]{1,0:T(8,128)S(1)}, u32[]{:S(2)}, u32[]{:S(2)}) collective-permute-start(f32[8,128]{1,0:T(8,128)S(1)} %get-tuple-element.62), channel_id=1, source_target_pairs={{0,3},{1,0},{2,1},{3,2},{4,7},{5,4},{6,5},{7,6},{8,11},{9,8},{10,9... | collective-permute-start | bytes 12296 | tf_op jit(solution)/shard_map/ppermute | solution.py:65
  38.2 1.6 %collective-permute-start.9 = (f32[8,128]{1,0:T(8,128)S(1)}, f32[8,128]{1,0:T(8,128)S(1)}, u32[]{:S(2)}, u32[]{:S(2)}) collective-permute-start(f32[8,128]{1,0:T(8,128)S(1)} %get-tuple-element.61), channel_id=1, source_target_pairs={{0,2},{1,3},{2,0},{3,1},{4,6},{5,7},{6,4},{7,5},{8,10},{9,11},{10,... | collective-permute-start | bytes 12296 | tf_op jit(solution)/shard_map/ppermute | solution.py:65
  40.9 2.1 %collective-permute-done.8.refs_1_ = f32[8,128]{1,0:T(8,128)S(1)} collective-permute-done((f32[8,128]{1,0:T(8,128)S(1)}, f32[8,128]{1,0:T(8,128)S(1)}, u32[]{:S(2)}, u32[]{:S(2)}) %collective-permute-start.8) | collective-permute-done | bytes 4128 | tf_op jit(solution)/shard_map/ppermute | solution.py:65
  45.7 3.4 %collective-permute-done.12.y_ref = f32[4,2560]{1,0:T(4,128)S(1)} collective-permute-done((f32[4,2560]{1,0:T(4,128)S(1)}, f32[4,2560]{1,0:T(4,128)S(1)}, u32[]{:S(2)}, u32[]{:S(2)}) %collective-permute-start.12) | collective-permute-done | bytes 40992 | tf_op jit(solution)/shard_map/ppermute | solution.py:70
  50.7 3.8 %collective-permute-done.13.y_ref = f32[4,2560]{1,0:T(4,128)S(1)} collective-permute-done((f32[4,2560]{1,0:T(4,128)S(1)}, f32[4,2560]{1,0:T(4,128)S(1)}, u32[]{:S(2)}, u32[]{:S(2)}) %collective-permute-start.13) | collective-permute-done | bytes 40992 | tf_op jit(solution)/shard_map/ppermute | solution.py:70
  55.5 1.5 %collective-permute-start.14 = (f32[4,2560]{1,0:T(4,128)S(1)}, f32[4,2560]{1,0:T(4,128)S(1)}, u32[]{:S(2)}, u32[]{:S(2)}) collective-permute-start(f32[4,2560]{1,0:T(4,128)S(1)} %add.11.x_ref), channel_id=1, source_target_pairs={{0,8},{4,12},{8,0},{12,4},{16,24},{20,28},{24,16},{28,20},{1,9},{5... | collective-permute-start | bytes 122888 | tf_op jit(solution)/shard_map/ppermute | solution.py:70
  57.0 2.5 %collective-permute-done.14.y_ref = f32[4,2560]{1,0:T(4,128)S(1)} collective-permute-done((f32[4,2560]{1,0:T(4,128)S(1)}, f32[4,2560]{1,0:T(4,128)S(1)}, u32[]{:S(2)}, u32[]{:S(2)}) %collective-permute-start.14) | collective-permute-done | bytes 40992 | tf_op jit(solution)/shard_map/ppermute | solution.py:70
  59.5 1.5 %collective-permute-start.15 = (f32[4,2560]{1,0:T(4,128)S(1)}, f32[4,2560]{1,0:T(4,128)S(1)}, u32[]{:S(2)}, u32[]{:S(2)}) collective-permute-start(f32[4,2560]{1,0:T(4,128)S(1)} %add.12.x_ref), channel_id=1, source_target_pairs={{0,16},{4,20},{8,24},{12,28},{16,0},{20,4},{24,8},{28,12},{1,17},{... | collective-permute-start | bytes 122888 | tf_op jit(solution)/shard_map/ppermute | solution.py:70
  61.0 2.0 %collective-permute-start.21 = (bf16[1,64,1536]{2,1,0:T(8,128)(2,1)S(1)}, bf16[1,64,1536]{2,1,0:T(8,128)(2,1)S(1)}, u32[]{:S(2)}, u32[]{:S(2)}) collective-permute-start(bf16[1,64,1536]{2,1,0:T(8,128)(2,1)S(1)} %get-tuple-element.81), channel_id=1, source_target_pairs={{0,2},{2,3},{3,1},{1,0},{4,6},{6,7},{7,5},{5,4},{8,10},{10,11},{11... | collective-permute-start | bytes 589832 | tf_op jit(solution)/shard_map/ppermute | solution.py:60
  65.5 2.1 %collective-permute-start.19 = (bf16[1,64,1024]{2,1,0:T(8,128)(2,1)S(1)}, bf16[1,64,1024]{2,1,0:T(8,128)(2,1)S(1)}, u32[]{:S(2)}, u32[]{:S(2)}) collective-permute-start(bf16[1,64,1024]{2,1,0:T(8,128)(2,1)S(1)} %get-tuple-element.79), channel_id=1, source_target_pairs={{0,2},{2,3},{3,1},{1,0},{4,6},{6,7},{7,5},{5,4},{8,10},{10,11},{11... | collective-permute-start | bytes 393224 | tf_op jit(solution)/shard_map/ppermute | solution.py:60
  68.3 2.8 %rebuild.4 = (bf16[768,5120]{1,0:T(8,128)(2,1)}, bf16[1,768,5120]{2,1,0:T(8,128)(2,1)}) custom-call(bf16[768,256]{1,0:T(8,128)(2,1)S(1)} %acts.1.acts_ref, bf16[768,24]{1,0:T(8,128)(2,1)S(1)} %get-tuple-element.73.left_ref, bf16[24,5120]{1,0:T(8,128)(2,1)S(1)} %get-tuple-element.76.right_ref, bf16[1,768,5120]{2,1,0:T(8,128)(2,1)S(1)} %get-tuple-element.58.e_ref, ...), custom_call_target="tpu_custom_call" | custom-call | flops 1 | bytes 1 | tf_op jit(solution)/shard_map/rebuild/pallas_call | solution.py:459
  71.1 2.8 %rebuild.5 = (bf16[768,5120]{1,0:T(8,128)(2,1)}, bf16[1,768,5120]{2,1,0:T(8,128)(2,1)}) custom-call(bf16[768,256]{1,0:T(8,128)(2,1)S(1)} %acts.1.acts_ref, bf16[768,24]{1,0:T(8,128)(2,1)S(1)} %get-tuple-element.73.left_ref, bf16[24,5120]{1,0:T(8,128)(2,1)S(1)} %get-tuple-element.76.right_ref, ...), custom_call_target="tpu_custom_call", output_to_operand_aliasing={{0}: (8, {}), {1}: (9, {})} | custom-call | flops 1 | bytes 1 | tf_op jit(solution)/shard_map/rebuild/pallas_call | solution.py:459
  73.9 2.1 %rebuild.6 = (bf16[768,5120]{1,0:T(8,128)(2,1)}, bf16[1,768,5120]{2,1,0:T(8,128)(2,1)}) custom-call(bf16[768,256]{1,0:T(8,128)(2,1)S(1)} %acts.1.acts_ref, bf16[768,24]{1,0:T(8,128)(2,1)S(1)} %get-tuple-element.73.left_ref, bf16[24,5120]{1,0:T(8,128)(2,1)S(1)} %get-tuple-element.76.right_ref, ...), custom_call_target="tpu_custom_call", output_to_operand_aliasing={{0}: (8, {}), {1}: (9, {})} | custom-call | flops 1 | bytes 1 | tf_op jit(solution)/shard_map/rebuild/pallas_call | solution.py:459
  76.1 2.2 %rebuild.7 = (bf16[768,5120]{1,0:T(8,128)(2,1)}, bf16[1,768,5120]{2,1,0:T(8,128)(2,1)}) custom-call(bf16[768,256]{1,0:T(8,128)(2,1)S(1)} %acts.1.acts_ref, bf16[768,24]{1,0:T(8,128)(2,1)S(1)} %get-tuple-element.73.left_ref, bf16[24,5120]{1,0:T(8,128)(2,1)S(1)} %get-tuple-element.76.right_ref, ...), custom_call_target="tpu_custom_call", output_to_operand_aliasing={{0}: (8, {}), {1}: (9, {})} | custom-call | flops 1 | bytes 1 | tf_op jit(solution)/shard_map/rebuild/pallas_call | solution.py:459
  (46 shorter events, 13.5 us)
Async XLA Ops:
  0.6 20.4 %collective-permute-start = (bf16[1,64,5120]{2,1,0:T(8,128)(2,1)}, bf16[1,64,5120]{2,1,0:T(8,128)(2,1)S(1)}, u32[]{:S(2)}, u32[]{:S(2)}) collective-permute-start(bf16[1,64,5120]{2,1,0:T(8,128)(2,1)} %refs_0_.7), channel_id=1, source_target_pairs={{0,2},{2,3},{3,1},{1,0},{4,6},{6,7},{7,5},{5,4},{8,10},{10,11},{11... | collective-permute-start | bytes 1966088 | tf_op jit(solution)/shard_map/ppermute | solution.py:60
  6.2 14.8 %collective-permute-start.1 = (f32[8,128]{1,0:T(8,128)S(1)}, f32[8,128]{1,0:T(8,128)S(1)}, u32[]{:S(2)}, u32[]{:S(2)}) collective-permute-start(f32[8,128]{1,0:T(8,128)S(1)} %get-tuple-element.50.refs_0_), channel_id=1, source_target_pairs={{0,1},{1,2},{2,3},{3,0},{4,5},{5,6},{6,7},{7,4},{8,9},{9,10},{10,1... | collective-permute-start | bytes 12296 | tf_op jit(solution)/shard_map/ppermute | solution.py:65
  6.3 14.7 %collective-permute-start.2 = (f32[8,128]{1,0:T(8,128)S(1)}, f32[8,128]{1,0:T(8,128)S(1)}, u32[]{:S(2)}, u32[]{:S(2)}) collective-permute-start(f32[8,128]{1,0:T(8,128)S(1)} %get-tuple-element.50.refs_0_), channel_id=1, source_target_pairs={{0,2},{1,3},{2,0},{3,1},{4,6},{5,7},{6,4},{7,5},{8,10},{9,11},{10,... | collective-permute-start | bytes 12296 | tf_op jit(solution)/shard_map/ppermute | solution.py:65
  8.2 12.8 %collective-permute-start.3 = (f32[8,128]{1,0:T(8,128)S(1)}, f32[8,128]{1,0:T(8,128)S(1)}, u32[]{:S(2)}, u32[]{:S(2)}) collective-permute-start(f32[8,128]{1,0:T(8,128)S(1)} %get-tuple-element.50.refs_0_), channel_id=1, source_target_pairs={{0,3},{1,0},{2,1},{3,2},{4,7},{5,4},{6,5},{7,6},{8,11},{9,8},{10,9... | collective-permute-start | bytes 12296 | tf_op jit(solution)/shard_map/ppermute | solution.py:65
  21.1 14.7 %collective-permute-start.6 = (bf16[1,64,3072]{2,1,0:T(8,128)(2,1)S(1)}, bf16[1,64,3072]{2,1,0:T(8,128)(2,1)S(1)}, u32[]{:S(2)}, u32[]{:S(2)}) collective-permute-start(bf16[1,64,3072]{2,1,0:T(8,128)(2,1)S(1)} %get-tuple-element.55), channel_id=1, source_target_pairs={{0,2},{2,3},{3,1},{1,0},{4,6},{6,7},{7,5},{5,4},{8,10},{10,11},{11... | collective-permute-start | bytes 1179656 | tf_op jit(solution)/shard_map/ppermute | solution.py:60
  22.7 4.2 %copy-start.1 = (bf16[1,256,768]{2,1,0:T(8,128)(2,1)S(1)}, bf16[1,256,768]{2,1,0:T(8,128)(2,1)}, u32[]{:S(2)}) copy-start(bf16[1,256,768]{2,1,0:T(8,128)(2,1)} %a_ref.5) | copy-start | bytes 1179652
  26.9 16.1 %copy-start = (bf16[1,64,5120]{2,1,0:T(8,128)(2,1)S(1)}, bf16[1,64,5120]{2,1,0:T(8,128)(2,1)}, u32[]{:S(2)}) copy-start(bf16[1,64,5120]{2,1,0:T(8,128)(2,1)} %refs_0_.7) | copy-start | bytes 1966084
  27.1 1.2 %collective-permute-start.4 = (f32[4,768]{1,0:T(4,128)S(1)}, f32[4,768]{1,0:T(4,128)S(1)}, u32[]{:S(2)}, u32[]{:S(2)}) collective-permute-start(f32[4,768]{1,0:T(4,128)S(1)} %left.1.x_ref), channel_id=1, source_target_pairs={{0,4},{4,0},{8,12},{12,8},{16,20},{20,16},{24,28},{28,24},{1,5},{5... | collective-permute-start | bytes 36872 | tf_op jit(solution)/shard_map/ppermute | solution.py:70
  28.4 3.7 %collective-permute-start.5 = (f32[4,768]{1,0:T(4,128)S(1)}, f32[4,768]{1,0:T(4,128)S(1)}, u32[]{:S(2)}, u32[]{:S(2)}) collective-permute-start(f32[4,768]{1,0:T(4,128)S(1)} %add.7.x_ref), channel_id=1, source_target_pairs={{0,8},{4,12},{8,0},{12,4},{16,24},{20,28},{24,16},{28,20},{1,9},{5... | collective-permute-start | bytes 36872 | tf_op jit(solution)/shard_map/ppermute | solution.py:70
  32.1 3.7 %collective-permute-start.7 = (f32[4,768]{1,0:T(4,128)S(1)}, f32[4,768]{1,0:T(4,128)S(1)}, u32[]{:S(2)}, u32[]{:S(2)}) collective-permute-start(f32[4,768]{1,0:T(4,128)S(1)} %add.8.x_ref), channel_id=1, source_target_pairs={{0,16},{4,20},{8,24},{12,28},{16,0},{20,4},{24,8},{28,12},{1,17},{... | collective-permute-start | bytes 36872 | tf_op jit(solution)/shard_map/ppermute | solution.py:70
  36.1 4.8 %collective-permute-start.10 = (f32[8,128]{1,0:T(8,128)S(1)}, f32[8,128]{1,0:T(8,128)S(1)}, u32[]{:S(2)}, u32[]{:S(2)}) collective-permute-start(f32[8,128]{1,0:T(8,128)S(1)} %get-tuple-element.62), channel_id=1, source_target_pairs={{0,3},{1,0},{2,1},{3,2},{4,7},{5,4},{6,5},{7,6},{8,11},{9,8},{10,9... | collective-permute-start | bytes 12296 | tf_op jit(solution)/shard_map/ppermute | solution.py:65
  37.6 5.4 %collective-permute-start.8 = (f32[8,128]{1,0:T(8,128)S(1)}, f32[8,128]{1,0:T(8,128)S(1)}, u32[]{:S(2)}, u32[]{:S(2)}) collective-permute-start(f32[8,128]{1,0:T(8,128)S(1)} %get-tuple-element.60), channel_id=1, source_target_pairs={{0,1},{1,2},{2,3},{3,0},{4,5},{5,6},{6,7},{7,4},{8,9},{9,10},{10,1... | collective-permute-start | bytes 12296 | tf_op jit(solution)/shard_map/ppermute | solution.py:65
  38.2 4.8 %collective-permute-start.9 = (f32[8,128]{1,0:T(8,128)S(1)}, f32[8,128]{1,0:T(8,128)S(1)}, u32[]{:S(2)}, u32[]{:S(2)}) collective-permute-start(f32[8,128]{1,0:T(8,128)S(1)} %get-tuple-element.61), channel_id=1, source_target_pairs={{0,2},{1,3},{2,0},{3,1},{4,6},{5,7},{6,4},{7,5},{8,10},{9,11},{10,... | collective-permute-start | bytes 12296 | tf_op jit(solution)/shard_map/ppermute | solution.py:65
  43.8 1.3 %collective-permute-start.11 = (f32[4,2560]{1,0:T(4,128)S(1)}, f32[4,2560]{1,0:T(4,128)S(1)}, u32[]{:S(2)}, u32[]{:S(2)}) collective-permute-start(f32[4,2560]{1,0:T(4,128)S(1)} %get-tuple-element.69), channel_id=1, source_target_pairs={{0,4},{4,0},{8,12},{12,8},{16,20},{20,16},{24,28},{28,24},{1,5},{5... | collective-permute-start | bytes 122888 | tf_op jit(solution)/shard_map/ppermute | solution.py:70
  45.1 4.0 %collective-permute-start.12 = (f32[4,2560]{1,0:T(4,128)S(1)}, f32[4,2560]{1,0:T(4,128)S(1)}, u32[]{:S(2)}, u32[]{:S(2)}) collective-permute-start(f32[4,2560]{1,0:T(4,128)S(1)} %add.9.x_ref), channel_id=1, source_target_pairs={{0,1},{1,0},{2,3},{3,2},{4,5},{5,4},{6,7},{7,6},{8,9},{9,8},{10,11... | collective-permute-start | bytes 122888 | tf_op jit(solution)/shard_map/ppermute | solution.py:70
  49.1 5.3 %collective-permute-start.13 = (f32[4,2560]{1,0:T(4,128)S(1)}, f32[4,2560]{1,0:T(4,128)S(1)}, u32[]{:S(2)}, u32[]{:S(2)}) collective-permute-start(f32[4,2560]{1,0:T(4,128)S(1)} %add.10.x_ref), channel_id=1, source_target_pairs={{0,2},{1,3},{2,0},{3,1},{4,6},{5,7},{6,4},{7,5},{8,10},{9,11},{10,... | collective-permute-start | bytes 122888 | tf_op jit(solution)/shard_map/ppermute | solution.py:70
  54.5 11.0 %collective-permute-start.17 = (bf16[1,64,2048]{2,1,0:T(8,128)(2,1)S(1)}, bf16[1,64,2048]{2,1,0:T(8,128)(2,1)S(1)}, u32[]{:S(2)}, u32[]{:S(2)}) collective-permute-start(bf16[1,64,2048]{2,1,0:T(8,128)(2,1)S(1)} %get-tuple-element.74), channel_id=1, source_target_pairs={{0,2},{2,3},{3,1},{1,0},{4,6},{6,7},{7,5},{5,4},{8,10},{10,11},{11... | collective-permute-start | bytes 786440 | tf_op jit(solution)/shard_map/ppermute | solution.py:60
  55.5 4.0 %collective-permute-start.14 = (f32[4,2560]{1,0:T(4,128)S(1)}, f32[4,2560]{1,0:T(4,128)S(1)}, u32[]{:S(2)}, u32[]{:S(2)}) collective-permute-start(f32[4,2560]{1,0:T(4,128)S(1)} %add.11.x_ref), channel_id=1, source_target_pairs={{0,8},{4,12},{8,0},{12,4},{16,24},{20,28},{24,16},{28,20},{1,9},{5... | collective-permute-start | bytes 122888 | tf_op jit(solution)/shard_map/ppermute | solution.py:70
  59.5 4.0 %collective-permute-start.15 = (f32[4,2560]{1,0:T(4,128)S(1)}, f32[4,2560]{1,0:T(4,128)S(1)}, u32[]{:S(2)}, u32[]{:S(2)}) collective-permute-start(f32[4,2560]{1,0:T(4,128)S(1)} %add.12.x_ref), channel_id=1, source_target_pairs={{0,16},{4,20},{8,24},{12,28},{16,0},{20,4},{24,8},{28,12},{1,17},{... | collective-permute-start | bytes 122888 | tf_op jit(solution)/shard_map/ppermute | solution.py:70
  61.0 7.2 %collective-permute-start.21 = (bf16[1,64,1536]{2,1,0:T(8,128)(2,1)S(1)}, bf16[1,64,1536]{2,1,0:T(8,128)(2,1)S(1)}, u32[]{:S(2)}, u32[]{:S(2)}) collective-permute-start(bf16[1,64,1536]{2,1,0:T(8,128)(2,1)S(1)} %get-tuple-element.81), channel_id=1, source_target_pairs={{0,2},{2,3},{3,1},{1,0},{4,6},{6,7},{7,5},{5,4},{8,10},{10,11},{11... | collective-permute-start | bytes 589832 | tf_op jit(solution)/shard_map/ppermute | solution.py:60
  63.1 8.0 %collective-permute-start.20 = (bf16[1,64,1536]{2,1,0:T(8,128)(2,1)S(1)}, bf16[1,64,1536]{2,1,0:T(8,128)(2,1)S(1)}, u32[]{:S(2)}, u32[]{:S(2)}) collective-permute-start(bf16[1,64,1536]{2,1,0:T(8,128)(2,1)S(1)} %get-tuple-element.80), channel_id=1, source_target_pairs={{0,2},{2,3},{3,1},{1,0},{4,6},{6,7},{7,5},{5,4},{8,10},{10,11},{11... | collective-permute-start | bytes 589832 | tf_op jit(solution)/shard_map/ppermute | solution.py:60
  63.5 1.2 %collective-permute-start.16 = (f32[4,2560]{1,0:T(4,128)S(1)}, f32[4,2560]{1,0:T(4,128)S(1)}, u32[]{:S(2)}, u32[]{:S(2)}) collective-permute-start(f32[4,2560]{1,0:T(4,128)S(1)} %add.13.mine_ref), channel_id=1, source_target_pairs={{0,4},{4,0},{8,12},{12,8},{16,20},{20,16},{24,28},{28,24},{1,5},{5... | collective-permute-start | bytes 122888 | tf_op jit(solution)/shard_map/ppermute | solution.py:70
  65.5 8.4 %collective-permute-start.19 = (bf16[1,64,1024]{2,1,0:T(8,128)(2,1)S(1)}, bf16[1,64,1024]{2,1,0:T(8,128)(2,1)S(1)}, u32[]{:S(2)}, u32[]{:S(2)}) collective-permute-start(bf16[1,64,1024]{2,1,0:T(8,128)(2,1)S(1)} %get-tuple-element.79), channel_id=1, source_target_pairs={{0,2},{2,3},{3,1},{1,0},{4,6},{6,7},{7,5},{5,4},{8,10},{10,11},{11... | collective-permute-start | bytes 393224 | tf_op jit(solution)/shard_map/ppermute | solution.py:60
  67.6 8.5 %collective-permute-start.18 = (bf16[1,64,1024]{2,1,0:T(8,128)(2,1)S(1)}, bf16[1,64,1024]{2,1,0:T(8,128)(2,1)S(1)}, u32[]{:S(2)}, u32[]{:S(2)}) collective-permute-start(bf16[1,64,1024]{2,1,0:T(8,128)(2,1)S(1)} %get-tuple-element.78), channel_id=1, source_target_pairs={{0,2},{2,3},{3,1},{1,0},{4,6},{6,7},{7,5},{5,4},{8,10},{10,11},{11... | collective-permute-start | bytes 393224 | tf_op jit(solution)/shard_map/ppermute | solution.py:60

commit v9 on v8

--- a/solution.py
+++ b/solution.py
@@ -358,8 +358,6 @@
         ],
         "token_factor", [hbm, hbm],
     )(pin(w), pin(out_grads))
-    gws = exchange([gw] * n, "tensor", n)
-
     ew, error_v = call(
         error_left_kernel,
         [sds((rank, rows), F32), sds((1, rows, width), BF16)],
@@ -367,6 +365,8 @@
         "error_left", [vmem, hbm], 4.6e9,
     )(w_terms, pin(error_buffer))
 
+    gw, ew = after(gw, ew)
+    gws = exchange([gw] * n, "tensor", n)
     ring[1], gws = after(ring[1], gws)
     x1, y1 = cut(ring[1], [2 * wide, 2 * narrow])
     xs, ys = [x1, step(x1)], [y1]
@@ -404,22 +404,20 @@
         "right",
     )(mean, right_raw, out_grads, *msgs)
     total = add(keep, swap(send, "dp", m, 1))
-    for bit in bits(n):
-        total = add(total, swap(total, "tensor", n, bit))
+    for _ in range(3, n):
+        last, total = after(ys[-1], total)
+        ys.append(step(last))
     for _ in range(4, n):
         last, total = after(xs[-1], total)
         xs.append(step(last))
+    for bit in bits(m)[1:]:
+        total = add(total, swap(total, "dp", m, bit))
+    (xs[-1], ys[-1]), total = after((xs[-1], ys[-1]), total)
+    for bit in bits(n):
+        total = add(total, swap(total, "tensor", n, bit))
     xa, xb = cut(xs[-1], [wide, wide])
-    xa, total = after(xa, total)
-    xa = step(xa)
-    for _ in range(3, n):
-        last, total = after(ys[-1], total)
-        ys.append(step(last))
-    total = add(total, swap(total, "dp", m, 2))
-    xb, total = after(xb, total)
-    xb = step(xb)
-    for bit in bits(m)[2:]:
-        total = add(total, swap(total, "dp", m, bit))
+    (xa, xb), total = after((xa, xb), total)
+    xa, xb = step(xa), step(xb)
 
     terms = len(LEFT_TERMS) * rank
     whole, left_terms, right_terms = call(

time: 78.4 us -> 78.1 us (level)
  waiting for transfers between devices: 30.4 us -> 27.5 us
  starting transfers between devices: 27.9 us -> 30.5 us
    ppermute x9, starting transfers between devices: 8.22 us -> 11.2 us  [swap(): return lax.ppermute(x, axis, [(i, i ^ bit) for i in range(n)])]
    ppermute x6, waiting for transfers between devices: 12.4 us -> 9.54 us  [exchange(): lax.ppermute(pieces[k], axis, [(i, (i + k) % n) for i in range(n)])]
    ppermute x9, waiting for transfers between devices: 18 us -> 17.1 us  [swap(): return lax.ppermute(x, axis, [(i, i ^ bit) for i in range(n)])]
    ppermute x7, waiting for transfers between devices: 0.02 us -> 0.83 us  [ring_step(): lax.ppermute(x, axis, [(ring[p], ring[(p + 1) % n]) for p in range(n)])]
  transfers between devices with their start and end apart: 22 -> 22, of which waited for: 11 -> 13; matrix products, arithmetic and copies ran while one was open for 0% -> 0% of each run, Pallas kernels for 20% -> 20%
where the time goes in v9:
time: 78.1 us; the launch traced here: 78 us
  starting transfers between devices  30.5 us (39%)
  waiting for transfers between devices  27.5 us (35%)
  Pallas kernels  19.1 us (24%)
  between operations  0.82 us (1%)
    ppermute x9, waiting for transfers between devices, swap(): return lax.ppermute(x, axis, [(i, i ^ bit) for i in range(n)])  17.1 us
    ppermute x9, starting transfers between devices, swap(): return lax.ppermute(x, axis, [(i, i ^ bit) for i in range(n)])  11.2 us
    ppermute x7, starting transfers between devices, ring_step(): lax.ppermute(x, axis, [(ring[p], ring[(p + 1) % n]) for p in range(n)])  10.7 us
    pallas_call x4, Pallas kernels, per_device(): pl.pallas_call(functools.partial(final_kernel, at, part, bases), in_specs...  9.9 us
    ppermute x6, waiting for transfers between devices, exchange(): lax.ppermute(pieces[k], axis, [(i, (i + k) % n) for i in range(n)])  9.54 us
    ppermute x6, starting transfers between devices, exchange(): lax.ppermute(pieces[k], axis, [(i, (i + k) % n) for i in range(n)])  8.61 us
    pallas_call x1, Pallas kernels, per_device(): call(error_left_kernel, [sds((rank, rows), F32), sds((1, rows, width), BF...  4.19 us
  transfers between devices with their start and end apart: 22, of which 13 were waited for; matrix products, arithmetic and copies ran while one was open for 0% of the time, Pallas kernels for 20%

profile of v9, /device:TPU:0, one launch (start us, length us, event | category | flops | bytes accessed | tf_op | source)
XLA Modules:
  0.0 78.0 jit_solution(16530046737736587632)
XLA Ops:
  0.6 4.1 %collective-permute-start = (bf16[1,64,5120]{2,1,0:T(8,128)(2,1)}, bf16[1,64,5120]{2,1,0:T(8,128)(2,1)S(1)}, u32[]{:S(2)}, u32[]{:S(2)}) collective-permute-start(bf16[1,64,5120]{2,1,0:T(8,128)(2,1)} %refs_0_.7), channel_id=1, source_target_pairs={{0,2},{2,3},{3,1},{1,0},{4,6},{6,7},{7,5},{5,4},{8,10},{10,11},{11... | collective-permute-start | bytes 1966088 | tf_op jit(solution)/shard_map/ppermute | solution.py:60
  6.2 4.2 %error_left.1 = (f32[4,768]{1,0:T(4,128)S(1)}, bf16[1,768,5120]{2,1,0:T(8,128)(2,1)S(1)}) custom-call(bf16[12,5120]{1,0:T(8,128)(2,1)S(1)} %get-tuple-element.52.terms_ref, bf16[1,768,5120]{2,1,0:T(8,128)(2,1)} %e_hbm.1), custom_call_target="tpu_custom_call" | custom-call | flops 4600000000 | bytes 1 | tf_op jit(solution)/shard_map/error_left/pallas_call | solution.py:361
  10.5 1.9 %collective-permute-start.2 = (f32[8,128]{1,0:T(8,128)S(1)}, f32[8,128]{1,0:T(8,128)S(1)}, u32[]{:S(2)}, u32[]{:S(2)}) collective-permute-start(f32[8,128]{1,0:T(8,128)S(1)} %get-tuple-element.56.refs_0_), channel_id=1, source_target_pairs={{0,2},{1,3},{2,0},{3,1},{4,6},{5,7},{6,4},{7,5},{8,10},{9,11},{10,... | collective-permute-start | bytes 12296 | tf_op jit(solution)/shard_map/ppermute | solution.py:65
  12.4 2.6 %collective-permute-start.3 = (f32[8,128]{1,0:T(8,128)S(1)}, f32[8,128]{1,0:T(8,128)S(1)}, u32[]{:S(2)}, u32[]{:S(2)}) collective-permute-start(f32[8,128]{1,0:T(8,128)S(1)} %get-tuple-element.56.refs_0_), channel_id=1, source_target_pairs={{0,3},{1,0},{2,1},{3,2},{4,7},{5,4},{6,5},{7,6},{8,11},{9,8},{10,9... | collective-permute-start | bytes 12296 | tf_op jit(solution)/shard_map/ppermute | solution.py:65
  15.0 6.0 %collective-permute-done.1.refs_1_ = f32[8,128]{1,0:T(8,128)S(1)} collective-permute-done((f32[8,128]{1,0:T(8,128)S(1)}, f32[8,128]{1,0:T(8,128)S(1)}, u32[]{:S(2)}, u32[]{:S(2)}) %collective-permute-start.1) | collective-permute-done | bytes 4128 | tf_op jit(solution)/shard_map/ppermute | solution.py:65
  21.1 1.6 %collective-permute-start.6 = (bf16[1,64,3072]{2,1,0:T(8,128)(2,1)S(1)}, bf16[1,64,3072]{2,1,0:T(8,128)(2,1)S(1)}, u32[]{:S(2)}, u32[]{:S(2)}) collective-permute-start(bf16[1,64,3072]{2,1,0:T(8,128)(2,1)S(1)} %get-tuple-element.61), channel_id=1, source_target_pairs={{0,2},{2,3},{3,1},{1,0},{4,6},{6,7},{7,5},{5,4},{8,10},{10,11},{11... | collective-permute-start | bytes 1179656 | tf_op jit(solution)/shard_map/ppermute | solution.py:60
  25.6 2.2 %collective-permute-done.5.y_ref = f32[4,768]{1,0:T(4,128)S(1)} collective-permute-done((f32[4,768]{1,0:T(4,128)S(1)}, f32[4,768]{1,0:T(4,128)S(1)}, u32[]{:S(2)}, u32[]{:S(2)}) %collective-permute-start.5) | collective-permute-done | bytes 12320 | tf_op jit(solution)/shard_map/ppermute | solution.py:70
  27.9 1.5 %collective-permute-start.7 = (f32[4,768]{1,0:T(4,128)S(1)}, f32[4,768]{1,0:T(4,128)S(1)}, u32[]{:S(2)}, u32[]{:S(2)}) collective-permute-start(f32[4,768]{1,0:T(4,128)S(1)} %add.8.x_ref), channel_id=1, source_target_pairs={{0,16},{4,20},{8,24},{12,28},{16,0},{20,4},{24,8},{28,12},{1,17},{... | collective-permute-start | bytes 36872 | tf_op jit(solution)/shard_map/ppermute | solution.py:70
  29.4 2.2 %collective-permute-done.7.y_ref = f32[4,768]{1,0:T(4,128)S(1)} collective-permute-done((f32[4,768]{1,0:T(4,128)S(1)}, f32[4,768]{1,0:T(4,128)S(1)}, u32[]{:S(2)}, u32[]{:S(2)}) %collective-permute-start.7) | collective-permute-done | bytes 12320 | tf_op jit(solution)/shard_map/ppermute | solution.py:70
  31.9 3.3 %collective-permute-start.10 = (f32[8,128]{1,0:T(8,128)S(1)}, f32[8,128]{1,0:T(8,128)S(1)}, u32[]{:S(2)}, u32[]{:S(2)}) collective-permute-start(f32[8,128]{1,0:T(8,128)S(1)} %get-tuple-element.68), channel_id=1, source_target_pairs={{0,3},{1,0},{2,1},{3,2},{4,7},{5,4},{6,5},{7,6},{8,11},{9,8},{10,9... | collective-permute-start | bytes 12296 | tf_op jit(solution)/shard_map/ppermute | solution.py:65
  37.1 3.5 %collective-permute-done.8.refs_1_ = f32[8,128]{1,0:T(8,128)S(1)} collective-permute-done((f32[8,128]{1,0:T(8,128)S(1)}, f32[8,128]{1,0:T(8,128)S(1)}, u32[]{:S(2)}, u32[]{:S(2)}) %collective-permute-start.8) | collective-permute-done | bytes 4128 | tf_op jit(solution)/shard_map/ppermute | solution.py:65
  42.7 1.6 %collective-permute-start.13 = (f32[4,2560]{1,0:T(4,128)S(1)}, f32[4,2560]{1,0:T(4,128)S(1)}, u32[]{:S(2)}, u32[]{:S(2)}) collective-permute-start(f32[4,2560]{1,0:T(4,128)S(1)} %add.9.x_ref), channel_id=1, source_target_pairs={{0,8},{4,12},{8,0},{12,4},{16,24},{20,28},{24,16},{28,20},{1,9},{5... | collective-permute-start | bytes 122888 | tf_op jit(solution)/shard_map/ppermute | solution.py:70
  44.3 2.5 %collective-permute-done.13.y_ref = f32[4,2560]{1,0:T(4,128)S(1)} collective-permute-done((f32[4,2560]{1,0:T(4,128)S(1)}, f32[4,2560]{1,0:T(4,128)S(1)}, u32[]{:S(2)}, u32[]{:S(2)}) %collective-permute-start.13) | collective-permute-done | bytes 40992 | tf_op jit(solution)/shard_map/ppermute | solution.py:70
  46.8 1.5 %collective-permute-start.14 = (f32[4,2560]{1,0:T(4,128)S(1)}, f32[4,2560]{1,0:T(4,128)S(1)}, u32[]{:S(2)}, u32[]{:S(2)}) collective-permute-start(f32[4,2560]{1,0:T(4,128)S(1)} %add.10.x_ref), channel_id=1, source_target_pairs={{0,16},{4,20},{8,24},{12,28},{16,0},{20,4},{24,8},{28,12},{1,17},{... | collective-permute-start | bytes 122888 | tf_op jit(solution)/shard_map/ppermute | solution.py:70
  48.3 2.5 %collective-permute-done.14.y_ref = f32[4,2560]{1,0:T(4,128)S(1)} collective-permute-done((f32[4,2560]{1,0:T(4,128)S(1)}, f32[4,2560]{1,0:T(4,128)S(1)}, u32[]{:S(2)}, u32[]{:S(2)}) %collective-permute-start.14) | collective-permute-done | bytes 40992 | tf_op jit(solution)/shard_map/ppermute | solution.py:70
  51.1 1.7 %collective-permute-start.15 = (f32[4,2560]{1,0:T(4,128)S(1)}, f32[4,2560]{1,0:T(4,128)S(1)}, u32[]{:S(2)}, u32[]{:S(2)}) collective-permute-start(f32[4,2560]{1,0:T(4,128)S(1)} %add.11.x_ref), channel_id=1, source_target_pairs={{0,1},{1,0},{2,3},{3,2},{4,5},{5,4},{6,7},{7,6},{8,9},{9,8},{10,11... | collective-permute-start | bytes 122888 | tf_op jit(solution)/shard_map/ppermute | solution.py:70
  52.9 2.3 %collective-permute-done.15.y_ref = f32[4,2560]{1,0:T(4,128)S(1)} collective-permute-done((f32[4,2560]{1,0:T(4,128)S(1)}, f32[4,2560]{1,0:T(4,128)S(1)}, u32[]{:S(2)}, u32[]{:S(2)}) %collective-permute-start.15) | collective-permute-done | bytes 40992 | tf_op jit(solution)/shard_map/ppermute | solution.py:70
  55.1 3.2 %collective-permute-start.16 = (f32[4,2560]{1,0:T(4,128)S(1)}, f32[4,2560]{1,0:T(4,128)S(1)}, u32[]{:S(2)}, u32[]{:S(2)}) collective-permute-start(f32[4,2560]{1,0:T(4,128)S(1)} %add.12.x_ref), channel_id=1, source_target_pairs={{0,2},{1,3},{2,0},{3,1},{4,6},{5,7},{6,4},{7,5},{8,10},{9,11},{10,... | collective-permute-start | bytes 122888 | tf_op jit(solution)/shard_map/ppermute | solution.py:70
  58.4 1.9 %collective-permute-done.16.y_ref = f32[4,2560]{1,0:T(4,128)S(1)} collective-permute-done((f32[4,2560]{1,0:T(4,128)S(1)}, f32[4,2560]{1,0:T(4,128)S(1)}, u32[]{:S(2)}, u32[]{:S(2)}) %collective-permute-start.16) | collective-permute-done | bytes 40992 | tf_op jit(solution)/shard_map/ppermute | solution.py:70
  60.3 3.3 %collective-permute-start.21 = (bf16[1,64,1536]{2,1,0:T(8,128)(2,1)S(1)}, bf16[1,64,1536]{2,1,0:T(8,128)(2,1)S(1)}, u32[]{:S(2)}, u32[]{:S(2)}) collective-permute-start(bf16[1,64,1536]{2,1,0:T(8,128)(2,1)S(1)} %get-tuple-element.89), channel_id=1, source_target_pairs={{0,2},{2,3},{3,1},{1,0},{4,6},{6,7},{7,5},{5,4},{8,10},{10,11},{11... | collective-permute-start | bytes 589832 | tf_op jit(solution)/shard_map/ppermute | solution.py:60
  67.5 2.8 %rebuild.4 = (bf16[768,5120]{1,0:T(8,128)(2,1)}, bf16[1,768,5120]{2,1,0:T(8,128)(2,1)}) custom-call(bf16[768,256]{1,0:T(8,128)(2,1)S(1)} %acts.1.acts_ref, bf16[768,24]{1,0:T(8,128)(2,1)S(1)} %get-tuple-element.81.left_ref, bf16[24,5120]{1,0:T(8,128)(2,1)S(1)} %get-tuple-element.84.right_ref, bf16[1,768,5120]{2,1,0:T(8,128)(2,1)S(1)} %get-tuple-element.64.e_ref, ...), custom_call_target="tpu_custom_call" | custom-call | flops 1 | bytes 1 | tf_op jit(solution)/shard_map/rebuild/pallas_call | solution.py:457
  70.8 2.8 %rebuild.5 = (bf16[768,5120]{1,0:T(8,128)(2,1)}, bf16[1,768,5120]{2,1,0:T(8,128)(2,1)}) custom-call(bf16[768,256]{1,0:T(8,128)(2,1)S(1)} %acts.1.acts_ref, bf16[768,24]{1,0:T(8,128)(2,1)S(1)} %get-tuple-element.81.left_ref, bf16[24,5120]{1,0:T(8,128)(2,1)S(1)} %get-tuple-element.84.right_ref, ...), custom_call_target="tpu_custom_call", output_to_operand_aliasing={{0}: (8, {}), {1}: (9, {})} | custom-call | flops 1 | bytes 1 | tf_op jit(solution)/shard_map/rebuild/pallas_call | solution.py:457
  73.7 2.2 %rebuild.6 = (bf16[768,5120]{1,0:T(8,128)(2,1)}, bf16[1,768,5120]{2,1,0:T(8,128)(2,1)}) custom-call(bf16[768,256]{1,0:T(8,128)(2,1)S(1)} %acts.1.acts_ref, bf16[768,24]{1,0:T(8,128)(2,1)S(1)} %get-tuple-element.81.left_ref, bf16[24,5120]{1,0:T(8,128)(2,1)S(1)} %get-tuple-element.84.right_ref, ...), custom_call_target="tpu_custom_call", output_to_operand_aliasing={{0}: (8, {}), {1}: (9, {})} | custom-call | flops 1 | bytes 1 | tf_op jit(solution)/shard_map/rebuild/pallas_call | solution.py:457
  75.8 2.2 %rebuild.7 = (bf16[768,5120]{1,0:T(8,128)(2,1)}, bf16[1,768,5120]{2,1,0:T(8,128)(2,1)}) custom-call(bf16[768,256]{1,0:T(8,128)(2,1)S(1)} %acts.1.acts_ref, bf16[768,24]{1,0:T(8,128)(2,1)S(1)} %get-tuple-element.81.left_ref, bf16[24,5120]{1,0:T(8,128)(2,1)S(1)} %get-tuple-element.84.right_ref, ...), custom_call_target="tpu_custom_call", output_to_operand_aliasing={{0}: (8, {}), {1}: (9, {})} | custom-call | flops 1 | bytes 1 | tf_op jit(solution)/shard_map/rebuild/pallas_call | solution.py:457
  (46 shorter events, 13.6 us)
Async XLA Ops:
  0.6 20.4 %collective-permute-start = (bf16[1,64,5120]{2,1,0:T(8,128)(2,1)}, bf16[1,64,5120]{2,1,0:T(8,128)(2,1)S(1)}, u32[]{:S(2)}, u32[]{:S(2)}) collective-permute-start(bf16[1,64,5120]{2,1,0:T(8,128)(2,1)} %refs_0_.7), channel_id=1, source_target_pairs={{0,2},{2,3},{3,1},{1,0},{4,6},{6,7},{7,5},{5,4},{8,10},{10,11},{11... | collective-permute-start | bytes 1966088 | tf_op jit(solution)/shard_map/ppermute | solution.py:60
  6.2 16.5 %copy-start.1 = (bf16[1,256,768]{2,1,0:T(8,128)(2,1)S(1)}, bf16[1,256,768]{2,1,0:T(8,128)(2,1)}, u32[]{:S(2)}) copy-start(bf16[1,256,768]{2,1,0:T(8,128)(2,1)} %a_ref.5) | copy-start | bytes 1179652
  10.4 30.2 %copy-start = (bf16[1,64,5120]{2,1,0:T(8,128)(2,1)S(1)}, bf16[1,64,5120]{2,1,0:T(8,128)(2,1)}, u32[]{:S(2)}) copy-start(bf16[1,64,5120]{2,1,0:T(8,128)(2,1)} %refs_0_.7) | copy-start | bytes 1966084
  10.4 10.6 %collective-permute-start.1 = (f32[8,128]{1,0:T(8,128)S(1)}, f32[8,128]{1,0:T(8,128)S(1)}, u32[]{:S(2)}, u32[]{:S(2)}) collective-permute-start(f32[8,128]{1,0:T(8,128)S(1)} %get-tuple-element.56.refs_0_), channel_id=1, source_target_pairs={{0,1},{1,2},{2,3},{3,0},{4,5},{5,6},{6,7},{7,4},{8,9},{9,10},{10,1... | collective-permute-start | bytes 12296 | tf_op jit(solution)/shard_map/ppermute | solution.py:65
  10.5 10.5 %collective-permute-start.2 = (f32[8,128]{1,0:T(8,128)S(1)}, f32[8,128]{1,0:T(8,128)S(1)}, u32[]{:S(2)}, u32[]{:S(2)}) collective-permute-start(f32[8,128]{1,0:T(8,128)S(1)} %get-tuple-element.56.refs_0_), channel_id=1, source_target_pairs={{0,2},{1,3},{2,0},{3,1},{4,6},{5,7},{6,4},{7,5},{8,10},{9,11},{10,... | collective-permute-start | bytes 12296 | tf_op jit(solution)/shard_map/ppermute | solution.py:65
  12.4 8.6 %collective-permute-start.3 = (f32[8,128]{1,0:T(8,128)S(1)}, f32[8,128]{1,0:T(8,128)S(1)}, u32[]{:S(2)}, u32[]{:S(2)}) collective-permute-start(f32[8,128]{1,0:T(8,128)S(1)} %get-tuple-element.56.refs_0_), channel_id=1, source_target_pairs={{0,3},{1,0},{2,1},{3,2},{4,7},{5,4},{6,5},{7,6},{8,11},{9,8},{10,9... | collective-permute-start | bytes 12296 | tf_op jit(solution)/shard_map/ppermute | solution.py:65
  21.1 10.5 %collective-permute-start.6 = (bf16[1,64,3072]{2,1,0:T(8,128)(2,1)S(1)}, bf16[1,64,3072]{2,1,0:T(8,128)(2,1)S(1)}, u32[]{:S(2)}, u32[]{:S(2)}) collective-permute-start(bf16[1,64,3072]{2,1,0:T(8,128)(2,1)S(1)} %get-tuple-element.61), channel_id=1, source_target_pairs={{0,2},{2,3},{3,1},{1,0},{4,6},{6,7},{7,5},{5,4},{8,10},{10,11},{11... | collective-permute-start | bytes 1179656 | tf_op jit(solution)/shard_map/ppermute | solution.py:60
  22.9 1.2 %collective-permute-start.4 = (f32[4,768]{1,0:T(4,128)S(1)}, f32[4,768]{1,0:T(4,128)S(1)}, u32[]{:S(2)}, u32[]{:S(2)}) collective-permute-start(f32[4,768]{1,0:T(4,128)S(1)} %left.1.x_ref), channel_id=1, source_target_pairs={{0,4},{4,0},{8,12},{12,8},{16,20},{20,16},{24,28},{28,24},{1,5},{5... | collective-permute-start | bytes 36872 | tf_op jit(solution)/shard_map/ppermute | solution.py:70
  24.2 3.7 %collective-permute-start.5 = (f32[4,768]{1,0:T(4,128)S(1)}, f32[4,768]{1,0:T(4,128)S(1)}, u32[]{:S(2)}, u32[]{:S(2)}) collective-permute-start(f32[4,768]{1,0:T(4,128)S(1)} %add.7.x_ref), channel_id=1, source_target_pairs={{0,8},{4,12},{8,0},{12,4},{16,24},{20,28},{24,16},{28,20},{1,9},{5... | collective-permute-start | bytes 36872 | tf_op jit(solution)/shard_map/ppermute | solution.py:70
  27.9 3.7 %collective-permute-start.7 = (f32[4,768]{1,0:T(4,128)S(1)}, f32[4,768]{1,0:T(4,128)S(1)}, u32[]{:S(2)}, u32[]{:S(2)}) collective-permute-start(f32[4,768]{1,0:T(4,128)S(1)} %add.8.x_ref), channel_id=1, source_target_pairs={{0,16},{4,20},{8,24},{12,28},{16,0},{20,4},{24,8},{28,12},{1,17},{... | collective-permute-start | bytes 36872 | tf_op jit(solution)/shard_map/ppermute | solution.py:70
  31.9 5.2 %collective-permute-start.10 = (f32[8,128]{1,0:T(8,128)S(1)}, f32[8,128]{1,0:T(8,128)S(1)}, u32[]{:S(2)}, u32[]{:S(2)}) collective-permute-start(f32[8,128]{1,0:T(8,128)S(1)} %get-tuple-element.68), channel_id=1, source_target_pairs={{0,3},{1,0},{2,1},{3,2},{4,7},{5,4},{6,5},{7,6},{8,11},{9,8},{10,9... | collective-permute-start | bytes 12296 | tf_op jit(solution)/shard_map/ppermute | solution.py:65
  35.2 5.4 %collective-permute-start.8 = (f32[8,128]{1,0:T(8,128)S(1)}, f32[8,128]{1,0:T(8,128)S(1)}, u32[]{:S(2)}, u32[]{:S(2)}) collective-permute-start(f32[8,128]{1,0:T(8,128)S(1)} %get-tuple-element.66), channel_id=1, source_target_pairs={{0,1},{1,2},{2,3},{3,0},{4,5},{5,6},{6,7},{7,4},{8,9},{9,10},{10,1... | collective-permute-start | bytes 12296 | tf_op jit(solution)/shard_map/ppermute | solution.py:65
  35.2 5.4 %collective-permute-start.9 = (f32[8,128]{1,0:T(8,128)S(1)}, f32[8,128]{1,0:T(8,128)S(1)}, u32[]{:S(2)}, u32[]{:S(2)}) collective-permute-start(f32[8,128]{1,0:T(8,128)S(1)} %get-tuple-element.67), channel_id=1, source_target_pairs={{0,2},{1,3},{2,0},{3,1},{4,6},{5,7},{6,4},{7,5},{8,10},{9,11},{10,... | collective-permute-start | bytes 12296 | tf_op jit(solution)/shard_map/ppermute | solution.py:65
  41.4 1.3 %collective-permute-start.11 = (f32[4,2560]{1,0:T(4,128)S(1)}, f32[4,2560]{1,0:T(4,128)S(1)}, u32[]{:S(2)}, u32[]{:S(2)}) collective-permute-start(f32[4,2560]{1,0:T(4,128)S(1)} %get-tuple-element.73), channel_id=1, source_target_pairs={{0,4},{4,0},{8,12},{12,8},{16,20},{20,16},{24,28},{28,24},{1,5},{5... | collective-permute-start | bytes 122888 | tf_op jit(solution)/shard_map/ppermute | solution.py:70
  42.7 8.4 %collective-permute-start.12 = (bf16[1,64,2048]{2,1,0:T(8,128)(2,1)S(1)}, bf16[1,64,2048]{2,1,0:T(8,128)(2,1)S(1)}, u32[]{:S(2)}, u32[]{:S(2)}) collective-permute-start(bf16[1,64,2048]{2,1,0:T(8,128)(2,1)S(1)} %get-tuple-element.74), channel_id=1, source_target_pairs={{0,2},{2,3},{3,1},{1,0},{4,6},{6,7},{7,5},{5,4},{8,10},{10,11},{11... | collective-permute-start | bytes 786440 | tf_op jit(solution)/shard_map/ppermute | solution.py:60
  42.7 4.1 %collective-permute-start.13 = (f32[4,2560]{1,0:T(4,128)S(1)}, f32[4,2560]{1,0:T(4,128)S(1)}, u32[]{:S(2)}, u32[]{:S(2)}) collective-permute-start(f32[4,2560]{1,0:T(4,128)S(1)} %add.9.x_ref), channel_id=1, source_target_pairs={{0,8},{4,12},{8,0},{12,4},{16,24},{20,28},{24,16},{28,20},{1,9},{5... | collective-permute-start | bytes 122888 | tf_op jit(solution)/shard_map/ppermute | solution.py:70
  46.8 4.0 %collective-permute-start.14 = (f32[4,2560]{1,0:T(4,128)S(1)}, f32[4,2560]{1,0:T(4,128)S(1)}, u32[]{:S(2)}, u32[]{:S(2)}) collective-permute-start(f32[4,2560]{1,0:T(4,128)S(1)} %add.10.x_ref), channel_id=1, source_target_pairs={{0,16},{4,20},{8,24},{12,28},{16,0},{20,4},{24,8},{28,12},{1,17},{... | collective-permute-start | bytes 122888 | tf_op jit(solution)/shard_map/ppermute | solution.py:70
  51.1 4.0 %collective-permute-start.15 = (f32[4,2560]{1,0:T(4,128)S(1)}, f32[4,2560]{1,0:T(4,128)S(1)}, u32[]{:S(2)}, u32[]{:S(2)}) collective-permute-start(f32[4,2560]{1,0:T(4,128)S(1)} %add.11.x_ref), channel_id=1, source_target_pairs={{0,1},{1,0},{2,3},{3,2},{4,5},{5,4},{6,7},{7,6},{8,9},{9,8},{10,11... | collective-permute-start | bytes 122888 | tf_op jit(solution)/shard_map/ppermute | solution.py:70
  55.1 5.2 %collective-permute-start.16 = (f32[4,2560]{1,0:T(4,128)S(1)}, f32[4,2560]{1,0:T(4,128)S(1)}, u32[]{:S(2)}, u32[]{:S(2)}) collective-permute-start(f32[4,2560]{1,0:T(4,128)S(1)} %add.12.x_ref), channel_id=1, source_target_pairs={{0,2},{1,3},{2,0},{3,1},{4,6},{5,7},{6,4},{7,5},{8,10},{9,11},{10,... | collective-permute-start | bytes 122888 | tf_op jit(solution)/shard_map/ppermute | solution.py:70
  60.3 7.1 %collective-permute-start.21 = (bf16[1,64,1536]{2,1,0:T(8,128)(2,1)S(1)}, bf16[1,64,1536]{2,1,0:T(8,128)(2,1)S(1)}, u32[]{:S(2)}, u32[]{:S(2)}) collective-permute-start(bf16[1,64,1536]{2,1,0:T(8,128)(2,1)S(1)} %get-tuple-element.89), channel_id=1, source_target_pairs={{0,2},{2,3},{3,1},{1,0},{4,6},{6,7},{7,5},{5,4},{8,10},{10,11},{11... | collective-permute-start | bytes 589832 | tf_op jit(solution)/shard_map/ppermute | solution.py:60
  63.7 7.2 %collective-permute-start.20 = (bf16[1,64,1536]{2,1,0:T(8,128)(2,1)S(1)}, bf16[1,64,1536]{2,1,0:T(8,128)(2,1)S(1)}, u32[]{:S(2)}, u32[]{:S(2)}) collective-permute-start(bf16[1,64,1536]{2,1,0:T(8,128)(2,1)S(1)} %get-tuple-element.88), channel_id=1, source_target_pairs={{0,2},{2,3},{3,1},{1,0},{4,6},{6,7},{7,5},{5,4},{8,10},{10,11},{11... | collective-permute-start | bytes 589832 | tf_op jit(solution)/shard_map/ppermute | solution.py:60
  63.7 1.2 %collective-permute-start.17 = (f32[4,2560]{1,0:T(4,128)S(1)}, f32[4,2560]{1,0:T(4,128)S(1)}, u32[]{:S(2)}, u32[]{:S(2)}) collective-permute-start(f32[4,2560]{1,0:T(4,128)S(1)} %add.13.mine_ref), channel_id=1, source_target_pairs={{0,4},{4,0},{8,12},{12,8},{16,20},{20,16},{24,28},{28,24},{1,5},{5... | collective-permute-start | bytes 122888 | tf_op jit(solution)/shard_map/ppermute | solution.py:70
  65.7 7.9 %collective-permute-start.19 = (bf16[1,64,1024]{2,1,0:T(8,128)(2,1)S(1)}, bf16[1,64,1024]{2,1,0:T(8,128)(2,1)S(1)}, u32[]{:S(2)}, u32[]{:S(2)}) collective-permute-start(bf16[1,64,1024]{2,1,0:T(8,128)(2,1)S(1)} %get-tuple-element.87), channel_id=1, source_target_pairs={{0,2},{2,3},{3,1},{1,0},{4,6},{6,7},{7,5},{5,4},{8,10},{10,11},{11... | collective-permute-start | bytes 393224 | tf_op jit(solution)/shard_map/ppermute | solution.py:60
  66.7 9.1 %collective-permute-start.18 = (bf16[1,64,1024]{2,1,0:T(8,128)(2,1)S(1)}, bf16[1,64,1024]{2,1,0:T(8,128)(2,1)S(1)}, u32[]{:S(2)}, u32[]{:S(2)}) collective-permute-start(bf16[1,64,1024]{2,1,0:T(8,128)(2,1)S(1)} %get-tuple-element.86), channel_id=1, source_target_pairs={{0,2},{2,3},{3,1},{1,0},{4,6},{6,7},{7,5},{5,4},{8,10},{10,11},{11... | collective-permute-start | bytes 393224 | tf_op jit(solution)/shard_map/ppermute | solution.py:60

commit v10 on v9

--- a/solution.py
+++ b/solution.py
@@ -11,6 +11,7 @@
 BF16 = jnp.bfloat16
 SHRINK = 2.0**-23
 TINY = 1e-30
+ROOM = 2.0**14
 BLOCK = 512
 
 
@@ -68,6 +69,13 @@
 
 def swap(x, axis, n, bit):
     return lax.ppermute(x, axis, [(i, i ^ bit) for i in range(n)])
+
+
+def swap_odd(x, m, n, dp_bit, tensor_bit):
+    pairs = [
+        (i * n + t, (i ^ dp_bit) * n + (t ^ tensor_bit)) for i in range(1, m, 2) for t in range(n)
+    ]
+    return lax.ppermute(x, ("dp", "tensor"), pairs)
 
 
 def bits(n):
@@ -134,26 +142,36 @@
     out_ref[...] = total
 
 
-def mean_kernel(n, scale, a_ref, x_ref, y_ref, p_ref, *refs):
-    msgs, p3, outbox = refs[:n], refs[n], refs[n + 1]
+def mean_kernel(scale, a_ref, x_ref, y_ref, p_ref, msg_ref, p3):
     rank = x_ref.shape[0]
-    tok = a_ref.shape[1] // n
-    me = lax.axis_index("tensor")
     mean = (x_ref[...] + y_ref[...]) * scale
     p_ref[...] = mean
     top = jnp.max(jnp.max(jnp.abs(mean), axis=1, keepdims=True), axis=0, keepdims=True)
     top = jnp.maximum(top, TINY)
-    parts = stack3(mean / (top * 1024.0), p3)
-    gram = [jnp.sum(mean * mean[i : i + 1, :], axis=1, keepdims=True) for i in range(rank)]
-    outbox[...] = jnp.zeros_like(outbox)
-    for t in range(n):
-        y = dot(parts, a_ref[0, t * tok : (t + 1) * tok, :], (1, 1))
-        outbox[t, 0:rank, 0:tok] = sum3(y, rank)
-        for i in range(rank):
-            outbox[t, rank : 2 * rank, i : i + 1] = gram[i]
-        outbox[t, rank : rank + 1, rank : rank + 1] = top
-    for k in range(n):
-        msgs[k][...] = outbox[lax.rem(me + k, n)]
+    parts = stack3(mean / (top * ROOM), p3)
+    msg_ref[...] = jnp.zeros_like(msg_ref)
+    msg_ref[0:rank, :] = sum3(dot(parts, a_ref[0], (1, 1)), rank)
+    for i in range(rank):
+        column = jnp.sum(mean * mean[i : i + 1, :], axis=1, keepdims=True)
+        msg_ref[rank : 2 * rank, i : i + 1] = column
+    msg_ref[rank : rank + 1, rank : rank + 1] = top
+
+
+def joined(x, y, rank):
+    top_x = x[rank : rank + 1, rank : rank + 1]
+    top_y = y[rank : rank + 1, rank : rank + 1]
+    top = jnp.maximum(top_x, top_y)
+    products = x[0:rank, :] * (top_x / top) + y[0:rank, :] * (top_y / top)
+    gram = x[rank : 2 * rank, 0:rank] + y[rank : 2 * rank, 0:rank]
+    return products, gram, top
+
+
+def join_kernel(rank, x_ref, y_ref, out_ref):
+    products, gram, top = joined(x_ref[...], y_ref[...], rank)
+    out_ref[...] = jnp.zeros_like(out_ref)
+    out_ref[0:rank, :] = products
+    out_ref[rank : 2 * rank, 0:rank] = gram
+    out_ref[rank : rank + 1, rank : rank + 1] = top
 
 
 def error_right_kernel(p_ref, e_ref, out_ref, p3):
@@ -198,38 +216,23 @@
     return rows
 
 
-def right_kernel(n, p_ref, r_ref, g_ref, *refs):
-    pieces = refs[:n]
-    ortho_ref, keep_ref, send_ref, inbox, z, z3, outbox = refs[n:]
+def right_kernel(n, p_ref, r_ref, g_ref, x_ref, y_ref, ortho_ref, out_ref, z, z3):
     rank = p_ref.shape[0]
     tok = g_ref.shape[1]
-    half = keep_ref.shape[1]
-    me_t = lax.axis_index("tensor")
-    core = lax.rem(lax.axis_index("dp"), 2)
-    for k in range(n):
-        inbox[lax.rem(me_t - k + n, n)] = pieces[k][...]
-    gram = inbox[0, rank : 2 * rank, 0:rank]
-    for t in range(1, n):
-        gram = gram + inbox[t, rank : 2 * rank, 0:rank]
+    products, gram, top = joined(x_ref[...], y_ref[...], rank)
     inv = lower_inverse(gram, rank)
-    for t in range(n):
-        top = inbox[t, rank : rank + 1, rank : rank + 1]
-        scaled = {key: value * top for key, value in inv.items()}
-        for i, row in enumerate(solve_rows(scaled, inbox[t, 0:rank, 0:tok], rank)):
-            if t == 0:
-                z[i : i + 1, :] = row
-            else:
-                z[i : i + 1, :] += row
+    scaled = {key: value * top for key, value in inv.items()}
+    for i, row in enumerate(solve_rows(scaled, products, rank)):
+        for t in range(n):
+            z[t, i : i + 1, :] = row[:, t * tok : (t + 1) * tok]
     for i, row in enumerate(solve_rows(inv, p_ref[...], rank)):
         ortho_ref[i : i + 1, :] = row
-    terms = stack3(z[...], z3)
-    for h in range(2):
-        cols = slice(h * half, (h + 1) * half)
-        fresh = sum3(dot(terms, g_ref[0, :, cols], (1, 0)), rank) * 1024.0
+    terms = stack3(z[lax.axis_index("tensor")], z3)
+    for c in range(r_ref.shape[1] // BLOCK):
+        cols = slice(c * BLOCK, (c + 1) * BLOCK)
+        fresh = sum3(dot(terms, g_ref[0, :, cols], (1, 0)), rank) * ROOM
         for i, row in enumerate(solve_rows(inv, r_ref[:, cols], rank)):
-            outbox[h, i : i + 1, :] = row + fresh[i : i + 1, :]
-    keep_ref[...] = outbox[core]
-    send_ref[...] = outbox[1 - core]
+            out_ref[i : i + 1, cols] = row + fresh[i : i + 1, :]
 
 
 def add_kernel(x_ref, y_ref, out_ref):
@@ -240,13 +243,18 @@
 RIGHT_TERMS = (0, 1, 0, 2, 0, 1)
 
 
-def factor_kernel(scale, ortho_ref, mine_ref, other_ref, whole_ref, left_ref, right_ref, inbox, left, right):
-    rank, half = mine_ref.shape
+def factor_kernel(scale, ortho_ref, mine_ref, other_ref, whole_ref, left_ref, right_ref, left, right):
+    rank = mine_ref.shape[0]
     core = lax.rem(lax.axis_index("dp"), 2)
-    inbox[core] = mine_ref[...]
-    inbox[1 - core] = other_ref[...]
-    for h in range(2):
-        whole_ref[:, h * half : (h + 1) * half] = inbox[h] * scale
+
+    @pl.when(core == 1)
+    def _():
+        whole_ref[...] = mine_ref[...] * scale
+
+    @pl.when(core == 0)
+    def _():
+        whole_ref[...] = other_ref[...] * scale
+
     for terms, x, ref in (
         (LEFT_TERMS, ortho_ref[...], left),
         (RIGHT_TERMS, whole_ref[...], right),
@@ -311,7 +319,6 @@
     _, tokens, rows = activations.shape
     _, tok, width = out_grads.shape
     rank = warm_factor.shape[1]
-    half = width // 2
     w = warm_factor.T
     sds = jax.ShapeDtypeStruct
     hbm = pl.BlockSpec(memory_space=pltpu.HBM)
@@ -343,7 +350,7 @@
     def step(x):
         return ring_step(x, "tensor", n)
 
-    wide = 6 * width // 20
+    wide = width // 4
     narrow = width // 2 - wide
     ring = [out_grads, step(out_grads)]
 
@@ -377,13 +384,19 @@
         left = add(left, swap(left, "dp", m, bit))
     xs[1], last = after(xs[1], swap(left, "dp", m, bits(m)[-1]))
 
-    mean, *msgs = call(
-        functools.partial(mean_kernel, n, 1.0 / (SHRINK * m)),
-        [sds((rank, rows), F32)] + [sds((8, 128), F32)] * n,
-        [pltpu.VMEM((3 * rank, rows), F32), pltpu.VMEM((n, 8, 128), F32)],
+    mean, msg = call(
+        functools.partial(mean_kernel, 1.0 / (SHRINK * m)),
+        [sds((rank, rows), F32), sds((2 * rank, tokens), F32)],
+        [pltpu.VMEM((3 * rank, rows), F32)],
         "mean",
     )(activations, left, last)
-    msgs = exchange(msgs, "tensor", n)
+
+    def join(x, y):
+        return call(functools.partial(join_kernel, rank), sds(x.shape, F32), [], "join")(x, y)
+
+    for bit in bits(n)[:-1]:
+        msg = join(msg, swap(msg, "tensor", n, bit))
+    msgs = [msg, swap(msg, "tensor", n, bits(n)[-1])]
 
     right_raw = call(
         error_right_kernel,
@@ -392,18 +405,13 @@
         "error_right", None, 1.2e9,
     )(mean, error_v)
 
-    ortho, keep, send = call(
+    ortho, total = call(
         functools.partial(right_kernel, n),
-        [sds((rank, rows), F32), sds((rank, half), F32), sds((rank, half), F32)],
-        [
-            pltpu.VMEM((n, 8, 128), F32),
-            pltpu.VMEM((rank, tok), F32),
-            pltpu.VMEM((3 * rank, tok), F32),
-            pltpu.VMEM((2, rank, half), F32),
-        ],
+        [sds((rank, rows), F32), sds((rank, width), F32)],
+        [pltpu.VMEM((n, rank, tok), F32), pltpu.VMEM((3 * rank, tok), F32)],
         "right",
     )(mean, right_raw, out_grads, *msgs)
-    total = add(keep, swap(send, "dp", m, 1))
+    total = add(total, swap(total, "dp", m, 1))
     for _ in range(3, n):
         last, total = after(ys[-1], total)
         ys.append(step(last))
@@ -411,12 +419,13 @@
         last, total = after(xs[-1], total)
         xs.append(step(last))
     for bit in bits(m)[1:]:
-        total = add(total, swap(total, "dp", m, bit))
+        total = add(total, swap_odd(total, m, n, bit, 0))
     (xs[-1], ys[-1]), total = after((xs[-1], ys[-1]), total)
     for bit in bits(n):
-        total = add(total, swap(total, "tensor", n, bit))
+        total = add(total, swap_odd(total, m, n, 0, bit))
+    other = lax.ppermute(total, "dp", [(i, i - 1) for i in range(1, m, 2)])
     xa, xb = cut(xs[-1], [wide, wide])
-    (xa, xb), total = after((xa, xb), total)
+    (xa, xb), (total, other) = after((xa, xb), (total, other))
     xa, xb = step(xa), step(xb)
 
     terms = len(LEFT_TERMS) * rank
@@ -424,12 +433,11 @@
         functools.partial(factor_kernel, 1.0 / m),
         [sds((rank, width), F32), sds((rows, terms), BF16), sds((terms, width), BF16)],
         [
-            pltpu.VMEM((2, rank, half), F32),
             pltpu.VMEM((terms, rows), F32),
             pltpu.VMEM((terms, width), F32),
         ],
         "factor",
-    )(ortho, total, swap(total, "dp", m, 1))
+    )(ortho, total, other)
 
     acts = call(
         functools.partial(acts_kernel, n),

time: 78.1 us -> 88.3 us (1.13)
  waiting for transfers between devices: 27.5 us -> 41.5 us
  starting transfers between devices: 30.5 us -> 26.5 us
    ppermute x0 -> x5, waiting for transfers between devices: none -> 13.7 us  [the longest x1 13.7 us: per_device(): other = lax.ppermute(total, 'dp', [(i, i - 1) for i in range(1, m, 2)])]
    ppermute x7, waiting for transfers between devices: 0.83 us -> 10.3 us  [ring_step(): lax.ppermute(x, axis, [(ring[p], ring[(p + 1) % n]) for p in range(n)])]
    ppermute x9 -> x6, waiting for transfers between devices: 17.1 us -> 11.5 us  [swap(): return lax.ppermute(x, axis, [(i, i ^ bit) for i in range(n)])]
    ppermute x9 -> x6, starting transfers between devices: 11.2 us -> 5.68 us  [swap(): return lax.ppermute(x, axis, [(i, i ^ bit) for i in range(n)])]
    ppermute x6 -> x3, starting transfers between devices: 8.61 us -> 4.55 us  [exchange(): lax.ppermute(pieces[k], axis, [(i, (i + k) % n) for i in range(n)])]
    ppermute x0 -> x5, starting transfers between devices: none -> 3.93 us  [the longest x4 2.64 us: swap_odd(): return lax.ppermute(x, ('dp', 'tensor'), pairs)]
    ppermute x6 -> x3, waiting for transfers between devices: 9.54 us -> 6.01 us  [exchange(): lax.ppermute(pieces[k], axis, [(i, (i + k) % n) for i in range(n)])]
    ppermute x7, starting transfers between devices: 10.7 us -> 12.3 us  [ring_step(): lax.ppermute(x, axis, [(ring[p], ring[(p + 1) % n]) for p in range(n)])]
  transfers between devices with their start and end apart: 22 -> 21, of which waited for: 13 -> 13; matrix products, arithmetic and copies ran while one was open for 0% -> 0% of each run, Pallas kernels for 20% -> 17%
where the time goes in v10:
time: 88.3 us; the launch traced here: 88.1 us
  waiting for transfers between devices  41.5 us (47%)
  starting transfers between devices  26.5 us (30%)
  Pallas kernels  19.2 us (22%)
  between operations  0.89 us (1%)
    ppermute x1, waiting for transfers between devices, per_device(): other = lax.ppermute(total, 'dp', [(i, i - 1) for i in range(1, m, 2)])  13.7 us
    ppermute x7, starting transfers between devices, ring_step(): lax.ppermute(x, axis, [(ring[p], ring[(p + 1) % n]) for p in range(n)])  12.3 us
    ppermute x6, waiting for transfers between devices, swap(): return lax.ppermute(x, axis, [(i, i ^ bit) for i in range(n)])  11.5 us
    ppermute x7, waiting for transfers between devices, ring_step(): lax.ppermute(x, axis, [(ring[p], ring[(p + 1) % n]) for p in range(n)])  10.3 us
    pallas_call x4, Pallas kernels, per_device(): pl.pallas_call(functools.partial(final_kernel, at, part, bases), in_specs...  9.88 us
    ppermute x3, waiting for transfers between devices, exchange(): lax.ppermute(pieces[k], axis, [(i, (i + k) % n) for i in range(n)])  6.01 us
    ppermute x6, starting transfers between devices, swap(): return lax.ppermute(x, axis, [(i, i ^ bit) for i in range(n)])  5.68 us
    ppermute x3, starting transfers between devices, exchange(): lax.ppermute(pieces[k], axis, [(i, (i + k) % n) for i in range(n)])  4.55 us
  transfers between devices with their start and end apart: 21, of which 13 were waited for; matrix products, arithmetic and copies ran while one was open for 0% of the time, Pallas kernels for 17%

profile of v10, /device:TPU:0, one launch (start us, length us, event | category | flops | bytes accessed | tf_op | source)
XLA Modules:
  0.0 88.1 jit_solution(11858368872812917669)
XLA Ops:
  0.6 4.1 %collective-permute-start = (bf16[1,64,5120]{2,1,0:T(8,128)(2,1)}, bf16[1,64,5120]{2,1,0:T(8,128)(2,1)S(1)}, u32[]{:S(2)}, u32[]{:S(2)}) collective-permute-start(bf16[1,64,5120]{2,1,0:T(8,128)(2,1)} %refs_0_.7), channel_id=1, source_target_pairs={{0,2},{2,3},{3,1},{1,0},{4,6},{6,7},{7,5},{5,4},{8,10},{10,11},{11... | collective-permute-start | bytes 1966088 | tf_op jit(solution)/shard_map/ppermute | solution.py:61
  4.7 1.5 %token_factor.1 = (f32[8,128]{1,0:T(8,128)S(1)}, bf16[12,5120]{1,0:T(8,128)(2,1)S(1)}) custom-call(f32[4,5120]{1,0:T(4,128)} %bitcast.2, bf16[1,64,5120]{2,1,0:T(8,128)(2,1)} %refs_0_.7), custom_call_target="tpu_custom_call" | custom-call | flops 1 | bytes 1 | tf_op jit(solution)/shard_map/token_factor/pallas_call | solution.py:357
  6.2 4.2 %error_left.1 = (f32[4,768]{1,0:T(4,128)S(1)}, bf16[1,768,5120]{2,1,0:T(8,128)(2,1)S(1)}) custom-call(bf16[12,5120]{1,0:T(8,128)(2,1)S(1)} %get-tuple-element.49.terms_ref, bf16[1,768,5120]{2,1,0:T(8,128)(2,1)} %e_hbm.1), custom_call_target="tpu_custom_call" | custom-call | flops 4600000000 | bytes 1 | tf_op jit(solution)/shard_map/error_left/pallas_call | solution.py:368
  10.5 1.9 %collective-permute-start.2 = (f32[8,128]{1,0:T(8,128)S(1)}, f32[8,128]{1,0:T(8,128)S(1)}, u32[]{:S(2)}, u32[]{:S(2)}) collective-permute-start(f32[8,128]{1,0:T(8,128)S(1)} %get-tuple-element.53.refs_0_), channel_id=1, source_target_pairs={{0,2},{1,3},{2,0},{3,1},{4,6},{5,7},{6,4},{7,5},{8,10},{9,11},{10,... | collective-permute-start | bytes 12296 | tf_op jit(solution)/shard_map/ppermute | solution.py:66
  12.4 2.6 %collective-permute-start.3 = (f32[8,128]{1,0:T(8,128)S(1)}, f32[8,128]{1,0:T(8,128)S(1)}, u32[]{:S(2)}, u32[]{:S(2)}) collective-permute-start(f32[8,128]{1,0:T(8,128)S(1)} %get-tuple-element.53.refs_0_), channel_id=1, source_target_pairs={{0,3},{1,0},{2,1},{3,2},{4,7},{5,4},{6,5},{7,6},{8,11},{9,8},{10,9... | collective-permute-start | bytes 12296 | tf_op jit(solution)/shard_map/ppermute | solution.py:66
  15.0 6.0 %collective-permute-done.1.refs_1_ = f32[8,128]{1,0:T(8,128)S(1)} collective-permute-done((f32[8,128]{1,0:T(8,128)S(1)}, f32[8,128]{1,0:T(8,128)S(1)}, u32[]{:S(2)}, u32[]{:S(2)}) %collective-permute-start.1) | collective-permute-done | bytes 4128 | tf_op jit(solution)/shard_map/ppermute | solution.py:66
  21.1 1.6 %collective-permute-start.6 = (bf16[1,64,2560]{2,1,0:T(8,128)(2,1)S(1)}, bf16[1,64,2560]{2,1,0:T(8,128)(2,1)S(1)}, u32[]{:S(2)}, u32[]{:S(2)}) collective-permute-start(bf16[1,64,2560]{2,1,0:T(8,128)(2,1)S(1)} %get-tuple-element.58), channel_id=1, source_target_pairs={{0,2},{2,3},{3,1},{1,0},{4,6},{6,7},{7,5},{5,4},{8,10},{10,11},{11... | collective-permute-start | bytes 983048 | tf_op jit(solution)/shard_map/ppermute | solution.py:61
  24.2 1.5 %collective-permute-start.5 = (f32[4,768]{1,0:T(4,128)S(1)}, f32[4,768]{1,0:T(4,128)S(1)}, u32[]{:S(2)}, u32[]{:S(2)}) collective-permute-start(f32[4,768]{1,0:T(4,128)S(1)} %add.7.x_ref), channel_id=1, source_target_pairs={{0,8},{4,12},{8,0},{12,4},{16,24},{20,28},{24,16},{28,20},{1,9},{5... | collective-permute-start | bytes 36872 | tf_op jit(solution)/shard_map/ppermute | solution.py:71
  25.6 2.2 %collective-permute-done.5.y_ref = f32[4,768]{1,0:T(4,128)S(1)} collective-permute-done((f32[4,768]{1,0:T(4,128)S(1)}, f32[4,768]{1,0:T(4,128)S(1)}, u32[]{:S(2)}, u32[]{:S(2)}) %collective-permute-start.5) | collective-permute-done | bytes 12320 | tf_op jit(solution)/shard_map/ppermute | solution.py:71
  27.9 1.5 %collective-permute-start.7 = (f32[4,768]{1,0:T(4,128)S(1)}, f32[4,768]{1,0:T(4,128)S(1)}, u32[]{:S(2)}, u32[]{:S(2)}) collective-permute-start(f32[4,768]{1,0:T(4,128)S(1)} %add.8.x_ref), channel_id=1, source_target_pairs={{0,16},{4,20},{8,24},{12,28},{16,0},{20,4},{24,8},{28,12},{1,17},{... | collective-permute-start | bytes 36872 | tf_op jit(solution)/shard_map/ppermute | solution.py:71
  29.4 2.2 %collective-permute-done.7.y_ref = f32[4,768]{1,0:T(4,128)S(1)} collective-permute-done((f32[4,768]{1,0:T(4,128)S(1)}, f32[4,768]{1,0:T(4,128)S(1)}, u32[]{:S(2)}, u32[]{:S(2)}) %collective-permute-start.7) | collective-permute-done | bytes 12320 | tf_op jit(solution)/shard_map/ppermute | solution.py:71
  32.7 2.8 %collective-permute-done.8.y_ref = f32[8,256]{1,0:T(8,128)S(1)} collective-permute-done((f32[8,256]{1,0:T(8,128)S(1)}, f32[8,256]{1,0:T(8,128)S(1)}, u32[]{:S(2)}, u32[]{:S(2)}) %collective-permute-start.8) | collective-permute-done | bytes 8224 | tf_op jit(solution)/shard_map/ppermute | solution.py:71
  35.6 1.6 %collective-permute-start.9 = (f32[8,256]{1,0:T(8,128)S(1)}, f32[8,256]{1,0:T(8,128)S(1)}, u32[]{:S(2)}, u32[]{:S(2)}) collective-permute-start(f32[8,256]{1,0:T(8,128)S(1)} %join.1.x_ref), channel_id=1, source_target_pairs={{0,2},{1,3},{2,0},{3,1},{4,6},{5,7},{6,4},{7,5},{8,10},{9,11},{10,... | collective-permute-start | bytes 24584 | tf_op jit(solution)/shard_map/ppermute | solution.py:71
  38.4 1.9 %collective-permute-done.9.y_ref = f32[8,256]{1,0:T(8,128)S(1)} collective-permute-done((f32[8,256]{1,0:T(8,128)S(1)}, f32[8,256]{1,0:T(8,128)S(1)}, u32[]{:S(2)}, u32[]{:S(2)}) %collective-permute-start.9) | collective-permute-done | bytes 8224 | tf_op jit(solution)/shard_map/ppermute | solution.py:71
  42.5 1.6 %collective-permute-start.11 = (bf16[1,64,2560]{2,1,0:T(8,128)(2,1)S(1)}, bf16[1,64,2560]{2,1,0:T(8,128)(2,1)S(1)}, u32[]{:S(2)}, u32[]{:S(2)}) collective-permute-start(bf16[1,64,2560]{2,1,0:T(8,128)(2,1)S(1)} %get-tuple-element.67), channel_id=1, source_target_pairs={{0,2},{2,3},{3,1},{1,0},{4,6},{6,7},{7,5},{5,4},{8,10},{10,11},{11... | collective-permute-start | bytes 983048 | tf_op jit(solution)/shard_map/ppermute | solution.py:61
  45.5 6.8 %collective-permute-done.11.x_ref.refs_2_ = bf16[1,64,2560]{2,1,0:T(8,128)(2,1)S(1)} collective-permute-done((bf16[1,64,2560]{2,1,0:T(8,128)(2,1)S(1)}, bf16[1,64,2560]{2,1,0:T(8,128)(2,1)S(1)}, u32[]{:S(2)}, u32[]{:S(2)}) %collective-permute-start.11) | collective-permute-done | bytes 327712 | tf_op jit(solution)/shard_map/ppermute | solution.py:61
  53.7 1.3 %collective-permute-start.16 = (f32[4,5120]{1,0:T(4,128)S(1)}, f32[4,5120]{1,0:T(4,128)S(1)}, u32[]{:S(2)}, u32[]{:S(2)}) collective-permute-start(f32[4,5120]{1,0:T(4,128)S(1)} %add.13.mine_ref), channel_id=1, source_target_pairs={{4,0},{12,8},{20,16},{28,24},{5,1},{13,9},{21,17},{29,25},{6,2},{1... | collective-permute-start | bytes 245768 | tf_op jit(solution)/shard_map/ppermute | solution.py:426
  55.1 13.7 %collective-permute-done.16.other_ref = f32[4,5120]{1,0:T(4,128)S(1)} collective-permute-done((f32[4,5120]{1,0:T(4,128)S(1)}, f32[4,5120]{1,0:T(4,128)S(1)}, u32[]{:S(2)}, u32[]{:S(2)}) %collective-permute-start.16) | collective-permute-done | bytes 81952 | tf_op jit(solution)/shard_map/ppermute | solution.py:426
  69.6 2.1 %collective-permute-start.19 = (bf16[1,64,1280]{2,1,0:T(8,128)(2,1)S(1)}, bf16[1,64,1280]{2,1,0:T(8,128)(2,1)S(1)}, u32[]{:S(2)}, u32[]{:S(2)}) collective-permute-start(bf16[1,64,1280]{2,1,0:T(8,128)(2,1)S(1)} %get-tuple-element.82), channel_id=1, source_target_pairs={{0,2},{2,3},{3,1},{1,0},{4,6},{6,7},{7,5},{5,4},{8,10},{10,11},{11... | collective-permute-start | bytes 491528 | tf_op jit(solution)/shard_map/ppermute | solution.py:61
  72.3 2.3 %collective-permute-start.17 = (bf16[1,64,1280]{2,1,0:T(8,128)(2,1)S(1)}, bf16[1,64,1280]{2,1,0:T(8,128)(2,1)S(1)}, u32[]{:S(2)}, u32[]{:S(2)}) collective-permute-start(bf16[1,64,1280]{2,1,0:T(8,128)(2,1)S(1)} %get-tuple-element.80), channel_id=1, source_target_pairs={{0,2},{2,3},{3,1},{1,0},{4,6},{6,7},{7,5},{5,4},{8,10},{10,11},{11... | collective-permute-start | bytes 491528 | tf_op jit(solution)/shard_map/ppermute | solution.py:61
  75.8 2.5 %rebuild.4 = (bf16[768,5120]{1,0:T(8,128)(2,1)}, bf16[1,768,5120]{2,1,0:T(8,128)(2,1)}) custom-call(bf16[768,256]{1,0:T(8,128)(2,1)S(1)} %acts.1.acts_ref, bf16[768,24]{1,0:T(8,128)(2,1)S(1)} %get-tuple-element.75.left_ref, bf16[24,5120]{1,0:T(8,128)(2,1)S(1)} %get-tuple-element.78.right_ref, bf16[1,768,5120]{2,1,0:T(8,128)(2,1)S(1)} %get-tuple-element.61.e_ref, ...), custom_call_target="tpu_custom_call" | custom-call | flops 1 | bytes 1 | tf_op jit(solution)/shard_map/rebuild/pallas_call | solution.py:465
  79.4 2.5 %rebuild.5 = (bf16[768,5120]{1,0:T(8,128)(2,1)}, bf16[1,768,5120]{2,1,0:T(8,128)(2,1)}) custom-call(bf16[768,256]{1,0:T(8,128)(2,1)S(1)} %acts.1.acts_ref, bf16[768,24]{1,0:T(8,128)(2,1)S(1)} %get-tuple-element.75.left_ref, bf16[24,5120]{1,0:T(8,128)(2,1)S(1)} %get-tuple-element.78.right_ref, ...), custom_call_target="tpu_custom_call", output_to_operand_aliasing={{0}: (8, {}), {1}: (9, {})} | custom-call | flops 1 | bytes 1 | tf_op jit(solution)/shard_map/rebuild/pallas_call | solution.py:465
  82.9 2.5 %rebuild.6 = (bf16[768,5120]{1,0:T(8,128)(2,1)}, bf16[1,768,5120]{2,1,0:T(8,128)(2,1)}) custom-call(bf16[768,256]{1,0:T(8,128)(2,1)S(1)} %acts.1.acts_ref, bf16[768,24]{1,0:T(8,128)(2,1)S(1)} %get-tuple-element.75.left_ref, bf16[24,5120]{1,0:T(8,128)(2,1)S(1)} %get-tuple-element.78.right_ref, ...), custom_call_target="tpu_custom_call", output_to_operand_aliasing={{0}: (8, {}), {1}: (9, {})} | custom-call | flops 1 | bytes 1 | tf_op jit(solution)/shard_map/rebuild/pallas_call | solution.py:465
  85.6 2.5 %rebuild.7 = (bf16[768,5120]{1,0:T(8,128)(2,1)}, bf16[1,768,5120]{2,1,0:T(8,128)(2,1)}) custom-call(bf16[768,256]{1,0:T(8,128)(2,1)S(1)} %acts.1.acts_ref, bf16[768,24]{1,0:T(8,128)(2,1)S(1)} %get-tuple-element.75.left_ref, bf16[24,5120]{1,0:T(8,128)(2,1)S(1)} %get-tuple-element.78.right_ref, ...), custom_call_target="tpu_custom_call", output_to_operand_aliasing={{0}: (8, {}), {1}: (9, {})} | custom-call | flops 1 | bytes 1 | tf_op jit(solution)/shard_map/rebuild/pallas_call | solution.py:465
  (45 shorter events, 13.9 us)
Async XLA Ops:
  0.6 20.4 %collective-permute-start = (bf16[1,64,5120]{2,1,0:T(8,128)(2,1)}, bf16[1,64,5120]{2,1,0:T(8,128)(2,1)S(1)}, u32[]{:S(2)}, u32[]{:S(2)}) collective-permute-start(bf16[1,64,5120]{2,1,0:T(8,128)(2,1)} %refs_0_.7), channel_id=1, source_target_pairs={{0,2},{2,3},{3,1},{1,0},{4,6},{6,7},{7,5},{5,4},{8,10},{10,11},{11... | collective-permute-start | bytes 1966088 | tf_op jit(solution)/shard_map/ppermute | solution.py:61
  6.2 16.5 %copy-start.1 = (bf16[1,256,768]{2,1,0:T(8,128)(2,1)S(1)}, bf16[1,256,768]{2,1,0:T(8,128)(2,1)}, u32[]{:S(2)}) copy-start(bf16[1,256,768]{2,1,0:T(8,128)(2,1)} %a_ref.5) | copy-start | bytes 1179652
  10.4 29.8 %copy-start = (bf16[1,64,5120]{2,1,0:T(8,128)(2,1)S(1)}, bf16[1,64,5120]{2,1,0:T(8,128)(2,1)}, u32[]{:S(2)}) copy-start(bf16[1,64,5120]{2,1,0:T(8,128)(2,1)} %refs_0_.7) | copy-start | bytes 1966084
  10.4 10.6 %collective-permute-start.1 = (f32[8,128]{1,0:T(8,128)S(1)}, f32[8,128]{1,0:T(8,128)S(1)}, u32[]{:S(2)}, u32[]{:S(2)}) collective-permute-start(f32[8,128]{1,0:T(8,128)S(1)} %get-tuple-element.53.refs_0_), channel_id=1, source_target_pairs={{0,1},{1,2},{2,3},{3,0},{4,5},{5,6},{6,7},{7,4},{8,9},{9,10},{10,1... | collective-permute-start | bytes 12296 | tf_op jit(solution)/shard_map/ppermute | solution.py:66
  10.5 10.5 %collective-permute-start.2 = (f32[8,128]{1,0:T(8,128)S(1)}, f32[8,128]{1,0:T(8,128)S(1)}, u32[]{:S(2)}, u32[]{:S(2)}) collective-permute-start(f32[8,128]{1,0:T(8,128)S(1)} %get-tuple-element.53.refs_0_), channel_id=1, source_target_pairs={{0,2},{1,3},{2,0},{3,1},{4,6},{5,7},{6,4},{7,5},{8,10},{9,11},{10,... | collective-permute-start | bytes 12296 | tf_op jit(solution)/shard_map/ppermute | solution.py:66
  12.4 8.6 %collective-permute-start.3 = (f32[8,128]{1,0:T(8,128)S(1)}, f32[8,128]{1,0:T(8,128)S(1)}, u32[]{:S(2)}, u32[]{:S(2)}) collective-permute-start(f32[8,128]{1,0:T(8,128)S(1)} %get-tuple-element.53.refs_0_), channel_id=1, source_target_pairs={{0,3},{1,0},{2,1},{3,2},{4,7},{5,4},{6,5},{7,6},{8,11},{9,8},{10,9... | collective-permute-start | bytes 12296 | tf_op jit(solution)/shard_map/ppermute | solution.py:66
  21.1 10.5 %collective-permute-start.6 = (bf16[1,64,2560]{2,1,0:T(8,128)(2,1)S(1)}, bf16[1,64,2560]{2,1,0:T(8,128)(2,1)S(1)}, u32[]{:S(2)}, u32[]{:S(2)}) collective-permute-start(bf16[1,64,2560]{2,1,0:T(8,128)(2,1)S(1)} %get-tuple-element.58), channel_id=1, source_target_pairs={{0,2},{2,3},{3,1},{1,0},{4,6},{6,7},{7,5},{5,4},{8,10},{10,11},{11... | collective-permute-start | bytes 983048 | tf_op jit(solution)/shard_map/ppermute | solution.py:61
  22.9 1.2 %collective-permute-start.4 = (f32[4,768]{1,0:T(4,128)S(1)}, f32[4,768]{1,0:T(4,128)S(1)}, u32[]{:S(2)}, u32[]{:S(2)}) collective-permute-start(f32[4,768]{1,0:T(4,128)S(1)} %left.1.x_ref), channel_id=1, source_target_pairs={{0,4},{4,0},{8,12},{12,8},{16,20},{20,16},{24,28},{28,24},{1,5},{5... | collective-permute-start | bytes 36872 | tf_op jit(solution)/shard_map/ppermute | solution.py:71
  24.2 3.7 %collective-permute-start.5 = (f32[4,768]{1,0:T(4,128)S(1)}, f32[4,768]{1,0:T(4,128)S(1)}, u32[]{:S(2)}, u32[]{:S(2)}) collective-permute-start(f32[4,768]{1,0:T(4,128)S(1)} %add.7.x_ref), channel_id=1, source_target_pairs={{0,8},{4,12},{8,0},{12,4},{16,24},{20,28},{24,16},{28,20},{1,9},{5... | collective-permute-start | bytes 36872 | tf_op jit(solution)/shard_map/ppermute | solution.py:71
  27.9 3.7 %collective-permute-start.7 = (f32[4,768]{1,0:T(4,128)S(1)}, f32[4,768]{1,0:T(4,128)S(1)}, u32[]{:S(2)}, u32[]{:S(2)}) collective-permute-start(f32[4,768]{1,0:T(4,128)S(1)} %add.8.x_ref), channel_id=1, source_target_pairs={{0,16},{4,20},{8,24},{12,28},{16,0},{20,4},{24,8},{28,12},{1,17},{... | collective-permute-start | bytes 36872 | tf_op jit(solution)/shard_map/ppermute | solution.py:71
  31.8 3.7 %collective-permute-start.8 = (f32[8,256]{1,0:T(8,128)S(1)}, f32[8,256]{1,0:T(8,128)S(1)}, u32[]{:S(2)}, u32[]{:S(2)}) collective-permute-start(f32[8,256]{1,0:T(8,128)S(1)} %get-tuple-element.62.x_ref), channel_id=1, source_target_pairs={{0,1},{1,0},{2,3},{3,2},{4,5},{5,4},{6,7},{7,6},{8,9},{9,8},{10,11... | collective-permute-start | bytes 24584 | tf_op jit(solution)/shard_map/ppermute | solution.py:71
  35.6 4.6 %collective-permute-start.9 = (f32[8,256]{1,0:T(8,128)S(1)}, f32[8,256]{1,0:T(8,128)S(1)}, u32[]{:S(2)}, u32[]{:S(2)}) collective-permute-start(f32[8,256]{1,0:T(8,128)S(1)} %join.1.x_ref), channel_id=1, source_target_pairs={{0,2},{1,3},{2,0},{3,1},{4,6},{5,7},{6,4},{7,5},{8,10},{9,11},{10,... | collective-permute-start | bytes 24584 | tf_op jit(solution)/shard_map/ppermute | solution.py:71
  41.1 1.3 %collective-permute-start.10 = (f32[4,5120]{1,0:T(4,128)S(1)}, f32[4,5120]{1,0:T(4,128)S(1)}, u32[]{:S(2)}, u32[]{:S(2)}) collective-permute-start(f32[4,5120]{1,0:T(4,128)S(1)} %get-tuple-element.66.x_ref), channel_id=1, source_target_pairs={{0,4},{4,0},{8,12},{12,8},{16,20},{20,16},{24,28},{28,24},{1,5},{5... | collective-permute-start | bytes 245768 | tf_op jit(solution)/shard_map/ppermute | solution.py:71
  42.5 9.8 %collective-permute-start.11 = (bf16[1,64,2560]{2,1,0:T(8,128)(2,1)S(1)}, bf16[1,64,2560]{2,1,0:T(8,128)(2,1)S(1)}, u32[]{:S(2)}, u32[]{:S(2)}) collective-permute-start(bf16[1,64,2560]{2,1,0:T(8,128)(2,1)S(1)} %get-tuple-element.67), channel_id=1, source_target_pairs={{0,2},{2,3},{3,1},{1,0},{4,6},{6,7},{7,5},{5,4},{8,10},{10,11},{11... | collective-permute-start | bytes 983048 | tf_op jit(solution)/shard_map/ppermute | solution.py:61
  44.1 0.7 collective-permute-start.12
  44.8 0.7 collective-permute-start.13
  52.3 0.7 collective-permute-start.14
  53.0 0.7 collective-permute-start.15
  53.7 15.1 %collective-permute-start.16 = (f32[4,5120]{1,0:T(4,128)S(1)}, f32[4,5120]{1,0:T(4,128)S(1)}, u32[]{:S(2)}, u32[]{:S(2)}) collective-permute-start(f32[4,5120]{1,0:T(4,128)S(1)} %add.13.mine_ref), channel_id=1, source_target_pairs={{4,0},{12,8},{20,16},{28,24},{5,1},{13,9},{21,17},{29,25},{6,2},{1... | collective-permute-start | bytes 245768 | tf_op jit(solution)/shard_map/ppermute | solution.py:426
  68.8 7.0 %collective-permute-start.20 = (bf16[1,64,1280]{2,1,0:T(8,128)(2,1)S(1)}, bf16[1,64,1280]{2,1,0:T(8,128)(2,1)S(1)}, u32[]{:S(2)}, u32[]{:S(2)}) collective-permute-start(bf16[1,64,1280]{2,1,0:T(8,128)(2,1)S(1)} %get-tuple-element.83), channel_id=1, source_target_pairs={{0,2},{2,3},{3,1},{1,0},{4,6},{6,7},{7,5},{5,4},{8,10},{10,11},{11... | collective-permute-start | bytes 491528 | tf_op jit(solution)/shard_map/ppermute | solution.py:61
  69.6 9.7 %collective-permute-start.19 = (bf16[1,64,1280]{2,1,0:T(8,128)(2,1)S(1)}, bf16[1,64,1280]{2,1,0:T(8,128)(2,1)S(1)}, u32[]{:S(2)}, u32[]{:S(2)}) collective-permute-start(bf16[1,64,1280]{2,1,0:T(8,128)(2,1)S(1)} %get-tuple-element.82), channel_id=1, source_target_pairs={{0,2},{2,3},{3,1},{1,0},{4,6},{6,7},{7,5},{5,4},{8,10},{10,11},{11... | collective-permute-start | bytes 491528 | tf_op jit(solution)/shard_map/ppermute | solution.py:61
  71.8 11.0 %collective-permute-start.18 = (bf16[1,64,1280]{2,1,0:T(8,128)(2,1)S(1)}, bf16[1,64,1280]{2,1,0:T(8,128)(2,1)S(1)}, u32[]{:S(2)}, u32[]{:S(2)}) collective-permute-start(bf16[1,64,1280]{2,1,0:T(8,128)(2,1)S(1)} %get-tuple-element.81), channel_id=1, source_target_pairs={{0,2},{2,3},{3,1},{1,0},{4,6},{6,7},{7,5},{5,4},{8,10},{10,11},{11... | collective-permute-start | bytes 491528 | tf_op jit(solution)/shard_map/ppermute | solution.py:61
  72.3 13.3 %collective-permute-start.17 = (bf16[1,64,1280]{2,1,0:T(8,128)(2,1)S(1)}, bf16[1,64,1280]{2,1,0:T(8,128)(2,1)S(1)}, u32[]{:S(2)}, u32[]{:S(2)}) collective-permute-start(bf16[1,64,1280]{2,1,0:T(8,128)(2,1)S(1)} %get-tuple-element.80), channel_id=1, source_target_pairs={{0,2},{2,3},{3,1},{1,0},{4,6},{6,7},{7,5},{5,4},{8,10},{10,11},{11... | collective-permute-start | bytes 491528 | tf_op jit(solution)/shard_map/ppermute | solution.py:61

commit v11 on v10

--- a/solution.py
+++ b/solution.py
@@ -71,32 +71,35 @@
     return lax.ppermute(x, axis, [(i, i ^ bit) for i in range(n)])
 
 
-def swap_odd(x, m, n, dp_bit, tensor_bit):
-    pairs = [
-        (i * n + t, (i ^ dp_bit) * n + (t ^ tensor_bit)) for i in range(1, m, 2) for t in range(n)
-    ]
-    return lax.ppermute(x, ("dp", "tensor"), pairs)
-
-
 def bits(n):
     assert n & (n - 1) == 0
     return [1 << i for i in range(n.bit_length() - 1)]
 
 
-def token_factor_kernel(w_hbm, g_hbm, gw_ref, terms_ref, w, g, w3, sems):
+def first_kernel(g_hbm, out_ref, sem):
+    copy = pltpu.make_async_copy(g_hbm.at[:, :, pl.ds(0, out_ref.shape[2])], out_ref, sem)
+    copy.start()
+    copy.wait()
+
+
+def token_factor_kernel(w_hbm, g_hbm, a_ref, gw_ref, terms_ref, b_ref, w, w3, sems):
     rank = w.shape[0]
+    part = a_ref.shape[2]
+    rest = b_ref.shape[2]
     copies = [
         pltpu.make_async_copy(w_hbm, w, sems.at[0]),
-        pltpu.make_async_copy(g_hbm, g, sems.at[1]),
+        pltpu.make_async_copy(g_hbm.at[:, :, pl.ds(part, rest)], b_ref, sems.at[1]),
     ]
     for copy in copies:
         copy.start()
     copies[0].wait()
     terms = stack3(w[...] * SHRINK, w3)
     terms_ref[...] = terms
+    total = dot(terms[:, :part], a_ref[0], (1, 1))
     copies[1].wait()
+    total += dot(terms[:, part:], b_ref[0], (1, 1))
     gw_ref[...] = jnp.zeros_like(gw_ref)
-    gw_ref[0:rank, 0 : g.shape[1]] = sum3(dot(terms, g[0], (1, 1)), rank)
+    gw_ref[0:rank, 0 : total.shape[1]] = sum3(total, rank)
 
 
 def cut_kernel(x_ref, *refs):
@@ -216,7 +219,7 @@
     return rows
 
 
-def right_kernel(n, p_ref, r_ref, g_ref, x_ref, y_ref, ortho_ref, out_ref, z, z3):
+def right_kernel(n, p_ref, r_ref, g_ref, x_ref, y_ref, ortho_ref, keep_ref, send_ref, z, z3, outbox):
     rank = p_ref.shape[0]
     tok = g_ref.shape[1]
     products, gram, top = joined(x_ref[...], y_ref[...], rank)
@@ -228,11 +231,15 @@
     for i, row in enumerate(solve_rows(inv, p_ref[...], rank)):
         ortho_ref[i : i + 1, :] = row
     terms = stack3(z[lax.axis_index("tensor")], z3)
-    for c in range(r_ref.shape[1] // BLOCK):
-        cols = slice(c * BLOCK, (c + 1) * BLOCK)
+    half = keep_ref.shape[1]
+    core = lax.rem(lax.axis_index("dp"), 2)
+    for h in range(2):
+        cols = slice(h * half, (h + 1) * half)
         fresh = sum3(dot(terms, g_ref[0, :, cols], (1, 0)), rank) * ROOM
         for i, row in enumerate(solve_rows(inv, r_ref[:, cols], rank)):
-            out_ref[i : i + 1, cols] = row + fresh[i : i + 1, :]
+            outbox[h, i : i + 1, :] = row + fresh[i : i + 1, :]
+    keep_ref[...] = outbox[core]
+    send_ref[...] = outbox[1 - core]
 
 
 def add_kernel(x_ref, y_ref, out_ref):
@@ -243,18 +250,13 @@
 RIGHT_TERMS = (0, 1, 0, 2, 0, 1)
 
 
-def factor_kernel(scale, ortho_ref, mine_ref, other_ref, whole_ref, left_ref, right_ref, left, right):
-    rank = mine_ref.shape[0]
+def factor_kernel(scale, ortho_ref, mine_ref, other_ref, whole_ref, left_ref, right_ref, inbox, left, right):
+    rank, half = mine_ref.shape
     core = lax.rem(lax.axis_index("dp"), 2)
-
-    @pl.when(core == 1)
-    def _():
-        whole_ref[...] = mine_ref[...] * scale
-
-    @pl.when(core == 0)
-    def _():
-        whole_ref[...] = other_ref[...] * scale
-
+    inbox[core] = mine_ref[...]
+    inbox[1 - core] = other_ref[...]
+    for h in range(2):
+        whole_ref[:, h * half : (h + 1) * half] = inbox[h] * scale
     for terms, x, ref in (
         (LEFT_TERMS, ortho_ref[...], left),
         (RIGHT_TERMS, whole_ref[...], right),
@@ -350,21 +352,21 @@
     def step(x):
         return ring_step(x, "tensor", n)
 
-    wide = width // 4
-    narrow = width // 2 - wide
-    ring = [out_grads, step(out_grads)]
-
-    gw, w_terms = call(
+    unit = width // 10
+    wide, parts = 3 * unit, [4 * unit, 3 * unit]
+    half = width // 2
+    first = call(first_kernel, sds((1, tok, wide), BF16), [dma(())], "first", [hbm])(pin(out_grads))
+    ring_a = [first, step(first)]
+
+    gw, w_terms, other = call(
         token_factor_kernel,
-        [sds((8, 128), F32), sds((3 * rank, width), BF16)],
-        [
-            pltpu.VMEM((rank, width), F32),
-            pltpu.VMEM((1, tok, width), BF16),
-            pltpu.VMEM((3 * rank, width), F32),
-            dma((2,)),
-        ],
-        "token_factor", [hbm, hbm],
-    )(pin(w), pin(out_grads))
+        [sds((8, 128), F32), sds((3 * rank, width), BF16), sds((1, tok, width - wide), BF16)],
+        [pltpu.VMEM((rank, width), F32), pltpu.VMEM((3 * rank, width), F32), dma((2,))],
+        "token_factor", [hbm, hbm, vmem],
+    )(pin(w), pin(out_grads), first)
+    gws = exchange([gw] * n, "tensor", n)
+    (ring_a[1], other, w_terms), gws[1] = after((ring_a[1], other, w_terms), gws[1])
+    ring_b = [other, step(other)]
     ew, error_v = call(
         error_left_kernel,
         [sds((rank, rows), F32), sds((1, rows, width), BF16)],
@@ -372,18 +374,17 @@
         "error_left", [vmem, hbm], 4.6e9,
     )(w_terms, pin(error_buffer))
 
-    gw, ew = after(gw, ew)
-    gws = exchange([gw] * n, "tensor", n)
-    ring[1], gws = after(ring[1], gws)
-    x1, y1 = cut(ring[1], [2 * wide, 2 * narrow])
-    xs, ys = [x1, step(x1)], [y1]
     left = call(
         left_kernel, sds((rank, rows), F32), [pltpu.VMEM((3 * rank, tok), F32)], "left"
     )(activations, ew, *gws)
     for bit in bits(m)[:-1]:
         left = add(left, swap(left, "dp", m, bit))
-    xs[1], last = after(xs[1], swap(left, "dp", m, bits(m)[-1]))
-
+        if bit == 1:
+            held, left = after(ring_a[1], left)
+            ring_a.append(step(held))
+    (ring_a[2], ring_b[1]), last = after(
+        (ring_a[2], ring_b[1]), swap(left, "dp", m, bits(m)[-1])
+    )
     mean, msg = call(
         functools.partial(mean_kernel, 1.0 / (SHRINK * m)),
         [sds((rank, rows), F32), sds((2 * rank, tokens), F32)],
@@ -405,39 +406,43 @@
         "error_right", None, 1.2e9,
     )(mean, error_v)
 
-    ortho, total = call(
+    ortho, keep, send = call(
         functools.partial(right_kernel, n),
-        [sds((rank, rows), F32), sds((rank, width), F32)],
-        [pltpu.VMEM((n, rank, tok), F32), pltpu.VMEM((3 * rank, tok), F32)],
+        [sds((rank, rows), F32), sds((rank, half), F32), sds((rank, half), F32)],
+        [
+            pltpu.VMEM((n, rank, tok), F32),
+            pltpu.VMEM((3 * rank, tok), F32),
+            pltpu.VMEM((2, rank, half), F32),
+        ],
         "right",
     )(mean, right_raw, out_grads, *msgs)
-    total = add(total, swap(total, "dp", m, 1))
-    for _ in range(3, n):
-        last, total = after(ys[-1], total)
-        ys.append(step(last))
+    total = add(keep, swap(send, "dp", m, 1))
+    held, total = after(ring_b[1], total)
+    ring_b.append(step(held))
+    for bit in bits(m)[1:]:
+        total = add(total, swap(total, "dp", m, bit))
     for _ in range(4, n):
-        last, total = after(xs[-1], total)
-        xs.append(step(last))
-    for bit in bits(m)[1:]:
-        total = add(total, swap_odd(total, m, n, bit, 0))
-    (xs[-1], ys[-1]), total = after((xs[-1], ys[-1]), total)
+        (held_a, held_b), total = after((ring_a[-1], ring_b[-1]), total)
+        ring_a.append(step(held_a))
+        ring_b.append(step(held_b))
+    ring_b[-1], total = after(ring_b[-1], total)
     for bit in bits(n):
-        total = add(total, swap_odd(total, m, n, 0, bit))
-    other = lax.ppermute(total, "dp", [(i, i - 1) for i in range(1, m, 2)])
-    xa, xb = cut(xs[-1], [wide, wide])
-    (xa, xb), (total, other) = after((xa, xb), (total, other))
-    xa, xb = step(xa), step(xb)
+        total = add(total, swap(total, "tensor", n, bit))
+    (held_a, held), total = after((ring_a[-1], ring_b[-1]), total)
+    ring_a.append(step(held_a))
+    newest = [step(x) for x in cut(held, parts)]
 
     terms = len(LEFT_TERMS) * rank
     whole, left_terms, right_terms = call(
         functools.partial(factor_kernel, 1.0 / m),
         [sds((rank, width), F32), sds((rows, terms), BF16), sds((terms, width), BF16)],
         [
+            pltpu.VMEM((2, rank, half), F32),
             pltpu.VMEM((terms, rows), F32),
             pltpu.VMEM((terms, width), F32),
         ],
         "factor",
-    )(ortho, total, other)
+    )(ortho, total, swap(total, "dp", m, 1))
 
     acts = call(
         functools.partial(acts_kernel, n),
@@ -445,19 +450,10 @@
         [pltpu.VMEM((tokens, rows), BF16)],
         "acts",
     )(activations)
-    last, right_terms = after(ys[-1], right_terms)
-    ya, yb = cut(last, [narrow, narrow])
-    pieces = []
-    at = 0
-    for part, base, held, newest in (
-        (wide, 0, xs, xa),
-        (wide, 0, xs, xb),
-        (narrow, 2 * wide, ys, step(ya)),
-        (narrow, 2 * wide, ys, step(yb)),
-    ):
-        slots = ring + held[1 : n - 2] + [newest]
-        bases = [0, 0] + [base] * (n - 3) + [at]
-        pieces.append((at, part, slots, bases))
+    pieces = [(0, wide, [out_grads, *ring_a[1:]], [0] * n)]
+    at = wide
+    for part, x in zip(parts, newest):
+        pieces.append((at, part, [out_grads, *ring_b[1:], x], [0] + [wide] * (n - 2) + [at]))
         at += part
 
     outs = ()

time: 88.3 us -> 81.9 us (0.928)
  waiting for transfers between devices: 41.5 us -> 30.1 us
  starting transfers between devices: 26.5 us -> 31.8 us
    ppermute x5 -> x0, waiting for transfers between devices: 13.7 us -> none  [the longest x1 13.7 us: per_device(): other = lax.ppermute(total, 'dp', [(i, i - 1) for i in range(1, m, 2)])]
    ppermute x6 -> x11, starting transfers between devices: 5.68 us -> 15.3 us  [swap(): return lax.ppermute(x, axis, [(i, i ^ bit) for i in range(n)])]
    ppermute x6 -> x11, waiting for transfers between devices: 11.5 us -> 20.2 us  [swap(): return lax.ppermute(x, axis, [(i, i ^ bit) for i in range(n)])]
    ppermute x3, waiting for transfers between devices: 6.01 us -> 1.58 us  [exchange(): lax.ppermute(pieces[k], axis, [(i, (i + k) % n) for i in range(n)])]
    ppermute x5 -> x0, starting transfers between devices: 3.93 us -> none  [the longest x4 2.64 us: swap_odd(): return lax.ppermute(x, ('dp', 'tensor'), pairs)]
    ppermute x7, waiting for transfers between devices: 10.3 us -> 8.32 us  [ring_step(): lax.ppermute(x, axis, [(ring[p], ring[(p + 1) % n]) for p in range(n)])]
    pallas_call x0 -> x1, Pallas kernels: none -> 0.94 us  [per_device(): call(first_kernel, sds((1, tok, wide), BF16), [dma(())], 'first', [hbm])]
    pallas_call x4 -> x3, Pallas kernels: 9.88 us -> 9.09 us  [per_device(): pl.pallas_call(functools.partial(final_kernel, at, part, bases), in_specs...]
  transfers between devices with their start and end apart: 21 -> 21, of which waited for: 13 -> 15; matrix products, arithmetic and copies ran while one was open for 0% -> 0% of each run, Pallas kernels for 17% -> 17%
where the time goes in v11:
time: 81.9 us; the launch traced here: 81.8 us
  starting transfers between devices  31.8 us (39%)
  waiting for transfers between devices  30.1 us (37%)
  Pallas kernels  19 us (23%)
    ppermute x11, waiting for transfers between devices, swap(): return lax.ppermute(x, axis, [(i, i ^ bit) for i in range(n)])  20.2 us
    ppermute x11, starting transfers between devices, swap(): return lax.ppermute(x, axis, [(i, i ^ bit) for i in range(n)])  15.3 us
    ppermute x7, starting transfers between devices, ring_step(): lax.ppermute(x, axis, [(ring[p], ring[(p + 1) % n]) for p in range(n)])  12.7 us
    pallas_call x3, Pallas kernels, per_device(): pl.pallas_call(functools.partial(final_kernel, at, part, bases), in_specs...  9.09 us
    ppermute x7, waiting for transfers between devices, ring_step(): lax.ppermute(x, axis, [(ring[p], ring[(p + 1) % n]) for p in range(n)])  8.32 us
    pallas_call x1, Pallas kernels, per_device(): call(error_left_kernel, [sds((rank, rows), F32), sds((1, rows, width), BF...  4.14 us
    ppermute x3, starting transfers between devices, exchange(): lax.ppermute(pieces[k], axis, [(i, (i + k) % n) for i in range(n)])  3.87 us
  transfers between devices with their start and end apart: 21, of which 15 were waited for; matrix products, arithmetic and copies ran while one was open for 0% of the time, Pallas kernels for 17%

profile of v11, /device:TPU:0, one launch (start us, length us, event | category | flops | bytes accessed | tf_op | source)
XLA Modules:
  0.0 81.8 jit_solution(7478409938700985913)
XLA Ops:
  1.6 4.1 %collective-permute-start = (bf16[1,64,1536]{2,1,0:T(8,128)(2,1)S(1)}, bf16[1,64,1536]{2,1,0:T(8,128)(2,1)S(1)}, u32[]{:S(2)}, u32[]{:S(2)}) collective-permute-start(bf16[1,64,1536]{2,1,0:T(8,128)(2,1)S(1)} %first.1.a_ref), channel_id=1, source_target_pairs={{0,2},{2,3},{3,1},{1,0},{4,6},{6,7},{7,5},{5,4},{8,10},{10,11},{11... | collective-permute-start | bytes 589832 | tf_op jit(solution)/shard_map/ppermute | solution.py:61
  7.1 3.8 %collective-permute-start.3 = (f32[8,128]{1,0:T(8,128)S(1)}, f32[8,128]{1,0:T(8,128)S(1)}, u32[]{:S(2)}, u32[]{:S(2)}) collective-permute-start(f32[8,128]{1,0:T(8,128)S(1)} %get-tuple-element.42.refs_0_), channel_id=1, source_target_pairs={{0,3},{1,0},{2,1},{3,2},{4,7},{5,4},{6,5},{7,6},{8,11},{9,8},{10,9... | collective-permute-start | bytes 12296 | tf_op jit(solution)/shard_map/ppermute | solution.py:66
  10.9 1.6 %collective-permute-done.1.refs_1_ = f32[8,128]{1,0:T(8,128)S(1)} collective-permute-done((f32[8,128]{1,0:T(8,128)S(1)}, f32[8,128]{1,0:T(8,128)S(1)}, u32[]{:S(2)}, u32[]{:S(2)}) %collective-permute-start.1) | collective-permute-done | bytes 4128 | tf_op jit(solution)/shard_map/ppermute | solution.py:66
  13.9 4.1 %error_left.1 = (f32[4,768]{1,0:T(4,128)S(1)}, bf16[1,768,5120]{2,1,0:T(8,128)(2,1)S(1)}) custom-call(bf16[12,5120]{1,0:T(8,128)(2,1)S(1)} %get-tuple-element.44.terms_ref, bf16[1,768,5120]{2,1,0:T(8,128)(2,1)} %e_hbm.1), custom_call_target="tpu_custom_call" | custom-call | flops 4600000000 | bytes 1 | tf_op jit(solution)/shard_map/error_left/pallas_call | solution.py:370
  21.1 2.2 %collective-permute-done.5.y_ref = f32[4,768]{1,0:T(4,128)S(1)} collective-permute-done((f32[4,768]{1,0:T(4,128)S(1)}, f32[4,768]{1,0:T(4,128)S(1)}, u32[]{:S(2)}, u32[]{:S(2)}) %collective-permute-start.5) | collective-permute-done | bytes 12320 | tf_op jit(solution)/shard_map/ppermute | solution.py:71
  23.3 1.5 %collective-permute-start.8 = (f32[4,768]{1,0:T(4,128)S(1)}, f32[4,768]{1,0:T(4,128)S(1)}, u32[]{:S(2)}, u32[]{:S(2)}) collective-permute-start(f32[4,768]{1,0:T(4,128)S(1)} %add.8.x_ref), channel_id=1, source_target_pairs={{0,16},{4,20},{8,24},{12,28},{16,0},{20,4},{24,8},{28,12},{1,17},{... | collective-permute-start | bytes 36872 | tf_op jit(solution)/shard_map/ppermute | solution.py:71
  24.8 2.2 %collective-permute-done.8.y_ref = f32[4,768]{1,0:T(4,128)S(1)} collective-permute-done((f32[4,768]{1,0:T(4,128)S(1)}, f32[4,768]{1,0:T(4,128)S(1)}, u32[]{:S(2)}, u32[]{:S(2)}) %collective-permute-start.8) | collective-permute-done | bytes 12320 | tf_op jit(solution)/shard_map/ppermute | solution.py:71
  29.3 2.4 %collective-permute-done.9.y_ref = f32[8,256]{1,0:T(8,128)S(1)} collective-permute-done((f32[8,256]{1,0:T(8,128)S(1)}, f32[8,256]{1,0:T(8,128)S(1)}, u32[]{:S(2)}, u32[]{:S(2)}) %collective-permute-start.9) | collective-permute-done | bytes 8224 | tf_op jit(solution)/shard_map/ppermute | solution.py:71
  31.8 2.5 %collective-permute-start.10 = (f32[8,256]{1,0:T(8,128)S(1)}, f32[8,256]{1,0:T(8,128)S(1)}, u32[]{:S(2)}, u32[]{:S(2)}) collective-permute-start(f32[8,256]{1,0:T(8,128)S(1)} %join.1.x_ref), channel_id=1, source_target_pairs={{0,2},{1,3},{2,0},{3,1},{4,6},{5,7},{6,4},{7,5},{8,10},{9,11},{10,... | collective-permute-start | bytes 24584 | tf_op jit(solution)/shard_map/ppermute | solution.py:71
  38.6 2.4 %collective-permute-start.12 = (bf16[1,64,3584]{2,1,0:T(8,128)(2,1)S(1)}, bf16[1,64,3584]{2,1,0:T(8,128)(2,1)S(1)}, u32[]{:S(2)}, u32[]{:S(2)}) collective-permute-start(bf16[1,64,3584]{2,1,0:T(8,128)(2,1)S(1)} %collective-permute-done.7.refs_1_), channel_id=1, source_target_pairs={{0,2},{2,3},{3,1},{1,0},{4,6},{6,7},{7,5},{5,4},{8,10},{10,11},{11... | collective-permute-start | bytes 1376264 | tf_op jit(solution)/shard_map/ppermute | solution.py:61
  42.5 2.5 %collective-permute-done.13.y_ref = f32[4,2560]{1,0:T(4,128)S(1)} collective-permute-done((f32[4,2560]{1,0:T(4,128)S(1)}, f32[4,2560]{1,0:T(4,128)S(1)}, u32[]{:S(2)}, u32[]{:S(2)}) %collective-permute-start.13) | collective-permute-done | bytes 40992 | tf_op jit(solution)/shard_map/ppermute | solution.py:71
  45.0 1.5 %collective-permute-start.14 = (f32[4,2560]{1,0:T(4,128)S(1)}, f32[4,2560]{1,0:T(4,128)S(1)}, u32[]{:S(2)}, u32[]{:S(2)}) collective-permute-start(f32[4,2560]{1,0:T(4,128)S(1)} %add.10.x_ref), channel_id=1, source_target_pairs={{0,16},{4,20},{8,24},{12,28},{16,0},{20,4},{24,8},{28,12},{1,17},{... | collective-permute-start | bytes 122888 | tf_op jit(solution)/shard_map/ppermute | solution.py:71
  46.6 2.5 %collective-permute-done.14.y_ref = f32[4,2560]{1,0:T(4,128)S(1)} collective-permute-done((f32[4,2560]{1,0:T(4,128)S(1)}, f32[4,2560]{1,0:T(4,128)S(1)}, u32[]{:S(2)}, u32[]{:S(2)}) %collective-permute-start.14) | collective-permute-done | bytes 40992 | tf_op jit(solution)/shard_map/ppermute | solution.py:71
  49.1 2.2 %collective-permute-done.12.x_ref.refs_2_ = bf16[1,64,3584]{2,1,0:T(8,128)(2,1)S(1)} collective-permute-done((bf16[1,64,3584]{2,1,0:T(8,128)(2,1)S(1)}, bf16[1,64,3584]{2,1,0:T(8,128)(2,1)S(1)}, u32[]{:S(2)}, u32[]{:S(2)}) %collective-permute-start.12) | collective-permute-done | bytes 458784 | tf_op jit(solution)/shard_map/ppermute | solution.py:61
  51.2 2.1 %collective-permute-start.15 = (f32[4,2560]{1,0:T(4,128)S(1)}, f32[4,2560]{1,0:T(4,128)S(1)}, u32[]{:S(2)}, u32[]{:S(2)}) collective-permute-start(f32[4,2560]{1,0:T(4,128)S(1)} %add.11.x_ref), channel_id=1, source_target_pairs={{0,1},{1,0},{2,3},{3,2},{4,5},{5,4},{6,7},{7,6},{8,9},{9,8},{10,11... | collective-permute-start | bytes 122888 | tf_op jit(solution)/shard_map/ppermute | solution.py:71
  53.3 2.0 %collective-permute-done.15.y_ref = f32[4,2560]{1,0:T(4,128)S(1)} collective-permute-done((f32[4,2560]{1,0:T(4,128)S(1)}, f32[4,2560]{1,0:T(4,128)S(1)}, u32[]{:S(2)}, u32[]{:S(2)}) %collective-permute-start.15) | collective-permute-done | bytes 40992 | tf_op jit(solution)/shard_map/ppermute | solution.py:71
  55.3 3.2 %collective-permute-start.16 = (f32[4,2560]{1,0:T(4,128)S(1)}, f32[4,2560]{1,0:T(4,128)S(1)}, u32[]{:S(2)}, u32[]{:S(2)}) collective-permute-start(f32[4,2560]{1,0:T(4,128)S(1)} %add.12.x_ref), channel_id=1, source_target_pairs={{0,2},{1,3},{2,0},{3,1},{4,6},{5,7},{6,4},{7,5},{8,10},{9,11},{10,... | collective-permute-start | bytes 122888 | tf_op jit(solution)/shard_map/ppermute | solution.py:71
  58.5 2.0 %collective-permute-done.16.y_ref = f32[4,2560]{1,0:T(4,128)S(1)} collective-permute-done((f32[4,2560]{1,0:T(4,128)S(1)}, f32[4,2560]{1,0:T(4,128)S(1)}, u32[]{:S(2)}, u32[]{:S(2)}) %collective-permute-start.16) | collective-permute-done | bytes 40992 | tf_op jit(solution)/shard_map/ppermute | solution.py:71
  60.6 3.0 %collective-permute-start.19 = (bf16[1,64,2048]{2,1,0:T(8,128)(2,1)S(1)}, bf16[1,64,2048]{2,1,0:T(8,128)(2,1)S(1)}, u32[]{:S(2)}, u32[]{:S(2)}) collective-permute-start(bf16[1,64,2048]{2,1,0:T(8,128)(2,1)S(1)} %get-tuple-element.68), channel_id=1, source_target_pairs={{0,2},{2,3},{3,1},{1,0},{4,6},{6,7},{7,5},{5,4},{8,10},{10,11},{11... | collective-permute-start | bytes 786440 | tf_op jit(solution)/shard_map/ppermute | solution.py:61
  63.6 1.7 %collective-permute-start.18 = (bf16[1,64,1536]{2,1,0:T(8,128)(2,1)S(1)}, bf16[1,64,1536]{2,1,0:T(8,128)(2,1)S(1)}, u32[]{:S(2)}, u32[]{:S(2)}) collective-permute-start(bf16[1,64,1536]{2,1,0:T(8,128)(2,1)S(1)} %get-tuple-element.67), channel_id=1, source_target_pairs={{0,2},{2,3},{3,1},{1,0},{4,6},{6,7},{7,5},{5,4},{8,10},{10,11},{11... | collective-permute-start | bytes 589832 | tf_op jit(solution)/shard_map/ppermute | solution.py:61
  67.2 5.4 %collective-permute-done.20.refs_3_ = bf16[1,64,1536]{2,1,0:T(8,128)(2,1)S(1)} collective-permute-done((bf16[1,64,1536]{2,1,0:T(8,128)(2,1)S(1)}, bf16[1,64,1536]{2,1,0:T(8,128)(2,1)S(1)}, u32[]{:S(2)}, u32[]{:S(2)}) %collective-permute-start.20) | collective-permute-done | bytes 196640 | tf_op jit(solution)/shard_map/ppermute | solution.py:61
  72.7 2.8 %rebuild.3 = (bf16[768,5120]{1,0:T(8,128)(2,1)}, bf16[1,768,5120]{2,1,0:T(8,128)(2,1)}) custom-call(bf16[768,256]{1,0:T(8,128)(2,1)S(1)} %acts.1.acts_ref, bf16[768,24]{1,0:T(8,128)(2,1)S(1)} %get-tuple-element.64.left_ref, bf16[24,5120]{1,0:T(8,128)(2,1)S(1)} %get-tuple-element.65.right_ref, bf16[1,768,5120]{2,1,0:T(8,128)(2,1)S(1)} %get-tuple-element.52.e_ref, ...), custom_call_target="tpu_custom_call" | custom-call | flops 1 | bytes 1 | tf_op jit(solution)/shard_map/rebuild/pallas_call | solution.py:461
  75.5 3.5 %rebuild.4 = (bf16[768,5120]{1,0:T(8,128)(2,1)}, bf16[1,768,5120]{2,1,0:T(8,128)(2,1)}) custom-call(bf16[768,256]{1,0:T(8,128)(2,1)S(1)} %acts.1.acts_ref, bf16[768,24]{1,0:T(8,128)(2,1)S(1)} %get-tuple-element.64.left_ref, bf16[24,5120]{1,0:T(8,128)(2,1)S(1)} %get-tuple-element.65.right_ref, ...), custom_call_target="tpu_custom_call", output_to_operand_aliasing={{0}: (8, {}), {1}: (9, {})} | custom-call | flops 1 | bytes 1 | tf_op jit(solution)/shard_map/rebuild/pallas_call | solution.py:461
  79.0 2.8 %rebuild.5 = (bf16[768,5120]{1,0:T(8,128)(2,1)}, bf16[1,768,5120]{2,1,0:T(8,128)(2,1)}) custom-call(bf16[768,256]{1,0:T(8,128)(2,1)S(1)} %acts.1.acts_ref, bf16[768,24]{1,0:T(8,128)(2,1)S(1)} %get-tuple-element.64.left_ref, bf16[24,5120]{1,0:T(8,128)(2,1)S(1)} %get-tuple-element.65.right_ref, ...), custom_call_target="tpu_custom_call", output_to_operand_aliasing={{0}: (8, {}), {1}: (9, {})} | custom-call | flops 1 | bytes 1 | tf_op jit(solution)/shard_map/rebuild/pallas_call | solution.py:461
  (43 shorter events, 17.0 us)
Async XLA Ops:
  1.6 10.9 %collective-permute-start = (bf16[1,64,1536]{2,1,0:T(8,128)(2,1)S(1)}, bf16[1,64,1536]{2,1,0:T(8,128)(2,1)S(1)}, u32[]{:S(2)}, u32[]{:S(2)}) collective-permute-start(bf16[1,64,1536]{2,1,0:T(8,128)(2,1)S(1)} %first.1.a_ref), channel_id=1, source_target_pairs={{0,2},{2,3},{3,1},{1,0},{4,6},{6,7},{7,5},{5,4},{8,10},{10,11},{11... | collective-permute-start | bytes 589832 | tf_op jit(solution)/shard_map/ppermute | solution.py:61
  7.0 5.5 %collective-permute-start.1 = (f32[8,128]{1,0:T(8,128)S(1)}, f32[8,128]{1,0:T(8,128)S(1)}, u32[]{:S(2)}, u32[]{:S(2)}) collective-permute-start(f32[8,128]{1,0:T(8,128)S(1)} %get-tuple-element.42.refs_0_), channel_id=1, source_target_pairs={{0,1},{1,2},{2,3},{3,0},{4,5},{5,6},{6,7},{7,4},{8,9},{9,10},{10,1... | collective-permute-start | bytes 12296 | tf_op jit(solution)/shard_map/ppermute | solution.py:66
  7.1 11.0 %collective-permute-start.3 = (f32[8,128]{1,0:T(8,128)S(1)}, f32[8,128]{1,0:T(8,128)S(1)}, u32[]{:S(2)}, u32[]{:S(2)}) collective-permute-start(f32[8,128]{1,0:T(8,128)S(1)} %get-tuple-element.42.refs_0_), channel_id=1, source_target_pairs={{0,3},{1,0},{2,1},{3,2},{4,7},{5,4},{6,5},{7,6},{8,11},{9,8},{10,9... | collective-permute-start | bytes 12296 | tf_op jit(solution)/shard_map/ppermute | solution.py:66
  10.9 7.2 %collective-permute-start.2 = (f32[8,128]{1,0:T(8,128)S(1)}, f32[8,128]{1,0:T(8,128)S(1)}, u32[]{:S(2)}, u32[]{:S(2)}) collective-permute-start(f32[8,128]{1,0:T(8,128)S(1)} %get-tuple-element.42.refs_0_), channel_id=1, source_target_pairs={{0,2},{1,3},{2,0},{3,1},{4,6},{5,7},{6,4},{7,5},{8,10},{9,11},{10,... | collective-permute-start | bytes 12296 | tf_op jit(solution)/shard_map/ppermute | solution.py:66
  12.5 5.6 %copy-start.1 = (bf16[1,256,768]{2,1,0:T(8,128)(2,1)S(1)}, bf16[1,256,768]{2,1,0:T(8,128)(2,1)}, u32[]{:S(2)}) copy-start(bf16[1,256,768]{2,1,0:T(8,128)(2,1)} %a_ref.5) | copy-start | bytes 1179652
  12.5 15.2 %collective-permute-start.7 = (bf16[1,64,3584]{2,1,0:T(8,128)(2,1)S(1)}, bf16[1,64,3584]{2,1,0:T(8,128)(2,1)S(1)}, u32[]{:S(2)}, u32[]{:S(2)}) collective-permute-start(bf16[1,64,3584]{2,1,0:T(8,128)(2,1)S(1)} %get-tuple-element.49), channel_id=1, source_target_pairs={{0,2},{2,3},{3,1},{1,0},{4,6},{6,7},{7,5},{5,4},{8,10},{10,11},{11... | collective-permute-start | bytes 1376264 | tf_op jit(solution)/shard_map/ppermute | solution.py:61
  18.1 18.4 %copy-start = (bf16[1,64,5120]{2,1,0:T(8,128)(2,1)S(1)}, bf16[1,64,5120]{2,1,0:T(8,128)(2,1)}, u32[]{:S(2)}) copy-start(bf16[1,64,5120]{2,1,0:T(8,128)(2,1)} %refs_0_.5) | copy-start | bytes 1966084
  18.3 1.2 %collective-permute-start.4 = (f32[4,768]{1,0:T(4,128)S(1)}, f32[4,768]{1,0:T(4,128)S(1)}, u32[]{:S(2)}, u32[]{:S(2)}) collective-permute-start(f32[4,768]{1,0:T(4,128)S(1)} %left.1.x_ref), channel_id=1, source_target_pairs={{0,4},{4,0},{8,12},{12,8},{16,20},{20,16},{24,28},{28,24},{1,5},{5... | collective-permute-start | bytes 36872 | tf_op jit(solution)/shard_map/ppermute | solution.py:71
  19.5 8.2 %collective-permute-start.6 = (bf16[1,64,1536]{2,1,0:T(8,128)(2,1)S(1)}, bf16[1,64,1536]{2,1,0:T(8,128)(2,1)S(1)}, u32[]{:S(2)}, u32[]{:S(2)}) collective-permute-start(bf16[1,64,1536]{2,1,0:T(8,128)(2,1)S(1)} %collective-permute-done.refs_1_), channel_id=1, source_target_pairs={{0,2},{2,3},{3,1},{1,0},{4,6},{6,7},{7,5},{5,4},{8,10},{10,11},{11... | collective-permute-start | bytes 589832 | tf_op jit(solution)/shard_map/ppermute | solution.py:61
  19.6 3.7 %collective-permute-start.5 = (f32[4,768]{1,0:T(4,128)S(1)}, f32[4,768]{1,0:T(4,128)S(1)}, u32[]{:S(2)}, u32[]{:S(2)}) collective-permute-start(f32[4,768]{1,0:T(4,128)S(1)} %add.7.x_ref), channel_id=1, source_target_pairs={{0,8},{4,12},{8,0},{12,4},{16,24},{20,28},{24,16},{28,20},{1,9},{5... | collective-permute-start | bytes 36872 | tf_op jit(solution)/shard_map/ppermute | solution.py:71
  23.3 3.7 %collective-permute-start.8 = (f32[4,768]{1,0:T(4,128)S(1)}, f32[4,768]{1,0:T(4,128)S(1)}, u32[]{:S(2)}, u32[]{:S(2)}) collective-permute-start(f32[4,768]{1,0:T(4,128)S(1)} %add.8.x_ref), channel_id=1, source_target_pairs={{0,16},{4,20},{8,24},{12,28},{16,0},{20,4},{24,8},{28,12},{1,17},{... | collective-permute-start | bytes 36872 | tf_op jit(solution)/shard_map/ppermute | solution.py:71
  28.0 3.7 %collective-permute-start.9 = (f32[8,256]{1,0:T(8,128)S(1)}, f32[8,256]{1,0:T(8,128)S(1)}, u32[]{:S(2)}, u32[]{:S(2)}) collective-permute-start(f32[8,256]{1,0:T(8,128)S(1)} %get-tuple-element.53.x_ref), channel_id=1, source_target_pairs={{0,1},{1,0},{2,3},{3,2},{4,5},{5,4},{6,7},{7,6},{8,9},{9,8},{10,11... | collective-permute-start | bytes 24584 | tf_op jit(solution)/shard_map/ppermute | solution.py:71
  31.8 4.6 %collective-permute-start.10 = (f32[8,256]{1,0:T(8,128)S(1)}, f32[8,256]{1,0:T(8,128)S(1)}, u32[]{:S(2)}, u32[]{:S(2)}) collective-permute-start(f32[8,256]{1,0:T(8,128)S(1)} %join.1.x_ref), channel_id=1, source_target_pairs={{0,2},{1,3},{2,0},{3,1},{4,6},{5,7},{6,4},{7,5},{8,10},{9,11},{10,... | collective-permute-start | bytes 24584 | tf_op jit(solution)/shard_map/ppermute | solution.py:71
  37.3 1.3 %collective-permute-start.11 = (f32[4,2560]{1,0:T(4,128)S(1)}, f32[4,2560]{1,0:T(4,128)S(1)}, u32[]{:S(2)}, u32[]{:S(2)}) collective-permute-start(f32[4,2560]{1,0:T(4,128)S(1)} %get-tuple-element.58), channel_id=1, source_target_pairs={{0,4},{4,0},{8,12},{12,8},{16,20},{20,16},{24,28},{28,24},{1,5},{5... | collective-permute-start | bytes 122888 | tf_op jit(solution)/shard_map/ppermute | solution.py:71
  38.6 12.6 %collective-permute-start.12 = (bf16[1,64,3584]{2,1,0:T(8,128)(2,1)S(1)}, bf16[1,64,3584]{2,1,0:T(8,128)(2,1)S(1)}, u32[]{:S(2)}, u32[]{:S(2)}) collective-permute-start(bf16[1,64,3584]{2,1,0:T(8,128)(2,1)S(1)} %collective-permute-done.7.refs_1_), channel_id=1, source_target_pairs={{0,2},{2,3},{3,1},{1,0},{4,6},{6,7},{7,5},{5,4},{8,10},{10,11},{11... | collective-permute-start | bytes 1376264 | tf_op jit(solution)/shard_map/ppermute | solution.py:61
  41.0 4.0 %collective-permute-start.13 = (f32[4,2560]{1,0:T(4,128)S(1)}, f32[4,2560]{1,0:T(4,128)S(1)}, u32[]{:S(2)}, u32[]{:S(2)}) collective-permute-start(f32[4,2560]{1,0:T(4,128)S(1)} %add.9.x_ref), channel_id=1, source_target_pairs={{0,8},{4,12},{8,0},{12,4},{16,24},{20,28},{24,16},{28,20},{1,9},{5... | collective-permute-start | bytes 122888 | tf_op jit(solution)/shard_map/ppermute | solution.py:71
  45.0 4.0 %collective-permute-start.14 = (f32[4,2560]{1,0:T(4,128)S(1)}, f32[4,2560]{1,0:T(4,128)S(1)}, u32[]{:S(2)}, u32[]{:S(2)}) collective-permute-start(f32[4,2560]{1,0:T(4,128)S(1)} %add.10.x_ref), channel_id=1, source_target_pairs={{0,16},{4,20},{8,24},{12,28},{16,0},{20,4},{24,8},{28,12},{1,17},{... | collective-permute-start | bytes 122888 | tf_op jit(solution)/shard_map/ppermute | solution.py:71
  51.2 4.1 %collective-permute-start.15 = (f32[4,2560]{1,0:T(4,128)S(1)}, f32[4,2560]{1,0:T(4,128)S(1)}, u32[]{:S(2)}, u32[]{:S(2)}) collective-permute-start(f32[4,2560]{1,0:T(4,128)S(1)} %add.11.x_ref), channel_id=1, source_target_pairs={{0,1},{1,0},{2,3},{3,2},{4,5},{5,4},{6,7},{7,6},{8,9},{9,8},{10,11... | collective-permute-start | bytes 122888 | tf_op jit(solution)/shard_map/ppermute | solution.py:71
  55.3 5.2 %collective-permute-start.16 = (f32[4,2560]{1,0:T(4,128)S(1)}, f32[4,2560]{1,0:T(4,128)S(1)}, u32[]{:S(2)}, u32[]{:S(2)}) collective-permute-start(f32[4,2560]{1,0:T(4,128)S(1)} %add.12.x_ref), channel_id=1, source_target_pairs={{0,2},{1,3},{2,0},{3,1},{4,6},{5,7},{6,4},{7,5},{8,10},{9,11},{10,... | collective-permute-start | bytes 122888 | tf_op jit(solution)/shard_map/ppermute | solution.py:71
  60.6 14.9 %collective-permute-start.19 = (bf16[1,64,2048]{2,1,0:T(8,128)(2,1)S(1)}, bf16[1,64,2048]{2,1,0:T(8,128)(2,1)S(1)}, u32[]{:S(2)}, u32[]{:S(2)}) collective-permute-start(bf16[1,64,2048]{2,1,0:T(8,128)(2,1)S(1)} %get-tuple-element.68), channel_id=1, source_target_pairs={{0,2},{2,3},{3,1},{1,0},{4,6},{6,7},{7,5},{5,4},{8,10},{10,11},{11... | collective-permute-start | bytes 786440 | tf_op jit(solution)/shard_map/ppermute | solution.py:61
  63.6 9.1 %collective-permute-start.20 = (bf16[1,64,1536]{2,1,0:T(8,128)(2,1)S(1)}, bf16[1,64,1536]{2,1,0:T(8,128)(2,1)S(1)}, u32[]{:S(2)}, u32[]{:S(2)}) collective-permute-start(bf16[1,64,1536]{2,1,0:T(8,128)(2,1)S(1)} %collective-permute-done.6.refs_2_), channel_id=1, source_target_pairs={{0,2},{2,3},{3,1},{1,0},{4,6},{6,7},{7,5},{5,4},{8,10},{10,11},{11... | collective-permute-start | bytes 589832 | tf_op jit(solution)/shard_map/ppermute | solution.py:61
  63.6 15.3 %collective-permute-start.18 = (bf16[1,64,1536]{2,1,0:T(8,128)(2,1)S(1)}, bf16[1,64,1536]{2,1,0:T(8,128)(2,1)S(1)}, u32[]{:S(2)}, u32[]{:S(2)}) collective-permute-start(bf16[1,64,1536]{2,1,0:T(8,128)(2,1)S(1)} %get-tuple-element.67), channel_id=1, source_target_pairs={{0,2},{2,3},{3,1},{1,0},{4,6},{6,7},{7,5},{5,4},{8,10},{10,11},{11... | collective-permute-start | bytes 589832 | tf_op jit(solution)/shard_map/ppermute | solution.py:61
  65.3 1.2 %collective-permute-start.17 = (f32[4,2560]{1,0:T(4,128)S(1)}, f32[4,2560]{1,0:T(4,128)S(1)}, u32[]{:S(2)}, u32[]{:S(2)}) collective-permute-start(f32[4,2560]{1,0:T(4,128)S(1)} %add.13.mine_ref), channel_id=1, source_target_pairs={{0,4},{4,0},{8,12},{12,8},{16,20},{20,16},{24,28},{28,24},{1,5},{5... | collective-permute-start | bytes 122888 | tf_op jit(solution)/shard_map/ppermute | solution.py:71

commit v12 on v11

--- a/solution.py
+++ b/solution.py
@@ -69,6 +69,15 @@
 
 def swap(x, axis, n, bit):
     return lax.ppermute(x, axis, [(i, i ^ bit) for i in range(n)])
+
+
+def swap_odd(x, m, n, dp_bit, tensor_bit):
+    pairs = []
+    for i in range(m):
+        for t in range(n):
+            to = (i ^ dp_bit, t ^ tensor_bit) if i % 2 else (i, t)
+            pairs.append((i * n + t, to[0] * n + to[1]))
+    return lax.ppermute(x, ("dp", "tensor"), pairs)
 
 
 def bits(n):
@@ -219,7 +228,7 @@
     return rows
 
 
-def right_kernel(n, p_ref, r_ref, g_ref, x_ref, y_ref, ortho_ref, keep_ref, send_ref, z, z3, outbox):
+def right_kernel(n, p_ref, r_ref, g_ref, x_ref, y_ref, ortho_ref, out_ref, z, z3):
     rank = p_ref.shape[0]
     tok = g_ref.shape[1]
     products, gram, top = joined(x_ref[...], y_ref[...], rank)
@@ -231,15 +240,11 @@
     for i, row in enumerate(solve_rows(inv, p_ref[...], rank)):
         ortho_ref[i : i + 1, :] = row
     terms = stack3(z[lax.axis_index("tensor")], z3)
-    half = keep_ref.shape[1]
-    core = lax.rem(lax.axis_index("dp"), 2)
-    for h in range(2):
-        cols = slice(h * half, (h + 1) * half)
+    for c in range(r_ref.shape[1] // BLOCK):
+        cols = slice(c * BLOCK, (c + 1) * BLOCK)
         fresh = sum3(dot(terms, g_ref[0, :, cols], (1, 0)), rank) * ROOM
         for i, row in enumerate(solve_rows(inv, r_ref[:, cols], rank)):
-            outbox[h, i : i + 1, :] = row + fresh[i : i + 1, :]
-    keep_ref[...] = outbox[core]
-    send_ref[...] = outbox[1 - core]
+            out_ref[i : i + 1, cols] = row + fresh[i : i + 1, :]
 
 
 def add_kernel(x_ref, y_ref, out_ref):
@@ -250,13 +255,18 @@
 RIGHT_TERMS = (0, 1, 0, 2, 0, 1)
 
 
-def factor_kernel(scale, ortho_ref, mine_ref, other_ref, whole_ref, left_ref, right_ref, inbox, left, right):
-    rank, half = mine_ref.shape
+def factor_kernel(scale, ortho_ref, mine_ref, other_ref, whole_ref, left_ref, right_ref, left, right):
+    rank = mine_ref.shape[0]
     core = lax.rem(lax.axis_index("dp"), 2)
-    inbox[core] = mine_ref[...]
-    inbox[1 - core] = other_ref[...]
-    for h in range(2):
-        whole_ref[:, h * half : (h + 1) * half] = inbox[h] * scale
+
+    @pl.when(core == 1)
+    def _():
+        whole_ref[...] = mine_ref[...] * scale
+
+    @pl.when(core == 0)
+    def _():
+        whole_ref[...] = other_ref[...] * scale
+
     for terms, x, ref in (
         (LEFT_TERMS, ortho_ref[...], left),
         (RIGHT_TERMS, whole_ref[...], right),
@@ -352,9 +362,7 @@
     def step(x):
         return ring_step(x, "tensor", n)
 
-    unit = width // 10
-    wide, parts = 3 * unit, [4 * unit, 3 * unit]
-    half = width // 2
+    wide, parts = width // 2, [width // 4] * 2
     first = call(first_kernel, sds((1, tok, wide), BF16), [dma(())], "first", [hbm])(pin(out_grads))
     ring_a = [first, step(first)]
 
@@ -365,13 +373,13 @@
         "token_factor", [hbm, hbm, vmem],
     )(pin(w), pin(out_grads), first)
     gws = exchange([gw] * n, "tensor", n)
-    (ring_a[1], other, w_terms), gws[1] = after((ring_a[1], other, w_terms), gws[1])
+    (ring_a[1], other, w_terms), gws = after((ring_a[1], other, w_terms), gws)
     ring_b = [other, step(other)]
     ew, error_v = call(
         error_left_kernel,
         [sds((rank, rows), F32), sds((1, rows, width), BF16)],
         [dma((rows // 128,))],
-        "error_left", [vmem, hbm], 4.6e9,
+        "error_left", [vmem, hbm],
     )(w_terms, pin(error_buffer))
 
     left = call(
@@ -380,11 +388,9 @@
     for bit in bits(m)[:-1]:
         left = add(left, swap(left, "dp", m, bit))
         if bit == 1:
-            held, left = after(ring_a[1], left)
+            (held, ring_b[1]), left = after((ring_a[1], ring_b[1]), left)
             ring_a.append(step(held))
-    (ring_a[2], ring_b[1]), last = after(
-        (ring_a[2], ring_b[1]), swap(left, "dp", m, bits(m)[-1])
-    )
+    ring_a[2], last = after(ring_a[2], swap(left, "dp", m, bits(m)[-1]))
     mean, msg = call(
         functools.partial(mean_kernel, 1.0 / (SHRINK * m)),
         [sds((rank, rows), F32), sds((2 * rank, tokens), F32)],
@@ -406,29 +412,26 @@
         "error_right", None, 1.2e9,
     )(mean, error_v)
 
-    ortho, keep, send = call(
+    ortho, total = call(
         functools.partial(right_kernel, n),
-        [sds((rank, rows), F32), sds((rank, half), F32), sds((rank, half), F32)],
-        [
-            pltpu.VMEM((n, rank, tok), F32),
-            pltpu.VMEM((3 * rank, tok), F32),
-            pltpu.VMEM((2, rank, half), F32),
-        ],
+        [sds((rank, rows), F32), sds((rank, width), F32)],
+        [pltpu.VMEM((n, rank, tok), F32), pltpu.VMEM((3 * rank, tok), F32)],
         "right",
     )(mean, right_raw, out_grads, *msgs)
-    total = add(keep, swap(send, "dp", m, 1))
+    total = add(total, swap(total, "dp", m, 1))
     held, total = after(ring_b[1], total)
     ring_b.append(step(held))
     for bit in bits(m)[1:]:
-        total = add(total, swap(total, "dp", m, bit))
+        total = add(total, swap_odd(total, m, n, bit, 0))
     for _ in range(4, n):
         (held_a, held_b), total = after((ring_a[-1], ring_b[-1]), total)
         ring_a.append(step(held_a))
         ring_b.append(step(held_b))
     ring_b[-1], total = after(ring_b[-1], total)
     for bit in bits(n):
-        total = add(total, swap(total, "tensor", n, bit))
-    (held_a, held), total = after((ring_a[-1], ring_b[-1]), total)
+        total = add(total, swap_odd(total, m, n, 0, bit))
+    other = swap(total, "dp", m, 1)
+    (held_a, held), other = after((ring_a[-1], ring_b[-1]), other)
     ring_a.append(step(held_a))
     newest = [step(x) for x in cut(held, parts)]
 
@@ -437,12 +440,11 @@
         functools.partial(factor_kernel, 1.0 / m),
         [sds((rank, width), F32), sds((rows, terms), BF16), sds((terms, width), BF16)],
         [
-            pltpu.VMEM((2, rank, half), F32),
             pltpu.VMEM((terms, rows), F32),
             pltpu.VMEM((terms, width), F32),
         ],
         "factor",
-    )(ortho, total, swap(total, "dp", m, 1))
+    )(ortho, total, other)
 
     acts = call(
         functools.partial(acts_kernel, n),

time: 81.9 us -> 89.3 us (1.090)
  waiting for transfers between devices: 30.1 us -> 34 us
  starting transfers between devices: 31.8 us -> 35.2 us
    ppermute x7, waiting for transfers between devices: 8.32 us -> 16.7 us  [ring_step(): lax.ppermute(x, axis, [(ring[p], ring[(p + 1) % n]) for p in range(n)])]
    ppermute x11 -> x7, waiting for transfers between devices: 20.2 us -> 13.1 us  [swap(): return lax.ppermute(x, axis, [(i, i ^ bit) for i in range(n)])]
    ppermute x0 -> x4, starting transfers between devices: none -> 2.64 us  [swap_odd(): return lax.ppermute(x, ('dp', 'tensor'), pairs)]
    ppermute x3, waiting for transfers between devices: 1.58 us -> 4.14 us  [exchange(): lax.ppermute(pieces[k], axis, [(i, (i + k) % n) for i in range(n)])]
    ppermute x11 -> x7, starting transfers between devices: 15.3 us -> 17.8 us  [swap(): return lax.ppermute(x, axis, [(i, i ^ bit) for i in range(n)])]
    ppermute x7, starting transfers between devices: 12.7 us -> 11.1 us  [ring_step(): lax.ppermute(x, axis, [(ring[p], ring[(p + 1) % n]) for p in range(n)])]
  transfers between devices with their start and end apart: 21 -> 21, of which waited for: 15 -> 13; matrix products, arithmetic and copies ran while one was open for 0% -> 0% of each run, Pallas kernels for 17% -> 16%
where the time goes in v12:
time: 89.3 us; the launch traced here: 89.1 us
  starting transfers between devices  35.2 us (39%)
  waiting for transfers between devices  34 us (38%)
  Pallas kernels  19.1 us (21%)
    ppermute x7, starting transfers between devices, swap(): return lax.ppermute(x, axis, [(i, i ^ bit) for i in range(n)])  17.8 us
    ppermute x7, waiting for transfers between devices, ring_step(): lax.ppermute(x, axis, [(ring[p], ring[(p + 1) % n]) for p in range(n)])  16.7 us
    ppermute x7, waiting for transfers between devices, swap(): return lax.ppermute(x, axis, [(i, i ^ bit) for i in range(n)])  13.1 us
    ppermute x7, starting transfers between devices, ring_step(): lax.ppermute(x, axis, [(ring[p], ring[(p + 1) % n]) for p in range(n)])  11.1 us
    pallas_call x3, Pallas kernels, per_device(): pl.pallas_call(functools.partial(final_kernel, at, part, bases), in_specs...  9.06 us
    pallas_call x1, Pallas kernels, per_device(): call(error_left_kernel, [sds((rank, rows), F32), sds((1, rows, width), BF...  4.14 us
    ppermute x3, waiting for transfers between devices, exchange(): lax.ppermute(pieces[k], axis, [(i, (i + k) % n) for i in range(n)])  4.14 us
    ppermute x3, starting transfers between devices, exchange(): lax.ppermute(pieces[k], axis, [(i, (i + k) % n) for i in range(n)])  3.65 us
  transfers between devices with their start and end apart: 21, of which 13 were waited for; matrix products, arithmetic and copies ran while one was open for 0% of the time, Pallas kernels for 16%

profile of v12, /device:TPU:0, one launch (start us, length us, event | category | flops | bytes accessed | tf_op | source)
XLA Modules:
  0.0 89.1 jit_solution(74849673320464124)
XLA Ops:
  1.7 4.1 %collective-permute-start = (bf16[1,64,2560]{2,1,0:T(8,128)(2,1)S(1)}, bf16[1,64,2560]{2,1,0:T(8,128)(2,1)S(1)}, u32[]{:S(2)}, u32[]{:S(2)}) collective-permute-start(bf16[1,64,2560]{2,1,0:T(8,128)(2,1)S(1)} %first.1.a_ref), channel_id=1, source_target_pairs={{0,2},{2,3},{3,1},{1,0},{4,6},{6,7},{7,5},{5,4},{8,10},{10,11},{11... | collective-permute-start | bytes 983048 | tf_op jit(solution)/shard_map/ppermute | solution.py:61
  5.8 1.3 %token_factor.1 = (f32[8,128]{1,0:T(8,128)S(1)}, bf16[12,5120]{1,0:T(8,128)(2,1)S(1)}, bf16[1,64,2560]{2,1,0:T(8,128)(2,1)S(1)}) custom-call(f32[4,5120]{1,0:T(4,128)} %bitcast.2, bf16[1,64,5120]{2,1,0:T(8,128)(2,1)} %refs_0_.5, bf16[1,64,2560]{2,1,0:T(8,128)(2,1)S(1)} %first.1.a_ref), custom_call_target="tpu_custom_call" | custom-call | flops 1 | bytes 1 | tf_op jit(solution)/shard_map/token_factor/pallas_call | solution.py:369
  7.1 1.4 %collective-permute-start.3 = (f32[8,128]{1,0:T(8,128)S(1)}, f32[8,128]{1,0:T(8,128)S(1)}, u32[]{:S(2)}, u32[]{:S(2)}) collective-permute-start(f32[8,128]{1,0:T(8,128)S(1)} %get-tuple-element.49.refs_0_), channel_id=1, source_target_pairs={{0,3},{1,0},{2,1},{3,2},{4,7},{5,4},{6,5},{7,6},{8,11},{9,8},{10,9... | collective-permute-start | bytes 12296 | tf_op jit(solution)/shard_map/ppermute | solution.py:66
  8.8 1.9 %collective-permute-start.1 = (f32[8,128]{1,0:T(8,128)S(1)}, f32[8,128]{1,0:T(8,128)S(1)}, u32[]{:S(2)}, u32[]{:S(2)}) collective-permute-start(f32[8,128]{1,0:T(8,128)S(1)} %get-tuple-element.49.refs_0_), channel_id=1, source_target_pairs={{0,1},{1,2},{2,3},{3,0},{4,5},{5,6},{6,7},{7,4},{8,9},{9,10},{10,1... | collective-permute-start | bytes 12296 | tf_op jit(solution)/shard_map/ppermute | solution.py:66
  10.8 2.2 %collective-permute-done.3.refs_3_ = f32[8,128]{1,0:T(8,128)S(1)} collective-permute-done((f32[8,128]{1,0:T(8,128)S(1)}, f32[8,128]{1,0:T(8,128)S(1)}, u32[]{:S(2)}, u32[]{:S(2)}) %collective-permute-start.3) | collective-permute-done | bytes 4128 | tf_op jit(solution)/shard_map/ppermute | solution.py:66
  13.0 1.9 %collective-permute-done.2.refs_2_ = f32[8,128]{1,0:T(8,128)S(1)} collective-permute-done((f32[8,128]{1,0:T(8,128)S(1)}, f32[8,128]{1,0:T(8,128)S(1)}, u32[]{:S(2)}, u32[]{:S(2)}) %collective-permute-start.2) | collective-permute-done | bytes 4128 | tf_op jit(solution)/shard_map/ppermute | solution.py:66
  14.9 1.6 %collective-permute-start.4 = (bf16[1,64,2560]{2,1,0:T(8,128)(2,1)S(1)}, bf16[1,64,2560]{2,1,0:T(8,128)(2,1)S(1)}, u32[]{:S(2)}, u32[]{:S(2)}) collective-permute-start(bf16[1,64,2560]{2,1,0:T(8,128)(2,1)S(1)} %get-tuple-element.46), channel_id=1, source_target_pairs={{0,2},{2,3},{3,1},{1,0},{4,6},{6,7},{7,5},{5,4},{8,10},{10,11},{11... | collective-permute-start | bytes 983048 | tf_op jit(solution)/shard_map/ppermute | solution.py:61
  16.5 4.1 %error_left.1 = (f32[4,768]{1,0:T(4,128)S(1)}, bf16[1,768,5120]{2,1,0:T(8,128)(2,1)S(1)}) custom-call(bf16[12,5120]{1,0:T(8,128)(2,1)S(1)} %get-tuple-element.47.terms_ref, bf16[1,768,5120]{2,1,0:T(8,128)(2,1)} %e_hbm.1), custom_call_target="tpu_custom_call" | custom-call | flops 1 | bytes 1 | tf_op jit(solution)/shard_map/error_left/pallas_call | solution.py:378
  22.1 2.6 %collective-permute-done.4.refs_1_ = bf16[1,64,2560]{2,1,0:T(8,128)(2,1)S(1)} collective-permute-done((bf16[1,64,2560]{2,1,0:T(8,128)(2,1)S(1)}, bf16[1,64,2560]{2,1,0:T(8,128)(2,1)S(1)}, u32[]{:S(2)}, u32[]{:S(2)}) %collective-permute-start.4) | collective-permute-done | bytes 327712 | tf_op jit(solution)/shard_map/ppermute | solution.py:61
  25.9 1.5 %collective-permute-start.6 = (f32[4,768]{1,0:T(4,128)S(1)}, f32[4,768]{1,0:T(4,128)S(1)}, u32[]{:S(2)}, u32[]{:S(2)}) collective-permute-start(f32[4,768]{1,0:T(4,128)S(1)} %add.7.x_ref), channel_id=1, source_target_pairs={{0,8},{4,12},{8,0},{12,4},{16,24},{20,28},{24,16},{28,20},{1,9},{5... | collective-permute-start | bytes 36872 | tf_op jit(solution)/shard_map/ppermute | solution.py:71
  27.4 2.2 %collective-permute-done.6.y_ref = f32[4,768]{1,0:T(4,128)S(1)} collective-permute-done((f32[4,768]{1,0:T(4,128)S(1)}, f32[4,768]{1,0:T(4,128)S(1)}, u32[]{:S(2)}, u32[]{:S(2)}) %collective-permute-start.6) | collective-permute-done | bytes 12320 | tf_op jit(solution)/shard_map/ppermute | solution.py:71
  29.6 1.5 %collective-permute-start.8 = (f32[4,768]{1,0:T(4,128)S(1)}, f32[4,768]{1,0:T(4,128)S(1)}, u32[]{:S(2)}, u32[]{:S(2)}) collective-permute-start(f32[4,768]{1,0:T(4,128)S(1)} %add.8.x_ref), channel_id=1, source_target_pairs={{0,16},{4,20},{8,24},{12,28},{16,0},{20,4},{24,8},{28,12},{1,17},{... | collective-permute-start | bytes 36872 | tf_op jit(solution)/shard_map/ppermute | solution.py:71
  31.1 2.2 %collective-permute-done.8.y_ref = f32[4,768]{1,0:T(4,128)S(1)} collective-permute-done((f32[4,768]{1,0:T(4,128)S(1)}, f32[4,768]{1,0:T(4,128)S(1)}, u32[]{:S(2)}, u32[]{:S(2)}) %collective-permute-start.8) | collective-permute-done | bytes 12320 | tf_op jit(solution)/shard_map/ppermute | solution.py:71
  34.4 3.1 %collective-permute-done.9.y_ref = f32[8,256]{1,0:T(8,128)S(1)} collective-permute-done((f32[8,256]{1,0:T(8,128)S(1)}, f32[8,256]{1,0:T(8,128)S(1)}, u32[]{:S(2)}, u32[]{:S(2)}) %collective-permute-start.9) | collective-permute-done | bytes 8224 | tf_op jit(solution)/shard_map/ppermute | solution.py:71
  37.6 1.3 %collective-permute-start.10 = (f32[8,256]{1,0:T(8,128)S(1)}, f32[8,256]{1,0:T(8,128)S(1)}, u32[]{:S(2)}, u32[]{:S(2)}) collective-permute-start(f32[8,256]{1,0:T(8,128)S(1)} %join.1.x_ref), channel_id=1, source_target_pairs={{0,2},{1,3},{2,0},{3,1},{4,6},{5,7},{6,4},{7,5},{8,10},{9,11},{10,... | collective-permute-start | bytes 24584 | tf_op jit(solution)/shard_map/ppermute | solution.py:71
  40.0 2.3 %collective-permute-done.10.y_ref = f32[8,256]{1,0:T(8,128)S(1)} collective-permute-done((f32[8,256]{1,0:T(8,128)S(1)}, f32[8,256]{1,0:T(8,128)S(1)}, u32[]{:S(2)}, u32[]{:S(2)}) %collective-permute-start.10) | collective-permute-done | bytes 8224 | tf_op jit(solution)/shard_map/ppermute | solution.py:71
  43.3 1.3 %collective-permute-done.11.y_ref = f32[4,5120]{1,0:T(4,128)S(1)} collective-permute-done((f32[4,5120]{1,0:T(4,128)S(1)}, f32[4,5120]{1,0:T(4,128)S(1)}, u32[]{:S(2)}, u32[]{:S(2)}) %collective-permute-start.11) | collective-permute-done | bytes 81952 | tf_op jit(solution)/shard_map/ppermute | solution.py:71
  47.1 7.2 %collective-permute-done.12.x_ref.refs_2_ = bf16[1,64,2560]{2,1,0:T(8,128)(2,1)S(1)} collective-permute-done((bf16[1,64,2560]{2,1,0:T(8,128)(2,1)S(1)}, bf16[1,64,2560]{2,1,0:T(8,128)(2,1)S(1)}, u32[]{:S(2)}, u32[]{:S(2)}) %collective-permute-start.12) | collective-permute-done | bytes 327712 | tf_op jit(solution)/shard_map/ppermute | solution.py:61
  55.8 12.8 %collective-permute-start.17 = (f32[4,5120]{1,0:T(4,128)S(1)}, f32[4,5120]{1,0:T(4,128)S(1)}, u32[]{:S(2)}, u32[]{:S(2)}) collective-permute-start(f32[4,5120]{1,0:T(4,128)S(1)} %add.13.mine_ref), channel_id=1, source_target_pairs={{0,4},{4,0},{8,12},{12,8},{16,20},{20,16},{24,28},{28,24},{1,5},{5... | collective-permute-start | bytes 245768 | tf_op jit(solution)/shard_map/ppermute | solution.py:71
  69.6 2.1 %collective-permute-start.19 = (bf16[1,64,1280]{2,1,0:T(8,128)(2,1)S(1)}, bf16[1,64,1280]{2,1,0:T(8,128)(2,1)S(1)}, u32[]{:S(2)}, u32[]{:S(2)}) collective-permute-start(bf16[1,64,1280]{2,1,0:T(8,128)(2,1)S(1)} %get-tuple-element.72), channel_id=1, source_target_pairs={{0,2},{2,3},{3,1},{1,0},{4,6},{6,7},{7,5},{5,4},{8,10},{10,11},{11... | collective-permute-start | bytes 491528 | tf_op jit(solution)/shard_map/ppermute | solution.py:61
  73.5 6.5 %collective-permute-done.20.refs_3_ = bf16[1,64,2560]{2,1,0:T(8,128)(2,1)S(1)} collective-permute-done((bf16[1,64,2560]{2,1,0:T(8,128)(2,1)S(1)}, bf16[1,64,2560]{2,1,0:T(8,128)(2,1)S(1)}, u32[]{:S(2)}, u32[]{:S(2)}) %collective-permute-start.20) | collective-permute-done | bytes 327712 | tf_op jit(solution)/shard_map/ppermute | solution.py:61
  80.0 4.1 %rebuild.3 = (bf16[768,5120]{1,0:T(8,128)(2,1)}, bf16[1,768,5120]{2,1,0:T(8,128)(2,1)}) custom-call(bf16[768,256]{1,0:T(8,128)(2,1)S(1)} %acts.1.acts_ref, bf16[768,24]{1,0:T(8,128)(2,1)S(1)} %get-tuple-element.68.left_ref, bf16[24,5120]{1,0:T(8,128)(2,1)S(1)} %get-tuple-element.69.right_ref, bf16[1,768,5120]{2,1,0:T(8,128)(2,1)S(1)} %get-tuple-element.57.e_ref, ...), custom_call_target="tpu_custom_call" | custom-call | flops 1 | bytes 1 | tf_op jit(solution)/shard_map/rebuild/pallas_call | solution.py:463
  84.1 2.5 %rebuild.4 = (bf16[768,5120]{1,0:T(8,128)(2,1)}, bf16[1,768,5120]{2,1,0:T(8,128)(2,1)}) custom-call(bf16[768,256]{1,0:T(8,128)(2,1)S(1)} %acts.1.acts_ref, bf16[768,24]{1,0:T(8,128)(2,1)S(1)} %get-tuple-element.68.left_ref, bf16[24,5120]{1,0:T(8,128)(2,1)S(1)} %get-tuple-element.69.right_ref, ...), custom_call_target="tpu_custom_call", output_to_operand_aliasing={{0}: (8, {}), {1}: (9, {})} | custom-call | flops 1 | bytes 1 | tf_op jit(solution)/shard_map/rebuild/pallas_call | solution.py:463
  86.6 2.5 %rebuild.5 = (bf16[768,5120]{1,0:T(8,128)(2,1)}, bf16[1,768,5120]{2,1,0:T(8,128)(2,1)}) custom-call(bf16[768,256]{1,0:T(8,128)(2,1)S(1)} %acts.1.acts_ref, bf16[768,24]{1,0:T(8,128)(2,1)S(1)} %get-tuple-element.68.left_ref, bf16[24,5120]{1,0:T(8,128)(2,1)S(1)} %get-tuple-element.69.right_ref, ...), custom_call_target="tpu_custom_call", output_to_operand_aliasing={{0}: (8, {}), {1}: (9, {})} | custom-call | flops 1 | bytes 1 | tf_op jit(solution)/shard_map/rebuild/pallas_call | solution.py:463
  (43 shorter events, 14.0 us)
Async XLA Ops:
  0.6 20.0 %copy-start.1 = (bf16[1,256,768]{2,1,0:T(8,128)(2,1)S(1)}, bf16[1,256,768]{2,1,0:T(8,128)(2,1)}, u32[]{:S(2)}) copy-start(bf16[1,256,768]{2,1,0:T(8,128)(2,1)} %a_ref.5) | copy-start | bytes 1179652
  1.7 13.2 %collective-permute-start = (bf16[1,64,2560]{2,1,0:T(8,128)(2,1)S(1)}, bf16[1,64,2560]{2,1,0:T(8,128)(2,1)S(1)}, u32[]{:S(2)}, u32[]{:S(2)}) collective-permute-start(bf16[1,64,2560]{2,1,0:T(8,128)(2,1)S(1)} %first.1.a_ref), channel_id=1, source_target_pairs={{0,2},{2,3},{3,1},{1,0},{4,6},{6,7},{7,5},{5,4},{8,10},{10,11},{11... | collective-permute-start | bytes 983048 | tf_op jit(solution)/shard_map/ppermute | solution.py:61
  7.1 5.9 %collective-permute-start.3 = (f32[8,128]{1,0:T(8,128)S(1)}, f32[8,128]{1,0:T(8,128)S(1)}, u32[]{:S(2)}, u32[]{:S(2)}) collective-permute-start(f32[8,128]{1,0:T(8,128)S(1)} %get-tuple-element.49.refs_0_), channel_id=1, source_target_pairs={{0,3},{1,0},{2,1},{3,2},{4,7},{5,4},{6,5},{7,6},{8,11},{9,8},{10,9... | collective-permute-start | bytes 12296 | tf_op jit(solution)/shard_map/ppermute | solution.py:66
  8.5 6.4 %collective-permute-start.2 = (f32[8,128]{1,0:T(8,128)S(1)}, f32[8,128]{1,0:T(8,128)S(1)}, u32[]{:S(2)}, u32[]{:S(2)}) collective-permute-start(f32[8,128]{1,0:T(8,128)S(1)} %get-tuple-element.49.refs_0_), channel_id=1, source_target_pairs={{0,2},{1,3},{2,0},{3,1},{4,6},{5,7},{6,4},{7,5},{8,10},{9,11},{10,... | collective-permute-start | bytes 12296 | tf_op jit(solution)/shard_map/ppermute | solution.py:66
  8.8 6.1 %collective-permute-start.1 = (f32[8,128]{1,0:T(8,128)S(1)}, f32[8,128]{1,0:T(8,128)S(1)}, u32[]{:S(2)}, u32[]{:S(2)}) collective-permute-start(f32[8,128]{1,0:T(8,128)S(1)} %get-tuple-element.49.refs_0_), channel_id=1, source_target_pairs={{0,1},{1,2},{2,3},{3,0},{4,5},{5,6},{6,7},{7,4},{8,9},{9,10},{10,1... | collective-permute-start | bytes 12296 | tf_op jit(solution)/shard_map/ppermute | solution.py:66
  14.9 27.4 %copy-start = (bf16[1,64,5120]{2,1,0:T(8,128)(2,1)S(1)}, bf16[1,64,5120]{2,1,0:T(8,128)(2,1)}, u32[]{:S(2)}) copy-start(bf16[1,64,5120]{2,1,0:T(8,128)(2,1)} %refs_0_.5) | copy-start | bytes 1966084
  14.9 9.8 %collective-permute-start.4 = (bf16[1,64,2560]{2,1,0:T(8,128)(2,1)S(1)}, bf16[1,64,2560]{2,1,0:T(8,128)(2,1)S(1)}, u32[]{:S(2)}, u32[]{:S(2)}) collective-permute-start(bf16[1,64,2560]{2,1,0:T(8,128)(2,1)S(1)} %get-tuple-element.46), channel_id=1, source_target_pairs={{0,2},{2,3},{3,1},{1,0},{4,6},{6,7},{7,5},{5,4},{8,10},{10,11},{11... | collective-permute-start | bytes 983048 | tf_op jit(solution)/shard_map/ppermute | solution.py:61
  20.8 1.2 %collective-permute-start.5 = (f32[4,768]{1,0:T(4,128)S(1)}, f32[4,768]{1,0:T(4,128)S(1)}, u32[]{:S(2)}, u32[]{:S(2)}) collective-permute-start(f32[4,768]{1,0:T(4,128)S(1)} %left.1.x_ref), channel_id=1, source_target_pairs={{0,4},{4,0},{8,12},{12,8},{16,20},{20,16},{24,28},{28,24},{1,5},{5... | collective-permute-start | bytes 36872 | tf_op jit(solution)/shard_map/ppermute | solution.py:71
  24.7 8.9 %collective-permute-start.7 = (bf16[1,64,2560]{2,1,0:T(8,128)(2,1)S(1)}, bf16[1,64,2560]{2,1,0:T(8,128)(2,1)S(1)}, u32[]{:S(2)}, u32[]{:S(2)}) collective-permute-start(bf16[1,64,2560]{2,1,0:T(8,128)(2,1)S(1)} %collective-permute-done.refs_1_), channel_id=1, source_target_pairs={{0,2},{2,3},{3,1},{1,0},{4,6},{6,7},{7,5},{5,4},{8,10},{10,11},{11... | collective-permute-start | bytes 983048 | tf_op jit(solution)/shard_map/ppermute | solution.py:61
  25.9 3.7 %collective-permute-start.6 = (f32[4,768]{1,0:T(4,128)S(1)}, f32[4,768]{1,0:T(4,128)S(1)}, u32[]{:S(2)}, u32[]{:S(2)}) collective-permute-start(f32[4,768]{1,0:T(4,128)S(1)} %add.7.x_ref), channel_id=1, source_target_pairs={{0,8},{4,12},{8,0},{12,4},{16,24},{20,28},{24,16},{28,20},{1,9},{5... | collective-permute-start | bytes 36872 | tf_op jit(solution)/shard_map/ppermute | solution.py:71
  29.6 3.7 %collective-permute-start.8 = (f32[4,768]{1,0:T(4,128)S(1)}, f32[4,768]{1,0:T(4,128)S(1)}, u32[]{:S(2)}, u32[]{:S(2)}) collective-permute-start(f32[4,768]{1,0:T(4,128)S(1)} %add.8.x_ref), channel_id=1, source_target_pairs={{0,16},{4,20},{8,24},{12,28},{16,0},{20,4},{24,8},{28,12},{1,17},{... | collective-permute-start | bytes 36872 | tf_op jit(solution)/shard_map/ppermute | solution.py:71
  33.8 3.7 %collective-permute-start.9 = (f32[8,256]{1,0:T(8,128)S(1)}, f32[8,256]{1,0:T(8,128)S(1)}, u32[]{:S(2)}, u32[]{:S(2)}) collective-permute-start(f32[8,256]{1,0:T(8,128)S(1)} %get-tuple-element.58.x_ref), channel_id=1, source_target_pairs={{0,1},{1,0},{2,3},{3,2},{4,5},{5,4},{6,7},{7,6},{8,9},{9,8},{10,11... | collective-permute-start | bytes 24584 | tf_op jit(solution)/shard_map/ppermute | solution.py:71
  37.6 4.7 %collective-permute-start.10 = (f32[8,256]{1,0:T(8,128)S(1)}, f32[8,256]{1,0:T(8,128)S(1)}, u32[]{:S(2)}, u32[]{:S(2)}) collective-permute-start(f32[8,256]{1,0:T(8,128)S(1)} %join.1.x_ref), channel_id=1, source_target_pairs={{0,2},{1,3},{2,0},{3,1},{4,6},{5,7},{6,4},{7,5},{8,10},{9,11},{10,... | collective-permute-start | bytes 24584 | tf_op jit(solution)/shard_map/ppermute | solution.py:71
  43.2 1.3 %collective-permute-start.11 = (f32[4,5120]{1,0:T(4,128)S(1)}, f32[4,5120]{1,0:T(4,128)S(1)}, u32[]{:S(2)}, u32[]{:S(2)}) collective-permute-start(f32[4,5120]{1,0:T(4,128)S(1)} %get-tuple-element.61.x_ref), channel_id=1, source_target_pairs={{0,4},{4,0},{8,12},{12,8},{16,20},{20,16},{24,28},{28,24},{1,5},{5... | collective-permute-start | bytes 245768 | tf_op jit(solution)/shard_map/ppermute | solution.py:71
  44.6 9.8 %collective-permute-start.12 = (bf16[1,64,2560]{2,1,0:T(8,128)(2,1)S(1)}, bf16[1,64,2560]{2,1,0:T(8,128)(2,1)S(1)}, u32[]{:S(2)}, u32[]{:S(2)}) collective-permute-start(bf16[1,64,2560]{2,1,0:T(8,128)(2,1)S(1)} %collective-permute-done.4.refs_1_), channel_id=1, source_target_pairs={{0,2},{2,3},{3,1},{1,0},{4,6},{6,7},{7,5},{5,4},{8,10},{10,11},{11... | collective-permute-start | bytes 983048 | tf_op jit(solution)/shard_map/ppermute | solution.py:61
  45.8 0.7 collective-permute-start.13
  46.4 0.7 collective-permute-start.14
  54.4 0.7 collective-permute-start.15
  55.1 0.7 collective-permute-start.16
  55.8 13.7 %collective-permute-start.17 = (f32[4,5120]{1,0:T(4,128)S(1)}, f32[4,5120]{1,0:T(4,128)S(1)}, u32[]{:S(2)}, u32[]{:S(2)}) collective-permute-start(f32[4,5120]{1,0:T(4,128)S(1)} %add.13.mine_ref), channel_id=1, source_target_pairs={{0,4},{4,0},{8,12},{12,8},{16,20},{20,16},{24,28},{28,24},{1,5},{5... | collective-permute-start | bytes 245768 | tf_op jit(solution)/shard_map/ppermute | solution.py:71
  69.5 10.5 %collective-permute-start.20 = (bf16[1,64,2560]{2,1,0:T(8,128)(2,1)S(1)}, bf16[1,64,2560]{2,1,0:T(8,128)(2,1)S(1)}, u32[]{:S(2)}, u32[]{:S(2)}) collective-permute-start(bf16[1,64,2560]{2,1,0:T(8,128)(2,1)S(1)} %collective-permute-done.7.refs_2_), channel_id=1, source_target_pairs={{0,2},{2,3},{3,1},{1,0},{4,6},{6,7},{7,5},{5,4},{8,10},{10,11},{11... | collective-permute-start | bytes 983048 | tf_op jit(solution)/shard_map/ppermute | solution.py:61
  69.6 14.6 %collective-permute-start.19 = (bf16[1,64,1280]{2,1,0:T(8,128)(2,1)S(1)}, bf16[1,64,1280]{2,1,0:T(8,128)(2,1)S(1)}, u32[]{:S(2)}, u32[]{:S(2)}) collective-permute-start(bf16[1,64,1280]{2,1,0:T(8,128)(2,1)S(1)} %get-tuple-element.72), channel_id=1, source_target_pairs={{0,2},{2,3},{3,1},{1,0},{4,6},{6,7},{7,5},{5,4},{8,10},{10,11},{11... | collective-permute-start | bytes 491528 | tf_op jit(solution)/shard_map/ppermute | solution.py:61
  71.7 15.0 %collective-permute-start.18 = (bf16[1,64,1280]{2,1,0:T(8,128)(2,1)S(1)}, bf16[1,64,1280]{2,1,0:T(8,128)(2,1)S(1)}, u32[]{:S(2)}, u32[]{:S(2)}) collective-permute-start(bf16[1,64,1280]{2,1,0:T(8,128)(2,1)S(1)} %get-tuple-element.71), channel_id=1, source_target_pairs={{0,2},{2,3},{3,1},{1,0},{4,6},{6,7},{7,5},{5,4},{8,10},{10,11},{11... | collective-permute-start | bytes 491528 | tf_op jit(solution)/shard_map/ppermute | solution.py:61

commit v13 on v9

--- a/solution.py
+++ b/solution.py
@@ -70,9 +70,22 @@
     return lax.ppermute(x, axis, [(i, i ^ bit) for i in range(n)])
 
 
-def bits(n):
+def groups(n):
     assert n & (n - 1) == 0
-    return [1 << i for i in range(n.bit_length() - 1)]
+    bits = [1 << i for i in range(n.bit_length() - 1)]
+    return [bits[i : i + 2] for i in range(0, len(bits), 2)]
+
+
+def terms_of(x, axis, n, group):
+    others = group if len(group) == 1 else [group[0], group[1], group[0] | group[1]]
+    return [x] + [swap(x, axis, n, bit) for bit in others]
+
+
+def total_of(refs):
+    total = refs[0][...] + refs[1][...]
+    if len(refs) == 4:
+        total = total + (refs[2][...] + refs[3][...])
+    return total
 
 
 def token_factor_kernel(w_hbm, g_hbm, gw_ref, terms_ref, w, g, w3, sems):
@@ -134,12 +147,12 @@
     out_ref[...] = total
 
 
-def mean_kernel(n, scale, a_ref, x_ref, y_ref, p_ref, *refs):
-    msgs, p3, outbox = refs[:n], refs[n], refs[n + 1]
-    rank = x_ref.shape[0]
+def mean_kernel(n, scale, a_ref, *refs):
+    terms, p_ref, msgs, p3, outbox = refs[: -n - 3], refs[-n - 3], refs[-n - 2 : -2], refs[-2], refs[-1]
+    rank = p_ref.shape[0]
     tok = a_ref.shape[1] // n
     me = lax.axis_index("tensor")
-    mean = (x_ref[...] + y_ref[...]) * scale
+    mean = total_of(terms) * scale
     p_ref[...] = mean
     top = jnp.max(jnp.max(jnp.abs(mean), axis=1, keepdims=True), axis=0, keepdims=True)
     top = jnp.maximum(top, TINY)
@@ -232,8 +245,8 @@
     send_ref[...] = outbox[1 - core]
 
 
-def add_kernel(x_ref, y_ref, out_ref):
-    out_ref[...] = x_ref[...] + y_ref[...]
+def add_kernel(*refs):
+    refs[-1][...] = total_of(refs[:-1])
 
 
 LEFT_TERMS = (0, 0, 1, 0, 2, 1)
@@ -330,8 +343,8 @@
             name=name,
         )
 
-    def add(x, y):
-        return call(add_kernel, sds(x.shape, F32), [], "add")(x, y)
+    def add(*terms):
+        return call(add_kernel, sds(terms[0].shape, F32), [], "add")(*terms)
 
     def after(x, y):
         return lax.optimization_barrier((x, y))
@@ -343,7 +356,7 @@
     def step(x):
         return ring_step(x, "tensor", n)
 
-    wide = 6 * width // 20
+    wide = width // 4
     narrow = width // 2 - wide
     ring = [out_grads, step(out_grads)]
 
@@ -373,16 +386,17 @@
     left = call(
         left_kernel, sds((rank, rows), F32), [pltpu.VMEM((3 * rank, tok), F32)], "left"
     )(activations, ew, *gws)
-    for bit in bits(m)[:-1]:
-        left = add(left, swap(left, "dp", m, bit))
-    xs[1], last = after(xs[1], swap(left, "dp", m, bits(m)[-1]))
-
+    left = add(left, swap(left, "dp", m, 1))
+    for group in groups(m // 2)[:-1]:
+        left = add(*terms_of(left, "dp", m, [2 * bit for bit in group]))
+    lefts = terms_of(left, "dp", m, [2 * bit for bit in groups(m // 2)[-1]])
+    xs[1], lefts[1:] = after(xs[1], lefts[1:])
     mean, *msgs = call(
         functools.partial(mean_kernel, n, 1.0 / (SHRINK * m)),
         [sds((rank, rows), F32)] + [sds((8, 128), F32)] * n,
         [pltpu.VMEM((3 * rank, rows), F32), pltpu.VMEM((n, 8, 128), F32)],
         "mean",
-    )(activations, left, last)
+    )(activations, *lefts)
     msgs = exchange(msgs, "tensor", n)
 
     right_raw = call(
@@ -410,11 +424,11 @@
     for _ in range(4, n):
         last, total = after(xs[-1], total)
         xs.append(step(last))
-    for bit in bits(m)[1:]:
-        total = add(total, swap(total, "dp", m, bit))
+    for group in groups(m // 2):
+        total = add(*terms_of(total, "dp", m, [2 * bit for bit in group]))
     (xs[-1], ys[-1]), total = after((xs[-1], ys[-1]), total)
-    for bit in bits(n):
-        total = add(total, swap(total, "tensor", n, bit))
+    for group in groups(n):
+        total = add(*terms_of(total, "tensor", n, group))
     xa, xb = cut(xs[-1], [wide, wide])
     (xa, xb), total = after((xa, xb), total)
     xa, xb = step(xa), step(xb)

time: 78.1 us -> 79.3 us (1.015)
  waiting for transfers between devices: 27.5 us -> 28.7 us
    ppermute x7, waiting for transfers between devices: 0.83 us -> 5.5 us  [ring_step(): lax.ppermute(x, axis, [(ring[p], ring[(p + 1) % n]) for p in range(n)])]
    ppermute x9 -> x12, waiting for transfers between devices: 17.1 us -> 13.5 us  [swap(): return lax.ppermute(x, axis, [(i, i ^ bit) for i in range(n)])]
    ppermute x9 -> x12, starting transfers between devices: 11.2 us -> 11.6 us  [swap(): return lax.ppermute(x, axis, [(i, i ^ bit) for i in range(n)])]
  transfers between devices with their start and end apart: 22 -> 25, of which waited for: 13 -> 18; matrix products, arithmetic and copies ran while one was open for 0% -> 0% of each run, Pallas kernels for 20% -> 19%
where the time goes in v13:
time: 79.3 us; the launch traced here: 79.2 us
  starting transfers between devices  30.6 us (39%)
  waiting for transfers between devices  28.7 us (36%)
  Pallas kernels  19.1 us (24%)
  between operations  0.81 us (1%)
    ppermute x12, waiting for transfers between devices, swap(): return lax.ppermute(x, axis, [(i, i ^ bit) for i in range(n)])  13.5 us
    ppermute x12, starting transfers between devices, swap(): return lax.ppermute(x, axis, [(i, i ^ bit) for i in range(n)])  11.6 us
    ppermute x7, starting transfers between devices, ring_step(): lax.ppermute(x, axis, [(ring[p], ring[(p + 1) % n]) for p in range(n)])  10.8 us
    pallas_call x4, Pallas kernels, per_device(): pl.pallas_call(functools.partial(final_kernel, at, part, bases), in_specs...  9.88 us
    ppermute x6, waiting for transfers between devices, exchange(): lax.ppermute(pieces[k], axis, [(i, (i + k) % n) for i in range(n)])  9.7 us
    ppermute x6, starting transfers between devices, exchange(): lax.ppermute(pieces[k], axis, [(i, (i + k) % n) for i in range(n)])  8.19 us
    ppermute x7, waiting for transfers between devices, ring_step(): lax.ppermute(x, axis, [(ring[p], ring[(p + 1) % n]) for p in range(n)])  5.5 us
    pallas_call x1, Pallas kernels, per_device(): call(error_left_kernel, [sds((rank, rows), F32), sds((1, rows, width), BF...  4.19 us
  transfers between devices with their start and end apart: 25, of which 18 were waited for; matrix products, arithmetic and copies ran while one was open for 0% of the time, Pallas kernels for 19%

profile of v13, /device:TPU:0, one launch (start us, length us, event | category | flops | bytes accessed | tf_op | source)
XLA Modules:
  0.0 79.2 jit_solution(5221025017758675799)
XLA Ops:
  0.6 4.1 %collective-permute-start = (bf16[1,64,5120]{2,1,0:T(8,128)(2,1)}, bf16[1,64,5120]{2,1,0:T(8,128)(2,1)S(1)}, u32[]{:S(2)}, u32[]{:S(2)}) collective-permute-start(bf16[1,64,5120]{2,1,0:T(8,128)(2,1)} %refs_0_.7), channel_id=1, source_target_pairs={{0,2},{2,3},{3,1},{1,0},{4,6},{6,7},{7,5},{5,4},{8,10},{10,11},{11... | collective-permute-start | bytes 1966088 | tf_op jit(solution)/shard_map/ppermute | solution.py:60
  4.7 1.5 %token_factor.1 = (f32[8,128]{1,0:T(8,128)S(1)}, bf16[12,5120]{1,0:T(8,128)(2,1)S(1)}) custom-call(f32[4,5120]{1,0:T(4,128)} %bitcast.2, bf16[1,64,5120]{2,1,0:T(8,128)(2,1)} %refs_0_.7), custom_call_target="tpu_custom_call" | custom-call | flops 1 | bytes 1 | tf_op jit(solution)/shard_map/token_factor/pallas_call | solution.py:363
  6.2 4.2 %error_left.1 = (f32[4,768]{1,0:T(4,128)S(1)}, bf16[1,768,5120]{2,1,0:T(8,128)(2,1)S(1)}) custom-call(bf16[12,5120]{1,0:T(8,128)(2,1)S(1)} %get-tuple-element.54.terms_ref, bf16[1,768,5120]{2,1,0:T(8,128)(2,1)} %e_hbm.1), custom_call_target="tpu_custom_call" | custom-call | flops 4600000000 | bytes 1 | tf_op jit(solution)/shard_map/error_left/pallas_call | solution.py:374
  10.5 1.9 %collective-permute-start.2 = (f32[8,128]{1,0:T(8,128)S(1)}, f32[8,128]{1,0:T(8,128)S(1)}, u32[]{:S(2)}, u32[]{:S(2)}) collective-permute-start(f32[8,128]{1,0:T(8,128)S(1)} %get-tuple-element.58.refs_0_), channel_id=1, source_target_pairs={{0,2},{1,3},{2,0},{3,1},{4,6},{5,7},{6,4},{7,5},{8,10},{9,11},{10,... | collective-permute-start | bytes 12296 | tf_op jit(solution)/shard_map/ppermute | solution.py:65
  12.4 2.6 %collective-permute-start.3 = (f32[8,128]{1,0:T(8,128)S(1)}, f32[8,128]{1,0:T(8,128)S(1)}, u32[]{:S(2)}, u32[]{:S(2)}) collective-permute-start(f32[8,128]{1,0:T(8,128)S(1)} %get-tuple-element.58.refs_0_), channel_id=1, source_target_pairs={{0,3},{1,0},{2,1},{3,2},{4,7},{5,4},{6,5},{7,6},{8,11},{9,8},{10,9... | collective-permute-start | bytes 12296 | tf_op jit(solution)/shard_map/ppermute | solution.py:65
  15.0 6.0 %collective-permute-done.1.refs_1_ = f32[8,128]{1,0:T(8,128)S(1)} collective-permute-done((f32[8,128]{1,0:T(8,128)S(1)}, f32[8,128]{1,0:T(8,128)S(1)}, u32[]{:S(2)}, u32[]{:S(2)}) %collective-permute-start.1) | collective-permute-done | bytes 4128 | tf_op jit(solution)/shard_map/ppermute | solution.py:65
  21.1 1.6 %collective-permute-start.5 = (bf16[1,64,2560]{2,1,0:T(8,128)(2,1)S(1)}, bf16[1,64,2560]{2,1,0:T(8,128)(2,1)S(1)}, u32[]{:S(2)}, u32[]{:S(2)}) collective-permute-start(bf16[1,64,2560]{2,1,0:T(8,128)(2,1)S(1)} %get-tuple-element.63), channel_id=1, source_target_pairs={{0,2},{2,3},{3,1},{1,0},{4,6},{6,7},{7,5},{5,4},{8,10},{10,11},{11... | collective-permute-start | bytes 983048 | tf_op jit(solution)/shard_map/ppermute | solution.py:60
  24.2 1.5 %collective-permute-start.6 = (f32[4,768]{1,0:T(4,128)S(1)}, f32[4,768]{1,0:T(4,128)S(1)}, u32[]{:S(2)}, u32[]{:S(2)}) collective-permute-start(f32[4,768]{1,0:T(4,128)S(1)} %add.4.refs_0_), channel_id=1, source_target_pairs={{0,8},{4,12},{8,0},{12,4},{16,24},{20,28},{24,16},{28,20},{1,9},{5... | collective-permute-start | bytes 36872 | tf_op jit(solution)/shard_map/ppermute | solution.py:70
  25.6 1.5 %collective-permute-start.7 = (f32[4,768]{1,0:T(4,128)S(1)}, f32[4,768]{1,0:T(4,128)S(1)}, u32[]{:S(2)}, u32[]{:S(2)}) collective-permute-start(f32[4,768]{1,0:T(4,128)S(1)} %add.4.refs_0_), channel_id=1, source_target_pairs={{0,16},{4,20},{8,24},{12,28},{16,0},{20,4},{24,8},{28,12},{1,17},{... | collective-permute-start | bytes 36872 | tf_op jit(solution)/shard_map/ppermute | solution.py:70
  27.9 1.5 %collective-permute-done.7.refs_2_ = f32[4,768]{1,0:T(4,128)S(1)} collective-permute-done((f32[4,768]{1,0:T(4,128)S(1)}, f32[4,768]{1,0:T(4,128)S(1)}, u32[]{:S(2)}, u32[]{:S(2)}) %collective-permute-start.7) | collective-permute-done | bytes 12320 | tf_op jit(solution)/shard_map/ppermute | solution.py:70
  29.3 2.4 %collective-permute-done.8.refs_3_ = f32[4,768]{1,0:T(4,128)S(1)} collective-permute-done((f32[4,768]{1,0:T(4,128)S(1)}, f32[4,768]{1,0:T(4,128)S(1)}, u32[]{:S(2)}, u32[]{:S(2)}) %collective-permute-start.8) | collective-permute-done | bytes 12320 | tf_op jit(solution)/shard_map/ppermute | solution.py:70
  32.1 1.6 %collective-permute-start.10 = (f32[8,128]{1,0:T(8,128)S(1)}, f32[8,128]{1,0:T(8,128)S(1)}, u32[]{:S(2)}, u32[]{:S(2)}) collective-permute-start(f32[8,128]{1,0:T(8,128)S(1)} %get-tuple-element.71), channel_id=1, source_target_pairs={{0,2},{1,3},{2,0},{3,1},{4,6},{5,7},{6,4},{7,5},{8,10},{9,11},{10,... | collective-permute-start | bytes 12296 | tf_op jit(solution)/shard_map/ppermute | solution.py:65
  37.3 3.2 %collective-permute-done.9.refs_1_ = f32[8,128]{1,0:T(8,128)S(1)} collective-permute-done((f32[8,128]{1,0:T(8,128)S(1)}, f32[8,128]{1,0:T(8,128)S(1)}, u32[]{:S(2)}, u32[]{:S(2)}) %collective-permute-start.9) | collective-permute-done | bytes 4128 | tf_op jit(solution)/shard_map/ppermute | solution.py:65
  42.7 1.6 %collective-permute-start.14 = (f32[4,2560]{1,0:T(4,128)S(1)}, f32[4,2560]{1,0:T(4,128)S(1)}, u32[]{:S(2)}, u32[]{:S(2)}) collective-permute-start(f32[4,2560]{1,0:T(4,128)S(1)} %add.5.refs_0_), channel_id=1, source_target_pairs={{0,8},{4,12},{8,0},{12,4},{16,24},{20,28},{24,16},{28,20},{1,9},{5... | collective-permute-start | bytes 122888 | tf_op jit(solution)/shard_map/ppermute | solution.py:70
  44.2 1.5 %collective-permute-start.15 = (f32[4,2560]{1,0:T(4,128)S(1)}, f32[4,2560]{1,0:T(4,128)S(1)}, u32[]{:S(2)}, u32[]{:S(2)}) collective-permute-start(f32[4,2560]{1,0:T(4,128)S(1)} %add.5.refs_0_), channel_id=1, source_target_pairs={{0,16},{4,20},{8,24},{12,28},{16,0},{20,4},{24,8},{28,12},{1,17},{... | collective-permute-start | bytes 122888 | tf_op jit(solution)/shard_map/ppermute | solution.py:70
  46.8 1.5 %collective-permute-done.15.refs_2_ = f32[4,2560]{1,0:T(4,128)S(1)} collective-permute-done((f32[4,2560]{1,0:T(4,128)S(1)}, f32[4,2560]{1,0:T(4,128)S(1)}, u32[]{:S(2)}, u32[]{:S(2)}) %collective-permute-start.15) | collective-permute-done | bytes 40992 | tf_op jit(solution)/shard_map/ppermute | solution.py:70
  48.2 2.4 %collective-permute-done.16.refs_3_ = f32[4,2560]{1,0:T(4,128)S(1)} collective-permute-done((f32[4,2560]{1,0:T(4,128)S(1)}, f32[4,2560]{1,0:T(4,128)S(1)}, u32[]{:S(2)}, u32[]{:S(2)}) %collective-permute-start.16) | collective-permute-done | bytes 40992 | tf_op jit(solution)/shard_map/ppermute | solution.py:70
  50.7 1.8 %collective-permute-done.13.x_ref.refs_2_ = bf16[1,64,2560]{2,1,0:T(8,128)(2,1)S(1)} collective-permute-done((bf16[1,64,2560]{2,1,0:T(8,128)(2,1)S(1)}, bf16[1,64,2560]{2,1,0:T(8,128)(2,1)S(1)}, u32[]{:S(2)}, u32[]{:S(2)}) %collective-permute-start.13) | collective-permute-done | bytes 327712 | tf_op jit(solution)/shard_map/ppermute | solution.py:60
  53.6 3.2 %collective-permute-start.19 = (f32[4,2560]{1,0:T(4,128)S(1)}, f32[4,2560]{1,0:T(4,128)S(1)}, u32[]{:S(2)}, u32[]{:S(2)}) collective-permute-start(f32[4,2560]{1,0:T(4,128)S(1)} %add.6.refs_0_), channel_id=1, source_target_pairs={{0,3},{1,2},{2,1},{3,0},{4,7},{5,6},{6,5},{7,4},{8,11},{9,10},{10,... | collective-permute-start | bytes 122888 | tf_op jit(solution)/shard_map/ppermute | solution.py:70
  60.1 3.2 %collective-permute-start.23 = (bf16[1,64,1280]{2,1,0:T(8,128)(2,1)S(1)}, bf16[1,64,1280]{2,1,0:T(8,128)(2,1)S(1)}, u32[]{:S(2)}, u32[]{:S(2)}) collective-permute-start(bf16[1,64,1280]{2,1,0:T(8,128)(2,1)S(1)} %get-tuple-element.92), channel_id=1, source_target_pairs={{0,2},{2,3},{3,1},{1,0},{4,6},{6,7},{7,5},{5,4},{8,10},{10,11},{11... | collective-permute-start | bytes 491528 | tf_op jit(solution)/shard_map/ppermute | solution.py:60
  66.6 2.5 %rebuild.4 = (bf16[768,5120]{1,0:T(8,128)(2,1)}, bf16[1,768,5120]{2,1,0:T(8,128)(2,1)}) custom-call(bf16[768,256]{1,0:T(8,128)(2,1)S(1)} %acts.1.acts_ref, bf16[768,24]{1,0:T(8,128)(2,1)S(1)} %get-tuple-element.85.left_ref, bf16[24,5120]{1,0:T(8,128)(2,1)S(1)} %get-tuple-element.88.right_ref, bf16[1,768,5120]{2,1,0:T(8,128)(2,1)S(1)} %get-tuple-element.68.e_ref, ...), custom_call_target="tpu_custom_call" | custom-call | flops 1 | bytes 1 | tf_op jit(solution)/shard_map/rebuild/pallas_call | solution.py:471
  70.1 2.5 %rebuild.5 = (bf16[768,5120]{1,0:T(8,128)(2,1)}, bf16[1,768,5120]{2,1,0:T(8,128)(2,1)}) custom-call(bf16[768,256]{1,0:T(8,128)(2,1)S(1)} %acts.1.acts_ref, bf16[768,24]{1,0:T(8,128)(2,1)S(1)} %get-tuple-element.85.left_ref, bf16[24,5120]{1,0:T(8,128)(2,1)S(1)} %get-tuple-element.88.right_ref, ...), custom_call_target="tpu_custom_call", output_to_operand_aliasing={{0}: (8, {}), {1}: (9, {})} | custom-call | flops 1 | bytes 1 | tf_op jit(solution)/shard_map/rebuild/pallas_call | solution.py:471
  73.7 2.5 %rebuild.6 = (bf16[768,5120]{1,0:T(8,128)(2,1)}, bf16[1,768,5120]{2,1,0:T(8,128)(2,1)}) custom-call(bf16[768,256]{1,0:T(8,128)(2,1)S(1)} %acts.1.acts_ref, bf16[768,24]{1,0:T(8,128)(2,1)S(1)} %get-tuple-element.85.left_ref, bf16[24,5120]{1,0:T(8,128)(2,1)S(1)} %get-tuple-element.88.right_ref, ...), custom_call_target="tpu_custom_call", output_to_operand_aliasing={{0}: (8, {}), {1}: (9, {})} | custom-call | flops 1 | bytes 1 | tf_op jit(solution)/shard_map/rebuild/pallas_call | solution.py:471
  76.7 2.5 %rebuild.7 = (bf16[768,5120]{1,0:T(8,128)(2,1)}, bf16[1,768,5120]{2,1,0:T(8,128)(2,1)}) custom-call(bf16[768,256]{1,0:T(8,128)(2,1)S(1)} %acts.1.acts_ref, bf16[768,24]{1,0:T(8,128)(2,1)S(1)} %get-tuple-element.85.left_ref, bf16[24,5120]{1,0:T(8,128)(2,1)S(1)} %get-tuple-element.88.right_ref, ...), custom_call_target="tpu_custom_call", output_to_operand_aliasing={{0}: (8, {}), {1}: (9, {})} | custom-call | flops 1 | bytes 1 | tf_op jit(solution)/shard_map/rebuild/pallas_call | solution.py:471
  (49 shorter events, 19.7 us)
Async XLA Ops:
  0.6 20.4 %collective-permute-start = (bf16[1,64,5120]{2,1,0:T(8,128)(2,1)}, bf16[1,64,5120]{2,1,0:T(8,128)(2,1)S(1)}, u32[]{:S(2)}, u32[]{:S(2)}) collective-permute-start(bf16[1,64,5120]{2,1,0:T(8,128)(2,1)} %refs_0_.7), channel_id=1, source_target_pairs={{0,2},{2,3},{3,1},{1,0},{4,6},{6,7},{7,5},{5,4},{8,10},{10,11},{11... | collective-permute-start | bytes 1966088 | tf_op jit(solution)/shard_map/ppermute | solution.py:60
  10.4 10.6 %collective-permute-start.1 = (f32[8,128]{1,0:T(8,128)S(1)}, f32[8,128]{1,0:T(8,128)S(1)}, u32[]{:S(2)}, u32[]{:S(2)}) collective-permute-start(f32[8,128]{1,0:T(8,128)S(1)} %get-tuple-element.58.refs_0_), channel_id=1, source_target_pairs={{0,1},{1,2},{2,3},{3,0},{4,5},{5,6},{6,7},{7,4},{8,9},{9,10},{10,1... | collective-permute-start | bytes 12296 | tf_op jit(solution)/shard_map/ppermute | solution.py:65
  10.5 10.5 %collective-permute-start.2 = (f32[8,128]{1,0:T(8,128)S(1)}, f32[8,128]{1,0:T(8,128)S(1)}, u32[]{:S(2)}, u32[]{:S(2)}) collective-permute-start(f32[8,128]{1,0:T(8,128)S(1)} %get-tuple-element.58.refs_0_), channel_id=1, source_target_pairs={{0,2},{1,3},{2,0},{3,1},{4,6},{5,7},{6,4},{7,5},{8,10},{9,11},{10,... | collective-permute-start | bytes 12296 | tf_op jit(solution)/shard_map/ppermute | solution.py:65
  12.4 8.6 %collective-permute-start.3 = (f32[8,128]{1,0:T(8,128)S(1)}, f32[8,128]{1,0:T(8,128)S(1)}, u32[]{:S(2)}, u32[]{:S(2)}) collective-permute-start(f32[8,128]{1,0:T(8,128)S(1)} %get-tuple-element.58.refs_0_), channel_id=1, source_target_pairs={{0,3},{1,0},{2,1},{3,2},{4,7},{5,4},{6,5},{7,6},{8,11},{9,8},{10,9... | collective-permute-start | bytes 12296 | tf_op jit(solution)/shard_map/ppermute | solution.py:65
  21.1 10.7 %collective-permute-start.5 = (bf16[1,64,2560]{2,1,0:T(8,128)(2,1)S(1)}, bf16[1,64,2560]{2,1,0:T(8,128)(2,1)S(1)}, u32[]{:S(2)}, u32[]{:S(2)}) collective-permute-start(bf16[1,64,2560]{2,1,0:T(8,128)(2,1)S(1)} %get-tuple-element.63), channel_id=1, source_target_pairs={{0,2},{2,3},{3,1},{1,0},{4,6},{6,7},{7,5},{5,4},{8,10},{10,11},{11... | collective-permute-start | bytes 983048 | tf_op jit(solution)/shard_map/ppermute | solution.py:60
  24.2 3.7 %collective-permute-start.6 = (f32[4,768]{1,0:T(4,128)S(1)}, f32[4,768]{1,0:T(4,128)S(1)}, u32[]{:S(2)}, u32[]{:S(2)}) collective-permute-start(f32[4,768]{1,0:T(4,128)S(1)} %add.4.refs_0_), channel_id=1, source_target_pairs={{0,8},{4,12},{8,0},{12,4},{16,24},{20,28},{24,16},{28,20},{1,9},{5... | collective-permute-start | bytes 36872 | tf_op jit(solution)/shard_map/ppermute | solution.py:70
  25.6 3.7 %collective-permute-start.7 = (f32[4,768]{1,0:T(4,128)S(1)}, f32[4,768]{1,0:T(4,128)S(1)}, u32[]{:S(2)}, u32[]{:S(2)}) collective-permute-start(f32[4,768]{1,0:T(4,128)S(1)} %add.4.refs_0_), channel_id=1, source_target_pairs={{0,16},{4,20},{8,24},{12,28},{16,0},{20,4},{24,8},{28,12},{1,17},{... | collective-permute-start | bytes 36872 | tf_op jit(solution)/shard_map/ppermute | solution.py:70
  27.2 4.6 %collective-permute-start.8 = (f32[4,768]{1,0:T(4,128)S(1)}, f32[4,768]{1,0:T(4,128)S(1)}, u32[]{:S(2)}, u32[]{:S(2)}) collective-permute-start(f32[4,768]{1,0:T(4,128)S(1)} %add.4.refs_0_), channel_id=1, source_target_pairs={{0,24},{4,28},{8,16},{12,20},{16,8},{20,12},{24,0},{28,4},{1,25},{... | collective-permute-start | bytes 36872 | tf_op jit(solution)/shard_map/ppermute | solution.py:70
  32.1 4.8 %collective-permute-start.10 = (f32[8,128]{1,0:T(8,128)S(1)}, f32[8,128]{1,0:T(8,128)S(1)}, u32[]{:S(2)}, u32[]{:S(2)}) collective-permute-start(f32[8,128]{1,0:T(8,128)S(1)} %get-tuple-element.71), channel_id=1, source_target_pairs={{0,2},{1,3},{2,0},{3,1},{4,6},{5,7},{6,4},{7,5},{8,10},{9,11},{10,... | collective-permute-start | bytes 12296 | tf_op jit(solution)/shard_map/ppermute | solution.py:65
  33.7 3.6 %collective-permute-start.11 = (f32[8,128]{1,0:T(8,128)S(1)}, f32[8,128]{1,0:T(8,128)S(1)}, u32[]{:S(2)}, u32[]{:S(2)}) collective-permute-start(f32[8,128]{1,0:T(8,128)S(1)} %get-tuple-element.72), channel_id=1, source_target_pairs={{0,3},{1,0},{2,1},{3,2},{4,7},{5,4},{6,5},{7,6},{8,11},{9,8},{10,9... | collective-permute-start | bytes 12296 | tf_op jit(solution)/shard_map/ppermute | solution.py:65
  35.1 5.4 %collective-permute-start.9 = (f32[8,128]{1,0:T(8,128)S(1)}, f32[8,128]{1,0:T(8,128)S(1)}, u32[]{:S(2)}, u32[]{:S(2)}) collective-permute-start(f32[8,128]{1,0:T(8,128)S(1)} %get-tuple-element.70), channel_id=1, source_target_pairs={{0,1},{1,2},{2,3},{3,0},{4,5},{5,6},{6,7},{7,4},{8,9},{9,10},{10,1... | collective-permute-start | bytes 12296 | tf_op jit(solution)/shard_map/ppermute | solution.py:65
  41.4 1.3 %collective-permute-start.12 = (f32[4,2560]{1,0:T(4,128)S(1)}, f32[4,2560]{1,0:T(4,128)S(1)}, u32[]{:S(2)}, u32[]{:S(2)}) collective-permute-start(f32[4,2560]{1,0:T(4,128)S(1)} %get-tuple-element.77), channel_id=1, source_target_pairs={{0,4},{4,0},{8,12},{12,8},{16,20},{20,16},{24,28},{28,24},{1,5},{5... | collective-permute-start | bytes 122888 | tf_op jit(solution)/shard_map/ppermute | solution.py:70
  42.7 9.8 %collective-permute-start.13 = (bf16[1,64,2560]{2,1,0:T(8,128)(2,1)S(1)}, bf16[1,64,2560]{2,1,0:T(8,128)(2,1)S(1)}, u32[]{:S(2)}, u32[]{:S(2)}) collective-permute-start(bf16[1,64,2560]{2,1,0:T(8,128)(2,1)S(1)} %get-tuple-element.78), channel_id=1, source_target_pairs={{0,2},{2,3},{3,1},{1,0},{4,6},{6,7},{7,5},{5,4},{8,10},{10,11},{11... | collective-permute-start | bytes 983048 | tf_op jit(solution)/shard_map/ppermute | solution.py:60
  42.7 4.1 %collective-permute-start.14 = (f32[4,2560]{1,0:T(4,128)S(1)}, f32[4,2560]{1,0:T(4,128)S(1)}, u32[]{:S(2)}, u32[]{:S(2)}) collective-permute-start(f32[4,2560]{1,0:T(4,128)S(1)} %add.5.refs_0_), channel_id=1, source_target_pairs={{0,8},{4,12},{8,0},{12,4},{16,24},{20,28},{24,16},{28,20},{1,9},{5... | collective-permute-start | bytes 122888 | tf_op jit(solution)/shard_map/ppermute | solution.py:70
  44.2 4.0 %collective-permute-start.15 = (f32[4,2560]{1,0:T(4,128)S(1)}, f32[4,2560]{1,0:T(4,128)S(1)}, u32[]{:S(2)}, u32[]{:S(2)}) collective-permute-start(f32[4,2560]{1,0:T(4,128)S(1)} %add.5.refs_0_), channel_id=1, source_target_pairs={{0,16},{4,20},{8,24},{12,28},{16,0},{20,4},{24,8},{28,12},{1,17},{... | collective-permute-start | bytes 122888 | tf_op jit(solution)/shard_map/ppermute | solution.py:70
  45.8 4.9 %collective-permute-start.16 = (f32[4,2560]{1,0:T(4,128)S(1)}, f32[4,2560]{1,0:T(4,128)S(1)}, u32[]{:S(2)}, u32[]{:S(2)}) collective-permute-start(f32[4,2560]{1,0:T(4,128)S(1)} %add.5.refs_0_), channel_id=1, source_target_pairs={{0,24},{4,28},{8,16},{12,20},{16,8},{20,12},{24,0},{28,4},{1,25},{... | collective-permute-start | bytes 122888 | tf_op jit(solution)/shard_map/ppermute | solution.py:70
  52.5 4.5 %collective-permute-start.17 = (f32[4,2560]{1,0:T(4,128)S(1)}, f32[4,2560]{1,0:T(4,128)S(1)}, u32[]{:S(2)}, u32[]{:S(2)}) collective-permute-start(f32[4,2560]{1,0:T(4,128)S(1)} %add.6.refs_0_), channel_id=1, source_target_pairs={{0,1},{1,0},{2,3},{3,2},{4,5},{5,4},{6,7},{7,6},{8,9},{9,8},{10,11... | collective-permute-start | bytes 122888 | tf_op jit(solution)/shard_map/ppermute | solution.py:70
  52.7 5.6 %collective-permute-start.18 = (f32[4,2560]{1,0:T(4,128)S(1)}, f32[4,2560]{1,0:T(4,128)S(1)}, u32[]{:S(2)}, u32[]{:S(2)}) collective-permute-start(f32[4,2560]{1,0:T(4,128)S(1)} %add.6.refs_0_), channel_id=1, source_target_pairs={{0,2},{1,3},{2,0},{3,1},{4,6},{5,7},{6,4},{7,5},{8,10},{9,11},{10,... | collective-permute-start | bytes 122888 | tf_op jit(solution)/shard_map/ppermute | solution.py:70
  53.6 5.8 %collective-permute-start.19 = (f32[4,2560]{1,0:T(4,128)S(1)}, f32[4,2560]{1,0:T(4,128)S(1)}, u32[]{:S(2)}, u32[]{:S(2)}) collective-permute-start(f32[4,2560]{1,0:T(4,128)S(1)} %add.6.refs_0_), channel_id=1, source_target_pairs={{0,3},{1,2},{2,1},{3,0},{4,7},{5,6},{6,5},{7,4},{8,11},{9,10},{10,... | collective-permute-start | bytes 122888 | tf_op jit(solution)/shard_map/ppermute | solution.py:70
  59.5 3.9 %collective-permute-start.20 = (f32[4,2560]{1,0:T(4,128)S(1)}, f32[4,2560]{1,0:T(4,128)S(1)}, u32[]{:S(2)}, u32[]{:S(2)}) collective-permute-start(f32[4,2560]{1,0:T(4,128)S(1)} %add.7.mine_ref), channel_id=1, source_target_pairs={{0,4},{4,0},{8,12},{12,8},{16,20},{20,16},{24,28},{28,24},{1,5},{5... | collective-permute-start | bytes 122888 | tf_op jit(solution)/shard_map/ppermute | solution.py:70
  59.6 7.1 %collective-permute-start.24 = (bf16[1,64,1280]{2,1,0:T(8,128)(2,1)S(1)}, bf16[1,64,1280]{2,1,0:T(8,128)(2,1)S(1)}, u32[]{:S(2)}, u32[]{:S(2)}) collective-permute-start(bf16[1,64,1280]{2,1,0:T(8,128)(2,1)S(1)} %get-tuple-element.93), channel_id=1, source_target_pairs={{0,2},{2,3},{3,1},{1,0},{4,6},{6,7},{7,5},{5,4},{8,10},{10,11},{11... | collective-permute-start | bytes 491528 | tf_op jit(solution)/shard_map/ppermute | solution.py:60
  60.1 10.0 %collective-permute-start.23 = (bf16[1,64,1280]{2,1,0:T(8,128)(2,1)S(1)}, bf16[1,64,1280]{2,1,0:T(8,128)(2,1)S(1)}, u32[]{:S(2)}, u32[]{:S(2)}) collective-permute-start(bf16[1,64,1280]{2,1,0:T(8,128)(2,1)S(1)} %get-tuple-element.92), channel_id=1, source_target_pairs={{0,2},{2,3},{3,1},{1,0},{4,6},{6,7},{7,5},{5,4},{8,10},{10,11},{11... | collective-permute-start | bytes 491528 | tf_op jit(solution)/shard_map/ppermute | solution.py:60
  64.1 9.5 %collective-permute-start.22 = (bf16[1,64,1280]{2,1,0:T(8,128)(2,1)S(1)}, bf16[1,64,1280]{2,1,0:T(8,128)(2,1)S(1)}, u32[]{:S(2)}, u32[]{:S(2)}) collective-permute-start(bf16[1,64,1280]{2,1,0:T(8,128)(2,1)S(1)} %get-tuple-element.91), channel_id=1, source_target_pairs={{0,2},{2,3},{3,1},{1,0},{4,6},{6,7},{7,5},{5,4},{8,10},{10,11},{11... | collective-permute-start | bytes 491528 | tf_op jit(solution)/shard_map/ppermute | solution.py:60
  64.3 12.4 %collective-permute-start.21 = (bf16[1,64,1280]{2,1,0:T(8,128)(2,1)S(1)}, bf16[1,64,1280]{2,1,0:T(8,128)(2,1)S(1)}, u32[]{:S(2)}, u32[]{:S(2)}) collective-permute-start(bf16[1,64,1280]{2,1,0:T(8,128)(2,1)S(1)} %get-tuple-element.90), channel_id=1, source_target_pairs={{0,2},{2,3},{3,1},{1,0},{4,6},{6,7},{7,5},{5,4},{8,10},{10,11},{11... | collective-permute-start | bytes 491528 | tf_op jit(solution)/shard_map/ppermute | solution.py:60
  (3 other events, 47.9 us)

commit v14 on v13

--- a/solution.py
+++ b/solution.py
@@ -11,6 +11,7 @@
 BF16 = jnp.bfloat16
 SHRINK = 2.0**-23
 TINY = 1e-30
+ROOM = 2.0**14
 BLOCK = 512
 
 
@@ -148,7 +149,8 @@
 
 
 def mean_kernel(n, scale, a_ref, *refs):
-    terms, p_ref, msgs, p3, outbox = refs[: -n - 3], refs[-n - 3], refs[-n - 2 : -2], refs[-2], refs[-1]
+    terms = refs[:-7]
+    p_ref, scaled_ref, extra_ref, held_ref, next_ref, p3, blocks = refs[-7:]
     rank = p_ref.shape[0]
     tok = a_ref.shape[1] // n
     me = lax.axis_index("tensor")
@@ -156,17 +158,20 @@
     p_ref[...] = mean
     top = jnp.max(jnp.max(jnp.abs(mean), axis=1, keepdims=True), axis=0, keepdims=True)
     top = jnp.maximum(top, TINY)
-    parts = stack3(mean / (top * 1024.0), p3)
-    gram = [jnp.sum(mean * mean[i : i + 1, :], axis=1, keepdims=True) for i in range(rank)]
-    outbox[...] = jnp.zeros_like(outbox)
+    scaled = mean / (top * ROOM)
+    scaled_ref[...] = scaled
+    parts = stack3(scaled, p3)
     for t in range(n):
-        y = dot(parts, a_ref[0, t * tok : (t + 1) * tok, :], (1, 1))
-        outbox[t, 0:rank, 0:tok] = sum3(y, rank)
-        for i in range(rank):
-            outbox[t, rank : 2 * rank, i : i + 1] = gram[i]
-        outbox[t, rank : rank + 1, rank : rank + 1] = top
-    for k in range(n):
-        msgs[k][...] = outbox[lax.rem(me + k, n)]
+        blocks[t] = sum3(dot(parts, a_ref[0, t * tok : (t + 1) * tok, :], (1, 1)), rank)
+    for s in range(n - 1):
+        held_ref[:, s * tok : (s + 1) * tok] = blocks[ring_source(me, s, n)]
+    next_ref[...] = jnp.zeros_like(next_ref)
+    next_ref[0:rank, 0:tok] = blocks[ring_source(me, n - 1, n)]
+    next_ref[rank : rank + 1, 0:1] = top
+    extra_ref[...] = jnp.zeros_like(extra_ref)
+    for i in range(rank):
+        extra_ref[:, i : i + 1] = jnp.sum(mean * mean[i : i + 1, :], axis=1, keepdims=True)
+    extra_ref[:, rank : rank + 1] = jnp.broadcast_to(top, (rank, 1))
 
 
 def error_right_kernel(p_ref, e_ref, out_ref, p3):
@@ -211,40 +216,49 @@
     return rows
 
 
-def right_kernel(n, p_ref, r_ref, g_ref, *refs):
-    pieces = refs[:n]
-    ortho_ref, keep_ref, send_ref, inbox, z, z3, outbox = refs[n:]
-    rank = p_ref.shape[0]
-    tok = g_ref.shape[1]
-    half = keep_ref.shape[1]
-    me_t = lax.axis_index("tensor")
+def right_kernel(r_ref, y_ref, got_ref, extra_ref, *refs):
+    held, (keep_ref, send_ref, y3, outbox) = refs[:-4], refs[-4:]
+    rank = r_ref.shape[0]
+    tok = held[0].shape[1]
+    half = r_ref.shape[1] // 2
     core = lax.rem(lax.axis_index("dp"), 2)
-    for k in range(n):
-        inbox[lax.rem(me_t - k + n, n)] = pieces[k][...]
-    gram = inbox[0, rank : 2 * rank, 0:rank]
-    for t in range(1, n):
-        gram = gram + inbox[t, rank : 2 * rank, 0:rank]
-    inv = lower_inverse(gram, rank)
-    for t in range(n):
-        top = inbox[t, rank : rank + 1, rank : rank + 1]
-        scaled = {key: value * top for key, value in inv.items()}
-        for i, row in enumerate(solve_rows(scaled, inbox[t, 0:rank, 0:tok], rank)):
-            if t == 0:
-                z[i : i + 1, :] = row
-            else:
-                z[i : i + 1, :] += row
-    for i, row in enumerate(solve_rows(inv, p_ref[...], rank)):
-        ortho_ref[i : i + 1, :] = row
-    terms = stack3(z[...], z3)
+    mine = extra_ref[0:1, rank : rank + 1]
+    theirs = got_ref[rank : rank + 1, 0:1]
+    top = jnp.maximum(mine, theirs)
+    products = y_ref[...] * (mine / top)
+    joint = products[:, 0:tok] + got_ref[0:rank, 0:tok] * (theirs / top)
+    terms = stack3(jnp.concatenate([joint, products[:, tok:]], axis=1), y3)
     for h in range(2):
-        cols = slice(h * half, (h + 1) * half)
-        fresh = sum3(dot(terms, g_ref[0, :, cols], (1, 0)), rank) * 1024.0
-        for i, row in enumerate(solve_rows(inv, r_ref[:, cols], rank)):
-            outbox[h, i : i + 1, :] = row + fresh[i : i + 1, :]
+        for c in range(half // BLOCK):
+            at = h * half + c * BLOCK
+            cols = slice(at, at + BLOCK)
+            grads = jnp.concatenate([g[0, :, cols] for g in held], axis=0)
+            fresh = sum3(dot(terms, grads, (1, 0)), rank)
+            outbox[h, :, c * BLOCK : (c + 1) * BLOCK] = r_ref[:, cols] * (mine / top) + fresh
+        outbox[h, :, half:] = extra_ref[...]
+        outbox[h, :, half + rank : half + rank + 1] = jnp.broadcast_to(top, (rank, 1))
     keep_ref[...] = outbox[core]
     send_ref[...] = outbox[1 - core]
 
 
+def join_kernel(rank, *refs):
+    xs, out_ref = refs[:-1], refs[-1]
+    half = out_ref.shape[1] - 128
+    mark = slice(half + rank, half + rank + 1)
+    tops = [x[0:1, mark] for x in xs]
+    top = jnp.maximum(tops[0], tops[1])
+    for other in tops[2:]:
+        top = jnp.maximum(top, other)
+
+    def total(terms):
+        first = terms[0] + terms[1]
+        return first + (terms[2] + terms[3]) if len(terms) == 4 else first
+
+    out_ref[:, :half] = total([x[:, :half] * (t / top) for x, t in zip(xs, tops)])
+    out_ref[:, half:] = total([x[:, half:] for x in xs])
+    out_ref[:, mark] = jnp.broadcast_to(top, (rank, 1))
+
+
 def add_kernel(*refs):
     refs[-1][...] = total_of(refs[:-1])
 
@@ -253,15 +267,22 @@
 RIGHT_TERMS = (0, 1, 0, 2, 0, 1)
 
 
-def factor_kernel(scale, ortho_ref, mine_ref, other_ref, whole_ref, left_ref, right_ref, inbox, left, right):
-    rank, half = mine_ref.shape
+def factor_kernel(m, p_ref, mine_ref, other_ref, whole_ref, left_ref, right_ref, inbox, ortho, left, right):
+    rank = mine_ref.shape[0]
+    half = mine_ref.shape[1] - 128
     core = lax.rem(lax.axis_index("dp"), 2)
     inbox[core] = mine_ref[...]
     inbox[1 - core] = other_ref[...]
+    inv = lower_inverse(inbox[0, :, half : half + rank] * (1.0 / m), rank)
+    top = inbox[0, 0:1, half + rank : half + rank + 1] * (ROOM / (m * m))
+    scaled = {key: value * top for key, value in inv.items()}
+    for i, row in enumerate(solve_rows(inv, p_ref[...], rank)):
+        ortho[i : i + 1, :] = row
     for h in range(2):
-        whole_ref[:, h * half : (h + 1) * half] = inbox[h] * scale
+        for i, row in enumerate(solve_rows(scaled, inbox[h, :, 0:half], rank)):
+            whole_ref[i : i + 1, h * half : (h + 1) * half] = row
     for terms, x, ref in (
-        (LEFT_TERMS, ortho_ref[...], left),
+        (LEFT_TERMS, ortho[...], left),
         (RIGHT_TERMS, whole_ref[...], right),
     ):
         parts = split(x)
@@ -356,8 +377,6 @@
     def step(x):
         return ring_step(x, "tensor", n)
 
-    wide = width // 4
-    narrow = width // 2 - wide
     ring = [out_grads, step(out_grads)]
 
     gw, w_terms = call(
@@ -381,8 +400,8 @@
     gw, ew = after(gw, ew)
     gws = exchange([gw] * n, "tensor", n)
     ring[1], gws = after(ring[1], gws)
-    x1, y1 = cut(ring[1], [2 * wide, 2 * narrow])
-    xs, ys = [x1, step(x1)], [y1]
+    for _ in range(n - 2 - 1):
+        ring.append(step(ring[-1]))
     left = call(
         left_kernel, sds((rank, rows), F32), [pltpu.VMEM((3 * rank, tok), F32)], "left"
     )(activations, ew, *gws)
@@ -390,60 +409,66 @@
     for group in groups(m // 2)[:-1]:
         left = add(*terms_of(left, "dp", m, [2 * bit for bit in group]))
     lefts = terms_of(left, "dp", m, [2 * bit for bit in groups(m // 2)[-1]])
-    xs[1], lefts[1:] = after(xs[1], lefts[1:])
-    mean, *msgs = call(
+    mean, scaled, extra, held, following = call(
         functools.partial(mean_kernel, n, 1.0 / (SHRINK * m)),
-        [sds((rank, rows), F32)] + [sds((8, 128), F32)] * n,
-        [pltpu.VMEM((3 * rank, rows), F32), pltpu.VMEM((n, 8, 128), F32)],
+        [
+            sds((rank, rows), F32),
+            sds((rank, rows), F32),
+            sds((rank, 128), F32),
+            sds((rank, (n - 1) * tok), F32),
+            sds((8, 128), F32),
+        ],
+        [pltpu.VMEM((3 * rank, rows), F32), pltpu.VMEM((n, rank, tok), F32)],
         "mean",
     )(activations, *lefts)
-    msgs = exchange(msgs, "tensor", n)
+    got = step(following)
 
     right_raw = call(
         error_right_kernel,
         sds((rank, width), F32),
         [pltpu.VMEM((3 * rank, rows), F32)],
         "error_right", None, 1.2e9,
-    )(mean, error_v)
-
-    ortho, keep, send = call(
-        functools.partial(right_kernel, n),
-        [sds((rank, rows), F32), sds((rank, half), F32), sds((rank, half), F32)],
+    )(scaled, error_v)
+
+    keep, send = call(
+        right_kernel,
+        [sds((rank, half + 128), F32)] * 2,
         [
-            pltpu.VMEM((n, 8, 128), F32),
-            pltpu.VMEM((rank, tok), F32),
-            pltpu.VMEM((3 * rank, tok), F32),
-            pltpu.VMEM((2, rank, half), F32),
+            pltpu.VMEM((3 * rank, (n - 1) * tok), F32),
+            pltpu.VMEM((2, rank, half + 128), F32),
         ],
         "right",
-    )(mean, right_raw, out_grads, *msgs)
+    )(right_raw, held, got, extra, *ring)
     total = add(keep, swap(send, "dp", m, 1))
-    for _ in range(3, n):
-        last, total = after(ys[-1], total)
-        ys.append(step(last))
-    for _ in range(4, n):
-        last, total = after(xs[-1], total)
-        xs.append(step(last))
+
+    widths = [half, half // 2, half // 2]
+    last, total = after(ring[-1], total)
+    newest = list(cut(last, widths))
+    newest[0] = step(newest[0])
     for group in groups(m // 2):
         total = add(*terms_of(total, "dp", m, [2 * bit for bit in group]))
-    (xs[-1], ys[-1]), total = after((xs[-1], ys[-1]), total)
+    newest[0], total = after(newest[0], total)
     for group in groups(n):
-        total = add(*terms_of(total, "tensor", n, group))
-    xa, xb = cut(xs[-1], [wide, wide])
-    (xa, xb), total = after((xa, xb), total)
-    xa, xb = step(xa), step(xb)
+        parts = terms_of(total, "tensor", n, group)
+        total = call(
+            functools.partial(join_kernel, rank), sds(total.shape, F32), [], "join"
+        )(*parts)
+    for c in range(1, len(widths)):
+        last, total = after(newest[c], total)
+        newest[c] = step(last)
 
     terms = len(LEFT_TERMS) * rank
     whole, left_terms, right_terms = call(
-        functools.partial(factor_kernel, 1.0 / m),
+        functools.partial(factor_kernel, m),
         [sds((rank, width), F32), sds((rows, terms), BF16), sds((terms, width), BF16)],
         [
-            pltpu.VMEM((2, rank, half), F32),
+            pltpu.VMEM((2, rank, half + 128), F32),
+            pltpu.VMEM((rank, rows), F32),
             pltpu.VMEM((terms, rows), F32),
             pltpu.VMEM((terms, width), F32),
         ],
         "factor",
-    )(ortho, total, swap(total, "dp", m, 1))
+    )(mean, total, swap(total, "dp", m, 1))
 
     acts = call(
         functools.partial(acts_kernel, n),
@@ -451,19 +476,10 @@
         [pltpu.VMEM((tokens, rows), BF16)],
         "acts",
     )(activations)
-    last, right_terms = after(ys[-1], right_terms)
-    ya, yb = cut(last, [narrow, narrow])
     pieces = []
     at = 0
-    for part, base, held, newest in (
-        (wide, 0, xs, xa),
-        (wide, 0, xs, xb),
-        (narrow, 2 * wide, ys, step(ya)),
-        (narrow, 2 * wide, ys, step(yb)),
-    ):
-        slots = ring + held[1 : n - 2] + [newest]
-        bases = [0, 0] + [base] * (n - 3) + [at]
-        pieces.append((at, part, slots, bases))
+    for part, x in zip(widths, newest):
+        pieces.append((at, part, ring + [x], [0] * (n - 1) + [at]))
         at += part
 
     outs = ()

time: 79.3 us -> 71.7 us (0.904)
  starting transfers between devices: 30.6 us -> 26.8 us
  waiting for transfers between devices: 28.7 us -> 25.2 us
    ppermute x6 -> x3, starting transfers between devices: 8.19 us -> 3.65 us  [exchange(): lax.ppermute(pieces[k], axis, [(i, (i + k) % n) for i in range(n)])]
    ppermute x6 -> x3, waiting for transfers between devices: 9.7 us -> 6.99 us  [exchange(): lax.ppermute(pieces[k], axis, [(i, (i + k) % n) for i in range(n)])]
    ppermute x12, waiting for transfers between devices: 13.5 us -> 12.5 us  [swap(): return lax.ppermute(x, axis, [(i, i ^ bit) for i in range(n)])]
    ppermute x7 -> x6, starting transfers between devices: 10.8 us -> 11.7 us  [ring_step(): lax.ppermute(x, axis, [(ring[p], ring[(p + 1) % n]) for p in range(n)])]
    pallas_call x4 -> x3, Pallas kernels: 9.88 us -> 9.08 us  [per_device(): pl.pallas_call(functools.partial(final_kernel, at, part, bases), in_specs...]
    pallas_call x2 -> x3, Pallas kernels: 1.52 us -> 1.95 us  [the longest x1 1.26 us: per_device(): call(functools.partial(factor_kernel, m), [sds((rank, width), F32), sds((...]
    ppermute x7 -> x6, waiting for transfers between devices: 5.5 us -> 5.78 us  [ring_step(): lax.ppermute(x, axis, [(ring[p], ring[(p + 1) % n]) for p in range(n)])]
  transfers between devices with their start and end apart: 25 -> 21, of which waited for: 18 -> 16; matrix products, arithmetic and copies ran while one was open for 0% -> 0% of each run, Pallas kernels for 19% -> 22%
where the time goes in v14:
time: 71.7 us; the launch traced here: 71.6 us
  starting transfers between devices  26.8 us (37%)
  waiting for transfers between devices  25.2 us (35%)
  Pallas kernels  18.7 us (26%)
  between operations  0.77 us (1%)
    ppermute x12, waiting for transfers between devices, swap(): return lax.ppermute(x, axis, [(i, i ^ bit) for i in range(n)])  12.5 us
    ppermute x6, starting transfers between devices, ring_step(): lax.ppermute(x, axis, [(ring[p], ring[(p + 1) % n]) for p in range(n)])  11.7 us
    ppermute x12, starting transfers between devices, swap(): return lax.ppermute(x, axis, [(i, i ^ bit) for i in range(n)])  11.5 us
    pallas_call x3, Pallas kernels, per_device(): pl.pallas_call(functools.partial(final_kernel, at, part, bases), in_specs...  9.08 us
    ppermute x3, waiting for transfers between devices, exchange(): lax.ppermute(pieces[k], axis, [(i, (i + k) % n) for i in range(n)])  6.99 us
    ppermute x6, waiting for transfers between devices, ring_step(): lax.ppermute(x, axis, [(ring[p], ring[(p + 1) % n]) for p in range(n)])  5.78 us
    pallas_call x1, Pallas kernels, per_device(): call(error_left_kernel, [sds((rank, rows), F32), sds((1, rows, width), BF...  4.19 us
    ppermute x3, starting transfers between devices, exchange(): lax.ppermute(pieces[k], axis, [(i, (i + k) % n) for i in range(n)])  3.65 us
  transfers between devices with their start and end apart: 21, of which 16 were waited for; matrix products, arithmetic and copies ran while one was open for 0% of the time, Pallas kernels for 22%

profile of v14, /device:TPU:0, one launch (start us, length us, event | category | flops | bytes accessed | tf_op | source)
XLA Modules:
  0.0 71.6 jit_solution(1862555497709790271)
XLA Ops:
  0.6 4.1 %collective-permute-start = (bf16[1,64,5120]{2,1,0:T(8,128)(2,1)}, bf16[1,64,5120]{2,1,0:T(8,128)(2,1)S(1)}, u32[]{:S(2)}, u32[]{:S(2)}) collective-permute-start(bf16[1,64,5120]{2,1,0:T(8,128)(2,1)} %refs_0_.7), channel_id=1, source_target_pairs={{0,2},{2,3},{3,1},{1,0},{4,6},{6,7},{7,5},{5,4},{8,10},{10,11},{11... | collective-permute-start | bytes 1966088 | tf_op jit(solution)/shard_map/ppermute | solution.py:61
  4.7 1.5 %token_factor.1 = (f32[8,128]{1,0:T(8,128)S(1)}, bf16[12,5120]{1,0:T(8,128)(2,1)S(1)}) custom-call(f32[4,5120]{1,0:T(4,128)} %bitcast.2, bf16[1,64,5120]{2,1,0:T(8,128)(2,1)} %refs_0_.7), custom_call_target="tpu_custom_call" | custom-call | flops 1 | bytes 1 | tf_op jit(solution)/shard_map/token_factor/pallas_call | solution.py:382
  6.2 4.2 %error_left.1 = (f32[4,768]{1,0:T(4,128)S(1)}, bf16[1,768,5120]{2,1,0:T(8,128)(2,1)S(1)}) custom-call(bf16[12,5120]{1,0:T(8,128)(2,1)S(1)} %get-tuple-element.42.terms_ref, bf16[1,768,5120]{2,1,0:T(8,128)(2,1)} %e_hbm.1), custom_call_target="tpu_custom_call" | custom-call | flops 4600000000 | bytes 1 | tf_op jit(solution)/shard_map/error_left/pallas_call | solution.py:393
  10.4 1.4 %collective-permute-start.3 = (f32[8,128]{1,0:T(8,128)S(1)}, f32[8,128]{1,0:T(8,128)S(1)}, u32[]{:S(2)}, u32[]{:S(2)}) collective-permute-start(f32[8,128]{1,0:T(8,128)S(1)} %get-tuple-element.46.refs_0_), channel_id=1, source_target_pairs={{0,3},{1,0},{2,1},{3,2},{4,7},{5,4},{6,5},{7,6},{8,11},{9,8},{10,9... | collective-permute-start | bytes 12296 | tf_op jit(solution)/shard_map/ppermute | solution.py:66
  12.1 1.9 %collective-permute-start.1 = (f32[8,128]{1,0:T(8,128)S(1)}, f32[8,128]{1,0:T(8,128)S(1)}, u32[]{:S(2)}, u32[]{:S(2)}) collective-permute-start(f32[8,128]{1,0:T(8,128)S(1)} %get-tuple-element.46.refs_0_), channel_id=1, source_target_pairs={{0,1},{1,2},{2,3},{3,0},{4,5},{5,6},{6,7},{7,4},{8,9},{9,10},{10,1... | collective-permute-start | bytes 12296 | tf_op jit(solution)/shard_map/ppermute | solution.py:66
  14.1 5.1 %collective-permute-done.3.refs_3_ = f32[8,128]{1,0:T(8,128)S(1)} collective-permute-done((f32[8,128]{1,0:T(8,128)S(1)}, f32[8,128]{1,0:T(8,128)S(1)}, u32[]{:S(2)}, u32[]{:S(2)}) %collective-permute-start.3) | collective-permute-done | bytes 4128 | tf_op jit(solution)/shard_map/ppermute | solution.py:66
  19.2 1.9 %collective-permute-done.2.refs_2_ = f32[8,128]{1,0:T(8,128)S(1)} collective-permute-done((f32[8,128]{1,0:T(8,128)S(1)}, f32[8,128]{1,0:T(8,128)S(1)}, u32[]{:S(2)}, u32[]{:S(2)}) %collective-permute-start.2) | collective-permute-done | bytes 4128 | tf_op jit(solution)/shard_map/ppermute | solution.py:66
  21.1 1.6 %collective-permute-start.8 = (bf16[1,64,5120]{2,1,0:T(8,128)(2,1)S(1)}, bf16[1,64,5120]{2,1,0:T(8,128)(2,1)S(1)}, u32[]{:S(2)}, u32[]{:S(2)}) collective-permute-start(bf16[1,64,5120]{2,1,0:T(8,128)(2,1)S(1)} %collective-permute-done.refs_1_), channel_id=1, source_target_pairs={{0,2},{2,3},{3,1},{1,0},{4,6},{6,7},{7,5},{5,4},{8,10},{10,11},{11... | collective-permute-start | bytes 1966088 | tf_op jit(solution)/shard_map/ppermute | solution.py:61
  24.1 2.4 %collective-permute-start.7 = (f32[4,768]{1,0:T(4,128)S(1)}, f32[4,768]{1,0:T(4,128)S(1)}, u32[]{:S(2)}, u32[]{:S(2)}) collective-permute-start(f32[4,768]{1,0:T(4,128)S(1)} %add.3.refs_0_), channel_id=1, source_target_pairs={{0,24},{4,28},{8,16},{12,20},{16,8},{20,12},{24,0},{28,4},{1,25},{... | collective-permute-start | bytes 36872 | tf_op jit(solution)/shard_map/ppermute | solution.py:71
  28.7 1.5 %collective-permute-done.6.refs_2_ = f32[4,768]{1,0:T(4,128)S(1)} collective-permute-done((f32[4,768]{1,0:T(4,128)S(1)}, f32[4,768]{1,0:T(4,128)S(1)}, u32[]{:S(2)}, u32[]{:S(2)}) %collective-permute-start.6) | collective-permute-done | bytes 12320 | tf_op jit(solution)/shard_map/ppermute | solution.py:71
  31.1 1.4 %collective-permute-start.9 = (f32[8,128]{1,0:T(8,128)S(1)}, f32[8,128]{1,0:T(8,128)S(1)}, u32[]{:S(2)}, u32[]{:S(2)}) collective-permute-start(f32[8,128]{1,0:T(8,128)S(1)} %get-tuple-element.55), channel_id=1, source_target_pairs={{0,2},{2,3},{3,1},{1,0},{4,6},{6,7},{7,5},{5,4},{8,10},{10,11},{11... | collective-permute-start | bytes 12296 | tf_op jit(solution)/shard_map/ppermute | solution.py:61
  33.7 4.2 %collective-permute-done.9.got_ref = f32[8,128]{1,0:T(8,128)S(1)} collective-permute-done((f32[8,128]{1,0:T(8,128)S(1)}, f32[8,128]{1,0:T(8,128)S(1)}, u32[]{:S(2)}, u32[]{:S(2)}) %collective-permute-start.9) | collective-permute-done | bytes 4128 | tf_op jit(solution)/shard_map/ppermute | solution.py:61
  41.1 2.4 %collective-permute-start.14 = (f32[4,2688]{1,0:T(4,128)S(1)}, f32[4,2688]{1,0:T(4,128)S(1)}, u32[]{:S(2)}, u32[]{:S(2)}) collective-permute-start(f32[4,2688]{1,0:T(4,128)S(1)} %add.4.refs_0_), channel_id=1, source_target_pairs={{0,24},{4,28},{8,16},{12,20},{16,8},{20,12},{24,0},{28,4},{1,25},{... | collective-permute-start | bytes 129032 | tf_op jit(solution)/shard_map/ppermute | solution.py:71
  44.6 1.5 %collective-permute-done.14.refs_3_ = f32[4,2688]{1,0:T(4,128)S(1)} collective-permute-done((f32[4,2688]{1,0:T(4,128)S(1)}, f32[4,2688]{1,0:T(4,128)S(1)}, u32[]{:S(2)}, u32[]{:S(2)}) %collective-permute-start.14) | collective-permute-done | bytes 43040 | tf_op jit(solution)/shard_map/ppermute | solution.py:71
  46.1 1.5 %collective-permute-done.13.refs_2_ = f32[4,2688]{1,0:T(4,128)S(1)} collective-permute-done((f32[4,2688]{1,0:T(4,128)S(1)}, f32[4,2688]{1,0:T(4,128)S(1)}, u32[]{:S(2)}, u32[]{:S(2)}) %collective-permute-start.13) | collective-permute-done | bytes 43040 | tf_op jit(solution)/shard_map/ppermute | solution.py:71
  48.1 1.6 %collective-permute-done.11.refs_3_ = bf16[1,64,2560]{2,1,0:T(8,128)(2,1)S(1)} collective-permute-done((bf16[1,64,2560]{2,1,0:T(8,128)(2,1)S(1)}, bf16[1,64,2560]{2,1,0:T(8,128)(2,1)S(1)}, u32[]{:S(2)}, u32[]{:S(2)}) %collective-permute-start.11) | collective-permute-done | bytes 327712 | tf_op jit(solution)/shard_map/ppermute | solution.py:61
  50.7 1.8 %collective-permute-start.16 = (f32[4,2688]{1,0:T(4,128)S(1)}, f32[4,2688]{1,0:T(4,128)S(1)}, u32[]{:S(2)}, u32[]{:S(2)}) collective-permute-start(f32[4,2688]{1,0:T(4,128)S(1)} %add.5.refs_0_), channel_id=1, source_target_pairs={{0,2},{1,3},{2,0},{3,1},{4,6},{5,7},{6,4},{7,5},{8,10},{9,11},{10,... | collective-permute-start | bytes 129032 | tf_op jit(solution)/shard_map/ppermute | solution.py:71
  52.5 1.6 %collective-permute-start.15 = (f32[4,2688]{1,0:T(4,128)S(1)}, f32[4,2688]{1,0:T(4,128)S(1)}, u32[]{:S(2)}, u32[]{:S(2)}) collective-permute-start(f32[4,2688]{1,0:T(4,128)S(1)} %add.5.refs_0_), channel_id=1, source_target_pairs={{0,1},{1,0},{2,3},{3,2},{4,5},{5,4},{6,7},{7,6},{8,9},{9,8},{10,11... | collective-permute-start | bytes 129032 | tf_op jit(solution)/shard_map/ppermute | solution.py:71
  54.1 1.6 %collective-permute-done.17.refs_3_ = f32[4,2688]{1,0:T(4,128)S(1)} collective-permute-done((f32[4,2688]{1,0:T(4,128)S(1)}, f32[4,2688]{1,0:T(4,128)S(1)}, u32[]{:S(2)}, u32[]{:S(2)}) %collective-permute-start.17) | collective-permute-done | bytes 43040 | tf_op jit(solution)/shard_map/ppermute | solution.py:71
  56.6 1.3 %collective-permute-start.20 = (bf16[1,64,1280]{2,1,0:T(8,128)(2,1)S(1)}, bf16[1,64,1280]{2,1,0:T(8,128)(2,1)S(1)}, u32[]{:S(2)}, u32[]{:S(2)}) collective-permute-start(bf16[1,64,1280]{2,1,0:T(8,128)(2,1)S(1)} %get-tuple-element.70), channel_id=1, source_target_pairs={{0,2},{2,3},{3,1},{1,0},{4,6},{6,7},{7,5},{5,4},{8,10},{10,11},{11... | collective-permute-start | bytes 491528 | tf_op jit(solution)/shard_map/ppermute | solution.py:61
  58.0 2.0 %collective-permute-start.19 = (bf16[1,64,1280]{2,1,0:T(8,128)(2,1)S(1)}, bf16[1,64,1280]{2,1,0:T(8,128)(2,1)S(1)}, u32[]{:S(2)}, u32[]{:S(2)}) collective-permute-start(bf16[1,64,1280]{2,1,0:T(8,128)(2,1)S(1)} %get-tuple-element.69), channel_id=1, source_target_pairs={{0,2},{2,3},{3,1},{1,0},{4,6},{6,7},{7,5},{5,4},{8,10},{10,11},{11... | collective-permute-start | bytes 491528 | tf_op jit(solution)/shard_map/ppermute | solution.py:61
  62.4 4.1 %rebuild.3 = (bf16[768,5120]{1,0:T(8,128)(2,1)}, bf16[1,768,5120]{2,1,0:T(8,128)(2,1)}) custom-call(bf16[768,256]{1,0:T(8,128)(2,1)S(1)} %acts.1.acts_ref, bf16[768,24]{1,0:T(8,128)(2,1)S(1)} %get-tuple-element.67.left_ref, bf16[24,5120]{1,0:T(8,128)(2,1)S(1)} %get-tuple-element.68.right_ref, bf16[1,768,5120]{2,1,0:T(8,128)(2,1)S(1)} %get-tuple-element.53.e_ref, ...), custom_call_target="tpu_custom_call" | custom-call | flops 1 | bytes 1 | tf_op jit(solution)/shard_map/rebuild/pallas_call | solution.py:487
  66.6 2.5 %rebuild.4 = (bf16[768,5120]{1,0:T(8,128)(2,1)}, bf16[1,768,5120]{2,1,0:T(8,128)(2,1)}) custom-call(bf16[768,256]{1,0:T(8,128)(2,1)S(1)} %acts.1.acts_ref, bf16[768,24]{1,0:T(8,128)(2,1)S(1)} %get-tuple-element.67.left_ref, bf16[24,5120]{1,0:T(8,128)(2,1)S(1)} %get-tuple-element.68.right_ref, ...), custom_call_target="tpu_custom_call", output_to_operand_aliasing={{0}: (8, {}), {1}: (9, {})} | custom-call | flops 1 | bytes 1 | tf_op jit(solution)/shard_map/rebuild/pallas_call | solution.py:487
  69.1 2.5 %rebuild.5 = (bf16[768,5120]{1,0:T(8,128)(2,1)}, bf16[1,768,5120]{2,1,0:T(8,128)(2,1)}) custom-call(bf16[768,256]{1,0:T(8,128)(2,1)S(1)} %acts.1.acts_ref, bf16[768,24]{1,0:T(8,128)(2,1)S(1)} %get-tuple-element.67.left_ref, bf16[24,5120]{1,0:T(8,128)(2,1)S(1)} %get-tuple-element.68.right_ref, ...), custom_call_target="tpu_custom_call", output_to_operand_aliasing={{0}: (8, {}), {1}: (9, {})} | custom-call | flops 1 | bytes 1 | tf_op jit(solution)/shard_map/rebuild/pallas_call | solution.py:487
  (38 shorter events, 15.0 us)
Async XLA Ops:
  0.6 20.5 %collective-permute-start = (bf16[1,64,5120]{2,1,0:T(8,128)(2,1)}, bf16[1,64,5120]{2,1,0:T(8,128)(2,1)S(1)}, u32[]{:S(2)}, u32[]{:S(2)}) collective-permute-start(bf16[1,64,5120]{2,1,0:T(8,128)(2,1)} %refs_0_.7), channel_id=1, source_target_pairs={{0,2},{2,3},{3,1},{1,0},{4,6},{6,7},{7,5},{5,4},{8,10},{10,11},{11... | collective-permute-start | bytes 1966088 | tf_op jit(solution)/shard_map/ppermute | solution.py:61
  6.2 16.5 %copy-start.1 = (bf16[1,256,768]{2,1,0:T(8,128)(2,1)S(1)}, bf16[1,256,768]{2,1,0:T(8,128)(2,1)}, u32[]{:S(2)}) copy-start(bf16[1,256,768]{2,1,0:T(8,128)(2,1)} %a_ref.5) | copy-start | bytes 1179652
  10.4 27.5 %copy-start = (bf16[1,64,5120]{2,1,0:T(8,128)(2,1)S(1)}, bf16[1,64,5120]{2,1,0:T(8,128)(2,1)}, u32[]{:S(2)}) copy-start(bf16[1,64,5120]{2,1,0:T(8,128)(2,1)} %refs_0_.7) | copy-start | bytes 1966084
  10.4 8.8 %collective-permute-start.3 = (f32[8,128]{1,0:T(8,128)S(1)}, f32[8,128]{1,0:T(8,128)S(1)}, u32[]{:S(2)}, u32[]{:S(2)}) collective-permute-start(f32[8,128]{1,0:T(8,128)S(1)} %get-tuple-element.46.refs_0_), channel_id=1, source_target_pairs={{0,3},{1,0},{2,1},{3,2},{4,7},{5,4},{6,5},{7,6},{8,11},{9,8},{10,9... | collective-permute-start | bytes 12296 | tf_op jit(solution)/shard_map/ppermute | solution.py:66
  11.8 9.2 %collective-permute-start.2 = (f32[8,128]{1,0:T(8,128)S(1)}, f32[8,128]{1,0:T(8,128)S(1)}, u32[]{:S(2)}, u32[]{:S(2)}) collective-permute-start(f32[8,128]{1,0:T(8,128)S(1)} %get-tuple-element.46.refs_0_), channel_id=1, source_target_pairs={{0,2},{1,3},{2,0},{3,1},{4,6},{5,7},{6,4},{7,5},{8,10},{9,11},{10,... | collective-permute-start | bytes 12296 | tf_op jit(solution)/shard_map/ppermute | solution.py:66
  12.1 8.9 %collective-permute-start.1 = (f32[8,128]{1,0:T(8,128)S(1)}, f32[8,128]{1,0:T(8,128)S(1)}, u32[]{:S(2)}, u32[]{:S(2)}) collective-permute-start(f32[8,128]{1,0:T(8,128)S(1)} %get-tuple-element.46.refs_0_), channel_id=1, source_target_pairs={{0,1},{1,2},{2,3},{3,0},{4,5},{5,6},{6,7},{7,4},{8,9},{9,10},{10,1... | collective-permute-start | bytes 12296 | tf_op jit(solution)/shard_map/ppermute | solution.py:66
  21.1 16.8 %collective-permute-start.8 = (bf16[1,64,5120]{2,1,0:T(8,128)(2,1)S(1)}, bf16[1,64,5120]{2,1,0:T(8,128)(2,1)S(1)}, u32[]{:S(2)}, u32[]{:S(2)}) collective-permute-start(bf16[1,64,5120]{2,1,0:T(8,128)(2,1)S(1)} %collective-permute-done.refs_1_), channel_id=1, source_target_pairs={{0,2},{2,3},{3,1},{1,0},{4,6},{6,7},{7,5},{5,4},{8,10},{10,11},{11... | collective-permute-start | bytes 1966088 | tf_op jit(solution)/shard_map/ppermute | solution.py:61
  22.9 1.2 %collective-permute-start.4 = (f32[4,768]{1,0:T(4,128)S(1)}, f32[4,768]{1,0:T(4,128)S(1)}, u32[]{:S(2)}, u32[]{:S(2)}) collective-permute-start(f32[4,768]{1,0:T(4,128)S(1)} %left.1.refs_0_), channel_id=1, source_target_pairs={{0,4},{4,0},{8,12},{12,8},{16,20},{20,16},{24,28},{28,24},{1,5},{5... | collective-permute-start | bytes 36872 | tf_op jit(solution)/shard_map/ppermute | solution.py:71
  24.1 4.6 %collective-permute-start.7 = (f32[4,768]{1,0:T(4,128)S(1)}, f32[4,768]{1,0:T(4,128)S(1)}, u32[]{:S(2)}, u32[]{:S(2)}) collective-permute-start(f32[4,768]{1,0:T(4,128)S(1)} %add.3.refs_0_), channel_id=1, source_target_pairs={{0,24},{4,28},{8,16},{12,20},{16,8},{20,12},{24,0},{28,4},{1,25},{... | collective-permute-start | bytes 36872 | tf_op jit(solution)/shard_map/ppermute | solution.py:71
  26.6 3.7 %collective-permute-start.6 = (f32[4,768]{1,0:T(4,128)S(1)}, f32[4,768]{1,0:T(4,128)S(1)}, u32[]{:S(2)}, u32[]{:S(2)}) collective-permute-start(f32[4,768]{1,0:T(4,128)S(1)} %add.3.refs_0_), channel_id=1, source_target_pairs={{0,16},{4,20},{8,24},{12,28},{16,0},{20,4},{24,8},{28,12},{1,17},{... | collective-permute-start | bytes 36872 | tf_op jit(solution)/shard_map/ppermute | solution.py:71
  27.1 3.7 %collective-permute-start.5 = (f32[4,768]{1,0:T(4,128)S(1)}, f32[4,768]{1,0:T(4,128)S(1)}, u32[]{:S(2)}, u32[]{:S(2)}) collective-permute-start(f32[4,768]{1,0:T(4,128)S(1)} %add.3.refs_0_), channel_id=1, source_target_pairs={{0,8},{4,12},{8,0},{12,4},{16,24},{20,28},{24,16},{28,20},{1,9},{5... | collective-permute-start | bytes 36872 | tf_op jit(solution)/shard_map/ppermute | solution.py:71
  31.1 6.8 %collective-permute-start.9 = (f32[8,128]{1,0:T(8,128)S(1)}, f32[8,128]{1,0:T(8,128)S(1)}, u32[]{:S(2)}, u32[]{:S(2)}) collective-permute-start(f32[8,128]{1,0:T(8,128)S(1)} %get-tuple-element.55), channel_id=1, source_target_pairs={{0,2},{2,3},{3,1},{1,0},{4,6},{6,7},{7,5},{5,4},{8,10},{10,11},{11... | collective-permute-start | bytes 12296 | tf_op jit(solution)/shard_map/ppermute | solution.py:61
  38.5 1.3 %collective-permute-start.10 = (f32[4,2688]{1,0:T(4,128)S(1)}, f32[4,2688]{1,0:T(4,128)S(1)}, u32[]{:S(2)}, u32[]{:S(2)}) collective-permute-start(f32[4,2688]{1,0:T(4,128)S(1)} %get-tuple-element.58), channel_id=1, source_target_pairs={{0,4},{4,0},{8,12},{12,8},{16,20},{20,16},{24,28},{28,24},{1,5},{5... | collective-permute-start | bytes 129032 | tf_op jit(solution)/shard_map/ppermute | solution.py:71
  39.9 9.8 %collective-permute-start.11 = (bf16[1,64,2560]{2,1,0:T(8,128)(2,1)S(1)}, bf16[1,64,2560]{2,1,0:T(8,128)(2,1)S(1)}, u32[]{:S(2)}, u32[]{:S(2)}) collective-permute-start(bf16[1,64,2560]{2,1,0:T(8,128)(2,1)S(1)} %get-tuple-element.62), channel_id=1, source_target_pairs={{0,2},{2,3},{3,1},{1,0},{4,6},{6,7},{7,5},{5,4},{8,10},{10,11},{11... | collective-permute-start | bytes 983048 | tf_op jit(solution)/shard_map/ppermute | solution.py:61
  41.1 5.0 %collective-permute-start.14 = (f32[4,2688]{1,0:T(4,128)S(1)}, f32[4,2688]{1,0:T(4,128)S(1)}, u32[]{:S(2)}, u32[]{:S(2)}) collective-permute-start(f32[4,2688]{1,0:T(4,128)S(1)} %add.4.refs_0_), channel_id=1, source_target_pairs={{0,24},{4,28},{8,16},{12,20},{16,8},{20,12},{24,0},{28,4},{1,25},{... | collective-permute-start | bytes 129032 | tf_op jit(solution)/shard_map/ppermute | solution.py:71
  43.6 4.0 %collective-permute-start.13 = (f32[4,2688]{1,0:T(4,128)S(1)}, f32[4,2688]{1,0:T(4,128)S(1)}, u32[]{:S(2)}, u32[]{:S(2)}) collective-permute-start(f32[4,2688]{1,0:T(4,128)S(1)} %add.4.refs_0_), channel_id=1, source_target_pairs={{0,16},{4,20},{8,24},{12,28},{16,0},{20,4},{24,8},{28,12},{1,17},{... | collective-permute-start | bytes 129032 | tf_op jit(solution)/shard_map/ppermute | solution.py:71
  44.1 4.0 %collective-permute-start.12 = (f32[4,2688]{1,0:T(4,128)S(1)}, f32[4,2688]{1,0:T(4,128)S(1)}, u32[]{:S(2)}, u32[]{:S(2)}) collective-permute-start(f32[4,2688]{1,0:T(4,128)S(1)} %add.4.refs_0_), channel_id=1, source_target_pairs={{0,8},{4,12},{8,0},{12,4},{16,24},{20,28},{24,16},{28,20},{1,9},{5... | collective-permute-start | bytes 129032 | tf_op jit(solution)/shard_map/ppermute | solution.py:71
  49.7 6.0 %collective-permute-start.17 = (f32[4,2688]{1,0:T(4,128)S(1)}, f32[4,2688]{1,0:T(4,128)S(1)}, u32[]{:S(2)}, u32[]{:S(2)}) collective-permute-start(f32[4,2688]{1,0:T(4,128)S(1)} %add.5.refs_0_), channel_id=1, source_target_pairs={{0,3},{1,2},{2,1},{3,0},{4,7},{5,6},{6,5},{7,4},{8,11},{9,10},{10,... | collective-permute-start | bytes 129032 | tf_op jit(solution)/shard_map/ppermute | solution.py:71
  50.7 5.3 %collective-permute-start.16 = (f32[4,2688]{1,0:T(4,128)S(1)}, f32[4,2688]{1,0:T(4,128)S(1)}, u32[]{:S(2)}, u32[]{:S(2)}) collective-permute-start(f32[4,2688]{1,0:T(4,128)S(1)} %add.5.refs_0_), channel_id=1, source_target_pairs={{0,2},{1,3},{2,0},{3,1},{4,6},{5,7},{6,4},{7,5},{8,10},{9,11},{10,... | collective-permute-start | bytes 129032 | tf_op jit(solution)/shard_map/ppermute | solution.py:71
  52.5 4.0 %collective-permute-start.15 = (f32[4,2688]{1,0:T(4,128)S(1)}, f32[4,2688]{1,0:T(4,128)S(1)}, u32[]{:S(2)}, u32[]{:S(2)}) collective-permute-start(f32[4,2688]{1,0:T(4,128)S(1)} %add.5.refs_0_), channel_id=1, source_target_pairs={{0,1},{1,0},{2,3},{3,2},{4,5},{5,4},{6,7},{7,6},{8,9},{9,8},{10,11... | collective-permute-start | bytes 129032 | tf_op jit(solution)/shard_map/ppermute | solution.py:71
  56.6 9.9 %collective-permute-start.20 = (bf16[1,64,1280]{2,1,0:T(8,128)(2,1)S(1)}, bf16[1,64,1280]{2,1,0:T(8,128)(2,1)S(1)}, u32[]{:S(2)}, u32[]{:S(2)}) collective-permute-start(bf16[1,64,1280]{2,1,0:T(8,128)(2,1)S(1)} %get-tuple-element.70), channel_id=1, source_target_pairs={{0,2},{2,3},{3,1},{1,0},{4,6},{6,7},{7,5},{5,4},{8,10},{10,11},{11... | collective-permute-start | bytes 491528 | tf_op jit(solution)/shard_map/ppermute | solution.py:61
  58.0 11.1 %collective-permute-start.19 = (bf16[1,64,1280]{2,1,0:T(8,128)(2,1)S(1)}, bf16[1,64,1280]{2,1,0:T(8,128)(2,1)S(1)}, u32[]{:S(2)}, u32[]{:S(2)}) collective-permute-start(bf16[1,64,1280]{2,1,0:T(8,128)(2,1)S(1)} %get-tuple-element.69), channel_id=1, source_target_pairs={{0,2},{2,3},{3,1},{1,0},{4,6},{6,7},{7,5},{5,4},{8,10},{10,11},{11... | collective-permute-start | bytes 491528 | tf_op jit(solution)/shard_map/ppermute | solution.py:61
  60.0 1.2 %collective-permute-start.18 = (f32[4,2688]{1,0:T(4,128)S(1)}, f32[4,2688]{1,0:T(4,128)S(1)}, u32[]{:S(2)}, u32[]{:S(2)}) collective-permute-start(f32[4,2688]{1,0:T(4,128)S(1)} %join.1.mine_ref), channel_id=1, source_target_pairs={{0,4},{4,0},{8,12},{12,8},{16,20},{20,16},{24,28},{28,24},{1,5},{5... | collective-permute-start | bytes 129032 | tf_op jit(solution)/shard_map/ppermute | solution.py:71

commit v15 on v14

--- a/solution.py
+++ b/solution.py
@@ -206,14 +206,12 @@
     return inv
 
 
-def solve_rows(inv, x, rank):
-    rows = []
-    for i in range(rank):
-        row = inv[i, 0] * x[0:1, :]
-        for j in range(1, i + 1):
-            row = row + inv[i, j] * x[j : j + 1, :]
-        rows.append(row)
-    return rows
+def solve(inv, x, rank):
+    total = 0.0
+    for j in range(rank):
+        column = [inv.get((i, j), jnp.zeros((1, 1), F32)) for i in range(rank)]
+        total = total + jnp.concatenate(column, axis=0) * x[j : j + 1, :]
+    return total
 
 
 def right_kernel(r_ref, y_ref, got_ref, extra_ref, *refs):
@@ -276,11 +274,9 @@
     inv = lower_inverse(inbox[0, :, half : half + rank] * (1.0 / m), rank)
     top = inbox[0, 0:1, half + rank : half + rank + 1] * (ROOM / (m * m))
     scaled = {key: value * top for key, value in inv.items()}
-    for i, row in enumerate(solve_rows(inv, p_ref[...], rank)):
-        ortho[i : i + 1, :] = row
+    ortho[...] = solve(inv, p_ref[...], rank)
     for h in range(2):
-        for i, row in enumerate(solve_rows(scaled, inbox[h, :, 0:half], rank)):
-            whole_ref[i : i + 1, h * half : (h + 1) * half] = row
+        whole_ref[:, h * half : (h + 1) * half] = solve(scaled, inbox[h, :, 0:half], rank)
     for terms, x, ref in (
         (LEFT_TERMS, ortho[...], left),
         (RIGHT_TERMS, whole_ref[...], right),
@@ -307,9 +303,11 @@
     rebuilt_hbm, error_hbm, rebuilt_v, error_v, sems = refs[-5:]
     rows = e_ref.shape[1]
     wide = 256
-    high = rows // sems.shape[0]
+    strips, sides, _ = sems.shape
+    high = rows // strips
+    side = part // sides
     copies = []
-    for r in range(sems.shape[0]):
+    for r in range(strips):
         here = slice(r * high, (r + 1) * high)
         for c in range(part // wide):
             cols = slice(c * wide, (c + 1) * wide)
@@ -323,18 +321,17 @@
             rebuilt = dot(left_ref[here, :], right_ref[:, there], (1, 0))
             rebuilt_v[here, cols] = rebuilt.astype(BF16)
             error_v[here, cols] = (matrix - rebuilt).astype(BF16)
-        strip = pl.ds(r * high, high)
-        span = pl.ds(at, part)
-        copies += [
-            pltpu.make_async_copy(
-                rebuilt_v.at[strip, :], rebuilt_hbm.at[strip, span], sems.at[r, 0]
-            ),
-            pltpu.make_async_copy(
-                error_v.at[strip, :], error_hbm.at[0, strip, span], sems.at[r, 1]
-            ),
-        ]
-        copies[-2].start()
-        copies[-1].start()
+            if (c + 1) * wide % side == 0:
+                k = c * wide // side
+                strip = pl.ds(r * high, high)
+                near = rebuilt_v.at[strip, pl.ds(k * side, side)]
+                far = rebuilt_hbm.at[strip, pl.ds(at + k * side, side)]
+                copies.append(pltpu.make_async_copy(near, far, sems.at[r, k, 0]))
+                near = error_v.at[strip, pl.ds(k * side, side)]
+                far = error_hbm.at[0, strip, pl.ds(at + k * side, side)]
+                copies.append(pltpu.make_async_copy(near, far, sems.at[r, k, 1]))
+                copies[-2].start()
+                copies[-1].start()
     for copy in copies:
         copy.wait()
 
@@ -441,7 +438,7 @@
     )(right_raw, held, got, extra, *ring)
     total = add(keep, swap(send, "dp", m, 1))
 
-    widths = [half, half // 2, half // 2]
+    widths = [width * 3 // 5, width * 2 // 5]
     last, total = after(ring[-1], total)
     newest = list(cut(last, widths))
     newest[0] = step(newest[0])
@@ -490,7 +487,7 @@
             out_specs=[pl.BlockSpec(memory_space=pl.ANY)] * 2,
             out_shape=[sds((rows, width), BF16), sds((1, rows, width), BF16)],
             input_output_aliases={4 + n + j: j for j in range(len(outs))},
-            scratch_shapes=[pltpu.VMEM((rows, part), BF16)] * 2 + [dma((3, 2))],
+            scratch_shapes=[pltpu.VMEM((rows, part), BF16)] * 2 + [dma((3, 2, 2))],
             compiler_params=params(16),
             cost_estimate=cost(0),
             name="rebuild",

time: 71.7 us -> 69.6 us (0.971)
  starting transfers between devices: 26.8 us -> 24.8 us
  Pallas kernels: 18.7 us -> 17.2 us
  waiting for transfers between devices: 25.2 us -> 26.6 us
    ppermute x6 -> x5, starting transfers between devices: 11.7 us -> 9.69 us  [ring_step(): lax.ppermute(x, axis, [(ring[p], ring[(p + 1) % n]) for p in range(n)])]
    pallas_call x3 -> x2, Pallas kernels: 9.08 us -> 7.51 us  [per_device(): pl.pallas_call(functools.partial(final_kernel, at, part, bases), in_specs...]
    ppermute x6 -> x5, waiting for transfers between devices: 5.78 us -> 7.18 us  [ring_step(): lax.ppermute(x, axis, [(ring[p], ring[(p + 1) % n]) for p in range(n)])]
  transfers between devices with their start and end apart: 21 -> 20, of which waited for: 16 -> 16; matrix products, arithmetic and copies ran while one was open for 0% -> 0% of each run, Pallas kernels for 22% -> 19%
where the time goes in v15:
time: 69.6 us; the launch traced here: 69.4 us
  waiting for transfers between devices  26.6 us (38%)
  starting transfers between devices  24.8 us (36%)
  Pallas kernels  17.2 us (25%)
  between operations  0.75 us (1%)
    ppermute x12, waiting for transfers between devices, swap(): return lax.ppermute(x, axis, [(i, i ^ bit) for i in range(n)])  12.5 us
    ppermute x12, starting transfers between devices, swap(): return lax.ppermute(x, axis, [(i, i ^ bit) for i in range(n)])  11.5 us
    ppermute x5, starting transfers between devices, ring_step(): lax.ppermute(x, axis, [(ring[p], ring[(p + 1) % n]) for p in range(n)])  9.69 us
    pallas_call x2, Pallas kernels, per_device(): pl.pallas_call(functools.partial(final_kernel, at, part, bases), in_specs...  7.51 us
    ppermute x5, waiting for transfers between devices, ring_step(): lax.ppermute(x, axis, [(ring[p], ring[(p + 1) % n]) for p in range(n)])  7.18 us
    ppermute x3, waiting for transfers between devices, exchange(): lax.ppermute(pieces[k], axis, [(i, (i + k) % n) for i in range(n)])  6.99 us
    pallas_call x1, Pallas kernels, per_device(): call(error_left_kernel, [sds((rank, rows), F32), sds((1, rows, width), BF...  4.19 us
    ppermute x3, starting transfers between devices, exchange(): lax.ppermute(pieces[k], axis, [(i, (i + k) % n) for i in range(n)])  3.65 us
  transfers between devices with their start and end apart: 20, of which 16 were waited for; matrix products, arithmetic and copies ran while one was open for 0% of the time, Pallas kernels for 19%

profile of v15, /device:TPU:0, one launch (start us, length us, event | category | flops | bytes accessed | tf_op | source)
XLA Modules:
  0.0 69.4 jit_solution(4796134642709854295)
XLA Ops:
  0.6 4.1 %collective-permute-start = (bf16[1,64,5120]{2,1,0:T(8,128)(2,1)}, bf16[1,64,5120]{2,1,0:T(8,128)(2,1)S(1)}, u32[]{:S(2)}, u32[]{:S(2)}) collective-permute-start(bf16[1,64,5120]{2,1,0:T(8,128)(2,1)} %refs_0_.5), channel_id=1, source_target_pairs={{0,2},{2,3},{3,1},{1,0},{4,6},{6,7},{7,5},{5,4},{8,10},{10,11},{11... | collective-permute-start | bytes 1966088 | tf_op jit(solution)/shard_map/ppermute | solution.py:61
  4.7 1.5 %token_factor.1 = (f32[8,128]{1,0:T(8,128)S(1)}, bf16[12,5120]{1,0:T(8,128)(2,1)S(1)}) custom-call(f32[4,5120]{1,0:T(4,128)} %bitcast.2, bf16[1,64,5120]{2,1,0:T(8,128)(2,1)} %refs_0_.5), custom_call_target="tpu_custom_call" | custom-call | flops 1 | bytes 1 | tf_op jit(solution)/shard_map/token_factor/pallas_call | solution.py:379
  6.2 4.2 %error_left.1 = (f32[4,768]{1,0:T(4,128)S(1)}, bf16[1,768,5120]{2,1,0:T(8,128)(2,1)S(1)}) custom-call(bf16[12,5120]{1,0:T(8,128)(2,1)S(1)} %get-tuple-element.37.terms_ref, bf16[1,768,5120]{2,1,0:T(8,128)(2,1)} %e_hbm.1), custom_call_target="tpu_custom_call" | custom-call | flops 4600000000 | bytes 1 | tf_op jit(solution)/shard_map/error_left/pallas_call | solution.py:390
  10.4 1.4 %collective-permute-start.3 = (f32[8,128]{1,0:T(8,128)S(1)}, f32[8,128]{1,0:T(8,128)S(1)}, u32[]{:S(2)}, u32[]{:S(2)}) collective-permute-start(f32[8,128]{1,0:T(8,128)S(1)} %get-tuple-element.41.refs_0_), channel_id=1, source_target_pairs={{0,3},{1,0},{2,1},{3,2},{4,7},{5,4},{6,5},{7,6},{8,11},{9,8},{10,9... | collective-permute-start | bytes 12296 | tf_op jit(solution)/shard_map/ppermute | solution.py:66
  12.1 1.9 %collective-permute-start.1 = (f32[8,128]{1,0:T(8,128)S(1)}, f32[8,128]{1,0:T(8,128)S(1)}, u32[]{:S(2)}, u32[]{:S(2)}) collective-permute-start(f32[8,128]{1,0:T(8,128)S(1)} %get-tuple-element.41.refs_0_), channel_id=1, source_target_pairs={{0,1},{1,2},{2,3},{3,0},{4,5},{5,6},{6,7},{7,4},{8,9},{9,10},{10,1... | collective-permute-start | bytes 12296 | tf_op jit(solution)/shard_map/ppermute | solution.py:66
  14.1 5.1 %collective-permute-done.3.refs_3_ = f32[8,128]{1,0:T(8,128)S(1)} collective-permute-done((f32[8,128]{1,0:T(8,128)S(1)}, f32[8,128]{1,0:T(8,128)S(1)}, u32[]{:S(2)}, u32[]{:S(2)}) %collective-permute-start.3) | collective-permute-done | bytes 4128 | tf_op jit(solution)/shard_map/ppermute | solution.py:66
  19.2 1.9 %collective-permute-done.2.refs_2_ = f32[8,128]{1,0:T(8,128)S(1)} collective-permute-done((f32[8,128]{1,0:T(8,128)S(1)}, f32[8,128]{1,0:T(8,128)S(1)}, u32[]{:S(2)}, u32[]{:S(2)}) %collective-permute-start.2) | collective-permute-done | bytes 4128 | tf_op jit(solution)/shard_map/ppermute | solution.py:66
  21.1 1.6 %collective-permute-start.8 = (bf16[1,64,5120]{2,1,0:T(8,128)(2,1)S(1)}, bf16[1,64,5120]{2,1,0:T(8,128)(2,1)S(1)}, u32[]{:S(2)}, u32[]{:S(2)}) collective-permute-start(bf16[1,64,5120]{2,1,0:T(8,128)(2,1)S(1)} %collective-permute-done.refs_1_), channel_id=1, source_target_pairs={{0,2},{2,3},{3,1},{1,0},{4,6},{6,7},{7,5},{5,4},{8,10},{10,11},{11... | collective-permute-start | bytes 1966088 | tf_op jit(solution)/shard_map/ppermute | solution.py:61
  24.1 2.4 %collective-permute-start.7 = (f32[4,768]{1,0:T(4,128)S(1)}, f32[4,768]{1,0:T(4,128)S(1)}, u32[]{:S(2)}, u32[]{:S(2)}) collective-permute-start(f32[4,768]{1,0:T(4,128)S(1)} %add.3.refs_0_), channel_id=1, source_target_pairs={{0,24},{4,28},{8,16},{12,20},{16,8},{20,12},{24,0},{28,4},{1,25},{... | collective-permute-start | bytes 36872 | tf_op jit(solution)/shard_map/ppermute | solution.py:71
  28.7 1.5 %collective-permute-done.6.refs_2_ = f32[4,768]{1,0:T(4,128)S(1)} collective-permute-done((f32[4,768]{1,0:T(4,128)S(1)}, f32[4,768]{1,0:T(4,128)S(1)}, u32[]{:S(2)}, u32[]{:S(2)}) %collective-permute-start.6) | collective-permute-done | bytes 12320 | tf_op jit(solution)/shard_map/ppermute | solution.py:71
  31.1 1.4 %collective-permute-start.9 = (f32[8,128]{1,0:T(8,128)S(1)}, f32[8,128]{1,0:T(8,128)S(1)}, u32[]{:S(2)}, u32[]{:S(2)}) collective-permute-start(f32[8,128]{1,0:T(8,128)S(1)} %get-tuple-element.50), channel_id=1, source_target_pairs={{0,2},{2,3},{3,1},{1,0},{4,6},{6,7},{7,5},{5,4},{8,10},{10,11},{11... | collective-permute-start | bytes 12296 | tf_op jit(solution)/shard_map/ppermute | solution.py:61
  33.7 4.2 %collective-permute-done.9.got_ref = f32[8,128]{1,0:T(8,128)S(1)} collective-permute-done((f32[8,128]{1,0:T(8,128)S(1)}, f32[8,128]{1,0:T(8,128)S(1)}, u32[]{:S(2)}, u32[]{:S(2)}) %collective-permute-start.9) | collective-permute-done | bytes 4128 | tf_op jit(solution)/shard_map/ppermute | solution.py:61
  39.9 1.3 %collective-permute-start.11 = (bf16[1,64,3072]{2,1,0:T(8,128)(2,1)S(1)}, bf16[1,64,3072]{2,1,0:T(8,128)(2,1)S(1)}, u32[]{:S(2)}, u32[]{:S(2)}) collective-permute-start(bf16[1,64,3072]{2,1,0:T(8,128)(2,1)S(1)} %get-tuple-element.56), channel_id=1, source_target_pairs={{0,2},{2,3},{3,1},{1,0},{4,6},{6,7},{7,5},{5,4},{8,10},{10,11},{11... | collective-permute-start | bytes 1179656 | tf_op jit(solution)/shard_map/ppermute | solution.py:61
  41.1 2.4 %collective-permute-start.14 = (f32[4,2688]{1,0:T(4,128)S(1)}, f32[4,2688]{1,0:T(4,128)S(1)}, u32[]{:S(2)}, u32[]{:S(2)}) collective-permute-start(f32[4,2688]{1,0:T(4,128)S(1)} %add.4.refs_0_), channel_id=1, source_target_pairs={{0,24},{4,28},{8,16},{12,20},{16,8},{20,12},{24,0},{28,4},{1,25},{... | collective-permute-start | bytes 129032 | tf_op jit(solution)/shard_map/ppermute | solution.py:71
  44.6 1.5 %collective-permute-done.14.refs_3_ = f32[4,2688]{1,0:T(4,128)S(1)} collective-permute-done((f32[4,2688]{1,0:T(4,128)S(1)}, f32[4,2688]{1,0:T(4,128)S(1)}, u32[]{:S(2)}, u32[]{:S(2)}) %collective-permute-start.14) | collective-permute-done | bytes 43040 | tf_op jit(solution)/shard_map/ppermute | solution.py:71
  46.1 1.5 %collective-permute-done.13.refs_2_ = f32[4,2688]{1,0:T(4,128)S(1)} collective-permute-done((f32[4,2688]{1,0:T(4,128)S(1)}, f32[4,2688]{1,0:T(4,128)S(1)}, u32[]{:S(2)}, u32[]{:S(2)}) %collective-permute-start.13) | collective-permute-done | bytes 43040 | tf_op jit(solution)/shard_map/ppermute | solution.py:71
  48.1 3.0 %collective-permute-done.11.refs_3_ = bf16[1,64,3072]{2,1,0:T(8,128)(2,1)S(1)} collective-permute-done((bf16[1,64,3072]{2,1,0:T(8,128)(2,1)S(1)}, bf16[1,64,3072]{2,1,0:T(8,128)(2,1)S(1)}, u32[]{:S(2)}, u32[]{:S(2)}) %collective-permute-start.11) | collective-permute-done | bytes 393248 | tf_op jit(solution)/shard_map/ppermute | solution.py:61
  52.0 1.8 %collective-permute-start.16 = (f32[4,2688]{1,0:T(4,128)S(1)}, f32[4,2688]{1,0:T(4,128)S(1)}, u32[]{:S(2)}, u32[]{:S(2)}) collective-permute-start(f32[4,2688]{1,0:T(4,128)S(1)} %add.5.refs_0_), channel_id=1, source_target_pairs={{0,2},{1,3},{2,0},{3,1},{4,6},{5,7},{6,4},{7,5},{8,10},{9,11},{10,... | collective-permute-start | bytes 129032 | tf_op jit(solution)/shard_map/ppermute | solution.py:71
  53.8 1.6 %collective-permute-start.15 = (f32[4,2688]{1,0:T(4,128)S(1)}, f32[4,2688]{1,0:T(4,128)S(1)}, u32[]{:S(2)}, u32[]{:S(2)}) collective-permute-start(f32[4,2688]{1,0:T(4,128)S(1)} %add.5.refs_0_), channel_id=1, source_target_pairs={{0,1},{1,0},{2,3},{3,2},{4,5},{5,4},{6,7},{7,6},{8,9},{9,8},{10,11... | collective-permute-start | bytes 129032 | tf_op jit(solution)/shard_map/ppermute | solution.py:71
  55.5 1.6 %collective-permute-done.17.refs_3_ = f32[4,2688]{1,0:T(4,128)S(1)} collective-permute-done((f32[4,2688]{1,0:T(4,128)S(1)}, f32[4,2688]{1,0:T(4,128)S(1)}, u32[]{:S(2)}, u32[]{:S(2)}) %collective-permute-start.17) | collective-permute-done | bytes 43040 | tf_op jit(solution)/shard_map/ppermute | solution.py:71
  58.0 1.3 %collective-permute-start.19 = (bf16[1,64,2048]{2,1,0:T(8,128)(2,1)S(1)}, bf16[1,64,2048]{2,1,0:T(8,128)(2,1)S(1)}, u32[]{:S(2)}, u32[]{:S(2)}) collective-permute-start(bf16[1,64,2048]{2,1,0:T(8,128)(2,1)S(1)} %get-tuple-element.62), channel_id=1, source_target_pairs={{0,2},{2,3},{3,1},{1,0},{4,6},{6,7},{7,5},{5,4},{8,10},{10,11},{11... | collective-permute-start | bytes 786440 | tf_op jit(solution)/shard_map/ppermute | solution.py:61
  60.5 1.3 %factor.1 = (f32[4,5120]{1,0:T(4,128)}, bf16[768,24]{1,0:T(8,128)(2,1)S(1)}, bf16[24,5120]{1,0:T(8,128)(2,1)S(1)}) custom-call(f32[4,768]{1,0:T(4,128)S(1)} %get-tuple-element.45.p_ref, f32[4,2688]{1,0:T(4,128)S(1)} %join.1.mine_ref, f32[4,2688]{1,0:T(4,128)S(1)} %collective-permute-done.18.other_ref), custom_call_target="tpu_custom_call" | custom-call | flops 1 | bytes 1 | tf_op jit(solution)/shard_map/factor/pallas_call | solution.py:458
  61.9 4.3 %rebuild.2 = (bf16[768,5120]{1,0:T(8,128)(2,1)}, bf16[1,768,5120]{2,1,0:T(8,128)(2,1)}) custom-call(bf16[768,256]{1,0:T(8,128)(2,1)S(1)} %acts.1.acts_ref, bf16[768,24]{1,0:T(8,128)(2,1)S(1)} %get-tuple-element.60.left_ref, bf16[24,5120]{1,0:T(8,128)(2,1)S(1)} %get-tuple-element.61.right_ref, bf16[1,768,5120]{2,1,0:T(8,128)(2,1)S(1)} %get-tuple-element.48.e_ref, ...), custom_call_target="tpu_custom_call" | custom-call | flops 1 | bytes 1 | tf_op jit(solution)/shard_map/rebuild/pallas_call | solution.py:484
  66.2 3.2 %rebuild.3 = (bf16[768,5120]{1,0:T(8,128)(2,1)}, bf16[1,768,5120]{2,1,0:T(8,128)(2,1)}) custom-call(bf16[768,256]{1,0:T(8,128)(2,1)S(1)} %acts.1.acts_ref, bf16[768,24]{1,0:T(8,128)(2,1)S(1)} %get-tuple-element.60.left_ref, bf16[24,5120]{1,0:T(8,128)(2,1)S(1)} %get-tuple-element.61.right_ref, ...), custom_call_target="tpu_custom_call", output_to_operand_aliasing={{0}: (8, {}), {1}: (9, {})} | custom-call | flops 1 | bytes 1 | tf_op jit(solution)/shard_map/rebuild/pallas_call | solution.py:484
  (35 shorter events, 12.4 us)
Async XLA Ops:
  0.6 20.5 %collective-permute-start = (bf16[1,64,5120]{2,1,0:T(8,128)(2,1)}, bf16[1,64,5120]{2,1,0:T(8,128)(2,1)S(1)}, u32[]{:S(2)}, u32[]{:S(2)}) collective-permute-start(bf16[1,64,5120]{2,1,0:T(8,128)(2,1)} %refs_0_.5), channel_id=1, source_target_pairs={{0,2},{2,3},{3,1},{1,0},{4,6},{6,7},{7,5},{5,4},{8,10},{10,11},{11... | collective-permute-start | bytes 1966088 | tf_op jit(solution)/shard_map/ppermute | solution.py:61
  6.2 16.5 %copy-start.1 = (bf16[1,256,768]{2,1,0:T(8,128)(2,1)S(1)}, bf16[1,256,768]{2,1,0:T(8,128)(2,1)}, u32[]{:S(2)}) copy-start(bf16[1,256,768]{2,1,0:T(8,128)(2,1)} %a_ref.5) | copy-start | bytes 1179652
  10.4 27.5 %copy-start = (bf16[1,64,5120]{2,1,0:T(8,128)(2,1)S(1)}, bf16[1,64,5120]{2,1,0:T(8,128)(2,1)}, u32[]{:S(2)}) copy-start(bf16[1,64,5120]{2,1,0:T(8,128)(2,1)} %refs_0_.5) | copy-start | bytes 1966084
  10.4 8.8 %collective-permute-start.3 = (f32[8,128]{1,0:T(8,128)S(1)}, f32[8,128]{1,0:T(8,128)S(1)}, u32[]{:S(2)}, u32[]{:S(2)}) collective-permute-start(f32[8,128]{1,0:T(8,128)S(1)} %get-tuple-element.41.refs_0_), channel_id=1, source_target_pairs={{0,3},{1,0},{2,1},{3,2},{4,7},{5,4},{6,5},{7,6},{8,11},{9,8},{10,9... | collective-permute-start | bytes 12296 | tf_op jit(solution)/shard_map/ppermute | solution.py:66
  11.8 9.2 %collective-permute-start.2 = (f32[8,128]{1,0:T(8,128)S(1)}, f32[8,128]{1,0:T(8,128)S(1)}, u32[]{:S(2)}, u32[]{:S(2)}) collective-permute-start(f32[8,128]{1,0:T(8,128)S(1)} %get-tuple-element.41.refs_0_), channel_id=1, source_target_pairs={{0,2},{1,3},{2,0},{3,1},{4,6},{5,7},{6,4},{7,5},{8,10},{9,11},{10,... | collective-permute-start | bytes 12296 | tf_op jit(solution)/shard_map/ppermute | solution.py:66
  12.1 8.9 %collective-permute-start.1 = (f32[8,128]{1,0:T(8,128)S(1)}, f32[8,128]{1,0:T(8,128)S(1)}, u32[]{:S(2)}, u32[]{:S(2)}) collective-permute-start(f32[8,128]{1,0:T(8,128)S(1)} %get-tuple-element.41.refs_0_), channel_id=1, source_target_pairs={{0,1},{1,2},{2,3},{3,0},{4,5},{5,6},{6,7},{7,4},{8,9},{9,10},{10,1... | collective-permute-start | bytes 12296 | tf_op jit(solution)/shard_map/ppermute | solution.py:66
  21.1 16.8 %collective-permute-start.8 = (bf16[1,64,5120]{2,1,0:T(8,128)(2,1)S(1)}, bf16[1,64,5120]{2,1,0:T(8,128)(2,1)S(1)}, u32[]{:S(2)}, u32[]{:S(2)}) collective-permute-start(bf16[1,64,5120]{2,1,0:T(8,128)(2,1)S(1)} %collective-permute-done.refs_1_), channel_id=1, source_target_pairs={{0,2},{2,3},{3,1},{1,0},{4,6},{6,7},{7,5},{5,4},{8,10},{10,11},{11... | collective-permute-start | bytes 1966088 | tf_op jit(solution)/shard_map/ppermute | solution.py:61
  22.9 1.2 %collective-permute-start.4 = (f32[4,768]{1,0:T(4,128)S(1)}, f32[4,768]{1,0:T(4,128)S(1)}, u32[]{:S(2)}, u32[]{:S(2)}) collective-permute-start(f32[4,768]{1,0:T(4,128)S(1)} %left.1.refs_0_), channel_id=1, source_target_pairs={{0,4},{4,0},{8,12},{12,8},{16,20},{20,16},{24,28},{28,24},{1,5},{5... | collective-permute-start | bytes 36872 | tf_op jit(solution)/shard_map/ppermute | solution.py:71
  24.1 4.6 %collective-permute-start.7 = (f32[4,768]{1,0:T(4,128)S(1)}, f32[4,768]{1,0:T(4,128)S(1)}, u32[]{:S(2)}, u32[]{:S(2)}) collective-permute-start(f32[4,768]{1,0:T(4,128)S(1)} %add.3.refs_0_), channel_id=1, source_target_pairs={{0,24},{4,28},{8,16},{12,20},{16,8},{20,12},{24,0},{28,4},{1,25},{... | collective-permute-start | bytes 36872 | tf_op jit(solution)/shard_map/ppermute | solution.py:71
  26.6 3.7 %collective-permute-start.6 = (f32[4,768]{1,0:T(4,128)S(1)}, f32[4,768]{1,0:T(4,128)S(1)}, u32[]{:S(2)}, u32[]{:S(2)}) collective-permute-start(f32[4,768]{1,0:T(4,128)S(1)} %add.3.refs_0_), channel_id=1, source_target_pairs={{0,16},{4,20},{8,24},{12,28},{16,0},{20,4},{24,8},{28,12},{1,17},{... | collective-permute-start | bytes 36872 | tf_op jit(solution)/shard_map/ppermute | solution.py:71
  27.1 3.7 %collective-permute-start.5 = (f32[4,768]{1,0:T(4,128)S(1)}, f32[4,768]{1,0:T(4,128)S(1)}, u32[]{:S(2)}, u32[]{:S(2)}) collective-permute-start(f32[4,768]{1,0:T(4,128)S(1)} %add.3.refs_0_), channel_id=1, source_target_pairs={{0,8},{4,12},{8,0},{12,4},{16,24},{20,28},{24,16},{28,20},{1,9},{5... | collective-permute-start | bytes 36872 | tf_op jit(solution)/shard_map/ppermute | solution.py:71
  31.1 6.8 %collective-permute-start.9 = (f32[8,128]{1,0:T(8,128)S(1)}, f32[8,128]{1,0:T(8,128)S(1)}, u32[]{:S(2)}, u32[]{:S(2)}) collective-permute-start(f32[8,128]{1,0:T(8,128)S(1)} %get-tuple-element.50), channel_id=1, source_target_pairs={{0,2},{2,3},{3,1},{1,0},{4,6},{6,7},{7,5},{5,4},{8,10},{10,11},{11... | collective-permute-start | bytes 12296 | tf_op jit(solution)/shard_map/ppermute | solution.py:61
  38.5 1.3 %collective-permute-start.10 = (f32[4,2688]{1,0:T(4,128)S(1)}, f32[4,2688]{1,0:T(4,128)S(1)}, u32[]{:S(2)}, u32[]{:S(2)}) collective-permute-start(f32[4,2688]{1,0:T(4,128)S(1)} %get-tuple-element.53), channel_id=1, source_target_pairs={{0,4},{4,0},{8,12},{12,8},{16,20},{20,16},{24,28},{28,24},{1,5},{5... | collective-permute-start | bytes 129032 | tf_op jit(solution)/shard_map/ppermute | solution.py:71
  39.9 11.2 %collective-permute-start.11 = (bf16[1,64,3072]{2,1,0:T(8,128)(2,1)S(1)}, bf16[1,64,3072]{2,1,0:T(8,128)(2,1)S(1)}, u32[]{:S(2)}, u32[]{:S(2)}) collective-permute-start(bf16[1,64,3072]{2,1,0:T(8,128)(2,1)S(1)} %get-tuple-element.56), channel_id=1, source_target_pairs={{0,2},{2,3},{3,1},{1,0},{4,6},{6,7},{7,5},{5,4},{8,10},{10,11},{11... | collective-permute-start | bytes 1179656 | tf_op jit(solution)/shard_map/ppermute | solution.py:61
  41.1 5.0 %collective-permute-start.14 = (f32[4,2688]{1,0:T(4,128)S(1)}, f32[4,2688]{1,0:T(4,128)S(1)}, u32[]{:S(2)}, u32[]{:S(2)}) collective-permute-start(f32[4,2688]{1,0:T(4,128)S(1)} %add.4.refs_0_), channel_id=1, source_target_pairs={{0,24},{4,28},{8,16},{12,20},{16,8},{20,12},{24,0},{28,4},{1,25},{... | collective-permute-start | bytes 129032 | tf_op jit(solution)/shard_map/ppermute | solution.py:71
  43.6 4.0 %collective-permute-start.13 = (f32[4,2688]{1,0:T(4,128)S(1)}, f32[4,2688]{1,0:T(4,128)S(1)}, u32[]{:S(2)}, u32[]{:S(2)}) collective-permute-start(f32[4,2688]{1,0:T(4,128)S(1)} %add.4.refs_0_), channel_id=1, source_target_pairs={{0,16},{4,20},{8,24},{12,28},{16,0},{20,4},{24,8},{28,12},{1,17},{... | collective-permute-start | bytes 129032 | tf_op jit(solution)/shard_map/ppermute | solution.py:71
  44.1 4.0 %collective-permute-start.12 = (f32[4,2688]{1,0:T(4,128)S(1)}, f32[4,2688]{1,0:T(4,128)S(1)}, u32[]{:S(2)}, u32[]{:S(2)}) collective-permute-start(f32[4,2688]{1,0:T(4,128)S(1)} %add.4.refs_0_), channel_id=1, source_target_pairs={{0,8},{4,12},{8,0},{12,4},{16,24},{20,28},{24,16},{28,20},{1,9},{5... | collective-permute-start | bytes 129032 | tf_op jit(solution)/shard_map/ppermute | solution.py:71
  51.1 6.0 %collective-permute-start.17 = (f32[4,2688]{1,0:T(4,128)S(1)}, f32[4,2688]{1,0:T(4,128)S(1)}, u32[]{:S(2)}, u32[]{:S(2)}) collective-permute-start(f32[4,2688]{1,0:T(4,128)S(1)} %add.5.refs_0_), channel_id=1, source_target_pairs={{0,3},{1,2},{2,1},{3,0},{4,7},{5,6},{6,5},{7,4},{8,11},{9,10},{10,... | collective-permute-start | bytes 129032 | tf_op jit(solution)/shard_map/ppermute | solution.py:71
  52.0 5.3 %collective-permute-start.16 = (f32[4,2688]{1,0:T(4,128)S(1)}, f32[4,2688]{1,0:T(4,128)S(1)}, u32[]{:S(2)}, u32[]{:S(2)}) collective-permute-start(f32[4,2688]{1,0:T(4,128)S(1)} %add.5.refs_0_), channel_id=1, source_target_pairs={{0,2},{1,3},{2,0},{3,1},{4,6},{5,7},{6,4},{7,5},{8,10},{9,11},{10,... | collective-permute-start | bytes 129032 | tf_op jit(solution)/shard_map/ppermute | solution.py:71
  53.8 4.0 %collective-permute-start.15 = (f32[4,2688]{1,0:T(4,128)S(1)}, f32[4,2688]{1,0:T(4,128)S(1)}, u32[]{:S(2)}, u32[]{:S(2)}) collective-permute-start(f32[4,2688]{1,0:T(4,128)S(1)} %add.5.refs_0_), channel_id=1, source_target_pairs={{0,1},{1,0},{2,3},{3,2},{4,5},{5,4},{6,7},{7,6},{8,9},{9,8},{10,11... | collective-permute-start | bytes 129032 | tf_op jit(solution)/shard_map/ppermute | solution.py:71
  58.0 8.2 %collective-permute-start.19 = (bf16[1,64,2048]{2,1,0:T(8,128)(2,1)S(1)}, bf16[1,64,2048]{2,1,0:T(8,128)(2,1)S(1)}, u32[]{:S(2)}, u32[]{:S(2)}) collective-permute-start(bf16[1,64,2048]{2,1,0:T(8,128)(2,1)S(1)} %get-tuple-element.62), channel_id=1, source_target_pairs={{0,2},{2,3},{3,1},{1,0},{4,6},{6,7},{7,5},{5,4},{8,10},{10,11},{11... | collective-permute-start | bytes 786440 | tf_op jit(solution)/shard_map/ppermute | solution.py:61
  59.3 1.2 %collective-permute-start.18 = (f32[4,2688]{1,0:T(4,128)S(1)}, f32[4,2688]{1,0:T(4,128)S(1)}, u32[]{:S(2)}, u32[]{:S(2)}) collective-permute-start(f32[4,2688]{1,0:T(4,128)S(1)} %join.1.mine_ref), channel_id=1, source_target_pairs={{0,4},{4,0},{8,12},{12,8},{16,20},{20,16},{24,28},{28,24},{1,5},{5... | collective-permute-start | bytes 129032 | tf_op jit(solution)/shard_map/ppermute | solution.py:71

commit v16 on v15

--- a/solution.py
+++ b/solution.py
@@ -11,6 +11,7 @@
 BF16 = jnp.bfloat16
 SHRINK = 2.0**-23
 TINY = 1e-30
+REBUILD = 4e9
 ROOM = 2.0**14
 BLOCK = 512
 
@@ -184,25 +185,23 @@
 
 def lower_inverse(gram, rank):
     at = lambda i, j: gram[i : i + 1, j : j + 1]
-    low = {}
+    low, inv = {}, {}
     for j in range(rank):
         d = at(j, j)
         for k in range(j):
             d = d - low[j, k] * low[j, k]
-        low[j, j] = jnp.sqrt(d)
+        inv[j, j] = lax.rsqrt(d)
         for i in range(j + 1, rank):
             v = at(i, j)
             for k in range(j):
                 v = v - low[i, k] * low[j, k]
-            low[i, j] = v / low[j, j]
-    inv = {}
+            low[i, j] = v * inv[j, j]
     for j in range(rank):
-        inv[j, j] = 1.0 / low[j, j]
         for i in range(j + 1, rank):
             v = low[i, j] * inv[j, j]
             for k in range(j + 1, i):
                 v = v + low[i, k] * inv[k, j]
-            inv[i, j] = -v / low[i, i]
+            inv[i, j] = -v * inv[i, i]
     return inv
 
 
@@ -427,6 +426,11 @@
         "error_right", None, 1.2e9,
     )(scaled, error_v)
 
+    widths = [width * 3 // 5, width * 2 // 5]
+    last, (got, right_raw) = after(ring[-1], (got, right_raw))
+    newest = list(cut(last, widths))
+    newest[0] = step(newest[0])
+
     keep, send = call(
         right_kernel,
         [sds((rank, half + 128), F32)] * 2,
@@ -438,10 +442,6 @@
     )(right_raw, held, got, extra, *ring)
     total = add(keep, swap(send, "dp", m, 1))
 
-    widths = [width * 3 // 5, width * 2 // 5]
-    last, total = after(ring[-1], total)
-    newest = list(cut(last, widths))
-    newest[0] = step(newest[0])
     for group in groups(m // 2):
         total = add(*terms_of(total, "dp", m, [2 * bit for bit in group]))
     newest[0], total = after(newest[0], total)
@@ -489,7 +489,7 @@
             input_output_aliases={4 + n + j: j for j in range(len(outs))},
             scratch_shapes=[pltpu.VMEM((rows, part), BF16)] * 2 + [dma((3, 2, 2))],
             compiler_params=params(16),
-            cost_estimate=cost(0),
+            cost_estimate=cost(REBUILD),
             name="rebuild",
         )(acts, left_terms, right_terms, error_v, *slots, *outs)
     rebuilt, error = outs

time: 69.6 us -> 67.7 us (0.973)
  waiting for transfers between devices: 26.6 us -> 24.4 us
    ppermute x5, waiting for transfers between devices: 7.18 us -> 5.94 us  [ring_step(): lax.ppermute(x, axis, [(ring[p], ring[(p + 1) % n]) for p in range(n)])]
    ppermute x12, waiting for transfers between devices: 12.5 us -> 11.5 us  [swap(): return lax.ppermute(x, axis, [(i, i ^ bit) for i in range(n)])]
  transfers between devices with their start and end apart: 20 -> 20, of which waited for: 16 -> 15; matrix products, arithmetic and copies ran while one was open for 0% -> 0% of each run, Pallas kernels for 19% -> 20%
where the time goes in v16:
time: 67.7 us; the launch traced here: 67.5 us
  starting transfers between devices  25.2 us (37%)
  waiting for transfers between devices  24.4 us (36%)
  Pallas kernels  17.1 us (25%)
  between operations  0.75 us (1%)
    ppermute x12, starting transfers between devices, swap(): return lax.ppermute(x, axis, [(i, i ^ bit) for i in range(n)])  11.6 us
    ppermute x12, waiting for transfers between devices, swap(): return lax.ppermute(x, axis, [(i, i ^ bit) for i in range(n)])  11.5 us
    ppermute x5, starting transfers between devices, ring_step(): lax.ppermute(x, axis, [(ring[p], ring[(p + 1) % n]) for p in range(n)])  9.95 us
    pallas_call x2, Pallas kernels, per_device(): pl.pallas_call(functools.partial(final_kernel, at, part, bases), in_specs...  7.5 us
    ppermute x3, waiting for transfers between devices, exchange(): lax.ppermute(pieces[k], axis, [(i, (i + k) % n) for i in range(n)])  6.99 us
    ppermute x5, waiting for transfers between devices, ring_step(): lax.ppermute(x, axis, [(ring[p], ring[(p + 1) % n]) for p in range(n)])  5.94 us
    pallas_call x1, Pallas kernels, per_device(): call(error_left_kernel, [sds((rank, rows), F32), sds((1, rows, width), BF...  4.19 us
    ppermute x3, starting transfers between devices, exchange(): lax.ppermute(pieces[k], axis, [(i, (i + k) % n) for i in range(n)])  3.65 us
  transfers between devices with their start and end apart: 20, of which 15 were waited for; matrix products, arithmetic and copies ran while one was open for 0% of the time, Pallas kernels for 20%

profile of v16, /device:TPU:0, one launch (start us, length us, event | category | flops | bytes accessed | tf_op | source)
XLA Modules:
  0.0 67.5 jit_solution(14667715807059400581)
XLA Ops:
  0.6 4.1 %collective-permute-start = (bf16[1,64,5120]{2,1,0:T(8,128)(2,1)}, bf16[1,64,5120]{2,1,0:T(8,128)(2,1)S(1)}, u32[]{:S(2)}, u32[]{:S(2)}) collective-permute-start(bf16[1,64,5120]{2,1,0:T(8,128)(2,1)} %refs_0_.5), channel_id=1, source_target_pairs={{0,2},{2,3},{3,1},{1,0},{4,6},{6,7},{7,5},{5,4},{8,10},{10,11},{11... | collective-permute-start | bytes 1966088 | tf_op jit(solution)/shard_map/ppermute | solution.py:62
  4.7 1.5 %token_factor.1 = (f32[8,128]{1,0:T(8,128)S(1)}, bf16[12,5120]{1,0:T(8,128)(2,1)S(1)}) custom-call(f32[4,5120]{1,0:T(4,128)} %bitcast.2, bf16[1,64,5120]{2,1,0:T(8,128)(2,1)} %refs_0_.5), custom_call_target="tpu_custom_call" | custom-call | flops 1 | bytes 1 | tf_op jit(solution)/shard_map/token_factor/pallas_call | solution.py:378
  6.2 4.2 %error_left.1 = (f32[4,768]{1,0:T(4,128)S(1)}, bf16[1,768,5120]{2,1,0:T(8,128)(2,1)S(1)}) custom-call(bf16[12,5120]{1,0:T(8,128)(2,1)S(1)} %get-tuple-element.38.terms_ref, bf16[1,768,5120]{2,1,0:T(8,128)(2,1)} %e_hbm.1), custom_call_target="tpu_custom_call" | custom-call | flops 4600000000 | bytes 1 | tf_op jit(solution)/shard_map/error_left/pallas_call | solution.py:389
  10.4 1.4 %collective-permute-start.3 = (f32[8,128]{1,0:T(8,128)S(1)}, f32[8,128]{1,0:T(8,128)S(1)}, u32[]{:S(2)}, u32[]{:S(2)}) collective-permute-start(f32[8,128]{1,0:T(8,128)S(1)} %get-tuple-element.42.refs_0_), channel_id=1, source_target_pairs={{0,3},{1,0},{2,1},{3,2},{4,7},{5,4},{6,5},{7,6},{8,11},{9,8},{10,9... | collective-permute-start | bytes 12296 | tf_op jit(solution)/shard_map/ppermute | solution.py:67
  12.1 1.9 %collective-permute-start.1 = (f32[8,128]{1,0:T(8,128)S(1)}, f32[8,128]{1,0:T(8,128)S(1)}, u32[]{:S(2)}, u32[]{:S(2)}) collective-permute-start(f32[8,128]{1,0:T(8,128)S(1)} %get-tuple-element.42.refs_0_), channel_id=1, source_target_pairs={{0,1},{1,2},{2,3},{3,0},{4,5},{5,6},{6,7},{7,4},{8,9},{9,10},{10,1... | collective-permute-start | bytes 12296 | tf_op jit(solution)/shard_map/ppermute | solution.py:67
  14.1 5.1 %collective-permute-done.3.refs_3_ = f32[8,128]{1,0:T(8,128)S(1)} collective-permute-done((f32[8,128]{1,0:T(8,128)S(1)}, f32[8,128]{1,0:T(8,128)S(1)}, u32[]{:S(2)}, u32[]{:S(2)}) %collective-permute-start.3) | collective-permute-done | bytes 4128 | tf_op jit(solution)/shard_map/ppermute | solution.py:67
  19.2 1.9 %collective-permute-done.2.refs_2_ = f32[8,128]{1,0:T(8,128)S(1)} collective-permute-done((f32[8,128]{1,0:T(8,128)S(1)}, f32[8,128]{1,0:T(8,128)S(1)}, u32[]{:S(2)}, u32[]{:S(2)}) %collective-permute-start.2) | collective-permute-done | bytes 4128 | tf_op jit(solution)/shard_map/ppermute | solution.py:67
  21.1 1.6 %collective-permute-start.8 = (bf16[1,64,5120]{2,1,0:T(8,128)(2,1)S(1)}, bf16[1,64,5120]{2,1,0:T(8,128)(2,1)S(1)}, u32[]{:S(2)}, u32[]{:S(2)}) collective-permute-start(bf16[1,64,5120]{2,1,0:T(8,128)(2,1)S(1)} %collective-permute-done.refs_1_), channel_id=1, source_target_pairs={{0,2},{2,3},{3,1},{1,0},{4,6},{6,7},{7,5},{5,4},{8,10},{10,11},{11... | collective-permute-start | bytes 1966088 | tf_op jit(solution)/shard_map/ppermute | solution.py:62
  24.1 2.4 %collective-permute-start.7 = (f32[4,768]{1,0:T(4,128)S(1)}, f32[4,768]{1,0:T(4,128)S(1)}, u32[]{:S(2)}, u32[]{:S(2)}) collective-permute-start(f32[4,768]{1,0:T(4,128)S(1)} %add.3.refs_0_), channel_id=1, source_target_pairs={{0,24},{4,28},{8,16},{12,20},{16,8},{20,12},{24,0},{28,4},{1,25},{... | collective-permute-start | bytes 36872 | tf_op jit(solution)/shard_map/ppermute | solution.py:72
  28.7 1.5 %collective-permute-done.6.refs_2_ = f32[4,768]{1,0:T(4,128)S(1)} collective-permute-done((f32[4,768]{1,0:T(4,128)S(1)}, f32[4,768]{1,0:T(4,128)S(1)}, u32[]{:S(2)}, u32[]{:S(2)}) %collective-permute-start.6) | collective-permute-done | bytes 12320 | tf_op jit(solution)/shard_map/ppermute | solution.py:72
  31.1 1.4 %collective-permute-start.9 = (f32[8,128]{1,0:T(8,128)S(1)}, f32[8,128]{1,0:T(8,128)S(1)}, u32[]{:S(2)}, u32[]{:S(2)}) collective-permute-start(f32[8,128]{1,0:T(8,128)S(1)} %get-tuple-element.48), channel_id=1, source_target_pairs={{0,2},{2,3},{3,1},{1,0},{4,6},{6,7},{7,5},{5,4},{8,10},{10,11},{11... | collective-permute-start | bytes 12296 | tf_op jit(solution)/shard_map/ppermute | solution.py:62
  33.7 4.2 %collective-permute-done.9.got_ref = f32[8,128]{1,0:T(8,128)S(1)} collective-permute-done((f32[8,128]{1,0:T(8,128)S(1)}, f32[8,128]{1,0:T(8,128)S(1)}, u32[]{:S(2)}, u32[]{:S(2)}) %collective-permute-start.9) | collective-permute-done | bytes 4128 | tf_op jit(solution)/shard_map/ppermute | solution.py:62
  38.0 1.3 %collective-permute-start.10 = (bf16[1,64,3072]{2,1,0:T(8,128)(2,1)S(1)}, bf16[1,64,3072]{2,1,0:T(8,128)(2,1)S(1)}, u32[]{:S(2)}, u32[]{:S(2)}) collective-permute-start(bf16[1,64,3072]{2,1,0:T(8,128)(2,1)S(1)} %get-tuple-element.53), channel_id=1, source_target_pairs={{0,2},{2,3},{3,1},{1,0},{4,6},{6,7},{7,5},{5,4},{8,10},{10,11},{11... | collective-permute-start | bytes 1179656 | tf_op jit(solution)/shard_map/ppermute | solution.py:62
  41.1 2.5 %collective-permute-start.14 = (f32[4,2688]{1,0:T(4,128)S(1)}, f32[4,2688]{1,0:T(4,128)S(1)}, u32[]{:S(2)}, u32[]{:S(2)}) collective-permute-start(f32[4,2688]{1,0:T(4,128)S(1)} %add.4.refs_0_), channel_id=1, source_target_pairs={{0,24},{4,28},{8,16},{12,20},{16,8},{20,12},{24,0},{28,4},{1,25},{... | collective-permute-start | bytes 129032 | tf_op jit(solution)/shard_map/ppermute | solution.py:72
  44.7 1.4 %collective-permute-done.14.refs_3_ = f32[4,2688]{1,0:T(4,128)S(1)} collective-permute-done((f32[4,2688]{1,0:T(4,128)S(1)}, f32[4,2688]{1,0:T(4,128)S(1)}, u32[]{:S(2)}, u32[]{:S(2)}) %collective-permute-start.14) | collective-permute-done | bytes 43040 | tf_op jit(solution)/shard_map/ppermute | solution.py:72
  46.1 1.5 %collective-permute-done.13.refs_2_ = f32[4,2688]{1,0:T(4,128)S(1)} collective-permute-done((f32[4,2688]{1,0:T(4,128)S(1)}, f32[4,2688]{1,0:T(4,128)S(1)}, u32[]{:S(2)}, u32[]{:S(2)}) %collective-permute-start.13) | collective-permute-done | bytes 43040 | tf_op jit(solution)/shard_map/ppermute | solution.py:72
  48.3 1.4 %collective-permute-start.17 = (f32[4,2688]{1,0:T(4,128)S(1)}, f32[4,2688]{1,0:T(4,128)S(1)}, u32[]{:S(2)}, u32[]{:S(2)}) collective-permute-start(f32[4,2688]{1,0:T(4,128)S(1)} %add.5.refs_0_), channel_id=1, source_target_pairs={{0,3},{1,2},{2,1},{3,0},{4,7},{5,6},{6,5},{7,4},{8,11},{9,10},{10,... | collective-permute-start | bytes 129032 | tf_op jit(solution)/shard_map/ppermute | solution.py:72
  50.5 2.2 %collective-permute-start.15 = (f32[4,2688]{1,0:T(4,128)S(1)}, f32[4,2688]{1,0:T(4,128)S(1)}, u32[]{:S(2)}, u32[]{:S(2)}) collective-permute-start(f32[4,2688]{1,0:T(4,128)S(1)} %add.5.refs_0_), channel_id=1, source_target_pairs={{0,1},{1,0},{2,3},{3,2},{4,5},{5,4},{6,7},{7,6},{8,9},{9,8},{10,11... | collective-permute-start | bytes 129032 | tf_op jit(solution)/shard_map/ppermute | solution.py:72
  52.7 1.4 %collective-permute-done.17.refs_3_ = f32[4,2688]{1,0:T(4,128)S(1)} collective-permute-done((f32[4,2688]{1,0:T(4,128)S(1)}, f32[4,2688]{1,0:T(4,128)S(1)}, u32[]{:S(2)}, u32[]{:S(2)}) %collective-permute-start.17) | collective-permute-done | bytes 43040 | tf_op jit(solution)/shard_map/ppermute | solution.py:72
  55.6 1.6 %collective-permute-start.19 = (bf16[1,64,2048]{2,1,0:T(8,128)(2,1)S(1)}, bf16[1,64,2048]{2,1,0:T(8,128)(2,1)S(1)}, u32[]{:S(2)}, u32[]{:S(2)}) collective-permute-start(bf16[1,64,2048]{2,1,0:T(8,128)(2,1)S(1)} %get-tuple-element.64), channel_id=1, source_target_pairs={{0,2},{2,3},{3,1},{1,0},{4,6},{6,7},{7,5},{5,4},{8,10},{10,11},{11... | collective-permute-start | bytes 786440 | tf_op jit(solution)/shard_map/ppermute | solution.py:62
  57.2 1.3 %factor.1 = (f32[4,5120]{1,0:T(4,128)}, bf16[768,24]{1,0:T(8,128)(2,1)S(1)}, bf16[24,5120]{1,0:T(8,128)(2,1)S(1)}) custom-call(f32[4,768]{1,0:T(4,128)S(1)} %get-tuple-element.46.p_ref, f32[4,2688]{1,0:T(4,128)S(1)} %join.1.mine_ref, f32[4,2688]{1,0:T(4,128)S(1)} %collective-permute-done.18.other_ref), custom_call_target="tpu_custom_call" | custom-call | flops 1 | bytes 1 | tf_op jit(solution)/shard_map/factor/pallas_call | solution.py:458
  58.5 4.3 %rebuild.2 = (bf16[768,5120]{1,0:T(8,128)(2,1)}, bf16[1,768,5120]{2,1,0:T(8,128)(2,1)}) custom-call(bf16[768,256]{1,0:T(8,128)(2,1)S(1)} %acts.1.acts_ref, bf16[768,24]{1,0:T(8,128)(2,1)S(1)} %get-tuple-element.62.left_ref, bf16[24,5120]{1,0:T(8,128)(2,1)S(1)} %get-tuple-element.63.right_ref, bf16[1,768,5120]{2,1,0:T(8,128)(2,1)S(1)} %get-tuple-element.50.e_ref, ...), custom_call_target="tpu_custom_call" | custom-call | flops 4000000000 | bytes 1 | tf_op jit(solution)/shard_map/rebuild/pallas_call | solution.py:484
  62.8 1.6 %collective-permute-done.19.refs_3_ = bf16[1,64,2048]{2,1,0:T(8,128)(2,1)S(1)} collective-permute-done((bf16[1,64,2048]{2,1,0:T(8,128)(2,1)S(1)}, bf16[1,64,2048]{2,1,0:T(8,128)(2,1)S(1)}, u32[]{:S(2)}, u32[]{:S(2)}) %collective-permute-start.19) | collective-permute-done | bytes 262176 | tf_op jit(solution)/shard_map/ppermute | solution.py:62
  64.3 3.2 %rebuild.3 = (bf16[768,5120]{1,0:T(8,128)(2,1)}, bf16[1,768,5120]{2,1,0:T(8,128)(2,1)}) custom-call(bf16[768,256]{1,0:T(8,128)(2,1)S(1)} %acts.1.acts_ref, bf16[768,24]{1,0:T(8,128)(2,1)S(1)} %get-tuple-element.62.left_ref, bf16[24,5120]{1,0:T(8,128)(2,1)S(1)} %get-tuple-element.63.right_ref, ...), custom_call_target="tpu_custom_call", output_to_operand_aliasing={{0}: (8, {}), {1}: (9, {})} | custom-call | flops 4000000000 | bytes 1 | tf_op jit(solution)/shard_map/rebuild/pallas_call | solution.py:484
  (35 shorter events, 11.7 us)
Async XLA Ops:
  0.6 20.5 %collective-permute-start = (bf16[1,64,5120]{2,1,0:T(8,128)(2,1)}, bf16[1,64,5120]{2,1,0:T(8,128)(2,1)S(1)}, u32[]{:S(2)}, u32[]{:S(2)}) collective-permute-start(bf16[1,64,5120]{2,1,0:T(8,128)(2,1)} %refs_0_.5), channel_id=1, source_target_pairs={{0,2},{2,3},{3,1},{1,0},{4,6},{6,7},{7,5},{5,4},{8,10},{10,11},{11... | collective-permute-start | bytes 1966088 | tf_op jit(solution)/shard_map/ppermute | solution.py:62
  6.2 16.5 %copy-start.1 = (bf16[1,256,768]{2,1,0:T(8,128)(2,1)S(1)}, bf16[1,256,768]{2,1,0:T(8,128)(2,1)}, u32[]{:S(2)}) copy-start(bf16[1,256,768]{2,1,0:T(8,128)(2,1)} %a_ref.5) | copy-start | bytes 1179652
  10.4 28.8 %copy-start = (bf16[1,64,5120]{2,1,0:T(8,128)(2,1)S(1)}, bf16[1,64,5120]{2,1,0:T(8,128)(2,1)}, u32[]{:S(2)}) copy-start(bf16[1,64,5120]{2,1,0:T(8,128)(2,1)} %refs_0_.5) | copy-start | bytes 1966084
  10.4 8.8 %collective-permute-start.3 = (f32[8,128]{1,0:T(8,128)S(1)}, f32[8,128]{1,0:T(8,128)S(1)}, u32[]{:S(2)}, u32[]{:S(2)}) collective-permute-start(f32[8,128]{1,0:T(8,128)S(1)} %get-tuple-element.42.refs_0_), channel_id=1, source_target_pairs={{0,3},{1,0},{2,1},{3,2},{4,7},{5,4},{6,5},{7,6},{8,11},{9,8},{10,9... | collective-permute-start | bytes 12296 | tf_op jit(solution)/shard_map/ppermute | solution.py:67
  11.8 9.2 %collective-permute-start.2 = (f32[8,128]{1,0:T(8,128)S(1)}, f32[8,128]{1,0:T(8,128)S(1)}, u32[]{:S(2)}, u32[]{:S(2)}) collective-permute-start(f32[8,128]{1,0:T(8,128)S(1)} %get-tuple-element.42.refs_0_), channel_id=1, source_target_pairs={{0,2},{1,3},{2,0},{3,1},{4,6},{5,7},{6,4},{7,5},{8,10},{9,11},{10,... | collective-permute-start | bytes 12296 | tf_op jit(solution)/shard_map/ppermute | solution.py:67
  12.1 8.9 %collective-permute-start.1 = (f32[8,128]{1,0:T(8,128)S(1)}, f32[8,128]{1,0:T(8,128)S(1)}, u32[]{:S(2)}, u32[]{:S(2)}) collective-permute-start(f32[8,128]{1,0:T(8,128)S(1)} %get-tuple-element.42.refs_0_), channel_id=1, source_target_pairs={{0,1},{1,2},{2,3},{3,0},{4,5},{5,6},{6,7},{7,4},{8,9},{9,10},{10,1... | collective-permute-start | bytes 12296 | tf_op jit(solution)/shard_map/ppermute | solution.py:67
  21.1 16.8 %collective-permute-start.8 = (bf16[1,64,5120]{2,1,0:T(8,128)(2,1)S(1)}, bf16[1,64,5120]{2,1,0:T(8,128)(2,1)S(1)}, u32[]{:S(2)}, u32[]{:S(2)}) collective-permute-start(bf16[1,64,5120]{2,1,0:T(8,128)(2,1)S(1)} %collective-permute-done.refs_1_), channel_id=1, source_target_pairs={{0,2},{2,3},{3,1},{1,0},{4,6},{6,7},{7,5},{5,4},{8,10},{10,11},{11... | collective-permute-start | bytes 1966088 | tf_op jit(solution)/shard_map/ppermute | solution.py:62
  22.9 1.2 %collective-permute-start.4 = (f32[4,768]{1,0:T(4,128)S(1)}, f32[4,768]{1,0:T(4,128)S(1)}, u32[]{:S(2)}, u32[]{:S(2)}) collective-permute-start(f32[4,768]{1,0:T(4,128)S(1)} %left.1.refs_0_), channel_id=1, source_target_pairs={{0,4},{4,0},{8,12},{12,8},{16,20},{20,16},{24,28},{28,24},{1,5},{5... | collective-permute-start | bytes 36872 | tf_op jit(solution)/shard_map/ppermute | solution.py:72
  24.1 4.6 %collective-permute-start.7 = (f32[4,768]{1,0:T(4,128)S(1)}, f32[4,768]{1,0:T(4,128)S(1)}, u32[]{:S(2)}, u32[]{:S(2)}) collective-permute-start(f32[4,768]{1,0:T(4,128)S(1)} %add.3.refs_0_), channel_id=1, source_target_pairs={{0,24},{4,28},{8,16},{12,20},{16,8},{20,12},{24,0},{28,4},{1,25},{... | collective-permute-start | bytes 36872 | tf_op jit(solution)/shard_map/ppermute | solution.py:72
  26.6 3.7 %collective-permute-start.6 = (f32[4,768]{1,0:T(4,128)S(1)}, f32[4,768]{1,0:T(4,128)S(1)}, u32[]{:S(2)}, u32[]{:S(2)}) collective-permute-start(f32[4,768]{1,0:T(4,128)S(1)} %add.3.refs_0_), channel_id=1, source_target_pairs={{0,16},{4,20},{8,24},{12,28},{16,0},{20,4},{24,8},{28,12},{1,17},{... | collective-permute-start | bytes 36872 | tf_op jit(solution)/shard_map/ppermute | solution.py:72
  27.1 3.7 %collective-permute-start.5 = (f32[4,768]{1,0:T(4,128)S(1)}, f32[4,768]{1,0:T(4,128)S(1)}, u32[]{:S(2)}, u32[]{:S(2)}) collective-permute-start(f32[4,768]{1,0:T(4,128)S(1)} %add.3.refs_0_), channel_id=1, source_target_pairs={{0,8},{4,12},{8,0},{12,4},{16,24},{20,28},{24,16},{28,20},{1,9},{5... | collective-permute-start | bytes 36872 | tf_op jit(solution)/shard_map/ppermute | solution.py:72
  31.1 6.8 %collective-permute-start.9 = (f32[8,128]{1,0:T(8,128)S(1)}, f32[8,128]{1,0:T(8,128)S(1)}, u32[]{:S(2)}, u32[]{:S(2)}) collective-permute-start(f32[8,128]{1,0:T(8,128)S(1)} %get-tuple-element.48), channel_id=1, source_target_pairs={{0,2},{2,3},{3,1},{1,0},{4,6},{6,7},{7,5},{5,4},{8,10},{10,11},{11... | collective-permute-start | bytes 12296 | tf_op jit(solution)/shard_map/ppermute | solution.py:62
  38.0 10.3 %collective-permute-start.10 = (bf16[1,64,3072]{2,1,0:T(8,128)(2,1)S(1)}, bf16[1,64,3072]{2,1,0:T(8,128)(2,1)S(1)}, u32[]{:S(2)}, u32[]{:S(2)}) collective-permute-start(bf16[1,64,3072]{2,1,0:T(8,128)(2,1)S(1)} %get-tuple-element.53), channel_id=1, source_target_pairs={{0,2},{2,3},{3,1},{1,0},{4,6},{6,7},{7,5},{5,4},{8,10},{10,11},{11... | collective-permute-start | bytes 1179656 | tf_op jit(solution)/shard_map/ppermute | solution.py:62
  39.8 1.3 %collective-permute-start.11 = (f32[4,2688]{1,0:T(4,128)S(1)}, f32[4,2688]{1,0:T(4,128)S(1)}, u32[]{:S(2)}, u32[]{:S(2)}) collective-permute-start(f32[4,2688]{1,0:T(4,128)S(1)} %get-tuple-element.59), channel_id=1, source_target_pairs={{0,4},{4,0},{8,12},{12,8},{16,20},{20,16},{24,28},{28,24},{1,5},{5... | collective-permute-start | bytes 129032 | tf_op jit(solution)/shard_map/ppermute | solution.py:72
  41.1 5.0 %collective-permute-start.14 = (f32[4,2688]{1,0:T(4,128)S(1)}, f32[4,2688]{1,0:T(4,128)S(1)}, u32[]{:S(2)}, u32[]{:S(2)}) collective-permute-start(f32[4,2688]{1,0:T(4,128)S(1)} %add.4.refs_0_), channel_id=1, source_target_pairs={{0,24},{4,28},{8,16},{12,20},{16,8},{20,12},{24,0},{28,4},{1,25},{... | collective-permute-start | bytes 129032 | tf_op jit(solution)/shard_map/ppermute | solution.py:72
  43.6 4.0 %collective-permute-start.13 = (f32[4,2688]{1,0:T(4,128)S(1)}, f32[4,2688]{1,0:T(4,128)S(1)}, u32[]{:S(2)}, u32[]{:S(2)}) collective-permute-start(f32[4,2688]{1,0:T(4,128)S(1)} %add.4.refs_0_), channel_id=1, source_target_pairs={{0,16},{4,20},{8,24},{12,28},{16,0},{20,4},{24,8},{28,12},{1,17},{... | collective-permute-start | bytes 129032 | tf_op jit(solution)/shard_map/ppermute | solution.py:72
  44.1 4.0 %collective-permute-start.12 = (f32[4,2688]{1,0:T(4,128)S(1)}, f32[4,2688]{1,0:T(4,128)S(1)}, u32[]{:S(2)}, u32[]{:S(2)}) collective-permute-start(f32[4,2688]{1,0:T(4,128)S(1)} %add.4.refs_0_), channel_id=1, source_target_pairs={{0,8},{4,12},{8,0},{12,4},{16,24},{20,28},{24,16},{28,20},{1,9},{5... | collective-permute-start | bytes 129032 | tf_op jit(solution)/shard_map/ppermute | solution.py:72
  48.3 5.8 %collective-permute-start.17 = (f32[4,2688]{1,0:T(4,128)S(1)}, f32[4,2688]{1,0:T(4,128)S(1)}, u32[]{:S(2)}, u32[]{:S(2)}) collective-permute-start(f32[4,2688]{1,0:T(4,128)S(1)} %add.5.refs_0_), channel_id=1, source_target_pairs={{0,3},{1,2},{2,1},{3,0},{4,7},{5,6},{6,5},{7,4},{8,11},{9,10},{10,... | collective-permute-start | bytes 129032 | tf_op jit(solution)/shard_map/ppermute | solution.py:72
  49.8 5.4 %collective-permute-start.16 = (f32[4,2688]{1,0:T(4,128)S(1)}, f32[4,2688]{1,0:T(4,128)S(1)}, u32[]{:S(2)}, u32[]{:S(2)}) collective-permute-start(f32[4,2688]{1,0:T(4,128)S(1)} %add.5.refs_0_), channel_id=1, source_target_pairs={{0,2},{1,3},{2,0},{3,1},{4,6},{5,7},{6,4},{7,5},{8,10},{9,11},{10,... | collective-permute-start | bytes 129032 | tf_op jit(solution)/shard_map/ppermute | solution.py:72
  50.5 4.7 %collective-permute-start.15 = (f32[4,2688]{1,0:T(4,128)S(1)}, f32[4,2688]{1,0:T(4,128)S(1)}, u32[]{:S(2)}, u32[]{:S(2)}) collective-permute-start(f32[4,2688]{1,0:T(4,128)S(1)} %add.5.refs_0_), channel_id=1, source_target_pairs={{0,1},{1,0},{2,3},{3,2},{4,5},{5,4},{6,7},{7,6},{8,9},{9,8},{10,11... | collective-permute-start | bytes 129032 | tf_op jit(solution)/shard_map/ppermute | solution.py:72
  55.3 1.9 %collective-permute-start.18 = (f32[4,2688]{1,0:T(4,128)S(1)}, f32[4,2688]{1,0:T(4,128)S(1)}, u32[]{:S(2)}, u32[]{:S(2)}) collective-permute-start(f32[4,2688]{1,0:T(4,128)S(1)} %join.1.mine_ref), channel_id=1, source_target_pairs={{0,4},{4,0},{8,12},{12,8},{16,20},{20,16},{24,28},{28,24},{1,5},{5... | collective-permute-start | bytes 129032 | tf_op jit(solution)/shard_map/ppermute | solution.py:72
  55.6 8.7 %collective-permute-start.19 = (bf16[1,64,2048]{2,1,0:T(8,128)(2,1)S(1)}, bf16[1,64,2048]{2,1,0:T(8,128)(2,1)S(1)}, u32[]{:S(2)}, u32[]{:S(2)}) collective-permute-start(bf16[1,64,2048]{2,1,0:T(8,128)(2,1)S(1)} %get-tuple-element.64), channel_id=1, source_target_pairs={{0,2},{2,3},{3,1},{1,0},{4,6},{6,7},{7,5},{5,4},{8,10},{10,11},{11... | collective-permute-start | bytes 786440 | tf_op jit(solution)/shard_map/ppermute | solution.py:62

commit v17 on v16

--- a/solution.py
+++ b/solution.py
@@ -264,27 +264,46 @@
 RIGHT_TERMS = (0, 1, 0, 2, 0, 1)
 
 
-def factor_kernel(m, p_ref, mine_ref, other_ref, whole_ref, left_ref, right_ref, inbox, ortho, left, right):
-    rank = mine_ref.shape[0]
-    half = mine_ref.shape[1] - 128
+def stack_terms(terms, x, ref):
+    parts = split(x)
+    rank = x.shape[0]
+    for i, term in enumerate(terms):
+        ref[i * rank : (i + 1) * rank, :] = parts[term]
+    return ref[...]
+
+
+def factor_solve(m, total_ref):
+    rank = total_ref.shape[0]
+    half = total_ref.shape[1] - 128
+    inv = lower_inverse(total_ref[:, half : half + rank] * (1.0 / m), rank)
+    top = total_ref[0:1, half + rank : half + rank + 1] * (ROOM / (m * m))
+    scaled = {key: value * top for key, value in inv.items()}
+    return inv, solve(scaled, total_ref[:, 0:half], rank)
+
+
+def half_kernel(m, p_ref, mine_ref, left_ref, whole_ref, right_ref, left, right):
+    inv, half = factor_solve(m, mine_ref)
+    whole_ref[...] = half
+    right_ref[...] = stack_terms(RIGHT_TERMS, half, right).astype(BF16)
+    ortho = solve(inv, p_ref[...], p_ref.shape[0])
+    left_ref[...] = stack_terms(LEFT_TERMS, ortho, left).T.astype(BF16)
+
+
+def factor_kernel(m, other_ref, mine_ref, mine_terms_ref, whole_ref, right_ref, right):
+    half = mine_ref.shape[1]
     core = lax.rem(lax.axis_index("dp"), 2)
-    inbox[core] = mine_ref[...]
-    inbox[1 - core] = other_ref[...]
-    inv = lower_inverse(inbox[0, :, half : half + rank] * (1.0 / m), rank)
-    top = inbox[0, 0:1, half + rank : half + rank + 1] * (ROOM / (m * m))
-    scaled = {key: value * top for key, value in inv.items()}
-    ortho[...] = solve(inv, p_ref[...], rank)
-    for h in range(2):
-        whole_ref[:, h * half : (h + 1) * half] = solve(scaled, inbox[h, :, 0:half], rank)
-    for terms, x, ref in (
-        (LEFT_TERMS, ortho[...], left),
-        (RIGHT_TERMS, whole_ref[...], right),
-    ):
-        parts = split(x)
-        for i, term in enumerate(terms):
-            ref[i * rank : (i + 1) * rank, :] = parts[term]
-    left_ref[...] = left[...].T.astype(BF16)
-    right_ref[...] = right[...].astype(BF16)
+    _, other = factor_solve(m, other_ref)
+    terms = stack_terms(RIGHT_TERMS, other, right).astype(BF16)
+    for c in range(2):
+
+        @pl.when(core == c)
+        def _():
+            here = slice(c * half, (c + 1) * half)
+            there = slice((1 - c) * half, (2 - c) * half)
+            whole_ref[:, here] = mine_ref[...]
+            whole_ref[:, there] = other
+            right_ref[:, here] = mine_terms_ref[...]
+            right_ref[:, there] = terms
 
 
 def acts_kernel(n, a_ref, out_ref, acts):
@@ -426,7 +445,7 @@
         "error_right", None, 1.2e9,
     )(scaled, error_v)
 
-    widths = [width * 3 // 5, width * 2 // 5]
+    widths = [width * 7 // 10, width * 3 // 10]
     last, (got, right_raw) = after(ring[-1], (got, right_raw))
     newest = list(cut(last, widths))
     newest[0] = step(newest[0])
@@ -455,17 +474,19 @@
         newest[c] = step(last)
 
     terms = len(LEFT_TERMS) * rank
-    whole, left_terms, right_terms = call(
+    other = swap(total, "dp", m, 1)
+    left_terms, mine, mine_terms = call(
+        functools.partial(half_kernel, m),
+        [sds((rows, terms), BF16), sds((rank, half), F32), sds((terms, half), BF16)],
+        [pltpu.VMEM((terms, rows), F32), pltpu.VMEM((terms, half), F32)],
+        "half", None, 1e9,
+    )(mean, total)
+    whole, right_terms = call(
         functools.partial(factor_kernel, m),
-        [sds((rank, width), F32), sds((rows, terms), BF16), sds((terms, width), BF16)],
-        [
-            pltpu.VMEM((2, rank, half + 128), F32),
-            pltpu.VMEM((rank, rows), F32),
-            pltpu.VMEM((terms, rows), F32),
-            pltpu.VMEM((terms, width), F32),
-        ],
+        [sds((rank, width), F32), sds((terms, width), BF16)],
+        [pltpu.VMEM((terms, half), F32)],
         "factor",
-    )(mean, total, swap(total, "dp", m, 1))
+    )(other, mine, mine_terms)
 
     acts = call(
         functools.partial(acts_kernel, n),

time: 67.7 us -> 67 us (0.990)
  waiting for transfers between devices: 24.4 us -> 23.6 us
  Pallas kernels: 17.1 us -> 17.8 us
    pallas_call x0 -> x1, Pallas kernels: none -> 0.7 us  [per_device(): call(functools.partial(half_kernel, m), [sds((rows, terms), BF16), sds((r...]
  transfers between devices with their start and end apart: 20 -> 20, of which waited for: 15 -> 14; matrix products, arithmetic and copies ran while one was open for 0% -> 0% of each run, Pallas kernels for 20% -> 22%
where the time goes in v17:
time: 67 us; the launch traced here: 66.8 us
  starting transfers between devices  24.6 us (37%)
  waiting for transfers between devices  23.6 us (35%)
  Pallas kernels  17.8 us (27%)
  between operations  0.77 us (1%)
    ppermute x12, starting transfers between devices, swap(): return lax.ppermute(x, axis, [(i, i ^ bit) for i in range(n)])  11.6 us
    ppermute x12, waiting for transfers between devices, swap(): return lax.ppermute(x, axis, [(i, i ^ bit) for i in range(n)])  10.9 us
    ppermute x5, starting transfers between devices, ring_step(): lax.ppermute(x, axis, [(ring[p], ring[(p + 1) % n]) for p in range(n)])  9.33 us
    pallas_call x2, Pallas kernels, per_device(): pl.pallas_call(functools.partial(final_kernel, at, part, bases), in_specs...  7.49 us
    ppermute x3, waiting for transfers between devices, exchange(): lax.ppermute(pieces[k], axis, [(i, (i + k) % n) for i in range(n)])  6.99 us
    ppermute x5, waiting for transfers between devices, ring_step(): lax.ppermute(x, axis, [(ring[p], ring[(p + 1) % n]) for p in range(n)])  5.78 us
    pallas_call x1, Pallas kernels, per_device(): call(error_left_kernel, [sds((rank, rows), F32), sds((1, rows, width), BF...  4.19 us
    ppermute x3, starting transfers between devices, exchange(): lax.ppermute(pieces[k], axis, [(i, (i + k) % n) for i in range(n)])  3.65 us
  transfers between devices with their start and end apart: 20, of which 14 were waited for; matrix products, arithmetic and copies ran while one was open for 0% of the time, Pallas kernels for 22%

profile of v17, /device:TPU:0, one launch (start us, length us, event | category | flops | bytes accessed | tf_op | source)
XLA Modules:
  0.0 66.8 jit_solution(8306040124414186629)
XLA Ops:
  0.6 4.1 %collective-permute-start = (bf16[1,64,5120]{2,1,0:T(8,128)(2,1)}, bf16[1,64,5120]{2,1,0:T(8,128)(2,1)S(1)}, u32[]{:S(2)}, u32[]{:S(2)}) collective-permute-start(bf16[1,64,5120]{2,1,0:T(8,128)(2,1)} %refs_0_.5), channel_id=1, source_target_pairs={{0,2},{2,3},{3,1},{1,0},{4,6},{6,7},{7,5},{5,4},{8,10},{10,11},{11... | collective-permute-start | bytes 1966088 | tf_op jit(solution)/shard_map/ppermute | solution.py:62
  4.7 1.5 %token_factor.1 = (f32[8,128]{1,0:T(8,128)S(1)}, bf16[12,5120]{1,0:T(8,128)(2,1)S(1)}) custom-call(f32[4,5120]{1,0:T(4,128)} %bitcast.2, bf16[1,64,5120]{2,1,0:T(8,128)(2,1)} %refs_0_.5), custom_call_target="tpu_custom_call" | custom-call | flops 1 | bytes 1 | tf_op jit(solution)/shard_map/token_factor/pallas_call | solution.py:397
  6.2 4.2 %error_left.1 = (f32[4,768]{1,0:T(4,128)S(1)}, bf16[1,768,5120]{2,1,0:T(8,128)(2,1)S(1)}) custom-call(bf16[12,5120]{1,0:T(8,128)(2,1)S(1)} %get-tuple-element.40.terms_ref, bf16[1,768,5120]{2,1,0:T(8,128)(2,1)} %e_hbm.1), custom_call_target="tpu_custom_call" | custom-call | flops 4600000000 | bytes 1 | tf_op jit(solution)/shard_map/error_left/pallas_call | solution.py:408
  10.4 1.4 %collective-permute-start.3 = (f32[8,128]{1,0:T(8,128)S(1)}, f32[8,128]{1,0:T(8,128)S(1)}, u32[]{:S(2)}, u32[]{:S(2)}) collective-permute-start(f32[8,128]{1,0:T(8,128)S(1)} %get-tuple-element.44.refs_0_), channel_id=1, source_target_pairs={{0,3},{1,0},{2,1},{3,2},{4,7},{5,4},{6,5},{7,6},{8,11},{9,8},{10,9... | collective-permute-start | bytes 12296 | tf_op jit(solution)/shard_map/ppermute | solution.py:67
  12.1 1.9 %collective-permute-start.1 = (f32[8,128]{1,0:T(8,128)S(1)}, f32[8,128]{1,0:T(8,128)S(1)}, u32[]{:S(2)}, u32[]{:S(2)}) collective-permute-start(f32[8,128]{1,0:T(8,128)S(1)} %get-tuple-element.44.refs_0_), channel_id=1, source_target_pairs={{0,1},{1,2},{2,3},{3,0},{4,5},{5,6},{6,7},{7,4},{8,9},{9,10},{10,1... | collective-permute-start | bytes 12296 | tf_op jit(solution)/shard_map/ppermute | solution.py:67
  14.1 5.1 %collective-permute-done.3.refs_3_ = f32[8,128]{1,0:T(8,128)S(1)} collective-permute-done((f32[8,128]{1,0:T(8,128)S(1)}, f32[8,128]{1,0:T(8,128)S(1)}, u32[]{:S(2)}, u32[]{:S(2)}) %collective-permute-start.3) | collective-permute-done | bytes 4128 | tf_op jit(solution)/shard_map/ppermute | solution.py:67
  19.2 1.9 %collective-permute-done.2.refs_2_ = f32[8,128]{1,0:T(8,128)S(1)} collective-permute-done((f32[8,128]{1,0:T(8,128)S(1)}, f32[8,128]{1,0:T(8,128)S(1)}, u32[]{:S(2)}, u32[]{:S(2)}) %collective-permute-start.2) | collective-permute-done | bytes 4128 | tf_op jit(solution)/shard_map/ppermute | solution.py:67
  21.1 1.6 %collective-permute-start.8 = (bf16[1,64,5120]{2,1,0:T(8,128)(2,1)S(1)}, bf16[1,64,5120]{2,1,0:T(8,128)(2,1)S(1)}, u32[]{:S(2)}, u32[]{:S(2)}) collective-permute-start(bf16[1,64,5120]{2,1,0:T(8,128)(2,1)S(1)} %collective-permute-done.refs_1_), channel_id=1, source_target_pairs={{0,2},{2,3},{3,1},{1,0},{4,6},{6,7},{7,5},{5,4},{8,10},{10,11},{11... | collective-permute-start | bytes 1966088 | tf_op jit(solution)/shard_map/ppermute | solution.py:62
  24.1 2.4 %collective-permute-start.7 = (f32[4,768]{1,0:T(4,128)S(1)}, f32[4,768]{1,0:T(4,128)S(1)}, u32[]{:S(2)}, u32[]{:S(2)}) collective-permute-start(f32[4,768]{1,0:T(4,128)S(1)} %add.3.refs_0_), channel_id=1, source_target_pairs={{0,24},{4,28},{8,16},{12,20},{16,8},{20,12},{24,0},{28,4},{1,25},{... | collective-permute-start | bytes 36872 | tf_op jit(solution)/shard_map/ppermute | solution.py:72
  28.7 1.5 %collective-permute-done.6.refs_2_ = f32[4,768]{1,0:T(4,128)S(1)} collective-permute-done((f32[4,768]{1,0:T(4,128)S(1)}, f32[4,768]{1,0:T(4,128)S(1)}, u32[]{:S(2)}, u32[]{:S(2)}) %collective-permute-start.6) | collective-permute-done | bytes 12320 | tf_op jit(solution)/shard_map/ppermute | solution.py:72
  31.1 1.4 %collective-permute-start.9 = (f32[8,128]{1,0:T(8,128)S(1)}, f32[8,128]{1,0:T(8,128)S(1)}, u32[]{:S(2)}, u32[]{:S(2)}) collective-permute-start(f32[8,128]{1,0:T(8,128)S(1)} %get-tuple-element.50), channel_id=1, source_target_pairs={{0,2},{2,3},{3,1},{1,0},{4,6},{6,7},{7,5},{5,4},{8,10},{10,11},{11... | collective-permute-start | bytes 12296 | tf_op jit(solution)/shard_map/ppermute | solution.py:62
  33.7 4.2 %collective-permute-done.9.got_ref = f32[8,128]{1,0:T(8,128)S(1)} collective-permute-done((f32[8,128]{1,0:T(8,128)S(1)}, f32[8,128]{1,0:T(8,128)S(1)}, u32[]{:S(2)}, u32[]{:S(2)}) %collective-permute-start.9) | collective-permute-done | bytes 4128 | tf_op jit(solution)/shard_map/ppermute | solution.py:62
  38.0 1.3 %collective-permute-start.10 = (bf16[1,64,3584]{2,1,0:T(8,128)(2,1)S(1)}, bf16[1,64,3584]{2,1,0:T(8,128)(2,1)S(1)}, u32[]{:S(2)}, u32[]{:S(2)}) collective-permute-start(bf16[1,64,3584]{2,1,0:T(8,128)(2,1)S(1)} %get-tuple-element.55), channel_id=1, source_target_pairs={{0,2},{2,3},{3,1},{1,0},{4,6},{6,7},{7,5},{5,4},{8,10},{10,11},{11... | collective-permute-start | bytes 1376264 | tf_op jit(solution)/shard_map/ppermute | solution.py:62
  39.9 1.2 %collective-permute-done.11.refs_1_ = f32[4,2688]{1,0:T(4,128)S(1)} collective-permute-done((f32[4,2688]{1,0:T(4,128)S(1)}, f32[4,2688]{1,0:T(4,128)S(1)}, u32[]{:S(2)}, u32[]{:S(2)}) %collective-permute-start.11) | collective-permute-done | bytes 43040 | tf_op jit(solution)/shard_map/ppermute | solution.py:72
  41.1 2.5 %collective-permute-start.14 = (f32[4,2688]{1,0:T(4,128)S(1)}, f32[4,2688]{1,0:T(4,128)S(1)}, u32[]{:S(2)}, u32[]{:S(2)}) collective-permute-start(f32[4,2688]{1,0:T(4,128)S(1)} %add.4.refs_0_), channel_id=1, source_target_pairs={{0,24},{4,28},{8,16},{12,20},{16,8},{20,12},{24,0},{28,4},{1,25},{... | collective-permute-start | bytes 129032 | tf_op jit(solution)/shard_map/ppermute | solution.py:72
  44.7 1.4 %collective-permute-done.14.refs_3_ = f32[4,2688]{1,0:T(4,128)S(1)} collective-permute-done((f32[4,2688]{1,0:T(4,128)S(1)}, f32[4,2688]{1,0:T(4,128)S(1)}, u32[]{:S(2)}, u32[]{:S(2)}) %collective-permute-start.14) | collective-permute-done | bytes 43040 | tf_op jit(solution)/shard_map/ppermute | solution.py:72
  46.1 1.5 %collective-permute-done.13.refs_2_ = f32[4,2688]{1,0:T(4,128)S(1)} collective-permute-done((f32[4,2688]{1,0:T(4,128)S(1)}, f32[4,2688]{1,0:T(4,128)S(1)}, u32[]{:S(2)}, u32[]{:S(2)}) %collective-permute-start.13) | collective-permute-done | bytes 43040 | tf_op jit(solution)/shard_map/ppermute | solution.py:72
  48.2 1.6 %collective-permute-done.10.refs_3_ = bf16[1,64,3584]{2,1,0:T(8,128)(2,1)S(1)} collective-permute-done((bf16[1,64,3584]{2,1,0:T(8,128)(2,1)S(1)}, bf16[1,64,3584]{2,1,0:T(8,128)(2,1)S(1)}, u32[]{:S(2)}, u32[]{:S(2)}) %collective-permute-start.10) | collective-permute-done | bytes 458784 | tf_op jit(solution)/shard_map/ppermute | solution.py:62
  49.8 1.9 %collective-permute-start.16 = (f32[4,2688]{1,0:T(4,128)S(1)}, f32[4,2688]{1,0:T(4,128)S(1)}, u32[]{:S(2)}, u32[]{:S(2)}) collective-permute-start(f32[4,2688]{1,0:T(4,128)S(1)} %add.5.refs_0_), channel_id=1, source_target_pairs={{0,2},{1,3},{2,0},{3,1},{4,6},{5,7},{6,4},{7,5},{8,10},{9,11},{10,... | collective-permute-start | bytes 129032 | tf_op jit(solution)/shard_map/ppermute | solution.py:72
  51.7 2.5 %collective-permute-start.15 = (f32[4,2688]{1,0:T(4,128)S(1)}, f32[4,2688]{1,0:T(4,128)S(1)}, u32[]{:S(2)}, u32[]{:S(2)}) collective-permute-start(f32[4,2688]{1,0:T(4,128)S(1)} %add.5.refs_0_), channel_id=1, source_target_pairs={{0,1},{1,0},{2,3},{3,2},{4,5},{5,4},{6,7},{7,6},{8,9},{9,8},{10,11... | collective-permute-start | bytes 129032 | tf_op jit(solution)/shard_map/ppermute | solution.py:72
  54.3 1.3 %collective-permute-done.17.refs_3_ = f32[4,2688]{1,0:T(4,128)S(1)} collective-permute-done((f32[4,2688]{1,0:T(4,128)S(1)}, f32[4,2688]{1,0:T(4,128)S(1)}, u32[]{:S(2)}, u32[]{:S(2)}) %collective-permute-start.17) | collective-permute-done | bytes 43040 | tf_op jit(solution)/shard_map/ppermute | solution.py:72
  58.1 1.2 %factor.1 = (f32[4,5120]{1,0:T(4,128)}, bf16[24,5120]{1,0:T(8,128)(2,1)S(1)}) custom-call(f32[4,2688]{1,0:T(4,128)S(1)} %collective-permute-done.18.other_ref, f32[4,2560]{1,0:T(4,128)S(1)} %get-tuple-element.65.mine_ref, bf16[24,2560]{1,0:T(8,128)(2,1)S(1)} %get-tuple-element.66.mine_terms_ref), custom_call_target="tpu_custom_call" | custom-call | flops 1 | bytes 1 | tf_op jit(solution)/shard_map/factor/pallas_call | solution.py:484
  59.3 4.8 %rebuild.2 = (bf16[768,5120]{1,0:T(8,128)(2,1)}, bf16[1,768,5120]{2,1,0:T(8,128)(2,1)}) custom-call(bf16[768,256]{1,0:T(8,128)(2,1)S(1)} %acts.1.acts_ref, bf16[768,24]{1,0:T(8,128)(2,1)S(1)} %get-tuple-element.64.left_ref, bf16[24,5120]{1,0:T(8,128)(2,1)S(1)} %get-tuple-element.67.right_ref, bf16[1,768,5120]{2,1,0:T(8,128)(2,1)S(1)} %get-tuple-element.52.e_ref, ...), custom_call_target="tpu_custom_call" | custom-call | flops 4000000000 | bytes 1 | tf_op jit(solution)/shard_map/rebuild/pallas_call | solution.py:505
  64.2 2.6 %rebuild.3 = (bf16[768,5120]{1,0:T(8,128)(2,1)}, bf16[1,768,5120]{2,1,0:T(8,128)(2,1)}) custom-call(bf16[768,256]{1,0:T(8,128)(2,1)S(1)} %acts.1.acts_ref, bf16[768,24]{1,0:T(8,128)(2,1)S(1)} %get-tuple-element.64.left_ref, bf16[24,5120]{1,0:T(8,128)(2,1)S(1)} %get-tuple-element.67.right_ref, ...), custom_call_target="tpu_custom_call", output_to_operand_aliasing={{0}: (8, {}), {1}: (9, {})} | custom-call | flops 4000000000 | bytes 1 | tf_op jit(solution)/shard_map/rebuild/pallas_call | solution.py:505
  (36 shorter events, 10.9 us)
Async XLA Ops:
  0.6 20.5 %collective-permute-start = (bf16[1,64,5120]{2,1,0:T(8,128)(2,1)}, bf16[1,64,5120]{2,1,0:T(8,128)(2,1)S(1)}, u32[]{:S(2)}, u32[]{:S(2)}) collective-permute-start(bf16[1,64,5120]{2,1,0:T(8,128)(2,1)} %refs_0_.5), channel_id=1, source_target_pairs={{0,2},{2,3},{3,1},{1,0},{4,6},{6,7},{7,5},{5,4},{8,10},{10,11},{11... | collective-permute-start | bytes 1966088 | tf_op jit(solution)/shard_map/ppermute | solution.py:62
  6.2 16.5 %copy-start.1 = (bf16[1,256,768]{2,1,0:T(8,128)(2,1)S(1)}, bf16[1,256,768]{2,1,0:T(8,128)(2,1)}, u32[]{:S(2)}) copy-start(bf16[1,256,768]{2,1,0:T(8,128)(2,1)} %a_ref.5) | copy-start | bytes 1179652
  10.4 28.9 %copy-start = (bf16[1,64,5120]{2,1,0:T(8,128)(2,1)S(1)}, bf16[1,64,5120]{2,1,0:T(8,128)(2,1)}, u32[]{:S(2)}) copy-start(bf16[1,64,5120]{2,1,0:T(8,128)(2,1)} %refs_0_.5) | copy-start | bytes 1966084
  10.4 8.8 %collective-permute-start.3 = (f32[8,128]{1,0:T(8,128)S(1)}, f32[8,128]{1,0:T(8,128)S(1)}, u32[]{:S(2)}, u32[]{:S(2)}) collective-permute-start(f32[8,128]{1,0:T(8,128)S(1)} %get-tuple-element.44.refs_0_), channel_id=1, source_target_pairs={{0,3},{1,0},{2,1},{3,2},{4,7},{5,4},{6,5},{7,6},{8,11},{9,8},{10,9... | collective-permute-start | bytes 12296 | tf_op jit(solution)/shard_map/ppermute | solution.py:67
  11.8 9.2 %collective-permute-start.2 = (f32[8,128]{1,0:T(8,128)S(1)}, f32[8,128]{1,0:T(8,128)S(1)}, u32[]{:S(2)}, u32[]{:S(2)}) collective-permute-start(f32[8,128]{1,0:T(8,128)S(1)} %get-tuple-element.44.refs_0_), channel_id=1, source_target_pairs={{0,2},{1,3},{2,0},{3,1},{4,6},{5,7},{6,4},{7,5},{8,10},{9,11},{10,... | collective-permute-start | bytes 12296 | tf_op jit(solution)/shard_map/ppermute | solution.py:67
  12.1 8.9 %collective-permute-start.1 = (f32[8,128]{1,0:T(8,128)S(1)}, f32[8,128]{1,0:T(8,128)S(1)}, u32[]{:S(2)}, u32[]{:S(2)}) collective-permute-start(f32[8,128]{1,0:T(8,128)S(1)} %get-tuple-element.44.refs_0_), channel_id=1, source_target_pairs={{0,1},{1,2},{2,3},{3,0},{4,5},{5,6},{6,7},{7,4},{8,9},{9,10},{10,1... | collective-permute-start | bytes 12296 | tf_op jit(solution)/shard_map/ppermute | solution.py:67
  21.1 16.8 %collective-permute-start.8 = (bf16[1,64,5120]{2,1,0:T(8,128)(2,1)S(1)}, bf16[1,64,5120]{2,1,0:T(8,128)(2,1)S(1)}, u32[]{:S(2)}, u32[]{:S(2)}) collective-permute-start(bf16[1,64,5120]{2,1,0:T(8,128)(2,1)S(1)} %collective-permute-done.refs_1_), channel_id=1, source_target_pairs={{0,2},{2,3},{3,1},{1,0},{4,6},{6,7},{7,5},{5,4},{8,10},{10,11},{11... | collective-permute-start | bytes 1966088 | tf_op jit(solution)/shard_map/ppermute | solution.py:62
  22.9 1.2 %collective-permute-start.4 = (f32[4,768]{1,0:T(4,128)S(1)}, f32[4,768]{1,0:T(4,128)S(1)}, u32[]{:S(2)}, u32[]{:S(2)}) collective-permute-start(f32[4,768]{1,0:T(4,128)S(1)} %left.1.refs_0_), channel_id=1, source_target_pairs={{0,4},{4,0},{8,12},{12,8},{16,20},{20,16},{24,28},{28,24},{1,5},{5... | collective-permute-start | bytes 36872 | tf_op jit(solution)/shard_map/ppermute | solution.py:72
  24.1 4.6 %collective-permute-start.7 = (f32[4,768]{1,0:T(4,128)S(1)}, f32[4,768]{1,0:T(4,128)S(1)}, u32[]{:S(2)}, u32[]{:S(2)}) collective-permute-start(f32[4,768]{1,0:T(4,128)S(1)} %add.3.refs_0_), channel_id=1, source_target_pairs={{0,24},{4,28},{8,16},{12,20},{16,8},{20,12},{24,0},{28,4},{1,25},{... | collective-permute-start | bytes 36872 | tf_op jit(solution)/shard_map/ppermute | solution.py:72
  26.6 3.7 %collective-permute-start.6 = (f32[4,768]{1,0:T(4,128)S(1)}, f32[4,768]{1,0:T(4,128)S(1)}, u32[]{:S(2)}, u32[]{:S(2)}) collective-permute-start(f32[4,768]{1,0:T(4,128)S(1)} %add.3.refs_0_), channel_id=1, source_target_pairs={{0,16},{4,20},{8,24},{12,28},{16,0},{20,4},{24,8},{28,12},{1,17},{... | collective-permute-start | bytes 36872 | tf_op jit(solution)/shard_map/ppermute | solution.py:72
  27.1 3.7 %collective-permute-start.5 = (f32[4,768]{1,0:T(4,128)S(1)}, f32[4,768]{1,0:T(4,128)S(1)}, u32[]{:S(2)}, u32[]{:S(2)}) collective-permute-start(f32[4,768]{1,0:T(4,128)S(1)} %add.3.refs_0_), channel_id=1, source_target_pairs={{0,8},{4,12},{8,0},{12,4},{16,24},{20,28},{24,16},{28,20},{1,9},{5... | collective-permute-start | bytes 36872 | tf_op jit(solution)/shard_map/ppermute | solution.py:72
  31.1 6.8 %collective-permute-start.9 = (f32[8,128]{1,0:T(8,128)S(1)}, f32[8,128]{1,0:T(8,128)S(1)}, u32[]{:S(2)}, u32[]{:S(2)}) collective-permute-start(f32[8,128]{1,0:T(8,128)S(1)} %get-tuple-element.50), channel_id=1, source_target_pairs={{0,2},{2,3},{3,1},{1,0},{4,6},{6,7},{7,5},{5,4},{8,10},{10,11},{11... | collective-permute-start | bytes 12296 | tf_op jit(solution)/shard_map/ppermute | solution.py:62
  38.0 11.7 %collective-permute-start.10 = (bf16[1,64,3584]{2,1,0:T(8,128)(2,1)S(1)}, bf16[1,64,3584]{2,1,0:T(8,128)(2,1)S(1)}, u32[]{:S(2)}, u32[]{:S(2)}) collective-permute-start(bf16[1,64,3584]{2,1,0:T(8,128)(2,1)S(1)} %get-tuple-element.55), channel_id=1, source_target_pairs={{0,2},{2,3},{3,1},{1,0},{4,6},{6,7},{7,5},{5,4},{8,10},{10,11},{11... | collective-permute-start | bytes 1376264 | tf_op jit(solution)/shard_map/ppermute | solution.py:62
  39.8 1.3 %collective-permute-start.11 = (f32[4,2688]{1,0:T(4,128)S(1)}, f32[4,2688]{1,0:T(4,128)S(1)}, u32[]{:S(2)}, u32[]{:S(2)}) collective-permute-start(f32[4,2688]{1,0:T(4,128)S(1)} %get-tuple-element.61), channel_id=1, source_target_pairs={{0,4},{4,0},{8,12},{12,8},{16,20},{20,16},{24,28},{28,24},{1,5},{5... | collective-permute-start | bytes 129032 | tf_op jit(solution)/shard_map/ppermute | solution.py:72
  41.1 5.0 %collective-permute-start.14 = (f32[4,2688]{1,0:T(4,128)S(1)}, f32[4,2688]{1,0:T(4,128)S(1)}, u32[]{:S(2)}, u32[]{:S(2)}) collective-permute-start(f32[4,2688]{1,0:T(4,128)S(1)} %add.4.refs_0_), channel_id=1, source_target_pairs={{0,24},{4,28},{8,16},{12,20},{16,8},{20,12},{24,0},{28,4},{1,25},{... | collective-permute-start | bytes 129032 | tf_op jit(solution)/shard_map/ppermute | solution.py:72
  43.6 4.0 %collective-permute-start.13 = (f32[4,2688]{1,0:T(4,128)S(1)}, f32[4,2688]{1,0:T(4,128)S(1)}, u32[]{:S(2)}, u32[]{:S(2)}) collective-permute-start(f32[4,2688]{1,0:T(4,128)S(1)} %add.4.refs_0_), channel_id=1, source_target_pairs={{0,16},{4,20},{8,24},{12,28},{16,0},{20,4},{24,8},{28,12},{1,17},{... | collective-permute-start | bytes 129032 | tf_op jit(solution)/shard_map/ppermute | solution.py:72
  44.2 4.0 %collective-permute-start.12 = (f32[4,2688]{1,0:T(4,128)S(1)}, f32[4,2688]{1,0:T(4,128)S(1)}, u32[]{:S(2)}, u32[]{:S(2)}) collective-permute-start(f32[4,2688]{1,0:T(4,128)S(1)} %add.4.refs_0_), channel_id=1, source_target_pairs={{0,8},{4,12},{8,0},{12,4},{16,24},{20,28},{24,16},{28,20},{1,9},{5... | collective-permute-start | bytes 129032 | tf_op jit(solution)/shard_map/ppermute | solution.py:72
  49.8 5.8 %collective-permute-start.17 = (f32[4,2688]{1,0:T(4,128)S(1)}, f32[4,2688]{1,0:T(4,128)S(1)}, u32[]{:S(2)}, u32[]{:S(2)}) collective-permute-start(f32[4,2688]{1,0:T(4,128)S(1)} %add.5.refs_0_), channel_id=1, source_target_pairs={{0,3},{1,2},{2,1},{3,0},{4,7},{5,6},{6,5},{7,4},{8,11},{9,10},{10,... | collective-permute-start | bytes 129032 | tf_op jit(solution)/shard_map/ppermute | solution.py:72
  49.8 5.8 %collective-permute-start.16 = (f32[4,2688]{1,0:T(4,128)S(1)}, f32[4,2688]{1,0:T(4,128)S(1)}, u32[]{:S(2)}, u32[]{:S(2)}) collective-permute-start(f32[4,2688]{1,0:T(4,128)S(1)} %add.5.refs_0_), channel_id=1, source_target_pairs={{0,2},{1,3},{2,0},{3,1},{4,6},{5,7},{6,4},{7,5},{8,10},{9,11},{10,... | collective-permute-start | bytes 129032 | tf_op jit(solution)/shard_map/ppermute | solution.py:72
  51.7 4.5 %collective-permute-start.15 = (f32[4,2688]{1,0:T(4,128)S(1)}, f32[4,2688]{1,0:T(4,128)S(1)}, u32[]{:S(2)}, u32[]{:S(2)}) collective-permute-start(f32[4,2688]{1,0:T(4,128)S(1)} %add.5.refs_0_), channel_id=1, source_target_pairs={{0,1},{1,0},{2,3},{3,2},{4,5},{5,4},{6,7},{7,6},{8,9},{9,8},{10,11... | collective-permute-start | bytes 129032 | tf_op jit(solution)/shard_map/ppermute | solution.py:72
  56.3 1.8 %collective-permute-start.18 = (f32[4,2688]{1,0:T(4,128)S(1)}, f32[4,2688]{1,0:T(4,128)S(1)}, u32[]{:S(2)}, u32[]{:S(2)}) collective-permute-start(f32[4,2688]{1,0:T(4,128)S(1)} %join.1.mine_ref), channel_id=1, source_target_pairs={{0,4},{4,0},{8,12},{12,8},{16,20},{20,16},{24,28},{28,24},{1,5},{5... | collective-permute-start | bytes 129032 | tf_op jit(solution)/shard_map/ppermute | solution.py:72
  56.4 7.8 %collective-permute-start.19 = (bf16[1,64,1536]{2,1,0:T(8,128)(2,1)S(1)}, bf16[1,64,1536]{2,1,0:T(8,128)(2,1)S(1)}, u32[]{:S(2)}, u32[]{:S(2)}) collective-permute-start(bf16[1,64,1536]{2,1,0:T(8,128)(2,1)S(1)} %get-tuple-element.68), channel_id=1, source_target_pairs={{0,2},{2,3},{3,1},{1,0},{4,6},{6,7},{7,5},{5,4},{8,10},{10,11},{11... | collective-permute-start | bytes 589832 | tf_op jit(solution)/shard_map/ppermute | solution.py:62

commit v18 on v17

--- a/solution.py
+++ b/solution.py
@@ -60,12 +60,6 @@
 def ring_step(x, axis, n):
     ring = ring_of(n)
     return lax.ppermute(x, axis, [(ring[p], ring[(p + 1) % n]) for p in range(n)])
-
-
-def exchange(pieces, axis, n):
-    return [pieces[0]] + [
-        lax.ppermute(pieces[k], axis, [(i, (i + k) % n) for i in range(n)]) for k in range(1, n)
-    ]
 
 
 def swap(x, axis, n, bit):
@@ -143,7 +137,7 @@
     me = lax.axis_index("tensor")
     total = e_ref[...]
     for k in range(n):
-        src = lax.rem(me - k + n, n)
+        src = me ^ k
         rows = a_ref[0, pl.ds(pl.multiple_of(src * tok, tok), tok), :]
         total += sum3(dot(stack3(gws[k][0:rank, 0:tok], g3), rows, (1, 0)), rank)
     out_ref[...] = total
@@ -316,15 +310,20 @@
     out_ref[...] = acts[...].T
 
 
-def final_kernel(at, part, bases, acts_ref, left_ref, right_ref, e_ref, *refs):
+def final_kernel(at, part, bases, last, acts_ref, left_ref, right_ref, e_ref, *refs):
     slots = refs[: len(bases)]
-    rebuilt_hbm, error_hbm, rebuilt_v, error_v, sems = refs[-5:]
+    outs, (rebuilt_v, error_v, sems) = refs[-5 - last : -3], refs[-3:]
+    rebuilt_hbm, error_hbm = outs[:2]
     rows = e_ref.shape[1]
     wide = 256
     strips, sides, _ = sems.shape
+    strips -= 1
     high = rows // strips
     side = part // sides
     copies = []
+    if last:
+        copies.append(pltpu.make_async_copy(refs[len(bases)], outs[2], sems.at[strips, 0, 0]))
+        copies[-1].start()
     for r in range(strips):
         here = slice(r * high, (r + 1) * high)
         for c in range(part // wide):
@@ -413,7 +412,7 @@
     )(w_terms, pin(error_buffer))
 
     gw, ew = after(gw, ew)
-    gws = exchange([gw] * n, "tensor", n)
+    gws = [gw] + [swap(gw, "tensor", n, k) for k in range(1, n)]
     ring[1], gws = after(ring[1], gws)
     for _ in range(n - 2 - 1):
         ring.append(step(ring[-1]))
@@ -502,19 +501,22 @@
 
     outs = ()
     for at, part, slots, bases in pieces:
+        last = at + part == width
+        inputs = [acts, left_terms, right_terms, error_v, *slots] + [whole] * last
         outs = pl.pallas_call(
-            functools.partial(final_kernel, at, part, bases),
-            in_specs=[vmem] * (4 + n) + [pl.BlockSpec(memory_space=pl.ANY)] * len(outs),
-            out_specs=[pl.BlockSpec(memory_space=pl.ANY)] * 2,
-            out_shape=[sds((rows, width), BF16), sds((1, rows, width), BF16)],
-            input_output_aliases={4 + n + j: j for j in range(len(outs))},
-            scratch_shapes=[pltpu.VMEM((rows, part), BF16)] * 2 + [dma((3, 2, 2))],
+            functools.partial(final_kernel, at, part, bases, last),
+            in_specs=[vmem] * len(inputs) + [pl.BlockSpec(memory_space=pl.ANY)] * len(outs),
+            out_specs=[pl.BlockSpec(memory_space=pl.ANY)] * (2 + last),
+            out_shape=[sds((rows, width), BF16), sds((1, rows, width), BF16)]
+            + [sds((rank, width), F32)] * last,
+            input_output_aliases={len(inputs) + k: k for k in range(len(outs))},
+            scratch_shapes=[pltpu.VMEM((rows, part), BF16)] * 2 + [dma((4, 2, 2))],
             compiler_params=params(16),
             cost_estimate=cost(REBUILD),
             name="rebuild",
-        )(acts, left_terms, right_terms, error_v, *slots, *outs)
-    rebuilt, error = outs
-    return rebuilt, error, whole.T
+        )(*inputs, *outs)
+    rebuilt, error, factor = outs
+    return rebuilt, error, factor.T
 
 
 def solution(mesh):

time: 67 us -> 68.5 us (1.022)
  starting transfers between devices: 24.6 us -> 26.1 us
  waiting for transfers between devices: 23.6 us -> 24.3 us
    ppermute x12 -> x15, waiting for transfers between devices: 10.9 us -> 18.5 us  [swap(): return lax.ppermute(x, axis, [(i, i ^ bit) for i in range(n)])]
    ppermute x3 -> x0, waiting for transfers between devices: 6.99 us -> none  [exchange(): lax.ppermute(pieces[k], axis, [(i, (i + k) % n) for i in range(n)])]
    ppermute x12 -> x15, starting transfers between devices: 11.6 us -> 16.1 us  [swap(): return lax.ppermute(x, axis, [(i, i ^ bit) for i in range(n)])]
    ppermute x3 -> x0, starting transfers between devices: 3.65 us -> none  [exchange(): lax.ppermute(pieces[k], axis, [(i, (i + k) % n) for i in range(n)])]
  transfers between devices with their start and end apart: 20 -> 20, of which waited for: 14 -> 15; matrix products, arithmetic and copies ran while one was open for 0% -> 0% of each run, Pallas kernels for 22% -> 21%
where the time goes in v18:
time: 68.5 us; the launch traced here: 68.4 us
  starting transfers between devices  26.1 us (38%)
  waiting for transfers between devices  24.3 us (35%)
  Pallas kernels  17.2 us (25%)
  between operations  0.78 us (1%)
    ppermute x15, waiting for transfers between devices, swap(): return lax.ppermute(x, axis, [(i, i ^ bit) for i in range(n)])  18.5 us
    ppermute x15, starting transfers between devices, swap(): return lax.ppermute(x, axis, [(i, i ^ bit) for i in range(n)])  16.1 us
    ppermute x5, starting transfers between devices, ring_step(): lax.ppermute(x, axis, [(ring[p], ring[(p + 1) % n]) for p in range(n)])  10 us
    pallas_call x2, Pallas kernels, per_device(): pl.pallas_call(functools.partial(final_kernel, at, part, bases, last), in...  7.57 us
    ppermute x5, waiting for transfers between devices, ring_step(): lax.ppermute(x, axis, [(ring[p], ring[(p + 1) % n]) for p in range(n)])  5.75 us
    pallas_call x1, Pallas kernels, per_device(): call(error_left_kernel, [sds((rank, rows), F32), sds((1, rows, width), BF...  4.19 us
    pallas_call x1, Pallas kernels, per_device(): call(token_factor_kernel, [sds((8, 128), F32), sds((3 * rank, width), BF1...  1.48 us
  transfers between devices with their start and end apart: 20, of which 15 were waited for; matrix products, arithmetic and copies ran while one was open for 0% of the time, Pallas kernels for 21%

profile of v18, /device:TPU:0, one launch (start us, length us, event | category | flops | bytes accessed | tf_op | source)
XLA Modules:
  0.0 68.4 jit_solution(12352644508316114094)
XLA Ops:
  0.6 4.1 %collective-permute-start = (bf16[1,64,5120]{2,1,0:T(8,128)(2,1)}, bf16[1,64,5120]{2,1,0:T(8,128)(2,1)S(1)}, u32[]{:S(2)}, u32[]{:S(2)}) collective-permute-start(bf16[1,64,5120]{2,1,0:T(8,128)(2,1)} %refs_0_.5), channel_id=1, source_target_pairs={{0,2},{2,3},{3,1},{1,0},{4,6},{6,7},{7,5},{5,4},{8,10},{10,11},{11... | collective-permute-start | bytes 1966088 | tf_op jit(solution)/shard_map/ppermute | solution.py:62
  4.7 1.5 %token_factor.1 = (f32[8,128]{1,0:T(8,128)S(1)}, bf16[12,5120]{1,0:T(8,128)(2,1)S(1)}) custom-call(f32[4,5120]{1,0:T(4,128)} %bitcast.2, bf16[1,64,5120]{2,1,0:T(8,128)(2,1)} %refs_0_.5), custom_call_target="tpu_custom_call" | custom-call | flops 1 | bytes 1 | tf_op jit(solution)/shard_map/token_factor/pallas_call | solution.py:396
  6.2 4.2 %error_left.1 = (f32[4,768]{1,0:T(4,128)S(1)}, bf16[1,768,5120]{2,1,0:T(8,128)(2,1)S(1)}) custom-call(bf16[12,5120]{1,0:T(8,128)(2,1)S(1)} %get-tuple-element.41.terms_ref, bf16[1,768,5120]{2,1,0:T(8,128)(2,1)} %e_hbm.1), custom_call_target="tpu_custom_call" | custom-call | flops 4600000000 | bytes 1 | tf_op jit(solution)/shard_map/error_left/pallas_call | solution.py:407
  10.4 1.4 %collective-permute-start.3 = (f32[8,128]{1,0:T(8,128)S(1)}, f32[8,128]{1,0:T(8,128)S(1)}, u32[]{:S(2)}, u32[]{:S(2)}) collective-permute-start(f32[8,128]{1,0:T(8,128)S(1)} %get-tuple-element.45.refs_0_), channel_id=1, source_target_pairs={{0,3},{1,2},{2,1},{3,0},{4,7},{5,6},{6,5},{7,4},{8,11},{9,10},{10,... | collective-permute-start | bytes 12296 | tf_op jit(solution)/shard_map/ppermute | solution.py:66
  12.1 2.7 %collective-permute-start.1 = (f32[8,128]{1,0:T(8,128)S(1)}, f32[8,128]{1,0:T(8,128)S(1)}, u32[]{:S(2)}, u32[]{:S(2)}) collective-permute-start(f32[8,128]{1,0:T(8,128)S(1)} %get-tuple-element.45.refs_0_), channel_id=1, source_target_pairs={{0,1},{1,0},{2,3},{3,2},{4,5},{5,4},{6,7},{7,6},{8,9},{9,8},{10,11... | collective-permute-start | bytes 12296 | tf_op jit(solution)/shard_map/ppermute | solution.py:66
  14.9 6.1 %collective-permute-done.3.refs_3_ = f32[8,128]{1,0:T(8,128)S(1)} collective-permute-done((f32[8,128]{1,0:T(8,128)S(1)}, f32[8,128]{1,0:T(8,128)S(1)}, u32[]{:S(2)}, u32[]{:S(2)}) %collective-permute-start.3) | collective-permute-done | bytes 4128 | tf_op jit(solution)/shard_map/ppermute | solution.py:66
  21.1 1.5 %collective-permute-start.8 = (bf16[1,64,5120]{2,1,0:T(8,128)(2,1)S(1)}, bf16[1,64,5120]{2,1,0:T(8,128)(2,1)S(1)}, u32[]{:S(2)}, u32[]{:S(2)}) collective-permute-start(bf16[1,64,5120]{2,1,0:T(8,128)(2,1)S(1)} %collective-permute-done.refs_1_), channel_id=1, source_target_pairs={{0,2},{2,3},{3,1},{1,0},{4,6},{6,7},{7,5},{5,4},{8,10},{10,11},{11... | collective-permute-start | bytes 1966088 | tf_op jit(solution)/shard_map/ppermute | solution.py:62
  22.9 1.2 %collective-permute-done.4.refs_1_ = f32[4,768]{1,0:T(4,128)S(1)} collective-permute-done((f32[4,768]{1,0:T(4,128)S(1)}, f32[4,768]{1,0:T(4,128)S(1)}, u32[]{:S(2)}, u32[]{:S(2)}) %collective-permute-start.4) | collective-permute-done | bytes 12320 | tf_op jit(solution)/shard_map/ppermute | solution.py:66
  24.0 2.4 %collective-permute-start.7 = (f32[4,768]{1,0:T(4,128)S(1)}, f32[4,768]{1,0:T(4,128)S(1)}, u32[]{:S(2)}, u32[]{:S(2)}) collective-permute-start(f32[4,768]{1,0:T(4,128)S(1)} %add.3.refs_0_), channel_id=1, source_target_pairs={{0,24},{4,28},{8,16},{12,20},{16,8},{20,12},{24,0},{28,4},{1,25},{... | collective-permute-start | bytes 36872 | tf_op jit(solution)/shard_map/ppermute | solution.py:66
  28.6 1.5 %collective-permute-done.6.refs_2_ = f32[4,768]{1,0:T(4,128)S(1)} collective-permute-done((f32[4,768]{1,0:T(4,128)S(1)}, f32[4,768]{1,0:T(4,128)S(1)}, u32[]{:S(2)}, u32[]{:S(2)}) %collective-permute-start.6) | collective-permute-done | bytes 12320 | tf_op jit(solution)/shard_map/ppermute | solution.py:66
  31.1 1.5 %collective-permute-start.9 = (f32[8,128]{1,0:T(8,128)S(1)}, f32[8,128]{1,0:T(8,128)S(1)}, u32[]{:S(2)}, u32[]{:S(2)}) collective-permute-start(f32[8,128]{1,0:T(8,128)S(1)} %get-tuple-element.51), channel_id=1, source_target_pairs={{0,2},{2,3},{3,1},{1,0},{4,6},{6,7},{7,5},{5,4},{8,10},{10,11},{11... | collective-permute-start | bytes 12296 | tf_op jit(solution)/shard_map/ppermute | solution.py:62
  33.8 4.2 %collective-permute-done.9.got_ref = f32[8,128]{1,0:T(8,128)S(1)} collective-permute-done((f32[8,128]{1,0:T(8,128)S(1)}, f32[8,128]{1,0:T(8,128)S(1)}, u32[]{:S(2)}, u32[]{:S(2)}) %collective-permute-start.9) | collective-permute-done | bytes 4128 | tf_op jit(solution)/shard_map/ppermute | solution.py:62
  38.0 1.3 %collective-permute-start.10 = (bf16[1,64,3584]{2,1,0:T(8,128)(2,1)S(1)}, bf16[1,64,3584]{2,1,0:T(8,128)(2,1)S(1)}, u32[]{:S(2)}, u32[]{:S(2)}) collective-permute-start(bf16[1,64,3584]{2,1,0:T(8,128)(2,1)S(1)} %get-tuple-element.56), channel_id=1, source_target_pairs={{0,2},{2,3},{3,1},{1,0},{4,6},{6,7},{7,5},{5,4},{8,10},{10,11},{11... | collective-permute-start | bytes 1376264 | tf_op jit(solution)/shard_map/ppermute | solution.py:62
  39.9 1.2 %collective-permute-done.11.refs_1_ = f32[4,2688]{1,0:T(4,128)S(1)} collective-permute-done((f32[4,2688]{1,0:T(4,128)S(1)}, f32[4,2688]{1,0:T(4,128)S(1)}, u32[]{:S(2)}, u32[]{:S(2)}) %collective-permute-start.11) | collective-permute-done | bytes 43040 | tf_op jit(solution)/shard_map/ppermute | solution.py:66
  41.1 2.5 %collective-permute-start.14 = (f32[4,2688]{1,0:T(4,128)S(1)}, f32[4,2688]{1,0:T(4,128)S(1)}, u32[]{:S(2)}, u32[]{:S(2)}) collective-permute-start(f32[4,2688]{1,0:T(4,128)S(1)} %add.4.refs_0_), channel_id=1, source_target_pairs={{0,24},{4,28},{8,16},{12,20},{16,8},{20,12},{24,0},{28,4},{1,25},{... | collective-permute-start | bytes 129032 | tf_op jit(solution)/shard_map/ppermute | solution.py:66
  44.7 1.4 %collective-permute-done.14.refs_3_ = f32[4,2688]{1,0:T(4,128)S(1)} collective-permute-done((f32[4,2688]{1,0:T(4,128)S(1)}, f32[4,2688]{1,0:T(4,128)S(1)}, u32[]{:S(2)}, u32[]{:S(2)}) %collective-permute-start.14) | collective-permute-done | bytes 43040 | tf_op jit(solution)/shard_map/ppermute | solution.py:66
  46.1 1.5 %collective-permute-done.13.refs_2_ = f32[4,2688]{1,0:T(4,128)S(1)} collective-permute-done((f32[4,2688]{1,0:T(4,128)S(1)}, f32[4,2688]{1,0:T(4,128)S(1)}, u32[]{:S(2)}, u32[]{:S(2)}) %collective-permute-start.13) | collective-permute-done | bytes 43040 | tf_op jit(solution)/shard_map/ppermute | solution.py:66
  48.2 1.6 %collective-permute-done.10.refs_3_ = bf16[1,64,3584]{2,1,0:T(8,128)(2,1)S(1)} collective-permute-done((bf16[1,64,3584]{2,1,0:T(8,128)(2,1)S(1)}, bf16[1,64,3584]{2,1,0:T(8,128)(2,1)S(1)}, u32[]{:S(2)}, u32[]{:S(2)}) %collective-permute-start.10) | collective-permute-done | bytes 458784 | tf_op jit(solution)/shard_map/ppermute | solution.py:62
  49.8 2.5 %collective-permute-start.17 = (f32[4,2688]{1,0:T(4,128)S(1)}, f32[4,2688]{1,0:T(4,128)S(1)}, u32[]{:S(2)}, u32[]{:S(2)}) collective-permute-start(f32[4,2688]{1,0:T(4,128)S(1)} %add.5.refs_0_), channel_id=1, source_target_pairs={{0,3},{1,2},{2,1},{3,0},{4,7},{5,6},{6,5},{7,4},{8,11},{9,10},{10,... | collective-permute-start | bytes 129032 | tf_op jit(solution)/shard_map/ppermute | solution.py:66
  54.3 1.6 %collective-permute-done.17.refs_3_ = f32[4,2688]{1,0:T(4,128)S(1)} collective-permute-done((f32[4,2688]{1,0:T(4,128)S(1)}, f32[4,2688]{1,0:T(4,128)S(1)}, u32[]{:S(2)}, u32[]{:S(2)}) %collective-permute-start.17) | collective-permute-done | bytes 43040 | tf_op jit(solution)/shard_map/ppermute | solution.py:66
  55.9 1.3 %collective-permute-done.16.refs_2_ = f32[4,2688]{1,0:T(4,128)S(1)} collective-permute-done((f32[4,2688]{1,0:T(4,128)S(1)}, f32[4,2688]{1,0:T(4,128)S(1)}, u32[]{:S(2)}, u32[]{:S(2)}) %collective-permute-start.16) | collective-permute-done | bytes 43040 | tf_op jit(solution)/shard_map/ppermute | solution.py:66
  57.9 1.6 %collective-permute-start.19 = (bf16[1,64,1536]{2,1,0:T(8,128)(2,1)S(1)}, bf16[1,64,1536]{2,1,0:T(8,128)(2,1)S(1)}, u32[]{:S(2)}, u32[]{:S(2)}) collective-permute-start(bf16[1,64,1536]{2,1,0:T(8,128)(2,1)S(1)} %get-tuple-element.69), channel_id=1, source_target_pairs={{0,2},{2,3},{3,1},{1,0},{4,6},{6,7},{7,5},{5,4},{8,10},{10,11},{11... | collective-permute-start | bytes 589832 | tf_op jit(solution)/shard_map/ppermute | solution.py:62
  60.8 4.9 %rebuild.2 = (bf16[768,5120]{1,0:T(8,128)(2,1)}, bf16[1,768,5120]{2,1,0:T(8,128)(2,1)}) custom-call(bf16[768,256]{1,0:T(8,128)(2,1)S(1)} %acts.1.acts_ref, bf16[768,24]{1,0:T(8,128)(2,1)S(1)} %get-tuple-element.65.left_ref, bf16[24,5120]{1,0:T(8,128)(2,1)S(1)} %get-tuple-element.68.right_ref, bf16[1,768,5120]{2,1,0:T(8,128)(2,1)S(1)} %get-tuple-element.53.e_ref, ...), custom_call_target="tpu_custom_call" | custom-call | flops 4000000000 | bytes 1 | tf_op jit(solution)/shard_map/rebuild/pallas_call | solution.py:506
  65.7 2.7 %rebuild.3 = (bf16[768,5120]{1,0:T(8,128)(2,1)}, bf16[1,768,5120]{2,1,0:T(8,128)(2,1)}, f32[4,5120]{1,0:T(4,128)}) custom-call(bf16[768,256]{1,0:T(8,128)(2,1)S(1)} %acts.1.acts_ref, bf16[768,24]{1,0:T(8,128)(2,1)S(1)} %get-tuple-element.65.left_ref, ...), custom_call_target="tpu_custom_call", output_to_operand_aliasing={{0}: (9, {}), {1}: (10, {})} | custom-call | flops 4000000000 | bytes 1 | tf_op jit(solution)/shard_map/rebuild/pallas_call | solution.py:506
  (36 shorter events, 11.2 us)
Async XLA Ops:
  0.6 20.5 %collective-permute-start = (bf16[1,64,5120]{2,1,0:T(8,128)(2,1)}, bf16[1,64,5120]{2,1,0:T(8,128)(2,1)S(1)}, u32[]{:S(2)}, u32[]{:S(2)}) collective-permute-start(bf16[1,64,5120]{2,1,0:T(8,128)(2,1)} %refs_0_.5), channel_id=1, source_target_pairs={{0,2},{2,3},{3,1},{1,0},{4,6},{6,7},{7,5},{5,4},{8,10},{10,11},{11... | collective-permute-start | bytes 1966088 | tf_op jit(solution)/shard_map/ppermute | solution.py:62
  6.2 16.4 %copy-start.1 = (bf16[1,256,768]{2,1,0:T(8,128)(2,1)S(1)}, bf16[1,256,768]{2,1,0:T(8,128)(2,1)}, u32[]{:S(2)}) copy-start(bf16[1,256,768]{2,1,0:T(8,128)(2,1)} %a_ref.5) | copy-start | bytes 1179652
  10.4 28.9 %copy-start = (bf16[1,64,5120]{2,1,0:T(8,128)(2,1)S(1)}, bf16[1,64,5120]{2,1,0:T(8,128)(2,1)}, u32[]{:S(2)}) copy-start(bf16[1,64,5120]{2,1,0:T(8,128)(2,1)} %refs_0_.5) | copy-start | bytes 1966084
  10.4 10.5 %collective-permute-start.3 = (f32[8,128]{1,0:T(8,128)S(1)}, f32[8,128]{1,0:T(8,128)S(1)}, u32[]{:S(2)}, u32[]{:S(2)}) collective-permute-start(f32[8,128]{1,0:T(8,128)S(1)} %get-tuple-element.45.refs_0_), channel_id=1, source_target_pairs={{0,3},{1,2},{2,1},{3,0},{4,7},{5,6},{6,5},{7,4},{8,11},{9,10},{10,... | collective-permute-start | bytes 12296 | tf_op jit(solution)/shard_map/ppermute | solution.py:66
  11.8 9.2 %collective-permute-start.2 = (f32[8,128]{1,0:T(8,128)S(1)}, f32[8,128]{1,0:T(8,128)S(1)}, u32[]{:S(2)}, u32[]{:S(2)}) collective-permute-start(f32[8,128]{1,0:T(8,128)S(1)} %get-tuple-element.45.refs_0_), channel_id=1, source_target_pairs={{0,2},{1,3},{2,0},{3,1},{4,6},{5,7},{6,4},{7,5},{8,10},{9,11},{10,... | collective-permute-start | bytes 12296 | tf_op jit(solution)/shard_map/ppermute | solution.py:66
  12.1 8.9 %collective-permute-start.1 = (f32[8,128]{1,0:T(8,128)S(1)}, f32[8,128]{1,0:T(8,128)S(1)}, u32[]{:S(2)}, u32[]{:S(2)}) collective-permute-start(f32[8,128]{1,0:T(8,128)S(1)} %get-tuple-element.45.refs_0_), channel_id=1, source_target_pairs={{0,1},{1,0},{2,3},{3,2},{4,5},{5,4},{6,7},{7,6},{8,9},{9,8},{10,11... | collective-permute-start | bytes 12296 | tf_op jit(solution)/shard_map/ppermute | solution.py:66
  21.1 16.8 %collective-permute-start.8 = (bf16[1,64,5120]{2,1,0:T(8,128)(2,1)S(1)}, bf16[1,64,5120]{2,1,0:T(8,128)(2,1)S(1)}, u32[]{:S(2)}, u32[]{:S(2)}) collective-permute-start(bf16[1,64,5120]{2,1,0:T(8,128)(2,1)S(1)} %collective-permute-done.refs_1_), channel_id=1, source_target_pairs={{0,2},{2,3},{3,1},{1,0},{4,6},{6,7},{7,5},{5,4},{8,10},{10,11},{11... | collective-permute-start | bytes 1966088 | tf_op jit(solution)/shard_map/ppermute | solution.py:62
  22.8 1.2 %collective-permute-start.4 = (f32[4,768]{1,0:T(4,128)S(1)}, f32[4,768]{1,0:T(4,128)S(1)}, u32[]{:S(2)}, u32[]{:S(2)}) collective-permute-start(f32[4,768]{1,0:T(4,128)S(1)} %left.1.refs_0_), channel_id=1, source_target_pairs={{0,4},{4,0},{8,12},{12,8},{16,20},{20,16},{24,28},{28,24},{1,5},{5... | collective-permute-start | bytes 36872 | tf_op jit(solution)/shard_map/ppermute | solution.py:66
  24.0 4.6 %collective-permute-start.7 = (f32[4,768]{1,0:T(4,128)S(1)}, f32[4,768]{1,0:T(4,128)S(1)}, u32[]{:S(2)}, u32[]{:S(2)}) collective-permute-start(f32[4,768]{1,0:T(4,128)S(1)} %add.3.refs_0_), channel_id=1, source_target_pairs={{0,24},{4,28},{8,16},{12,20},{16,8},{20,12},{24,0},{28,4},{1,25},{... | collective-permute-start | bytes 36872 | tf_op jit(solution)/shard_map/ppermute | solution.py:66
  26.5 3.7 %collective-permute-start.6 = (f32[4,768]{1,0:T(4,128)S(1)}, f32[4,768]{1,0:T(4,128)S(1)}, u32[]{:S(2)}, u32[]{:S(2)}) collective-permute-start(f32[4,768]{1,0:T(4,128)S(1)} %add.3.refs_0_), channel_id=1, source_target_pairs={{0,16},{4,20},{8,24},{12,28},{16,0},{20,4},{24,8},{28,12},{1,17},{... | collective-permute-start | bytes 36872 | tf_op jit(solution)/shard_map/ppermute | solution.py:66
  27.0 3.7 %collective-permute-start.5 = (f32[4,768]{1,0:T(4,128)S(1)}, f32[4,768]{1,0:T(4,128)S(1)}, u32[]{:S(2)}, u32[]{:S(2)}) collective-permute-start(f32[4,768]{1,0:T(4,128)S(1)} %add.3.refs_0_), channel_id=1, source_target_pairs={{0,8},{4,12},{8,0},{12,4},{16,24},{20,28},{24,16},{28,20},{1,9},{5... | collective-permute-start | bytes 36872 | tf_op jit(solution)/shard_map/ppermute | solution.py:66
  31.1 6.8 %collective-permute-start.9 = (f32[8,128]{1,0:T(8,128)S(1)}, f32[8,128]{1,0:T(8,128)S(1)}, u32[]{:S(2)}, u32[]{:S(2)}) collective-permute-start(f32[8,128]{1,0:T(8,128)S(1)} %get-tuple-element.51), channel_id=1, source_target_pairs={{0,2},{2,3},{3,1},{1,0},{4,6},{6,7},{7,5},{5,4},{8,10},{10,11},{11... | collective-permute-start | bytes 12296 | tf_op jit(solution)/shard_map/ppermute | solution.py:62
  38.0 11.7 %collective-permute-start.10 = (bf16[1,64,3584]{2,1,0:T(8,128)(2,1)S(1)}, bf16[1,64,3584]{2,1,0:T(8,128)(2,1)S(1)}, u32[]{:S(2)}, u32[]{:S(2)}) collective-permute-start(bf16[1,64,3584]{2,1,0:T(8,128)(2,1)S(1)} %get-tuple-element.56), channel_id=1, source_target_pairs={{0,2},{2,3},{3,1},{1,0},{4,6},{6,7},{7,5},{5,4},{8,10},{10,11},{11... | collective-permute-start | bytes 1376264 | tf_op jit(solution)/shard_map/ppermute | solution.py:62
  39.8 1.3 %collective-permute-start.11 = (f32[4,2688]{1,0:T(4,128)S(1)}, f32[4,2688]{1,0:T(4,128)S(1)}, u32[]{:S(2)}, u32[]{:S(2)}) collective-permute-start(f32[4,2688]{1,0:T(4,128)S(1)} %get-tuple-element.62), channel_id=1, source_target_pairs={{0,4},{4,0},{8,12},{12,8},{16,20},{20,16},{24,28},{28,24},{1,5},{5... | collective-permute-start | bytes 129032 | tf_op jit(solution)/shard_map/ppermute | solution.py:66
  41.1 5.0 %collective-permute-start.14 = (f32[4,2688]{1,0:T(4,128)S(1)}, f32[4,2688]{1,0:T(4,128)S(1)}, u32[]{:S(2)}, u32[]{:S(2)}) collective-permute-start(f32[4,2688]{1,0:T(4,128)S(1)} %add.4.refs_0_), channel_id=1, source_target_pairs={{0,24},{4,28},{8,16},{12,20},{16,8},{20,12},{24,0},{28,4},{1,25},{... | collective-permute-start | bytes 129032 | tf_op jit(solution)/shard_map/ppermute | solution.py:66
  43.6 4.0 %collective-permute-start.13 = (f32[4,2688]{1,0:T(4,128)S(1)}, f32[4,2688]{1,0:T(4,128)S(1)}, u32[]{:S(2)}, u32[]{:S(2)}) collective-permute-start(f32[4,2688]{1,0:T(4,128)S(1)} %add.4.refs_0_), channel_id=1, source_target_pairs={{0,16},{4,20},{8,24},{12,28},{16,0},{20,4},{24,8},{28,12},{1,17},{... | collective-permute-start | bytes 129032 | tf_op jit(solution)/shard_map/ppermute | solution.py:66
  44.2 4.0 %collective-permute-start.12 = (f32[4,2688]{1,0:T(4,128)S(1)}, f32[4,2688]{1,0:T(4,128)S(1)}, u32[]{:S(2)}, u32[]{:S(2)}) collective-permute-start(f32[4,2688]{1,0:T(4,128)S(1)} %add.4.refs_0_), channel_id=1, source_target_pairs={{0,8},{4,12},{8,0},{12,4},{16,24},{20,28},{24,16},{28,20},{1,9},{5... | collective-permute-start | bytes 129032 | tf_op jit(solution)/shard_map/ppermute | solution.py:66
  49.8 6.1 %collective-permute-start.17 = (f32[4,2688]{1,0:T(4,128)S(1)}, f32[4,2688]{1,0:T(4,128)S(1)}, u32[]{:S(2)}, u32[]{:S(2)}) collective-permute-start(f32[4,2688]{1,0:T(4,128)S(1)} %add.5.refs_0_), channel_id=1, source_target_pairs={{0,3},{1,2},{2,1},{3,0},{4,7},{5,6},{6,5},{7,4},{8,11},{9,10},{10,... | collective-permute-start | bytes 129032 | tf_op jit(solution)/shard_map/ppermute | solution.py:66
  52.2 5.0 %collective-permute-start.16 = (f32[4,2688]{1,0:T(4,128)S(1)}, f32[4,2688]{1,0:T(4,128)S(1)}, u32[]{:S(2)}, u32[]{:S(2)}) collective-permute-start(f32[4,2688]{1,0:T(4,128)S(1)} %add.5.refs_0_), channel_id=1, source_target_pairs={{0,2},{1,3},{2,0},{3,1},{4,6},{5,7},{6,4},{7,5},{8,10},{9,11},{10,... | collective-permute-start | bytes 129032 | tf_op jit(solution)/shard_map/ppermute | solution.py:66
  53.2 4.5 %collective-permute-start.15 = (f32[4,2688]{1,0:T(4,128)S(1)}, f32[4,2688]{1,0:T(4,128)S(1)}, u32[]{:S(2)}, u32[]{:S(2)}) collective-permute-start(f32[4,2688]{1,0:T(4,128)S(1)} %add.5.refs_0_), channel_id=1, source_target_pairs={{0,1},{1,0},{2,3},{3,2},{4,5},{5,4},{6,7},{7,6},{8,9},{9,8},{10,11... | collective-permute-start | bytes 129032 | tf_op jit(solution)/shard_map/ppermute | solution.py:66
  57.8 2.4 %collective-permute-start.18 = (f32[4,2688]{1,0:T(4,128)S(1)}, f32[4,2688]{1,0:T(4,128)S(1)}, u32[]{:S(2)}, u32[]{:S(2)}) collective-permute-start(f32[4,2688]{1,0:T(4,128)S(1)} %join.1.mine_ref), channel_id=1, source_target_pairs={{0,4},{4,0},{8,12},{12,8},{16,20},{20,16},{24,28},{28,24},{1,5},{5... | collective-permute-start | bytes 129032 | tf_op jit(solution)/shard_map/ppermute | solution.py:66
  57.9 7.8 %collective-permute-start.19 = (bf16[1,64,1536]{2,1,0:T(8,128)(2,1)S(1)}, bf16[1,64,1536]{2,1,0:T(8,128)(2,1)S(1)}, u32[]{:S(2)}, u32[]{:S(2)}) collective-permute-start(bf16[1,64,1536]{2,1,0:T(8,128)(2,1)S(1)} %get-tuple-element.69), channel_id=1, source_target_pairs={{0,2},{2,3},{3,1},{1,0},{4,6},{6,7},{7,5},{5,4},{8,10},{10,11},{11... | collective-permute-start | bytes 589832 | tf_op jit(solution)/shard_map/ppermute | solution.py:62

commit v19 on v18

--- a/solution.py
+++ b/solution.py
@@ -60,6 +60,12 @@
 def ring_step(x, axis, n):
     ring = ring_of(n)
     return lax.ppermute(x, axis, [(ring[p], ring[(p + 1) % n]) for p in range(n)])
+
+
+def exchange(pieces, axis, n):
+    return [pieces[0]] + [
+        lax.ppermute(pieces[k], axis, [(i, (i + k) % n) for i in range(n)]) for k in range(1, n)
+    ]
 
 
 def swap(x, axis, n, bit):
@@ -137,7 +143,7 @@
     me = lax.axis_index("tensor")
     total = e_ref[...]
     for k in range(n):
-        src = me ^ k
+        src = lax.rem(me - k + n, n)
         rows = a_ref[0, pl.ds(pl.multiple_of(src * tok, tok), tok), :]
         total += sum3(dot(stack3(gws[k][0:rank, 0:tok], g3), rows, (1, 0)), rank)
     out_ref[...] = total
@@ -412,7 +418,7 @@
     )(w_terms, pin(error_buffer))
 
     gw, ew = after(gw, ew)
-    gws = [gw] + [swap(gw, "tensor", n, k) for k in range(1, n)]
+    gws = exchange([gw] * n, "tensor", n)
     ring[1], gws = after(ring[1], gws)
     for _ in range(n - 2 - 1):
         ring.append(step(ring[-1]))

time: 68.5 us -> 66.8 us (0.975)
  starting transfers between devices: 26.1 us -> 24.6 us
    ppermute x15 -> x12, waiting for transfers between devices: 18.5 us -> 10.9 us  [swap(): return lax.ppermute(x, axis, [(i, i ^ bit) for i in range(n)])]
    ppermute x0 -> x3, waiting for transfers between devices: none -> 6.99 us  [exchange(): lax.ppermute(pieces[k], axis, [(i, (i + k) % n) for i in range(n)])]
    ppermute x15 -> x12, starting transfers between devices: 16.1 us -> 11.6 us  [swap(): return lax.ppermute(x, axis, [(i, i ^ bit) for i in range(n)])]
    ppermute x0 -> x3, starting transfers between devices: none -> 3.65 us  [exchange(): lax.ppermute(pieces[k], axis, [(i, (i + k) % n) for i in range(n)])]
where the time goes in v19:
time: 66.8 us; the launch traced here: 66.6 us
  starting transfers between devices  24.6 us (37%)
  waiting for transfers between devices  24 us (36%)
  Pallas kernels  17.2 us (26%)
  between operations  0.77 us (1%)
    ppermute x12, starting transfers between devices, swap(): return lax.ppermute(x, axis, [(i, i ^ bit) for i in range(n)])  11.6 us
    ppermute x12, waiting for transfers between devices, swap(): return lax.ppermute(x, axis, [(i, i ^ bit) for i in range(n)])  10.9 us
    ppermute x5, starting transfers between devices, ring_step(): lax.ppermute(x, axis, [(ring[p], ring[(p + 1) % n]) for p in range(n)])  9.33 us
    pallas_call x2, Pallas kernels, per_device(): pl.pallas_call(functools.partial(final_kernel, at, part, bases, last), in...  7.57 us
    ppermute x3, waiting for transfers between devices, exchange(): lax.ppermute(pieces[k], axis, [(i, (i + k) % n) for i in range(n)])  6.99 us
    ppermute x5, waiting for transfers between devices, ring_step(): lax.ppermute(x, axis, [(ring[p], ring[(p + 1) % n]) for p in range(n)])  6.17 us
    pallas_call x1, Pallas kernels, per_device(): call(error_left_kernel, [sds((rank, rows), F32), sds((1, rows, width), BF...  4.19 us
    ppermute x3, starting transfers between devices, exchange(): lax.ppermute(pieces[k], axis, [(i, (i + k) % n) for i in range(n)])  3.65 us
  transfers between devices with their start and end apart: 20, of which 15 were waited for; matrix products, arithmetic and copies ran while one was open for 0% of the time, Pallas kernels for 21%

profile of v19, /device:TPU:0, one launch (start us, length us, event | category | flops | bytes accessed | tf_op | source)
XLA Modules:
  0.0 66.6 jit_solution(1884037297935387771)
XLA Ops:
  0.6 4.1 %collective-permute-start = (bf16[1,64,5120]{2,1,0:T(8,128)(2,1)}, bf16[1,64,5120]{2,1,0:T(8,128)(2,1)S(1)}, u32[]{:S(2)}, u32[]{:S(2)}) collective-permute-start(bf16[1,64,5120]{2,1,0:T(8,128)(2,1)} %refs_0_.5), channel_id=1, source_target_pairs={{0,2},{2,3},{3,1},{1,0},{4,6},{6,7},{7,5},{5,4},{8,10},{10,11},{11... | collective-permute-start | bytes 1966088 | tf_op jit(solution)/shard_map/ppermute | solution.py:62
  4.7 1.5 %token_factor.1 = (f32[8,128]{1,0:T(8,128)S(1)}, bf16[12,5120]{1,0:T(8,128)(2,1)S(1)}) custom-call(f32[4,5120]{1,0:T(4,128)} %bitcast.2, bf16[1,64,5120]{2,1,0:T(8,128)(2,1)} %refs_0_.5), custom_call_target="tpu_custom_call" | custom-call | flops 1 | bytes 1 | tf_op jit(solution)/shard_map/token_factor/pallas_call | solution.py:402
  6.2 4.2 %error_left.1 = (f32[4,768]{1,0:T(4,128)S(1)}, bf16[1,768,5120]{2,1,0:T(8,128)(2,1)S(1)}) custom-call(bf16[12,5120]{1,0:T(8,128)(2,1)S(1)} %get-tuple-element.41.terms_ref, bf16[1,768,5120]{2,1,0:T(8,128)(2,1)} %e_hbm.1), custom_call_target="tpu_custom_call" | custom-call | flops 4600000000 | bytes 1 | tf_op jit(solution)/shard_map/error_left/pallas_call | solution.py:413
  10.4 1.4 %collective-permute-start.3 = (f32[8,128]{1,0:T(8,128)S(1)}, f32[8,128]{1,0:T(8,128)S(1)}, u32[]{:S(2)}, u32[]{:S(2)}) collective-permute-start(f32[8,128]{1,0:T(8,128)S(1)} %get-tuple-element.45.refs_0_), channel_id=1, source_target_pairs={{0,3},{1,0},{2,1},{3,2},{4,7},{5,4},{6,5},{7,6},{8,11},{9,8},{10,9... | collective-permute-start | bytes 12296 | tf_op jit(solution)/shard_map/ppermute | solution.py:67
  12.1 1.9 %collective-permute-start.1 = (f32[8,128]{1,0:T(8,128)S(1)}, f32[8,128]{1,0:T(8,128)S(1)}, u32[]{:S(2)}, u32[]{:S(2)}) collective-permute-start(f32[8,128]{1,0:T(8,128)S(1)} %get-tuple-element.45.refs_0_), channel_id=1, source_target_pairs={{0,1},{1,2},{2,3},{3,0},{4,5},{5,6},{6,7},{7,4},{8,9},{9,10},{10,1... | collective-permute-start | bytes 12296 | tf_op jit(solution)/shard_map/ppermute | solution.py:67
  14.1 5.1 %collective-permute-done.3.refs_3_ = f32[8,128]{1,0:T(8,128)S(1)} collective-permute-done((f32[8,128]{1,0:T(8,128)S(1)}, f32[8,128]{1,0:T(8,128)S(1)}, u32[]{:S(2)}, u32[]{:S(2)}) %collective-permute-start.3) | collective-permute-done | bytes 4128 | tf_op jit(solution)/shard_map/ppermute | solution.py:67
  19.2 1.9 %collective-permute-done.2.refs_2_ = f32[8,128]{1,0:T(8,128)S(1)} collective-permute-done((f32[8,128]{1,0:T(8,128)S(1)}, f32[8,128]{1,0:T(8,128)S(1)}, u32[]{:S(2)}, u32[]{:S(2)}) %collective-permute-start.2) | collective-permute-done | bytes 4128 | tf_op jit(solution)/shard_map/ppermute | solution.py:67
  21.1 1.6 %collective-permute-start.8 = (bf16[1,64,5120]{2,1,0:T(8,128)(2,1)S(1)}, bf16[1,64,5120]{2,1,0:T(8,128)(2,1)S(1)}, u32[]{:S(2)}, u32[]{:S(2)}) collective-permute-start(bf16[1,64,5120]{2,1,0:T(8,128)(2,1)S(1)} %collective-permute-done.refs_1_), channel_id=1, source_target_pairs={{0,2},{2,3},{3,1},{1,0},{4,6},{6,7},{7,5},{5,4},{8,10},{10,11},{11... | collective-permute-start | bytes 1966088 | tf_op jit(solution)/shard_map/ppermute | solution.py:62
  22.9 1.2 %collective-permute-done.4.refs_1_ = f32[4,768]{1,0:T(4,128)S(1)} collective-permute-done((f32[4,768]{1,0:T(4,128)S(1)}, f32[4,768]{1,0:T(4,128)S(1)}, u32[]{:S(2)}, u32[]{:S(2)}) %collective-permute-start.4) | collective-permute-done | bytes 12320 | tf_op jit(solution)/shard_map/ppermute | solution.py:72
  24.1 2.4 %collective-permute-start.7 = (f32[4,768]{1,0:T(4,128)S(1)}, f32[4,768]{1,0:T(4,128)S(1)}, u32[]{:S(2)}, u32[]{:S(2)}) collective-permute-start(f32[4,768]{1,0:T(4,128)S(1)} %add.3.refs_0_), channel_id=1, source_target_pairs={{0,24},{4,28},{8,16},{12,20},{16,8},{20,12},{24,0},{28,4},{1,25},{... | collective-permute-start | bytes 36872 | tf_op jit(solution)/shard_map/ppermute | solution.py:72
  28.7 1.5 %collective-permute-done.6.refs_2_ = f32[4,768]{1,0:T(4,128)S(1)} collective-permute-done((f32[4,768]{1,0:T(4,128)S(1)}, f32[4,768]{1,0:T(4,128)S(1)}, u32[]{:S(2)}, u32[]{:S(2)}) %collective-permute-start.6) | collective-permute-done | bytes 12320 | tf_op jit(solution)/shard_map/ppermute | solution.py:72
  31.1 1.4 %collective-permute-start.9 = (f32[8,128]{1,0:T(8,128)S(1)}, f32[8,128]{1,0:T(8,128)S(1)}, u32[]{:S(2)}, u32[]{:S(2)}) collective-permute-start(f32[8,128]{1,0:T(8,128)S(1)} %get-tuple-element.51), channel_id=1, source_target_pairs={{0,2},{2,3},{3,1},{1,0},{4,6},{6,7},{7,5},{5,4},{8,10},{10,11},{11... | collective-permute-start | bytes 12296 | tf_op jit(solution)/shard_map/ppermute | solution.py:62
  33.7 4.2 %collective-permute-done.9.got_ref = f32[8,128]{1,0:T(8,128)S(1)} collective-permute-done((f32[8,128]{1,0:T(8,128)S(1)}, f32[8,128]{1,0:T(8,128)S(1)}, u32[]{:S(2)}, u32[]{:S(2)}) %collective-permute-start.9) | collective-permute-done | bytes 4128 | tf_op jit(solution)/shard_map/ppermute | solution.py:62
  38.0 1.3 %collective-permute-start.10 = (bf16[1,64,3584]{2,1,0:T(8,128)(2,1)S(1)}, bf16[1,64,3584]{2,1,0:T(8,128)(2,1)S(1)}, u32[]{:S(2)}, u32[]{:S(2)}) collective-permute-start(bf16[1,64,3584]{2,1,0:T(8,128)(2,1)S(1)} %get-tuple-element.56), channel_id=1, source_target_pairs={{0,2},{2,3},{3,1},{1,0},{4,6},{6,7},{7,5},{5,4},{8,10},{10,11},{11... | collective-permute-start | bytes 1376264 | tf_op jit(solution)/shard_map/ppermute | solution.py:62
  39.9 1.2 %collective-permute-done.11.refs_1_ = f32[4,2688]{1,0:T(4,128)S(1)} collective-permute-done((f32[4,2688]{1,0:T(4,128)S(1)}, f32[4,2688]{1,0:T(4,128)S(1)}, u32[]{:S(2)}, u32[]{:S(2)}) %collective-permute-start.11) | collective-permute-done | bytes 43040 | tf_op jit(solution)/shard_map/ppermute | solution.py:72
  41.1 2.5 %collective-permute-start.14 = (f32[4,2688]{1,0:T(4,128)S(1)}, f32[4,2688]{1,0:T(4,128)S(1)}, u32[]{:S(2)}, u32[]{:S(2)}) collective-permute-start(f32[4,2688]{1,0:T(4,128)S(1)} %add.4.refs_0_), channel_id=1, source_target_pairs={{0,24},{4,28},{8,16},{12,20},{16,8},{20,12},{24,0},{28,4},{1,25},{... | collective-permute-start | bytes 129032 | tf_op jit(solution)/shard_map/ppermute | solution.py:72
  44.7 1.4 %collective-permute-done.14.refs_3_ = f32[4,2688]{1,0:T(4,128)S(1)} collective-permute-done((f32[4,2688]{1,0:T(4,128)S(1)}, f32[4,2688]{1,0:T(4,128)S(1)}, u32[]{:S(2)}, u32[]{:S(2)}) %collective-permute-start.14) | collective-permute-done | bytes 43040 | tf_op jit(solution)/shard_map/ppermute | solution.py:72
  46.1 1.5 %collective-permute-done.13.refs_2_ = f32[4,2688]{1,0:T(4,128)S(1)} collective-permute-done((f32[4,2688]{1,0:T(4,128)S(1)}, f32[4,2688]{1,0:T(4,128)S(1)}, u32[]{:S(2)}, u32[]{:S(2)}) %collective-permute-start.13) | collective-permute-done | bytes 43040 | tf_op jit(solution)/shard_map/ppermute | solution.py:72
  48.2 1.6 %collective-permute-done.10.refs_3_ = bf16[1,64,3584]{2,1,0:T(8,128)(2,1)S(1)} collective-permute-done((bf16[1,64,3584]{2,1,0:T(8,128)(2,1)S(1)}, bf16[1,64,3584]{2,1,0:T(8,128)(2,1)S(1)}, u32[]{:S(2)}, u32[]{:S(2)}) %collective-permute-start.10) | collective-permute-done | bytes 458784 | tf_op jit(solution)/shard_map/ppermute | solution.py:62
  49.8 1.9 %collective-permute-start.16 = (f32[4,2688]{1,0:T(4,128)S(1)}, f32[4,2688]{1,0:T(4,128)S(1)}, u32[]{:S(2)}, u32[]{:S(2)}) collective-permute-start(f32[4,2688]{1,0:T(4,128)S(1)} %add.5.refs_0_), channel_id=1, source_target_pairs={{0,2},{1,3},{2,0},{3,1},{4,6},{5,7},{6,4},{7,5},{8,10},{9,11},{10,... | collective-permute-start | bytes 129032 | tf_op jit(solution)/shard_map/ppermute | solution.py:72
  51.7 2.5 %collective-permute-start.15 = (f32[4,2688]{1,0:T(4,128)S(1)}, f32[4,2688]{1,0:T(4,128)S(1)}, u32[]{:S(2)}, u32[]{:S(2)}) collective-permute-start(f32[4,2688]{1,0:T(4,128)S(1)} %add.5.refs_0_), channel_id=1, source_target_pairs={{0,1},{1,0},{2,3},{3,2},{4,5},{5,4},{6,7},{7,6},{8,9},{9,8},{10,11... | collective-permute-start | bytes 129032 | tf_op jit(solution)/shard_map/ppermute | solution.py:72
  54.3 1.3 %collective-permute-done.17.refs_3_ = f32[4,2688]{1,0:T(4,128)S(1)} collective-permute-done((f32[4,2688]{1,0:T(4,128)S(1)}, f32[4,2688]{1,0:T(4,128)S(1)}, u32[]{:S(2)}, u32[]{:S(2)}) %collective-permute-start.17) | collective-permute-done | bytes 43040 | tf_op jit(solution)/shard_map/ppermute | solution.py:72
  58.7 4.9 %rebuild.2 = (bf16[768,5120]{1,0:T(8,128)(2,1)}, bf16[1,768,5120]{2,1,0:T(8,128)(2,1)}) custom-call(bf16[768,256]{1,0:T(8,128)(2,1)S(1)} %acts.1.acts_ref, bf16[768,24]{1,0:T(8,128)(2,1)S(1)} %get-tuple-element.65.left_ref, bf16[24,5120]{1,0:T(8,128)(2,1)S(1)} %get-tuple-element.68.right_ref, bf16[1,768,5120]{2,1,0:T(8,128)(2,1)S(1)} %get-tuple-element.53.e_ref, ...), custom_call_target="tpu_custom_call" | custom-call | flops 4000000000 | bytes 1 | tf_op jit(solution)/shard_map/rebuild/pallas_call | solution.py:512
  64.0 2.7 %rebuild.3 = (bf16[768,5120]{1,0:T(8,128)(2,1)}, bf16[1,768,5120]{2,1,0:T(8,128)(2,1)}, f32[4,5120]{1,0:T(4,128)}) custom-call(bf16[768,256]{1,0:T(8,128)(2,1)S(1)} %acts.1.acts_ref, bf16[768,24]{1,0:T(8,128)(2,1)S(1)} %get-tuple-element.65.left_ref, ...), custom_call_target="tpu_custom_call", output_to_operand_aliasing={{0}: (9, {}), {1}: (10, {})} | custom-call | flops 4000000000 | bytes 1 | tf_op jit(solution)/shard_map/rebuild/pallas_call | solution.py:512
  (36 shorter events, 10.7 us)
Async XLA Ops:
  0.6 20.5 %collective-permute-start = (bf16[1,64,5120]{2,1,0:T(8,128)(2,1)}, bf16[1,64,5120]{2,1,0:T(8,128)(2,1)S(1)}, u32[]{:S(2)}, u32[]{:S(2)}) collective-permute-start(bf16[1,64,5120]{2,1,0:T(8,128)(2,1)} %refs_0_.5), channel_id=1, source_target_pairs={{0,2},{2,3},{3,1},{1,0},{4,6},{6,7},{7,5},{5,4},{8,10},{10,11},{11... | collective-permute-start | bytes 1966088 | tf_op jit(solution)/shard_map/ppermute | solution.py:62
  6.2 16.5 %copy-start.1 = (bf16[1,256,768]{2,1,0:T(8,128)(2,1)S(1)}, bf16[1,256,768]{2,1,0:T(8,128)(2,1)}, u32[]{:S(2)}) copy-start(bf16[1,256,768]{2,1,0:T(8,128)(2,1)} %a_ref.5) | copy-start | bytes 1179652
  10.4 28.9 %copy-start = (bf16[1,64,5120]{2,1,0:T(8,128)(2,1)S(1)}, bf16[1,64,5120]{2,1,0:T(8,128)(2,1)}, u32[]{:S(2)}) copy-start(bf16[1,64,5120]{2,1,0:T(8,128)(2,1)} %refs_0_.5) | copy-start | bytes 1966084
  10.4 8.8 %collective-permute-start.3 = (f32[8,128]{1,0:T(8,128)S(1)}, f32[8,128]{1,0:T(8,128)S(1)}, u32[]{:S(2)}, u32[]{:S(2)}) collective-permute-start(f32[8,128]{1,0:T(8,128)S(1)} %get-tuple-element.45.refs_0_), channel_id=1, source_target_pairs={{0,3},{1,0},{2,1},{3,2},{4,7},{5,4},{6,5},{7,6},{8,11},{9,8},{10,9... | collective-permute-start | bytes 12296 | tf_op jit(solution)/shard_map/ppermute | solution.py:67
  11.8 9.2 %collective-permute-start.2 = (f32[8,128]{1,0:T(8,128)S(1)}, f32[8,128]{1,0:T(8,128)S(1)}, u32[]{:S(2)}, u32[]{:S(2)}) collective-permute-start(f32[8,128]{1,0:T(8,128)S(1)} %get-tuple-element.45.refs_0_), channel_id=1, source_target_pairs={{0,2},{1,3},{2,0},{3,1},{4,6},{5,7},{6,4},{7,5},{8,10},{9,11},{10,... | collective-permute-start | bytes 12296 | tf_op jit(solution)/shard_map/ppermute | solution.py:67
  12.1 8.9 %collective-permute-start.1 = (f32[8,128]{1,0:T(8,128)S(1)}, f32[8,128]{1,0:T(8,128)S(1)}, u32[]{:S(2)}, u32[]{:S(2)}) collective-permute-start(f32[8,128]{1,0:T(8,128)S(1)} %get-tuple-element.45.refs_0_), channel_id=1, source_target_pairs={{0,1},{1,2},{2,3},{3,0},{4,5},{5,6},{6,7},{7,4},{8,9},{9,10},{10,1... | collective-permute-start | bytes 12296 | tf_op jit(solution)/shard_map/ppermute | solution.py:67
  21.1 16.8 %collective-permute-start.8 = (bf16[1,64,5120]{2,1,0:T(8,128)(2,1)S(1)}, bf16[1,64,5120]{2,1,0:T(8,128)(2,1)S(1)}, u32[]{:S(2)}, u32[]{:S(2)}) collective-permute-start(bf16[1,64,5120]{2,1,0:T(8,128)(2,1)S(1)} %collective-permute-done.refs_1_), channel_id=1, source_target_pairs={{0,2},{2,3},{3,1},{1,0},{4,6},{6,7},{7,5},{5,4},{8,10},{10,11},{11... | collective-permute-start | bytes 1966088 | tf_op jit(solution)/shard_map/ppermute | solution.py:62
  22.9 1.2 %collective-permute-start.4 = (f32[4,768]{1,0:T(4,128)S(1)}, f32[4,768]{1,0:T(4,128)S(1)}, u32[]{:S(2)}, u32[]{:S(2)}) collective-permute-start(f32[4,768]{1,0:T(4,128)S(1)} %left.1.refs_0_), channel_id=1, source_target_pairs={{0,4},{4,0},{8,12},{12,8},{16,20},{20,16},{24,28},{28,24},{1,5},{5... | collective-permute-start | bytes 36872 | tf_op jit(solution)/shard_map/ppermute | solution.py:72
  24.1 4.6 %collective-permute-start.7 = (f32[4,768]{1,0:T(4,128)S(1)}, f32[4,768]{1,0:T(4,128)S(1)}, u32[]{:S(2)}, u32[]{:S(2)}) collective-permute-start(f32[4,768]{1,0:T(4,128)S(1)} %add.3.refs_0_), channel_id=1, source_target_pairs={{0,24},{4,28},{8,16},{12,20},{16,8},{20,12},{24,0},{28,4},{1,25},{... | collective-permute-start | bytes 36872 | tf_op jit(solution)/shard_map/ppermute | solution.py:72
  26.6 3.7 %collective-permute-start.6 = (f32[4,768]{1,0:T(4,128)S(1)}, f32[4,768]{1,0:T(4,128)S(1)}, u32[]{:S(2)}, u32[]{:S(2)}) collective-permute-start(f32[4,768]{1,0:T(4,128)S(1)} %add.3.refs_0_), channel_id=1, source_target_pairs={{0,16},{4,20},{8,24},{12,28},{16,0},{20,4},{24,8},{28,12},{1,17},{... | collective-permute-start | bytes 36872 | tf_op jit(solution)/shard_map/ppermute | solution.py:72
  27.1 3.7 %collective-permute-start.5 = (f32[4,768]{1,0:T(4,128)S(1)}, f32[4,768]{1,0:T(4,128)S(1)}, u32[]{:S(2)}, u32[]{:S(2)}) collective-permute-start(f32[4,768]{1,0:T(4,128)S(1)} %add.3.refs_0_), channel_id=1, source_target_pairs={{0,8},{4,12},{8,0},{12,4},{16,24},{20,28},{24,16},{28,20},{1,9},{5... | collective-permute-start | bytes 36872 | tf_op jit(solution)/shard_map/ppermute | solution.py:72
  31.1 6.8 %collective-permute-start.9 = (f32[8,128]{1,0:T(8,128)S(1)}, f32[8,128]{1,0:T(8,128)S(1)}, u32[]{:S(2)}, u32[]{:S(2)}) collective-permute-start(f32[8,128]{1,0:T(8,128)S(1)} %get-tuple-element.51), channel_id=1, source_target_pairs={{0,2},{2,3},{3,1},{1,0},{4,6},{6,7},{7,5},{5,4},{8,10},{10,11},{11... | collective-permute-start | bytes 12296 | tf_op jit(solution)/shard_map/ppermute | solution.py:62
  38.0 11.7 %collective-permute-start.10 = (bf16[1,64,3584]{2,1,0:T(8,128)(2,1)S(1)}, bf16[1,64,3584]{2,1,0:T(8,128)(2,1)S(1)}, u32[]{:S(2)}, u32[]{:S(2)}) collective-permute-start(bf16[1,64,3584]{2,1,0:T(8,128)(2,1)S(1)} %get-tuple-element.56), channel_id=1, source_target_pairs={{0,2},{2,3},{3,1},{1,0},{4,6},{6,7},{7,5},{5,4},{8,10},{10,11},{11... | collective-permute-start | bytes 1376264 | tf_op jit(solution)/shard_map/ppermute | solution.py:62
  39.8 1.3 %collective-permute-start.11 = (f32[4,2688]{1,0:T(4,128)S(1)}, f32[4,2688]{1,0:T(4,128)S(1)}, u32[]{:S(2)}, u32[]{:S(2)}) collective-permute-start(f32[4,2688]{1,0:T(4,128)S(1)} %get-tuple-element.62), channel_id=1, source_target_pairs={{0,4},{4,0},{8,12},{12,8},{16,20},{20,16},{24,28},{28,24},{1,5},{5... | collective-permute-start | bytes 129032 | tf_op jit(solution)/shard_map/ppermute | solution.py:72
  41.1 5.0 %collective-permute-start.14 = (f32[4,2688]{1,0:T(4,128)S(1)}, f32[4,2688]{1,0:T(4,128)S(1)}, u32[]{:S(2)}, u32[]{:S(2)}) collective-permute-start(f32[4,2688]{1,0:T(4,128)S(1)} %add.4.refs_0_), channel_id=1, source_target_pairs={{0,24},{4,28},{8,16},{12,20},{16,8},{20,12},{24,0},{28,4},{1,25},{... | collective-permute-start | bytes 129032 | tf_op jit(solution)/shard_map/ppermute | solution.py:72
  43.6 4.0 %collective-permute-start.13 = (f32[4,2688]{1,0:T(4,128)S(1)}, f32[4,2688]{1,0:T(4,128)S(1)}, u32[]{:S(2)}, u32[]{:S(2)}) collective-permute-start(f32[4,2688]{1,0:T(4,128)S(1)} %add.4.refs_0_), channel_id=1, source_target_pairs={{0,16},{4,20},{8,24},{12,28},{16,0},{20,4},{24,8},{28,12},{1,17},{... | collective-permute-start | bytes 129032 | tf_op jit(solution)/shard_map/ppermute | solution.py:72
  44.2 4.0 %collective-permute-start.12 = (f32[4,2688]{1,0:T(4,128)S(1)}, f32[4,2688]{1,0:T(4,128)S(1)}, u32[]{:S(2)}, u32[]{:S(2)}) collective-permute-start(f32[4,2688]{1,0:T(4,128)S(1)} %add.4.refs_0_), channel_id=1, source_target_pairs={{0,8},{4,12},{8,0},{12,4},{16,24},{20,28},{24,16},{28,20},{1,9},{5... | collective-permute-start | bytes 129032 | tf_op jit(solution)/shard_map/ppermute | solution.py:72
  49.8 5.8 %collective-permute-start.17 = (f32[4,2688]{1,0:T(4,128)S(1)}, f32[4,2688]{1,0:T(4,128)S(1)}, u32[]{:S(2)}, u32[]{:S(2)}) collective-permute-start(f32[4,2688]{1,0:T(4,128)S(1)} %add.5.refs_0_), channel_id=1, source_target_pairs={{0,3},{1,2},{2,1},{3,0},{4,7},{5,6},{6,5},{7,4},{8,11},{9,10},{10,... | collective-permute-start | bytes 129032 | tf_op jit(solution)/shard_map/ppermute | solution.py:72
  49.8 5.8 %collective-permute-start.16 = (f32[4,2688]{1,0:T(4,128)S(1)}, f32[4,2688]{1,0:T(4,128)S(1)}, u32[]{:S(2)}, u32[]{:S(2)}) collective-permute-start(f32[4,2688]{1,0:T(4,128)S(1)} %add.5.refs_0_), channel_id=1, source_target_pairs={{0,2},{1,3},{2,0},{3,1},{4,6},{5,7},{6,4},{7,5},{8,10},{9,11},{10,... | collective-permute-start | bytes 129032 | tf_op jit(solution)/shard_map/ppermute | solution.py:72
  51.7 4.5 %collective-permute-start.15 = (f32[4,2688]{1,0:T(4,128)S(1)}, f32[4,2688]{1,0:T(4,128)S(1)}, u32[]{:S(2)}, u32[]{:S(2)}) collective-permute-start(f32[4,2688]{1,0:T(4,128)S(1)} %add.5.refs_0_), channel_id=1, source_target_pairs={{0,1},{1,0},{2,3},{3,2},{4,5},{5,4},{6,7},{7,6},{8,9},{9,8},{10,11... | collective-permute-start | bytes 129032 | tf_op jit(solution)/shard_map/ppermute | solution.py:72
  56.3 1.8 %collective-permute-start.18 = (f32[4,2688]{1,0:T(4,128)S(1)}, f32[4,2688]{1,0:T(4,128)S(1)}, u32[]{:S(2)}, u32[]{:S(2)}) collective-permute-start(f32[4,2688]{1,0:T(4,128)S(1)} %join.1.mine_ref), channel_id=1, source_target_pairs={{0,4},{4,0},{8,12},{12,8},{16,20},{20,16},{24,28},{28,24},{1,5},{5... | collective-permute-start | bytes 129032 | tf_op jit(solution)/shard_map/ppermute | solution.py:72
  56.4 7.6 %collective-permute-start.19 = (bf16[1,64,1536]{2,1,0:T(8,128)(2,1)S(1)}, bf16[1,64,1536]{2,1,0:T(8,128)(2,1)S(1)}, u32[]{:S(2)}, u32[]{:S(2)}) collective-permute-start(bf16[1,64,1536]{2,1,0:T(8,128)(2,1)S(1)} %get-tuple-element.69), channel_id=1, source_target_pairs={{0,2},{2,3},{3,1},{1,0},{4,6},{6,7},{7,5},{5,4},{8,10},{10,11},{11... | collective-permute-start | bytes 589832 | tf_op jit(solution)/shard_map/ppermute | solution.py:62

commit v20 on v19

--- a/solution.py
+++ b/solution.py
@@ -322,10 +322,10 @@
     rebuilt_hbm, error_hbm = outs[:2]
     rows = e_ref.shape[1]
     wide = 256
-    strips, sides, _ = sems.shape
-    strips -= 1
+    strips = sems.shape[0] - 1
     high = rows // strips
-    side = part // sides
+    tiles = part // wide
+    group = -(-tiles // sems.shape[1])
     copies = []
     if last:
         copies.append(pltpu.make_async_copy(refs[len(bases)], outs[2], sems.at[strips, 0, 0]))
@@ -344,15 +344,19 @@
             rebuilt = dot(left_ref[here, :], right_ref[:, there], (1, 0))
             rebuilt_v[here, cols] = rebuilt.astype(BF16)
             error_v[here, cols] = (matrix - rebuilt).astype(BF16)
-            if (c + 1) * wide % side == 0:
-                k = c * wide // side
-                strip = pl.ds(r * high, high)
-                near = rebuilt_v.at[strip, pl.ds(k * side, side)]
-                far = rebuilt_hbm.at[strip, pl.ds(at + k * side, side)]
-                copies.append(pltpu.make_async_copy(near, far, sems.at[r, k, 0]))
-                near = error_v.at[strip, pl.ds(k * side, side)]
-                far = error_hbm.at[0, strip, pl.ds(at + k * side, side)]
-                copies.append(pltpu.make_async_copy(near, far, sems.at[r, k, 1]))
+            if (c + 1) % group == 0 or c + 1 == tiles:
+                k = c // group
+                size = (c + 1 - k * group) * wide
+                strip, span = pl.ds(r * high, high), pl.ds(k * group * wide, size)
+                far = pl.ds(at + k * group * wide, size)
+                copies += [
+                    pltpu.make_async_copy(
+                        rebuilt_v.at[strip, span], rebuilt_hbm.at[strip, far], sems.at[r, k, 0]
+                    ),
+                    pltpu.make_async_copy(
+                        error_v.at[strip, span], error_hbm.at[0, strip, far], sems.at[r, k, 1]
+                    ),
+                ]
                 copies[-2].start()
                 copies[-1].start()
     for copy in copies:
@@ -468,9 +472,10 @@
 
     for group in groups(m // 2):
         total = add(*terms_of(total, "dp", m, [2 * bit for bit in group]))
-    newest[0], total = after(newest[0], total)
     for group in groups(n):
         parts = terms_of(total, "tensor", n, group)
+        if group == groups(n)[-1]:
+            newest[0], parts[1:] = after(newest[0], parts[1:])
         total = call(
             functools.partial(join_kernel, rank), sds(total.shape, F32), [], "join"
         )(*parts)
@@ -516,7 +521,7 @@
             out_shape=[sds((rows, width), BF16), sds((1, rows, width), BF16)]
             + [sds((rank, width), F32)] * last,
             input_output_aliases={len(inputs) + k: k for k in range(len(outs))},
-            scratch_shapes=[pltpu.VMEM((rows, part), BF16)] * 2 + [dma((4, 2, 2))],
+            scratch_shapes=[pltpu.VMEM((rows, part), BF16)] * 2 + [dma((4, 4 if part > half else 3, 2))],
             compiler_params=params(16),
             cost_estimate=cost(REBUILD),
             name="rebuild",

time: 66.8 us -> 66 us (0.988)
  waiting for transfers between devices: 24 us -> 22.5 us
  starting transfers between devices: 24.6 us -> 25.4 us
    ppermute x5, waiting for transfers between devices: 6.17 us -> 4.2 us  [ring_step(): lax.ppermute(x, axis, [(ring[p], ring[(p + 1) % n]) for p in range(n)])]
    ppermute x5, starting transfers between devices: 9.33 us -> 10.1 us  [ring_step(): lax.ppermute(x, axis, [(ring[p], ring[(p + 1) % n]) for p in range(n)])]
  transfers between devices with their start and end apart: 20 -> 20, of which waited for: 15 -> 13; matrix products, arithmetic and copies ran while one was open for 0% -> 0% of each run, Pallas kernels for 21% -> 22%
where the time goes in v20:
time: 66 us; the launch traced here: 65.8 us
  starting transfers between devices  25.4 us (38%)
  waiting for transfers between devices  22.5 us (34%)
  Pallas kernels  17.1 us (26%)
  between operations  0.78 us (1%)
    ppermute x12, starting transfers between devices, swap(): return lax.ppermute(x, axis, [(i, i ^ bit) for i in range(n)])  11.7 us
    ppermute x12, waiting for transfers between devices, swap(): return lax.ppermute(x, axis, [(i, i ^ bit) for i in range(n)])  11.3 us
    ppermute x5, starting transfers between devices, ring_step(): lax.ppermute(x, axis, [(ring[p], ring[(p + 1) % n]) for p in range(n)])  10.1 us
    pallas_call x2, Pallas kernels, per_device(): pl.pallas_call(functools.partial(final_kernel, at, part, bases, last), in...  7.45 us
    ppermute x3, waiting for transfers between devices, exchange(): lax.ppermute(pieces[k], axis, [(i, (i + k) % n) for i in range(n)])  6.99 us
    ppermute x5, waiting for transfers between devices, ring_step(): lax.ppermute(x, axis, [(ring[p], ring[(p + 1) % n]) for p in range(n)])  4.2 us
    pallas_call x1, Pallas kernels, per_device(): call(error_left_kernel, [sds((rank, rows), F32), sds((1, rows, width), BF...  4.19 us
    ppermute x3, starting transfers between devices, exchange(): lax.ppermute(pieces[k], axis, [(i, (i + k) % n) for i in range(n)])  3.65 us
  transfers between devices with their start and end apart: 20, of which 13 were waited for; matrix products, arithmetic and copies ran while one was open for 0% of the time, Pallas kernels for 22%

profile of v20, /device:TPU:0, one launch (start us, length us, event | category | flops | bytes accessed | tf_op | source)
XLA Modules:
  0.0 65.8 jit_solution(14246303520686720596)
XLA Ops:
  0.6 4.1 %collective-permute-start = (bf16[1,64,5120]{2,1,0:T(8,128)(2,1)}, bf16[1,64,5120]{2,1,0:T(8,128)(2,1)S(1)}, u32[]{:S(2)}, u32[]{:S(2)}) collective-permute-start(bf16[1,64,5120]{2,1,0:T(8,128)(2,1)} %refs_0_.5), channel_id=1, source_target_pairs={{0,2},{2,3},{3,1},{1,0},{4,6},{6,7},{7,5},{5,4},{8,10},{10,11},{11... | collective-permute-start | bytes 1966088 | tf_op jit(solution)/shard_map/ppermute | solution.py:62
  4.7 1.5 %token_factor.1 = (f32[8,128]{1,0:T(8,128)S(1)}, bf16[12,5120]{1,0:T(8,128)(2,1)S(1)}) custom-call(f32[4,5120]{1,0:T(4,128)} %bitcast.2, bf16[1,64,5120]{2,1,0:T(8,128)(2,1)} %refs_0_.5), custom_call_target="tpu_custom_call" | custom-call | flops 1 | bytes 1 | tf_op jit(solution)/shard_map/token_factor/pallas_call | solution.py:406
  6.2 4.2 %error_left.1 = (f32[4,768]{1,0:T(4,128)S(1)}, bf16[1,768,5120]{2,1,0:T(8,128)(2,1)S(1)}) custom-call(bf16[12,5120]{1,0:T(8,128)(2,1)S(1)} %get-tuple-element.43.terms_ref, bf16[1,768,5120]{2,1,0:T(8,128)(2,1)} %e_hbm.1), custom_call_target="tpu_custom_call" | custom-call | flops 4600000000 | bytes 1 | tf_op jit(solution)/shard_map/error_left/pallas_call | solution.py:417
  10.4 1.4 %collective-permute-start.3 = (f32[8,128]{1,0:T(8,128)S(1)}, f32[8,128]{1,0:T(8,128)S(1)}, u32[]{:S(2)}, u32[]{:S(2)}) collective-permute-start(f32[8,128]{1,0:T(8,128)S(1)} %get-tuple-element.47.refs_0_), channel_id=1, source_target_pairs={{0,3},{1,0},{2,1},{3,2},{4,7},{5,4},{6,5},{7,6},{8,11},{9,8},{10,9... | collective-permute-start | bytes 12296 | tf_op jit(solution)/shard_map/ppermute | solution.py:67
  12.1 1.9 %collective-permute-start.1 = (f32[8,128]{1,0:T(8,128)S(1)}, f32[8,128]{1,0:T(8,128)S(1)}, u32[]{:S(2)}, u32[]{:S(2)}) collective-permute-start(f32[8,128]{1,0:T(8,128)S(1)} %get-tuple-element.47.refs_0_), channel_id=1, source_target_pairs={{0,1},{1,2},{2,3},{3,0},{4,5},{5,6},{6,7},{7,4},{8,9},{9,10},{10,1... | collective-permute-start | bytes 12296 | tf_op jit(solution)/shard_map/ppermute | solution.py:67
  14.1 5.1 %collective-permute-done.3.refs_3_ = f32[8,128]{1,0:T(8,128)S(1)} collective-permute-done((f32[8,128]{1,0:T(8,128)S(1)}, f32[8,128]{1,0:T(8,128)S(1)}, u32[]{:S(2)}, u32[]{:S(2)}) %collective-permute-start.3) | collective-permute-done | bytes 4128 | tf_op jit(solution)/shard_map/ppermute | solution.py:67
  19.2 1.9 %collective-permute-done.2.refs_2_ = f32[8,128]{1,0:T(8,128)S(1)} collective-permute-done((f32[8,128]{1,0:T(8,128)S(1)}, f32[8,128]{1,0:T(8,128)S(1)}, u32[]{:S(2)}, u32[]{:S(2)}) %collective-permute-start.2) | collective-permute-done | bytes 4128 | tf_op jit(solution)/shard_map/ppermute | solution.py:67
  21.1 1.6 %collective-permute-start.8 = (bf16[1,64,5120]{2,1,0:T(8,128)(2,1)S(1)}, bf16[1,64,5120]{2,1,0:T(8,128)(2,1)S(1)}, u32[]{:S(2)}, u32[]{:S(2)}) collective-permute-start(bf16[1,64,5120]{2,1,0:T(8,128)(2,1)S(1)} %collective-permute-done.refs_1_), channel_id=1, source_target_pairs={{0,2},{2,3},{3,1},{1,0},{4,6},{6,7},{7,5},{5,4},{8,10},{10,11},{11... | collective-permute-start | bytes 1966088 | tf_op jit(solution)/shard_map/ppermute | solution.py:62
  22.9 1.2 %collective-permute-done.4.refs_1_ = f32[4,768]{1,0:T(4,128)S(1)} collective-permute-done((f32[4,768]{1,0:T(4,128)S(1)}, f32[4,768]{1,0:T(4,128)S(1)}, u32[]{:S(2)}, u32[]{:S(2)}) %collective-permute-start.4) | collective-permute-done | bytes 12320 | tf_op jit(solution)/shard_map/ppermute | solution.py:72
  24.1 2.4 %collective-permute-start.7 = (f32[4,768]{1,0:T(4,128)S(1)}, f32[4,768]{1,0:T(4,128)S(1)}, u32[]{:S(2)}, u32[]{:S(2)}) collective-permute-start(f32[4,768]{1,0:T(4,128)S(1)} %add.3.refs_0_), channel_id=1, source_target_pairs={{0,24},{4,28},{8,16},{12,20},{16,8},{20,12},{24,0},{28,4},{1,25},{... | collective-permute-start | bytes 36872 | tf_op jit(solution)/shard_map/ppermute | solution.py:72
  28.7 1.5 %collective-permute-done.6.refs_2_ = f32[4,768]{1,0:T(4,128)S(1)} collective-permute-done((f32[4,768]{1,0:T(4,128)S(1)}, f32[4,768]{1,0:T(4,128)S(1)}, u32[]{:S(2)}, u32[]{:S(2)}) %collective-permute-start.6) | collective-permute-done | bytes 12320 | tf_op jit(solution)/shard_map/ppermute | solution.py:72
  31.1 1.4 %collective-permute-start.9 = (f32[8,128]{1,0:T(8,128)S(1)}, f32[8,128]{1,0:T(8,128)S(1)}, u32[]{:S(2)}, u32[]{:S(2)}) collective-permute-start(f32[8,128]{1,0:T(8,128)S(1)} %get-tuple-element.53), channel_id=1, source_target_pairs={{0,2},{2,3},{3,1},{1,0},{4,6},{6,7},{7,5},{5,4},{8,10},{10,11},{11... | collective-permute-start | bytes 12296 | tf_op jit(solution)/shard_map/ppermute | solution.py:62
  33.7 4.2 %collective-permute-done.9.got_ref = f32[8,128]{1,0:T(8,128)S(1)} collective-permute-done((f32[8,128]{1,0:T(8,128)S(1)}, f32[8,128]{1,0:T(8,128)S(1)}, u32[]{:S(2)}, u32[]{:S(2)}) %collective-permute-start.9) | collective-permute-done | bytes 4128 | tf_op jit(solution)/shard_map/ppermute | solution.py:62
  38.0 1.3 %collective-permute-start.14 = (bf16[1,64,3584]{2,1,0:T(8,128)(2,1)S(1)}, bf16[1,64,3584]{2,1,0:T(8,128)(2,1)S(1)}, u32[]{:S(2)}, u32[]{:S(2)}) collective-permute-start(bf16[1,64,3584]{2,1,0:T(8,128)(2,1)S(1)} %get-tuple-element.64), channel_id=1, source_target_pairs={{0,2},{2,3},{3,1},{1,0},{4,6},{6,7},{7,5},{5,4},{8,10},{10,11},{11... | collective-permute-start | bytes 1376264 | tf_op jit(solution)/shard_map/ppermute | solution.py:62
  39.9 1.2 %collective-permute-done.10.refs_1_ = f32[4,2688]{1,0:T(4,128)S(1)} collective-permute-done((f32[4,2688]{1,0:T(4,128)S(1)}, f32[4,2688]{1,0:T(4,128)S(1)}, u32[]{:S(2)}, u32[]{:S(2)}) %collective-permute-start.10) | collective-permute-done | bytes 43040 | tf_op jit(solution)/shard_map/ppermute | solution.py:72
  41.1 2.5 %collective-permute-start.13 = (f32[4,2688]{1,0:T(4,128)S(1)}, f32[4,2688]{1,0:T(4,128)S(1)}, u32[]{:S(2)}, u32[]{:S(2)}) collective-permute-start(f32[4,2688]{1,0:T(4,128)S(1)} %add.4.refs_0_), channel_id=1, source_target_pairs={{0,24},{4,28},{8,16},{12,20},{16,8},{20,12},{24,0},{28,4},{1,25},{... | collective-permute-start | bytes 129032 | tf_op jit(solution)/shard_map/ppermute | solution.py:72
  44.7 1.4 %collective-permute-done.13.refs_3_ = f32[4,2688]{1,0:T(4,128)S(1)} collective-permute-done((f32[4,2688]{1,0:T(4,128)S(1)}, f32[4,2688]{1,0:T(4,128)S(1)}, u32[]{:S(2)}, u32[]{:S(2)}) %collective-permute-start.13) | collective-permute-done | bytes 43040 | tf_op jit(solution)/shard_map/ppermute | solution.py:72
  46.1 1.5 %collective-permute-done.12.refs_2_ = f32[4,2688]{1,0:T(4,128)S(1)} collective-permute-done((f32[4,2688]{1,0:T(4,128)S(1)}, f32[4,2688]{1,0:T(4,128)S(1)}, u32[]{:S(2)}, u32[]{:S(2)}) %collective-permute-start.12) | collective-permute-done | bytes 43040 | tf_op jit(solution)/shard_map/ppermute | solution.py:72
  48.2 1.6 %collective-permute-start.17 = (f32[4,2688]{1,0:T(4,128)S(1)}, f32[4,2688]{1,0:T(4,128)S(1)}, u32[]{:S(2)}, u32[]{:S(2)}) collective-permute-start(f32[4,2688]{1,0:T(4,128)S(1)} %add.5.refs_0_), channel_id=1, source_target_pairs={{0,3},{1,2},{2,1},{3,0},{4,7},{5,6},{6,5},{7,4},{8,11},{9,10},{10,... | collective-permute-start | bytes 129032 | tf_op jit(solution)/shard_map/ppermute | solution.py:72
  50.5 2.1 %collective-permute-start.15 = (f32[4,2688]{1,0:T(4,128)S(1)}, f32[4,2688]{1,0:T(4,128)S(1)}, u32[]{:S(2)}, u32[]{:S(2)}) collective-permute-start(f32[4,2688]{1,0:T(4,128)S(1)} %add.5.refs_0_), channel_id=1, source_target_pairs={{0,1},{1,0},{2,3},{3,2},{4,5},{5,4},{6,7},{7,6},{8,9},{9,8},{10,11... | collective-permute-start | bytes 129032 | tf_op jit(solution)/shard_map/ppermute | solution.py:72
  52.8 1.3 %collective-permute-done.17.refs_3_ = f32[4,2688]{1,0:T(4,128)S(1)} collective-permute-done((f32[4,2688]{1,0:T(4,128)S(1)}, f32[4,2688]{1,0:T(4,128)S(1)}, u32[]{:S(2)}, u32[]{:S(2)}) %collective-permute-start.17) | collective-permute-done | bytes 43040 | tf_op jit(solution)/shard_map/ppermute | solution.py:72
  55.3 1.7 %collective-permute-start.19 = (bf16[1,64,1536]{2,1,0:T(8,128)(2,1)S(1)}, bf16[1,64,1536]{2,1,0:T(8,128)(2,1)S(1)}, u32[]{:S(2)}, u32[]{:S(2)}) collective-permute-start(bf16[1,64,1536]{2,1,0:T(8,128)(2,1)S(1)} %get-tuple-element.73), channel_id=1, source_target_pairs={{0,2},{2,3},{3,1},{1,0},{4,6},{6,7},{7,5},{5,4},{8,10},{10,11},{11... | collective-permute-start | bytes 589832 | tf_op jit(solution)/shard_map/ppermute | solution.py:62
  58.3 4.8 %rebuild.2 = (bf16[768,5120]{1,0:T(8,128)(2,1)}, bf16[1,768,5120]{2,1,0:T(8,128)(2,1)}) custom-call(bf16[768,256]{1,0:T(8,128)(2,1)S(1)} %acts.1.acts_ref, bf16[768,24]{1,0:T(8,128)(2,1)S(1)} %get-tuple-element.69.left_ref, bf16[24,5120]{1,0:T(8,128)(2,1)S(1)} %get-tuple-element.72.right_ref, bf16[1,768,5120]{2,1,0:T(8,128)(2,1)S(1)} %get-tuple-element.55.e_ref, ...), custom_call_target="tpu_custom_call" | custom-call | flops 4000000000 | bytes 1 | tf_op jit(solution)/shard_map/rebuild/pallas_call | solution.py:517
  63.1 2.7 %rebuild.3 = (bf16[768,5120]{1,0:T(8,128)(2,1)}, bf16[1,768,5120]{2,1,0:T(8,128)(2,1)}, f32[4,5120]{1,0:T(4,128)}) custom-call(bf16[768,256]{1,0:T(8,128)(2,1)S(1)} %acts.1.acts_ref, bf16[768,24]{1,0:T(8,128)(2,1)S(1)} %get-tuple-element.69.left_ref, ...), custom_call_target="tpu_custom_call", output_to_operand_aliasing={{0}: (9, {}), {1}: (10, {})} | custom-call | flops 4000000000 | bytes 1 | tf_op jit(solution)/shard_map/rebuild/pallas_call | solution.py:517
  (36 shorter events, 10.5 us)
Async XLA Ops:
  0.6 20.5 %collective-permute-start = (bf16[1,64,5120]{2,1,0:T(8,128)(2,1)}, bf16[1,64,5120]{2,1,0:T(8,128)(2,1)S(1)}, u32[]{:S(2)}, u32[]{:S(2)}) collective-permute-start(bf16[1,64,5120]{2,1,0:T(8,128)(2,1)} %refs_0_.5), channel_id=1, source_target_pairs={{0,2},{2,3},{3,1},{1,0},{4,6},{6,7},{7,5},{5,4},{8,10},{10,11},{11... | collective-permute-start | bytes 1966088 | tf_op jit(solution)/shard_map/ppermute | solution.py:62
  6.2 16.5 %copy-start.1 = (bf16[1,256,768]{2,1,0:T(8,128)(2,1)S(1)}, bf16[1,256,768]{2,1,0:T(8,128)(2,1)}, u32[]{:S(2)}) copy-start(bf16[1,256,768]{2,1,0:T(8,128)(2,1)} %a_ref.5) | copy-start | bytes 1179652
  10.4 28.9 %copy-start = (bf16[1,64,5120]{2,1,0:T(8,128)(2,1)S(1)}, bf16[1,64,5120]{2,1,0:T(8,128)(2,1)}, u32[]{:S(2)}) copy-start(bf16[1,64,5120]{2,1,0:T(8,128)(2,1)} %refs_0_.5) | copy-start | bytes 1966084
  10.4 8.8 %collective-permute-start.3 = (f32[8,128]{1,0:T(8,128)S(1)}, f32[8,128]{1,0:T(8,128)S(1)}, u32[]{:S(2)}, u32[]{:S(2)}) collective-permute-start(f32[8,128]{1,0:T(8,128)S(1)} %get-tuple-element.47.refs_0_), channel_id=1, source_target_pairs={{0,3},{1,0},{2,1},{3,2},{4,7},{5,4},{6,5},{7,6},{8,11},{9,8},{10,9... | collective-permute-start | bytes 12296 | tf_op jit(solution)/shard_map/ppermute | solution.py:67
  11.8 9.2 %collective-permute-start.2 = (f32[8,128]{1,0:T(8,128)S(1)}, f32[8,128]{1,0:T(8,128)S(1)}, u32[]{:S(2)}, u32[]{:S(2)}) collective-permute-start(f32[8,128]{1,0:T(8,128)S(1)} %get-tuple-element.47.refs_0_), channel_id=1, source_target_pairs={{0,2},{1,3},{2,0},{3,1},{4,6},{5,7},{6,4},{7,5},{8,10},{9,11},{10,... | collective-permute-start | bytes 12296 | tf_op jit(solution)/shard_map/ppermute | solution.py:67
  12.1 8.9 %collective-permute-start.1 = (f32[8,128]{1,0:T(8,128)S(1)}, f32[8,128]{1,0:T(8,128)S(1)}, u32[]{:S(2)}, u32[]{:S(2)}) collective-permute-start(f32[8,128]{1,0:T(8,128)S(1)} %get-tuple-element.47.refs_0_), channel_id=1, source_target_pairs={{0,1},{1,2},{2,3},{3,0},{4,5},{5,6},{6,7},{7,4},{8,9},{9,10},{10,1... | collective-permute-start | bytes 12296 | tf_op jit(solution)/shard_map/ppermute | solution.py:67
  21.1 16.8 %collective-permute-start.8 = (bf16[1,64,5120]{2,1,0:T(8,128)(2,1)S(1)}, bf16[1,64,5120]{2,1,0:T(8,128)(2,1)S(1)}, u32[]{:S(2)}, u32[]{:S(2)}) collective-permute-start(bf16[1,64,5120]{2,1,0:T(8,128)(2,1)S(1)} %collective-permute-done.refs_1_), channel_id=1, source_target_pairs={{0,2},{2,3},{3,1},{1,0},{4,6},{6,7},{7,5},{5,4},{8,10},{10,11},{11... | collective-permute-start | bytes 1966088 | tf_op jit(solution)/shard_map/ppermute | solution.py:62
  22.9 1.2 %collective-permute-start.4 = (f32[4,768]{1,0:T(4,128)S(1)}, f32[4,768]{1,0:T(4,128)S(1)}, u32[]{:S(2)}, u32[]{:S(2)}) collective-permute-start(f32[4,768]{1,0:T(4,128)S(1)} %left.1.refs_0_), channel_id=1, source_target_pairs={{0,4},{4,0},{8,12},{12,8},{16,20},{20,16},{24,28},{28,24},{1,5},{5... | collective-permute-start | bytes 36872 | tf_op jit(solution)/shard_map/ppermute | solution.py:72
  24.1 4.6 %collective-permute-start.7 = (f32[4,768]{1,0:T(4,128)S(1)}, f32[4,768]{1,0:T(4,128)S(1)}, u32[]{:S(2)}, u32[]{:S(2)}) collective-permute-start(f32[4,768]{1,0:T(4,128)S(1)} %add.3.refs_0_), channel_id=1, source_target_pairs={{0,24},{4,28},{8,16},{12,20},{16,8},{20,12},{24,0},{28,4},{1,25},{... | collective-permute-start | bytes 36872 | tf_op jit(solution)/shard_map/ppermute | solution.py:72
  26.6 3.7 %collective-permute-start.6 = (f32[4,768]{1,0:T(4,128)S(1)}, f32[4,768]{1,0:T(4,128)S(1)}, u32[]{:S(2)}, u32[]{:S(2)}) collective-permute-start(f32[4,768]{1,0:T(4,128)S(1)} %add.3.refs_0_), channel_id=1, source_target_pairs={{0,16},{4,20},{8,24},{12,28},{16,0},{20,4},{24,8},{28,12},{1,17},{... | collective-permute-start | bytes 36872 | tf_op jit(solution)/shard_map/ppermute | solution.py:72
  27.1 3.7 %collective-permute-start.5 = (f32[4,768]{1,0:T(4,128)S(1)}, f32[4,768]{1,0:T(4,128)S(1)}, u32[]{:S(2)}, u32[]{:S(2)}) collective-permute-start(f32[4,768]{1,0:T(4,128)S(1)} %add.3.refs_0_), channel_id=1, source_target_pairs={{0,8},{4,12},{8,0},{12,4},{16,24},{20,28},{24,16},{28,20},{1,9},{5... | collective-permute-start | bytes 36872 | tf_op jit(solution)/shard_map/ppermute | solution.py:72
  31.1 6.8 %collective-permute-start.9 = (f32[8,128]{1,0:T(8,128)S(1)}, f32[8,128]{1,0:T(8,128)S(1)}, u32[]{:S(2)}, u32[]{:S(2)}) collective-permute-start(f32[8,128]{1,0:T(8,128)S(1)} %get-tuple-element.53), channel_id=1, source_target_pairs={{0,2},{2,3},{3,1},{1,0},{4,6},{6,7},{7,5},{5,4},{8,10},{10,11},{11... | collective-permute-start | bytes 12296 | tf_op jit(solution)/shard_map/ppermute | solution.py:62
  38.0 17.1 %collective-permute-start.14 = (bf16[1,64,3584]{2,1,0:T(8,128)(2,1)S(1)}, bf16[1,64,3584]{2,1,0:T(8,128)(2,1)S(1)}, u32[]{:S(2)}, u32[]{:S(2)}) collective-permute-start(bf16[1,64,3584]{2,1,0:T(8,128)(2,1)S(1)} %get-tuple-element.64), channel_id=1, source_target_pairs={{0,2},{2,3},{3,1},{1,0},{4,6},{6,7},{7,5},{5,4},{8,10},{10,11},{11... | collective-permute-start | bytes 1376264 | tf_op jit(solution)/shard_map/ppermute | solution.py:62
  39.8 1.3 %collective-permute-start.10 = (f32[4,2688]{1,0:T(4,128)S(1)}, f32[4,2688]{1,0:T(4,128)S(1)}, u32[]{:S(2)}, u32[]{:S(2)}) collective-permute-start(f32[4,2688]{1,0:T(4,128)S(1)} %get-tuple-element.63), channel_id=1, source_target_pairs={{0,4},{4,0},{8,12},{12,8},{16,20},{20,16},{24,28},{28,24},{1,5},{5... | collective-permute-start | bytes 129032 | tf_op jit(solution)/shard_map/ppermute | solution.py:72
  41.1 5.0 %collective-permute-start.13 = (f32[4,2688]{1,0:T(4,128)S(1)}, f32[4,2688]{1,0:T(4,128)S(1)}, u32[]{:S(2)}, u32[]{:S(2)}) collective-permute-start(f32[4,2688]{1,0:T(4,128)S(1)} %add.4.refs_0_), channel_id=1, source_target_pairs={{0,24},{4,28},{8,16},{12,20},{16,8},{20,12},{24,0},{28,4},{1,25},{... | collective-permute-start | bytes 129032 | tf_op jit(solution)/shard_map/ppermute | solution.py:72
  43.6 4.0 %collective-permute-start.12 = (f32[4,2688]{1,0:T(4,128)S(1)}, f32[4,2688]{1,0:T(4,128)S(1)}, u32[]{:S(2)}, u32[]{:S(2)}) collective-permute-start(f32[4,2688]{1,0:T(4,128)S(1)} %add.4.refs_0_), channel_id=1, source_target_pairs={{0,16},{4,20},{8,24},{12,28},{16,0},{20,4},{24,8},{28,12},{1,17},{... | collective-permute-start | bytes 129032 | tf_op jit(solution)/shard_map/ppermute | solution.py:72
  44.2 4.0 %collective-permute-start.11 = (f32[4,2688]{1,0:T(4,128)S(1)}, f32[4,2688]{1,0:T(4,128)S(1)}, u32[]{:S(2)}, u32[]{:S(2)}) collective-permute-start(f32[4,2688]{1,0:T(4,128)S(1)} %add.4.refs_0_), channel_id=1, source_target_pairs={{0,8},{4,12},{8,0},{12,4},{16,24},{20,28},{24,16},{28,20},{1,9},{5... | collective-permute-start | bytes 129032 | tf_op jit(solution)/shard_map/ppermute | solution.py:72
  48.2 5.9 %collective-permute-start.17 = (f32[4,2688]{1,0:T(4,128)S(1)}, f32[4,2688]{1,0:T(4,128)S(1)}, u32[]{:S(2)}, u32[]{:S(2)}) collective-permute-start(f32[4,2688]{1,0:T(4,128)S(1)} %add.5.refs_0_), channel_id=1, source_target_pairs={{0,3},{1,2},{2,1},{3,0},{4,7},{5,6},{6,5},{7,4},{8,11},{9,10},{10,... | collective-permute-start | bytes 129032 | tf_op jit(solution)/shard_map/ppermute | solution.py:72
  49.8 5.3 %collective-permute-start.16 = (f32[4,2688]{1,0:T(4,128)S(1)}, f32[4,2688]{1,0:T(4,128)S(1)}, u32[]{:S(2)}, u32[]{:S(2)}) collective-permute-start(f32[4,2688]{1,0:T(4,128)S(1)} %add.5.refs_0_), channel_id=1, source_target_pairs={{0,2},{1,3},{2,0},{3,1},{4,6},{5,7},{6,4},{7,5},{8,10},{9,11},{10,... | collective-permute-start | bytes 129032 | tf_op jit(solution)/shard_map/ppermute | solution.py:72
  50.5 4.6 %collective-permute-start.15 = (f32[4,2688]{1,0:T(4,128)S(1)}, f32[4,2688]{1,0:T(4,128)S(1)}, u32[]{:S(2)}, u32[]{:S(2)}) collective-permute-start(f32[4,2688]{1,0:T(4,128)S(1)} %add.5.refs_0_), channel_id=1, source_target_pairs={{0,1},{1,0},{2,3},{3,2},{4,5},{5,4},{6,7},{7,6},{8,9},{9,8},{10,11... | collective-permute-start | bytes 129032 | tf_op jit(solution)/shard_map/ppermute | solution.py:72
  55.3 2.5 %collective-permute-start.18 = (f32[4,2688]{1,0:T(4,128)S(1)}, f32[4,2688]{1,0:T(4,128)S(1)}, u32[]{:S(2)}, u32[]{:S(2)}) collective-permute-start(f32[4,2688]{1,0:T(4,128)S(1)} %join.1.mine_ref), channel_id=1, source_target_pairs={{0,4},{4,0},{8,12},{12,8},{16,20},{20,16},{24,28},{28,24},{1,5},{5... | collective-permute-start | bytes 129032 | tf_op jit(solution)/shard_map/ppermute | solution.py:72
  55.3 7.8 %collective-permute-start.19 = (bf16[1,64,1536]{2,1,0:T(8,128)(2,1)S(1)}, bf16[1,64,1536]{2,1,0:T(8,128)(2,1)S(1)}, u32[]{:S(2)}, u32[]{:S(2)}) collective-permute-start(bf16[1,64,1536]{2,1,0:T(8,128)(2,1)S(1)} %get-tuple-element.73), channel_id=1, source_target_pairs={{0,2},{2,3},{3,1},{1,0},{4,6},{6,7},{7,5},{5,4},{8,10},{10,11},{11... | collective-permute-start | bytes 589832 | tf_op jit(solution)/shard_map/ppermute | solution.py:62

commit v21 on v20

--- a/solution.py
+++ b/solution.py
@@ -12,6 +12,7 @@
 SHRINK = 2.0**-23
 TINY = 1e-30
 REBUILD = 4e9
+RIGHT = 8e9
 ROOM = 2.0**14
 BLOCK = 512
 
@@ -57,9 +58,9 @@
     return jnp.where(2 * place < n, 2 * place, 2 * (n - place) - 1)
 
 
-def ring_step(x, axis, n):
+def ring_step(x, axis, n, by=1):
     ring = ring_of(n)
-    return lax.ppermute(x, axis, [(ring[p], ring[(p + 1) % n]) for p in range(n)])
+    return lax.ppermute(x, axis, [(ring[p], ring[(p + by) % n]) for p in range(n)])
 
 
 def exchange(pieces, axis, n):
@@ -455,9 +456,9 @@
     )(scaled, error_v)
 
     widths = [width * 7 // 10, width * 3 // 10]
-    last, (got, right_raw) = after(ring[-1], (got, right_raw))
-    newest = list(cut(last, widths))
-    newest[0] = step(newest[0])
+    newest = list(cut(out_grads, widths))
+    newest[0], right_raw = after(newest[0], right_raw)
+    newest[0] = ring_step(newest[0], "tensor", n, -1)
 
     keep, send = call(
         right_kernel,
@@ -466,7 +467,7 @@
             pltpu.VMEM((3 * rank, (n - 1) * tok), F32),
             pltpu.VMEM((2, rank, half + 128), F32),
         ],
-        "right",
+        "right", None, RIGHT,
     )(right_raw, held, got, extra, *ring)
     total = add(keep, swap(send, "dp", m, 1))
 
@@ -481,7 +482,7 @@
         )(*parts)
     for c in range(1, len(widths)):
         last, total = after(newest[c], total)
-        newest[c] = step(last)
+        newest[c] = ring_step(last, "tensor", n, -1)
 
     terms = len(LEFT_TERMS) * rank
     other = swap(total, "dp", m, 1)

time: 66 us -> 74.3 us (1.13)
  waiting for transfers between devices: 22.5 us -> 31.1 us
    ppermute x5, waiting for transfers between devices: 4.2 us -> 13.4 us  [ring_step(): lax.ppermute(x, axis, [(ring[p], ring[(p + by) % n]) for p in range(n)])]
  transfers between devices with their start and end apart: 20 -> 20, of which waited for: 13 -> 13; matrix products, arithmetic and copies ran while one was open for 0% -> 0% of each run, Pallas kernels for 22% -> 19%
where the time goes in v21:
time: 74.3 us; the launch traced here: 74.2 us
  waiting for transfers between devices  31.1 us (42%)
  starting transfers between devices  25.1 us (34%)
  Pallas kernels  17.1 us (23%)
  between operations  0.79 us (1%)
    ppermute x5, waiting for transfers between devices, ring_step(): lax.ppermute(x, axis, [(ring[p], ring[(p + by) % n]) for p in range(n)])  13.4 us
    ppermute x12, starting transfers between devices, swap(): return lax.ppermute(x, axis, [(i, i ^ bit) for i in range(n)])  11.7 us
    ppermute x12, waiting for transfers between devices, swap(): return lax.ppermute(x, axis, [(i, i ^ bit) for i in range(n)])  10.7 us
    ppermute x5, starting transfers between devices, ring_step(): lax.ppermute(x, axis, [(ring[p], ring[(p + by) % n]) for p in range(n)])  9.78 us
    pallas_call x2, Pallas kernels, per_device(): pl.pallas_call(functools.partial(final_kernel, at, part, bases, last), in...  7.46 us
    ppermute x3, waiting for transfers between devices, exchange(): lax.ppermute(pieces[k], axis, [(i, (i + k) % n) for i in range(n)])  6.96 us
    pallas_call x1, Pallas kernels, per_device(): call(error_left_kernel, [sds((rank, rows), F32), sds((1, rows, width), BF...  4.23 us
    ppermute x3, starting transfers between devices, exchange(): lax.ppermute(pieces[k], axis, [(i, (i + k) % n) for i in range(n)])  3.65 us
  transfers between devices with their start and end apart: 20, of which 13 were waited for; matrix products, arithmetic and copies ran while one was open for 0% of the time, Pallas kernels for 19%

profile of v21, /device:TPU:0, one launch (start us, length us, event | category | flops | bytes accessed | tf_op | source)
XLA Modules:
  0.0 74.2 jit_solution(17476008513712348178)
XLA Ops:
  0.6 4.1 %collective-permute-start = (bf16[1,64,5120]{2,1,0:T(8,128)(2,1)}, bf16[1,64,5120]{2,1,0:T(8,128)(2,1)S(1)}, u32[]{:S(2)}, u32[]{:S(2)}) collective-permute-start(bf16[1,64,5120]{2,1,0:T(8,128)(2,1)} %refs_0_.5), channel_id=1, source_target_pairs={{0,2},{2,3},{3,1},{1,0},{4,6},{6,7},{7,5},{5,4},{8,10},{10,11},{11... | collective-permute-start | bytes 1966088 | tf_op jit(solution)/shard_map/ppermute | solution.py:63
  4.7 1.5 %token_factor.1 = (f32[8,128]{1,0:T(8,128)S(1)}, bf16[12,5120]{1,0:T(8,128)(2,1)S(1)}) custom-call(f32[4,5120]{1,0:T(4,128)} %bitcast.2, bf16[1,64,5120]{2,1,0:T(8,128)(2,1)} %refs_0_.5), custom_call_target="tpu_custom_call" | custom-call | flops 1 | bytes 1 | tf_op jit(solution)/shard_map/token_factor/pallas_call | solution.py:407
  6.2 4.2 %error_left.1 = (f32[4,768]{1,0:T(4,128)S(1)}, bf16[1,768,5120]{2,1,0:T(8,128)(2,1)S(1)}) custom-call(bf16[12,5120]{1,0:T(8,128)(2,1)S(1)} %get-tuple-element.42.terms_ref, bf16[1,768,5120]{2,1,0:T(8,128)(2,1)} %e_hbm.1), custom_call_target="tpu_custom_call" | custom-call | flops 4600000000 | bytes 1 | tf_op jit(solution)/shard_map/error_left/pallas_call | solution.py:418
  10.5 1.4 %collective-permute-start.3 = (f32[8,128]{1,0:T(8,128)S(1)}, f32[8,128]{1,0:T(8,128)S(1)}, u32[]{:S(2)}, u32[]{:S(2)}) collective-permute-start(f32[8,128]{1,0:T(8,128)S(1)} %get-tuple-element.46.refs_0_), channel_id=1, source_target_pairs={{0,3},{1,0},{2,1},{3,2},{4,7},{5,4},{6,5},{7,6},{8,11},{9,8},{10,9... | collective-permute-start | bytes 12296 | tf_op jit(solution)/shard_map/ppermute | solution.py:68
  12.2 1.9 %collective-permute-start.1 = (f32[8,128]{1,0:T(8,128)S(1)}, f32[8,128]{1,0:T(8,128)S(1)}, u32[]{:S(2)}, u32[]{:S(2)}) collective-permute-start(f32[8,128]{1,0:T(8,128)S(1)} %get-tuple-element.46.refs_0_), channel_id=1, source_target_pairs={{0,1},{1,2},{2,3},{3,0},{4,5},{5,6},{6,7},{7,4},{8,9},{9,10},{10,1... | collective-permute-start | bytes 12296 | tf_op jit(solution)/shard_map/ppermute | solution.py:68
  14.1 5.1 %collective-permute-done.3.refs_3_ = f32[8,128]{1,0:T(8,128)S(1)} collective-permute-done((f32[8,128]{1,0:T(8,128)S(1)}, f32[8,128]{1,0:T(8,128)S(1)}, u32[]{:S(2)}, u32[]{:S(2)}) %collective-permute-start.3) | collective-permute-done | bytes 4128 | tf_op jit(solution)/shard_map/ppermute | solution.py:68
  19.2 1.9 %collective-permute-done.2.refs_2_ = f32[8,128]{1,0:T(8,128)S(1)} collective-permute-done((f32[8,128]{1,0:T(8,128)S(1)}, f32[8,128]{1,0:T(8,128)S(1)}, u32[]{:S(2)}, u32[]{:S(2)}) %collective-permute-start.2) | collective-permute-done | bytes 4128 | tf_op jit(solution)/shard_map/ppermute | solution.py:68
  21.1 1.6 %collective-permute-start.9 = (bf16[1,64,5120]{2,1,0:T(8,128)(2,1)S(1)}, bf16[1,64,5120]{2,1,0:T(8,128)(2,1)S(1)}, u32[]{:S(2)}, u32[]{:S(2)}) collective-permute-start(bf16[1,64,5120]{2,1,0:T(8,128)(2,1)S(1)} %collective-permute-done.refs_1_), channel_id=1, source_target_pairs={{0,2},{2,3},{3,1},{1,0},{4,6},{6,7},{7,5},{5,4},{8,10},{10,11},{11... | collective-permute-start | bytes 1966088 | tf_op jit(solution)/shard_map/ppermute | solution.py:63
  22.9 1.2 %collective-permute-done.4.refs_1_ = f32[4,768]{1,0:T(4,128)S(1)} collective-permute-done((f32[4,768]{1,0:T(4,128)S(1)}, f32[4,768]{1,0:T(4,128)S(1)}, u32[]{:S(2)}, u32[]{:S(2)}) %collective-permute-start.4) | collective-permute-done | bytes 12320 | tf_op jit(solution)/shard_map/ppermute | solution.py:73
  24.1 2.4 %collective-permute-start.7 = (f32[4,768]{1,0:T(4,128)S(1)}, f32[4,768]{1,0:T(4,128)S(1)}, u32[]{:S(2)}, u32[]{:S(2)}) collective-permute-start(f32[4,768]{1,0:T(4,128)S(1)} %add.3.refs_0_), channel_id=1, source_target_pairs={{0,24},{4,28},{8,16},{12,20},{16,8},{20,12},{24,0},{28,4},{1,25},{... | collective-permute-start | bytes 36872 | tf_op jit(solution)/shard_map/ppermute | solution.py:73
  27.7 1.0 %collective-permute-done.7.refs_3_ = f32[4,768]{1,0:T(4,128)S(1)} collective-permute-done((f32[4,768]{1,0:T(4,128)S(1)}, f32[4,768]{1,0:T(4,128)S(1)}, u32[]{:S(2)}, u32[]{:S(2)}) %collective-permute-start.7) | collective-permute-done | bytes 12320 | tf_op jit(solution)/shard_map/ppermute | solution.py:73
  28.7 1.5 %collective-permute-done.6.refs_2_ = f32[4,768]{1,0:T(4,128)S(1)} collective-permute-done((f32[4,768]{1,0:T(4,128)S(1)}, f32[4,768]{1,0:T(4,128)S(1)}, u32[]{:S(2)}, u32[]{:S(2)}) %collective-permute-start.6) | collective-permute-done | bytes 12320 | tf_op jit(solution)/shard_map/ppermute | solution.py:73
  31.1 1.4 %collective-permute-start.8 = (f32[8,128]{1,0:T(8,128)S(1)}, f32[8,128]{1,0:T(8,128)S(1)}, u32[]{:S(2)}, u32[]{:S(2)}) collective-permute-start(f32[8,128]{1,0:T(8,128)S(1)} %get-tuple-element.57), channel_id=1, source_target_pairs={{0,2},{2,3},{3,1},{1,0},{4,6},{6,7},{7,5},{5,4},{8,10},{10,11},{11... | collective-permute-start | bytes 12296 | tf_op jit(solution)/shard_map/ppermute | solution.py:63
  32.6 1.1 %error_right.1.r_ref = f32[4,5120]{1,0:T(4,128)S(1)} custom-call(f32[4,768]{1,0:T(4,128)S(1)} %get-tuple-element.53.p_ref, bf16[1,768,5120]{2,1,0:T(8,128)(2,1)S(1)} %get-tuple-element.54.e_ref), custom_call_target="tpu_custom_call" | custom-call | flops 1200000000 | bytes 1 | tf_op jit(solution)/shard_map/error_right/pallas_call | solution.py:451
  34.3 13.4 %collective-permute-done.8.got_ref = f32[8,128]{1,0:T(8,128)S(1)} collective-permute-done((f32[8,128]{1,0:T(8,128)S(1)}, f32[8,128]{1,0:T(8,128)S(1)}, u32[]{:S(2)}, u32[]{:S(2)}) %collective-permute-start.8) | collective-permute-done | bytes 4128 | tf_op jit(solution)/shard_map/ppermute | solution.py:63
  48.4 1.2 %collective-permute-done.10.refs_1_ = f32[4,2688]{1,0:T(4,128)S(1)} collective-permute-done((f32[4,2688]{1,0:T(4,128)S(1)}, f32[4,2688]{1,0:T(4,128)S(1)}, u32[]{:S(2)}, u32[]{:S(2)}) %collective-permute-start.10) | collective-permute-done | bytes 43040 | tf_op jit(solution)/shard_map/ppermute | solution.py:73
  49.6 2.5 %collective-permute-start.13 = (f32[4,2688]{1,0:T(4,128)S(1)}, f32[4,2688]{1,0:T(4,128)S(1)}, u32[]{:S(2)}, u32[]{:S(2)}) collective-permute-start(f32[4,2688]{1,0:T(4,128)S(1)} %add.4.refs_0_), channel_id=1, source_target_pairs={{0,24},{4,28},{8,16},{12,20},{16,8},{20,12},{24,0},{28,4},{1,25},{... | collective-permute-start | bytes 129032 | tf_op jit(solution)/shard_map/ppermute | solution.py:73
  53.1 1.4 %collective-permute-done.13.refs_3_ = f32[4,2688]{1,0:T(4,128)S(1)} collective-permute-done((f32[4,2688]{1,0:T(4,128)S(1)}, f32[4,2688]{1,0:T(4,128)S(1)}, u32[]{:S(2)}, u32[]{:S(2)}) %collective-permute-start.13) | collective-permute-done | bytes 43040 | tf_op jit(solution)/shard_map/ppermute | solution.py:73
  54.6 1.5 %collective-permute-done.12.refs_2_ = f32[4,2688]{1,0:T(4,128)S(1)} collective-permute-done((f32[4,2688]{1,0:T(4,128)S(1)}, f32[4,2688]{1,0:T(4,128)S(1)}, u32[]{:S(2)}, u32[]{:S(2)}) %collective-permute-start.12) | collective-permute-done | bytes 43040 | tf_op jit(solution)/shard_map/ppermute | solution.py:73
  56.8 4.3 %collective-permute-start.15 = (f32[4,2688]{1,0:T(4,128)S(1)}, f32[4,2688]{1,0:T(4,128)S(1)}, u32[]{:S(2)}, u32[]{:S(2)}) collective-permute-start(f32[4,2688]{1,0:T(4,128)S(1)} %add.5.refs_0_), channel_id=1, source_target_pairs={{0,1},{1,0},{2,3},{3,2},{4,5},{5,4},{6,7},{7,6},{8,9},{9,8},{10,11... | collective-permute-start | bytes 129032 | tf_op jit(solution)/shard_map/ppermute | solution.py:73
  61.3 1.3 %collective-permute-done.17.refs_3_ = f32[4,2688]{1,0:T(4,128)S(1)} collective-permute-done((f32[4,2688]{1,0:T(4,128)S(1)}, f32[4,2688]{1,0:T(4,128)S(1)}, u32[]{:S(2)}, u32[]{:S(2)}) %collective-permute-start.17) | collective-permute-done | bytes 43040 | tf_op jit(solution)/shard_map/ppermute | solution.py:73
  63.3 2.1 %collective-permute-start.19 = (bf16[1,64,1536]{2,1,0:T(8,128)(2,1)S(1)}, bf16[1,64,1536]{2,1,0:T(8,128)(2,1)S(1)}, u32[]{:S(2)}, u32[]{:S(2)}) collective-permute-start(bf16[1,64,1536]{2,1,0:T(8,128)(2,1)S(1)} %get-tuple-element.71), channel_id=1, source_target_pairs={{0,1},{2,0},{3,2},{1,3},{4,5},{6,4},{7,6},{5,7},{8,9},{10,8},{11,1... | collective-permute-start | bytes 589832 | tf_op jit(solution)/shard_map/ppermute | solution.py:63
  66.7 4.8 %rebuild.2 = (bf16[768,5120]{1,0:T(8,128)(2,1)}, bf16[1,768,5120]{2,1,0:T(8,128)(2,1)}) custom-call(bf16[768,256]{1,0:T(8,128)(2,1)S(1)} %acts.1.acts_ref, bf16[768,24]{1,0:T(8,128)(2,1)S(1)} %get-tuple-element.67.left_ref, bf16[24,5120]{1,0:T(8,128)(2,1)S(1)} %get-tuple-element.70.right_ref, bf16[1,768,5120]{2,1,0:T(8,128)(2,1)S(1)} %get-tuple-element.54.e_ref, ...), custom_call_target="tpu_custom_call" | custom-call | flops 4000000000 | bytes 1 | tf_op jit(solution)/shard_map/rebuild/pallas_call | solution.py:518
  71.5 2.7 %rebuild.3 = (bf16[768,5120]{1,0:T(8,128)(2,1)}, bf16[1,768,5120]{2,1,0:T(8,128)(2,1)}, f32[4,5120]{1,0:T(4,128)}) custom-call(bf16[768,256]{1,0:T(8,128)(2,1)S(1)} %acts.1.acts_ref, bf16[768,24]{1,0:T(8,128)(2,1)S(1)} %get-tuple-element.67.left_ref, ...), custom_call_target="tpu_custom_call", output_to_operand_aliasing={{0}: (9, {}), {1}: (10, {})} | custom-call | flops 4000000000 | bytes 1 | tf_op jit(solution)/shard_map/rebuild/pallas_call | solution.py:518
  (36 shorter events, 7.8 us)
Async XLA Ops:
  0.6 20.5 %collective-permute-start = (bf16[1,64,5120]{2,1,0:T(8,128)(2,1)}, bf16[1,64,5120]{2,1,0:T(8,128)(2,1)S(1)}, u32[]{:S(2)}, u32[]{:S(2)}) collective-permute-start(bf16[1,64,5120]{2,1,0:T(8,128)(2,1)} %refs_0_.5), channel_id=1, source_target_pairs={{0,2},{2,3},{3,1},{1,0},{4,6},{6,7},{7,5},{5,4},{8,10},{10,11},{11... | collective-permute-start | bytes 1966088 | tf_op jit(solution)/shard_map/ppermute | solution.py:63
  6.2 16.5 %copy-start.1 = (bf16[1,256,768]{2,1,0:T(8,128)(2,1)S(1)}, bf16[1,256,768]{2,1,0:T(8,128)(2,1)}, u32[]{:S(2)}) copy-start(bf16[1,256,768]{2,1,0:T(8,128)(2,1)} %a_ref.5) | copy-start | bytes 1179652
  6.2 21.4 %copy-start = (bf16[1,64,5120]{2,1,0:T(8,128)(2,1)S(1)}, bf16[1,64,5120]{2,1,0:T(8,128)(2,1)}, u32[]{:S(2)}) copy-start(bf16[1,64,5120]{2,1,0:T(8,128)(2,1)} %refs_0_.5) | copy-start | bytes 1966084
  10.5 8.7 %collective-permute-start.3 = (f32[8,128]{1,0:T(8,128)S(1)}, f32[8,128]{1,0:T(8,128)S(1)}, u32[]{:S(2)}, u32[]{:S(2)}) collective-permute-start(f32[8,128]{1,0:T(8,128)S(1)} %get-tuple-element.46.refs_0_), channel_id=1, source_target_pairs={{0,3},{1,0},{2,1},{3,2},{4,7},{5,4},{6,5},{7,6},{8,11},{9,8},{10,9... | collective-permute-start | bytes 12296 | tf_op jit(solution)/shard_map/ppermute | solution.py:68
  11.9 9.2 %collective-permute-start.2 = (f32[8,128]{1,0:T(8,128)S(1)}, f32[8,128]{1,0:T(8,128)S(1)}, u32[]{:S(2)}, u32[]{:S(2)}) collective-permute-start(f32[8,128]{1,0:T(8,128)S(1)} %get-tuple-element.46.refs_0_), channel_id=1, source_target_pairs={{0,2},{1,3},{2,0},{3,1},{4,6},{5,7},{6,4},{7,5},{8,10},{9,11},{10,... | collective-permute-start | bytes 12296 | tf_op jit(solution)/shard_map/ppermute | solution.py:68
  12.2 8.9 %collective-permute-start.1 = (f32[8,128]{1,0:T(8,128)S(1)}, f32[8,128]{1,0:T(8,128)S(1)}, u32[]{:S(2)}, u32[]{:S(2)}) collective-permute-start(f32[8,128]{1,0:T(8,128)S(1)} %get-tuple-element.46.refs_0_), channel_id=1, source_target_pairs={{0,1},{1,2},{2,3},{3,0},{4,5},{5,6},{6,7},{7,4},{8,9},{9,10},{10,1... | collective-permute-start | bytes 12296 | tf_op jit(solution)/shard_map/ppermute | solution.py:68
  21.1 26.7 %collective-permute-start.9 = (bf16[1,64,5120]{2,1,0:T(8,128)(2,1)S(1)}, bf16[1,64,5120]{2,1,0:T(8,128)(2,1)S(1)}, u32[]{:S(2)}, u32[]{:S(2)}) collective-permute-start(bf16[1,64,5120]{2,1,0:T(8,128)(2,1)S(1)} %collective-permute-done.refs_1_), channel_id=1, source_target_pairs={{0,2},{2,3},{3,1},{1,0},{4,6},{6,7},{7,5},{5,4},{8,10},{10,11},{11... | collective-permute-start | bytes 1966088 | tf_op jit(solution)/shard_map/ppermute | solution.py:63
  22.9 1.2 %collective-permute-start.4 = (f32[4,768]{1,0:T(4,128)S(1)}, f32[4,768]{1,0:T(4,128)S(1)}, u32[]{:S(2)}, u32[]{:S(2)}) collective-permute-start(f32[4,768]{1,0:T(4,128)S(1)} %left.1.refs_0_), channel_id=1, source_target_pairs={{0,4},{4,0},{8,12},{12,8},{16,20},{20,16},{24,28},{28,24},{1,5},{5... | collective-permute-start | bytes 36872 | tf_op jit(solution)/shard_map/ppermute | solution.py:73
  24.1 4.6 %collective-permute-start.7 = (f32[4,768]{1,0:T(4,128)S(1)}, f32[4,768]{1,0:T(4,128)S(1)}, u32[]{:S(2)}, u32[]{:S(2)}) collective-permute-start(f32[4,768]{1,0:T(4,128)S(1)} %add.3.refs_0_), channel_id=1, source_target_pairs={{0,24},{4,28},{8,16},{12,20},{16,8},{20,12},{24,0},{28,4},{1,25},{... | collective-permute-start | bytes 36872 | tf_op jit(solution)/shard_map/ppermute | solution.py:73
  26.6 3.7 %collective-permute-start.6 = (f32[4,768]{1,0:T(4,128)S(1)}, f32[4,768]{1,0:T(4,128)S(1)}, u32[]{:S(2)}, u32[]{:S(2)}) collective-permute-start(f32[4,768]{1,0:T(4,128)S(1)} %add.3.refs_0_), channel_id=1, source_target_pairs={{0,16},{4,20},{8,24},{12,28},{16,0},{20,4},{24,8},{28,12},{1,17},{... | collective-permute-start | bytes 36872 | tf_op jit(solution)/shard_map/ppermute | solution.py:73
  27.1 3.7 %collective-permute-start.5 = (f32[4,768]{1,0:T(4,128)S(1)}, f32[4,768]{1,0:T(4,128)S(1)}, u32[]{:S(2)}, u32[]{:S(2)}) collective-permute-start(f32[4,768]{1,0:T(4,128)S(1)} %add.3.refs_0_), channel_id=1, source_target_pairs={{0,8},{4,12},{8,0},{12,4},{16,24},{20,28},{24,16},{28,20},{1,9},{5... | collective-permute-start | bytes 36872 | tf_op jit(solution)/shard_map/ppermute | solution.py:73
  31.1 16.6 %collective-permute-start.8 = (f32[8,128]{1,0:T(8,128)S(1)}, f32[8,128]{1,0:T(8,128)S(1)}, u32[]{:S(2)}, u32[]{:S(2)}) collective-permute-start(f32[8,128]{1,0:T(8,128)S(1)} %get-tuple-element.57), channel_id=1, source_target_pairs={{0,2},{2,3},{3,1},{1,0},{4,6},{6,7},{7,5},{5,4},{8,10},{10,11},{11... | collective-permute-start | bytes 12296 | tf_op jit(solution)/shard_map/ppermute | solution.py:63
  33.7 27.5 %collective-permute-start.14 = (bf16[1,64,3584]{2,1,0:T(8,128)(2,1)S(1)}, bf16[1,64,3584]{2,1,0:T(8,128)(2,1)S(1)}, u32[]{:S(2)}, u32[]{:S(2)}) collective-permute-start(bf16[1,64,3584]{2,1,0:T(8,128)(2,1)S(1)} %get-tuple-element.62), channel_id=1, source_target_pairs={{0,1},{2,0},{3,2},{1,3},{4,5},{6,4},{7,6},{5,7},{8,9},{10,8},{11,1... | collective-permute-start | bytes 1376264 | tf_op jit(solution)/shard_map/ppermute | solution.py:63
  48.3 1.3 %collective-permute-start.10 = (f32[4,2688]{1,0:T(4,128)S(1)}, f32[4,2688]{1,0:T(4,128)S(1)}, u32[]{:S(2)}, u32[]{:S(2)}) collective-permute-start(f32[4,2688]{1,0:T(4,128)S(1)} %get-tuple-element.61), channel_id=1, source_target_pairs={{0,4},{4,0},{8,12},{12,8},{16,20},{20,16},{24,28},{28,24},{1,5},{5... | collective-permute-start | bytes 129032 | tf_op jit(solution)/shard_map/ppermute | solution.py:73
  49.6 5.0 %collective-permute-start.13 = (f32[4,2688]{1,0:T(4,128)S(1)}, f32[4,2688]{1,0:T(4,128)S(1)}, u32[]{:S(2)}, u32[]{:S(2)}) collective-permute-start(f32[4,2688]{1,0:T(4,128)S(1)} %add.4.refs_0_), channel_id=1, source_target_pairs={{0,24},{4,28},{8,16},{12,20},{16,8},{20,12},{24,0},{28,4},{1,25},{... | collective-permute-start | bytes 129032 | tf_op jit(solution)/shard_map/ppermute | solution.py:73
  52.1 4.0 %collective-permute-start.12 = (f32[4,2688]{1,0:T(4,128)S(1)}, f32[4,2688]{1,0:T(4,128)S(1)}, u32[]{:S(2)}, u32[]{:S(2)}) collective-permute-start(f32[4,2688]{1,0:T(4,128)S(1)} %add.4.refs_0_), channel_id=1, source_target_pairs={{0,16},{4,20},{8,24},{12,28},{16,0},{20,4},{24,8},{28,12},{1,17},{... | collective-permute-start | bytes 129032 | tf_op jit(solution)/shard_map/ppermute | solution.py:73
  52.6 4.0 %collective-permute-start.11 = (f32[4,2688]{1,0:T(4,128)S(1)}, f32[4,2688]{1,0:T(4,128)S(1)}, u32[]{:S(2)}, u32[]{:S(2)}) collective-permute-start(f32[4,2688]{1,0:T(4,128)S(1)} %add.4.refs_0_), channel_id=1, source_target_pairs={{0,8},{4,12},{8,0},{12,4},{16,24},{20,28},{24,16},{28,20},{1,9},{5... | collective-permute-start | bytes 129032 | tf_op jit(solution)/shard_map/ppermute | solution.py:73
  56.6 5.9 %collective-permute-start.17 = (f32[4,2688]{1,0:T(4,128)S(1)}, f32[4,2688]{1,0:T(4,128)S(1)}, u32[]{:S(2)}, u32[]{:S(2)}) collective-permute-start(f32[4,2688]{1,0:T(4,128)S(1)} %add.5.refs_0_), channel_id=1, source_target_pairs={{0,3},{1,2},{2,1},{3,0},{4,7},{5,6},{6,5},{7,4},{8,11},{9,10},{10,... | collective-permute-start | bytes 129032 | tf_op jit(solution)/shard_map/ppermute | solution.py:73
  56.7 5.8 %collective-permute-start.16 = (f32[4,2688]{1,0:T(4,128)S(1)}, f32[4,2688]{1,0:T(4,128)S(1)}, u32[]{:S(2)}, u32[]{:S(2)}) collective-permute-start(f32[4,2688]{1,0:T(4,128)S(1)} %add.5.refs_0_), channel_id=1, source_target_pairs={{0,2},{1,3},{2,0},{3,1},{4,6},{5,7},{6,4},{7,5},{8,10},{9,11},{10,... | collective-permute-start | bytes 129032 | tf_op jit(solution)/shard_map/ppermute | solution.py:73
  56.8 6.3 %collective-permute-start.15 = (f32[4,2688]{1,0:T(4,128)S(1)}, f32[4,2688]{1,0:T(4,128)S(1)}, u32[]{:S(2)}, u32[]{:S(2)}) collective-permute-start(f32[4,2688]{1,0:T(4,128)S(1)} %add.5.refs_0_), channel_id=1, source_target_pairs={{0,1},{1,0},{2,3},{3,2},{4,5},{5,4},{6,7},{7,6},{8,9},{9,8},{10,11... | collective-permute-start | bytes 129032 | tf_op jit(solution)/shard_map/ppermute | solution.py:73
  63.2 2.9 %collective-permute-start.18 = (f32[4,2688]{1,0:T(4,128)S(1)}, f32[4,2688]{1,0:T(4,128)S(1)}, u32[]{:S(2)}, u32[]{:S(2)}) collective-permute-start(f32[4,2688]{1,0:T(4,128)S(1)} %join.1.mine_ref), channel_id=1, source_target_pairs={{0,4},{4,0},{8,12},{12,8},{16,20},{20,16},{24,28},{28,24},{1,5},{5... | collective-permute-start | bytes 129032 | tf_op jit(solution)/shard_map/ppermute | solution.py:73
  63.3 8.2 %collective-permute-start.19 = (bf16[1,64,1536]{2,1,0:T(8,128)(2,1)S(1)}, bf16[1,64,1536]{2,1,0:T(8,128)(2,1)S(1)}, u32[]{:S(2)}, u32[]{:S(2)}) collective-permute-start(bf16[1,64,1536]{2,1,0:T(8,128)(2,1)S(1)} %get-tuple-element.71), channel_id=1, source_target_pairs={{0,1},{2,0},{3,2},{1,3},{4,5},{6,4},{7,6},{5,7},{8,9},{10,8},{11,1... | collective-permute-start | bytes 589832 | tf_op jit(solution)/shard_map/ppermute | solution.py:63

commit v22 on v20

--- a/solution.py
+++ b/solution.py
@@ -521,7 +521,7 @@
             out_shape=[sds((rows, width), BF16), sds((1, rows, width), BF16)]
             + [sds((rank, width), F32)] * last,
             input_output_aliases={len(inputs) + k: k for k in range(len(outs))},
-            scratch_shapes=[pltpu.VMEM((rows, part), BF16)] * 2 + [dma((4, 4 if part > half else 3, 2))],
+            scratch_shapes=[pltpu.VMEM((rows, part), BF16)] * 2 + [dma((3, 4 if part > half else 3, 2))],
             compiler_params=params(16),
             cost_estimate=cost(REBUILD),
             name="rebuild",

time: 66 us -> 66.1 us (level)
  no operation moved by 1% of the time
where the time goes in v22:
time: 66.1 us; the launch traced here: 65.9 us
  starting transfers between devices  25.4 us (38%)
  waiting for transfers between devices  22.5 us (34%)
  Pallas kernels  17.2 us (26%)
  between operations  0.78 us (1%)
    ppermute x12, starting transfers between devices, swap(): return lax.ppermute(x, axis, [(i, i ^ bit) for i in range(n)])  11.7 us
    ppermute x12, waiting for transfers between devices, swap(): return lax.ppermute(x, axis, [(i, i ^ bit) for i in range(n)])  11.3 us
    ppermute x5, starting transfers between devices, ring_step(): lax.ppermute(x, axis, [(ring[p], ring[(p + 1) % n]) for p in range(n)])  10.1 us
    pallas_call x2, Pallas kernels, per_device(): pl.pallas_call(functools.partial(final_kernel, at, part, bases, last), in...  7.57 us
    ppermute x3, waiting for transfers between devices, exchange(): lax.ppermute(pieces[k], axis, [(i, (i + k) % n) for i in range(n)])  6.99 us
    ppermute x5, waiting for transfers between devices, ring_step(): lax.ppermute(x, axis, [(ring[p], ring[(p + 1) % n]) for p in range(n)])  4.2 us
    pallas_call x1, Pallas kernels, per_device(): call(error_left_kernel, [sds((rank, rows), F32), sds((1, rows, width), BF...  4.19 us
    ppermute x3, starting transfers between devices, exchange(): lax.ppermute(pieces[k], axis, [(i, (i + k) % n) for i in range(n)])  3.65 us
  transfers between devices with their start and end apart: 20, of which 13 were waited for; matrix products, arithmetic and copies ran while one was open for 0% of the time, Pallas kernels for 22%

profile of v22, /device:TPU:0, one launch (start us, length us, event | category | flops | bytes accessed | tf_op | source)
XLA Modules:
  0.0 65.9 jit_solution(12379057977726846223)
XLA Ops:
  0.6 4.1 %collective-permute-start = (bf16[1,64,5120]{2,1,0:T(8,128)(2,1)}, bf16[1,64,5120]{2,1,0:T(8,128)(2,1)S(1)}, u32[]{:S(2)}, u32[]{:S(2)}) collective-permute-start(bf16[1,64,5120]{2,1,0:T(8,128)(2,1)} %refs_0_.5), channel_id=1, source_target_pairs={{0,2},{2,3},{3,1},{1,0},{4,6},{6,7},{7,5},{5,4},{8,10},{10,11},{11... | collective-permute-start | bytes 1966088 | tf_op jit(solution)/shard_map/ppermute | solution.py:62
  4.7 1.5 %token_factor.1 = (f32[8,128]{1,0:T(8,128)S(1)}, bf16[12,5120]{1,0:T(8,128)(2,1)S(1)}) custom-call(f32[4,5120]{1,0:T(4,128)} %bitcast.2, bf16[1,64,5120]{2,1,0:T(8,128)(2,1)} %refs_0_.5), custom_call_target="tpu_custom_call" | custom-call | flops 1 | bytes 1 | tf_op jit(solution)/shard_map/token_factor/pallas_call | solution.py:406
  6.2 4.2 %error_left.1 = (f32[4,768]{1,0:T(4,128)S(1)}, bf16[1,768,5120]{2,1,0:T(8,128)(2,1)S(1)}) custom-call(bf16[12,5120]{1,0:T(8,128)(2,1)S(1)} %get-tuple-element.43.terms_ref, bf16[1,768,5120]{2,1,0:T(8,128)(2,1)} %e_hbm.1), custom_call_target="tpu_custom_call" | custom-call | flops 4600000000 | bytes 1 | tf_op jit(solution)/shard_map/error_left/pallas_call | solution.py:417
  10.4 1.4 %collective-permute-start.3 = (f32[8,128]{1,0:T(8,128)S(1)}, f32[8,128]{1,0:T(8,128)S(1)}, u32[]{:S(2)}, u32[]{:S(2)}) collective-permute-start(f32[8,128]{1,0:T(8,128)S(1)} %get-tuple-element.47.refs_0_), channel_id=1, source_target_pairs={{0,3},{1,0},{2,1},{3,2},{4,7},{5,4},{6,5},{7,6},{8,11},{9,8},{10,9... | collective-permute-start | bytes 12296 | tf_op jit(solution)/shard_map/ppermute | solution.py:67
  12.1 1.9 %collective-permute-start.1 = (f32[8,128]{1,0:T(8,128)S(1)}, f32[8,128]{1,0:T(8,128)S(1)}, u32[]{:S(2)}, u32[]{:S(2)}) collective-permute-start(f32[8,128]{1,0:T(8,128)S(1)} %get-tuple-element.47.refs_0_), channel_id=1, source_target_pairs={{0,1},{1,2},{2,3},{3,0},{4,5},{5,6},{6,7},{7,4},{8,9},{9,10},{10,1... | collective-permute-start | bytes 12296 | tf_op jit(solution)/shard_map/ppermute | solution.py:67
  14.1 5.1 %collective-permute-done.3.refs_3_ = f32[8,128]{1,0:T(8,128)S(1)} collective-permute-done((f32[8,128]{1,0:T(8,128)S(1)}, f32[8,128]{1,0:T(8,128)S(1)}, u32[]{:S(2)}, u32[]{:S(2)}) %collective-permute-start.3) | collective-permute-done | bytes 4128 | tf_op jit(solution)/shard_map/ppermute | solution.py:67
  19.2 1.9 %collective-permute-done.2.refs_2_ = f32[8,128]{1,0:T(8,128)S(1)} collective-permute-done((f32[8,128]{1,0:T(8,128)S(1)}, f32[8,128]{1,0:T(8,128)S(1)}, u32[]{:S(2)}, u32[]{:S(2)}) %collective-permute-start.2) | collective-permute-done | bytes 4128 | tf_op jit(solution)/shard_map/ppermute | solution.py:67
  21.1 1.6 %collective-permute-start.8 = (bf16[1,64,5120]{2,1,0:T(8,128)(2,1)S(1)}, bf16[1,64,5120]{2,1,0:T(8,128)(2,1)S(1)}, u32[]{:S(2)}, u32[]{:S(2)}) collective-permute-start(bf16[1,64,5120]{2,1,0:T(8,128)(2,1)S(1)} %collective-permute-done.refs_1_), channel_id=1, source_target_pairs={{0,2},{2,3},{3,1},{1,0},{4,6},{6,7},{7,5},{5,4},{8,10},{10,11},{11... | collective-permute-start | bytes 1966088 | tf_op jit(solution)/shard_map/ppermute | solution.py:62
  22.9 1.2 %collective-permute-done.4.refs_1_ = f32[4,768]{1,0:T(4,128)S(1)} collective-permute-done((f32[4,768]{1,0:T(4,128)S(1)}, f32[4,768]{1,0:T(4,128)S(1)}, u32[]{:S(2)}, u32[]{:S(2)}) %collective-permute-start.4) | collective-permute-done | bytes 12320 | tf_op jit(solution)/shard_map/ppermute | solution.py:72
  24.1 2.4 %collective-permute-start.7 = (f32[4,768]{1,0:T(4,128)S(1)}, f32[4,768]{1,0:T(4,128)S(1)}, u32[]{:S(2)}, u32[]{:S(2)}) collective-permute-start(f32[4,768]{1,0:T(4,128)S(1)} %add.3.refs_0_), channel_id=1, source_target_pairs={{0,24},{4,28},{8,16},{12,20},{16,8},{20,12},{24,0},{28,4},{1,25},{... | collective-permute-start | bytes 36872 | tf_op jit(solution)/shard_map/ppermute | solution.py:72
  28.7 1.5 %collective-permute-done.6.refs_2_ = f32[4,768]{1,0:T(4,128)S(1)} collective-permute-done((f32[4,768]{1,0:T(4,128)S(1)}, f32[4,768]{1,0:T(4,128)S(1)}, u32[]{:S(2)}, u32[]{:S(2)}) %collective-permute-start.6) | collective-permute-done | bytes 12320 | tf_op jit(solution)/shard_map/ppermute | solution.py:72
  31.1 1.4 %collective-permute-start.9 = (f32[8,128]{1,0:T(8,128)S(1)}, f32[8,128]{1,0:T(8,128)S(1)}, u32[]{:S(2)}, u32[]{:S(2)}) collective-permute-start(f32[8,128]{1,0:T(8,128)S(1)} %get-tuple-element.53), channel_id=1, source_target_pairs={{0,2},{2,3},{3,1},{1,0},{4,6},{6,7},{7,5},{5,4},{8,10},{10,11},{11... | collective-permute-start | bytes 12296 | tf_op jit(solution)/shard_map/ppermute | solution.py:62
  33.7 4.2 %collective-permute-done.9.got_ref = f32[8,128]{1,0:T(8,128)S(1)} collective-permute-done((f32[8,128]{1,0:T(8,128)S(1)}, f32[8,128]{1,0:T(8,128)S(1)}, u32[]{:S(2)}, u32[]{:S(2)}) %collective-permute-start.9) | collective-permute-done | bytes 4128 | tf_op jit(solution)/shard_map/ppermute | solution.py:62
  38.0 1.3 %collective-permute-start.14 = (bf16[1,64,3584]{2,1,0:T(8,128)(2,1)S(1)}, bf16[1,64,3584]{2,1,0:T(8,128)(2,1)S(1)}, u32[]{:S(2)}, u32[]{:S(2)}) collective-permute-start(bf16[1,64,3584]{2,1,0:T(8,128)(2,1)S(1)} %get-tuple-element.64), channel_id=1, source_target_pairs={{0,2},{2,3},{3,1},{1,0},{4,6},{6,7},{7,5},{5,4},{8,10},{10,11},{11... | collective-permute-start | bytes 1376264 | tf_op jit(solution)/shard_map/ppermute | solution.py:62
  39.9 1.2 %collective-permute-done.10.refs_1_ = f32[4,2688]{1,0:T(4,128)S(1)} collective-permute-done((f32[4,2688]{1,0:T(4,128)S(1)}, f32[4,2688]{1,0:T(4,128)S(1)}, u32[]{:S(2)}, u32[]{:S(2)}) %collective-permute-start.10) | collective-permute-done | bytes 43040 | tf_op jit(solution)/shard_map/ppermute | solution.py:72
  41.1 2.5 %collective-permute-start.13 = (f32[4,2688]{1,0:T(4,128)S(1)}, f32[4,2688]{1,0:T(4,128)S(1)}, u32[]{:S(2)}, u32[]{:S(2)}) collective-permute-start(f32[4,2688]{1,0:T(4,128)S(1)} %add.4.refs_0_), channel_id=1, source_target_pairs={{0,24},{4,28},{8,16},{12,20},{16,8},{20,12},{24,0},{28,4},{1,25},{... | collective-permute-start | bytes 129032 | tf_op jit(solution)/shard_map/ppermute | solution.py:72
  44.7 1.4 %collective-permute-done.13.refs_3_ = f32[4,2688]{1,0:T(4,128)S(1)} collective-permute-done((f32[4,2688]{1,0:T(4,128)S(1)}, f32[4,2688]{1,0:T(4,128)S(1)}, u32[]{:S(2)}, u32[]{:S(2)}) %collective-permute-start.13) | collective-permute-done | bytes 43040 | tf_op jit(solution)/shard_map/ppermute | solution.py:72
  46.1 1.5 %collective-permute-done.12.refs_2_ = f32[4,2688]{1,0:T(4,128)S(1)} collective-permute-done((f32[4,2688]{1,0:T(4,128)S(1)}, f32[4,2688]{1,0:T(4,128)S(1)}, u32[]{:S(2)}, u32[]{:S(2)}) %collective-permute-start.12) | collective-permute-done | bytes 43040 | tf_op jit(solution)/shard_map/ppermute | solution.py:72
  48.2 1.6 %collective-permute-start.17 = (f32[4,2688]{1,0:T(4,128)S(1)}, f32[4,2688]{1,0:T(4,128)S(1)}, u32[]{:S(2)}, u32[]{:S(2)}) collective-permute-start(f32[4,2688]{1,0:T(4,128)S(1)} %add.5.refs_0_), channel_id=1, source_target_pairs={{0,3},{1,2},{2,1},{3,0},{4,7},{5,6},{6,5},{7,4},{8,11},{9,10},{10,... | collective-permute-start | bytes 129032 | tf_op jit(solution)/shard_map/ppermute | solution.py:72
  50.5 2.1 %collective-permute-start.15 = (f32[4,2688]{1,0:T(4,128)S(1)}, f32[4,2688]{1,0:T(4,128)S(1)}, u32[]{:S(2)}, u32[]{:S(2)}) collective-permute-start(f32[4,2688]{1,0:T(4,128)S(1)} %add.5.refs_0_), channel_id=1, source_target_pairs={{0,1},{1,0},{2,3},{3,2},{4,5},{5,4},{6,7},{7,6},{8,9},{9,8},{10,11... | collective-permute-start | bytes 129032 | tf_op jit(solution)/shard_map/ppermute | solution.py:72
  52.8 1.3 %collective-permute-done.17.refs_3_ = f32[4,2688]{1,0:T(4,128)S(1)} collective-permute-done((f32[4,2688]{1,0:T(4,128)S(1)}, f32[4,2688]{1,0:T(4,128)S(1)}, u32[]{:S(2)}, u32[]{:S(2)}) %collective-permute-start.17) | collective-permute-done | bytes 43040 | tf_op jit(solution)/shard_map/ppermute | solution.py:72
  55.3 1.7 %collective-permute-start.19 = (bf16[1,64,1536]{2,1,0:T(8,128)(2,1)S(1)}, bf16[1,64,1536]{2,1,0:T(8,128)(2,1)S(1)}, u32[]{:S(2)}, u32[]{:S(2)}) collective-permute-start(bf16[1,64,1536]{2,1,0:T(8,128)(2,1)S(1)} %get-tuple-element.73), channel_id=1, source_target_pairs={{0,2},{2,3},{3,1},{1,0},{4,6},{6,7},{7,5},{5,4},{8,10},{10,11},{11... | collective-permute-start | bytes 589832 | tf_op jit(solution)/shard_map/ppermute | solution.py:62
  58.3 4.9 %rebuild.2 = (bf16[768,5120]{1,0:T(8,128)(2,1)}, bf16[1,768,5120]{2,1,0:T(8,128)(2,1)}) custom-call(bf16[768,256]{1,0:T(8,128)(2,1)S(1)} %acts.1.acts_ref, bf16[768,24]{1,0:T(8,128)(2,1)S(1)} %get-tuple-element.69.left_ref, bf16[24,5120]{1,0:T(8,128)(2,1)S(1)} %get-tuple-element.72.right_ref, bf16[1,768,5120]{2,1,0:T(8,128)(2,1)S(1)} %get-tuple-element.55.e_ref, ...), custom_call_target="tpu_custom_call" | custom-call | flops 4000000000 | bytes 1 | tf_op jit(solution)/shard_map/rebuild/pallas_call | solution.py:517
  63.2 2.7 %rebuild.3 = (bf16[768,5120]{1,0:T(8,128)(2,1)}, bf16[1,768,5120]{2,1,0:T(8,128)(2,1)}, f32[4,5120]{1,0:T(4,128)}) custom-call(bf16[768,256]{1,0:T(8,128)(2,1)S(1)} %acts.1.acts_ref, bf16[768,24]{1,0:T(8,128)(2,1)S(1)} %get-tuple-element.69.left_ref, ...), custom_call_target="tpu_custom_call", output_to_operand_aliasing={{0}: (9, {}), {1}: (10, {})} | custom-call | flops 4000000000 | bytes 1 | tf_op jit(solution)/shard_map/rebuild/pallas_call | solution.py:517
  (36 shorter events, 10.5 us)
Async XLA Ops:
  0.6 20.5 %collective-permute-start = (bf16[1,64,5120]{2,1,0:T(8,128)(2,1)}, bf16[1,64,5120]{2,1,0:T(8,128)(2,1)S(1)}, u32[]{:S(2)}, u32[]{:S(2)}) collective-permute-start(bf16[1,64,5120]{2,1,0:T(8,128)(2,1)} %refs_0_.5), channel_id=1, source_target_pairs={{0,2},{2,3},{3,1},{1,0},{4,6},{6,7},{7,5},{5,4},{8,10},{10,11},{11... | collective-permute-start | bytes 1966088 | tf_op jit(solution)/shard_map/ppermute | solution.py:62
  6.2 16.5 %copy-start.1 = (bf16[1,256,768]{2,1,0:T(8,128)(2,1)S(1)}, bf16[1,256,768]{2,1,0:T(8,128)(2,1)}, u32[]{:S(2)}) copy-start(bf16[1,256,768]{2,1,0:T(8,128)(2,1)} %a_ref.5) | copy-start | bytes 1179652
  10.4 28.9 %copy-start = (bf16[1,64,5120]{2,1,0:T(8,128)(2,1)S(1)}, bf16[1,64,5120]{2,1,0:T(8,128)(2,1)}, u32[]{:S(2)}) copy-start(bf16[1,64,5120]{2,1,0:T(8,128)(2,1)} %refs_0_.5) | copy-start | bytes 1966084
  10.4 8.8 %collective-permute-start.3 = (f32[8,128]{1,0:T(8,128)S(1)}, f32[8,128]{1,0:T(8,128)S(1)}, u32[]{:S(2)}, u32[]{:S(2)}) collective-permute-start(f32[8,128]{1,0:T(8,128)S(1)} %get-tuple-element.47.refs_0_), channel_id=1, source_target_pairs={{0,3},{1,0},{2,1},{3,2},{4,7},{5,4},{6,5},{7,6},{8,11},{9,8},{10,9... | collective-permute-start | bytes 12296 | tf_op jit(solution)/shard_map/ppermute | solution.py:67
  11.8 9.2 %collective-permute-start.2 = (f32[8,128]{1,0:T(8,128)S(1)}, f32[8,128]{1,0:T(8,128)S(1)}, u32[]{:S(2)}, u32[]{:S(2)}) collective-permute-start(f32[8,128]{1,0:T(8,128)S(1)} %get-tuple-element.47.refs_0_), channel_id=1, source_target_pairs={{0,2},{1,3},{2,0},{3,1},{4,6},{5,7},{6,4},{7,5},{8,10},{9,11},{10,... | collective-permute-start | bytes 12296 | tf_op jit(solution)/shard_map/ppermute | solution.py:67
  12.1 8.9 %collective-permute-start.1 = (f32[8,128]{1,0:T(8,128)S(1)}, f32[8,128]{1,0:T(8,128)S(1)}, u32[]{:S(2)}, u32[]{:S(2)}) collective-permute-start(f32[8,128]{1,0:T(8,128)S(1)} %get-tuple-element.47.refs_0_), channel_id=1, source_target_pairs={{0,1},{1,2},{2,3},{3,0},{4,5},{5,6},{6,7},{7,4},{8,9},{9,10},{10,1... | collective-permute-start | bytes 12296 | tf_op jit(solution)/shard_map/ppermute | solution.py:67
  21.1 16.8 %collective-permute-start.8 = (bf16[1,64,5120]{2,1,0:T(8,128)(2,1)S(1)}, bf16[1,64,5120]{2,1,0:T(8,128)(2,1)S(1)}, u32[]{:S(2)}, u32[]{:S(2)}) collective-permute-start(bf16[1,64,5120]{2,1,0:T(8,128)(2,1)S(1)} %collective-permute-done.refs_1_), channel_id=1, source_target_pairs={{0,2},{2,3},{3,1},{1,0},{4,6},{6,7},{7,5},{5,4},{8,10},{10,11},{11... | collective-permute-start | bytes 1966088 | tf_op jit(solution)/shard_map/ppermute | solution.py:62
  22.9 1.2 %collective-permute-start.4 = (f32[4,768]{1,0:T(4,128)S(1)}, f32[4,768]{1,0:T(4,128)S(1)}, u32[]{:S(2)}, u32[]{:S(2)}) collective-permute-start(f32[4,768]{1,0:T(4,128)S(1)} %left.1.refs_0_), channel_id=1, source_target_pairs={{0,4},{4,0},{8,12},{12,8},{16,20},{20,16},{24,28},{28,24},{1,5},{5... | collective-permute-start | bytes 36872 | tf_op jit(solution)/shard_map/ppermute | solution.py:72
  24.1 4.6 %collective-permute-start.7 = (f32[4,768]{1,0:T(4,128)S(1)}, f32[4,768]{1,0:T(4,128)S(1)}, u32[]{:S(2)}, u32[]{:S(2)}) collective-permute-start(f32[4,768]{1,0:T(4,128)S(1)} %add.3.refs_0_), channel_id=1, source_target_pairs={{0,24},{4,28},{8,16},{12,20},{16,8},{20,12},{24,0},{28,4},{1,25},{... | collective-permute-start | bytes 36872 | tf_op jit(solution)/shard_map/ppermute | solution.py:72
  26.6 3.7 %collective-permute-start.6 = (f32[4,768]{1,0:T(4,128)S(1)}, f32[4,768]{1,0:T(4,128)S(1)}, u32[]{:S(2)}, u32[]{:S(2)}) collective-permute-start(f32[4,768]{1,0:T(4,128)S(1)} %add.3.refs_0_), channel_id=1, source_target_pairs={{0,16},{4,20},{8,24},{12,28},{16,0},{20,4},{24,8},{28,12},{1,17},{... | collective-permute-start | bytes 36872 | tf_op jit(solution)/shard_map/ppermute | solution.py:72
  27.1 3.7 %collective-permute-start.5 = (f32[4,768]{1,0:T(4,128)S(1)}, f32[4,768]{1,0:T(4,128)S(1)}, u32[]{:S(2)}, u32[]{:S(2)}) collective-permute-start(f32[4,768]{1,0:T(4,128)S(1)} %add.3.refs_0_), channel_id=1, source_target_pairs={{0,8},{4,12},{8,0},{12,4},{16,24},{20,28},{24,16},{28,20},{1,9},{5... | collective-permute-start | bytes 36872 | tf_op jit(solution)/shard_map/ppermute | solution.py:72
  31.1 6.8 %collective-permute-start.9 = (f32[8,128]{1,0:T(8,128)S(1)}, f32[8,128]{1,0:T(8,128)S(1)}, u32[]{:S(2)}, u32[]{:S(2)}) collective-permute-start(f32[8,128]{1,0:T(8,128)S(1)} %get-tuple-element.53), channel_id=1, source_target_pairs={{0,2},{2,3},{3,1},{1,0},{4,6},{6,7},{7,5},{5,4},{8,10},{10,11},{11... | collective-permute-start | bytes 12296 | tf_op jit(solution)/shard_map/ppermute | solution.py:62
  38.0 17.1 %collective-permute-start.14 = (bf16[1,64,3584]{2,1,0:T(8,128)(2,1)S(1)}, bf16[1,64,3584]{2,1,0:T(8,128)(2,1)S(1)}, u32[]{:S(2)}, u32[]{:S(2)}) collective-permute-start(bf16[1,64,3584]{2,1,0:T(8,128)(2,1)S(1)} %get-tuple-element.64), channel_id=1, source_target_pairs={{0,2},{2,3},{3,1},{1,0},{4,6},{6,7},{7,5},{5,4},{8,10},{10,11},{11... | collective-permute-start | bytes 1376264 | tf_op jit(solution)/shard_map/ppermute | solution.py:62
  39.8 1.3 %collective-permute-start.10 = (f32[4,2688]{1,0:T(4,128)S(1)}, f32[4,2688]{1,0:T(4,128)S(1)}, u32[]{:S(2)}, u32[]{:S(2)}) collective-permute-start(f32[4,2688]{1,0:T(4,128)S(1)} %get-tuple-element.63), channel_id=1, source_target_pairs={{0,4},{4,0},{8,12},{12,8},{16,20},{20,16},{24,28},{28,24},{1,5},{5... | collective-permute-start | bytes 129032 | tf_op jit(solution)/shard_map/ppermute | solution.py:72
  41.1 5.0 %collective-permute-start.13 = (f32[4,2688]{1,0:T(4,128)S(1)}, f32[4,2688]{1,0:T(4,128)S(1)}, u32[]{:S(2)}, u32[]{:S(2)}) collective-permute-start(f32[4,2688]{1,0:T(4,128)S(1)} %add.4.refs_0_), channel_id=1, source_target_pairs={{0,24},{4,28},{8,16},{12,20},{16,8},{20,12},{24,0},{28,4},{1,25},{... | collective-permute-start | bytes 129032 | tf_op jit(solution)/shard_map/ppermute | solution.py:72
  43.6 4.0 %collective-permute-start.12 = (f32[4,2688]{1,0:T(4,128)S(1)}, f32[4,2688]{1,0:T(4,128)S(1)}, u32[]{:S(2)}, u32[]{:S(2)}) collective-permute-start(f32[4,2688]{1,0:T(4,128)S(1)} %add.4.refs_0_), channel_id=1, source_target_pairs={{0,16},{4,20},{8,24},{12,28},{16,0},{20,4},{24,8},{28,12},{1,17},{... | collective-permute-start | bytes 129032 | tf_op jit(solution)/shard_map/ppermute | solution.py:72
  44.2 4.0 %collective-permute-start.11 = (f32[4,2688]{1,0:T(4,128)S(1)}, f32[4,2688]{1,0:T(4,128)S(1)}, u32[]{:S(2)}, u32[]{:S(2)}) collective-permute-start(f32[4,2688]{1,0:T(4,128)S(1)} %add.4.refs_0_), channel_id=1, source_target_pairs={{0,8},{4,12},{8,0},{12,4},{16,24},{20,28},{24,16},{28,20},{1,9},{5... | collective-permute-start | bytes 129032 | tf_op jit(solution)/shard_map/ppermute | solution.py:72
  48.2 5.9 %collective-permute-start.17 = (f32[4,2688]{1,0:T(4,128)S(1)}, f32[4,2688]{1,0:T(4,128)S(1)}, u32[]{:S(2)}, u32[]{:S(2)}) collective-permute-start(f32[4,2688]{1,0:T(4,128)S(1)} %add.5.refs_0_), channel_id=1, source_target_pairs={{0,3},{1,2},{2,1},{3,0},{4,7},{5,6},{6,5},{7,4},{8,11},{9,10},{10,... | collective-permute-start | bytes 129032 | tf_op jit(solution)/shard_map/ppermute | solution.py:72
  49.8 5.3 %collective-permute-start.16 = (f32[4,2688]{1,0:T(4,128)S(1)}, f32[4,2688]{1,0:T(4,128)S(1)}, u32[]{:S(2)}, u32[]{:S(2)}) collective-permute-start(f32[4,2688]{1,0:T(4,128)S(1)} %add.5.refs_0_), channel_id=1, source_target_pairs={{0,2},{1,3},{2,0},{3,1},{4,6},{5,7},{6,4},{7,5},{8,10},{9,11},{10,... | collective-permute-start | bytes 129032 | tf_op jit(solution)/shard_map/ppermute | solution.py:72
  50.5 4.6 %collective-permute-start.15 = (f32[4,2688]{1,0:T(4,128)S(1)}, f32[4,2688]{1,0:T(4,128)S(1)}, u32[]{:S(2)}, u32[]{:S(2)}) collective-permute-start(f32[4,2688]{1,0:T(4,128)S(1)} %add.5.refs_0_), channel_id=1, source_target_pairs={{0,1},{1,0},{2,3},{3,2},{4,5},{5,4},{6,7},{7,6},{8,9},{9,8},{10,11... | collective-permute-start | bytes 129032 | tf_op jit(solution)/shard_map/ppermute | solution.py:72
  55.3 2.5 %collective-permute-start.18 = (f32[4,2688]{1,0:T(4,128)S(1)}, f32[4,2688]{1,0:T(4,128)S(1)}, u32[]{:S(2)}, u32[]{:S(2)}) collective-permute-start(f32[4,2688]{1,0:T(4,128)S(1)} %join.1.mine_ref), channel_id=1, source_target_pairs={{0,4},{4,0},{8,12},{12,8},{16,20},{20,16},{24,28},{28,24},{1,5},{5... | collective-permute-start | bytes 129032 | tf_op jit(solution)/shard_map/ppermute | solution.py:72
  55.3 7.9 %collective-permute-start.19 = (bf16[1,64,1536]{2,1,0:T(8,128)(2,1)S(1)}, bf16[1,64,1536]{2,1,0:T(8,128)(2,1)S(1)}, u32[]{:S(2)}, u32[]{:S(2)}) collective-permute-start(bf16[1,64,1536]{2,1,0:T(8,128)(2,1)S(1)} %get-tuple-element.73), channel_id=1, source_target_pairs={{0,2},{2,3},{3,1},{1,0},{4,6},{6,7},{7,5},{5,4},{8,10},{10,11},{11... | collective-permute-start | bytes 589832 | tf_op jit(solution)/shard_map/ppermute | solution.py:62

commit v23 on v22

--- a/solution.py
+++ b/solution.py
@@ -521,7 +521,7 @@
             out_shape=[sds((rows, width), BF16), sds((1, rows, width), BF16)]
             + [sds((rank, width), F32)] * last,
             input_output_aliases={len(inputs) + k: k for k in range(len(outs))},
-            scratch_shapes=[pltpu.VMEM((rows, part), BF16)] * 2 + [dma((3, 4 if part > half else 3, 2))],
+            scratch_shapes=[pltpu.VMEM((rows, part), BF16)] * 2 + [dma((7, 4 if part > half else 3, 2))],
             compiler_params=params(16),
             cost_estimate=cost(REBUILD),
             name="rebuild",

time: 66.1 us -> 66.1 us (level)
  no operation moved by 1% of the time
where the time goes in v23:
time: 66.1 us; the launch traced here: 66 us
  starting transfers between devices  25.4 us (38%)
  waiting for transfers between devices  22.5 us (34%)
  Pallas kernels  17.2 us (26%)
  between operations  0.78 us (1%)
    ppermute x12, starting transfers between devices, swap(): return lax.ppermute(x, axis, [(i, i ^ bit) for i in range(n)])  11.7 us
    ppermute x12, waiting for transfers between devices, swap(): return lax.ppermute(x, axis, [(i, i ^ bit) for i in range(n)])  11.3 us
    ppermute x5, starting transfers between devices, ring_step(): lax.ppermute(x, axis, [(ring[p], ring[(p + 1) % n]) for p in range(n)])  10.1 us
    pallas_call x2, Pallas kernels, per_device(): pl.pallas_call(functools.partial(final_kernel, at, part, bases, last), in...  7.59 us
    ppermute x3, waiting for transfers between devices, exchange(): lax.ppermute(pieces[k], axis, [(i, (i + k) % n) for i in range(n)])  6.99 us
    ppermute x5, waiting for transfers between devices, ring_step(): lax.ppermute(x, axis, [(ring[p], ring[(p + 1) % n]) for p in range(n)])  4.2 us
    pallas_call x1, Pallas kernels, per_device(): call(error_left_kernel, [sds((rank, rows), F32), sds((1, rows, width), BF...  4.19 us
    ppermute x3, starting transfers between devices, exchange(): lax.ppermute(pieces[k], axis, [(i, (i + k) % n) for i in range(n)])  3.65 us
  transfers between devices with their start and end apart: 20, of which 13 were waited for; matrix products, arithmetic and copies ran while one was open for 0% of the time, Pallas kernels for 22%

profile of v23, /device:TPU:0, one launch (start us, length us, event | category | flops | bytes accessed | tf_op | source)
XLA Modules:
  0.0 66.0 jit_solution(17532399138151911374)
XLA Ops:
  0.6 4.1 %collective-permute-start = (bf16[1,64,5120]{2,1,0:T(8,128)(2,1)}, bf16[1,64,5120]{2,1,0:T(8,128)(2,1)S(1)}, u32[]{:S(2)}, u32[]{:S(2)}) collective-permute-start(bf16[1,64,5120]{2,1,0:T(8,128)(2,1)} %refs_0_.5), channel_id=1, source_target_pairs={{0,2},{2,3},{3,1},{1,0},{4,6},{6,7},{7,5},{5,4},{8,10},{10,11},{11... | collective-permute-start | bytes 1966088 | tf_op jit(solution)/shard_map/ppermute | solution.py:62
  4.7 1.5 %token_factor.1 = (f32[8,128]{1,0:T(8,128)S(1)}, bf16[12,5120]{1,0:T(8,128)(2,1)S(1)}) custom-call(f32[4,5120]{1,0:T(4,128)} %bitcast.2, bf16[1,64,5120]{2,1,0:T(8,128)(2,1)} %refs_0_.5), custom_call_target="tpu_custom_call" | custom-call | flops 1 | bytes 1 | tf_op jit(solution)/shard_map/token_factor/pallas_call | solution.py:406
  6.2 4.2 %error_left.1 = (f32[4,768]{1,0:T(4,128)S(1)}, bf16[1,768,5120]{2,1,0:T(8,128)(2,1)S(1)}) custom-call(bf16[12,5120]{1,0:T(8,128)(2,1)S(1)} %get-tuple-element.43.terms_ref, bf16[1,768,5120]{2,1,0:T(8,128)(2,1)} %e_hbm.1), custom_call_target="tpu_custom_call" | custom-call | flops 4600000000 | bytes 1 | tf_op jit(solution)/shard_map/error_left/pallas_call | solution.py:417
  10.4 1.4 %collective-permute-start.3 = (f32[8,128]{1,0:T(8,128)S(1)}, f32[8,128]{1,0:T(8,128)S(1)}, u32[]{:S(2)}, u32[]{:S(2)}) collective-permute-start(f32[8,128]{1,0:T(8,128)S(1)} %get-tuple-element.47.refs_0_), channel_id=1, source_target_pairs={{0,3},{1,0},{2,1},{3,2},{4,7},{5,4},{6,5},{7,6},{8,11},{9,8},{10,9... | collective-permute-start | bytes 12296 | tf_op jit(solution)/shard_map/ppermute | solution.py:67
  12.1 1.9 %collective-permute-start.1 = (f32[8,128]{1,0:T(8,128)S(1)}, f32[8,128]{1,0:T(8,128)S(1)}, u32[]{:S(2)}, u32[]{:S(2)}) collective-permute-start(f32[8,128]{1,0:T(8,128)S(1)} %get-tuple-element.47.refs_0_), channel_id=1, source_target_pairs={{0,1},{1,2},{2,3},{3,0},{4,5},{5,6},{6,7},{7,4},{8,9},{9,10},{10,1... | collective-permute-start | bytes 12296 | tf_op jit(solution)/shard_map/ppermute | solution.py:67
  14.1 5.1 %collective-permute-done.3.refs_3_ = f32[8,128]{1,0:T(8,128)S(1)} collective-permute-done((f32[8,128]{1,0:T(8,128)S(1)}, f32[8,128]{1,0:T(8,128)S(1)}, u32[]{:S(2)}, u32[]{:S(2)}) %collective-permute-start.3) | collective-permute-done | bytes 4128 | tf_op jit(solution)/shard_map/ppermute | solution.py:67
  19.2 1.9 %collective-permute-done.2.refs_2_ = f32[8,128]{1,0:T(8,128)S(1)} collective-permute-done((f32[8,128]{1,0:T(8,128)S(1)}, f32[8,128]{1,0:T(8,128)S(1)}, u32[]{:S(2)}, u32[]{:S(2)}) %collective-permute-start.2) | collective-permute-done | bytes 4128 | tf_op jit(solution)/shard_map/ppermute | solution.py:67
  21.1 1.6 %collective-permute-start.8 = (bf16[1,64,5120]{2,1,0:T(8,128)(2,1)S(1)}, bf16[1,64,5120]{2,1,0:T(8,128)(2,1)S(1)}, u32[]{:S(2)}, u32[]{:S(2)}) collective-permute-start(bf16[1,64,5120]{2,1,0:T(8,128)(2,1)S(1)} %collective-permute-done.refs_1_), channel_id=1, source_target_pairs={{0,2},{2,3},{3,1},{1,0},{4,6},{6,7},{7,5},{5,4},{8,10},{10,11},{11... | collective-permute-start | bytes 1966088 | tf_op jit(solution)/shard_map/ppermute | solution.py:62
  22.9 1.2 %collective-permute-done.4.refs_1_ = f32[4,768]{1,0:T(4,128)S(1)} collective-permute-done((f32[4,768]{1,0:T(4,128)S(1)}, f32[4,768]{1,0:T(4,128)S(1)}, u32[]{:S(2)}, u32[]{:S(2)}) %collective-permute-start.4) | collective-permute-done | bytes 12320 | tf_op jit(solution)/shard_map/ppermute | solution.py:72
  24.1 2.4 %collective-permute-start.7 = (f32[4,768]{1,0:T(4,128)S(1)}, f32[4,768]{1,0:T(4,128)S(1)}, u32[]{:S(2)}, u32[]{:S(2)}) collective-permute-start(f32[4,768]{1,0:T(4,128)S(1)} %add.3.refs_0_), channel_id=1, source_target_pairs={{0,24},{4,28},{8,16},{12,20},{16,8},{20,12},{24,0},{28,4},{1,25},{... | collective-permute-start | bytes 36872 | tf_op jit(solution)/shard_map/ppermute | solution.py:72
  28.7 1.5 %collective-permute-done.6.refs_2_ = f32[4,768]{1,0:T(4,128)S(1)} collective-permute-done((f32[4,768]{1,0:T(4,128)S(1)}, f32[4,768]{1,0:T(4,128)S(1)}, u32[]{:S(2)}, u32[]{:S(2)}) %collective-permute-start.6) | collective-permute-done | bytes 12320 | tf_op jit(solution)/shard_map/ppermute | solution.py:72
  31.1 1.4 %collective-permute-start.9 = (f32[8,128]{1,0:T(8,128)S(1)}, f32[8,128]{1,0:T(8,128)S(1)}, u32[]{:S(2)}, u32[]{:S(2)}) collective-permute-start(f32[8,128]{1,0:T(8,128)S(1)} %get-tuple-element.53), channel_id=1, source_target_pairs={{0,2},{2,3},{3,1},{1,0},{4,6},{6,7},{7,5},{5,4},{8,10},{10,11},{11... | collective-permute-start | bytes 12296 | tf_op jit(solution)/shard_map/ppermute | solution.py:62
  33.7 4.2 %collective-permute-done.9.got_ref = f32[8,128]{1,0:T(8,128)S(1)} collective-permute-done((f32[8,128]{1,0:T(8,128)S(1)}, f32[8,128]{1,0:T(8,128)S(1)}, u32[]{:S(2)}, u32[]{:S(2)}) %collective-permute-start.9) | collective-permute-done | bytes 4128 | tf_op jit(solution)/shard_map/ppermute | solution.py:62
  38.0 1.3 %collective-permute-start.14 = (bf16[1,64,3584]{2,1,0:T(8,128)(2,1)S(1)}, bf16[1,64,3584]{2,1,0:T(8,128)(2,1)S(1)}, u32[]{:S(2)}, u32[]{:S(2)}) collective-permute-start(bf16[1,64,3584]{2,1,0:T(8,128)(2,1)S(1)} %get-tuple-element.64), channel_id=1, source_target_pairs={{0,2},{2,3},{3,1},{1,0},{4,6},{6,7},{7,5},{5,4},{8,10},{10,11},{11... | collective-permute-start | bytes 1376264 | tf_op jit(solution)/shard_map/ppermute | solution.py:62
  39.9 1.2 %collective-permute-done.10.refs_1_ = f32[4,2688]{1,0:T(4,128)S(1)} collective-permute-done((f32[4,2688]{1,0:T(4,128)S(1)}, f32[4,2688]{1,0:T(4,128)S(1)}, u32[]{:S(2)}, u32[]{:S(2)}) %collective-permute-start.10) | collective-permute-done | bytes 43040 | tf_op jit(solution)/shard_map/ppermute | solution.py:72
  41.1 2.5 %collective-permute-start.13 = (f32[4,2688]{1,0:T(4,128)S(1)}, f32[4,2688]{1,0:T(4,128)S(1)}, u32[]{:S(2)}, u32[]{:S(2)}) collective-permute-start(f32[4,2688]{1,0:T(4,128)S(1)} %add.4.refs_0_), channel_id=1, source_target_pairs={{0,24},{4,28},{8,16},{12,20},{16,8},{20,12},{24,0},{28,4},{1,25},{... | collective-permute-start | bytes 129032 | tf_op jit(solution)/shard_map/ppermute | solution.py:72
  44.7 1.4 %collective-permute-done.13.refs_3_ = f32[4,2688]{1,0:T(4,128)S(1)} collective-permute-done((f32[4,2688]{1,0:T(4,128)S(1)}, f32[4,2688]{1,0:T(4,128)S(1)}, u32[]{:S(2)}, u32[]{:S(2)}) %collective-permute-start.13) | collective-permute-done | bytes 43040 | tf_op jit(solution)/shard_map/ppermute | solution.py:72
  46.1 1.5 %collective-permute-done.12.refs_2_ = f32[4,2688]{1,0:T(4,128)S(1)} collective-permute-done((f32[4,2688]{1,0:T(4,128)S(1)}, f32[4,2688]{1,0:T(4,128)S(1)}, u32[]{:S(2)}, u32[]{:S(2)}) %collective-permute-start.12) | collective-permute-done | bytes 43040 | tf_op jit(solution)/shard_map/ppermute | solution.py:72
  48.2 1.6 %collective-permute-start.17 = (f32[4,2688]{1,0:T(4,128)S(1)}, f32[4,2688]{1,0:T(4,128)S(1)}, u32[]{:S(2)}, u32[]{:S(2)}) collective-permute-start(f32[4,2688]{1,0:T(4,128)S(1)} %add.5.refs_0_), channel_id=1, source_target_pairs={{0,3},{1,2},{2,1},{3,0},{4,7},{5,6},{6,5},{7,4},{8,11},{9,10},{10,... | collective-permute-start | bytes 129032 | tf_op jit(solution)/shard_map/ppermute | solution.py:72
  50.5 2.1 %collective-permute-start.15 = (f32[4,2688]{1,0:T(4,128)S(1)}, f32[4,2688]{1,0:T(4,128)S(1)}, u32[]{:S(2)}, u32[]{:S(2)}) collective-permute-start(f32[4,2688]{1,0:T(4,128)S(1)} %add.5.refs_0_), channel_id=1, source_target_pairs={{0,1},{1,0},{2,3},{3,2},{4,5},{5,4},{6,7},{7,6},{8,9},{9,8},{10,11... | collective-permute-start | bytes 129032 | tf_op jit(solution)/shard_map/ppermute | solution.py:72
  52.8 1.3 %collective-permute-done.17.refs_3_ = f32[4,2688]{1,0:T(4,128)S(1)} collective-permute-done((f32[4,2688]{1,0:T(4,128)S(1)}, f32[4,2688]{1,0:T(4,128)S(1)}, u32[]{:S(2)}, u32[]{:S(2)}) %collective-permute-start.17) | collective-permute-done | bytes 43040 | tf_op jit(solution)/shard_map/ppermute | solution.py:72
  55.3 1.7 %collective-permute-start.19 = (bf16[1,64,1536]{2,1,0:T(8,128)(2,1)S(1)}, bf16[1,64,1536]{2,1,0:T(8,128)(2,1)S(1)}, u32[]{:S(2)}, u32[]{:S(2)}) collective-permute-start(bf16[1,64,1536]{2,1,0:T(8,128)(2,1)S(1)} %get-tuple-element.73), channel_id=1, source_target_pairs={{0,2},{2,3},{3,1},{1,0},{4,6},{6,7},{7,5},{5,4},{8,10},{10,11},{11... | collective-permute-start | bytes 589832 | tf_op jit(solution)/shard_map/ppermute | solution.py:62
  58.3 4.8 %rebuild.2 = (bf16[768,5120]{1,0:T(8,128)(2,1)}, bf16[1,768,5120]{2,1,0:T(8,128)(2,1)}) custom-call(bf16[768,256]{1,0:T(8,128)(2,1)S(1)} %acts.1.acts_ref, bf16[768,24]{1,0:T(8,128)(2,1)S(1)} %get-tuple-element.69.left_ref, bf16[24,5120]{1,0:T(8,128)(2,1)S(1)} %get-tuple-element.72.right_ref, bf16[1,768,5120]{2,1,0:T(8,128)(2,1)S(1)} %get-tuple-element.55.e_ref, ...), custom_call_target="tpu_custom_call" | custom-call | flops 4000000000 | bytes 1 | tf_op jit(solution)/shard_map/rebuild/pallas_call | solution.py:517
  63.2 2.8 %rebuild.3 = (bf16[768,5120]{1,0:T(8,128)(2,1)}, bf16[1,768,5120]{2,1,0:T(8,128)(2,1)}, f32[4,5120]{1,0:T(4,128)}) custom-call(bf16[768,256]{1,0:T(8,128)(2,1)S(1)} %acts.1.acts_ref, bf16[768,24]{1,0:T(8,128)(2,1)S(1)} %get-tuple-element.69.left_ref, ...), custom_call_target="tpu_custom_call", output_to_operand_aliasing={{0}: (9, {}), {1}: (10, {})} | custom-call | flops 4000000000 | bytes 1 | tf_op jit(solution)/shard_map/rebuild/pallas_call | solution.py:517
  (36 shorter events, 10.5 us)
Async XLA Ops:
  0.6 20.5 %collective-permute-start = (bf16[1,64,5120]{2,1,0:T(8,128)(2,1)}, bf16[1,64,5120]{2,1,0:T(8,128)(2,1)S(1)}, u32[]{:S(2)}, u32[]{:S(2)}) collective-permute-start(bf16[1,64,5120]{2,1,0:T(8,128)(2,1)} %refs_0_.5), channel_id=1, source_target_pairs={{0,2},{2,3},{3,1},{1,0},{4,6},{6,7},{7,5},{5,4},{8,10},{10,11},{11... | collective-permute-start | bytes 1966088 | tf_op jit(solution)/shard_map/ppermute | solution.py:62
  6.2 16.5 %copy-start.1 = (bf16[1,256,768]{2,1,0:T(8,128)(2,1)S(1)}, bf16[1,256,768]{2,1,0:T(8,128)(2,1)}, u32[]{:S(2)}) copy-start(bf16[1,256,768]{2,1,0:T(8,128)(2,1)} %a_ref.5) | copy-start | bytes 1179652
  10.4 28.9 %copy-start = (bf16[1,64,5120]{2,1,0:T(8,128)(2,1)S(1)}, bf16[1,64,5120]{2,1,0:T(8,128)(2,1)}, u32[]{:S(2)}) copy-start(bf16[1,64,5120]{2,1,0:T(8,128)(2,1)} %refs_0_.5) | copy-start | bytes 1966084
  10.4 8.8 %collective-permute-start.3 = (f32[8,128]{1,0:T(8,128)S(1)}, f32[8,128]{1,0:T(8,128)S(1)}, u32[]{:S(2)}, u32[]{:S(2)}) collective-permute-start(f32[8,128]{1,0:T(8,128)S(1)} %get-tuple-element.47.refs_0_), channel_id=1, source_target_pairs={{0,3},{1,0},{2,1},{3,2},{4,7},{5,4},{6,5},{7,6},{8,11},{9,8},{10,9... | collective-permute-start | bytes 12296 | tf_op jit(solution)/shard_map/ppermute | solution.py:67
  11.8 9.2 %collective-permute-start.2 = (f32[8,128]{1,0:T(8,128)S(1)}, f32[8,128]{1,0:T(8,128)S(1)}, u32[]{:S(2)}, u32[]{:S(2)}) collective-permute-start(f32[8,128]{1,0:T(8,128)S(1)} %get-tuple-element.47.refs_0_), channel_id=1, source_target_pairs={{0,2},{1,3},{2,0},{3,1},{4,6},{5,7},{6,4},{7,5},{8,10},{9,11},{10,... | collective-permute-start | bytes 12296 | tf_op jit(solution)/shard_map/ppermute | solution.py:67
  12.1 8.9 %collective-permute-start.1 = (f32[8,128]{1,0:T(8,128)S(1)}, f32[8,128]{1,0:T(8,128)S(1)}, u32[]{:S(2)}, u32[]{:S(2)}) collective-permute-start(f32[8,128]{1,0:T(8,128)S(1)} %get-tuple-element.47.refs_0_), channel_id=1, source_target_pairs={{0,1},{1,2},{2,3},{3,0},{4,5},{5,6},{6,7},{7,4},{8,9},{9,10},{10,1... | collective-permute-start | bytes 12296 | tf_op jit(solution)/shard_map/ppermute | solution.py:67
  21.1 16.8 %collective-permute-start.8 = (bf16[1,64,5120]{2,1,0:T(8,128)(2,1)S(1)}, bf16[1,64,5120]{2,1,0:T(8,128)(2,1)S(1)}, u32[]{:S(2)}, u32[]{:S(2)}) collective-permute-start(bf16[1,64,5120]{2,1,0:T(8,128)(2,1)S(1)} %collective-permute-done.refs_1_), channel_id=1, source_target_pairs={{0,2},{2,3},{3,1},{1,0},{4,6},{6,7},{7,5},{5,4},{8,10},{10,11},{11... | collective-permute-start | bytes 1966088 | tf_op jit(solution)/shard_map/ppermute | solution.py:62
  22.9 1.2 %collective-permute-start.4 = (f32[4,768]{1,0:T(4,128)S(1)}, f32[4,768]{1,0:T(4,128)S(1)}, u32[]{:S(2)}, u32[]{:S(2)}) collective-permute-start(f32[4,768]{1,0:T(4,128)S(1)} %left.1.refs_0_), channel_id=1, source_target_pairs={{0,4},{4,0},{8,12},{12,8},{16,20},{20,16},{24,28},{28,24},{1,5},{5... | collective-permute-start | bytes 36872 | tf_op jit(solution)/shard_map/ppermute | solution.py:72
  24.1 4.6 %collective-permute-start.7 = (f32[4,768]{1,0:T(4,128)S(1)}, f32[4,768]{1,0:T(4,128)S(1)}, u32[]{:S(2)}, u32[]{:S(2)}) collective-permute-start(f32[4,768]{1,0:T(4,128)S(1)} %add.3.refs_0_), channel_id=1, source_target_pairs={{0,24},{4,28},{8,16},{12,20},{16,8},{20,12},{24,0},{28,4},{1,25},{... | collective-permute-start | bytes 36872 | tf_op jit(solution)/shard_map/ppermute | solution.py:72
  26.6 3.7 %collective-permute-start.6 = (f32[4,768]{1,0:T(4,128)S(1)}, f32[4,768]{1,0:T(4,128)S(1)}, u32[]{:S(2)}, u32[]{:S(2)}) collective-permute-start(f32[4,768]{1,0:T(4,128)S(1)} %add.3.refs_0_), channel_id=1, source_target_pairs={{0,16},{4,20},{8,24},{12,28},{16,0},{20,4},{24,8},{28,12},{1,17},{... | collective-permute-start | bytes 36872 | tf_op jit(solution)/shard_map/ppermute | solution.py:72
  27.1 3.7 %collective-permute-start.5 = (f32[4,768]{1,0:T(4,128)S(1)}, f32[4,768]{1,0:T(4,128)S(1)}, u32[]{:S(2)}, u32[]{:S(2)}) collective-permute-start(f32[4,768]{1,0:T(4,128)S(1)} %add.3.refs_0_), channel_id=1, source_target_pairs={{0,8},{4,12},{8,0},{12,4},{16,24},{20,28},{24,16},{28,20},{1,9},{5... | collective-permute-start | bytes 36872 | tf_op jit(solution)/shard_map/ppermute | solution.py:72
  31.1 6.8 %collective-permute-start.9 = (f32[8,128]{1,0:T(8,128)S(1)}, f32[8,128]{1,0:T(8,128)S(1)}, u32[]{:S(2)}, u32[]{:S(2)}) collective-permute-start(f32[8,128]{1,0:T(8,128)S(1)} %get-tuple-element.53), channel_id=1, source_target_pairs={{0,2},{2,3},{3,1},{1,0},{4,6},{6,7},{7,5},{5,4},{8,10},{10,11},{11... | collective-permute-start | bytes 12296 | tf_op jit(solution)/shard_map/ppermute | solution.py:62
  38.0 17.1 %collective-permute-start.14 = (bf16[1,64,3584]{2,1,0:T(8,128)(2,1)S(1)}, bf16[1,64,3584]{2,1,0:T(8,128)(2,1)S(1)}, u32[]{:S(2)}, u32[]{:S(2)}) collective-permute-start(bf16[1,64,3584]{2,1,0:T(8,128)(2,1)S(1)} %get-tuple-element.64), channel_id=1, source_target_pairs={{0,2},{2,3},{3,1},{1,0},{4,6},{6,7},{7,5},{5,4},{8,10},{10,11},{11... | collective-permute-start | bytes 1376264 | tf_op jit(solution)/shard_map/ppermute | solution.py:62
  39.8 1.3 %collective-permute-start.10 = (f32[4,2688]{1,0:T(4,128)S(1)}, f32[4,2688]{1,0:T(4,128)S(1)}, u32[]{:S(2)}, u32[]{:S(2)}) collective-permute-start(f32[4,2688]{1,0:T(4,128)S(1)} %get-tuple-element.63), channel_id=1, source_target_pairs={{0,4},{4,0},{8,12},{12,8},{16,20},{20,16},{24,28},{28,24},{1,5},{5... | collective-permute-start | bytes 129032 | tf_op jit(solution)/shard_map/ppermute | solution.py:72
  41.1 5.0 %collective-permute-start.13 = (f32[4,2688]{1,0:T(4,128)S(1)}, f32[4,2688]{1,0:T(4,128)S(1)}, u32[]{:S(2)}, u32[]{:S(2)}) collective-permute-start(f32[4,2688]{1,0:T(4,128)S(1)} %add.4.refs_0_), channel_id=1, source_target_pairs={{0,24},{4,28},{8,16},{12,20},{16,8},{20,12},{24,0},{28,4},{1,25},{... | collective-permute-start | bytes 129032 | tf_op jit(solution)/shard_map/ppermute | solution.py:72
  43.6 4.0 %collective-permute-start.12 = (f32[4,2688]{1,0:T(4,128)S(1)}, f32[4,2688]{1,0:T(4,128)S(1)}, u32[]{:S(2)}, u32[]{:S(2)}) collective-permute-start(f32[4,2688]{1,0:T(4,128)S(1)} %add.4.refs_0_), channel_id=1, source_target_pairs={{0,16},{4,20},{8,24},{12,28},{16,0},{20,4},{24,8},{28,12},{1,17},{... | collective-permute-start | bytes 129032 | tf_op jit(solution)/shard_map/ppermute | solution.py:72
  44.2 4.0 %collective-permute-start.11 = (f32[4,2688]{1,0:T(4,128)S(1)}, f32[4,2688]{1,0:T(4,128)S(1)}, u32[]{:S(2)}, u32[]{:S(2)}) collective-permute-start(f32[4,2688]{1,0:T(4,128)S(1)} %add.4.refs_0_), channel_id=1, source_target_pairs={{0,8},{4,12},{8,0},{12,4},{16,24},{20,28},{24,16},{28,20},{1,9},{5... | collective-permute-start | bytes 129032 | tf_op jit(solution)/shard_map/ppermute | solution.py:72
  48.2 5.9 %collective-permute-start.17 = (f32[4,2688]{1,0:T(4,128)S(1)}, f32[4,2688]{1,0:T(4,128)S(1)}, u32[]{:S(2)}, u32[]{:S(2)}) collective-permute-start(f32[4,2688]{1,0:T(4,128)S(1)} %add.5.refs_0_), channel_id=1, source_target_pairs={{0,3},{1,2},{2,1},{3,0},{4,7},{5,6},{6,5},{7,4},{8,11},{9,10},{10,... | collective-permute-start | bytes 129032 | tf_op jit(solution)/shard_map/ppermute | solution.py:72
  49.8 5.3 %collective-permute-start.16 = (f32[4,2688]{1,0:T(4,128)S(1)}, f32[4,2688]{1,0:T(4,128)S(1)}, u32[]{:S(2)}, u32[]{:S(2)}) collective-permute-start(f32[4,2688]{1,0:T(4,128)S(1)} %add.5.refs_0_), channel_id=1, source_target_pairs={{0,2},{1,3},{2,0},{3,1},{4,6},{5,7},{6,4},{7,5},{8,10},{9,11},{10,... | collective-permute-start | bytes 129032 | tf_op jit(solution)/shard_map/ppermute | solution.py:72
  50.5 4.6 %collective-permute-start.15 = (f32[4,2688]{1,0:T(4,128)S(1)}, f32[4,2688]{1,0:T(4,128)S(1)}, u32[]{:S(2)}, u32[]{:S(2)}) collective-permute-start(f32[4,2688]{1,0:T(4,128)S(1)} %add.5.refs_0_), channel_id=1, source_target_pairs={{0,1},{1,0},{2,3},{3,2},{4,5},{5,4},{6,7},{7,6},{8,9},{9,8},{10,11... | collective-permute-start | bytes 129032 | tf_op jit(solution)/shard_map/ppermute | solution.py:72
  55.3 2.5 %collective-permute-start.18 = (f32[4,2688]{1,0:T(4,128)S(1)}, f32[4,2688]{1,0:T(4,128)S(1)}, u32[]{:S(2)}, u32[]{:S(2)}) collective-permute-start(f32[4,2688]{1,0:T(4,128)S(1)} %join.1.mine_ref), channel_id=1, source_target_pairs={{0,4},{4,0},{8,12},{12,8},{16,20},{20,16},{24,28},{28,24},{1,5},{5... | collective-permute-start | bytes 129032 | tf_op jit(solution)/shard_map/ppermute | solution.py:72
  55.3 7.9 %collective-permute-start.19 = (bf16[1,64,1536]{2,1,0:T(8,128)(2,1)S(1)}, bf16[1,64,1536]{2,1,0:T(8,128)(2,1)S(1)}, u32[]{:S(2)}, u32[]{:S(2)}) collective-permute-start(bf16[1,64,1536]{2,1,0:T(8,128)(2,1)S(1)} %get-tuple-element.73), channel_id=1, source_target_pairs={{0,2},{2,3},{3,1},{1,0},{4,6},{6,7},{7,5},{5,4},{8,10},{10,11},{11... | collective-permute-start | bytes 589832 | tf_op jit(solution)/shard_map/ppermute | solution.py:62

commit v24 on v20

--- a/solution.py
+++ b/solution.py
@@ -278,21 +278,26 @@
     inv = lower_inverse(total_ref[:, half : half + rank] * (1.0 / m), rank)
     top = total_ref[0:1, half + rank : half + rank + 1] * (ROOM / (m * m))
     scaled = {key: value * top for key, value in inv.items()}
-    return inv, solve(scaled, total_ref[:, 0:half], rank)
-
-
-def half_kernel(m, p_ref, mine_ref, left_ref, whole_ref, right_ref, left, right):
-    inv, half = factor_solve(m, mine_ref)
+    return inv, scaled, solve(scaled, total_ref[:, 0:half], rank)
+
+
+def half_kernel(m, p_ref, mine_ref, left_ref, whole_ref, right_ref, inv_ref, left, right):
+    inv, scaled, half = factor_solve(m, mine_ref)
+    inv_ref[...] = jnp.zeros_like(inv_ref)
+    for (i, j), value in scaled.items():
+        inv_ref[i : i + 1, j : j + 1] = value
     whole_ref[...] = half
     right_ref[...] = stack_terms(RIGHT_TERMS, half, right).astype(BF16)
     ortho = solve(inv, p_ref[...], p_ref.shape[0])
     left_ref[...] = stack_terms(LEFT_TERMS, ortho, left).T.astype(BF16)
 
 
-def factor_kernel(m, other_ref, mine_ref, mine_terms_ref, whole_ref, right_ref, right):
-    half = mine_ref.shape[1]
+def factor_kernel(other_ref, mine_ref, mine_terms_ref, inv_ref, whole_ref, right_ref, right):
+    rank, half = mine_ref.shape
     core = lax.rem(lax.axis_index("dp"), 2)
-    _, other = factor_solve(m, other_ref)
+    other = 0.0
+    for j in range(rank):
+        other = other + inv_ref[0:rank, j : j + 1] * other_ref[j : j + 1, 0:half]
     terms = stack_terms(RIGHT_TERMS, other, right).astype(BF16)
     for c in range(2):
 
@@ -454,7 +459,7 @@
         "error_right", None, 1.2e9,
     )(scaled, error_v)
 
-    widths = [width * 7 // 10, width * 3 // 10]
+    widths = [width * 3 // 4, width // 4]
     last, (got, right_raw) = after(ring[-1], (got, right_raw))
     newest = list(cut(last, widths))
     newest[0] = step(newest[0])
@@ -485,18 +490,23 @@
 
     terms = len(LEFT_TERMS) * rank
     other = swap(total, "dp", m, 1)
-    left_terms, mine, mine_terms = call(
+    left_terms, mine, mine_terms, inverse = call(
         functools.partial(half_kernel, m),
-        [sds((rows, terms), BF16), sds((rank, half), F32), sds((terms, half), BF16)],
+        [
+            sds((rows, terms), BF16),
+            sds((rank, half), F32),
+            sds((terms, half), BF16),
+            sds((8, 128), F32),
+        ],
         [pltpu.VMEM((terms, rows), F32), pltpu.VMEM((terms, half), F32)],
         "half", None, 1e9,
     )(mean, total)
     whole, right_terms = call(
-        functools.partial(factor_kernel, m),
+        factor_kernel,
         [sds((rank, width), F32), sds((terms, width), BF16)],
         [pltpu.VMEM((terms, half), F32)],
         "factor",
-    )(other, mine, mine_terms)
+    )(other, mine, mine_terms, inverse)
 
     acts = call(
         functools.partial(acts_kernel, n),

time: 66 us -> 65.5 us (level)
  transfers between devices with their start and end apart: 20 -> 20, of which waited for: 13 -> 13; matrix products, arithmetic and copies ran while one was open for 0% -> 0% of each run, Pallas kernels for 22% -> 21%
where the time goes in v24:
time: 65.5 us; the launch traced here: 65.4 us
  starting transfers between devices  25.4 us (39%)
  waiting for transfers between devices  22.5 us (34%)
  Pallas kernels  16.6 us (25%)
  between operations  0.78 us (1%)
    ppermute x12, starting transfers between devices, swap(): return lax.ppermute(x, axis, [(i, i ^ bit) for i in range(n)])  11.7 us
    ppermute x12, waiting for transfers between devices, swap(): return lax.ppermute(x, axis, [(i, i ^ bit) for i in range(n)])  11.3 us
    ppermute x5, starting transfers between devices, ring_step(): lax.ppermute(x, axis, [(ring[p], ring[(p + 1) % n]) for p in range(n)])  10.1 us
    pallas_call x2, Pallas kernels, per_device(): pl.pallas_call(functools.partial(final_kernel, at, part, bases, last), in...  7.43 us
    ppermute x3, waiting for transfers between devices, exchange(): lax.ppermute(pieces[k], axis, [(i, (i + k) % n) for i in range(n)])  6.99 us
    ppermute x5, waiting for transfers between devices, ring_step(): lax.ppermute(x, axis, [(ring[p], ring[(p + 1) % n]) for p in range(n)])  4.2 us
    pallas_call x1, Pallas kernels, per_device(): call(error_left_kernel, [sds((rank, rows), F32), sds((1, rows, width), BF...  4.19 us
    ppermute x3, starting transfers between devices, exchange(): lax.ppermute(pieces[k], axis, [(i, (i + k) % n) for i in range(n)])  3.65 us
  transfers between devices with their start and end apart: 20, of which 13 were waited for; matrix products, arithmetic and copies ran while one was open for 0% of the time, Pallas kernels for 21%

profile of v24, /device:TPU:0, one launch (start us, length us, event | category | flops | bytes accessed | tf_op | source)
XLA Modules:
  0.0 65.4 jit_solution(6123012113882320344)
XLA Ops:
  0.6 4.1 %collective-permute-start = (bf16[1,64,5120]{2,1,0:T(8,128)(2,1)}, bf16[1,64,5120]{2,1,0:T(8,128)(2,1)S(1)}, u32[]{:S(2)}, u32[]{:S(2)}) collective-permute-start(bf16[1,64,5120]{2,1,0:T(8,128)(2,1)} %refs_0_.5), channel_id=1, source_target_pairs={{0,2},{2,3},{3,1},{1,0},{4,6},{6,7},{7,5},{5,4},{8,10},{10,11},{11... | collective-permute-start | bytes 1966088 | tf_op jit(solution)/shard_map/ppermute | solution.py:62
  4.7 1.5 %token_factor.1 = (f32[8,128]{1,0:T(8,128)S(1)}, bf16[12,5120]{1,0:T(8,128)(2,1)S(1)}) custom-call(f32[4,5120]{1,0:T(4,128)} %bitcast.2, bf16[1,64,5120]{2,1,0:T(8,128)(2,1)} %refs_0_.5), custom_call_target="tpu_custom_call" | custom-call | flops 1 | bytes 1 | tf_op jit(solution)/shard_map/token_factor/pallas_call | solution.py:411
  6.2 4.2 %error_left.1 = (f32[4,768]{1,0:T(4,128)S(1)}, bf16[1,768,5120]{2,1,0:T(8,128)(2,1)S(1)}) custom-call(bf16[12,5120]{1,0:T(8,128)(2,1)S(1)} %get-tuple-element.44.terms_ref, bf16[1,768,5120]{2,1,0:T(8,128)(2,1)} %e_hbm.1), custom_call_target="tpu_custom_call" | custom-call | flops 4600000000 | bytes 1 | tf_op jit(solution)/shard_map/error_left/pallas_call | solution.py:422
  10.4 1.4 %collective-permute-start.3 = (f32[8,128]{1,0:T(8,128)S(1)}, f32[8,128]{1,0:T(8,128)S(1)}, u32[]{:S(2)}, u32[]{:S(2)}) collective-permute-start(f32[8,128]{1,0:T(8,128)S(1)} %get-tuple-element.48.refs_0_), channel_id=1, source_target_pairs={{0,3},{1,0},{2,1},{3,2},{4,7},{5,4},{6,5},{7,6},{8,11},{9,8},{10,9... | collective-permute-start | bytes 12296 | tf_op jit(solution)/shard_map/ppermute | solution.py:67
  12.1 1.9 %collective-permute-start.1 = (f32[8,128]{1,0:T(8,128)S(1)}, f32[8,128]{1,0:T(8,128)S(1)}, u32[]{:S(2)}, u32[]{:S(2)}) collective-permute-start(f32[8,128]{1,0:T(8,128)S(1)} %get-tuple-element.48.refs_0_), channel_id=1, source_target_pairs={{0,1},{1,2},{2,3},{3,0},{4,5},{5,6},{6,7},{7,4},{8,9},{9,10},{10,1... | collective-permute-start | bytes 12296 | tf_op jit(solution)/shard_map/ppermute | solution.py:67
  14.1 5.1 %collective-permute-done.3.refs_3_ = f32[8,128]{1,0:T(8,128)S(1)} collective-permute-done((f32[8,128]{1,0:T(8,128)S(1)}, f32[8,128]{1,0:T(8,128)S(1)}, u32[]{:S(2)}, u32[]{:S(2)}) %collective-permute-start.3) | collective-permute-done | bytes 4128 | tf_op jit(solution)/shard_map/ppermute | solution.py:67
  19.2 1.9 %collective-permute-done.2.refs_2_ = f32[8,128]{1,0:T(8,128)S(1)} collective-permute-done((f32[8,128]{1,0:T(8,128)S(1)}, f32[8,128]{1,0:T(8,128)S(1)}, u32[]{:S(2)}, u32[]{:S(2)}) %collective-permute-start.2) | collective-permute-done | bytes 4128 | tf_op jit(solution)/shard_map/ppermute | solution.py:67
  21.1 1.6 %collective-permute-start.8 = (bf16[1,64,5120]{2,1,0:T(8,128)(2,1)S(1)}, bf16[1,64,5120]{2,1,0:T(8,128)(2,1)S(1)}, u32[]{:S(2)}, u32[]{:S(2)}) collective-permute-start(bf16[1,64,5120]{2,1,0:T(8,128)(2,1)S(1)} %collective-permute-done.refs_1_), channel_id=1, source_target_pairs={{0,2},{2,3},{3,1},{1,0},{4,6},{6,7},{7,5},{5,4},{8,10},{10,11},{11... | collective-permute-start | bytes 1966088 | tf_op jit(solution)/shard_map/ppermute | solution.py:62
  22.9 1.2 %collective-permute-done.4.refs_1_ = f32[4,768]{1,0:T(4,128)S(1)} collective-permute-done((f32[4,768]{1,0:T(4,128)S(1)}, f32[4,768]{1,0:T(4,128)S(1)}, u32[]{:S(2)}, u32[]{:S(2)}) %collective-permute-start.4) | collective-permute-done | bytes 12320 | tf_op jit(solution)/shard_map/ppermute | solution.py:72
  24.1 2.4 %collective-permute-start.7 = (f32[4,768]{1,0:T(4,128)S(1)}, f32[4,768]{1,0:T(4,128)S(1)}, u32[]{:S(2)}, u32[]{:S(2)}) collective-permute-start(f32[4,768]{1,0:T(4,128)S(1)} %add.3.refs_0_), channel_id=1, source_target_pairs={{0,24},{4,28},{8,16},{12,20},{16,8},{20,12},{24,0},{28,4},{1,25},{... | collective-permute-start | bytes 36872 | tf_op jit(solution)/shard_map/ppermute | solution.py:72
  28.7 1.5 %collective-permute-done.6.refs_2_ = f32[4,768]{1,0:T(4,128)S(1)} collective-permute-done((f32[4,768]{1,0:T(4,128)S(1)}, f32[4,768]{1,0:T(4,128)S(1)}, u32[]{:S(2)}, u32[]{:S(2)}) %collective-permute-start.6) | collective-permute-done | bytes 12320 | tf_op jit(solution)/shard_map/ppermute | solution.py:72
  31.1 1.4 %collective-permute-start.9 = (f32[8,128]{1,0:T(8,128)S(1)}, f32[8,128]{1,0:T(8,128)S(1)}, u32[]{:S(2)}, u32[]{:S(2)}) collective-permute-start(f32[8,128]{1,0:T(8,128)S(1)} %get-tuple-element.54), channel_id=1, source_target_pairs={{0,2},{2,3},{3,1},{1,0},{4,6},{6,7},{7,5},{5,4},{8,10},{10,11},{11... | collective-permute-start | bytes 12296 | tf_op jit(solution)/shard_map/ppermute | solution.py:62
  33.7 4.2 %collective-permute-done.9.got_ref = f32[8,128]{1,0:T(8,128)S(1)} collective-permute-done((f32[8,128]{1,0:T(8,128)S(1)}, f32[8,128]{1,0:T(8,128)S(1)}, u32[]{:S(2)}, u32[]{:S(2)}) %collective-permute-start.9) | collective-permute-done | bytes 4128 | tf_op jit(solution)/shard_map/ppermute | solution.py:62
  38.0 1.3 %collective-permute-start.14 = (bf16[1,64,3840]{2,1,0:T(8,128)(2,1)S(1)}, bf16[1,64,3840]{2,1,0:T(8,128)(2,1)S(1)}, u32[]{:S(2)}, u32[]{:S(2)}) collective-permute-start(bf16[1,64,3840]{2,1,0:T(8,128)(2,1)S(1)} %get-tuple-element.65), channel_id=1, source_target_pairs={{0,2},{2,3},{3,1},{1,0},{4,6},{6,7},{7,5},{5,4},{8,10},{10,11},{11... | collective-permute-start | bytes 1474568 | tf_op jit(solution)/shard_map/ppermute | solution.py:62
  39.9 1.2 %collective-permute-done.10.refs_1_ = f32[4,2688]{1,0:T(4,128)S(1)} collective-permute-done((f32[4,2688]{1,0:T(4,128)S(1)}, f32[4,2688]{1,0:T(4,128)S(1)}, u32[]{:S(2)}, u32[]{:S(2)}) %collective-permute-start.10) | collective-permute-done | bytes 43040 | tf_op jit(solution)/shard_map/ppermute | solution.py:72
  41.1 2.5 %collective-permute-start.13 = (f32[4,2688]{1,0:T(4,128)S(1)}, f32[4,2688]{1,0:T(4,128)S(1)}, u32[]{:S(2)}, u32[]{:S(2)}) collective-permute-start(f32[4,2688]{1,0:T(4,128)S(1)} %add.4.refs_0_), channel_id=1, source_target_pairs={{0,24},{4,28},{8,16},{12,20},{16,8},{20,12},{24,0},{28,4},{1,25},{... | collective-permute-start | bytes 129032 | tf_op jit(solution)/shard_map/ppermute | solution.py:72
  44.7 1.4 %collective-permute-done.13.refs_3_ = f32[4,2688]{1,0:T(4,128)S(1)} collective-permute-done((f32[4,2688]{1,0:T(4,128)S(1)}, f32[4,2688]{1,0:T(4,128)S(1)}, u32[]{:S(2)}, u32[]{:S(2)}) %collective-permute-start.13) | collective-permute-done | bytes 43040 | tf_op jit(solution)/shard_map/ppermute | solution.py:72
  46.1 1.5 %collective-permute-done.12.refs_2_ = f32[4,2688]{1,0:T(4,128)S(1)} collective-permute-done((f32[4,2688]{1,0:T(4,128)S(1)}, f32[4,2688]{1,0:T(4,128)S(1)}, u32[]{:S(2)}, u32[]{:S(2)}) %collective-permute-start.12) | collective-permute-done | bytes 43040 | tf_op jit(solution)/shard_map/ppermute | solution.py:72
  48.2 1.6 %collective-permute-start.17 = (f32[4,2688]{1,0:T(4,128)S(1)}, f32[4,2688]{1,0:T(4,128)S(1)}, u32[]{:S(2)}, u32[]{:S(2)}) collective-permute-start(f32[4,2688]{1,0:T(4,128)S(1)} %add.5.refs_0_), channel_id=1, source_target_pairs={{0,3},{1,2},{2,1},{3,0},{4,7},{5,6},{6,5},{7,4},{8,11},{9,10},{10,... | collective-permute-start | bytes 129032 | tf_op jit(solution)/shard_map/ppermute | solution.py:72
  50.5 2.1 %collective-permute-start.15 = (f32[4,2688]{1,0:T(4,128)S(1)}, f32[4,2688]{1,0:T(4,128)S(1)}, u32[]{:S(2)}, u32[]{:S(2)}) collective-permute-start(f32[4,2688]{1,0:T(4,128)S(1)} %add.5.refs_0_), channel_id=1, source_target_pairs={{0,1},{1,0},{2,3},{3,2},{4,5},{5,4},{6,7},{7,6},{8,9},{9,8},{10,11... | collective-permute-start | bytes 129032 | tf_op jit(solution)/shard_map/ppermute | solution.py:72
  52.8 1.3 %collective-permute-done.17.refs_3_ = f32[4,2688]{1,0:T(4,128)S(1)} collective-permute-done((f32[4,2688]{1,0:T(4,128)S(1)}, f32[4,2688]{1,0:T(4,128)S(1)}, u32[]{:S(2)}, u32[]{:S(2)}) %collective-permute-start.17) | collective-permute-done | bytes 43040 | tf_op jit(solution)/shard_map/ppermute | solution.py:72
  55.3 1.7 %collective-permute-start.19 = (bf16[1,64,1280]{2,1,0:T(8,128)(2,1)S(1)}, bf16[1,64,1280]{2,1,0:T(8,128)(2,1)S(1)}, u32[]{:S(2)}, u32[]{:S(2)}) collective-permute-start(bf16[1,64,1280]{2,1,0:T(8,128)(2,1)S(1)} %get-tuple-element.75), channel_id=1, source_target_pairs={{0,2},{2,3},{3,1},{1,0},{4,6},{6,7},{7,5},{5,4},{8,10},{10,11},{11... | collective-permute-start | bytes 491528 | tf_op jit(solution)/shard_map/ppermute | solution.py:62
  57.9 5.0 %rebuild.2 = (bf16[768,5120]{1,0:T(8,128)(2,1)}, bf16[1,768,5120]{2,1,0:T(8,128)(2,1)}) custom-call(bf16[768,256]{1,0:T(8,128)(2,1)S(1)} %acts.1.acts_ref, bf16[768,24]{1,0:T(8,128)(2,1)S(1)} %get-tuple-element.70.left_ref, bf16[24,5120]{1,0:T(8,128)(2,1)S(1)} %get-tuple-element.74.right_ref, bf16[1,768,5120]{2,1,0:T(8,128)(2,1)S(1)} %get-tuple-element.56.e_ref, ...), custom_call_target="tpu_custom_call" | custom-call | flops 4000000000 | bytes 1 | tf_op jit(solution)/shard_map/rebuild/pallas_call | solution.py:527
  62.9 2.4 %rebuild.3 = (bf16[768,5120]{1,0:T(8,128)(2,1)}, bf16[1,768,5120]{2,1,0:T(8,128)(2,1)}, f32[4,5120]{1,0:T(4,128)}) custom-call(bf16[768,256]{1,0:T(8,128)(2,1)S(1)} %acts.1.acts_ref, bf16[768,24]{1,0:T(8,128)(2,1)S(1)} %get-tuple-element.70.left_ref, ...), custom_call_target="tpu_custom_call", output_to_operand_aliasing={{0}: (9, {}), {1}: (10, {})} | custom-call | flops 4000000000 | bytes 1 | tf_op jit(solution)/shard_map/rebuild/pallas_call | solution.py:527
  (36 shorter events, 10.1 us)
Async XLA Ops:
  0.6 20.5 %collective-permute-start = (bf16[1,64,5120]{2,1,0:T(8,128)(2,1)}, bf16[1,64,5120]{2,1,0:T(8,128)(2,1)S(1)}, u32[]{:S(2)}, u32[]{:S(2)}) collective-permute-start(bf16[1,64,5120]{2,1,0:T(8,128)(2,1)} %refs_0_.5), channel_id=1, source_target_pairs={{0,2},{2,3},{3,1},{1,0},{4,6},{6,7},{7,5},{5,4},{8,10},{10,11},{11... | collective-permute-start | bytes 1966088 | tf_op jit(solution)/shard_map/ppermute | solution.py:62
  6.2 16.5 %copy-start.1 = (bf16[1,256,768]{2,1,0:T(8,128)(2,1)S(1)}, bf16[1,256,768]{2,1,0:T(8,128)(2,1)}, u32[]{:S(2)}) copy-start(bf16[1,256,768]{2,1,0:T(8,128)(2,1)} %a_ref.5) | copy-start | bytes 1179652
  10.4 28.9 %copy-start = (bf16[1,64,5120]{2,1,0:T(8,128)(2,1)S(1)}, bf16[1,64,5120]{2,1,0:T(8,128)(2,1)}, u32[]{:S(2)}) copy-start(bf16[1,64,5120]{2,1,0:T(8,128)(2,1)} %refs_0_.5) | copy-start | bytes 1966084
  10.4 8.8 %collective-permute-start.3 = (f32[8,128]{1,0:T(8,128)S(1)}, f32[8,128]{1,0:T(8,128)S(1)}, u32[]{:S(2)}, u32[]{:S(2)}) collective-permute-start(f32[8,128]{1,0:T(8,128)S(1)} %get-tuple-element.48.refs_0_), channel_id=1, source_target_pairs={{0,3},{1,0},{2,1},{3,2},{4,7},{5,4},{6,5},{7,6},{8,11},{9,8},{10,9... | collective-permute-start | bytes 12296 | tf_op jit(solution)/shard_map/ppermute | solution.py:67
  11.8 9.2 %collective-permute-start.2 = (f32[8,128]{1,0:T(8,128)S(1)}, f32[8,128]{1,0:T(8,128)S(1)}, u32[]{:S(2)}, u32[]{:S(2)}) collective-permute-start(f32[8,128]{1,0:T(8,128)S(1)} %get-tuple-element.48.refs_0_), channel_id=1, source_target_pairs={{0,2},{1,3},{2,0},{3,1},{4,6},{5,7},{6,4},{7,5},{8,10},{9,11},{10,... | collective-permute-start | bytes 12296 | tf_op jit(solution)/shard_map/ppermute | solution.py:67
  12.1 8.9 %collective-permute-start.1 = (f32[8,128]{1,0:T(8,128)S(1)}, f32[8,128]{1,0:T(8,128)S(1)}, u32[]{:S(2)}, u32[]{:S(2)}) collective-permute-start(f32[8,128]{1,0:T(8,128)S(1)} %get-tuple-element.48.refs_0_), channel_id=1, source_target_pairs={{0,1},{1,2},{2,3},{3,0},{4,5},{5,6},{6,7},{7,4},{8,9},{9,10},{10,1... | collective-permute-start | bytes 12296 | tf_op jit(solution)/shard_map/ppermute | solution.py:67
  21.1 16.8 %collective-permute-start.8 = (bf16[1,64,5120]{2,1,0:T(8,128)(2,1)S(1)}, bf16[1,64,5120]{2,1,0:T(8,128)(2,1)S(1)}, u32[]{:S(2)}, u32[]{:S(2)}) collective-permute-start(bf16[1,64,5120]{2,1,0:T(8,128)(2,1)S(1)} %collective-permute-done.refs_1_), channel_id=1, source_target_pairs={{0,2},{2,3},{3,1},{1,0},{4,6},{6,7},{7,5},{5,4},{8,10},{10,11},{11... | collective-permute-start | bytes 1966088 | tf_op jit(solution)/shard_map/ppermute | solution.py:62
  22.9 1.2 %collective-permute-start.4 = (f32[4,768]{1,0:T(4,128)S(1)}, f32[4,768]{1,0:T(4,128)S(1)}, u32[]{:S(2)}, u32[]{:S(2)}) collective-permute-start(f32[4,768]{1,0:T(4,128)S(1)} %left.1.refs_0_), channel_id=1, source_target_pairs={{0,4},{4,0},{8,12},{12,8},{16,20},{20,16},{24,28},{28,24},{1,5},{5... | collective-permute-start | bytes 36872 | tf_op jit(solution)/shard_map/ppermute | solution.py:72
  24.1 4.6 %collective-permute-start.7 = (f32[4,768]{1,0:T(4,128)S(1)}, f32[4,768]{1,0:T(4,128)S(1)}, u32[]{:S(2)}, u32[]{:S(2)}) collective-permute-start(f32[4,768]{1,0:T(4,128)S(1)} %add.3.refs_0_), channel_id=1, source_target_pairs={{0,24},{4,28},{8,16},{12,20},{16,8},{20,12},{24,0},{28,4},{1,25},{... | collective-permute-start | bytes 36872 | tf_op jit(solution)/shard_map/ppermute | solution.py:72
  26.6 3.7 %collective-permute-start.6 = (f32[4,768]{1,0:T(4,128)S(1)}, f32[4,768]{1,0:T(4,128)S(1)}, u32[]{:S(2)}, u32[]{:S(2)}) collective-permute-start(f32[4,768]{1,0:T(4,128)S(1)} %add.3.refs_0_), channel_id=1, source_target_pairs={{0,16},{4,20},{8,24},{12,28},{16,0},{20,4},{24,8},{28,12},{1,17},{... | collective-permute-start | bytes 36872 | tf_op jit(solution)/shard_map/ppermute | solution.py:72
  27.1 3.7 %collective-permute-start.5 = (f32[4,768]{1,0:T(4,128)S(1)}, f32[4,768]{1,0:T(4,128)S(1)}, u32[]{:S(2)}, u32[]{:S(2)}) collective-permute-start(f32[4,768]{1,0:T(4,128)S(1)} %add.3.refs_0_), channel_id=1, source_target_pairs={{0,8},{4,12},{8,0},{12,4},{16,24},{20,28},{24,16},{28,20},{1,9},{5... | collective-permute-start | bytes 36872 | tf_op jit(solution)/shard_map/ppermute | solution.py:72
  31.1 6.8 %collective-permute-start.9 = (f32[8,128]{1,0:T(8,128)S(1)}, f32[8,128]{1,0:T(8,128)S(1)}, u32[]{:S(2)}, u32[]{:S(2)}) collective-permute-start(f32[8,128]{1,0:T(8,128)S(1)} %get-tuple-element.54), channel_id=1, source_target_pairs={{0,2},{2,3},{3,1},{1,0},{4,6},{6,7},{7,5},{5,4},{8,10},{10,11},{11... | collective-permute-start | bytes 12296 | tf_op jit(solution)/shard_map/ppermute | solution.py:62
  38.0 17.1 %collective-permute-start.14 = (bf16[1,64,3840]{2,1,0:T(8,128)(2,1)S(1)}, bf16[1,64,3840]{2,1,0:T(8,128)(2,1)S(1)}, u32[]{:S(2)}, u32[]{:S(2)}) collective-permute-start(bf16[1,64,3840]{2,1,0:T(8,128)(2,1)S(1)} %get-tuple-element.65), channel_id=1, source_target_pairs={{0,2},{2,3},{3,1},{1,0},{4,6},{6,7},{7,5},{5,4},{8,10},{10,11},{11... | collective-permute-start | bytes 1474568 | tf_op jit(solution)/shard_map/ppermute | solution.py:62
  39.8 1.3 %collective-permute-start.10 = (f32[4,2688]{1,0:T(4,128)S(1)}, f32[4,2688]{1,0:T(4,128)S(1)}, u32[]{:S(2)}, u32[]{:S(2)}) collective-permute-start(f32[4,2688]{1,0:T(4,128)S(1)} %get-tuple-element.64), channel_id=1, source_target_pairs={{0,4},{4,0},{8,12},{12,8},{16,20},{20,16},{24,28},{28,24},{1,5},{5... | collective-permute-start | bytes 129032 | tf_op jit(solution)/shard_map/ppermute | solution.py:72
  41.1 5.0 %collective-permute-start.13 = (f32[4,2688]{1,0:T(4,128)S(1)}, f32[4,2688]{1,0:T(4,128)S(1)}, u32[]{:S(2)}, u32[]{:S(2)}) collective-permute-start(f32[4,2688]{1,0:T(4,128)S(1)} %add.4.refs_0_), channel_id=1, source_target_pairs={{0,24},{4,28},{8,16},{12,20},{16,8},{20,12},{24,0},{28,4},{1,25},{... | collective-permute-start | bytes 129032 | tf_op jit(solution)/shard_map/ppermute | solution.py:72
  43.6 4.0 %collective-permute-start.12 = (f32[4,2688]{1,0:T(4,128)S(1)}, f32[4,2688]{1,0:T(4,128)S(1)}, u32[]{:S(2)}, u32[]{:S(2)}) collective-permute-start(f32[4,2688]{1,0:T(4,128)S(1)} %add.4.refs_0_), channel_id=1, source_target_pairs={{0,16},{4,20},{8,24},{12,28},{16,0},{20,4},{24,8},{28,12},{1,17},{... | collective-permute-start | bytes 129032 | tf_op jit(solution)/shard_map/ppermute | solution.py:72
  44.2 4.0 %collective-permute-start.11 = (f32[4,2688]{1,0:T(4,128)S(1)}, f32[4,2688]{1,0:T(4,128)S(1)}, u32[]{:S(2)}, u32[]{:S(2)}) collective-permute-start(f32[4,2688]{1,0:T(4,128)S(1)} %add.4.refs_0_), channel_id=1, source_target_pairs={{0,8},{4,12},{8,0},{12,4},{16,24},{20,28},{24,16},{28,20},{1,9},{5... | collective-permute-start | bytes 129032 | tf_op jit(solution)/shard_map/ppermute | solution.py:72
  48.2 5.9 %collective-permute-start.17 = (f32[4,2688]{1,0:T(4,128)S(1)}, f32[4,2688]{1,0:T(4,128)S(1)}, u32[]{:S(2)}, u32[]{:S(2)}) collective-permute-start(f32[4,2688]{1,0:T(4,128)S(1)} %add.5.refs_0_), channel_id=1, source_target_pairs={{0,3},{1,2},{2,1},{3,0},{4,7},{5,6},{6,5},{7,4},{8,11},{9,10},{10,... | collective-permute-start | bytes 129032 | tf_op jit(solution)/shard_map/ppermute | solution.py:72
  49.8 5.3 %collective-permute-start.16 = (f32[4,2688]{1,0:T(4,128)S(1)}, f32[4,2688]{1,0:T(4,128)S(1)}, u32[]{:S(2)}, u32[]{:S(2)}) collective-permute-start(f32[4,2688]{1,0:T(4,128)S(1)} %add.5.refs_0_), channel_id=1, source_target_pairs={{0,2},{1,3},{2,0},{3,1},{4,6},{5,7},{6,4},{7,5},{8,10},{9,11},{10,... | collective-permute-start | bytes 129032 | tf_op jit(solution)/shard_map/ppermute | solution.py:72
  50.5 4.6 %collective-permute-start.15 = (f32[4,2688]{1,0:T(4,128)S(1)}, f32[4,2688]{1,0:T(4,128)S(1)}, u32[]{:S(2)}, u32[]{:S(2)}) collective-permute-start(f32[4,2688]{1,0:T(4,128)S(1)} %add.5.refs_0_), channel_id=1, source_target_pairs={{0,1},{1,0},{2,3},{3,2},{4,5},{5,4},{6,7},{7,6},{8,9},{9,8},{10,11... | collective-permute-start | bytes 129032 | tf_op jit(solution)/shard_map/ppermute | solution.py:72
  55.3 2.5 %collective-permute-start.18 = (f32[4,2688]{1,0:T(4,128)S(1)}, f32[4,2688]{1,0:T(4,128)S(1)}, u32[]{:S(2)}, u32[]{:S(2)}) collective-permute-start(f32[4,2688]{1,0:T(4,128)S(1)} %join.1.mine_ref), channel_id=1, source_target_pairs={{0,4},{4,0},{8,12},{12,8},{16,20},{20,16},{24,28},{28,24},{1,5},{5... | collective-permute-start | bytes 129032 | tf_op jit(solution)/shard_map/ppermute | solution.py:72
  55.3 7.6 %collective-permute-start.19 = (bf16[1,64,1280]{2,1,0:T(8,128)(2,1)S(1)}, bf16[1,64,1280]{2,1,0:T(8,128)(2,1)S(1)}, u32[]{:S(2)}, u32[]{:S(2)}) collective-permute-start(bf16[1,64,1280]{2,1,0:T(8,128)(2,1)S(1)} %get-tuple-element.75), channel_id=1, source_target_pairs={{0,2},{2,3},{3,1},{1,0},{4,6},{6,7},{7,5},{5,4},{8,10},{10,11},{11... | collective-permute-start | bytes 491528 | tf_op jit(solution)/shard_map/ppermute | solution.py:62
